TPU v7x, 32 devices: a whole 2x2x4 slice. The times are simulated.
32 devices in a mesh: dp: 8 (over z, y), mp: 4 (over x, core).
Axes of the slice: x: 2, y: 2, z: 4, core: 2. Of those that a mesh axis runs over, the one named last changes fastest.
Arguments:
- layer_input: bfloat16 [1024, 16, 1024], P('dp'), may hold values from -6 to 6
- frame_mask: int32 [1024], P('dp'), may hold values 0 or 1
- gain_attn: bfloat16 [2, 1024], P(None, 'dp'), may hold values from 0.099609375 to 1.8984375
- w_query: bfloat16 [2, 1024, 1024], P(None, 'dp', 'mp'), may hold values from -0.1875 to 0.1875
- w_key: bfloat16 [2, 1024, 1024], P(None, 'dp', 'mp'), may hold values from -0.1875 to 0.1875
- w_value: bfloat16 [2, 1024, 1024], P(None, 'dp', 'mp'), may hold values from -0.1875 to 0.1875
- w_out: bfloat16 [2, 1024, 1024], P(None, 'mp', 'dp'), may hold values from -0.375 to 0.375
- gain_ffn: bfloat16 [2, 1024], P(None, 'dp'), may hold values from 0.099609375 to 1.8984375
- w_gate: bfloat16 [2, 1024, 4096], P(None, 'dp', 'mp'), may hold values from -0.1875 to 0.1875
- w_up: bfloat16 [2, 1024, 4096], P(None, 'dp', 'mp'), may hold values from -0.1875 to 0.1875
- w_down: bfloat16 [2, 4096, 1024], P(None, 'mp', 'dp'), may hold values from -0.09375 to 0.09375
- cotangent: bfloat16 [1024, 16, 1024], P('dp'), may hold values from -6 to 6
Outputs:
- output: bfloat16 [1024, 16, 1024], P('dp')
- grad_input: bfloat16 [1024, 16, 1024], P('dp')
- grad_gain_attn: float32 [2, 1024], P(None, 'dp')
- grad_w_query: float32 [2, 1024, 1024], P(None, 'dp', 'mp')
- grad_w_key: float32 [2, 1024, 1024], P(None, 'dp', 'mp')
- grad_w_value: float32 [2, 1024, 1024], P(None, 'dp', 'mp')
- grad_w_out: float32 [2, 1024, 1024], P(None, 'mp', 'dp')
- grad_gain_ffn: float32 [2, 1024], P(None, 'dp')
- grad_w_gate: float32 [2, 1024, 4096], P(None, 'dp', 'mp')
- grad_w_up: float32 [2, 1024, 4096], P(None, 'dp', 'mp')
- grad_w_down: float32 [2, 4096, 1024], P(None, 'mp', 'dp')
Inputs may be any that keep to these rules, and one draw needn't show every extreme that they name: `frame_mask`: 1 marks a frame that counts, 0 a padded frame.
All inputs are finite; a program needn't handle non-finite values. No bound on the sum of `frame_mask` on one device may be relied on, other than what follows from the above.
Results may differ from a plain program's by a relative error of at most 0.012.
Values may be sent and summed in bfloat16 or wider, within the bound.
No kernel may reach another device: no remote copies, remote signals or barrier semaphores. Data moves between devices by JAX's collectives and lax.ppermute only.
A program may use at most 192 MiB of HBM per device.

v0:
```python
import jax
import jax.numpy as jnp
from jax import lax
from jax.sharding import PartitionSpec as P

HEADS = 16
HDIM = 64


EPS = 1e-05
NEG = -1e30


def by_set(left, weight):
    frames, steps, inner = left.shape
    count = weight.shape[0]
    split = left.reshape(frames, count, steps // count, inner)
    result = jnp.einsum("fcgk,cke->fcge", split, weight, preferred_element_type=jnp.float32)
    return result.reshape(frames, steps, weight.shape[2])


def back_set(grad, weight):
    frames, steps, width = grad.shape
    count = weight.shape[0]
    split = grad.reshape(frames, count, steps // count, width)
    result = jnp.einsum("fcge,cke->fcgk", split, weight, preferred_element_type=jnp.float32)
    return result.reshape(frames, steps, weight.shape[1])


def grad_set(left, grad, count):
    frames, steps, inner = left.shape
    first = left.reshape(frames, count, steps // count, inner)
    second = grad.reshape(frames, count, steps // count, grad.shape[2])
    return jnp.einsum("fcgk,fcge->cke", first, second, preferred_element_type=jnp.float32)


def steps_gain(gain, steps):
    return jnp.repeat(gain.astype(jnp.float32), steps // gain.shape[0], axis=0)


def norm_forward(value, gain_steps):
    scale = lax.rsqrt(jnp.mean(value * value, axis=-1, keepdims=True) + EPS)
    normed = value * scale
    return (normed, scale, (normed * gain_steps).astype(jnp.bfloat16))


def norm_backward(grad_hidden, normed, scale, gain_steps, count):
    scaled = grad_hidden * gain_steps
    grad_value = scale * (scaled - normed * jnp.mean(scaled * normed, axis=-1, keepdims=True))
    per_step = jnp.sum(grad_hidden * normed, axis=0)
    grad_gain = per_step.reshape(count, -1, per_step.shape[-1]).sum(axis=1)
    return (grad_value, grad_gain)


def scores_of(query_heads, key_heads, steps):
    raw = jnp.einsum(
        "fshe,fthe->fhst", query_heads, key_heads, preferred_element_type=jnp.float32
    ) * HDIM ** (-0.5)
    causal = jnp.arange(steps)[:, None] >= jnp.arange(steps)[None, :]
    return jnp.where(causal, raw, NEG)


def on_device(
    layer_input,
    frame_mask,
    gain_attn,
    w_query,
    w_key,
    w_value,
    w_out,
    gain_ffn,
    w_gate,
    w_up,
    w_down,
    cotangent,
):
    frames, steps, width = layer_input.shape
    count = gain_attn.shape[0]
    heads = HEADS // lax.axis_size("mp")
    g_attn, wq, wk, wv, wo, g_ffn, wg, wu, wd = (
        lax.all_gather(gain_attn, "dp", axis=1, tiled=True),
        lax.all_gather(w_query, "dp", axis=1, tiled=True),
        lax.all_gather(w_key, "dp", axis=1, tiled=True),
        lax.all_gather(w_value, "dp", axis=1, tiled=True),
        lax.all_gather(w_out, "dp", axis=2, tiled=True),
        lax.all_gather(gain_ffn, "dp", axis=1, tiled=True),
        lax.all_gather(w_gate, "dp", axis=1, tiled=True),
        lax.all_gather(w_up, "dp", axis=1, tiled=True),
        lax.all_gather(w_down, "dp", axis=2, tiled=True),
    )
    gain_one = steps_gain(g_attn, steps)
    gain_two = steps_gain(g_ffn, steps)
    inputs = layer_input.astype(jnp.float32)
    normed_one, scale_one, hidden_one = norm_forward(inputs, gain_one)
    query = by_set(hidden_one, wq).astype(jnp.bfloat16)
    key = by_set(hidden_one, wk).astype(jnp.bfloat16)
    value = by_set(hidden_one, wv).astype(jnp.bfloat16)
    query_heads = query.reshape(frames, steps, heads, HDIM)
    key_heads = key.reshape(frames, steps, heads, HDIM)
    value_heads = value.reshape(frames, steps, heads, HDIM)
    masked = scores_of(query_heads, key_heads, steps)
    log_total = jax.nn.logsumexp(masked, axis=-1, keepdims=True)
    probs = jnp.exp(masked - log_total).astype(jnp.bfloat16)
    mixed = jnp.einsum("fhst,fthe->fshe", probs, value_heads, preferred_element_type=jnp.float32)
    mixed = mixed.reshape(frames, steps, -1).astype(jnp.bfloat16)
    attended = lax.psum(by_set(mixed, wo), "mp")
    middle = inputs + attended
    normed_two, scale_two, hidden_two = norm_forward(middle, gain_two)
    gate = by_set(hidden_two, wg)
    up = by_set(hidden_two, wu)
    sigma = jax.nn.sigmoid(gate)
    active = gate * sigma
    inner = (active * up).astype(jnp.bfloat16)
    mlp_out = lax.psum(by_set(inner, wd), "mp")
    output = (middle + mlp_out).astype(jnp.bfloat16)
    b_attn, back_q, back_k, back_v, back_o, b_ffn, back_g, back_u, back_d = (
        lax.all_gather(gain_attn, "dp", axis=1, tiled=True),
        lax.all_gather(w_query, "dp", axis=1, tiled=True),
        lax.all_gather(w_key, "dp", axis=1, tiled=True),
        lax.all_gather(w_value, "dp", axis=1, tiled=True),
        lax.all_gather(w_out, "dp", axis=2, tiled=True),
        lax.all_gather(gain_ffn, "dp", axis=1, tiled=True),
        lax.all_gather(w_gate, "dp", axis=1, tiled=True),
        lax.all_gather(w_up, "dp", axis=1, tiled=True),
        lax.all_gather(w_down, "dp", axis=2, tiled=True),
    )
    back_one = steps_gain(b_attn, steps)
    back_two = steps_gain(b_ffn, steps)
    grad_out = cotangent.astype(jnp.float32) * frame_mask.astype(jnp.float32)[:, None, None]
    grad_low = grad_out.astype(jnp.bfloat16)
    d_down = grad_set(inner, grad_low, count)
    d_inner = back_set(grad_low, back_d)
    d_gate = (d_inner * up * sigma * (1.0 + gate * (1.0 - sigma))).astype(jnp.bfloat16)
    d_up = (d_inner * active).astype(jnp.bfloat16)
    d_w_gate = grad_set(hidden_two, d_gate, count)
    d_w_up = grad_set(hidden_two, d_up, count)
    partial_two = back_set(d_gate, back_g) + back_set(d_up, back_u)
    grad_hidden_two = lax.psum(partial_two, "mp")
    grad_norm_two, d_gain_ffn = norm_backward(
        grad_hidden_two, normed_two, scale_two, back_two, count
    )
    grad_middle = grad_out + grad_norm_two
    middle_low = grad_middle.astype(jnp.bfloat16)
    d_w_out = grad_set(mixed, middle_low, count)
    d_mixed = back_set(middle_low, back_o).astype(jnp.bfloat16)
    d_heads = d_mixed.reshape(frames, steps, heads, HDIM)
    again_masked = scores_of(query_heads, key_heads, steps)
    soft = jnp.exp(again_masked - log_total)
    d_probs = jnp.einsum(
        "fshe,fthe->fhst", d_heads, value_heads, preferred_element_type=jnp.float32
    )
    d_scores = (soft * (d_probs - jnp.sum(soft * d_probs, axis=-1, keepdims=True))).astype(
        jnp.bfloat16
    )
    d_query = jnp.einsum(
        "fhst,fthe->fshe", d_scores, key_heads, preferred_element_type=jnp.float32
    ) * HDIM ** (-0.5)
    d_key = jnp.einsum(
        "fhst,fshe->fthe", d_scores, query_heads, preferred_element_type=jnp.float32
    ) * HDIM ** (-0.5)
    d_value = jnp.einsum("fhst,fshe->fthe", probs, d_heads, preferred_element_type=jnp.float32)
    d_query = d_query.reshape(frames, steps, -1).astype(jnp.bfloat16)
    d_key = d_key.reshape(frames, steps, -1).astype(jnp.bfloat16)
    d_value = d_value.reshape(frames, steps, -1).astype(jnp.bfloat16)
    d_w_query = grad_set(hidden_one, d_query, count)
    d_w_key = grad_set(hidden_one, d_key, count)
    d_w_value = grad_set(hidden_one, d_value, count)
    partial_one = back_set(d_query, back_q) + back_set(d_key, back_k) + back_set(d_value, back_v)
    grad_hidden_one = lax.psum(partial_one, "mp")
    grad_norm_one, d_gain_attn = norm_backward(
        grad_hidden_one, normed_one, scale_one, back_one, count
    )
    grad_input = (grad_middle + grad_norm_one).astype(jnp.bfloat16)
    results = tuple(
        (
            lax.psum_scatter(d_gain_attn, "dp", scatter_dimension=1, tiled=True),
            lax.psum_scatter(d_w_query, "dp", scatter_dimension=1, tiled=True),
            lax.psum_scatter(d_w_key, "dp", scatter_dimension=1, tiled=True),
            lax.psum_scatter(d_w_value, "dp", scatter_dimension=1, tiled=True),
            lax.psum_scatter(d_w_out, "dp", scatter_dimension=2, tiled=True),
            lax.psum_scatter(d_gain_ffn, "dp", scatter_dimension=1, tiled=True),
            lax.psum_scatter(d_w_gate, "dp", scatter_dimension=1, tiled=True),
            lax.psum_scatter(d_w_up, "dp", scatter_dimension=1, tiled=True),
            lax.psum_scatter(d_down, "dp", scatter_dimension=2, tiled=True),
        )
    )
    return (output, grad_input) + results


def solution(mesh):
    return jax.shard_map(
        on_device,
        mesh=mesh,
        in_specs=(
            P("dp", None, None),
            P("dp"),
            P(None, "dp"),
            P(None, "dp", "mp"),
            P(None, "dp", "mp"),
            P(None, "dp", "mp"),
            P(None, "mp", "dp"),
            P(None, "dp"),
            P(None, "dp", "mp"),
            P(None, "dp", "mp"),
            P(None, "mp", "dp"),
            P("dp", None, None),
        ),
        out_specs=(
            P("dp", None, None),
            P("dp", None, None),
            P(None, "dp"),
            P(None, "dp", "mp"),
            P(None, "dp", "mp"),
            P(None, "dp", "mp"),
            P(None, "mp", "dp"),
            P(None, "dp"),
            P(None, "dp", "mp"),
            P(None, "dp", "mp"),
            P(None, "mp", "dp"),
        ),
        check_vma=False,
    )
```

profile of v0, /device:TPU:0, one launch (start us, length us, event | category | flops | bytes accessed | tf_op | source)
XLA Modules:
  0.0 1998.1 jit_solution(5342908050317111217)
XLA Ops:
  10.0 22.5 %all_gather.36 = bf16[2,1024]{1,0:T(2,128)(2,1)S(1)} all-gather(bf16[2,128]{1,0:T(2,128)(2,1)} %param.14), channel_id=1, replica_groups=mesh['dp'=8,'mp'=4] {'dp'}, dimensions={1}, use_global_device_ids=true | all-gather | bytes 4608 | tf_op jit(solution)/shard_map/all_gather | solution.py:81
  32.5 3.1 fusion.11
  36.3 2.6 fusion.24
  38.8 14.2 all-gather.10.cloned.1.call-done
  53.1 7.0 fusion.93
  60.1 34.1 %all-gather.12.cloned.1.call-done = bf16[2,1024,256]{2,1,0:T(8,128)(2,1)} async-done(((bf16[2,128,256]{2,1,0:T(8,128)(2,1)}), bf16[2,1024,256]{2,1,0:T(8,128)(2,1)}) %all-gather.12.cloned.1.call-update) | async-done | bytes 1048592 | tf_op jit(solution)/shard_map/all_gather | solution.py:83
  94.2 8.0 fusion.90
  102.2 33.2 %all-gather.8.cloned.1.call-done = bf16[2,1024,256]{2,1,0:T(8,128)(2,1)} async-done(((bf16[2,128,256]{2,1,0:T(8,128)(2,1)}), bf16[2,1024,256]{2,1,0:T(8,128)(2,1)}) %all-gather.8.cloned.1.call-update) | async-done | bytes 1048592 | tf_op jit(solution)/shard_map/all_gather | solution.py:84
  135.4 8.2 fusion.96
  144.3 3.0 copy.144
  148.9 3.8 copy.145
  154.3 3.8 copy.146
  158.1 2.9 fusion.59
  166.5 3.6 copy.148
  170.1 5.5 all-gather.14.cloned.1.call-done
  175.6 2.5 fusion.108
  178.1 8.1 copy.150
  188.4 18.4 all_gather.41
  206.8 5.1 fusion.23
  211.9 126.3 %all-reduce.5.cloned.1.call-done = f32[128,16,1024]{2,1,0:T(8,128)} async-done(((f32[128,16,1024]{2,1,0:T(8,128)}), f32[128,16,1024]{2,1,0:T(8,128)}) %all-reduce.5.cloned.1.call-update) | async-done | bytes 8388624 | tf_op jit(solution)/shard_map/psum | solution.py:106
  338.2 5.7 multiply_reduce_fusion.2
  343.9 3.2 copy-done
  347.2 2.6 fusion.22
  349.7 64.0 %all-gather.18.cloned.1.call-done = bf16[2,1024,1024]{2,1,0:T(8,128)(2,1)} async-done(((bf16[2,128,1024]{2,1,0:T(8,128)(2,1)}), bf16[2,1024,1024]{2,1,0:T(8,128)(2,1)}) %all-gather.18.cloned.1.call-update) | async-done | bytes 4194320 | tf_op jit(solution)/shard_map/all_gather | solution.py:88
  413.8 13.9 fusion.27
  427.7 60.0 %all-gather.16.cloned.1.call-done = bf16[2,1024,1024]{2,1,0:T(8,128)(2,1)} async-done(((bf16[2,128,1024]{2,1,0:T(8,128)(2,1)}), bf16[2,1024,1024]{2,1,0:T(8,128)(2,1)}) %all-gather.16.cloned.1.call-update) | async-done | bytes 4194320 | tf_op jit(solution)/shard_map/all_gather | solution.py:87
  487.6 14.4 fusion.31
  502.0 61.0 %all-gather.20.cloned.1.call-done = bf16[2,1024,1024]{2,1,0:T(8,128)(2,1)} async-done(((bf16[2,1024,128]{2,1,0:T(8,128)(2,1)}), bf16[2,1024,1024]{2,1,0:T(8,128)(2,1)}) %all-gather.20.cloned.1.call-update) | async-done | bytes 4194320 | tf_op jit(solution)/shard_map/all_gather | solution.py:89
  563.0 17.5 fusion.14
  580.5 11.4 fusion.25
  591.8 8.4 fusion.66
  600.3 8.1 copy.155
  608.5 7.5 fusion.35
  616.0 8.1 copy.153
  624.1 135.5 %all-reduce.7.cloned.1.call-done = f32[128,16,1024]{2,1,0:T(8,128)} async-done(((f32[128,16,1024]{2,1,0:T(8,128)}), f32[128,16,1024]{2,1,0:T(8,128)}) %all-reduce.7.cloned.1.call-update) | async-done | bytes 8388624 | tf_op jit(solution)/shard_map/psum | solution.py:138
  759.6 7.0 multiply_reduce_fusion
  769.0 5.2 convert_bitcast_fusion
  776.2 5.6 fusion.87
  783.4 3.8 copy.158
  787.2 5.5 convert_bitcast_fusion.1
  796.0 2.5 fusion.74
  803.2 3.2 copy.162
  806.4 3.2 copy.165
  809.6 2.8 fusion.101
  814.0 5.4 add_add_fusion
  819.4 11.5 copy.170
  832.1 288.0 %all-reduce.9.cloned.1.call-done = (f32[128,16,1024]{2,1,0:T(8,128)}, f32[128,16,1024]{2,1,0:T(8,128)}) async-done(((f32[128,16,1024]{2,1,0:T(8,128)}, f32[128,16,1024]{2,1,0:T(8,128)}), (f32[128,16,1024]{2,1,0:T(8,128)}, f32[128,16,1024]{2,1,0:T(8,128)})) %all-reduce.9.cloned.1.call-update) | async-done | bytes 16777232 | tf_op jit(solution)/shard_map/psum | solution.py:114
  1120.0 6.4 fusion.10
  1128.1 8.8 fusion.70
  1138.6 5.6 convolution_bitcast_fusion.2
  1145.2 5.3 convolution_bitcast_fusion.1
  1151.5 5.3 convolution_bitcast_fusion
  1157.0 13.7 fusion.56
  1170.8 11.6 fusion.53
  1182.7 11.6 fusion.50
  1196.1 18.5 fusion.9
  1214.6 35.3 %reduce-scatter.28.cloned.1.call-done = f32[128,2]{1,0:T(8,128)} async-done(((f32[1024,2]{1,0:T(8,128)}), f32[128,2]{1,0:T(8,128)}) %reduce-scatter.28.cloned.1.call-update) | async-done | bytes 1040
  1251.4 70.0 %reduce-scatter.20.cloned.1.call-done = f32[2,256,128]{2,1,0:T(8,128)} async-done(((f32[2,256,1024]{2,1,0:T(8,128)}), f32[2,256,128]{2,1,0:T(8,128)}) %reduce-scatter.20.cloned.1.call-update) | async-done | bytes 262160 | tf_op jit(solution)/shard_map/reduce_scatter | solution.py:180
  1321.3 70.9 %reduce-scatter.14.cloned.1.call-done = f32[2,128,256]{2,1,0:T(8,128)} async-done(((f32[2,1024,256]{2,1,0:T(8,128)}), f32[2,128,256]{2,1,0:T(8,128)}) %reduce-scatter.14.cloned.1.call-update) | async-done | bytes 262160 | tf_op jit(solution)/shard_map/reduce_scatter | solution.py:177
  1392.2 70.9 %reduce-scatter.16.cloned.1.call-done = f32[2,128,256]{2,1,0:T(8,128)} async-done(((f32[2,1024,256]{2,1,0:T(8,128)}), f32[2,128,256]{2,1,0:T(8,128)}) %reduce-scatter.16.cloned.1.call-update) | async-done | bytes 262160 | tf_op jit(solution)/shard_map/reduce_scatter | solution.py:178
  1463.1 70.9 %reduce-scatter.18.cloned.1.call-done = f32[2,128,256]{2,1,0:T(8,128)} async-done(((f32[2,1024,256]{2,1,0:T(8,128)}), f32[2,128,256]{2,1,0:T(8,128)}) %reduce-scatter.18.cloned.1.call-update) | async-done | bytes 262160 | tf_op jit(solution)/shard_map/reduce_scatter | solution.py:179
  1534.0 152.5 %reduce-scatter.26.cloned.1.call-done = f32[2,1024,128]{2,1,0:T(8,128)} async-done(((f32[2,1024,1024]{2,1,0:T(8,128)}), f32[2,1024,128]{2,1,0:T(8,128)}) %reduce-scatter.26.cloned.1.call-update) | async-done | bytes 1048592 | tf_op jit(solution)/shard_map/reduce_scatter | solution.py:184
  1686.5 152.6 %reduce-scatter.24.cloned.1.call-done = f32[2,128,1024]{2,1,0:T(8,128)} async-done(((f32[2,1024,1024]{2,1,0:T(8,128)}), f32[2,128,1024]{2,1,0:T(8,128)}) %reduce-scatter.24.cloned.1.call-update) | async-done | bytes 1048592 | tf_op jit(solution)/shard_map/reduce_scatter | solution.py:183
  1839.0 152.3 %reduce-scatter.22.cloned.1.call-done = f32[2,128,1024]{2,1,0:T(8,128)} async-done(((f32[2,1024,1024]{2,1,0:T(8,128)}), f32[2,128,1024]{2,1,0:T(8,128)}) %reduce-scatter.22.cloned.1.call-update) | async-done | bytes 1048592 | tf_op jit(solution)/shard_map/reduce_scatter | solution.py:182
  (138 shorter events, 40.4 us)
Async XLA Ops:
  7.2 45.9 %all-gather.10.cloned.1.call-start = ((), (), s32[]{:S(2)}) async-start(), calls=%async_computation.10 | async-start | bytes 1179648 | tf_op jit(solution)/shard_map/all_gather | solution.py:82
  7.9 86.3 %all-gather.12.cloned.1.call-start = ((), (), s32[]{:S(2)}) async-start(), calls=%async_computation.11 | async-start | bytes 1179648 | tf_op jit(solution)/shard_map/all_gather | solution.py:83
  8.7 126.7 %all-gather.8.cloned.1.call-start = ((), (), s32[]{:S(2)}) async-start(), calls=%async_computation.9 | async-start | bytes 1179648 | tf_op jit(solution)/shard_map/all_gather | solution.py:84
  9.4 166.2 %all-gather.14.cloned.1.call-start = ((), (), s32[]{:S(2)}) async-start(), calls=%async_computation.12 | async-start | bytes 1179648 | tf_op jit(solution)/shard_map/all_gather | solution.py:85
  10.0 328.2 %all-reduce.5.cloned.1.call-start = ((), (), s32[]{:S(2)}) async-start(), calls=%async_computation.13 | async-start | bytes 16777216 | tf_op jit(solution)/shard_map/psum | solution.py:106
  10.0 26.3 %copy-start.3 = (bf16[128,16,1024]{2,1,0:T(8,128)(2,1)S(1)}, bf16[128,16,1024]{2,1,0:T(8,128)(2,1)}, u32[]{:S(2)}) copy-start(bf16[128,16,1024]{2,1,0:T(8,128)(2,1)} %param.12) | copy-start | bytes 12582916
  32.5 3.1 copy-start.17
  35.7 0.6 copy-start.20
  161.0 2.1 copy-start.1
  161.0 3.1 copy-start.7
  170.1 8.1 copy-start.11
  186.2 2.2 copy-start.33
  186.2 2.2 copy-start.31
  186.3 227.5 %all-gather.18.cloned.1.call-start = ((), (), s32[]{:S(2)}) async-start(), calls=%async_computation.15 | async-start | bytes 4718592 | tf_op jit(solution)/shard_map/all_gather | solution.py:88
  186.8 300.8 %all-gather.16.cloned.1.call-start = ((), (), s32[]{:S(2)}) async-start(), calls=%async_computation.14 | async-start | bytes 4718592 | tf_op jit(solution)/shard_map/all_gather | solution.py:87
  187.6 375.4 %all-gather.20.cloned.1.call-start = ((), (), s32[]{:S(2)}) async-start(), calls=%async_computation.16 | async-start | bytes 4718592 | tf_op jit(solution)/shard_map/all_gather | solution.py:89
  188.3 571.3 %all-reduce.7.cloned.1.call-start = ((), (), s32[]{:S(2)}) async-start(), calls=%async_computation.17 | async-start | bytes 16777216 | tf_op jit(solution)/shard_map/psum | solution.py:138
  188.4 578.2 %copy-start.29 = (f32[128]{0:T(128)}, f32[128]{0:T(128)S(1)}, u32[]{:S(2)}) copy-start(f32[128]{0:T(128)S(1)} %convert_element_type.154) | copy-start | bytes 1540
  206.8 559.8 %copy-start.13 = (f32[16,1024]{1,0:T(8,128)}, f32[16,1024]{1,0:T(8,128)S(1)}, u32[]{:S(2)}) copy-start(f32[16,1024]{1,0:T(8,128)S(1)} %broadcast_bitcast_fusion) | copy-start | bytes 196612
  343.9 3.3 copy-start
  343.9 422.7 %copy-start.15 = (f32[128,16]{1,0:T(8,128)}, f32[128,16]{1,0:T(8,128)S(1)}, u32[]{:S(2)}) copy-start(f32[128,16]{1,0:T(8,128)S(1)} %add_rsqrt_fusion) | copy-start | bytes 24580
  580.5 11.4 copy-start.32
  608.4 511.6 %all-reduce.9.cloned.1.call-start = ((), (), s32[]{:S(2)}) async-start(), calls=%async_computation.27 | async-start | bytes 33554432 | tf_op jit(solution)/shard_map/psum | solution.py:114
  759.6 8.2 copy-start.4
  759.6 9.4 copy-start.5
  769.0 5.2 copy-start.26
  769.0 7.2 copy-start.24
  774.2 2.0 copy-start.12
  787.2 5.6 copy-start.2
  787.2 5.6 copy-start.8
  787.2 5.6 copy-start.9
  796.0 2.6 copy-start.6
  798.6 2.2 copy-start.10
  809.6 2.8 copy-start.23
  812.4 1.6 copy-start.25
  830.9 289.2 %copy-start.18 = (f32[16,1024]{1,0:T(8,128)S(1)}, f32[16,1024]{1,0:T(8,128)}, u32[]{:S(2)}) copy-start(f32[16,1024]{1,0:T(8,128)} %copy-done.17) | copy-start | bytes 196612
  830.9 289.2 %copy-start.21 = (f32[128,16]{1,0:T(8,128)S(1)}, f32[128,16]{1,0:T(8,128)}, u32[]{:S(2)}) copy-start(f32[128,16]{1,0:T(8,128)} %copy-done.20) | copy-start | bytes 24580
  830.9 363.5 %reduce-scatter.30.cloned.1.call-start = ((), (), s32[]{:S(2)}) async-start(), calls=%async_computation.26 | async-start | bytes 589824
  832.0 417.9 %reduce-scatter.28.cloned.1.call-start = ((), (), s32[]{:S(2)}) async-start(), calls=%async_computation.25 | async-start | bytes 589824
  1127.6 193.7 %reduce-scatter.20.cloned.1.call-start = ((), (), s32[]{:S(2)}) async-start(), calls=%async_computation.21 | async-start | bytes 2359296 | tf_op jit(solution)/shard_map/reduce_scatter | solution.py:180
  1136.9 255.4 %reduce-scatter.14.cloned.1.call-start = ((), (), s32[]{:S(2)}) async-start(), calls=%async_computation.18 | async-start | bytes 2359296 | tf_op jit(solution)/shard_map/reduce_scatter | solution.py:177
  1144.2 318.9 %reduce-scatter.16.cloned.1.call-start = ((), (), s32[]{:S(2)}) async-start(), calls=%async_computation.19 | async-start | bytes 2359296 | tf_op jit(solution)/shard_map/reduce_scatter | solution.py:178
  1150.5 383.5 %reduce-scatter.18.cloned.1.call-start = ((), (), s32[]{:S(2)}) async-start(), calls=%async_computation.20 | async-start | bytes 2359296 | tf_op jit(solution)/shard_map/reduce_scatter | solution.py:179
  1156.8 529.7 %reduce-scatter.26.cloned.1.call-start = ((), (), s32[]{:S(2)}) async-start(), calls=%async_computation.24 | async-start | bytes 9437184 | tf_op jit(solution)/shard_map/reduce_scatter | solution.py:184
  1170.8 668.3 %reduce-scatter.24.cloned.1.call-start = ((), (), s32[]{:S(2)}) async-start(), calls=%async_computation.23 | async-start | bytes 9437184 | tf_op jit(solution)/shard_map/reduce_scatter | solution.py:183
  1182.4 808.9 %reduce-scatter.22.cloned.1.call-start = ((), (), s32[]{:S(2)}) async-start(), calls=%async_computation.22 | async-start | bytes 9437184 | tf_op jit(solution)/shard_map/reduce_scatter | solution.py:182
  1194.3 1.7 copy-start.28
  1194.3 1.7 copy-start.14
  1194.3 1.7 copy-start.16
  1194.3 1.7 copy-start.19
  1194.3 1.7 copy-start.22
  1194.3 1.7 copy-start.27
  1194.3 1.7 copy-start.30
Sparse Core Ops, SparseCore 0:
  10.2 42.8 all-gather.9
  55.2 38.9 all-gather.11
  96.4 38.9 all-gather.7
  137.3 38.2 all-gather.13
  186.4 151.7 all-reduce.4
  340.2 73.5 all-gather.17
  415.9 71.6 all-gather.15
  489.7 73.2 all-gather.19
  608.5 151.0 all-reduce.6
  831.0 288.9 all-reduce.8
  1123.4 61.9 reduce-scatter.29
  1188.9 60.9 reduce-scatter.27
  1254.0 67.2 reduce-scatter.19
  1325.3 66.8 reduce-scatter.13
  1396.2 66.9 reduce-scatter.15
  1467.1 66.8 reduce-scatter.17
  1538.0 148.4 reduce-scatter.25
  1691.0 148.0 reduce-scatter.23
  1843.2 148.0 reduce-scatter.21
where the time goes:
time: 2010 us; the launch traced here: 2000 us
  waiting for transfers between devices  1600 us (80%)
  matrix products  194 us (10%)
  local copies, waits for them, and re-layouts  86 us (4%)
  other arithmetic  59.6 us (3%)
  blocking collectives  40.8 us (2%)
    psum x1, waiting for transfers between devices, on_device(): mlp_out = lax.psum(by_set(inner, wd), 'mp')  288 us
    reduce_scatter x1, waiting for transfers between devices, on_device(): lax.psum_scatter(d_w_up, 'dp', scatter_dimension=1, tiled=True)  153 us
    reduce_scatter x1, waiting for transfers between devices, on_device(): lax.psum_scatter(d_down, 'dp', scatter_dimension=2, tiled=True)  152 us
    reduce_scatter x1, waiting for transfers between devices, on_device(): lax.psum_scatter(d_w_gate, 'dp', scatter_dimension=1, tiled=True)  152 us
    psum x1, waiting for transfers between devices, on_device(): grad_hidden_two = lax.psum(partial_two, 'mp')  135 us
    psum x1, waiting for transfers between devices, on_device(): attended = lax.psum(by_set(mixed, wo), 'mp')  126 us
    reduce_scatter x1, waiting for transfers between devices, on_device(): lax.psum_scatter(d_w_key, 'dp', scatter_dimension=1, tiled=True)  70.9 us
    reduce_scatter x1, waiting for transfers between devices, on_device(): lax.psum_scatter(d_w_query, 'dp', scatter_dimension=1, tiled=True)  70.9 us
  transfers between devices with their start and end apart: 19, of which 18 were waited for; matrix products, arithmetic and copies ran while one was open for 10% of the time, Pallas kernels for 0%

commit v1 on v0

v1 whole, which is shorter than its diff:
```python
import functools

import jax
import jax.numpy as jnp
from jax import lax
from jax.experimental import pallas as pl
from jax.experimental.pallas import tpu as pltpu
from jax.sharding import PartitionSpec as P

HDIM = 64
EPS = 1e-05
NEG = -1e30
BF = jnp.bfloat16
F32 = jnp.float32
NN = (((1,), (0,)), ((), ()))
NT = (((1,), (1,)), ((), ()))
TN = (((0,), (0,)), ((), ()))
MIB = 1024 * 1024
SUB = 128
PAIR = 2 * HDIM


def mm(left, right, dims=NN):
    return lax.dot_general(left, right, dims, preferred_element_type=F32)


def kernel_call(body, grid, ins, in_specs, outs, out_specs, flops, scratch=(), vmem=56):
    moved = sum(a.size * a.dtype.itemsize for a in ins) + sum(
        o.size * jnp.dtype(o.dtype).itemsize for o in outs
    )
    return pl.pallas_call(
        body,
        grid=grid,
        in_specs=in_specs,
        out_specs=out_specs,
        out_shape=outs,
        scratch_shapes=scratch,
        compiler_params=pltpu.CompilerParams(vmem_limit_bytes=vmem * MIB),
        cost_estimate=pl.CostEstimate(flops=flops, bytes_accessed=moved, transcendentals=0),
    )(*ins)


def whole(shape):
    return pl.BlockSpec(shape, lambda i: (0,) * len(shape))


def rows_of(rows, width):
    return pl.BlockSpec((rows, width), lambda i: (i, 0))


def out_of(shape, kind=BF):
    return jax.ShapeDtypeStruct(shape, kind)


def split_sets(block):
    frames, steps, width = block.shape
    parts = block.reshape(frames, 2, steps // 2, width)
    return [parts[:, c].reshape(frames * steps // 2, width) for c in range(2)]


def join_sets(first, second, frames):
    width = first.shape[1]
    both = [p.reshape(frames, 1, first.shape[0] // frames, width) for p in (first, second)]
    return jnp.concatenate(both, axis=1).reshape(frames, -1, width)


def prepare_body(x_ref, cot_ref, mask_ref, x0, x1, g0, g1):
    for ref, part in zip((x0, x1), split_sets(x_ref[...].astype(F32))):
        ref[...] = part.astype(BF)
    grad = cot_ref[...].astype(F32) * mask_ref[...]
    for ref, part in zip((g0, g1), split_sets(grad)):
        ref[...] = part.astype(BF)


def prepare(x, cot, mask):
    frames, steps, width = x.shape
    block = 16
    half = steps // 2
    cube = pl.BlockSpec((block, steps, width), lambda i: (i, 0, 0))
    flat = rows_of(block * half, width)
    tokens = out_of((frames * half, width))
    return kernel_call(
        prepare_body,
        (frames // block,),
        (x, cot, mask),
        [cube, cube, pl.BlockSpec((block, 1, 1), lambda i: (i, 0, 0))],
        [tokens] * 4,
        [flat] * 4,
        0,
    )


def norm(value):
    scale = lax.rsqrt(jnp.mean(value * value, axis=-1, keepdims=True) + EPS)
    return value * scale, scale


def lanes_low(shape):
    return lax.broadcasted_iota(jnp.int32, shape, 1) < HDIM


def stack_heads(pair):
    low = lanes_low(pair.shape)
    zero = jnp.zeros_like(pair)
    return jnp.concatenate([jnp.where(low, pair, zero), jnp.where(low, zero, pair)], axis=0)


def pick_heads(stacked):
    half = stacked.shape[0] // 2
    low = lanes_low((half, stacked.shape[1]))
    return jnp.where(low, stacked[:half], stacked[half:])


def visible(rows, keys, steps):
    row = lax.broadcasted_iota(jnp.int32, (rows, keys), 0) % SUB
    key = lax.broadcasted_iota(jnp.int32, (rows, keys), 1)
    same = row // steps == (key % SUB) // steps
    if keys == SUB:
        return same & (row >= key)
    return same & ((key < SUB) | (row >= key - SUB))


def softmax(query, keys, steps):
    raw = mm(query, keys, NT) * HDIM ** (-0.5)
    masked = jnp.where(visible(raw.shape[0], raw.shape[1], steps), raw, NEG)
    top = jnp.max(masked, axis=-1, keepdims=True)
    power = jnp.exp(masked - top)
    return power / jnp.sum(power, axis=-1, keepdims=True)


def attend_body(steps, heads_width, later, *refs):
    if later:
        x_ref, w_ref, gain_ref, before_ref, h_ref, qkv_ref, mixed_ref, part_ref = refs
    else:
        x_ref, w_ref, gain_ref, h_ref, qkv_ref, mixed_ref, part_ref = refs
    hw = heads_width
    normed, _ = norm(x_ref[...].astype(F32))
    hidden = (normed * gain_ref[...]).astype(BF)
    h_ref[...] = hidden
    qkv = mm(hidden, w_ref[:, : 3 * hw]).astype(BF)
    qkv_ref[...] = qkv
    for s in range(x_ref.shape[0] // SUB):
        rows = slice(s * SUB, (s + 1) * SUB)
        for j in range(hw // PAIR):
            q, k, v = (qkv[rows, t * hw + j * PAIR : t * hw + (j + 1) * PAIR] for t in range(3))
            if later:
                k_old, v_old = (
                    before_ref[rows, t * hw + j * PAIR : t * hw + (j + 1) * PAIR] for t in (1, 2)
                )
                k = jnp.concatenate([k_old, k], axis=0)
                v = jnp.concatenate([v_old, v], axis=0)
            probs = softmax(stack_heads(q), k, steps).astype(BF)
            mixed_ref[rows, j * PAIR : (j + 1) * PAIR] = pick_heads(mm(probs, v)).astype(BF)
    part_ref[...] = mm(mixed_ref[...], w_ref[:, 3 * hw :], NT).astype(BF)


def attend(x, w, gain, before, steps):
    tokens, width = x.shape
    hw = w.shape[1] // 4
    block = 256
    ins = [x, w, gain]
    specs = [rows_of(block, width), whole(w.shape), whole(gain.shape)]
    if before is not None:
        ins.append(before)
        specs.append(rows_of(block, 3 * hw))
    widths = (width, 3 * hw, hw, width)
    return kernel_call(
        functools.partial(attend_body, steps, hw, before is not None),
        (tokens // block,),
        ins,
        specs,
        [out_of((tokens, n)) for n in widths],
        [rows_of(block, n) for n in widths],
        2 * tokens * width * 4 * hw,
    )


def second_norm_body(x_ref, att_ref, gain_ref, h_ref):
    normed, _ = norm(x_ref[...].astype(F32) + att_ref[...].astype(F32))
    h_ref[...] = (normed * gain_ref[...]).astype(BF)


def second_norm(x, att, gain):
    tokens, width = x.shape
    block = 256
    flat = rows_of(block, width)
    return kernel_call(
        second_norm_body,
        (tokens // block,),
        (x, att, gain),
        [flat, flat, whole(gain.shape)],
        [out_of(x.shape)],
        [flat],
        0,
    )[0]


def hidden_body(h_ref, g_ref, wg_ref, wu_ref, wd_ref, inner_ref, dgate_ref, dup_ref):
    chunk = 256
    for s in range(h_ref.shape[0] // chunk):
        rows = slice(s * chunk, (s + 1) * chunk)
        gate = mm(h_ref[rows], wg_ref[...])
        up = mm(h_ref[rows], wu_ref[...])
        d_inner = mm(g_ref[rows], wd_ref[...])
        sigma = 1.0 / (1.0 + jnp.exp(-gate))
        active = gate * sigma
        inner_ref[rows] = (active * up).astype(BF)
        dup_ref[rows] = (d_inner * active).astype(BF)
        dgate_ref[rows] = (d_inner * up * sigma * (1.0 + gate * (1.0 - sigma))).astype(BF)


def hidden_units(h, g, w):
    tokens, width = h.shape
    units = w.shape[1] // 3
    block = 256
    steps = units // block
    cols = [
        pl.BlockSpec((width, block), lambda i, t=t: (0, t * steps + i)) for t in range(3)
    ]
    flat = pl.BlockSpec((tokens, block), lambda i: (0, i))
    return kernel_call(
        hidden_body,
        (steps,),
        (h, g, w, w, w),
        [whole(h.shape), whole(g.shape)] + cols,
        [out_of((tokens, units))] * 3,
        [flat] * 3,
        6 * tokens * width * units,
    )


def back_units_body(units, dgate_ref, dup_ref, inner_ref, w_ref, dh_ref, out_ref):
    grad = mm(dgate_ref[...], w_ref[:, :units], NT) + mm(dup_ref[...], w_ref[:, units : 2 * units], NT)
    dh_ref[...] = grad.astype(BF)
    out_ref[...] = mm(inner_ref[...], w_ref[:, 2 * units :], NT).astype(BF)


def back_units(d_gate, d_up, inner, w):
    tokens, units = inner.shape
    width = w.shape[0]
    block = 256
    flat = rows_of(block, units)
    wide = rows_of(block, width)
    return kernel_call(
        functools.partial(back_units_body, units),
        (tokens // block,),
        (d_gate, d_up, inner, w),
        [flat] * 3 + [whole(w.shape)],
        [out_of((tokens, width))] * 2,
        [wide] * 2,
        6 * tokens * width * units,
    )


def unit_grads_body(units, h_ref, g_ref, dgate_ref, dup_ref, inner_ref, w_ref):
    w_ref[:, :units] = mm(h_ref[...], dgate_ref[...], TN).astype(BF)
    w_ref[:, units : 2 * units] = mm(h_ref[...], dup_ref[...], TN).astype(BF)
    w_ref[:, 2 * units :] = mm(g_ref[...], inner_ref[...], TN).astype(BF)


def unit_grads(h, g, d_gate, d_up, inner):
    tokens, width = h.shape
    units = inner.shape[1]
    block = 256
    cols = pl.BlockSpec((tokens, block), lambda i: (0, i))
    return kernel_call(
        functools.partial(unit_grads_body, units),
        (width // block,),
        (h, g, d_gate, d_up, inner),
        [cols] * 2 + [whole((tokens, units))] * 3,
        [out_of((width, 3 * units))],
        [rows_of(block, 3 * units)],
        6 * tokens * width * units,
    )[0]


def norm_back(grad_hidden, value, gain):
    normed, scale = norm(value)
    scaled = grad_hidden * gain
    back = scale * (scaled - normed * jnp.mean(scaled * normed, axis=-1, keepdims=True))
    return back, jnp.sum(grad_hidden * normed, axis=0, keepdims=True)


def middle_body(x_ref, att_ref, g_ref, dh_ref, gain_ref, dm_ref, dgain_ref):
    value = x_ref[...].astype(F32) + att_ref[...].astype(F32)
    back, d_gain = norm_back(dh_ref[...].astype(F32), value, gain_ref[...])
    dm_ref[...] = (g_ref[...].astype(F32) + back).astype(BF)

    @pl.when(pl.program_id(0) == 0)
    def _():
        dgain_ref[...] = jnp.zeros_like(dgain_ref)

    dgain_ref[...] += d_gain


def middle_back(x, att, g, dh, gain):
    tokens, width = x.shape
    block = 256
    flat = rows_of(block, width)
    return kernel_call(
        middle_body,
        (tokens // block,),
        (x, att, g, dh, gain),
        [flat] * 4 + [whole(gain.shape)],
        [out_of(x.shape), out_of((1, width), F32)],
        [flat, whole((1, width))],
        0,
    )


def attend_back_body(steps, hw, dm0, dm1, w0, w1, qkv0, qkv1, dqkv0, dqkv1, dh0, dh1):
    scale = HDIM ** (-0.5)
    d_mixed = [mm(d[...], w[:, 3 * hw :]).astype(BF) for d, w in ((dm0, w0), (dm1, w1))]
    for s in range(dm0.shape[0] // SUB):
        rows = slice(s * SUB, (s + 1) * SUB)
        for j in range(hw // PAIR):
            cols = [slice(t * hw + j * PAIR, t * hw + (j + 1) * PAIR) for t in range(3)]
            q0, k0, v0 = (qkv0[rows, c] for c in cols)
            q1, k1, v1 = (qkv1[rows, c] for c in cols)
            keys = (k0, jnp.concatenate([k0, k1], axis=0))
            values = (v0, jnp.concatenate([v0, v1], axis=0))
            d_k, d_v = [], []
            for c, (q, out_ref) in enumerate(((q0, dqkv0), (q1, dqkv1))):
                q_two = stack_heads(q)
                d_two = stack_heads(d_mixed[c][rows, cols[0]])
                soft = softmax(q_two, keys[c], steps)
                d_probs = mm(d_two, values[c], NT)
                inside = jnp.sum(soft * d_probs, axis=-1, keepdims=True)
                d_scores = (soft * (d_probs - inside)).astype(BF)
                d_q = pick_heads(mm(d_scores, keys[c])) * scale
                out_ref[rows, cols[0]] = d_q.astype(BF)
                d_k.append(mm(d_scores, q_two, TN) * scale)
                d_v.append(mm(soft.astype(BF), d_two, TN))
            dqkv0[rows, cols[1]] = (d_k[0] + d_k[1][:SUB]).astype(BF)
            dqkv1[rows, cols[1]] = d_k[1][SUB:].astype(BF)
            dqkv0[rows, cols[2]] = (d_v[0] + d_v[1][:SUB]).astype(BF)
            dqkv1[rows, cols[2]] = d_v[1][SUB:].astype(BF)
    dh0[...] = mm(dqkv0[...], w0[:, : 3 * hw], NT).astype(BF)
    dh1[...] = mm(dqkv1[...], w1[:, : 3 * hw], NT).astype(BF)


def attend_back(dm, w, qkv, steps):
    tokens, width = dm[0].shape
    hw = w[0].shape[1] // 4
    block = 256
    return kernel_call(
        functools.partial(attend_back_body, steps, hw),
        (tokens // block,),
        (*dm, *w, *qkv),
        [rows_of(block, width)] * 2 + [whole(w[0].shape)] * 2 + [rows_of(block, 3 * hw)] * 2,
        [out_of((tokens, 3 * hw))] * 2 + [out_of((tokens, width))] * 2,
        [rows_of(block, 3 * hw)] * 2 + [rows_of(block, width)] * 2,
        4 * tokens * width * 4 * hw,
    )


def attend_grads_body(hw, h_ref, dqkv_ref, dm_ref, mixed_ref, w_ref):
    w_ref[:, : 3 * hw] = mm(h_ref[...], dqkv_ref[...], TN).astype(BF)
    w_ref[:, 3 * hw :] = mm(dm_ref[...], mixed_ref[...], TN).astype(BF)


def attend_grads(h, d_qkv, dm, mixed):
    tokens, width = h.shape
    hw = mixed.shape[1]
    block = 256
    cols = pl.BlockSpec((tokens, block), lambda i: (0, i))
    return kernel_call(
        functools.partial(attend_grads_body, hw),
        (width // block,),
        (h, d_qkv, dm, mixed),
        [cols, whole(d_qkv.shape), cols, whole(mixed.shape)],
        [out_of((width, 4 * hw))],
        [rows_of(block, 4 * hw)],
        2 * tokens * width * 4 * hw,
    )[0]


def output_body(x0, x1, a0, a1, m0, m1, out_ref):
    sums = [
        x[...].astype(F32) + a[...].astype(F32) + m[...].astype(F32)
        for x, a, m in ((x0, a0, m0), (x1, a1, m1))
    ]
    out_ref[...] = join_sets(*sums, out_ref.shape[0]).astype(BF)


def output_of(x, att, mlp, shape):
    frames, steps, width = shape
    block = 32
    flat = rows_of(block * steps // 2, width)
    return kernel_call(
        output_body,
        (frames // block,),
        (*x, *att, *mlp),
        [flat] * 6,
        [out_of(shape)],
        [pl.BlockSpec((block, steps, width), lambda i: (i, 0, 0))],
        0,
    )[0]


def input_body(x0, x1, dm0, dm1, dh0, dh1, gain_ref, out_ref, dgain_ref):
    sums, gains = [], []
    for c, (x, dm, dh) in enumerate(((x0, dm0, dh0), (x1, dm1, dh1))):
        back, d_gain = norm_back(dh[...].astype(F32), x[...].astype(F32), gain_ref[c : c + 1])
        sums.append(dm[...].astype(F32) + back)
        gains.append(d_gain)
    out_ref[...] = join_sets(*sums, out_ref.shape[0]).astype(BF)

    @pl.when(pl.program_id(0) == 0)
    def _():
        dgain_ref[...] = jnp.zeros_like(dgain_ref)

    dgain_ref[...] += jnp.concatenate(gains, axis=0)


def input_back(x, dm, dh, gain, shape):
    frames, steps, width = shape
    block = 32
    flat = rows_of(block * steps // 2, width)
    return kernel_call(
        input_body,
        (frames // block,),
        (*x, *dm, *dh, gain),
        [flat] * 6 + [whole(gain.shape)],
        [out_of(shape), out_of(gain.shape, F32)],
        [pl.BlockSpec((block, steps, width), lambda i: (i, 0, 0)), whole(gain.shape)],
        0,
    )


class Ring:
    def __init__(self, size):
        self.size = size
        half = size // 2
        order = [2 * q for q in range(half)] + [2 * (size - 1 - q) + 1 for q in range(half, size)]
        self.ahead = [(order[q], order[(q + 1) % size]) for q in range(size)]
        self.behind = [(b, a) for a, b in self.ahead]
        me = lax.axis_index("dp")
        self.me = me
        self.place = jnp.where(me % 2 == 0, me // 2, size - 1 - me // 2)

    def owner(self, offset):
        q = lax.rem(self.place + offset + self.size, self.size)
        return jnp.where(q < self.size // 2, 2 * q, 2 * (self.size - 1 - q) + 1)

    def gather(self, first, second):
        n = self.size
        if n > 16:
            return lax.all_gather(first, "dp"), lax.all_gather(second, "dp")
        put = lambda whole_, part, at: lax.dynamic_update_index_in_dim(whole_, part, at, 0)
        a, b = first, second
        all_a = put(jnp.zeros((n, *a.shape), a.dtype), a, self.me)
        all_b = put(jnp.zeros((n, *b.shape), b.dtype), b, self.me)
        for k in range(1, n):
            a = lax.ppermute(a, "dp", self.ahead)
            b = lax.ppermute(b, "dp", self.behind)
            all_a = put(all_a, a, self.owner(-k))
            all_b = put(all_b, b, self.owner(k))
        return all_a, all_b

    def scatter(self, first, second):
        n = self.size
        if n > 16:
            return tuple(
                lax.psum_scatter(g, "dp", scatter_dimension=0).astype(F32) for g in (first, second)
            )
        at = lambda g, offset: lax.dynamic_index_in_dim(g, self.owner(offset), 0, keepdims=False)
        a, b = at(first, -1), at(second, 1)
        for k in range(2, n + 1):
            a = lax.ppermute(a, "dp", self.ahead).astype(F32) + at(first, -k).astype(F32)
            b = lax.ppermute(b, "dp", self.behind).astype(F32) + at(second, k).astype(F32)
            if k < n:
                a, b = a.astype(BF), b.astype(BF)
        return a, b

    def doubling(self, value, join):
        step = 1
        while step < self.size:
            other = lax.ppermute(value, "dp", [(i, i ^ step) for i in range(self.size)])
            value = join(value, other, (self.me // step) % 2)
            step *= 2
        return value


def gather_small(ring, value):
    def join(mine, other, bit):
        return jnp.where(
            bit == 0, jnp.concatenate([mine, other], 0), jnp.concatenate([other, mine], 0)
        )

    return ring.doubling(value[None], join)


def sum_heads(part):
    size = lax.axis_size("mp")
    if size != 4:
        return lax.psum(part, "mp")
    near = [(i, i ^ 1) for i in range(size)]
    far = [(i, i ^ 2) for i in range(size)]
    bit = lax.axis_index("mp") % 2
    halves = part.reshape(2, part.shape[0] // 2, part.shape[1])
    mine = lax.dynamic_index_in_dim(halves, bit, 0, keepdims=False)
    other = lax.dynamic_index_in_dim(halves, 1 - bit, 0, keepdims=False)
    got = lax.ppermute(other, "mp", near)
    mine = (mine.astype(F32) + got.astype(F32)).astype(BF)
    got = lax.ppermute(mine, "mp", far)
    mine = (mine.astype(F32) + got.astype(F32)).astype(BF)
    got = lax.ppermute(mine, "mp", near)
    return jnp.where(
        bit == 0, jnp.concatenate([mine, got], 0), jnp.concatenate([got, mine], 0)
    )


def on_device(
    layer_input, frame_mask, gain_attn, w_query, w_key, w_value, w_out, gain_ffn, w_gate, w_up,
    w_down, cotangent,
):
    frames, steps, width = layer_input.shape
    sets = gain_attn.shape[0]
    ring = Ring(lax.axis_size("dp"))
    n = ring.size
    hw = w_query.shape[2]
    units = w_gate.shape[2]
    own = width // n
    each = steps // sets

    small = jnp.concatenate([gain_attn, gain_ffn], 0).astype(F32)
    gains = gather_small(ring, small).transpose(1, 0, 2).reshape(2 * sets, width)
    g_attn, g_ffn = gains[:sets], gains[sets:]
    attn_own = jnp.concatenate([w_query, w_key, w_value, w_out.transpose(0, 2, 1)], 2)
    ffn_own = jnp.concatenate([w_gate, w_up, w_down.transpose(0, 2, 1)], 2)
    w_attn = [w.reshape(width, 4 * hw) for w in ring.gather(attn_own[0], attn_own[1])]
    w_ffn = []
    for c in range(sets):
        pieces = ring.gather(ffn_own[c, : own // 2], ffn_own[c, own // 2 :])
        w_ffn.append(jnp.stack(pieces, 1).reshape(width, 3 * units))

    mask = frame_mask.astype(F32).reshape(frames, 1, 1)
    x0, x1, g0, g1 = prepare(layer_input, cotangent, mask)
    x, g = (x0, x1), (g0, g1)
    h1, qkv, mixed, att, h2, inner, d_gate, d_up, dm, mlp, w_grads, d_gain_ffn = ([] for _ in range(12))
    for c in range(sets):
        out = attend(x[c], w_attn[c], g_attn[c : c + 1], qkv[0] if c else None, each)
        h1.append(out[0])
        qkv.append(out[1])
        mixed.append(out[2])
        att.append(sum_heads(out[3]))
    for c in range(sets):
        h2.append(second_norm(x[c], att[c], g_ffn[c : c + 1]))
        one, two, three = hidden_units(h2[c], g[c], w_ffn[c])
        dh, partial = back_units(two, three, one, w_ffn[c])
        grads = unit_grads(h2[c], g[c], two, three, one)
        low, d_gain = middle_back(x[c], att[c], g[c], sum_heads(dh), g_ffn[c : c + 1])
        dm.append(low)
        d_gain_ffn.append(d_gain)
        mlp.append(sum_heads(partial))
        blocks = grads.reshape(n, 2, own // 2, 3 * units)
        w_grads.append(jnp.concatenate(ring.scatter(blocks[:, 0], blocks[:, 1]), 0))
    output = output_of(x, att, mlp, layer_input.shape)
    dqkv0, dqkv1, part0, part1 = attend_back(dm, w_attn, qkv, each)
    attn_grads = [
        attend_grads(h1[c], d, dm[c], mixed[c]).reshape(n, own, 4 * hw)
        for c, d in enumerate((dqkv0, dqkv1))
    ]
    dh1 = (sum_heads(part0), sum_heads(part1))
    grad_input, d_gain_attn = input_back(x, dm, dh1, g_attn, layer_input.shape)
    attn_own_grads = jnp.stack(ring.scatter(*attn_grads))
    ffn_own_grads = jnp.stack(w_grads)

    d_gains = jnp.concatenate([d_gain_attn, *d_gain_ffn], 0)
    d_gains = ring.doubling(d_gains, lambda mine, other, bit: mine + other)
    d_gains = lax.dynamic_slice_in_dim(d_gains, ring.me * own, own, 1)
    d_query, d_key, d_value, d_out = (attn_own_grads[..., t * hw : (t + 1) * hw] for t in range(4))
    dw_gate, dw_up, dw_down = (ffn_own_grads[..., t * units : (t + 1) * units] for t in range(3))
    return (
        output, grad_input, d_gains[:sets], d_query, d_key, d_value, d_out.transpose(0, 2, 1),
        d_gains[sets:], dw_gate, dw_up, dw_down.transpose(0, 2, 1),
    )


def solution(mesh):
    rows = P("dp", None, None)
    gain = P(None, "dp")
    into = P(None, "dp", "mp")
    back = P(None, "mp", "dp")
    weights = (gain, into, into, into, back, gain, into, into, back)
    return jax.shard_map(
        on_device,
        mesh=mesh,
        in_specs=(rows, P("dp"), *weights, rows),
        out_specs=(rows, rows, *weights),
        check_vma=False,
    )
```

time: 2010 us -> 768 us (0.38)
  waiting for transfers between devices: 1600 us -> 260 us
  matrix products: 194 us -> 0 us
  Pallas kernels: 0 us -> 179 us
  starting transfers between devices: 1.55 us -> 109 us
  blocking collectives: 40.8 us -> 0 us
  local copies, waits for them, and re-layouts: 86 us -> 126 us
  other arithmetic: 59.6 us -> 81.4 us
    reduce_scatter x7 -> x0, waiting for transfers between devices: 740 us -> none  [the longest x1 153 us: on_device(): lax.psum_scatter(d_w_up, 'dp', scatter_dimension=1, tiled=True)]
    psum x3 -> x0, waiting for transfers between devices: 550 us -> none  [the longest x1 288 us: on_device(): mlp_out = lax.psum(by_set(inner, wd), 'mp')]
    all_gather x7 -> x0, waiting for transfers between devices: 272 us -> none  [the longest x1 64 us: on_device(): lax.all_gather(w_up, 'dp', axis=1, tiled=True)]
    ppermute x0 -> x114, waiting for transfers between devices: none -> 260 us  [the longest x21 75.5 us: scatter(): lax.ppermute(b, 'dp', self.behind).astype(F32) + at(second, k).astype(F32)]
    dot_general x27 -> x0, matrix products: 194 us -> none  [the longest x7 61.9 us: grad_set(): jnp.einsum('fcgk,fcge->cke', first, second, preferred_element_type=jnp.fl...]
    pallas_call x0 -> x18, Pallas kernels: none -> 179 us  [kernel_call(): pl.pallas_call(body, grid=grid, in_specs=in_specs, out_specs=out_specs, o...]
    ppermute x0 -> x114, starting transfers between devices: none -> 109 us  [the longest x21 25.7 us: gather(): a = lax.ppermute(a, 'dp', self.ahead)]
    dynamic_update_slice x0 -> x48, local copies, waits for them, and re-layouts: none -> 49.4 us  [gather(): lax.dynamic_update_index_in_dim(whole_, part, at, 0)]
  transfers between devices with their start and end apart: 19 -> 114, of which waited for: 18 -> 44; matrix products, arithmetic and copies ran while one was open for 10% -> 26% of each run, Pallas kernels for 0% -> 18%
where the time goes in v1:
time: 768 us; the launch traced here: 757 us
  waiting for transfers between devices  260 us (34%)
  Pallas kernels  179 us (23%)
  local copies, waits for them, and re-layouts  126 us (16%)
  starting transfers between devices  109 us (14%)
  other arithmetic  81.4 us (11%)
    pallas_call x18, Pallas kernels, kernel_call(): pl.pallas_call(body, grid=grid, in_specs=in_specs, out_specs=out_specs, o...  179 us
    ppermute x21, waiting for transfers between devices, scatter(): lax.ppermute(b, 'dp', self.behind).astype(F32) + at(second, k).astype(F32)  75.5 us
    ppermute x21, waiting for transfers between devices, scatter(): lax.ppermute(a, 'dp', self.ahead).astype(F32) + at(first, -k).astype(F32)  62 us
    ppermute x8, waiting for transfers between devices, sum_heads(): got = lax.ppermute(mine, 'mp', far)  60.4 us
    dynamic_update_slice x48, local copies, waits for them, and re-layouts, gather(): lax.dynamic_update_index_in_dim(whole_, part, at, 0)  49.4 us
    ppermute x21, waiting for transfers between devices, gather(): b = lax.ppermute(b, 'dp', self.behind)  28.5 us
    unnamed x90, local copies, waits for them, and re-layouts  27.6 us
    select_n x8, other arithmetic, sum_heads(): jnp.where(bit == 0, jnp.concatenate([mine, got], 0), jnp.concatenate([got...  27.4 us
  transfers between devices with their start and end apart: 114, of which 44 were waited for; matrix products, arithmetic and copies ran while one was open for 26% of the time, Pallas kernels for 18%

profile of v1, /device:TPU:0, one launch (start us, length us, event | category | flops | bytes accessed | tf_op | source)
XLA Modules:
  0.0 757.4 jit_solution(305119409133370984)
XLA Ops:
  1.4 3.0 collective-permute-start.7
  29.8 3.8 collective-permute-done.8
  33.6 2.6 collective-permute-start.9
  37.0 9.1 %shard_map.203 = (bf16[1024,1024]{1,0:T(8,128)(2,1)}, bf16[1024,1024]{1,0:T(8,128)(2,1)}, bf16[1024,1024]{1,0:T(8,128)(2,1)}, bf16[1024,1024]{1,0:T(8,128)(2,1)}) custom-call(bf16[128,16,1024]{2,1,0:T(8,128)(2,1)} %x_ref.1, bf16[128,16,1024]{2,1,0:T(8,128)(2,1)} %cot_ref.1, f32[128,1,1]{2,1,0:T(1,128)} %copy.102.mask_ref), custom_call_target="tpu_custom_call" | custom-call | bytes 16777728 | tf_op jit(solution)/shard_map/pallas_call | solution.py:31
  46.0 2.7 collective-permute-start.30
  64.5 2.9 collective-permute-done.47
  69.5 3.5 collective-permute-done.14
  80.5 3.9 collective-permute-done.15
  112.5 5.7 collective-permute-done.25
  136.3 4.3 collective-permute-done.26
  157.9 3.9 collective-permute-done.19
  168.7 11.4 %shard_map.204 = (bf16[1024,1024]{1,0:T(8,128)(2,1)}, bf16[1024,768]{1,0:T(8,128)(2,1)}, bf16[1024,256]{1,0:T(8,128)(2,1)}, bf16[1024,1024]{1,0:T(8,128)(2,1)}) custom-call(bf16[1024,1024]{1,0:T(8,128)(2,1)} %get-tuple-element.43.refs_0_.x_ref.x0, bf16[1024,1024]{1,0:T(8,128)(2,1)} %bitcast.342, f32[1,1024]{1,0:T(1,128)} %get-tuple-element.135.refs_2_), custom_call_target="tpu_custom_call" | custom-call | flops 2147483648 | bytes 10489856 | tf_op jit(solution)/shard_map/pallas_call | solution.py:31
  183.1 10.6 %shard_map.205 = (bf16[1024,1024]{1,0:T(8,128)(2,1)}, bf16[1024,768]{1,0:T(8,128)(2,1)}, bf16[1024,256]{1,0:T(8,128)(2,1)}, bf16[1024,1024]{1,0:T(8,128)(2,1)}) custom-call(bf16[1024,1024]{1,0:T(8,128)(2,1)} %get-tuple-element.44.refs_0_.x_ref.x1, bf16[1024,1024]{1,0:T(8,128)(2,1)} %bitcast.26.refs_1_.w1, f32[1,1024]{1,0:T(1,128)} %get-tuple-element.134.refs_2_, ...), custom_call_target="tpu_custom_call" | custom-call | flops 2147483648 | bytes 12062720 | tf_op jit(solution)/shard_map/pallas_call | solution.py:31
  203.6 5.5 collective-permute-done.45
  209.1 7.4 collective-permute-done.28
  217.3 2.7 collective-permute-done.52
  222.9 8.3 %collective-permute-done.53 = bf16[64,3072]{1,0:T(8,128)(2,1)S(1)} collective-permute-done((bf16[64,3072]{1,0:T(8,128)(2,1)S(1)}, bf16[64,3072]{1,0:T(8,128)(2,1)S(1)}, u32[]{:S(2)}, u32[]{:S(2)}) %collective-permute-start.53) | collective-permute-done | bytes 393248 | tf_op jit(solution)/shard_map/ppermute | solution.py:456
  242.9 18.9 %collective-permute-done.21 = bf16[512,1024]{1,0:T(8,128)(2,1)S(1)} collective-permute-done((bf16[512,1024]{1,0:T(8,128)(2,1)S(1)}, bf16[512,1024]{1,0:T(8,128)(2,1)S(1)}, u32[]{:S(2)}, u32[]{:S(2)}) %collective-permute-start.21) | collective-permute-done | bytes 1048608 | tf_op jit(solution)/shard_map/ppermute | solution.py:506
  262.3 3.3 pad_maximum_fusion
  265.5 5.1 pad_maximum_fusion.1
  270.6 10.9 %collective-permute-done.11 = bf16[512,1024]{1,0:T(8,128)(2,1)S(1)} collective-permute-done((bf16[512,1024]{1,0:T(8,128)(2,1)S(1)}, bf16[512,1024]{1,0:T(8,128)(2,1)S(1)}, u32[]{:S(2)}, u32[]{:S(2)}) %collective-permute-start.11) | collective-permute-done | bytes 1048608 | tf_op jit(solution)/shard_map/ppermute | solution.py:506
  284.3 5.0 shard_map.209.h_ref
  289.3 11.9 %shard_map.210 = (bf16[1024,1024]{1,0:T(8,128)(2,1)}, bf16[1024,1024]{1,0:T(8,128)(2,1)}, bf16[1024,1024]{1,0:T(8,128)(2,1)}) custom-call(bf16[1024,1024]{1,0:T(8,128)(2,1)} %shard_map.209.h_ref, bf16[1024,1024]{1,0:T(8,128)(2,1)} %get-tuple-element.53.g_ref, bf16[1024,3072]{1,0:T(8,128)(2,1)} %bitcast.322, bf16[1024,3072]{1,0:T(8,128)(2,1)} %bitcast.323, ...), custom_call_target="tpu_custom_call" | custom-call | flops 6442450944 | bytes 29360128 | tf_op jit(solution)/shard_map/pallas_call | solution.py:31
  301.1 11.8 %shard_map.211 = (bf16[1024,1024]{1,0:T(8,128)(2,1)}, bf16[1024,1024]{1,0:T(8,128)(2,1)}) custom-call(bf16[1024,1024]{1,0:T(8,128)(2,1)} %get-tuple-element.54.dgate_ref, bf16[1024,1024]{1,0:T(8,128)(2,1)} %get-tuple-element.55.dup_ref, bf16[1024,1024]{1,0:T(8,128)(2,1)} %get-tuple-element.56.inner_ref, bf16[1024,3072]{1,0:T(8,128)(2,1)} %bitcast.325), custom_call_target="tpu_custom_call" | custom-call | flops 6442450944 | bytes 16777216 | tf_op jit(solution)/shard_map/pallas_call | solution.py:31
  313.0 11.7 %shard_map.220 = bf16[1024,3072]{1,0:T(8,128)(2,1)} custom-call(bf16[1024,1024]{1,0:T(8,128)(2,1)} %shard_map.209.h_ref, bf16[1024,1024]{1,0:T(8,128)(2,1)} %get-tuple-element.53.g_ref, bf16[1024,1024]{1,0:T(8,128)(2,1)} %get-tuple-element.54.dgate_ref, bf16[1024,1024]{1,0:T(8,128)(2,1)} %get-tuple-element.55.dup_ref, ...), custom_call_target="tpu_custom_call" | custom-call | flops 6442450944 | bytes 16777216 | tf_op jit(solution)/shard_map/pallas_call | solution.py:31
  327.0 4.6 shard_map.206.h_ref
  331.6 11.9 %shard_map.207 = (bf16[1024,1024]{1,0:T(8,128)(2,1)}, bf16[1024,1024]{1,0:T(8,128)(2,1)}, bf16[1024,1024]{1,0:T(8,128)(2,1)}) custom-call(bf16[1024,1024]{1,0:T(8,128)(2,1)} %shard_map.206.h_ref, bf16[1024,1024]{1,0:T(8,128)(2,1)} %get-tuple-element.48.g_ref, bf16[1024,3072]{1,0:T(8,128)(2,1)} %bitcast.314, bf16[1024,3072]{1,0:T(8,128)(2,1)} %bitcast.315, ...), custom_call_target="tpu_custom_call" | custom-call | flops 6442450944 | bytes 29360128 | tf_op jit(solution)/shard_map/pallas_call | solution.py:31
  343.5 11.9 %shard_map.208 = (bf16[1024,1024]{1,0:T(8,128)(2,1)}, bf16[1024,1024]{1,0:T(8,128)(2,1)}) custom-call(bf16[1024,1024]{1,0:T(8,128)(2,1)} %get-tuple-element.49.dgate_ref, bf16[1024,1024]{1,0:T(8,128)(2,1)} %get-tuple-element.50.dup_ref, bf16[1024,1024]{1,0:T(8,128)(2,1)} %get-tuple-element.51.inner_ref, bf16[1024,3072]{1,0:T(8,128)(2,1)} %bitcast.317), custom_call_target="tpu_custom_call" | custom-call | flops 6442450944 | bytes 16777216 | tf_op jit(solution)/shard_map/pallas_call | solution.py:31
  355.4 11.9 %shard_map.219 = bf16[1024,3072]{1,0:T(8,128)(2,1)} custom-call(bf16[1024,1024]{1,0:T(8,128)(2,1)} %shard_map.206.h_ref, bf16[1024,1024]{1,0:T(8,128)(2,1)} %get-tuple-element.48.g_ref, bf16[1024,1024]{1,0:T(8,128)(2,1)} %get-tuple-element.49.dgate_ref, bf16[1024,1024]{1,0:T(8,128)(2,1)} %get-tuple-element.50.dup_ref, ...), custom_call_target="tpu_custom_call" | custom-call | flops 6442450944 | bytes 16777216 | tf_op jit(solution)/shard_map/pallas_call | solution.py:31
  374.2 6.8 collective-permute-done.107
  384.0 4.9 collective-permute-done.93
  391.9 8.9 %collective-permute-done.108 = bf16[64,3072]{1,0:T(8,128)(2,1)S(1)} collective-permute-done((bf16[64,3072]{1,0:T(8,128)(2,1)S(1)}, bf16[64,3072]{1,0:T(8,128)(2,1)S(1)}, u32[]{:S(2)}, u32[]{:S(2)}) %collective-permute-start.108) | collective-permute-done | bytes 393248 | tf_op jit(solution)/shard_map/ppermute | solution.py:471
  401.6 7.6 %collective-permute-done.101 = bf16[64,3072]{1,0:T(8,128)(2,1)S(1)} collective-permute-done((bf16[64,3072]{1,0:T(8,128)(2,1)S(1)}, bf16[64,3072]{1,0:T(8,128)(2,1)S(1)}, u32[]{:S(2)}, u32[]{:S(2)}) %collective-permute-start.101) | collective-permute-done | bytes 393248 | tf_op jit(solution)/shard_map/ppermute | solution.py:470
  410.4 6.6 collective-permute-done.94
  417.8 8.4 %collective-permute-done.87 = bf16[64,3072]{1,0:T(8,128)(2,1)S(1)} collective-permute-done((bf16[64,3072]{1,0:T(8,128)(2,1)S(1)}, bf16[64,3072]{1,0:T(8,128)(2,1)S(1)}, u32[]{:S(2)}, u32[]{:S(2)}) %collective-permute-start.87) | collective-permute-done | bytes 393248 | tf_op jit(solution)/shard_map/ppermute | solution.py:470
  442.9 6.6 collective-permute-done.110
  450.3 7.0 collective-permute-done.103
  458.5 6.6 collective-permute-done.96
  465.9 7.0 collective-permute-done.89
  474.0 7.2 collective-permute-done.111
  481.8 8.5 %collective-permute-done.104 = bf16[64,3072]{1,0:T(8,128)(2,1)S(1)} collective-permute-done((bf16[64,3072]{1,0:T(8,128)(2,1)S(1)}, bf16[64,3072]{1,0:T(8,128)(2,1)S(1)}, u32[]{:S(2)}, u32[]{:S(2)}) %collective-permute-start.104) | collective-permute-done | bytes 393248 | tf_op jit(solution)/shard_map/ppermute | solution.py:470
  490.4 9.8 %collective-permute-done.97 = bf16[64,3072]{1,0:T(8,128)(2,1)S(1)} collective-permute-done((bf16[64,3072]{1,0:T(8,128)(2,1)S(1)}, bf16[64,3072]{1,0:T(8,128)(2,1)S(1)}, u32[]{:S(2)}, u32[]{:S(2)}) %collective-permute-start.97) | collective-permute-done | bytes 393248 | tf_op jit(solution)/shard_map/ppermute | solution.py:471
  500.4 8.6 %collective-permute-done.90 = bf16[64,3072]{1,0:T(8,128)(2,1)S(1)} collective-permute-done((bf16[64,3072]{1,0:T(8,128)(2,1)S(1)}, bf16[64,3072]{1,0:T(8,128)(2,1)S(1)}, u32[]{:S(2)}, u32[]{:S(2)}) %collective-permute-start.90) | collective-permute-done | bytes 393248 | tf_op jit(solution)/shard_map/ppermute | solution.py:470
  523.2 8.1 %collective-permute-done.113 = bf16[64,3072]{1,0:T(8,128)(2,1)S(1)} collective-permute-done((bf16[64,3072]{1,0:T(8,128)(2,1)S(1)}, bf16[64,3072]{1,0:T(8,128)(2,1)S(1)}, u32[]{:S(2)}, u32[]{:S(2)}) %collective-permute-start.113) | collective-permute-done | bytes 393248 | tf_op jit(solution)/shard_map/ppermute | solution.py:471
  533.2 8.2 %collective-permute-done.99 = bf16[64,3072]{1,0:T(8,128)(2,1)S(1)} collective-permute-done((bf16[64,3072]{1,0:T(8,128)(2,1)S(1)}, bf16[64,3072]{1,0:T(8,128)(2,1)S(1)}, u32[]{:S(2)}, u32[]{:S(2)}) %collective-permute-start.99) | collective-permute-done | bytes 393248 | tf_op jit(solution)/shard_map/ppermute | solution.py:471
  541.7 10.4 %collective-permute-done.92 = bf16[64,3072]{1,0:T(8,128)(2,1)S(1)} collective-permute-done((bf16[64,3072]{1,0:T(8,128)(2,1)S(1)}, bf16[64,3072]{1,0:T(8,128)(2,1)S(1)}, u32[]{:S(2)}, u32[]{:S(2)}) %collective-permute-start.92) | collective-permute-done | bytes 393248 | tf_op jit(solution)/shard_map/ppermute | solution.py:470
  554.7 6.4 shard_map.214
  561.1 3.9 maximum_select_fusion.4.dh_ref
  565.0 6.4 shard_map.213
  571.4 25.0 %shard_map.215 = (bf16[1024,768]{1,0:T(8,128)(2,1)}, bf16[1024,768]{1,0:T(8,128)(2,1)}, bf16[1024,1024]{1,0:T(8,128)(2,1)}, bf16[1024,1024]{1,0:T(8,128)(2,1)}) custom-call(bf16[1024,1024]{1,0:T(8,128)(2,1)} %get-tuple-element.59.dm0.dm_ref, bf16[1024,1024]{1,0:T(8,128)(2,1)} %get-tuple-element.61.dm1.dm_ref, bf16[1024,1024]{1,0:T(8,128)(2,1)} %bitcast.343, ...), custom_call_target="tpu_custom_call" | custom-call | flops 4294967296 | bytes 18874368 | tf_op jit(solution)/shard_map/pallas_call | solution.py:31
  596.4 6.4 shard_map.218
  602.8 2.8 constant_dynamic-slice_fusion.1
  609.1 6.4 shard_map.217
  615.5 2.8 constant_dynamic-slice_fusion.9
  645.9 2.7 copy.142
  658.9 2.6 fusion
  663.7 4.8 maximum_select_fusion.3.m1
  673.5 10.6 %collective-permute-done.64 = bf16[512,1024]{1,0:T(8,128)(2,1)} collective-permute-done((bf16[512,1024]{1,0:T(8,128)(2,1)S(1)}, bf16[512,1024]{1,0:T(8,128)(2,1)}, u32[]{:S(2)}, u32[]{:S(2)}) %collective-permute-start.64) | collective-permute-done | bytes 1048608 | tf_op jit(solution)/shard_map/ppermute | solution.py:506
  685.8 18.0 %collective-permute-done.67 = bf16[512,1024]{1,0:T(8,128)(2,1)} collective-permute-done((bf16[512,1024]{1,0:T(8,128)(2,1)}, bf16[512,1024]{1,0:T(8,128)(2,1)}, u32[]{:S(2)}, u32[]{:S(2)}) %collective-permute-start.67) | collective-permute-done | bytes 1048608 | tf_op jit(solution)/shard_map/ppermute | solution.py:506
  707.0 3.9 maximum_select_fusion.2.m0
  714.4 7.2 shard_map.212
  725.8 4.1 maximum_select_fusion.6.dh0
  729.8 3.9 maximum_select_fusion.7.dh1
  733.7 9.0 %shard_map.216 = (bf16[128,16,1024]{2,1,0:T(8,128)(2,1)}, f32[2,1024]{1,0:T(2,128)}) custom-call(bf16[1024,1024]{1,0:T(8,128)(2,1)} %get-tuple-element.43.refs_0_.x_ref.x0, bf16[1024,1024]{1,0:T(8,128)(2,1)} %get-tuple-element.44.refs_0_.x_ref.x1, bf16[1024,1024]{1,0:T(8,128)(2,1)} %get-tuple-element.59.dm0.dm_ref, ...), custom_call_target="tpu_custom_call" | custom-call | bytes 16793600 | tf_op jit(solution)/shard_map/pallas_call | solution.py:31
  (450 shorter events, 287.5 us)
Async XLA Ops:
  1.4 26.8 %collective-permute-start.7 = (f32[1,4,128]{2,1,0:T(4,128)S(1)}, f32[1,4,128]{2,1,0:T(4,128)S(1)}, u32[]{:S(2)}, u32[]{:S(2)}) collective-permute-start(f32[1,4,128]{2,1,0:T(4,128)S(1)} %maximum_convert_fusion), channel_id=1, source_target_pairs={{0,4},{4,0},{8,12},{12,8},{16,20},{20,16},{24,28},{28,24},{1,5},{5... | collective-permute-start | bytes 6152 | tf_op jit(solution)/shard_map/ppermute | solution.py:479
  9.4 40.5 %collective-permute-start.13 = (bf16[128,1024]{0,1:T(8,128)(2,1)}, bf16[128,1024]{0,1:T(8,128)(2,1)S(1)}, u32[]{:S(2)}, u32[]{:S(2)}) collective-permute-start(bf16[128,1024]{0,1:T(8,128)(2,1)} %get-tuple-element.128), channel_id=1, source_target_pairs={{8,0},{16,8},{24,16},{28,24},{20,28},{12,20},{4,12},{0,4},{9,1},{1... | collective-permute-start | bytes 786440 | tf_op jit(solution)/shard_map/ppermute | solution.py:456
  9.4 42.3 %collective-permute-start = (bf16[128,1024]{0,1:T(8,128)(2,1)}, bf16[128,1024]{0,1:T(8,128)(2,1)}, u32[]{:S(2)}, u32[]{:S(2)}) collective-permute-start(bf16[128,1024]{0,1:T(8,128)(2,1)} %get-tuple-element.129), channel_id=1, source_target_pairs={{0,8},{8,16},{16,24},{24,28},{28,20},{20,12},{12,4},{4,0},{1,9},{9... | collective-permute-start | bytes 786440 | tf_op jit(solution)/shard_map/ppermute | solution.py:455
  14.0 42.0 %collective-permute-start.40 = (bf16[64,3072]{1,0:T(8,128)(2,1)}, bf16[64,3072]{1,0:T(8,128)(2,1)}, u32[]{:S(2)}, u32[]{:S(2)}) collective-permute-start(bf16[64,3072]{1,0:T(8,128)(2,1)} %get-tuple-element.120), channel_id=1, source_target_pairs={{0,8},{8,16},{16,24},{24,28},{28,20},{20,12},{12,4},{4,0},{1,9},{9... | collective-permute-start | bytes 1179656 | tf_op jit(solution)/shard_map/ppermute | solution.py:455
  15.6 43.4 %collective-permute-start.23 = (bf16[64,3072]{1,0:T(8,128)(2,1)}, bf16[64,3072]{1,0:T(8,128)(2,1)}, u32[]{:S(2)}, u32[]{:S(2)}) collective-permute-start(bf16[64,3072]{1,0:T(8,128)(2,1)} %get-tuple-element.121), channel_id=1, source_target_pairs={{0,8},{8,16},{16,24},{24,28},{28,20},{20,12},{12,4},{4,0},{1,9},{9... | collective-permute-start | bytes 1179656 | tf_op jit(solution)/shard_map/ppermute | solution.py:455
  46.0 16.1 %collective-permute-start.30 = (bf16[64,3072]{1,0:T(8,128)(2,1)}, bf16[64,3072]{1,0:T(8,128)(2,1)}, u32[]{:S(2)}, u32[]{:S(2)}) collective-permute-start(bf16[64,3072]{1,0:T(8,128)(2,1)} %get-tuple-element.122), channel_id=1, source_target_pairs={{8,0},{16,8},{24,16},{28,24},{20,28},{12,20},{4,12},{0,4},{9,1},{1... | collective-permute-start | bytes 1179656 | tf_op jit(solution)/shard_map/ppermute | solution.py:456
  49.9 17.4 %collective-permute-start.47 = (bf16[64,3072]{1,0:T(8,128)(2,1)}, bf16[64,3072]{1,0:T(8,128)(2,1)}, u32[]{:S(2)}, u32[]{:S(2)}) collective-permute-start(bf16[64,3072]{1,0:T(8,128)(2,1)} %get-tuple-element.123), channel_id=1, source_target_pairs={{8,0},{16,8},{24,16},{28,24},{20,28},{12,20},{4,12},{0,4},{9,1},{1... | collective-permute-start | bytes 1179656 | tf_op jit(solution)/shard_map/ppermute | solution.py:456
  53.5 19.4 %collective-permute-start.14 = (bf16[128,1024]{0,1:T(8,128)(2,1)}, bf16[128,1024]{0,1:T(8,128)(2,1)}, u32[]{:S(2)}, u32[]{:S(2)}) collective-permute-start(bf16[128,1024]{0,1:T(8,128)(2,1)} %copy-done.26), channel_id=1, source_target_pairs={{8,0},{16,8},{24,16},{28,24},{20,28},{12,20},{4,12},{0,4},{9,1},{1... | collective-permute-start | bytes 786440 | tf_op jit(solution)/shard_map/ppermute | solution.py:456
  56.0 19.1 %collective-permute-start.1 = (bf16[128,1024]{0,1:T(8,128)(2,1)}, bf16[128,1024]{0,1:T(8,128)(2,1)}, u32[]{:S(2)}, u32[]{:S(2)}) collective-permute-start(bf16[128,1024]{0,1:T(8,128)(2,1)} %collective-permute-done), channel_id=1, source_target_pairs={{0,8},{8,16},{16,24},{24,28},{28,20},{20,12},{12,4},{4,0},{1,9},{9... | collective-permute-start | bytes 786440 | tf_op jit(solution)/shard_map/ppermute | solution.py:455
  59.0 32.8 %collective-permute-start.41 = (bf16[64,3072]{1,0:T(8,128)(2,1)}, bf16[64,3072]{1,0:T(8,128)(2,1)}, u32[]{:S(2)}, u32[]{:S(2)}) collective-permute-start(bf16[64,3072]{1,0:T(8,128)(2,1)} %collective-permute-done.40), channel_id=1, source_target_pairs={{0,8},{8,16},{16,24},{24,28},{28,20},{20,12},{12,4},{4,0},{1,9},{9... | collective-permute-start | bytes 1179656 | tf_op jit(solution)/shard_map/ppermute | solution.py:455
  62.2 32.4 %collective-permute-start.24 = (bf16[64,3072]{1,0:T(8,128)(2,1)}, bf16[64,3072]{1,0:T(8,128)(2,1)}, u32[]{:S(2)}, u32[]{:S(2)}) collective-permute-start(bf16[64,3072]{1,0:T(8,128)(2,1)} %collective-permute-done.23), channel_id=1, source_target_pairs={{0,8},{8,16},{16,24},{24,28},{28,20},{20,12},{12,4},{4,0},{1,9},{9... | collective-permute-start | bytes 1179656 | tf_op jit(solution)/shard_map/ppermute | solution.py:455
  67.3 29.3 %collective-permute-start.31 = (bf16[64,3072]{1,0:T(8,128)(2,1)}, bf16[64,3072]{1,0:T(8,128)(2,1)}, u32[]{:S(2)}, u32[]{:S(2)}) collective-permute-start(bf16[64,3072]{1,0:T(8,128)(2,1)} %collective-permute-done.30), channel_id=1, source_target_pairs={{8,0},{16,8},{24,16},{28,24},{20,28},{12,20},{4,12},{0,4},{9,1},{1... | collective-permute-start | bytes 1179656 | tf_op jit(solution)/shard_map/ppermute | solution.py:456
  84.4 15.7 %collective-permute-start.48 = (bf16[64,3072]{1,0:T(8,128)(2,1)}, bf16[64,3072]{1,0:T(8,128)(2,1)}, u32[]{:S(2)}, u32[]{:S(2)}) collective-permute-start(bf16[64,3072]{1,0:T(8,128)(2,1)} %collective-permute-done.47), channel_id=1, source_target_pairs={{8,0},{16,8},{24,16},{28,24},{20,28},{12,20},{4,12},{0,4},{9,1},{1... | collective-permute-start | bytes 1179656 | tf_op jit(solution)/shard_map/ppermute | solution.py:456
  94.5 15.4 %collective-permute-start.42 = (bf16[64,3072]{1,0:T(8,128)(2,1)}, bf16[64,3072]{1,0:T(8,128)(2,1)}, u32[]{:S(2)}, u32[]{:S(2)}) collective-permute-start(bf16[64,3072]{1,0:T(8,128)(2,1)} %collective-permute-done.41), channel_id=1, source_target_pairs={{0,8},{8,16},{16,24},{24,28},{28,20},{20,12},{12,4},{4,0},{1,9},{9... | collective-permute-start | bytes 1179656 | tf_op jit(solution)/shard_map/ppermute | solution.py:455
  96.7 21.5 %collective-permute-start.25 = (bf16[64,3072]{1,0:T(8,128)(2,1)}, bf16[64,3072]{1,0:T(8,128)(2,1)}, u32[]{:S(2)}, u32[]{:S(2)}) collective-permute-start(bf16[64,3072]{1,0:T(8,128)(2,1)} %collective-permute-done.24), channel_id=1, source_target_pairs={{0,8},{8,16},{16,24},{24,28},{28,20},{20,12},{12,4},{4,0},{1,9},{9... | collective-permute-start | bytes 1179656 | tf_op jit(solution)/shard_map/ppermute | solution.py:455
  100.2 21.5 %collective-permute-start.32 = (bf16[64,3072]{1,0:T(8,128)(2,1)}, bf16[64,3072]{1,0:T(8,128)(2,1)}, u32[]{:S(2)}, u32[]{:S(2)}) collective-permute-start(bf16[64,3072]{1,0:T(8,128)(2,1)} %collective-permute-done.31), channel_id=1, source_target_pairs={{8,0},{16,8},{24,16},{28,24},{20,28},{12,20},{4,12},{0,4},{9,1},{1... | collective-permute-start | bytes 1179656 | tf_op jit(solution)/shard_map/ppermute | solution.py:456
  102.3 21.5 %collective-permute-start.49 = (bf16[64,3072]{1,0:T(8,128)(2,1)}, bf16[64,3072]{1,0:T(8,128)(2,1)}, u32[]{:S(2)}, u32[]{:S(2)}) collective-permute-start(bf16[64,3072]{1,0:T(8,128)(2,1)} %collective-permute-done.48), channel_id=1, source_target_pairs={{8,0},{16,8},{24,16},{28,24},{20,28},{12,20},{4,12},{0,4},{9,1},{1... | collective-permute-start | bytes 1179656 | tf_op jit(solution)/shard_map/ppermute | solution.py:456
  106.9 20.4 %collective-permute-start.17 = (bf16[128,1024]{0,1:T(8,128)(2,1)}, bf16[128,1024]{0,1:T(8,128)(2,1)S(1)}, u32[]{:S(2)}, u32[]{:S(2)}) collective-permute-start(bf16[128,1024]{0,1:T(8,128)(2,1)} %copy-done.27), channel_id=1, source_target_pairs={{8,0},{16,8},{24,16},{28,24},{20,28},{12,20},{4,12},{0,4},{9,1},{1... | collective-permute-start | bytes 786440 | tf_op jit(solution)/shard_map/ppermute | solution.py:456
  110.0 19.1 %collective-permute-start.4 = (bf16[128,1024]{0,1:T(8,128)(2,1)}, bf16[128,1024]{0,1:T(8,128)(2,1)}, u32[]{:S(2)}, u32[]{:S(2)}) collective-permute-start(bf16[128,1024]{0,1:T(8,128)(2,1)} %collective-permute-done.3), channel_id=1, source_target_pairs={{0,8},{8,16},{16,24},{24,28},{28,20},{20,12},{12,4},{4,0},{1,9},{9... | collective-permute-start | bytes 786440 | tf_op jit(solution)/shard_map/ppermute | solution.py:455
  121.7 19.0 %collective-permute-start.26 = (bf16[64,3072]{1,0:T(8,128)(2,1)}, bf16[64,3072]{1,0:T(8,128)(2,1)}, u32[]{:S(2)}, u32[]{:S(2)}) collective-permute-start(bf16[64,3072]{1,0:T(8,128)(2,1)} %collective-permute-done.25), channel_id=1, source_target_pairs={{0,8},{8,16},{16,24},{24,28},{28,20},{20,12},{12,4},{4,0},{1,9},{9... | collective-permute-start | bytes 1179656 | tf_op jit(solution)/shard_map/ppermute | solution.py:455
  123.8 20.4 %collective-permute-start.33 = (bf16[64,3072]{1,0:T(8,128)(2,1)}, bf16[64,3072]{1,0:T(8,128)(2,1)}, u32[]{:S(2)}, u32[]{:S(2)}) collective-permute-start(bf16[64,3072]{1,0:T(8,128)(2,1)} %collective-permute-done.32), channel_id=1, source_target_pairs={{8,0},{16,8},{24,16},{28,24},{20,28},{12,20},{4,12},{0,4},{9,1},{1... | collective-permute-start | bytes 1179656 | tf_op jit(solution)/shard_map/ppermute | solution.py:456
  127.3 21.9 %collective-permute-start.50 = (bf16[64,3072]{1,0:T(8,128)(2,1)}, bf16[64,3072]{1,0:T(8,128)(2,1)}, u32[]{:S(2)}, u32[]{:S(2)}) collective-permute-start(bf16[64,3072]{1,0:T(8,128)(2,1)} %collective-permute-done.49), channel_id=1, source_target_pairs={{8,0},{16,8},{24,16},{28,24},{20,28},{12,20},{4,12},{0,4},{9,1},{1... | collective-permute-start | bytes 1179656 | tf_op jit(solution)/shard_map/ppermute | solution.py:456
  130.8 16.2 %collective-permute-start.18 = (bf16[128,1024]{0,1:T(8,128)(2,1)}, bf16[128,1024]{0,1:T(8,128)(2,1)}, u32[]{:S(2)}, u32[]{:S(2)}) collective-permute-start(bf16[128,1024]{0,1:T(8,128)(2,1)} %copy-done.28), channel_id=1, source_target_pairs={{8,0},{16,8},{24,16},{28,24},{20,28},{12,20},{4,12},{0,4},{9,1},{1... | collective-permute-start | bytes 786440 | tf_op jit(solution)/shard_map/ppermute | solution.py:456
  140.6 54.5 %collective-permute-start.44 = (bf16[64,3072]{1,0:T(8,128)(2,1)}, bf16[64,3072]{1,0:T(8,128)(2,1)}, u32[]{:S(2)}, u32[]{:S(2)}) collective-permute-start(bf16[64,3072]{1,0:T(8,128)(2,1)} %collective-permute-done.43), channel_id=1, source_target_pairs={{0,8},{8,16},{16,24},{24,28},{28,20},{20,12},{12,4},{4,0},{1,9},{9... | collective-permute-start | bytes 1179656 | tf_op jit(solution)/shard_map/ppermute | solution.py:455
  144.1 52.6 %collective-permute-start.27 = (bf16[64,3072]{1,0:T(8,128)(2,1)}, bf16[64,3072]{1,0:T(8,128)(2,1)}, u32[]{:S(2)}, u32[]{:S(2)}) collective-permute-start(bf16[64,3072]{1,0:T(8,128)(2,1)} %collective-permute-done.26), channel_id=1, source_target_pairs={{0,8},{8,16},{16,24},{24,28},{28,20},{20,12},{12,4},{4,0},{1,9},{9... | collective-permute-start | bytes 1179656 | tf_op jit(solution)/shard_map/ppermute | solution.py:455
  147.1 51.5 %collective-permute-start.34 = (bf16[64,3072]{1,0:T(8,128)(2,1)}, bf16[64,3072]{1,0:T(8,128)(2,1)}, u32[]{:S(2)}, u32[]{:S(2)}) collective-permute-start(bf16[64,3072]{1,0:T(8,128)(2,1)} %collective-permute-done.33), channel_id=1, source_target_pairs={{8,0},{16,8},{24,16},{28,24},{20,28},{12,20},{4,12},{0,4},{9,1},{1... | collective-permute-start | bytes 1179656 | tf_op jit(solution)/shard_map/ppermute | solution.py:456
  149.1 16.1 %collective-permute-start.6 = (bf16[128,1024]{0,1:T(8,128)(2,1)}, bf16[128,1024]{0,1:T(8,128)(2,1)}, u32[]{:S(2)}, u32[]{:S(2)}) collective-permute-start(bf16[128,1024]{0,1:T(8,128)(2,1)} %collective-permute-done.5), channel_id=1, source_target_pairs={{0,8},{8,16},{16,24},{24,28},{28,20},{20,12},{12,4},{4,0},{1,9},{9... | collective-permute-start | bytes 786440 | tf_op jit(solution)/shard_map/ppermute | solution.py:455
  161.8 39.1 %collective-permute-start.51 = (bf16[64,3072]{1,0:T(8,128)(2,1)}, bf16[64,3072]{1,0:T(8,128)(2,1)}, u32[]{:S(2)}, u32[]{:S(2)}) collective-permute-start(bf16[64,3072]{1,0:T(8,128)(2,1)} %collective-permute-done.50), channel_id=1, source_target_pairs={{8,0},{16,8},{24,16},{28,24},{20,28},{12,20},{4,12},{0,4},{9,1},{1... | collective-permute-start | bytes 1179656 | tf_op jit(solution)/shard_map/ppermute | solution.py:456
  182.3 57.4 %collective-permute-start.10 = (bf16[512,1024]{1,0:T(8,128)(2,1)}, bf16[512,1024]{1,0:T(8,128)(2,1)}, u32[]{:S(2)}, u32[]{:S(2)}) collective-permute-start(bf16[512,1024]{1,0:T(8,128)(2,1)} %dynamic-slice_bitcast_fusion.7), channel_id=1, source_target_pairs={{0,1},{1,0},{2,3},{3,2},{4,5},{5,4},{6,7},{7,6},{8,9},{9,8},{10,11... | collective-permute-start | bytes 3145736 | tf_op jit(solution)/shard_map/ppermute | solution.py:504
  195.2 40.0 %collective-permute-start.20 = (bf16[512,1024]{1,0:T(8,128)(2,1)S(1)}, bf16[512,1024]{1,0:T(8,128)(2,1)S(1)}, u32[]{:S(2)}, u32[]{:S(2)}) collective-permute-start(bf16[512,1024]{1,0:T(8,128)(2,1)S(1)} %dynamic-slice_bitcast_fusion.6), channel_id=1, source_target_pairs={{0,1},{1,0},{2,3},{3,2},{4,5},{5,4},{6,7},{7,6},{8,9},{9,8},{10,11... | collective-permute-start | bytes 3145736 | tf_op jit(solution)/shard_map/ppermute | solution.py:504
  198.6 17.9 %collective-permute-start.28 = (bf16[64,3072]{1,0:T(8,128)(2,1)}, bf16[64,3072]{1,0:T(8,128)(2,1)S(1)}, u32[]{:S(2)}, u32[]{:S(2)}) collective-permute-start(bf16[64,3072]{1,0:T(8,128)(2,1)} %collective-permute-done.27), channel_id=1, source_target_pairs={{0,8},{8,16},{16,24},{24,28},{28,20},{20,12},{12,4},{4,0},{1,9},{9... | collective-permute-start | bytes 1179656 | tf_op jit(solution)/shard_map/ppermute | solution.py:455
  200.9 21.0 %collective-permute-start.35 = (bf16[64,3072]{1,0:T(8,128)(2,1)}, bf16[64,3072]{1,0:T(8,128)(2,1)S(1)}, u32[]{:S(2)}, u32[]{:S(2)}) collective-permute-start(bf16[64,3072]{1,0:T(8,128)(2,1)} %collective-permute-done.34), channel_id=1, source_target_pairs={{8,0},{16,8},{24,16},{28,24},{20,28},{12,20},{4,12},{0,4},{9,1},{1... | collective-permute-start | bytes 1179656 | tf_op jit(solution)/shard_map/ppermute | solution.py:456
  216.5 23.1 %collective-permute-start.46 = (bf16[64,3072]{1,0:T(8,128)(2,1)S(1)}, bf16[64,3072]{1,0:T(8,128)(2,1)S(1)}, u32[]{:S(2)}, u32[]{:S(2)}) collective-permute-start(bf16[64,3072]{1,0:T(8,128)(2,1)S(1)} %collective-permute-done.45), channel_id=1, source_target_pairs={{0,8},{8,16},{16,24},{24,28},{28,20},{20,12},{12,4},{4,0},{1,9},{9... | collective-permute-start | bytes 1179656 | tf_op jit(solution)/shard_map/ppermute | solution.py:455
  235.6 26.2 %collective-permute-start.21 = (bf16[512,1024]{1,0:T(8,128)(2,1)S(1)}, bf16[512,1024]{1,0:T(8,128)(2,1)S(1)}, u32[]{:S(2)}, u32[]{:S(2)}) collective-permute-start(bf16[512,1024]{1,0:T(8,128)(2,1)S(1)} %fusion.6), channel_id=1, source_target_pairs={{0,2},{1,3},{2,0},{3,1},{4,6},{5,7},{6,4},{7,5},{8,10},{9,11},{10,... | collective-permute-start | bytes 3145736 | tf_op jit(solution)/shard_map/ppermute | solution.py:506
  241.4 40.1 %collective-permute-start.11 = (bf16[512,1024]{1,0:T(8,128)(2,1)S(1)}, bf16[512,1024]{1,0:T(8,128)(2,1)S(1)}, u32[]{:S(2)}, u32[]{:S(2)}) collective-permute-start(bf16[512,1024]{1,0:T(8,128)(2,1)S(1)} %fusion.7), channel_id=1, source_target_pairs={{0,2},{1,3},{2,0},{3,1},{4,6},{5,7},{6,4},{7,5},{8,10},{9,11},{10,... | collective-permute-start | bytes 3145736 | tf_op jit(solution)/shard_map/ppermute | solution.py:506
  262.2 19.8 %collective-permute-start.22 = (bf16[512,1024]{1,0:T(8,128)(2,1)S(1)}, bf16[512,1024]{1,0:T(8,128)(2,1)S(1)}, u32[]{:S(2)}, u32[]{:S(2)}) collective-permute-start(bf16[512,1024]{1,0:T(8,128)(2,1)S(1)} %add_convert_fusion.6), channel_id=1, source_target_pairs={{0,1},{1,0},{2,3},{3,2},{4,5},{5,4},{6,7},{7,6},{8,9},{9,8},{10,11... | collective-permute-start | bytes 3145736 | tf_op jit(solution)/shard_map/ppermute | solution.py:508
  281.9 42.8 %collective-permute-start.12 = (bf16[512,1024]{1,0:T(8,128)(2,1)S(1)}, bf16[512,1024]{1,0:T(8,128)(2,1)S(1)}, u32[]{:S(2)}, u32[]{:S(2)}) collective-permute-start(bf16[512,1024]{1,0:T(8,128)(2,1)S(1)} %add_convert_fusion.7), channel_id=1, source_target_pairs={{0,1},{1,0},{2,3},{3,2},{4,5},{5,4},{6,7},{7,6},{8,9},{9,8},{10,11... | collective-permute-start | bytes 3145736 | tf_op jit(solution)/shard_map/ppermute | solution.py:508
  371.1 57.2 %collective-permute-start.54 = (bf16[512,1024]{1,0:T(8,128)(2,1)S(1)}, bf16[512,1024]{1,0:T(8,128)(2,1)}, u32[]{:S(2)}, u32[]{:S(2)}) collective-permute-start(bf16[512,1024]{1,0:T(8,128)(2,1)S(1)} %dynamic-slice_bitcast_fusion.4), channel_id=1, source_target_pairs={{0,1},{1,0},{2,3},{3,2},{4,5},{5,4},{6,7},{7,6},{8,9},{9,8},{10,11... | collective-permute-start | bytes 3145736 | tf_op jit(solution)/shard_map/ppermute | solution.py:504
  371.2 58.8 %collective-permute-start.60 = (bf16[512,1024]{1,0:T(8,128)(2,1)S(1)}, bf16[512,1024]{1,0:T(8,128)(2,1)}, u32[]{:S(2)}, u32[]{:S(2)}) collective-permute-start(bf16[512,1024]{1,0:T(8,128)(2,1)S(1)} %dynamic-slice_bitcast_fusion.2), channel_id=1, source_target_pairs={{0,1},{1,0},{2,3},{3,2},{4,5},{5,4},{6,7},{7,6},{8,9},{9,8},{10,11... | collective-permute-start | bytes 3145736 | tf_op jit(solution)/shard_map/ppermute | solution.py:504
  372.4 16.6 %collective-permute-start.93 = (bf16[64,3072]{1,0:T(8,128)(2,1)S(1)}, bf16[64,3072]{1,0:T(8,128)(2,1)S(1)}, u32[]{:S(2)}, u32[]{:S(2)}) collective-permute-start(bf16[64,3072]{1,0:T(8,128)(2,1)S(1)} %dynamic-slice_bitcast_fusion.10), channel_id=1, source_target_pairs={{8,0},{16,8},{24,16},{28,24},{20,28},{12,20},{4,12},{0,4},{9,1},{1... | collective-permute-start | bytes 1179656 | tf_op jit(solution)/shard_map/ppermute | solution.py:471
  382.9 50.9 %collective-permute-start.37 = (bf16[512,1024]{1,0:T(8,128)(2,1)S(1)}, bf16[512,1024]{1,0:T(8,128)(2,1)S(1)}, u32[]{:S(2)}, u32[]{:S(2)}) collective-permute-start(bf16[512,1024]{1,0:T(8,128)(2,1)S(1)} %dynamic-slice_bitcast_fusion.5), channel_id=1, source_target_pairs={{0,1},{1,0},{2,3},{3,2},{4,5},{5,4},{6,7},{7,6},{8,9},{9,8},{10,11... | collective-permute-start | bytes 3145736 | tf_op jit(solution)/shard_map/ppermute | solution.py:504
  388.9 45.3 %collective-permute-start.57 = (bf16[512,1024]{1,0:T(8,128)(2,1)S(1)}, bf16[512,1024]{1,0:T(8,128)(2,1)S(1)}, u32[]{:S(2)}, u32[]{:S(2)}) collective-permute-start(bf16[512,1024]{1,0:T(8,128)(2,1)S(1)} %dynamic-slice_bitcast_fusion.3), channel_id=1, source_target_pairs={{0,1},{1,0},{2,3},{3,2},{4,5},{5,4},{6,7},{7,6},{8,9},{9,8},{10,11... | collective-permute-start | bytes 3145736 | tf_op jit(solution)/shard_map/ppermute | solution.py:504
  434.2 75.1 %collective-permute-start.55 = (bf16[512,1024]{1,0:T(8,128)(2,1)S(1)}, bf16[512,1024]{1,0:T(8,128)(2,1)S(1)}, u32[]{:S(2)}, u32[]{:S(2)}) collective-permute-start(bf16[512,1024]{1,0:T(8,128)(2,1)S(1)} %fusion.4), channel_id=1, source_target_pairs={{0,2},{1,3},{2,0},{3,1},{4,6},{5,7},{6,4},{7,5},{8,10},{9,11},{10,... | collective-permute-start | bytes 3145736 | tf_op jit(solution)/shard_map/ppermute | solution.py:506
  436.7 75.9 %collective-permute-start.61 = (bf16[512,1024]{1,0:T(8,128)(2,1)S(1)}, bf16[512,1024]{1,0:T(8,128)(2,1)S(1)}, u32[]{:S(2)}, u32[]{:S(2)}) collective-permute-start(bf16[512,1024]{1,0:T(8,128)(2,1)S(1)} %fusion.2), channel_id=1, source_target_pairs={{0,2},{1,3},{2,0},{3,1},{4,6},{5,7},{6,4},{7,5},{8,10},{9,11},{10,... | collective-permute-start | bytes 3145736 | tf_op jit(solution)/shard_map/ppermute | solution.py:506
  437.4 75.8 %collective-permute-start.38 = (bf16[512,1024]{1,0:T(8,128)(2,1)S(1)}, bf16[512,1024]{1,0:T(8,128)(2,1)S(1)}, u32[]{:S(2)}, u32[]{:S(2)}) collective-permute-start(bf16[512,1024]{1,0:T(8,128)(2,1)S(1)} %fusion.5), channel_id=1, source_target_pairs={{0,2},{1,3},{2,0},{3,1},{4,6},{5,7},{6,4},{7,5},{8,10},{9,11},{10,... | collective-permute-start | bytes 3145736 | tf_op jit(solution)/shard_map/ppermute | solution.py:506
  439.8 78.6 %collective-permute-start.58 = (bf16[512,1024]{1,0:T(8,128)(2,1)S(1)}, bf16[512,1024]{1,0:T(8,128)(2,1)S(1)}, u32[]{:S(2)}, u32[]{:S(2)}) collective-permute-start(bf16[512,1024]{1,0:T(8,128)(2,1)S(1)} %fusion.3), channel_id=1, source_target_pairs={{0,2},{1,3},{2,0},{3,1},{4,6},{5,7},{6,4},{7,5},{8,10},{9,11},{10,... | collective-permute-start | bytes 3145736 | tf_op jit(solution)/shard_map/ppermute | solution.py:506
  518.5 144.9 %collective-permute-start.56 = (bf16[512,1024]{1,0:T(8,128)(2,1)}, bf16[512,1024]{1,0:T(8,128)(2,1)}, u32[]{:S(2)}, u32[]{:S(2)}) collective-permute-start(bf16[512,1024]{1,0:T(8,128)(2,1)} %add_convert_fusion.4), channel_id=1, source_target_pairs={{0,1},{1,0},{2,3},{3,2},{4,5},{5,4},{6,7},{7,6},{8,9},{9,8},{10,11... | collective-permute-start | bytes 3145736 | tf_op jit(solution)/shard_map/ppermute | solution.py:508
  518.9 33.5 %collective-permute-start.62 = (bf16[512,1024]{1,0:T(8,128)(2,1)S(1)}, bf16[512,1024]{1,0:T(8,128)(2,1)S(1)}, u32[]{:S(2)}, u32[]{:S(2)}) collective-permute-start(bf16[512,1024]{1,0:T(8,128)(2,1)S(1)} %add_convert_fusion.2), channel_id=1, source_target_pairs={{0,1},{1,0},{2,3},{3,2},{4,5},{5,4},{6,7},{7,6},{8,9},{9,8},{10,11... | collective-permute-start | bytes 3145736 | tf_op jit(solution)/shard_map/ppermute | solution.py:508
  519.6 41.5 %collective-permute-start.59 = (bf16[512,1024]{1,0:T(8,128)(2,1)S(1)}, bf16[512,1024]{1,0:T(8,128)(2,1)}, u32[]{:S(2)}, u32[]{:S(2)}) collective-permute-start(bf16[512,1024]{1,0:T(8,128)(2,1)S(1)} %add_convert_fusion.3), channel_id=1, source_target_pairs={{0,1},{1,0},{2,3},{3,2},{4,5},{5,4},{6,7},{7,6},{8,9},{9,8},{10,11... | collective-permute-start | bytes 3145736 | tf_op jit(solution)/shard_map/ppermute | solution.py:508
  521.7 19.9 %collective-permute-start.106 = (bf16[64,3072]{1,0:T(8,128)(2,1)S(1)}, bf16[64,3072]{1,0:T(8,128)(2,1)S(1)}, u32[]{:S(2)}, u32[]{:S(2)}) collective-permute-start(bf16[64,3072]{1,0:T(8,128)(2,1)S(1)} %fusion.17), channel_id=1, source_target_pairs={{0,8},{8,16},{16,24},{24,28},{28,20},{20,12},{12,4},{4,0},{1,9},{9... | collective-permute-start | bytes 1179656 | tf_op jit(solution)/shard_map/ppermute | solution.py:470
  607.4 18.9 %collective-permute-start.79 = (bf16[128,1024]{0,1:T(8,128)(2,1)}, bf16[128,1024]{0,1:T(8,128)(2,1)}, u32[]{:S(2)}, u32[]{:S(2)}) collective-permute-start(bf16[128,1024]{0,1:T(8,128)(2,1)} %bitcast.348), channel_id=1, source_target_pairs={{8,0},{16,8},{24,16},{28,24},{20,28},{12,20},{4,12},{0,4},{9,1},{1... | collective-permute-start | bytes 786440 | tf_op jit(solution)/shard_map/ppermute | solution.py:471
  637.8 16.4 %collective-permute-start.63 = (bf16[512,1024]{1,0:T(8,128)(2,1)}, bf16[512,1024]{1,0:T(8,128)(2,1)}, u32[]{:S(2)}, u32[]{:S(2)}) collective-permute-start(bf16[512,1024]{1,0:T(8,128)(2,1)} %dynamic-slice_bitcast_fusion.1), channel_id=1, source_target_pairs={{0,1},{1,0},{2,3},{3,2},{4,5},{5,4},{6,7},{7,6},{8,9},{9,8},{10,11... | collective-permute-start | bytes 3145736 | tf_op jit(solution)/shard_map/ppermute | solution.py:504
  637.8 20.0 %collective-permute-start.66 = (bf16[512,1024]{1,0:T(8,128)(2,1)}, bf16[512,1024]{1,0:T(8,128)(2,1)}, u32[]{:S(2)}, u32[]{:S(2)}) collective-permute-start(bf16[512,1024]{1,0:T(8,128)(2,1)} %dynamic-slice_bitcast_fusion), channel_id=1, source_target_pairs={{0,1},{1,0},{2,3},{3,2},{4,5},{5,4},{6,7},{7,6},{8,9},{9,8},{10,11... | collective-permute-start | bytes 3145736 | tf_op jit(solution)/shard_map/ppermute | solution.py:504
  649.2 57.8 %collective-permute-start.39 = (bf16[512,1024]{1,0:T(8,128)(2,1)S(1)}, bf16[512,1024]{1,0:T(8,128)(2,1)}, u32[]{:S(2)}, u32[]{:S(2)}) collective-permute-start(bf16[512,1024]{1,0:T(8,128)(2,1)S(1)} %copy-done.7), channel_id=1, source_target_pairs={{0,1},{1,0},{2,3},{3,2},{4,5},{5,4},{6,7},{7,6},{8,9},{9,8},{10,11... | collective-permute-start | bytes 3145736 | tf_op jit(solution)/shard_map/ppermute | solution.py:508
  654.2 15.5 %collective-permute-start.75 = (bf16[128,1024]{0,1:T(8,128)(2,1)}, bf16[128,1024]{0,1:T(8,128)(2,1)S(1)}, u32[]{:S(2)}, u32[]{:S(2)}) collective-permute-start(bf16[128,1024]{0,1:T(8,128)(2,1)} %fusion.46), channel_id=1, source_target_pairs={{0,8},{8,16},{16,24},{24,28},{28,20},{20,12},{12,4},{4,0},{1,9},{9... | collective-permute-start | bytes 786440 | tf_op jit(solution)/shard_map/ppermute | solution.py:470
  657.9 26.3 %collective-permute-start.64 = (bf16[512,1024]{1,0:T(8,128)(2,1)S(1)}, bf16[512,1024]{1,0:T(8,128)(2,1)}, u32[]{:S(2)}, u32[]{:S(2)}) collective-permute-start(bf16[512,1024]{1,0:T(8,128)(2,1)S(1)} %fusion.1), channel_id=1, source_target_pairs={{0,2},{1,3},{2,0},{3,1},{4,6},{5,7},{6,4},{7,5},{8,10},{9,11},{10,... | collective-permute-start | bytes 3145736 | tf_op jit(solution)/shard_map/ppermute | solution.py:506
  661.5 42.3 %collective-permute-start.67 = (bf16[512,1024]{1,0:T(8,128)(2,1)}, bf16[512,1024]{1,0:T(8,128)(2,1)}, u32[]{:S(2)}, u32[]{:S(2)}) collective-permute-start(bf16[512,1024]{1,0:T(8,128)(2,1)} %fusion), channel_id=1, source_target_pairs={{0,2},{1,3},{2,0},{3,1},{4,6},{5,7},{6,4},{7,5},{8,10},{9,11},{10,... | collective-permute-start | bytes 3145736 | tf_op jit(solution)/shard_map/ppermute | solution.py:506
  669.7 36.1 %collective-permute-start.76 = (bf16[128,1024]{0,1:T(8,128)(2,1)S(1)}, bf16[128,1024]{0,1:T(8,128)(2,1)S(1)}, u32[]{:S(2)}, u32[]{:S(2)}) collective-permute-start(bf16[128,1024]{0,1:T(8,128)(2,1)S(1)} %fusion.45), channel_id=1, source_target_pairs={{0,8},{8,16},{16,24},{24,28},{28,20},{20,12},{12,4},{4,0},{1,9},{9... | collective-permute-start | bytes 786440 | tf_op jit(solution)/shard_map/ppermute | solution.py:470
  673.2 48.4 %collective-permute-start.84 = (bf16[128,1024]{0,1:T(8,128)(2,1)}, bf16[128,1024]{0,1:T(8,128)(2,1)}, u32[]{:S(2)}, u32[]{:S(2)}) collective-permute-start(bf16[128,1024]{0,1:T(8,128)(2,1)} %fusion.37), channel_id=1, source_target_pairs={{8,0},{16,8},{24,16},{28,24},{20,28},{12,20},{4,12},{0,4},{9,1},{1... | collective-permute-start | bytes 786440 | tf_op jit(solution)/shard_map/ppermute | solution.py:471
  685.8 40.0 %collective-permute-start.65 = (bf16[512,1024]{1,0:T(8,128)(2,1)S(1)}, bf16[512,1024]{1,0:T(8,128)(2,1)}, u32[]{:S(2)}, u32[]{:S(2)}) collective-permute-start(bf16[512,1024]{1,0:T(8,128)(2,1)S(1)} %add_convert_fusion.1), channel_id=1, source_target_pairs={{0,1},{1,0},{2,3},{3,2},{4,5},{5,4},{6,7},{7,6},{8,9},{9,8},{10,11... | collective-permute-start | bytes 3145736 | tf_op jit(solution)/shard_map/ppermute | solution.py:508
  705.8 24.1 %collective-permute-start.68 = (bf16[512,1024]{1,0:T(8,128)(2,1)S(1)}, bf16[512,1024]{1,0:T(8,128)(2,1)}, u32[]{:S(2)}, u32[]{:S(2)}) collective-permute-start(bf16[512,1024]{1,0:T(8,128)(2,1)S(1)} %add_convert_fusion), channel_id=1, source_target_pairs={{0,1},{1,0},{2,3},{3,2},{4,5},{5,4},{6,7},{7,6},{8,9},{9,8},{10,11... | collective-permute-start | bytes 3145736 | tf_op jit(solution)/shard_map/ppermute | solution.py:508
  706.7 17.7 %collective-permute-start.77 = (bf16[128,1024]{0,1:T(8,128)(2,1)}, bf16[128,1024]{0,1:T(8,128)(2,1)}, u32[]{:S(2)}, u32[]{:S(2)}) collective-permute-start(bf16[128,1024]{0,1:T(8,128)(2,1)} %fusion.44), channel_id=1, source_target_pairs={{0,8},{8,16},{16,24},{24,28},{28,20},{20,12},{12,4},{4,0},{1,9},{9... | collective-permute-start | bytes 786440 | tf_op jit(solution)/shard_map/ppermute | solution.py:470
  722.6 22.6 %collective-permute-start.85 = (bf16[128,1024]{0,1:T(8,128)(2,1)S(1)}, bf16[128,1024]{0,1:T(8,128)(2,1)S(1)}, u32[]{:S(2)}, u32[]{:S(2)}) collective-permute-start(bf16[128,1024]{0,1:T(8,128)(2,1)S(1)} %fusion.36), channel_id=1, source_target_pairs={{8,0},{16,8},{24,16},{28,24},{20,28},{12,20},{4,12},{0,4},{9,1},{1... | collective-permute-start | bytes 786440 | tf_op jit(solution)/shard_map/ppermute | solution.py:471
  725.4 23.9 %collective-permute-start.78 = (bf16[128,1024]{0,1:T(8,128)(2,1)S(1)}, bf16[128,1024]{0,1:T(8,128)(2,1)S(1)}, u32[]{:S(2)}, u32[]{:S(2)}) collective-permute-start(bf16[128,1024]{0,1:T(8,128)(2,1)S(1)} %fusion.43), channel_id=1, source_target_pairs={{0,8},{8,16},{16,24},{24,28},{28,20},{20,12},{12,4},{4,0},{1,9},{9... | collective-permute-start | bytes 786440 | tf_op jit(solution)/shard_map/ppermute | solution.py:470
  (84 other events, 735.9 us)

commit v2 on v1

v2 whole, which is shorter than its diff:
```python
import functools

import jax
import jax.numpy as jnp
from jax import lax
from jax.experimental import pallas as pl
from jax.experimental.pallas import tpu as pltpu
from jax.sharding import PartitionSpec as P

HDIM = 64
EPS = 1e-05
NEG = -1e30
BF = jnp.bfloat16
F32 = jnp.float32
NN = (((1,), (0,)), ((), ()))
NT = (((1,), (1,)), ((), ()))
TN = (((0,), (0,)), ((), ()))
MIB = 1024 * 1024
SUB = 128
PAIR = 2 * HDIM
ROWS = 256
HBM = pl.BlockSpec(memory_space=pl.ANY)


def mm(left, right, dims=NN):
    return lax.dot_general(left, right, dims, preferred_element_type=F32)


def kernel_call(body, grid, ins, in_specs, outs, out_specs, flops, scratch=(), scalars=None, alias=None):
    moved = sum(a.size * a.dtype.itemsize for a in ins) + sum(
        o.size * jnp.dtype(o.dtype).itemsize for o in outs
    )
    spec = pltpu.PrefetchScalarGridSpec(
        num_scalar_prefetch=0 if scalars is None else 1,
        grid=grid,
        in_specs=in_specs,
        out_specs=out_specs,
        scratch_shapes=scratch,
    )
    args = ins if scalars is None else (scalars, *ins)
    return pl.pallas_call(
        body,
        grid_spec=spec,
        out_shape=outs,
        input_output_aliases=alias or {},
        compiler_params=pltpu.CompilerParams(vmem_limit_bytes=56 * MIB),
        cost_estimate=pl.CostEstimate(flops=flops, bytes_accessed=moved, transcendentals=0),
    )(*args)


def whole(shape):
    return pl.BlockSpec(shape, lambda *i: (0,) * len(shape))


def rows_of(rows, width, start=0):
    return pl.BlockSpec((rows, width), lambda i, *_: (i + start, 0))


def out_of(shape, kind=BF):
    return jax.ShapeDtypeStruct(shape, kind)


def prepare_body(_, x_ref, cot_ref, mask_ref, x0, x1, g0, g1):
    def split(block):
        frames, steps, width = block.shape
        parts = block.reshape(frames, 2, steps // 2, width)
        return [parts[:, c].reshape(frames * steps // 2, width) for c in range(2)]

    for ref, part in zip((x0, x1), split(x_ref[...].astype(F32))):
        ref[...] = part.astype(BF)
    grad = cot_ref[...].astype(F32) * mask_ref[...]
    for ref, part in zip((g0, g1), split(grad)):
        ref[...] = part.astype(BF)


def prepare(x, cot, mask, places, blocks):
    frames, steps, width = x.shape
    cut = width // blocks
    half = frames // 2
    cube = pl.BlockSpec((half, steps, cut), lambda i, t, p: ((i + p[blocks]) % 2, 0, p[t]))
    flat = pl.BlockSpec((half * steps // 2, cut), lambda i, t, p: (i, t))
    mask_spec = pl.BlockSpec((half, 1, 1), lambda i, t, p: ((i + p[blocks]) % 2, 0, 0))
    return kernel_call(
        prepare_body,
        (2, blocks),
        (x, cot, mask),
        [cube, cube, mask_spec],
        [out_of((frames * steps // 2, width))] * 4,
        [flat] * 4,
        0,
        scalars=places,
    )


def pack_attn_body(wq, wk, wv, wo, first, second):
    hw = wq.shape[2]
    for c, ref in enumerate((first, second)):
        for t, w in enumerate((wq, wk, wv)):
            ref[:, t * hw : (t + 1) * hw] = w[c]
        ref[:, 3 * hw :] = wo[c].T


def pack_attn(wq, wk, wv, wo):
    own, hw = wq.shape[1:]
    piece = (own, 4 * hw)
    return kernel_call(
        pack_attn_body,
        (1,),
        (wq, wk, wv, wo),
        [whole(w.shape) for w in (wq, wk, wv, wo)],
        [out_of(piece)] * 2,
        [whole(piece)] * 2,
        0,
    )


def pack_ffn_body(wg, wu, wd, after, first, second):
    units = wg.shape[2]
    half = wg.shape[1] // 2
    for k, ref in enumerate((first, second)):
        rows = slice(k * half, (k + 1) * half)
        ref[:, :units] = wg[0, rows]
        ref[:, units : 2 * units] = wu[0, rows]
    turned = wd[0].T
    first[:, 2 * units :] = turned[:half]
    second[:, 2 * units :] = turned[half:]


def pack_ffn(wg, wu, wd, c, after):
    own, units = wg.shape[1:]
    piece = (own // 2, 3 * units)
    into = pl.BlockSpec((1, own, units), lambda i: (c, 0, 0))
    back = pl.BlockSpec((1, units, own), lambda i: (c, 0, 0))
    return kernel_call(
        pack_ffn_body,
        (1,),
        (wg, wu, wd, after),
        [into, into, back, HBM],
        [out_of(piece)] * 2,
        [whole(piece)] * 2,
        0,
    )


def norm(value):
    scale = lax.rsqrt(jnp.mean(value * value, axis=-1, keepdims=True) + EPS)
    return value * scale, scale


def lanes_low(shape):
    return lax.broadcasted_iota(jnp.int32, shape, 1) < HDIM


def stack_heads(pair):
    low = lanes_low(pair.shape)
    zero = jnp.zeros_like(pair)
    return jnp.concatenate([jnp.where(low, pair, zero), jnp.where(low, zero, pair)], axis=0)


def pick_heads(stacked):
    half = stacked.shape[0] // 2
    low = lanes_low((half, stacked.shape[1]))
    return jnp.where(low, stacked[:half], stacked[half:])


def visible(rows, keys, steps):
    row = lax.broadcasted_iota(jnp.int32, (rows, keys), 0) % SUB
    key = lax.broadcasted_iota(jnp.int32, (rows, keys), 1)
    same = row // steps == (key % SUB) // steps
    if keys == SUB:
        return same & (row >= key)
    return same & ((key < SUB) | (row >= key - SUB))


def softmax(query, keys, steps):
    raw = mm(query, keys, NT) * HDIM ** (-0.5)
    masked = jnp.where(visible(raw.shape[0], raw.shape[1], steps), raw, NEG)
    top = jnp.max(masked, axis=-1, keepdims=True)
    power = jnp.exp(masked - top)
    return power / jnp.sum(power, axis=-1, keepdims=True)


class Pieces:
    def __init__(self, arrays, groups):
        self.arrays = arrays
        self.count = len(arrays)
        self.groups = groups
        self.shape = (sum(a.shape[0] for a in arrays), arrays[0].shape[1])
        self.scratch = [pltpu.VMEM(self.shape, BF), pltpu.SemaphoreType.DMA((groups, self.count))]

    def copies(self, refs, memory, sems, group):
        row = 0
        wide = self.shape[1] // self.groups
        for k, ref in enumerate(refs):
            cols = pl.ds(group * wide, wide)
            rows = pl.ds(row, ref.shape[0])
            yield pltpu.make_async_copy(ref.at[:, cols], memory.at[rows, cols], sems.at[group, k])
            row += ref.shape[0]

    def start(self, refs, memory, sems, order):
        @pl.when(pl.program_id(0) == 0)
        def _():
            for group in order:
                for copy in self.copies(refs, memory, sems, group):
                    copy.start()

    def wait(self, refs, memory, sems, group):
        @pl.when(pl.program_id(0) == 0)
        def _():
            for copy in self.copies(refs, memory, sems, group):
                copy.wait()


def attend_body(pieces, steps, hw, later, *refs):
    x_ref, gain_ref, *refs = refs
    if later:
        before_ref, *refs = refs
    w_refs, refs = refs[: pieces.count], refs[pieces.count :]
    h_ref, qkv_ref, mixed_ref, part_ref, w_ref, sems = refs
    pieces.start(w_refs, w_ref, sems, range(1))
    normed, _ = norm(x_ref[...].astype(F32))
    hidden = (normed * gain_ref[...]).astype(BF)
    h_ref[...] = hidden
    pieces.wait(w_refs, w_ref, sems, 0)
    qkv = mm(hidden, w_ref[:, : 3 * hw]).astype(BF)
    qkv_ref[...] = qkv
    for s in range(x_ref.shape[0] // SUB):
        rows = slice(s * SUB, (s + 1) * SUB)
        for j in range(hw // PAIR):
            q, k, v = (qkv[rows, t * hw + j * PAIR : t * hw + (j + 1) * PAIR] for t in range(3))
            if later:
                k_old, v_old = (
                    before_ref[rows, t * hw + j * PAIR : t * hw + (j + 1) * PAIR] for t in (1, 2)
                )
                k = jnp.concatenate([k_old, k], axis=0)
                v = jnp.concatenate([v_old, v], axis=0)
            probs = softmax(stack_heads(q), k, steps).astype(BF)
            mixed_ref[rows, j * PAIR : (j + 1) * PAIR] = pick_heads(mm(probs, v)).astype(BF)
    part_ref[...] = mm(mixed_ref[...], w_ref[:, 3 * hw :], NT).astype(BF)


def attend(x, gain, before, w, half, steps):
    tokens, width = x.shape[0] // 2, x.shape[1]
    pieces = Pieces(w, 1)
    hw = pieces.shape[1] // 4
    count = tokens // ROWS
    ins = [x, gain]
    specs = [rows_of(ROWS, width, half * count), whole(gain.shape)]
    if before is not None:
        ins.append(before)
        specs.append(rows_of(ROWS, 3 * hw))
    widths = (width, 3 * hw, hw, width)
    return kernel_call(
        functools.partial(attend_body, pieces, steps, hw, before is not None),
        (count,),
        [*ins, *w],
        [*specs, *[HBM] * pieces.count],
        [out_of((tokens, n)) for n in widths],
        [rows_of(ROWS, n) for n in widths],
        2 * tokens * width * 4 * hw,
        pieces.scratch,
    )


def units_body(pieces, units, *refs):
    x_ref, att_ref, g_ref, gain_ref, *refs = refs
    w_refs, refs = refs[: pieces.count], refs[pieces.count :]
    h_ref, inner_ref, dgate_ref, dup_ref, dh_ref, mlp_ref, w_ref, sems = refs
    pieces.start(w_refs, w_ref, sems, (2, 0, 1))
    normed, _ = norm(x_ref[...].astype(F32) + att_ref[...].astype(F32))
    hidden = (normed * gain_ref[...]).astype(BF)
    h_ref[...] = hidden
    for group in (2, 0, 1):
        pieces.wait(w_refs, w_ref, sems, group)
    cut = 256
    for u in range(units // cut):
        cols = [slice(t * units + u * cut, t * units + (u + 1) * cut) for t in range(3)]
        d_inner = mm(g_ref[...], w_ref[:, cols[2]])
        gate = mm(hidden, w_ref[:, cols[0]])
        up = mm(hidden, w_ref[:, cols[1]])
        sigma = 1.0 / (1.0 + jnp.exp(-gate))
        active = gate * sigma
        inner_ref[:, cols[0]] = (active * up).astype(BF)
        dup_ref[:, cols[0]] = (d_inner * active).astype(BF)
        dgate_ref[:, cols[0]] = (d_inner * up * sigma * (1.0 + gate * (1.0 - sigma))).astype(BF)
    grad = mm(dgate_ref[...], w_ref[:, :units], NT) + mm(dup_ref[...], w_ref[:, units : 2 * units], NT)
    dh_ref[...] = grad.astype(BF)
    mlp_ref[...] = mm(inner_ref[...], w_ref[:, 2 * units :], NT).astype(BF)


def hidden_units(x, att, g, gain, w, half):
    tokens, width = att.shape
    pieces = Pieces(w, 3)
    units = pieces.shape[1] // 3
    count = tokens // ROWS
    part = rows_of(ROWS, width, half * count)
    widths = (width, units, units, units, width, width)
    return kernel_call(
        functools.partial(units_body, pieces, units),
        (count,),
        (x, att, g, gain, *w),
        [part, rows_of(ROWS, width), part, whole(gain.shape), *[HBM] * pieces.count],
        [out_of((tokens, n)) for n in widths],
        [rows_of(ROWS, n) for n in widths],
        12 * tokens * width * units,
        pieces.scratch,
    )


def tn_pair(left, right):
    return mm(left[0][...], right[0][...], TN) + mm(left[1][...], right[1][...], TN)


def store_rows(refs, block, rows, cols, value):
    start = 0
    for ref in refs:
        low, high = max(start, block * rows), min(start + ref.shape[0], (block + 1) * rows)
        if low < high:
            ref[low - start : high - start, cols] = value[low - block * rows : high - block * rows]
        start += ref.shape[0]


def grads_body(columns, count, *refs):
    inputs = max(max(r) for _, r in columns) + 1
    outs = refs[inputs:]
    values = [
        tn_pair([refs[k] for k in left], [refs[k] for k in right]).astype(BF) for left, right in columns
    ]
    for block in range(count):

        @pl.when(pl.program_id(0) == block)
        def _():
            at = 0
            for value in values:
                store_rows(outs, block, ROWS, slice(at, at + value.shape[1]), value)
                at += value.shape[1]


def weight_grads(columns, heights):
    ins, specs, places = [], [], []
    for left, right in columns:
        at = []
        for array, start in left:
            ins.append(array)
            rows = array.shape[0] if start is None else array.shape[0] // 2
            specs.append(pl.BlockSpec((rows, ROWS), lambda i, s=start or 0: (s, i)))
            at.append(len(ins) - 1)
        places.append(tuple(at))
    pairs = []
    for (left, right), at in zip(columns, places):
        spot = []
        for array in right:
            ins.append(array)
            specs.append(whole(array.shape))
            spot.append(len(ins) - 1)
        pairs.append((at, tuple(spot)))
    total = sum(right[0].shape[1] for _, right in columns)
    tokens = sum(a.shape[0] for a in columns[0][1])
    width = sum(heights)
    return kernel_call(
        functools.partial(grads_body, pairs, width // ROWS),
        (width // ROWS,),
        ins,
        specs,
        [out_of((n, total)) for n in heights],
        [whole((n, total)) for n in heights],
        2 * tokens * width * total,
    )


def norm_back(grad_hidden, value, gain):
    normed, scale = norm(value)
    scaled = grad_hidden * gain
    back = scale * (scaled - normed * jnp.mean(scaled * normed, axis=-1, keepdims=True))
    return back, jnp.sum(grad_hidden * normed, axis=0, keepdims=True)


def add_up(ref, value):
    @pl.when(pl.program_id(0) == 0)
    def _():
        ref[...] = jnp.zeros_like(ref)

    ref[...] += value


def middle_body(x_ref, att_ref, g_ref, dh_ref, gain_ref, dm_ref, dgain_ref):
    value = x_ref[...].astype(F32) + att_ref[...].astype(F32)
    back, d_gain = norm_back(dh_ref[...].astype(F32), value, gain_ref[...])
    dm_ref[...] = (g_ref[...].astype(F32) + back).astype(BF)
    add_up(dgain_ref, d_gain)


def middle_back(x, att, g, dh, gain, half):
    tokens, width = att.shape
    count = tokens // ROWS
    part, flat = rows_of(ROWS, width, half * count), rows_of(ROWS, width)
    return kernel_call(
        middle_body,
        (count,),
        (x, att, g, dh, gain),
        [part, flat, part, flat, whole(gain.shape)],
        [out_of((tokens, width)), out_of((1, width), F32)],
        [flat, whole((1, width))],
        0,
    )


def attend_back_body(pieces, steps, hw, x0, x1, dm0, dm1, qkv0, qkv1, *refs):
    n = pieces[0].count
    sides = (refs[:n], refs[n : 2 * n])
    dqkv0, dqkv1, dh0, dh1, dgain, w0, sems0, w1, sems1 = refs[2 * n :]
    for p, s, w, sems in zip(pieces, sides, (w0, w1), (sems0, sems1)):
        p.start(s, w, sems, range(1))
    normed = [norm(x[...].astype(F32))[0] for x in (x0, x1)]
    for p, s, w, sems in zip(pieces, sides, (w0, w1), (sems0, sems1)):
        p.wait(s, w, sems, 0)
    scale = HDIM ** (-0.5)
    d_mixed = [mm(d[...], w[:, 3 * hw :]).astype(BF) for d, w in ((dm0, w0), (dm1, w1))]
    for s in range(dm0.shape[0] // SUB):
        rows = slice(s * SUB, (s + 1) * SUB)
        for j in range(hw // PAIR):
            cols = [slice(t * hw + j * PAIR, t * hw + (j + 1) * PAIR) for t in range(3)]
            q0, k0, v0 = (qkv0[rows, c] for c in cols)
            q1, k1, v1 = (qkv1[rows, c] for c in cols)
            keys = (k0, jnp.concatenate([k0, k1], axis=0))
            values = (v0, jnp.concatenate([v0, v1], axis=0))
            d_k, d_v = [], []
            for c, (q, out_ref) in enumerate(((q0, dqkv0), (q1, dqkv1))):
                q_two = stack_heads(q)
                d_two = stack_heads(d_mixed[c][rows, cols[0]])
                soft = softmax(q_two, keys[c], steps)
                d_probs = mm(d_two, values[c], NT)
                inside = jnp.sum(soft * d_probs, axis=-1, keepdims=True)
                d_scores = (soft * (d_probs - inside)).astype(BF)
                d_q = pick_heads(mm(d_scores, keys[c])) * scale
                out_ref[rows, cols[0]] = d_q.astype(BF)
                d_k.append(mm(d_scores, q_two, TN) * scale)
                d_v.append(mm(soft.astype(BF), d_two, TN))
            dqkv0[rows, cols[1]] = (d_k[0] + d_k[1][:SUB]).astype(BF)
            dqkv1[rows, cols[1]] = d_k[1][SUB:].astype(BF)
            dqkv0[rows, cols[2]] = (d_v[0] + d_v[1][:SUB]).astype(BF)
            dqkv1[rows, cols[2]] = d_v[1][SUB:].astype(BF)
    gains = []
    for c, (d, w, out_ref) in enumerate(((dqkv0, w0, dh0), (dqkv1, w1, dh1))):
        grad = mm(d[...], w[:, : 3 * hw], NT)
        out_ref[...] = grad.astype(BF)
        gains.append(jnp.sum(grad * normed[c], axis=0, keepdims=True))
    add_up(dgain, jnp.concatenate(gains, axis=0))


def attend_back(x, dm, qkv, w, half, steps):
    tokens, width = dm[0].shape
    count = tokens // ROWS
    pieces = [Pieces(side, 1) for side in w]
    hw = pieces[0].shape[1] // 4
    part, flat, thin = rows_of(ROWS, width, half * count), rows_of(ROWS, width), rows_of(ROWS, 3 * hw)
    return kernel_call(
        functools.partial(attend_back_body, pieces, steps, hw),
        (count,),
        (*x, *dm, *qkv, *w[0], *w[1]),
        [part] * 2 + [flat] * 2 + [thin] * 2 + [HBM] * (2 * pieces[0].count),
        [out_of((tokens, 3 * hw))] * 2 + [out_of((tokens, width))] * 2 + [out_of((2, width), F32)],
        [thin] * 2 + [flat] * 2 + [whole((2, width))],
        4 * tokens * width * 4 * hw,
        pieces[0].scratch + pieces[1].scratch,
    )


def store_frames(out_ref, sums, places, blocks):
    frames, _, width = out_ref.shape
    cut = width // blocks
    both = [p.reshape(frames, 1, p.shape[0] // frames, width) for p in sums]
    joined = jnp.concatenate(both, axis=1).reshape(frames, -1, width).astype(BF)
    if blocks == 1:
        out_ref[...] = joined
        return
    for t in range(blocks):
        at = pl.multiple_of(places[t] * cut, cut)
        out_ref[:, :, pl.ds(at, cut)] = joined[:, :, t * cut : (t + 1) * cut]


def output_body(blocks, places, x0, x1, a0, a1, m0, m1, *refs):
    sums = [
        x[...].astype(F32) + a[...].astype(F32) + m[...].astype(F32)
        for x, a, m in ((x0, a0, m0), (x1, a1, m1))
    ]
    store_frames(refs[-1], sums, places, blocks)


def input_body(blocks, places, x0, x1, dm0, dm1, dh0, dh1, gain_ref, *refs):
    sums = []
    for c, (x, dm, dh) in enumerate(((x0, dm0, dh0), (x1, dm1, dh1))):
        back, _ = norm_back(dh[...].astype(F32), x[...].astype(F32), gain_ref[c : c + 1])
        sums.append(dm[...].astype(F32) + back)
    store_frames(refs[-1], sums, places, blocks)


def join_frames(body, x, sides, extra, before, half, places, blocks, shape):
    frames, steps, width = shape
    block = 16
    count = frames // 2 // block
    rows = block * steps // 2
    ins = [*x, *sides, *extra]
    specs = [rows_of(rows, width, half * count)] * 2 + [rows_of(rows, width)] * len(sides)
    specs += [whole(e.shape) for e in extra]
    alias = {}
    if before is not None:
        ins.append(before)
        specs.append(HBM)
        alias = {len(ins): 0}
    cube = pl.BlockSpec((block, steps, width), lambda i, p: (i + (half + p[blocks]) % 2 * count, 0, 0))
    return kernel_call(
        functools.partial(body, blocks),
        (count,),
        ins,
        specs,
        [out_of(shape)],
        [cube],
        0,
        scalars=places,
        alias=alias,
    )[0]


def finish_ffn_body(units, *refs):
    ins, (gate, up, down) = refs[:8], refs[8:]
    for c in range(2):
        for k in range(2):
            got, own = ins[4 * c + 2 * k : 4 * c + 2 * k + 2]
            half = got.shape[0]
            total = got[...].astype(F32) + own[...].astype(F32)
            rows = slice(k * half, (k + 1) * half)
            gate[c, rows] = total[:, :units]
            up[c, rows] = total[:, units : 2 * units]
        both = [
            (ins[4 * c + 2 * k][:, 2 * units :].astype(F32) + ins[4 * c + 2 * k + 1][:, 2 * units :].astype(F32))
            for k in range(2)
        ]
        down[c] = jnp.concatenate(both, axis=0).T


def finish_ffn(parts):
    half, total = parts[0].shape
    units = total // 3
    into, back = (2, 2 * half, units), (2, units, 2 * half)
    shapes = (into, into, back)
    return kernel_call(
        functools.partial(finish_ffn_body, units),
        (1,),
        parts,
        [whole(p.shape) for p in parts],
        [out_of(s, F32) for s in shapes],
        [whole(s) for s in shapes],
        0,
    )


def finish_attn_body(hw, *refs):
    ins, outs = refs[:4], refs[4:]
    for c in range(2):
        total = ins[2 * c][...].astype(F32) + ins[2 * c + 1][...].astype(F32)
        for t in range(3):
            outs[t][c] = total[:, t * hw : (t + 1) * hw]
        outs[3][c] = total[:, 3 * hw :].T


def finish_attn(parts):
    own, total = parts[0].shape
    hw = total // 4
    into, back = (2, own, hw), (2, hw, own)
    shapes = (into, into, into, back)
    return kernel_call(
        functools.partial(finish_attn_body, hw),
        (1,),
        parts,
        [whole(p.shape) for p in parts],
        [out_of(s, F32) for s in shapes],
        [whole(s) for s in shapes],
        0,
    )


class Ring:
    def __init__(self, size):
        self.size = size
        self.rings = size <= 16
        half = size // 2
        order = [2 * q for q in range(half)] + [2 * (size - 1 - q) + 1 for q in range(half, size)]
        self.ahead = [(order[q], order[(q + 1) % size]) for q in range(size)]
        self.behind = [(b, a) for a, b in self.ahead]
        self.me = lax.axis_index("dp")
        place = jnp.where(self.me % 2 == 0, self.me // 2, size - 1 - self.me // 2)
        q = lax.rem(place + jnp.arange(size, dtype=jnp.int32), size)
        self.order = jnp.where(q < half, 2 * q, 2 * (size - 1 - q) + 1).astype(jnp.int32)

    def gather(self, first, second):
        n = self.size
        if not self.rings:
            return [lax.all_gather(first, "dp")], [lax.all_gather(second, "dp")]
        a, b = [first], [second]
        for _ in range(1, n):
            a.append(lax.ppermute(a[-1], "dp", self.ahead))
            b.append(lax.ppermute(b[-1], "dp", self.behind))
        return [a[-t % n] for t in range(n)], b

    def scatter(self, first, second):
        n = self.size
        a, b = first[n - 1], second[1]
        for k in range(2, n + 1):
            a = lax.ppermute(a, "dp", self.ahead)
            b = lax.ppermute(b, "dp", self.behind)
            if k < n:
                a = (a.astype(F32) + first[n - k].astype(F32)).astype(BF)
                b = (b.astype(F32) + second[k].astype(F32)).astype(BF)
        return [a, first[0]], [b, second[0]]

    def gather_small(self, value):
        step = 1
        value = value[None]
        while step < self.size:
            other = lax.ppermute(value, "dp", [(i, i ^ step) for i in range(self.size)])
            bit = (self.me // step) % 2
            value = jnp.where(
                bit == 0,
                jnp.concatenate([value, other], 0),
                jnp.concatenate([other, value], 0),
            )
            step *= 2
        return value


def sum_heads(mine, other):
    size = lax.axis_size("mp")
    near = [(i, i ^ 1) for i in range(size)]
    far = [(i, i ^ 2) for i in range(size)]
    got = lax.ppermute(other, "mp", near)
    mine = (mine.astype(F32) + got.astype(F32)).astype(BF)
    got = lax.ppermute(mine, "mp", far)
    mine = (mine.astype(F32) + got.astype(F32)).astype(BF)
    return mine, lax.ppermute(mine, "mp", near)


def on_device(
    layer_input, frame_mask, gain_attn, w_query, w_key, w_value, w_out, gain_ffn, w_gate, w_up,
    w_down, cotangent,
):
    frames, steps, width = layer_input.shape
    sets = gain_attn.shape[0]
    ring = Ring(lax.axis_size("dp"))
    n = ring.size
    own = width // n
    each = steps // sets
    blocks = n if ring.rings else 1
    order = ring.order if ring.rings else jnp.zeros((1,), jnp.int32)
    places = jnp.concatenate([order, (lax.axis_index("mp") % 2).astype(jnp.int32)[None]])

    first, second = pack_attn(w_query, w_key, w_value, w_out)
    w_attn = ring.gather(first, second)
    after = w_attn[1][-2] if ring.rings else first
    w_ffn = []
    for c in range(sets):
        first, second = pack_ffn(w_gate, w_up, w_down, c, after)
        a, b = ring.gather(first, second)
        after = b[-2] if ring.rings else first
        if ring.rings:
            w_ffn.append([piece for pair in zip(a, b) for piece in pair])
        else:
            w_ffn.append([jnp.concatenate([a[0], b[0]], 1).reshape(width, -1)])
    if not ring.rings:
        w_attn = [[w[0].reshape(width, -1)] for w in w_attn]

    small = jnp.concatenate([gain_attn, gain_ffn], 0).astype(F32)
    gains = ring.gather_small(small)
    if ring.rings:
        gains = jnp.take(gains, order, axis=0)
    gains = gains.transpose(1, 0, 2).reshape(2 * sets, width)
    g_attn, g_ffn = gains[:sets], gains[sets:]

    mask = frame_mask.astype(F32).reshape(frames, 1, 1)
    x0, x1, g0, g1 = prepare(layer_input, cotangent, mask, places, blocks)
    x, g = (x0, x1), (g0, g1)
    h1, qkv, mixed, att, h2, inner, d_gate, d_up, dm, mlp = ([[None] * 2 for _ in range(sets)] for _ in range(10))
    for c in range(sets):
        part = [None, None]
        for h in (1, 0):
            before = qkv[0][h] if c else None
            h1[c][h], qkv[c][h], mixed[c][h], part[h] = attend(
                x[c], g_attn[c : c + 1], before, w_attn[c], h, each
            )
        att[c] = sum_heads(*part)
    scattered, d_gain_ffn = [], []
    for c in range(sets):
        dh, out = [None] * 2, [None] * 2
        for h in (1, 0):
            h2[c][h], inner[c][h], d_gate[c][h], d_up[c][h], dh[h], out[h] = hidden_units(
                x[c], att[c][h], g[c], g_ffn[c : c + 1], w_ffn[c], h
            )
        heights = [own // 2] * (2 * n) if ring.rings else [width]
        halves = [(a, None) for a in h2[c]]
        pieces = weight_grads(
            [
                (halves, d_gate[c]),
                (halves, d_up[c]),
                ([(g[c], 0), (g[c], 1)], inner[c]),
            ],
            heights,
        )
        dh = sum_heads(*dh)
        mlp[c] = sum_heads(*out)
        total = 0.0
        for h in range(2):
            dm[c][h], d_gain = middle_back(x[c], att[c][h], g[c], dh[h], g_ffn[c : c + 1], h)
            total = total + d_gain
        d_gain_ffn.append(total)
        if ring.rings:
            sides = ring.scatter(pieces[0::2], pieces[1::2])
            scattered += sides[0] + sides[1]
        else:
            whole_ = lax.psum_scatter(pieces[0], "dp", scatter_dimension=0, tiled=True)
            for part in jnp.split(whole_, 2, 0):
                scattered += [part, jnp.zeros_like(part)]
    d_gate_w, d_up_w, d_down_w = finish_ffn(scattered)
    output = None
    for h in range(2):
        sides = [att[0][h], att[1][h], mlp[0][h], mlp[1][h]]
        output = join_frames(output_body, x, sides, [], output, h, places, blocks, layer_input.shape)

    d_qkv, part = [[None] * 2 for _ in range(sets)], [[None] * 2 for _ in range(sets)]
    d_gain_attn = 0.0
    for h in (1, 0):
        d_qkv[0][h], d_qkv[1][h], part[0][h], part[1][h], d_gain = attend_back(
            x, [d[h] for d in dm], [q[h] for q in qkv], w_attn, h, each
        )
        d_gain_attn = d_gain_attn + d_gain
    sides = []
    for c in range(sets):
        sides.append(
            weight_grads(
                [
                    ([(a, None) for a in h1[c]], d_qkv[c]),
                    ([(a, None) for a in dm[c]], mixed[c]),
                ],
                [own] * n if ring.rings else [width],
            )
        )
    dh1 = [sum_heads(*p) for p in part]
    grad_input = None
    for h in range(2):
        last = [dm[0][h], dm[1][h], dh1[0][h], dh1[1][h]]
        grad_input = join_frames(input_body, x, last, [g_attn], grad_input, h, places, blocks, layer_input.shape)
    if ring.rings:
        first, second = ring.scatter(*sides)
        scattered = first + second
    else:
        scattered = []
        for side in sides:
            part = lax.psum_scatter(side[0], "dp", scatter_dimension=0, tiled=True)
            scattered += [part, jnp.zeros_like(part)]
    d_query, d_key, d_value, d_out = finish_attn(scattered)

    shared = lax.axis_size("mp")
    d_gains = jnp.concatenate([d_gain_attn, *[d / shared for d in d_gain_ffn]], 0)
    d_gains = d_gains.reshape(2 * sets, blocks, width // blocks)
    if ring.rings:
        spots = jnp.argsort(order)
        d_gains = jnp.take(d_gains, spots, axis=1)
    d_gains = lax.psum(d_gains.reshape(2 * sets, width), ("dp", "mp"))
    d_gains = lax.dynamic_slice_in_dim(d_gains, ring.me * own, own, 1)
    return (
        output, grad_input, d_gains[:sets], d_query, d_key, d_value, d_out,
        d_gains[sets:], d_gate_w, d_up_w, d_down_w,
    )


def solution(mesh):
    rows = P("dp", None, None)
    gain = P(None, "dp")
    into = P(None, "dp", "mp")
    back = P(None, "mp", "dp")
    weights = (gain, into, into, into, back, gain, into, into, back)
    return jax.shard_map(
        on_device,
        mesh=mesh,
        in_specs=(rows, P("dp"), *weights, rows),
        out_specs=(rows, rows, *weights),
        check_vma=False,
    )
```

time: 768 us -> 651 us (0.85)
  local copies, waits for them, and re-layouts: 126 us -> 11.8 us
  waiting for transfers between devices: 260 us -> 202 us
  other arithmetic: 81.4 us -> 34.3 us
  Pallas kernels: 179 us -> 225 us
  blocking collectives: 0 us -> 39.6 us
  starting transfers between devices: 109 us -> 126 us
    dynamic_update_slice x48 -> x0, local copies, waits for them, and re-layouts: 49.4 us -> none  [gather(): lax.dynamic_update_index_in_dim(whole_, part, at, 0)]
    pallas_call x18 -> x28, Pallas kernels: 179 us -> 225 us  [kernel_call(): pl.pallas_call(body, grid_spec=spec, out_shape=outs, input_output_aliases...]
    psum x0 -> x1, blocking collectives: none -> 39.6 us  [on_device(): d_gains = lax.psum(d_gains.reshape(2 * sets, width), ('dp', 'mp'))]
    ppermute x8, waiting for transfers between devices: 60.4 us -> 24.8 us  [sum_heads(): got = lax.ppermute(mine, 'mp', far)]
    select_n x10 -> x8, other arithmetic: 27.4 us -> 0.13 us  [the longest x2 0.09 us: on_device(): gains = jnp.take(gains, order, axis=0)]
    ppermute x98 -> x95, waiting for transfers between devices: 200 us -> 178 us  [the longest x21 71.5 us: scatter(): b = lax.ppermute(b, 'dp', self.behind)]
    unnamed x90 -> x204, local copies, waits for them, and re-layouts: 27.6 us -> 8.06 us
    broadcast_in_dim x14 -> x1, local copies, waits for them, and re-layouts: 19.4 us -> 0.08 us  [on_device(): d_gains = jnp.take(d_gains, spots, axis=1)]
  transfers between devices with their start and end apart: 114 -> 111, of which waited for: 44 -> 43; matrix products, arithmetic and copies ran while one was open for 26% -> 6% of each run, Pallas kernels for 18% -> 34%
where the time goes in v2:
time: 651 us; the launch traced here: 642 us
  Pallas kernels  225 us (35%)
  waiting for transfers between devices  202 us (31%)
  starting transfers between devices  126 us (19%)
  blocking collectives  39.6 us (6%)
  other arithmetic  34.3 us (5%)
  local copies, waits for them, and re-layouts  11.8 us (2%)
    pallas_call x28, Pallas kernels, kernel_call(): pl.pallas_call(body, grid_spec=spec, out_shape=outs, input_output_aliases...  225 us
    ppermute x21, waiting for transfers between devices, scatter(): b = lax.ppermute(b, 'dp', self.behind)  71.5 us
    ppermute x21, waiting for transfers between devices, gather(): b.append(lax.ppermute(b[-1], 'dp', self.behind))  45.1 us
    psum x1, blocking collectives, on_device(): d_gains = lax.psum(d_gains.reshape(2 * sets, width), ('dp', 'mp'))  39.6 us
    ppermute x21, waiting for transfers between devices, scatter(): a = lax.ppermute(a, 'dp', self.ahead)  33.8 us
    ppermute x21, starting transfers between devices, gather(): a.append(lax.ppermute(a[-1], 'dp', self.ahead))  30.7 us
    ppermute x21, starting transfers between devices, scatter(): a = lax.ppermute(a, 'dp', self.ahead)  30.2 us
    ppermute x21, waiting for transfers between devices, gather(): a.append(lax.ppermute(a[-1], 'dp', self.ahead))  27.2 us
  transfers between devices with their start and end apart: 111, of which 43 were waited for; matrix products, arithmetic and copies ran while one was open for 6% of the time, Pallas kernels for 34%

profile of v2, /device:TPU:0, one launch (start us, length us, event | category | flops | bytes accessed | tf_op | source)
XLA Modules:
  0.0 641.8 jit_solution(6468044501537198096)
XLA Ops:
  2.6 3.0 collective-permute-start.3
  5.6 6.5 %collective-permute-done.3.refs_9_.refs_7_ = bf16[128,1024]{1,0:T(8,128)(2,1)S(1)} collective-permute-done((bf16[128,1024]{1,0:T(8,128)(2,1)}, bf16[128,1024]{1,0:T(8,128)(2,1)S(1)}, u32[]{:S(2)}, u32[]{:S(2)}) %collective-permute-start.3) | collective-permute-done | bytes 262176 | tf_op jit(solution)/shard_map/ppermute | solution.py:602
  14.1 5.5 collective-permute-done.4.refs_8_.refs_6_
  30.9 2.4 collective-permute-done.6.refs_6_.refs_4_
  38.8 2.7 collective-permute-done.7.refs_5_.refs_3_
  41.5 2.5 collective-permute-start.8
  44.0 2.7 collective-permute-start.2
  48.0 12.8 %shard_map.203 = (bf16[1024,1024]{1,0:T(8,128)(2,1)}, bf16[1024,1024]{1,0:T(8,128)(2,1)}, bf16[1024,1024]{1,0:T(8,128)(2,1)}, bf16[1024,1024]{1,0:T(8,128)(2,1)}) custom-call(s32[9]{0:T(128)} %pad_add_fusion._.places, bf16[128,16,1024]{2,1,0:T(8,128)(2,1)} %x_ref.1, bf16[128,16,1024]{2,1,0:T(8,128)(2,1)} %cot_ref.1, f32[128,1,1]{2,1,0:T(1,128)} %copy.26.mask_ref), custom_call_target="tpu_custom_call" | custom-call | bytes 16777728 | tf_op jit(solution)/shard_map/pallas_call | solution.py:41
  64.3 3.6 collective-permute-done.17.refs_8_.refs_13_
  69.1 7.8 %shard_map.206 = (bf16[512,1024]{1,0:T(8,128)(2,1)}, bf16[512,768]{1,0:T(8,128)(2,1)}, bf16[512,256]{1,0:T(8,128)(2,1)}, bf16[512,1024]{1,0:T(8,128)(2,1)}) custom-call(bf16[1024,1024]{1,0:T(8,128)(2,1)} %get-tuple-element.135.refs_0_.x0.x_ref, f32[1,1024]{1,0:T(1,128)} %get-tuple-element.262.refs_1_, bf16[128,1024]{1,0:T(8,128)(2,1)} %get-tuple-element.137.refs_2_.refs_0_, ...), custom_call_target="tpu_custom_call" | custom-call | flops 1073741824 | bytes 7344128 | tf_op jit(solution)/shard_map/pallas_call | solution.py:41
  81.9 9.7 %collective-permute-done.30.refs_7_ = bf16[64,3072]{1,0:T(8,128)(2,1)S(1)} collective-permute-done((bf16[64,3072]{1,0:T(8,128)(2,1)}, bf16[64,3072]{1,0:T(8,128)(2,1)S(1)}, u32[]{:S(2)}, u32[]{:S(2)}) %collective-permute-start.30) | collective-permute-done | bytes 393248 | tf_op jit(solution)/shard_map/ppermute | solution.py:603
  93.6 7.9 %shard_map.205 = (bf16[512,1024]{1,0:T(8,128)(2,1)}, bf16[512,768]{1,0:T(8,128)(2,1)}, bf16[512,256]{1,0:T(8,128)(2,1)}, bf16[512,1024]{1,0:T(8,128)(2,1)}) custom-call(bf16[1024,1024]{1,0:T(8,128)(2,1)} %get-tuple-element.135.refs_0_.x0.x_ref, f32[1,1024]{1,0:T(1,128)} %get-tuple-element.262.refs_1_, bf16[128,1024]{1,0:T(8,128)(2,1)} %get-tuple-element.137.refs_2_.refs_0_, ...), custom_call_target="tpu_custom_call" | custom-call | flops 1073741824 | bytes 7344128 | tf_op jit(solution)/shard_map/pallas_call | solution.py:41
  109.1 5.2 collective-permute-done.32.refs_11_
  117.3 2.6 collective-permute-done.19.refs_10_.refs_15_
  120.7 7.4 %shard_map.208 = (bf16[512,1024]{1,0:T(8,128)(2,1)}, bf16[512,768]{1,0:T(8,128)(2,1)}, bf16[512,256]{1,0:T(8,128)(2,1)}, bf16[512,1024]{1,0:T(8,128)(2,1)}) custom-call(bf16[1024,1024]{1,0:T(8,128)(2,1)} %get-tuple-element.136.refs_0_.x1.x_ref, f32[1,1024]{1,0:T(1,128)} %get-tuple-element.261.refs_1_, bf16[512,768]{1,0:T(8,128)(2,1)} %get-tuple-element.143.refs_2_.qkv0, ...), custom_call_target="tpu_custom_call" | custom-call | flops 1073741824 | bytes 8130560 | tf_op jit(solution)/shard_map/pallas_call | solution.py:41
  130.4 9.7 %collective-permute-done.34.refs_15_ = bf16[64,3072]{1,0:T(8,128)(2,1)} collective-permute-done((bf16[64,3072]{1,0:T(8,128)(2,1)}, bf16[64,3072]{1,0:T(8,128)(2,1)}, u32[]{:S(2)}, u32[]{:S(2)}) %collective-permute-start.34) | collective-permute-done | bytes 393248 | tf_op jit(solution)/shard_map/ppermute | solution.py:603
  143.8 7.2 %collective-permute-done.35.refs_17_.after = bf16[64,3072]{1,0:T(8,128)(2,1)} collective-permute-done((bf16[64,3072]{1,0:T(8,128)(2,1)}, bf16[64,3072]{1,0:T(8,128)(2,1)}, u32[]{:S(2)}, u32[]{:S(2)}) %collective-permute-start.35) | collective-permute-done | bytes 393248 | tf_op jit(solution)/shard_map/ppermute | solution.py:603
  157.5 7.4 %shard_map.207 = (bf16[512,1024]{1,0:T(8,128)(2,1)}, bf16[512,768]{1,0:T(8,128)(2,1)}, bf16[512,256]{1,0:T(8,128)(2,1)}, bf16[512,1024]{1,0:T(8,128)(2,1)}) custom-call(bf16[1024,1024]{1,0:T(8,128)(2,1)} %get-tuple-element.136.refs_0_.x1.x_ref, f32[1,1024]{1,0:T(1,128)} %get-tuple-element.261.refs_1_, bf16[512,768]{1,0:T(8,128)(2,1)} %get-tuple-element.140.refs_2_.qkv0, ...), custom_call_target="tpu_custom_call" | custom-call | flops 1073741824 | bytes 8130560 | tf_op jit(solution)/shard_map/pallas_call | solution.py:41
  169.8 3.2 collective-permute-done.36.refs_19_
  174.6 13.8 %shard_map.210 = (bf16[512,1024]{1,0:T(8,128)(2,1)}, bf16[512,1024]{1,0:T(8,128)(2,1)}, bf16[512,1024]{1,0:T(8,128)(2,1)}, bf16[512,1024]{1,0:T(8,128)(2,1)}, bf...) custom-call(bf16[1024,1024]{1,0:T(8,128)(2,1)} %get-tuple-element.135.refs_0_.x0.x_ref, bf16[512,1024]{1,0:T(8,128)(2,1)} %copy-done, ...), custom_call_target="tpu_custom_call" | custom-call | flops 6442450944 | bytes 17829888 | tf_op jit(solution)/shard_map/pallas_call | solution.py:41
  192.2 13.7 %shard_map.211 = (bf16[512,1024]{1,0:T(8,128)(2,1)}, bf16[512,1024]{1,0:T(8,128)(2,1)}, bf16[512,1024]{1,0:T(8,128)(2,1)}, bf16[512,1024]{1,0:T(8,128)(2,1)}, bf...) custom-call(bf16[1024,1024]{1,0:T(8,128)(2,1)} %get-tuple-element.135.refs_0_.x0.x_ref, bf16[512,1024]{1,0:T(8,128)(2,1)} %copy-done.19, ...), custom_call_target="tpu_custom_call" | custom-call | flops 6442450944 | bytes 17829888 | tf_op jit(solution)/shard_map/pallas_call | solution.py:41
  205.9 14.3 %shard_map.228 = (bf16[64,3072]{1,0:T(8,128)(2,1)}, bf16[64,3072]{1,0:T(8,128)(2,1)}, bf16[64,3072]{1,0:T(8,128)(2,1)}, bf16[64,3072]{1,0:T(8,128)(2,1)}, bf16[6...) custom-call(bf16[512,1024]{1,0:T(8,128)(2,1)} %get-tuple-element.208, ...), custom_call_target="tpu_custom_call" | custom-call | flops 6442450944 | bytes 20971520 | tf_op jit(solution)/shard_map/pallas_call | solution.py:41
  225.6 3.2 collective-permute-done.90
  231.3 3.5 collective-permute-done.83
  234.9 10.2 %collective-permute-done.91 = bf16[64,3072]{1,0:T(8,128)(2,1)S(1)} collective-permute-done((bf16[64,3072]{1,0:T(8,128)(2,1)S(1)}, bf16[64,3072]{1,0:T(8,128)(2,1)S(1)}, u32[]{:S(2)}, u32[]{:S(2)}) %collective-permute-start.91) | collective-permute-done | bytes 393248 | tf_op jit(solution)/shard_map/ppermute | solution.py:611
  248.5 7.2 %collective-permute-done.84 = bf16[64,3072]{1,0:T(8,128)(2,1)S(1)} collective-permute-done((bf16[64,3072]{1,0:T(8,128)(2,1)S(1)}, bf16[64,3072]{1,0:T(8,128)(2,1)S(1)}, u32[]{:S(2)}, u32[]{:S(2)}) %collective-permute-start.84) | collective-permute-done | bytes 393248 | tf_op jit(solution)/shard_map/ppermute | solution.py:610
  255.7 2.8 collective-permute-start.51
  263.3 2.5 collective-permute-done.51.refs_15_
  265.8 3.0 collective-permute-start.45
  269.3 5.0 collective-permute-done.92
  275.9 2.5 collective-permute-start.93
  278.5 6.5 %collective-permute-done.93 = bf16[64,3072]{1,0:T(8,128)(2,1)S(1)} collective-permute-done((bf16[64,3072]{1,0:T(8,128)(2,1)S(1)}, bf16[64,3072]{1,0:T(8,128)(2,1)S(1)}, u32[]{:S(2)}, u32[]{:S(2)}) %collective-permute-start.93) | collective-permute-done | bytes 393248 | tf_op jit(solution)/shard_map/ppermute | solution.py:611
  285.0 2.8 collective-permute-start.86
  290.6 4.2 collective-permute-done.86
  296.6 5.2 collective-permute-done.46.refs_6_
  304.3 13.9 %shard_map.213 = (bf16[512,1024]{1,0:T(8,128)(2,1)}, bf16[512,1024]{1,0:T(8,128)(2,1)}, bf16[512,1024]{1,0:T(8,128)(2,1)}, bf16[512,1024]{1,0:T(8,128)(2,1)}, bf...) custom-call(bf16[1024,1024]{1,0:T(8,128)(2,1)} %get-tuple-element.136.refs_0_.x1.x_ref, bf16[512,1024]{1,0:T(8,128)(2,1)} %copy-done.1, ...), custom_call_target="tpu_custom_call" | custom-call | flops 6442450944 | bytes 17829888 | tf_op jit(solution)/shard_map/pallas_call | solution.py:41
  319.3 13.7 %shard_map.214 = (bf16[512,1024]{1,0:T(8,128)(2,1)}, bf16[512,1024]{1,0:T(8,128)(2,1)}, bf16[512,1024]{1,0:T(8,128)(2,1)}, bf16[512,1024]{1,0:T(8,128)(2,1)}, bf...) custom-call(bf16[1024,1024]{1,0:T(8,128)(2,1)} %get-tuple-element.136.refs_0_.x1.x_ref, bf16[512,1024]{1,0:T(8,128)(2,1)} %copy-done.20, ...), custom_call_target="tpu_custom_call" | custom-call | flops 6442450944 | bytes 17829888 | tf_op jit(solution)/shard_map/pallas_call | solution.py:41
  333.0 14.4 %shard_map.229 = (bf16[64,3072]{1,0:T(8,128)(2,1)}, bf16[64,3072]{1,0:T(8,128)(2,1)}, bf16[64,3072]{1,0:T(8,128)(2,1)}, bf16[64,3072]{1,0:T(8,128)(2,1)}, bf16[6...) custom-call(bf16[512,1024]{1,0:T(8,128)(2,1)} %get-tuple-element.232, ...), custom_call_target="tpu_custom_call" | custom-call | flops 6442450944 | bytes 20971520 | tf_op jit(solution)/shard_map/pallas_call | solution.py:41
  352.6 3.7 shard_map.219
  361.4 6.5 %collective-permute-done.95 = bf16[64,3072]{1,0:T(8,128)(2,1)S(1)} collective-permute-done((bf16[64,3072]{1,0:T(8,128)(2,1)}, bf16[64,3072]{1,0:T(8,128)(2,1)S(1)}, u32[]{:S(2)}, u32[]{:S(2)}) %collective-permute-start.95) | collective-permute-done | bytes 393248 | tf_op jit(solution)/shard_map/ppermute | solution.py:611
  371.1 7.4 %collective-permute-done.105 = bf16[64,3072]{1,0:T(8,128)(2,1)S(1)} collective-permute-done((bf16[64,3072]{1,0:T(8,128)(2,1)S(1)}, bf16[64,3072]{1,0:T(8,128)(2,1)S(1)}, u32[]{:S(2)}, u32[]{:S(2)}) %collective-permute-start.105) | collective-permute-done | bytes 393248 | tf_op jit(solution)/shard_map/ppermute | solution.py:611
  384.3 12.4 %collective-permute-done.106 = bf16[64,3072]{1,0:T(8,128)(2,1)S(1)} collective-permute-done((bf16[64,3072]{1,0:T(8,128)(2,1)S(1)}, bf16[64,3072]{1,0:T(8,128)(2,1)S(1)}, u32[]{:S(2)}, u32[]{:S(2)}) %collective-permute-start.106) | collective-permute-done | bytes 393248 | tf_op jit(solution)/shard_map/ppermute | solution.py:611
  400.8 3.7 shard_map.217
  408.4 5.3 collective-permute-done.100
  414.8 7.9 %collective-permute-done.108 = bf16[64,3072]{1,0:T(8,128)(2,1)S(1)} collective-permute-done((bf16[64,3072]{1,0:T(8,128)(2,1)S(1)}, bf16[64,3072]{1,0:T(8,128)(2,1)S(1)}, u32[]{:S(2)}, u32[]{:S(2)}) %collective-permute-start.108) | collective-permute-done | bytes 393248 | tf_op jit(solution)/shard_map/ppermute | solution.py:611
  425.4 5.2 collective-permute-done.101
  430.6 3.8 shard_map.220
  434.4 16.4 %shard_map.221 = (bf16[512,768]{1,0:T(8,128)(2,1)}, bf16[512,768]{1,0:T(8,128)(2,1)}, bf16[512,1024]{1,0:T(8,128)(2,1)}, bf16[512,1024]{1,0:T(8,128)(2,1)}, f32[2,1024]{1,0:T(2,128)}) custom-call(bf16[1024,1024]{1,0:T(8,128)(2,1)} %get-tuple-element.135.refs_0_.x0.x_ref, bf16[1024,1024]{1,0:T(8,128)(2,1)} %get-tuple-element.136.refs_0_.x1.x_ref, ...), custom_call_target="tpu_custom_call" | custom-call | flops 2147483648 | bytes 15736832 | tf_op jit(solution)/shard_map/pallas_call | solution.py:41
  454.1 3.7 shard_map.218
  457.8 16.3 %shard_map.222 = (bf16[512,768]{1,0:T(8,128)(2,1)}, bf16[512,768]{1,0:T(8,128)(2,1)}, bf16[512,1024]{1,0:T(8,128)(2,1)}, bf16[512,1024]{1,0:T(8,128)(2,1)}, f32[2,1024]{1,0:T(2,128)}) custom-call(bf16[1024,1024]{1,0:T(8,128)(2,1)} %get-tuple-element.135.refs_0_.x0.x_ref, bf16[1024,1024]{1,0:T(8,128)(2,1)} %get-tuple-element.136.refs_0_.x1.x_ref, ...), custom_call_target="tpu_custom_call" | custom-call | flops 2147483648 | bytes 15736832 | tf_op jit(solution)/shard_map/pallas_call | solution.py:41
  474.1 7.0 %shard_map.226 = (bf16[128,1024]{1,0:T(8,128)(2,1)}, bf16[128,1024]{1,0:T(8,128)(2,1)}, bf16[128,1024]{1,0:T(8,128)(2,1)}, bf16[128,1024]{1,0:T(8,128)(2,1)}, bf...) custom-call(bf16[512,1024]{1,0:T(8,128)(2,1)} %get-tuple-element.190, ...), custom_call_target="tpu_custom_call" | custom-call | flops 2147483648 | bytes 8388608 | tf_op jit(solution)/shard_map/pallas_call | solution.py:41
  481.4 7.0 %shard_map.225 = (bf16[128,1024]{1,0:T(8,128)(2,1)}, bf16[128,1024]{1,0:T(8,128)(2,1)}, bf16[128,1024]{1,0:T(8,128)(2,1)}, bf16[128,1024]{1,0:T(8,128)(2,1)}, bf...) custom-call(bf16[512,1024]{1,0:T(8,128)(2,1)} %get-tuple-element.176, ...), custom_call_target="tpu_custom_call" | custom-call | flops 2147483648 | bytes 8388608 | tf_op jit(solution)/shard_map/pallas_call | solution.py:41
  491.0 6.0 collective-permute-done.69
  503.0 5.7 shard_map.215.refs_0_
  509.9 4.0 shard_map.230
  517.1 6.3 collective-permute-done.78
  535.7 3.7 collective-permute-done.80
  543.7 8.7 %collective-permute-done.67 = bf16[512,1024]{1,0:T(8,128)(2,1)} collective-permute-done((bf16[512,1024]{1,0:T(8,128)(2,1)S(1)}, bf16[512,1024]{1,0:T(8,128)(2,1)}, u32[]{:S(2)}, u32[]{:S(2)}) %collective-permute-start.67) | collective-permute-done | bytes 1048608 | tf_op jit(solution)/shard_map/ppermute | solution.py:638
  554.2 2.6 add_convert_fusion.dh1
  556.8 16.1 %collective-permute-done.64 = bf16[512,1024]{1,0:T(8,128)(2,1)} collective-permute-done((bf16[512,1024]{1,0:T(8,128)(2,1)}, bf16[512,1024]{1,0:T(8,128)(2,1)}, u32[]{:S(2)}, u32[]{:S(2)}) %collective-permute-start.64) | collective-permute-done | bytes 1048608 | tf_op jit(solution)/shard_map/ppermute | solution.py:638
  575.4 39.6 %psum.7 = f32[4,1024]{1,0:T(4,128)S(1)} all-reduce(f32[4,1024]{1,0:T(4,128)S(1)} %bitcast_select_fusion), channel_id=1, replica_groups=mesh['dp'=8,'mp'=4] {'dp','mp'}, use_global_device_ids=true, to_apply=%region_1.2 | all-reduce | flops 4096 | bytes 32768 | tf_op jit(solution)/shard_map/psum | solution.py:767
  619.6 5.6 shard_map.216
  629.0 6.3 shard_map.223.refs_0_
  635.3 6.3 shard_map.224
  (472 shorter events, 169.8 us)
Async XLA Ops:
  21.8 13.8 %collective-permute-start = (f32[1,4,128]{2,1,0:T(4,128)S(1)}, f32[1,4,128]{2,1,0:T(4,128)S(1)}, u32[]{:S(2)}, u32[]{:S(2)}) collective-permute-start(f32[1,4,128]{2,1,0:T(4,128)S(1)} %maximum_convert_fusion), channel_id=1, source_target_pairs={{0,4},{4,0},{8,12},{12,8},{16,20},{20,16},{24,28},{28,24},{1,5},{5... | collective-permute-start | bytes 6152 | tf_op jit(solution)/shard_map/ppermute | solution.py:621
  37.2 24.3 %collective-permute-start.16 = (bf16[128,1024]{1,0:T(8,128)(2,1)S(1)}, bf16[128,1024]{1,0:T(8,128)(2,1)S(1)}, u32[]{:S(2)}, u32[]{:S(2)}) collective-permute-start(bf16[128,1024]{1,0:T(8,128)(2,1)S(1)} %collective-permute-done.15.refs_6_.refs_11_), channel_id=1, source_target_pairs={{8,0},{16,8},{24,16},{28,24},{20,28},{12,20},{4,12},{0,4},{9,1},{1... | collective-permute-start | bytes 786440 | tf_op jit(solution)/shard_map/ppermute | solution.py:603
  41.5 20.5 %collective-permute-start.8 = (bf16[128,1024]{1,0:T(8,128)(2,1)S(1)}, bf16[128,1024]{1,0:T(8,128)(2,1)S(1)}, u32[]{:S(2)}, u32[]{:S(2)}) collective-permute-start(bf16[128,1024]{1,0:T(8,128)(2,1)S(1)} %collective-permute-done.7.refs_5_.refs_3_), channel_id=1, source_target_pairs={{0,8},{8,16},{16,24},{24,28},{28,20},{20,12},{12,4},{4,0},{1,9},{9... | collective-permute-start | bytes 786440 | tf_op jit(solution)/shard_map/ppermute | solution.py:602
  44.0 16.9 %collective-permute-start.2 = (f32[4,4,128]{2,1,0:T(4,128)S(1)}, f32[4,4,128]{2,1,0:T(4,128)S(1)}, u32[]{:S(2)}, u32[]{:S(2)}) collective-permute-start(f32[4,4,128]{2,1,0:T(4,128)S(1)} %maximum_select_fusion.1), channel_id=1, source_target_pairs={{0,16},{4,20},{8,24},{12,28},{16,0},{20,4},{24,8},{28,12},{1,17},{... | collective-permute-start | bytes 24584 | tf_op jit(solution)/shard_map/ppermute | solution.py:621
  76.9 27.4 %collective-permute-start.10 = (bf16[512,1024]{1,0:T(8,128)(2,1)}, bf16[512,1024]{1,0:T(8,128)(2,1)S(1)}, u32[]{:S(2)}, u32[]{:S(2)}) collective-permute-start(bf16[512,1024]{1,0:T(8,128)(2,1)} %get-tuple-element.139), channel_id=1, source_target_pairs={{0,1},{1,0},{2,3},{3,2},{4,5},{5,4},{6,7},{7,6},{8,9},{9,8},{10,11... | collective-permute-start | bytes 3145736 | tf_op jit(solution)/shard_map/ppermute | solution.py:636
  102.3 12.1 %collective-permute-start.32 = (bf16[64,3072]{1,0:T(8,128)(2,1)S(1)}, bf16[64,3072]{1,0:T(8,128)(2,1)S(1)}, u32[]{:S(2)}, u32[]{:S(2)}) collective-permute-start(bf16[64,3072]{1,0:T(8,128)(2,1)S(1)} %collective-permute-done.31.refs_9_), channel_id=1, source_target_pairs={{8,0},{16,8},{24,16},{28,24},{20,28},{12,20},{4,12},{0,4},{9,1},{1... | collective-permute-start | bytes 1179656 | tf_op jit(solution)/shard_map/ppermute | solution.py:603
  103.9 12.1 %collective-permute-start.25 = (bf16[64,3072]{1,0:T(8,128)(2,1)S(1)}, bf16[64,3072]{1,0:T(8,128)(2,1)S(1)}, u32[]{:S(2)}, u32[]{:S(2)}) collective-permute-start(bf16[64,3072]{1,0:T(8,128)(2,1)S(1)} %collective-permute-done.24.refs_16_), channel_id=1, source_target_pairs={{0,8},{8,16},{16,24},{24,28},{28,20},{20,12},{12,4},{4,0},{1,9},{9... | collective-permute-start | bytes 1179656 | tf_op jit(solution)/shard_map/ppermute | solution.py:602
  105.9 36.1 %collective-permute-start.11 = (bf16[512,1024]{1,0:T(8,128)(2,1)S(1)}, bf16[512,1024]{1,0:T(8,128)(2,1)}, u32[]{:S(2)}, u32[]{:S(2)}) collective-permute-start(bf16[512,1024]{1,0:T(8,128)(2,1)S(1)} %add_convert_fusion.15), channel_id=1, source_target_pairs={{0,2},{1,3},{2,0},{3,1},{4,6},{5,7},{6,4},{7,5},{8,10},{9,11},{10,... | collective-permute-start | bytes 3145736 | tf_op jit(solution)/shard_map/ppermute | solution.py:638
  107.5 12.4 %collective-permute-start.19 = (bf16[128,1024]{1,0:T(8,128)(2,1)S(1)}, bf16[128,1024]{1,0:T(8,128)(2,1)S(1)}, u32[]{:S(2)}, u32[]{:S(2)}) collective-permute-start(bf16[128,1024]{1,0:T(8,128)(2,1)S(1)} %copy-done.3), channel_id=1, source_target_pairs={{8,0},{16,8},{24,16},{28,24},{20,28},{12,20},{4,12},{0,4},{9,1},{1... | collective-permute-start | bytes 786440 | tf_op jit(solution)/shard_map/ppermute | solution.py:603
  114.3 13.8 %collective-permute-start.33 = (bf16[64,3072]{1,0:T(8,128)(2,1)S(1)}, bf16[64,3072]{1,0:T(8,128)(2,1)}, u32[]{:S(2)}, u32[]{:S(2)}) collective-permute-start(bf16[64,3072]{1,0:T(8,128)(2,1)S(1)} %collective-permute-done.32.refs_11_), channel_id=1, source_target_pairs={{8,0},{16,8},{24,16},{28,24},{20,28},{12,20},{4,12},{0,4},{9,1},{1... | collective-permute-start | bytes 1179656 | tf_op jit(solution)/shard_map/ppermute | solution.py:603
  115.9 13.9 %collective-permute-start.26 = (bf16[64,3072]{1,0:T(8,128)(2,1)S(1)}, bf16[64,3072]{1,0:T(8,128)(2,1)}, u32[]{:S(2)}, u32[]{:S(2)}) collective-permute-start(bf16[64,3072]{1,0:T(8,128)(2,1)S(1)} %collective-permute-done.25.refs_14_), channel_id=1, source_target_pairs={{0,8},{8,16},{16,24},{24,28},{28,20},{20,12},{12,4},{4,0},{1,9},{9... | collective-permute-start | bytes 1179656 | tf_op jit(solution)/shard_map/ppermute | solution.py:602
  128.1 27.1 %collective-permute-start.20 = (bf16[512,1024]{1,0:T(8,128)(2,1)}, bf16[512,1024]{1,0:T(8,128)(2,1)S(1)}, u32[]{:S(2)}, u32[]{:S(2)}) collective-permute-start(bf16[512,1024]{1,0:T(8,128)(2,1)} %get-tuple-element.144), channel_id=1, source_target_pairs={{0,1},{1,0},{2,3},{3,2},{4,5},{5,4},{6,7},{7,6},{8,9},{9,8},{10,11... | collective-permute-start | bytes 3145736 | tf_op jit(solution)/shard_map/ppermute | solution.py:636
  141.6 15.2 %collective-permute-start.28 = (bf16[64,3072]{1,0:T(8,128)(2,1)}, bf16[64,3072]{1,0:T(8,128)(2,1)}, u32[]{:S(2)}, u32[]{:S(2)}) collective-permute-start(bf16[64,3072]{1,0:T(8,128)(2,1)} %collective-permute-done.27.refs_10_), channel_id=1, source_target_pairs={{0,8},{8,16},{16,24},{24,28},{28,20},{20,12},{12,4},{4,0},{1,9},{9... | collective-permute-start | bytes 1179656 | tf_op jit(solution)/shard_map/ppermute | solution.py:602
  143.7 47.4 %collective-permute-start.12 = (bf16[512,1024]{1,0:T(8,128)(2,1)S(1)}, bf16[512,1024]{1,0:T(8,128)(2,1)S(1)}, u32[]{:S(2)}, u32[]{:S(2)}) collective-permute-start(bf16[512,1024]{1,0:T(8,128)(2,1)S(1)} %add_convert_fusion.14.refs_1_.a0.att_ref), channel_id=1, source_target_pairs={{0,1},{1,0},{2,3},{3,2},{4,5},{5,4},{6,7},{7,6},{8,9},{9,8},{10,11... | collective-permute-start | bytes 3145736 | tf_op jit(solution)/shard_map/ppermute | solution.py:640
  153.2 13.4 %collective-permute-start.40 = (bf16[64,3072]{1,0:T(8,128)(2,1)}, bf16[64,3072]{1,0:T(8,128)(2,1)S(1)}, u32[]{:S(2)}, u32[]{:S(2)}) collective-permute-start(bf16[64,3072]{1,0:T(8,128)(2,1)} %get-tuple-element.151.refs_4_), channel_id=1, source_target_pairs={{0,8},{8,16},{16,24},{24,28},{28,20},{20,12},{12,4},{4,0},{1,9},{9... | collective-permute-start | bytes 1179656 | tf_op jit(solution)/shard_map/ppermute | solution.py:602
  154.8 13.4 %collective-permute-start.47 = (bf16[64,3072]{1,0:T(8,128)(2,1)}, bf16[64,3072]{1,0:T(8,128)(2,1)S(1)}, u32[]{:S(2)}, u32[]{:S(2)}) collective-permute-start(bf16[64,3072]{1,0:T(8,128)(2,1)} %get-tuple-element.152.refs_5_), channel_id=1, source_target_pairs={{8,0},{16,8},{24,16},{28,24},{20,28},{12,20},{4,12},{0,4},{9,1},{1... | collective-permute-start | bytes 1179656 | tf_op jit(solution)/shard_map/ppermute | solution.py:603
  155.2 17.7 %collective-permute-start.36 = (bf16[64,3072]{1,0:T(8,128)(2,1)}, bf16[64,3072]{1,0:T(8,128)(2,1)S(1)}, u32[]{:S(2)}, u32[]{:S(2)}) collective-permute-start(bf16[64,3072]{1,0:T(8,128)(2,1)} %collective-permute-done.35.refs_17_.after), channel_id=1, source_target_pairs={{8,0},{16,8},{24,16},{28,24},{20,28},{12,20},{4,12},{0,4},{9,1},{1... | collective-permute-start | bytes 1179656 | tf_op jit(solution)/shard_map/ppermute | solution.py:603
  156.8 17.1 %collective-permute-start.29 = (bf16[64,3072]{1,0:T(8,128)(2,1)}, bf16[64,3072]{1,0:T(8,128)(2,1)S(1)}, u32[]{:S(2)}, u32[]{:S(2)}) collective-permute-start(bf16[64,3072]{1,0:T(8,128)(2,1)} %collective-permute-done.28.refs_8_), channel_id=1, source_target_pairs={{0,8},{8,16},{16,24},{24,28},{28,20},{20,12},{12,4},{4,0},{1,9},{9... | collective-permute-start | bytes 1179656 | tf_op jit(solution)/shard_map/ppermute | solution.py:602
  166.6 55.9 %collective-permute-start.21 = (bf16[512,1024]{1,0:T(8,128)(2,1)S(1)}, bf16[512,1024]{1,0:T(8,128)(2,1)S(1)}, u32[]{:S(2)}, u32[]{:S(2)}) collective-permute-start(bf16[512,1024]{1,0:T(8,128)(2,1)S(1)} %add_convert_fusion.13), channel_id=1, source_target_pairs={{0,2},{1,3},{2,0},{3,1},{4,6},{5,7},{6,4},{7,5},{8,10},{9,11},{10,... | collective-permute-start | bytes 3145736 | tf_op jit(solution)/shard_map/ppermute | solution.py:638
  168.2 20.3 %collective-permute-start.41 = (bf16[64,3072]{1,0:T(8,128)(2,1)S(1)}, bf16[64,3072]{1,0:T(8,128)(2,1)S(1)}, u32[]{:S(2)}, u32[]{:S(2)}) collective-permute-start(bf16[64,3072]{1,0:T(8,128)(2,1)S(1)} %collective-permute-done.40.refs_18_), channel_id=1, source_target_pairs={{0,8},{8,16},{16,24},{24,28},{28,20},{20,12},{12,4},{4,0},{1,9},{9... | collective-permute-start | bytes 1179656 | tf_op jit(solution)/shard_map/ppermute | solution.py:602
  173.0 17.3 %collective-permute-start.48 = (bf16[64,3072]{1,0:T(8,128)(2,1)S(1)}, bf16[64,3072]{1,0:T(8,128)(2,1)S(1)}, u32[]{:S(2)}, u32[]{:S(2)}) collective-permute-start(bf16[64,3072]{1,0:T(8,128)(2,1)S(1)} %collective-permute-done.47.refs_7_), channel_id=1, source_target_pairs={{8,0},{16,8},{24,16},{28,24},{20,28},{12,20},{4,12},{0,4},{9,1},{1... | collective-permute-start | bytes 1179656 | tf_op jit(solution)/shard_map/ppermute | solution.py:603
  188.5 34.9 %collective-permute-start.42 = (bf16[64,3072]{1,0:T(8,128)(2,1)S(1)}, bf16[64,3072]{1,0:T(8,128)(2,1)S(1)}, u32[]{:S(2)}, u32[]{:S(2)}) collective-permute-start(bf16[64,3072]{1,0:T(8,128)(2,1)S(1)} %collective-permute-done.41.refs_16_), channel_id=1, source_target_pairs={{0,8},{8,16},{16,24},{24,28},{28,20},{20,12},{12,4},{4,0},{1,9},{9... | collective-permute-start | bytes 1179656 | tf_op jit(solution)/shard_map/ppermute | solution.py:602
  190.2 33.8 %collective-permute-start.49 = (bf16[64,3072]{1,0:T(8,128)(2,1)S(1)}, bf16[64,3072]{1,0:T(8,128)(2,1)S(1)}, u32[]{:S(2)}, u32[]{:S(2)}) collective-permute-start(bf16[64,3072]{1,0:T(8,128)(2,1)S(1)} %collective-permute-done.48.refs_9_), channel_id=1, source_target_pairs={{8,0},{16,8},{24,16},{28,24},{20,28},{12,20},{4,12},{0,4},{9,1},{1... | collective-permute-start | bytes 1179656 | tf_op jit(solution)/shard_map/ppermute | solution.py:603
  223.4 35.2 %collective-permute-start.57 = (bf16[512,1024]{1,0:T(8,128)(2,1)S(1)}, bf16[512,1024]{1,0:T(8,128)(2,1)S(1)}, u32[]{:S(2)}, u32[]{:S(2)}) collective-permute-start(bf16[512,1024]{1,0:T(8,128)(2,1)S(1)} %copy-done.79), channel_id=1, source_target_pairs={{0,1},{1,0},{2,3},{3,2},{4,5},{5,4},{6,7},{7,6},{8,9},{9,8},{10,11... | collective-permute-start | bytes 3145736 | tf_op jit(solution)/shard_map/ppermute | solution.py:636
  223.4 45.4 %collective-permute-start.37 = (bf16[512,1024]{1,0:T(8,128)(2,1)S(1)}, bf16[512,1024]{1,0:T(8,128)(2,1)S(1)}, u32[]{:S(2)}, u32[]{:S(2)}) collective-permute-start(bf16[512,1024]{1,0:T(8,128)(2,1)S(1)} %copy-done.78), channel_id=1, source_target_pairs={{0,1},{1,0},{2,3},{3,2},{4,5},{5,4},{6,7},{7,6},{8,9},{9,8},{10,11... | collective-permute-start | bytes 3145736 | tf_op jit(solution)/shard_map/ppermute | solution.py:636
  224.0 22.9 %collective-permute-start.43 = (bf16[64,3072]{1,0:T(8,128)(2,1)S(1)}, bf16[64,3072]{1,0:T(8,128)(2,1)S(1)}, u32[]{:S(2)}, u32[]{:S(2)}) collective-permute-start(bf16[64,3072]{1,0:T(8,128)(2,1)S(1)} %collective-permute-done.42.refs_14_), channel_id=1, source_target_pairs={{0,8},{8,16},{16,24},{24,28},{28,20},{20,12},{12,4},{4,0},{1,9},{9... | collective-permute-start | bytes 1179656 | tf_op jit(solution)/shard_map/ppermute | solution.py:602
  228.8 18.1 %collective-permute-start.50 = (bf16[64,3072]{1,0:T(8,128)(2,1)S(1)}, bf16[64,3072]{1,0:T(8,128)(2,1)S(1)}, u32[]{:S(2)}, u32[]{:S(2)}) collective-permute-start(bf16[64,3072]{1,0:T(8,128)(2,1)S(1)} %collective-permute-done.49.refs_11_), channel_id=1, source_target_pairs={{8,0},{16,8},{24,16},{28,24},{20,28},{12,20},{4,12},{0,4},{9,1},{1... | collective-permute-start | bytes 1179656 | tf_op jit(solution)/shard_map/ppermute | solution.py:603
  246.9 71.4 %collective-permute-start.22 = (bf16[512,1024]{1,0:T(8,128)(2,1)S(1)}, bf16[512,1024]{1,0:T(8,128)(2,1)S(1)}, u32[]{:S(2)}, u32[]{:S(2)}) collective-permute-start(bf16[512,1024]{1,0:T(8,128)(2,1)S(1)} %add_convert_fusion.12.refs_1_.a1.att_ref), channel_id=1, source_target_pairs={{0,1},{1,0},{2,3},{3,2},{4,5},{5,4},{6,7},{7,6},{8,9},{9,8},{10,11... | collective-permute-start | bytes 3145736 | tf_op jit(solution)/shard_map/ppermute | solution.py:640
  247.0 14.3 %collective-permute-start.44 = (bf16[64,3072]{1,0:T(8,128)(2,1)S(1)}, bf16[64,3072]{1,0:T(8,128)(2,1)S(1)}, u32[]{:S(2)}, u32[]{:S(2)}) collective-permute-start(bf16[64,3072]{1,0:T(8,128)(2,1)S(1)} %collective-permute-done.43.refs_12_), channel_id=1, source_target_pairs={{0,8},{8,16},{16,24},{24,28},{28,20},{20,12},{12,4},{4,0},{1,9},{9... | collective-permute-start | bytes 1179656 | tf_op jit(solution)/shard_map/ppermute | solution.py:602
  258.6 15.6 %collective-permute-start.92 = (bf16[64,3072]{1,0:T(8,128)(2,1)S(1)}, bf16[64,3072]{1,0:T(8,128)(2,1)S(1)}, u32[]{:S(2)}, u32[]{:S(2)}) collective-permute-start(bf16[64,3072]{1,0:T(8,128)(2,1)S(1)} %add_convert_fusion.32), channel_id=1, source_target_pairs={{8,0},{16,8},{24,16},{28,24},{20,28},{12,20},{4,12},{0,4},{9,1},{1... | collective-permute-start | bytes 1179656 | tf_op jit(solution)/shard_map/ppermute | solution.py:611
  261.3 14.5 %collective-permute-start.85 = (bf16[64,3072]{1,0:T(8,128)(2,1)S(1)}, bf16[64,3072]{1,0:T(8,128)(2,1)S(1)}, u32[]{:S(2)}, u32[]{:S(2)}) collective-permute-start(bf16[64,3072]{1,0:T(8,128)(2,1)S(1)} %add_convert_fusion.38), channel_id=1, source_target_pairs={{0,8},{8,16},{16,24},{24,28},{28,20},{20,12},{12,4},{4,0},{1,9},{9... | collective-permute-start | bytes 1179656 | tf_op jit(solution)/shard_map/ppermute | solution.py:610
  265.8 22.1 %collective-permute-start.45 = (bf16[64,3072]{1,0:T(8,128)(2,1)S(1)}, bf16[64,3072]{1,0:T(8,128)(2,1)S(1)}, u32[]{:S(2)}, u32[]{:S(2)}) collective-permute-start(bf16[64,3072]{1,0:T(8,128)(2,1)S(1)} %collective-permute-done.44.refs_10_), channel_id=1, source_target_pairs={{0,8},{8,16},{16,24},{24,28},{28,20},{20,12},{12,4},{4,0},{1,9},{9... | collective-permute-start | bytes 1179656 | tf_op jit(solution)/shard_map/ppermute | solution.py:602
  268.8 19.9 %collective-permute-start.52 = (bf16[64,3072]{1,0:T(8,128)(2,1)S(1)}, bf16[64,3072]{1,0:T(8,128)(2,1)S(1)}, u32[]{:S(2)}, u32[]{:S(2)}) collective-permute-start(bf16[64,3072]{1,0:T(8,128)(2,1)S(1)} %collective-permute-done.51.refs_15_), channel_id=1, source_target_pairs={{8,0},{16,8},{24,16},{28,24},{20,28},{12,20},{4,12},{0,4},{9,1},{1... | collective-permute-start | bytes 1179656 | tf_op jit(solution)/shard_map/ppermute | solution.py:603
  274.2 76.3 %collective-permute-start.58 = (bf16[512,1024]{1,0:T(8,128)(2,1)S(1)}, bf16[512,1024]{1,0:T(8,128)(2,1)S(1)}, u32[]{:S(2)}, u32[]{:S(2)}) collective-permute-start(bf16[512,1024]{1,0:T(8,128)(2,1)S(1)} %add_convert_fusion.7), channel_id=1, source_target_pairs={{0,2},{1,3},{2,0},{3,1},{4,6},{5,7},{6,4},{7,5},{8,10},{9,11},{10,... | collective-permute-start | bytes 3145736 | tf_op jit(solution)/shard_map/ppermute | solution.py:638
  287.9 68.4 %collective-permute-start.38 = (bf16[512,1024]{1,0:T(8,128)(2,1)S(1)}, bf16[512,1024]{1,0:T(8,128)(2,1)S(1)}, u32[]{:S(2)}, u32[]{:S(2)}) collective-permute-start(bf16[512,1024]{1,0:T(8,128)(2,1)S(1)} %add_convert_fusion.11), channel_id=1, source_target_pairs={{0,2},{1,3},{2,0},{3,1},{4,6},{5,7},{6,4},{7,5},{8,10},{9,11},{10,... | collective-permute-start | bytes 3145736 | tf_op jit(solution)/shard_map/ppermute | solution.py:638
  288.7 13.0 %collective-permute-start.46 = (bf16[64,3072]{1,0:T(8,128)(2,1)S(1)}, bf16[64,3072]{1,0:T(8,128)(2,1)}, u32[]{:S(2)}, u32[]{:S(2)}) collective-permute-start(bf16[64,3072]{1,0:T(8,128)(2,1)S(1)} %collective-permute-done.45.refs_8_), channel_id=1, source_target_pairs={{0,8},{8,16},{16,24},{24,28},{28,20},{20,12},{12,4},{4,0},{1,9},{9... | collective-permute-start | bytes 1179656 | tf_op jit(solution)/shard_map/ppermute | solution.py:602
  301.7 47.2 %collective-permute-start.94 = (bf16[64,3072]{1,0:T(8,128)(2,1)S(1)}, bf16[64,3072]{1,0:T(8,128)(2,1)S(1)}, u32[]{:S(2)}, u32[]{:S(2)}) collective-permute-start(bf16[64,3072]{1,0:T(8,128)(2,1)S(1)} %add_convert_fusion.30), channel_id=1, source_target_pairs={{8,0},{16,8},{24,16},{28,24},{20,28},{12,20},{4,12},{0,4},{9,1},{1... | collective-permute-start | bytes 1179656 | tf_op jit(solution)/shard_map/ppermute | solution.py:611
  303.6 46.9 %collective-permute-start.87 = (bf16[64,3072]{1,0:T(8,128)(2,1)S(1)}, bf16[64,3072]{1,0:T(8,128)(2,1)S(1)}, u32[]{:S(2)}, u32[]{:S(2)}) collective-permute-start(bf16[64,3072]{1,0:T(8,128)(2,1)S(1)} %add_convert_fusion.36), channel_id=1, source_target_pairs={{0,8},{8,16},{16,24},{24,28},{28,20},{20,12},{12,4},{4,0},{1,9},{9... | collective-permute-start | bytes 1179656 | tf_op jit(solution)/shard_map/ppermute | solution.py:610
  349.0 12.2 %collective-permute-start.97 = (bf16[64,3072]{1,0:T(8,128)(2,1)}, bf16[64,3072]{1,0:T(8,128)(2,1)S(1)}, u32[]{:S(2)}, u32[]{:S(2)}) collective-permute-start(bf16[64,3072]{1,0:T(8,128)(2,1)} %get-tuple-element.240), channel_id=1, source_target_pairs={{0,8},{8,16},{16,24},{24,28},{28,20},{20,12},{12,4},{4,0},{1,9},{9... | collective-permute-start | bytes 1179656 | tf_op jit(solution)/shard_map/ppermute | solution.py:610
  350.5 30.8 %collective-permute-start.60 = (bf16[512,1024]{1,0:T(8,128)(2,1)}, bf16[512,1024]{1,0:T(8,128)(2,1)S(1)}, u32[]{:S(2)}, u32[]{:S(2)}) collective-permute-start(bf16[512,1024]{1,0:T(8,128)(2,1)} %get-tuple-element.159), channel_id=1, source_target_pairs={{0,1},{1,0},{2,3},{3,2},{4,5},{5,4},{6,7},{7,6},{8,9},{9,8},{10,11... | collective-permute-start | bytes 3145736 | tf_op jit(solution)/shard_map/ppermute | solution.py:636
  350.6 32.0 %collective-permute-start.54 = (bf16[512,1024]{1,0:T(8,128)(2,1)}, bf16[512,1024]{1,0:T(8,128)(2,1)S(1)}, u32[]{:S(2)}, u32[]{:S(2)}) collective-permute-start(bf16[512,1024]{1,0:T(8,128)(2,1)} %get-tuple-element.154), channel_id=1, source_target_pairs={{0,1},{1,0},{2,3},{3,2},{4,5},{5,4},{6,7},{7,6},{8,9},{9,8},{10,11... | collective-permute-start | bytes 3145736 | tf_op jit(solution)/shard_map/ppermute | solution.py:636
  361.2 38.2 %collective-permute-start.59 = (bf16[512,1024]{1,0:T(8,128)(2,1)S(1)}, bf16[512,1024]{1,0:T(8,128)(2,1)S(1)}, u32[]{:S(2)}, u32[]{:S(2)}) collective-permute-start(bf16[512,1024]{1,0:T(8,128)(2,1)S(1)} %copy-done.21), channel_id=1, source_target_pairs={{0,1},{1,0},{2,3},{3,2},{4,5},{5,4},{6,7},{7,6},{8,9},{9,8},{10,11... | collective-permute-start | bytes 3145736 | tf_op jit(solution)/shard_map/ppermute | solution.py:640
  378.5 121.0 %collective-permute-start.96 = (bf16[64,3072]{1,0:T(8,128)(2,1)S(1)}, bf16[64,3072]{1,0:T(8,128)(2,1)S(1)}, u32[]{:S(2)}, u32[]{:S(2)}) collective-permute-start(bf16[64,3072]{1,0:T(8,128)(2,1)S(1)} %add_convert_fusion.28), channel_id=1, source_target_pairs={{8,0},{16,8},{24,16},{28,24},{20,28},{12,20},{4,12},{0,4},{9,1},{1... | collective-permute-start | bytes 1179656 | tf_op jit(solution)/shard_map/ppermute | solution.py:611
  380.0 128.8 %collective-permute-start.89 = (bf16[64,3072]{1,0:T(8,128)(2,1)S(1)}, bf16[64,3072]{1,0:T(8,128)(2,1)S(1)}, u32[]{:S(2)}, u32[]{:S(2)}) collective-permute-start(bf16[64,3072]{1,0:T(8,128)(2,1)S(1)} %add_convert_fusion.34), channel_id=1, source_target_pairs={{0,8},{8,16},{16,24},{24,28},{28,20},{20,12},{12,4},{4,0},{1,9},{9... | collective-permute-start | bytes 1179656 | tf_op jit(solution)/shard_map/ppermute | solution.py:610
  381.3 15.4 %collective-permute-start.106 = (bf16[64,3072]{1,0:T(8,128)(2,1)S(1)}, bf16[64,3072]{1,0:T(8,128)(2,1)S(1)}, u32[]{:S(2)}, u32[]{:S(2)}) collective-permute-start(bf16[64,3072]{1,0:T(8,128)(2,1)S(1)} %add_convert_fusion.20), channel_id=1, source_target_pairs={{8,0},{16,8},{24,16},{28,24},{20,28},{12,20},{4,12},{0,4},{9,1},{1... | collective-permute-start | bytes 1179656 | tf_op jit(solution)/shard_map/ppermute | solution.py:611
  382.6 14.7 %collective-permute-start.99 = (bf16[64,3072]{1,0:T(8,128)(2,1)S(1)}, bf16[64,3072]{1,0:T(8,128)(2,1)S(1)}, u32[]{:S(2)}, u32[]{:S(2)}) collective-permute-start(bf16[64,3072]{1,0:T(8,128)(2,1)S(1)} %add_convert_fusion.26), channel_id=1, source_target_pairs={{0,8},{8,16},{16,24},{24,28},{28,20},{20,12},{12,4},{4,0},{1,9},{9... | collective-permute-start | bytes 1179656 | tf_op jit(solution)/shard_map/ppermute | solution.py:610
  396.7 27.6 %collective-permute-start.61 = (bf16[512,1024]{1,0:T(8,128)(2,1)S(1)}, bf16[512,1024]{1,0:T(8,128)(2,1)S(1)}, u32[]{:S(2)}, u32[]{:S(2)}) collective-permute-start(bf16[512,1024]{1,0:T(8,128)(2,1)S(1)} %add_convert_fusion.5), channel_id=1, source_target_pairs={{0,2},{1,3},{2,0},{3,1},{4,6},{5,7},{6,4},{7,5},{8,10},{9,11},{10,... | collective-permute-start | bytes 3145736 | tf_op jit(solution)/shard_map/ppermute | solution.py:638
  399.4 100.2 %collective-permute-start.55 = (bf16[512,1024]{1,0:T(8,128)(2,1)S(1)}, bf16[512,1024]{1,0:T(8,128)(2,1)S(1)}, u32[]{:S(2)}, u32[]{:S(2)}) collective-permute-start(bf16[512,1024]{1,0:T(8,128)(2,1)S(1)} %add_convert_fusion.9), channel_id=1, source_target_pairs={{0,2},{1,3},{2,0},{3,1},{4,6},{5,7},{6,4},{7,5},{8,10},{9,11},{10,... | collective-permute-start | bytes 3145736 | tf_op jit(solution)/shard_map/ppermute | solution.py:638
  424.3 26.5 %collective-permute-start.109 = (bf16[64,3072]{1,0:T(8,128)(2,1)S(1)}, bf16[64,3072]{1,0:T(8,128)(2,1)S(1)}, u32[]{:S(2)}, u32[]{:S(2)}) collective-permute-start(bf16[64,3072]{1,0:T(8,128)(2,1)S(1)} %add_convert_fusion.17), channel_id=1, source_target_pairs={{8,0},{16,8},{24,16},{28,24},{20,28},{12,20},{4,12},{0,4},{9,1},{1... | collective-permute-start | bytes 1179656 | tf_op jit(solution)/shard_map/ppermute | solution.py:611
  430.5 22.6 %collective-permute-start.62 = (bf16[512,1024]{1,0:T(8,128)(2,1)S(1)}, bf16[512,1024]{1,0:T(8,128)(2,1)S(1)}, u32[]{:S(2)}, u32[]{:S(2)}) collective-permute-start(bf16[512,1024]{1,0:T(8,128)(2,1)S(1)} %add_convert_fusion.4.dh_ref), channel_id=1, source_target_pairs={{0,1},{1,0},{2,3},{3,2},{4,5},{5,4},{6,7},{7,6},{8,9},{9,8},{10,11... | collective-permute-start | bytes 3145736 | tf_op jit(solution)/shard_map/ppermute | solution.py:640
  450.8 37.7 %collective-permute-start.102 = (bf16[64,3072]{1,0:T(8,128)(2,1)S(1)}, bf16[64,3072]{1,0:T(8,128)(2,1)S(1)}, u32[]{:S(2)}, u32[]{:S(2)}) collective-permute-start(bf16[64,3072]{1,0:T(8,128)(2,1)S(1)} %add_convert_fusion.23), channel_id=1, source_target_pairs={{0,8},{8,16},{16,24},{24,28},{28,20},{20,12},{12,4},{4,0},{1,9},{9... | collective-permute-start | bytes 1179656 | tf_op jit(solution)/shard_map/ppermute | solution.py:610
  490.9 18.0 %collective-permute-start.110 = (bf16[64,3072]{1,0:T(8,128)(2,1)S(1)}, bf16[64,3072]{1,0:T(8,128)(2,1)S(1)}, u32[]{:S(2)}, u32[]{:S(2)}) collective-permute-start(bf16[64,3072]{1,0:T(8,128)(2,1)S(1)} %add_convert_fusion.16), channel_id=1, source_target_pairs={{8,0},{16,8},{24,16},{28,24},{20,28},{12,20},{4,12},{0,4},{9,1},{1... | collective-permute-start | bytes 1179656 | tf_op jit(solution)/shard_map/ppermute | solution.py:611
  497.0 12.1 %collective-permute-start.103 = (bf16[64,3072]{1,0:T(8,128)(2,1)S(1)}, bf16[64,3072]{1,0:T(8,128)(2,1)S(1)}, u32[]{:S(2)}, u32[]{:S(2)}) collective-permute-start(bf16[64,3072]{1,0:T(8,128)(2,1)S(1)} %add_convert_fusion.22), channel_id=1, source_target_pairs={{0,8},{8,16},{16,24},{24,28},{28,20},{20,12},{12,4},{4,0},{1,9},{9... | collective-permute-start | bytes 1179656 | tf_op jit(solution)/shard_map/ppermute | solution.py:610
  499.5 14.9 %collective-permute-start.77 = (bf16[128,1024]{1,0:T(8,128)(2,1)S(1)}, bf16[128,1024]{1,0:T(8,128)(2,1)S(1)}, u32[]{:S(2)}, u32[]{:S(2)}) collective-permute-start(bf16[128,1024]{1,0:T(8,128)(2,1)S(1)} %add_convert_fusion.45), channel_id=1, source_target_pairs={{8,0},{16,8},{24,16},{28,24},{20,28},{12,20},{4,12},{0,4},{9,1},{1... | collective-permute-start | bytes 786440 | tf_op jit(solution)/shard_map/ppermute | solution.py:611
  499.6 16.3 %collective-permute-start.70 = (bf16[128,1024]{1,0:T(8,128)(2,1)S(1)}, bf16[128,1024]{1,0:T(8,128)(2,1)S(1)}, u32[]{:S(2)}, u32[]{:S(2)}) collective-permute-start(bf16[128,1024]{1,0:T(8,128)(2,1)S(1)} %add_convert_fusion.51), channel_id=1, source_target_pairs={{0,8},{8,16},{16,24},{24,28},{28,20},{20,12},{12,4},{4,0},{1,9},{9... | collective-permute-start | bytes 786440 | tf_op jit(solution)/shard_map/ppermute | solution.py:610
  508.8 110.7 %collective-permute-start.39 = (bf16[512,1024]{1,0:T(8,128)(2,1)S(1)}, bf16[512,1024]{1,0:T(8,128)(2,1)}, u32[]{:S(2)}, u32[]{:S(2)}) collective-permute-start(bf16[512,1024]{1,0:T(8,128)(2,1)S(1)} %copy-done.4), channel_id=1, source_target_pairs={{0,1},{1,0},{2,3},{3,2},{4,5},{5,4},{6,7},{7,6},{8,9},{9,8},{10,11... | collective-permute-start | bytes 3145736 | tf_op jit(solution)/shard_map/ppermute | solution.py:640
  514.3 13.3 %collective-permute-start.63 = (bf16[512,1024]{1,0:T(8,128)(2,1)S(1)}, bf16[512,1024]{1,0:T(8,128)(2,1)S(1)}, u32[]{:S(2)}, u32[]{:S(2)}) collective-permute-start(bf16[512,1024]{1,0:T(8,128)(2,1)S(1)} %copy-done.77), channel_id=1, source_target_pairs={{0,1},{1,0},{2,3},{3,2},{4,5},{5,4},{6,7},{7,6},{8,9},{9,8},{10,11... | collective-permute-start | bytes 3145736 | tf_op jit(solution)/shard_map/ppermute | solution.py:636
  526.2 26.3 %collective-permute-start.67 = (bf16[512,1024]{1,0:T(8,128)(2,1)S(1)}, bf16[512,1024]{1,0:T(8,128)(2,1)}, u32[]{:S(2)}, u32[]{:S(2)}) collective-permute-start(bf16[512,1024]{1,0:T(8,128)(2,1)S(1)} %add_convert_fusion.1), channel_id=1, source_target_pairs={{0,2},{1,3},{2,0},{3,1},{4,6},{5,7},{6,4},{7,5},{8,10},{9,11},{10,... | collective-permute-start | bytes 3145736 | tf_op jit(solution)/shard_map/ppermute | solution.py:638
  529.0 43.8 %collective-permute-start.64 = (bf16[512,1024]{1,0:T(8,128)(2,1)}, bf16[512,1024]{1,0:T(8,128)(2,1)}, u32[]{:S(2)}, u32[]{:S(2)}) collective-permute-start(bf16[512,1024]{1,0:T(8,128)(2,1)} %add_convert_fusion.3), channel_id=1, source_target_pairs={{0,2},{1,3},{2,0},{3,1},{4,6},{5,7},{6,4},{7,5},{8,10},{9,11},{10,... | collective-permute-start | bytes 3145736 | tf_op jit(solution)/shard_map/ppermute | solution.py:638
  539.4 80.2 %collective-permute-start.56 = (bf16[512,1024]{1,0:T(8,128)(2,1)S(1)}, bf16[512,1024]{1,0:T(8,128)(2,1)}, u32[]{:S(2)}, u32[]{:S(2)}) collective-permute-start(bf16[512,1024]{1,0:T(8,128)(2,1)S(1)} %copy-done.5), channel_id=1, source_target_pairs={{0,1},{1,0},{2,3},{3,2},{4,5},{5,4},{6,7},{7,6},{8,9},{9,8},{10,11... | collective-permute-start | bytes 3145736 | tf_op jit(solution)/shard_map/ppermute | solution.py:640
  540.4 34.4 %collective-permute-start.81 = (bf16[128,1024]{1,0:T(8,128)(2,1)S(1)}, bf16[128,1024]{1,0:T(8,128)(2,1)}, u32[]{:S(2)}, u32[]{:S(2)}) collective-permute-start(bf16[128,1024]{1,0:T(8,128)(2,1)S(1)} %add_convert_fusion.41), channel_id=1, source_target_pairs={{8,0},{16,8},{24,16},{28,24},{20,28},{12,20},{4,12},{0,4},{9,1},{1... | collective-permute-start | bytes 786440 | tf_op jit(solution)/shard_map/ppermute | solution.py:611
  552.4 63.6 %collective-permute-start.74 = (bf16[128,1024]{1,0:T(8,128)(2,1)}, bf16[128,1024]{1,0:T(8,128)(2,1)}, u32[]{:S(2)}, u32[]{:S(2)}) collective-permute-start(bf16[128,1024]{1,0:T(8,128)(2,1)} %add_convert_fusion.47), channel_id=1, source_target_pairs={{0,8},{8,16},{16,24},{24,28},{28,20},{20,12},{12,4},{4,0},{1,9},{9... | collective-permute-start | bytes 786440 | tf_op jit(solution)/shard_map/ppermute | solution.py:610
  572.9 62.4 %collective-permute-start.68 = (bf16[512,1024]{1,0:T(8,128)(2,1)}, bf16[512,1024]{1,0:T(8,128)(2,1)}, u32[]{:S(2)}, u32[]{:S(2)}) collective-permute-start(bf16[512,1024]{1,0:T(8,128)(2,1)} %add_convert_fusion.dh1), channel_id=1, source_target_pairs={{0,1},{1,0},{2,3},{3,2},{4,5},{5,4},{6,7},{7,6},{8,9},{9,8},{10,11... | collective-permute-start | bytes 3145736 | tf_op jit(solution)/shard_map/ppermute | solution.py:640
  574.8 60.5 %collective-permute-start.65 = (bf16[512,1024]{1,0:T(8,128)(2,1)S(1)}, bf16[512,1024]{1,0:T(8,128)(2,1)}, u32[]{:S(2)}, u32[]{:S(2)}) collective-permute-start(bf16[512,1024]{1,0:T(8,128)(2,1)S(1)} %add_convert_fusion.2.dh0), channel_id=1, source_target_pairs={{0,1},{1,0},{2,3},{3,2},{4,5},{5,4},{6,7},{7,6},{8,9},{9,8},{10,11... | collective-permute-start | bytes 3145736 | tf_op jit(solution)/shard_map/ppermute | solution.py:640
  (149 other events, 1856.8 us)

commit v3 on v2

v3 whole, which is shorter than its diff:
```python
import functools

import jax
import jax.numpy as jnp
from jax import lax
from jax.experimental import pallas as pl
from jax.experimental.pallas import tpu as pltpu
from jax.sharding import PartitionSpec as P

HDIM = 64
EPS = 1e-05
NEG = -1e30
BF = jnp.bfloat16
F32 = jnp.float32
NN = (((1,), (0,)), ((), ()))
NT = (((1,), (1,)), ((), ()))
TN = (((0,), (0,)), ((), ()))
MIB = 1024 * 1024
SUB = 128
PAIR = 2 * HDIM
ROWS = 256
HBM = pl.BlockSpec(memory_space=pl.ANY)


def mm(left, right, dims=NN):
    return lax.dot_general(left, right, dims, preferred_element_type=F32)


def kernel_call(body, grid, ins, in_specs, outs, out_specs, flops, scratch=(), scalars=None, alias=None):
    moved = sum(a.size * a.dtype.itemsize for a in ins) + sum(
        o.size * jnp.dtype(o.dtype).itemsize for o in outs
    )
    spec = pltpu.PrefetchScalarGridSpec(
        num_scalar_prefetch=0 if scalars is None else 1,
        grid=grid,
        in_specs=in_specs,
        out_specs=out_specs,
        scratch_shapes=scratch,
    )
    args = ins if scalars is None else (scalars, *ins)
    return pl.pallas_call(
        body,
        grid_spec=spec,
        out_shape=outs,
        input_output_aliases=alias or {},
        compiler_params=pltpu.CompilerParams(vmem_limit_bytes=56 * MIB),
        cost_estimate=pl.CostEstimate(flops=1, bytes_accessed=1, transcendentals=0),
    )(*args)


def whole(shape):
    return pl.BlockSpec(shape, lambda *i: (0,) * len(shape))


def rows_of(rows, width, start=0):
    return pl.BlockSpec((rows, width), lambda i, *_: (i + start, 0))


def out_of(shape, kind=BF):
    return jax.ShapeDtypeStruct(shape, kind)


class Halves:
    def __init__(self, tokens):
        self.count = tokens // 2 // ROWS
        self.grid = (2 * self.count,)

    def block(self, i, places):
        half = (1 - i // self.count + places[places.shape[0] - 1]) % 2
        return half * self.count + i % self.count

    def both(self, width):
        return pl.BlockSpec((ROWS, width), lambda i, p: (self.block(i, p), 0))

    def pair(self, width):
        return [
            pl.BlockSpec((ROWS, width), lambda i, p: (jnp.maximum(i - self.count, 0), 0)),
            pl.BlockSpec((ROWS, width), lambda i, p: (jnp.minimum(i, self.count - 1), 0)),
        ]

    def pick(self, pair):
        return jnp.where(pl.program_id(0) < self.count, pair[1][...], pair[0][...])

    def put(self, pair, value):
        for k in range(2):

            @pl.when((pl.program_id(0) < self.count) == (k == 1))
            def _():
                pair[k][...] = value


def split_sets(value, sets):
    frames, steps, width = value.shape
    parts = value.reshape(frames, sets, steps // sets, width)
    return [parts[:, c].reshape(-1, width) for c in range(sets)]


def pack_attn_body(wq, wk, wv, wo, first, second):
    hw = wq.shape[2]
    for c, ref in enumerate((first, second)):
        for t, w in enumerate((wq, wk, wv)):
            ref[:, t * hw : (t + 1) * hw] = w[c]
        ref[:, 3 * hw :] = wo[c].T


def pack_attn(wq, wk, wv, wo):
    own, hw = wq.shape[1:]
    piece = (own, 4 * hw)
    return kernel_call(
        pack_attn_body,
        (1,),
        (wq, wk, wv, wo),
        [whole(w.shape) for w in (wq, wk, wv, wo)],
        [out_of(piece)] * 2,
        [whole(piece)] * 2,
        0,
    )


def pack_ffn_body(wg, wu, wd, first, second):
    units = wg.shape[2]
    half = wg.shape[1] // 2
    for k, ref in enumerate((first, second)):
        rows = slice(k * half, (k + 1) * half)
        ref[:, :units] = wg[0, rows]
        ref[:, units : 2 * units] = wu[0, rows]
    turned = wd[0].T
    first[:, 2 * units :] = turned[:half]
    second[:, 2 * units :] = turned[half:]


def pack_ffn(wg, wu, wd, c):
    own, units = wg.shape[1:]
    piece = (own // 2, 3 * units)
    into = pl.BlockSpec((1, own, units), lambda i: (c, 0, 0))
    back = pl.BlockSpec((1, units, own), lambda i: (c, 0, 0))
    return kernel_call(
        pack_ffn_body,
        (1,),
        (wg, wu, wd),
        [into, into, back],
        [out_of(piece)] * 2,
        [whole(piece)] * 2,
        0,
    )


def norm(value):
    scale = lax.rsqrt(jnp.mean(value * value, axis=-1, keepdims=True) + EPS)
    return value * scale, scale


def lanes_low(shape):
    return lax.broadcasted_iota(jnp.int32, shape, 1) < HDIM


def stack_heads(pair):
    low = lanes_low(pair.shape)
    zero = jnp.zeros_like(pair)
    return jnp.concatenate([jnp.where(low, pair, zero), jnp.where(low, zero, pair)], axis=0)


def pick_heads(stacked):
    half = stacked.shape[0] // 2
    low = lanes_low((half, stacked.shape[1]))
    return jnp.where(low, stacked[:half], stacked[half:])


def visible(rows, keys, steps):
    row = lax.broadcasted_iota(jnp.int32, (rows, keys), 0) % SUB
    key = lax.broadcasted_iota(jnp.int32, (rows, keys), 1)
    same = row // steps == (key % SUB) // steps
    if keys == SUB:
        return same & (row >= key)
    return same & ((key < SUB) | (row >= key - SUB))


def softmax(query, keys, steps):
    raw = mm(query, keys, NT) * HDIM ** (-0.5)
    masked = jnp.where(visible(raw.shape[0], raw.shape[1], steps), raw, NEG)
    top = jnp.max(masked, axis=-1, keepdims=True)
    power = jnp.exp(masked - top)
    return power / jnp.sum(power, axis=-1, keepdims=True)


class Pieces:
    def __init__(self, arrays, groups):
        self.arrays = arrays
        self.count = len(arrays)
        self.groups = groups
        self.shape = (sum(a.shape[0] for a in arrays), arrays[0].shape[1])
        self.scratch = [pltpu.VMEM(self.shape, BF), pltpu.SemaphoreType.DMA((groups, self.count))]

    def copies(self, refs, places, memory, sems, group):
        wide = self.shape[1] // self.groups
        cols = pl.ds(group * wide, wide)
        for k, ref in enumerate(refs):
            if self.count == 1:
                start = 0
            else:
                parts = self.count // (places.shape[0] - 1)
                start = (places[k // parts] * parts + k % parts) * ref.shape[0]
                start = pl.multiple_of(start, ref.shape[0])
            rows = pl.ds(start, ref.shape[0])
            yield pltpu.make_async_copy(ref.at[:, cols], memory.at[rows, cols], sems.at[group, k])

    def start(self, refs, places, memory, sems, order):
        @pl.when(pl.program_id(0) == 0)
        def _():
            for group in order:
                for copy in self.copies(refs, places, memory, sems, group):
                    copy.start()

    def wait(self, refs, places, memory, sems, group):
        @pl.when(pl.program_id(0) == 0)
        def _():
            for copy in self.copies(refs, places, memory, sems, group):
                copy.wait()


def attend_body(pieces, halves, steps, hw, later, places, *refs):
    x_ref, gain_ref, *refs = refs
    if later:
        before_ref, *refs = refs
    w_refs, refs = refs[: pieces.count], refs[pieces.count :]
    h_ref, qkv_ref, mixed_ref, mine_ref, other_ref, w_ref, sems = refs
    pieces.start(w_refs, places, w_ref, sems, range(1))
    normed, _ = norm(x_ref[...].astype(F32))
    hidden = (normed * gain_ref[...]).astype(BF)
    h_ref[...] = hidden
    pieces.wait(w_refs, places, w_ref, sems, 0)
    qkv = mm(hidden, w_ref[:, : 3 * hw]).astype(BF)
    qkv_ref[...] = qkv
    for s in range(x_ref.shape[0] // SUB):
        rows = slice(s * SUB, (s + 1) * SUB)
        for j in range(hw // PAIR):
            q, k, v = (qkv[rows, t * hw + j * PAIR : t * hw + (j + 1) * PAIR] for t in range(3))
            if later:
                k_old, v_old = (
                    before_ref[rows, t * hw + j * PAIR : t * hw + (j + 1) * PAIR] for t in (1, 2)
                )
                k = jnp.concatenate([k_old, k], axis=0)
                v = jnp.concatenate([v_old, v], axis=0)
            probs = softmax(stack_heads(q), k, steps).astype(BF)
            mixed_ref[rows, j * PAIR : (j + 1) * PAIR] = pick_heads(mm(probs, v)).astype(BF)
    halves.put((mine_ref, other_ref), mm(mixed_ref[...], w_ref[:, 3 * hw :], NT).astype(BF))


def attend(places, x, gain, before, w, steps):
    tokens, width = x.shape
    pieces, halves = Pieces(w, 1), Halves(tokens)
    hw = pieces.shape[1] // 4
    ins = [x, gain]
    specs = [halves.both(width), whole(gain.shape)]
    if before is not None:
        ins.append(before)
        specs.append(halves.both(3 * hw))
    widths = (width, 3 * hw, hw)
    *out, mine, other = kernel_call(
        functools.partial(attend_body, pieces, halves, steps, hw, before is not None),
        halves.grid,
        [*ins, *w],
        [*specs, *[HBM] * pieces.count],
        [out_of((tokens, n)) for n in widths] + [out_of((tokens // 2, width))] * 2,
        [halves.both(n) for n in widths] + halves.pair(width),
        2 * tokens * width * 4 * hw,
        pieces.scratch,
        places,
    )
    return *out, (mine, other)


def units_body(pieces, halves, units, places, *refs):
    x_ref, att0, att1, g_ref, gain_ref, *refs = refs
    w_refs, refs = refs[: pieces.count], refs[pieces.count :]
    h_ref, inner_ref, dgate_ref, dup_ref, dh0, dh1, mlp0, mlp1, w_ref, sems = refs
    pieces.start(w_refs, places, w_ref, sems, (2, 0, 1))
    normed, _ = norm(x_ref[...].astype(F32) + halves.pick((att0, att1)).astype(F32))
    hidden = (normed * gain_ref[...]).astype(BF)
    h_ref[...] = hidden
    cut = 256
    cols = [
        [slice(t * units + u * cut, t * units + (u + 1) * cut) for t in range(3)] for u in range(units // cut)
    ]
    pieces.wait(w_refs, places, w_ref, sems, 2)
    d_inners = [mm(g_ref[...], w_ref[:, c[2]]) for c in cols]
    pieces.wait(w_refs, places, w_ref, sems, 0)
    pieces.wait(w_refs, places, w_ref, sems, 1)
    for c, d_inner in zip(cols, d_inners):
        gate = mm(hidden, w_ref[:, c[0]])
        up = mm(hidden, w_ref[:, c[1]])
        sigma = 1.0 / (1.0 + jnp.exp(-gate))
        active = gate * sigma
        inner_ref[:, c[0]] = (active * up).astype(BF)
        dup_ref[:, c[0]] = (d_inner * active).astype(BF)
        dgate_ref[:, c[0]] = (d_inner * up * sigma * (1.0 + gate * (1.0 - sigma))).astype(BF)
    grad = mm(dgate_ref[...], w_ref[:, :units], NT) + mm(dup_ref[...], w_ref[:, units : 2 * units], NT)
    halves.put((dh0, dh1), grad.astype(BF))
    halves.put((mlp0, mlp1), mm(inner_ref[...], w_ref[:, 2 * units :], NT).astype(BF))


def hidden_units(places, x, att, g, gain, w):
    tokens, width = x.shape
    pieces, halves = Pieces(w, 3), Halves(tokens)
    units = pieces.shape[1] // 3
    part = halves.both(width)
    widths = (width, units, units, units)
    *out, dh0, dh1, mlp0, mlp1 = kernel_call(
        functools.partial(units_body, pieces, halves, units),
        halves.grid,
        (x, *att, g, gain, *w),
        [part, *halves.pair(width), part, whole(gain.shape), *[HBM] * pieces.count],
        [out_of((tokens, n)) for n in widths] + [out_of((tokens // 2, width))] * 4,
        [halves.both(n) for n in widths] + halves.pair(width) * 2,
        12 * tokens * width * units,
        pieces.scratch,
        places,
    )
    return *out, (dh0, dh1), (mlp0, mlp1)


def grads_body(columns, parts, steps, places, *refs):
    inputs = max(right for _, right in columns) + 1
    ins, outs = refs[:inputs], refs[inputs:]
    values = []
    for slots, k in columns:
        rows = [ins[s][...] for s in slots]
        rows = jnp.concatenate(rows, axis=1) if len(rows) > 1 else rows[0]
        values.append(mm(rows, ins[k][...], TN).astype(BF))
    if parts == 0:
        at = 0
        for value in values:
            outs[0][:, at : at + value.shape[1]] = value
            at += value.shape[1]
        return
    *outs, buffer, sems = outs
    height = outs[0].shape[0]
    per = buffer.shape[1] // height

    def copies(block):
        for k in range(per):
            rows = buffer.at[block % 2, pl.ds(k * height, height)]
            yield pltpu.make_async_copy(rows, outs[block * per + k], sems.at[block % 2, k])

    for block in range(steps):

        @pl.when(pl.program_id(0) == block)
        def _():
            if block >= 2:
                for copy in copies(block - 2):
                    copy.wait()
            at = 0
            for value in values:
                buffer[block % 2, :, at : at + value.shape[1]] = value
                at += value.shape[1]
            for copy in copies(block):
                copy.start()
            if block == steps - 1:
                for last in range(max(0, steps - 2), steps):
                    for copy in copies(last):
                        copy.wait()


def weight_grads(places, columns, parts):
    count = places.shape[0] - 1
    tokens, width = columns[0][0].shape
    own = width // count
    steps = width // ROWS
    slots = ROWS // own if parts else 1
    ins, specs, marks = [], [], []
    for left, _ in columns:
        mark = []
        for k in range(slots):
            place = (lambda i, p, k=k: (0, p[i * slots + k])) if parts else (lambda i, p: (0, i))
            ins.append(left)
            specs.append(pl.BlockSpec((tokens, ROWS // slots), place))
            mark.append(len(ins) - 1)
        marks.append(tuple(mark))
    pairs = []
    for (_, right), mark in zip(columns, marks):
        ins.append(right)
        specs.append(whole(right.shape))
        pairs.append((mark, len(ins) - 1))
    total = sum(right.shape[1] for _, right in columns)
    if parts:
        outs = [out_of((own // parts, total))] * (parts * count)
        out_specs = [HBM] * len(outs)
        scratch = [pltpu.VMEM((2, ROWS, total), BF), pltpu.SemaphoreType.DMA((2, slots * parts))]
    else:
        outs, out_specs, scratch = [out_of((width, total))], [rows_of(ROWS, total)], []
    return kernel_call(
        functools.partial(grads_body, pairs, parts, steps),
        (steps,),
        ins,
        specs,
        outs,
        out_specs,
        2 * tokens * width * total,
        scratch,
        places,
    )


def norm_back(grad_hidden, value, gain):
    normed, scale = norm(value)
    scaled = grad_hidden * gain
    back = scale * (scaled - normed * jnp.mean(scaled * normed, axis=-1, keepdims=True))
    return back, jnp.sum(grad_hidden * normed, axis=0, keepdims=True)


def add_up(ref, value):
    @pl.when(pl.program_id(0) == 0)
    def _():
        ref[...] = jnp.zeros_like(ref)

    ref[...] += value


def middle_body(halves, _, x_ref, att0, att1, g_ref, dh0, dh1, gain_ref, dm_ref, dgain_ref):
    value = x_ref[...].astype(F32) + halves.pick((att0, att1)).astype(F32)
    back, d_gain = norm_back(halves.pick((dh0, dh1)).astype(F32), value, gain_ref[...])
    dm_ref[...] = (g_ref[...].astype(F32) + back).astype(BF)
    add_up(dgain_ref, d_gain)


def middle_back(places, x, att, g, dh, gain):
    tokens, width = x.shape
    halves = Halves(tokens)
    part, pair = halves.both(width), halves.pair(width)
    return kernel_call(
        functools.partial(middle_body, halves),
        halves.grid,
        (x, *att, g, *dh, gain),
        [part, *pair, part, *pair, whole(gain.shape)],
        [out_of((tokens, width)), out_of((1, width), F32)],
        [part, whole((1, width))],
        0,
        (),
        places,
    )


def attend_back_body(pieces, steps, hw, places, x0, x1, dm0, dm1, qkv0, qkv1, *refs):
    n = pieces[0].count
    sides = (refs[:n], refs[n : 2 * n])
    dqkv0, dqkv1, mine, other, dgain, w0, sems0, w1, sems1 = refs[-9:]
    for p, s, w, sems in zip(pieces, sides, (w0, w1), (sems0, sems1)):
        p.start(s, places, w, sems, range(1))
    normed = [norm(x[...].astype(F32))[0] for x in (x0, x1)]
    for p, s, w, sems in zip(pieces, sides, (w0, w1), (sems0, sems1)):
        p.wait(s, places, w, sems, 0)
    scale = HDIM ** (-0.5)
    d_mixed = [mm(d[...], w[:, 3 * hw :]).astype(BF) for d, w in ((dm0, w0), (dm1, w1))]
    for s in range(dm0.shape[0] // SUB):
        rows = slice(s * SUB, (s + 1) * SUB)
        for j in range(hw // PAIR):
            cols = [slice(t * hw + j * PAIR, t * hw + (j + 1) * PAIR) for t in range(3)]
            q0, k0, v0 = (qkv0[rows, c] for c in cols)
            q1, k1, v1 = (qkv1[rows, c] for c in cols)
            keys = (k0, jnp.concatenate([k0, k1], axis=0))
            values = (v0, jnp.concatenate([v0, v1], axis=0))
            d_k, d_v = [], []
            for c, (q, out_ref) in enumerate(((q0, dqkv0), (q1, dqkv1))):
                q_two = stack_heads(q)
                d_two = stack_heads(d_mixed[c][rows, cols[0]])
                soft = softmax(q_two, keys[c], steps)
                d_probs = mm(d_two, values[c], NT)
                inside = jnp.sum(soft * d_probs, axis=-1, keepdims=True)
                d_scores = (soft * (d_probs - inside)).astype(BF)
                d_q = pick_heads(mm(d_scores, keys[c])) * scale
                out_ref[rows, cols[0]] = d_q.astype(BF)
                d_k.append(mm(d_scores, q_two, TN) * scale)
                d_v.append(mm(soft.astype(BF), d_two, TN))
            dqkv0[rows, cols[1]] = (d_k[0] + d_k[1][:SUB]).astype(BF)
            dqkv1[rows, cols[1]] = d_k[1][SUB:].astype(BF)
            dqkv0[rows, cols[2]] = (d_v[0] + d_v[1][:SUB]).astype(BF)
            dqkv1[rows, cols[2]] = d_v[1][SUB:].astype(BF)
    gains = []
    for c, (d, w) in enumerate(((dqkv0, w0), (dqkv1, w1))):
        grad = mm(d[...], w[:, : 3 * hw], NT)
        gains.append(jnp.sum(grad * normed[c], axis=0, keepdims=True))
        for k, ref in enumerate((other, mine)):

            @pl.when(pl.program_id(0) == k)
            def _():
                ref[c * ROWS : (c + 1) * ROWS] = grad.astype(BF)

    add_up(dgain, jnp.concatenate(gains, axis=0))


def attend_back(places, x, dm, qkv, w, part, before, steps):
    tokens, width = dm[0].shape
    halves = Halves(tokens)
    pieces = [Pieces(side, 1) for side in w]
    hw = pieces[0].shape[1] // 4
    spot = lambda i, p: (halves.block(i * halves.count, p) + part, 0)
    flat, thin = pl.BlockSpec((ROWS, width), spot), pl.BlockSpec((ROWS, 3 * hw), spot)
    ins = [*x, *dm, *qkv, *w[0], *w[1], *(before or ())]
    specs = [flat] * 4 + [thin] * 2 + [HBM] * (len(ins) - 6)
    alias = {len(ins) - 1: 0, len(ins): 1} if before else {}
    d0, d1, mine, other, d_gain = kernel_call(
        functools.partial(attend_back_body, pieces, steps, hw),
        (2,),
        ins,
        specs,
        [out_of((tokens, 3 * hw))] * 2 + [out_of((2 * ROWS, width))] * 2 + [out_of((2, width), F32)],
        [thin] * 2 + [whole((2 * ROWS, width))] * 2 + [whole((2, width))],
        8 * ROWS * width * 4 * hw,
        pieces[0].scratch + pieces[1].scratch,
        places,
        alias,
    )
    return (d0, d1), (mine, other), d_gain


def store_frames(out_ref, sums):
    frames, _, width = out_ref.shape
    both = [p.reshape(frames, 1, p.shape[0] // frames, width) for p in sums]
    out_ref[...] = jnp.concatenate(both, axis=1).reshape(frames, -1, width).astype(BF)


def output_body(halves, _, x0, x1, *refs):
    *refs, out_ref = refs
    pairs = [halves.pick(refs[k : k + 2]).astype(F32) for k in range(0, 8, 2)]
    sums = [x[...].astype(F32) + pairs[2 * c] + pairs[2 * c + 1] for c, x in enumerate((x0, x1))]
    store_frames(out_ref, sums)


def output_of(places, x, att, mlp, shape):
    frames, steps, width = shape
    halves = Halves(x[0].shape[0])
    sides = [a for c in range(2) for pair in (att[c], mlp[c]) for a in pair]
    cube = pl.BlockSpec((2 * ROWS // steps, steps, width), lambda i, p: (halves.block(i, p), 0, 0))
    return kernel_call(
        functools.partial(output_body, halves),
        halves.grid,
        [*x, *sides],
        [halves.both(width)] * 2 + halves.pair(width) * 4,
        [out_of(shape)],
        [cube],
        0,
        (),
        places,
    )[0]


def input_body(_, x0, x1, dm0, dm1, mine, other, gain_ref, *refs):
    first = pl.program_id(0) == 0
    sums = []
    for c, (x, dm) in enumerate(((x0, dm0), (x1, dm1))):
        rows = slice(c * ROWS, (c + 1) * ROWS)
        dh = jnp.where(first, other[rows], mine[rows]).astype(F32)
        back, _ = norm_back(dh, x[...].astype(F32), gain_ref[c : c + 1])
        sums.append(dm[...].astype(F32) + back)
    store_frames(refs[-1], sums)


def input_back(places, x, dm, dh, gain, part, before, shape):
    frames, steps, width = shape
    halves = Halves(x[0].shape[0])
    block = lambda i, p: halves.block(i * halves.count, p) + part
    flat = pl.BlockSpec((ROWS, width), lambda i, p: (block(i, p), 0))
    cube = pl.BlockSpec((2 * ROWS // steps, steps, width), lambda i, p: (block(i, p), 0, 0))
    ins = [*x, *dm, *dh, gain]
    specs = [flat] * 4 + [whole(d.shape) for d in dh] + [whole(gain.shape)]
    alias = {}
    if before is not None:
        ins.append(before)
        specs.append(HBM)
        alias = {len(ins): 0}
    return kernel_call(input_body, (2,), ins, specs, [out_of(shape)], [cube], 0, (), places, alias)[0]


def add_terms(refs):
    total = refs[0][...].astype(F32)
    for ref in refs[1:]:
        total = total + ref[...].astype(F32)
    return total


def finish_body(layout, turned, *refs):
    count = sum(len(terms) for side in layout for terms in side)
    ins, outs = list(refs[:count]), refs[count:]
    wide = ins[0].shape[1] // len(outs)
    for c, side in enumerate(layout):
        sums = []
        for terms in side:
            sums.append(add_terms([ins.pop(0) for _ in terms]))
        total = jnp.concatenate(sums, axis=0) if len(sums) > 1 else sums[0]
        for t, ref in enumerate(outs):
            part = total[:, t * wide : (t + 1) * wide]
            ref[c] = part.T if t == turned else part


def finish(sides, kinds):
    arrays = [a for side in sides for terms in side for a in terms]
    own = sum(terms[0].shape[0] for terms in sides[0])
    wide = arrays[0].shape[1] // kinds
    shapes = [(len(sides), own, wide)] * (kinds - 1) + [(len(sides), wide, own)]
    layout = [[[0] * len(terms) for terms in side] for side in sides]
    return kernel_call(
        functools.partial(finish_body, layout, kinds - 1),
        (1,),
        arrays,
        [whole(a.shape) for a in arrays],
        [out_of(s, F32) for s in shapes],
        [whole(s) for s in shapes],
        0,
    )


class Ring:
    def __init__(self, size):
        self.size = size
        self.rings = size <= 16
        half = size // 2
        order = [2 * q for q in range(half)] + [2 * (size - 1 - q) + 1 for q in range(half, size)]
        self.ahead = [(order[q], order[(q + 1) % size]) for q in range(size)]
        self.behind = [(b, a) for a, b in self.ahead]
        self.me = lax.axis_index("dp")
        place = jnp.where(self.me % 2 == 0, self.me // 2, size - 1 - self.me // 2)
        q = lax.rem(place + jnp.arange(size, dtype=jnp.int32), size)
        self.order = jnp.where(q < half, 2 * q, 2 * (size - 1 - q) + 1).astype(jnp.int32)


class Rounds:
    def __init__(self):
        self.done = ()

    def now(self, value):
        return lax.optimization_barrier((value, *self.done))[0] if self.done else value

    def close(self, *arrays):
        self.done = arrays


class Gather:
    def __init__(self, rounds, ring, first, second):
        self.rounds, self.ring, self.a, self.b = rounds, ring, [first], [second]

    def step(self):
        self.a.append(lax.ppermute(self.rounds.now(self.a[-1]), "dp", self.ring.ahead))
        self.b.append(lax.ppermute(self.rounds.now(self.b[-1]), "dp", self.ring.behind))
        return self.a[-1], self.b[-1]

    def slots(self):
        return [self.a[-t % self.ring.size] for t in range(self.ring.size)], self.b


class Scatter:
    def __init__(self, rounds, ring, first, second):
        self.rounds, self.ring, self.first, self.second = rounds, ring, first, second
        self.a, self.b = first[-1], second[1]
        self.k = 1

    def step(self):
        n = self.ring.size
        self.k += 1
        if self.k > 2:
            self.a = (self.a.astype(F32) + self.first[n - self.k + 1].astype(F32)).astype(BF)
            self.b = (self.b.astype(F32) + self.second[self.k - 1].astype(F32)).astype(BF)
        self.a = lax.ppermute(self.rounds.now(self.a), "dp", self.ring.ahead)
        self.b = lax.ppermute(self.rounds.now(self.b), "dp", self.ring.behind)
        return self.a, self.b

    def sums(self):
        return [self.a, self.first[0]], [self.b, self.second[0]]


class HeadSum:
    def __init__(self, rounds, pair):
        size = lax.axis_size("mp")
        self.rounds, self.pair = rounds, pair
        self.near_moves = [(i, i ^ 1) for i in range(size)]
        self.far_moves = [(i, i ^ 2) for i in range(size)]

    def add(self, one, two):
        return (one.astype(F32) + two.astype(F32)).astype(BF)

    def near(self):
        got = lax.ppermute(self.rounds.now(self.pair[1]), "mp", self.near_moves)
        self.mine = self.add(self.pair[0], got)
        return self.mine

    def far(self):
        self.got = lax.ppermute(self.rounds.now(self.mine), "mp", self.far_moves)
        return self.got

    def last(self):
        self.mine = self.add(self.mine, self.rounds.now(self.got))
        self.sum = (self.mine, lax.ppermute(self.mine, "mp", self.near_moves))
        return self.sum[1]


def exchange_steps(axes):
    for axis in axes:
        size, step = lax.axis_size(axis), 1
        while step < size:
            yield axis, [(i, i ^ step) for i in range(size)], step
            step *= 2


def on_device(
    layer_input, frame_mask, gain_attn, w_query, w_key, w_value, w_out, gain_ffn, w_gate, w_up,
    w_down, cotangent,
):
    sets, width = gain_attn.shape[0], layer_input.shape[2]
    shape = layer_input.shape
    each = shape[1] // sets
    ring = Ring(lax.axis_size("dp"))
    rings, n = ring.rings, ring.size
    own = width // n
    places = jnp.concatenate([ring.order, (lax.axis_index("mp") % 2).astype(jnp.int32)[None]])
    gather = lambda value: lax.all_gather(value, "dp", tiled=True)
    scatter = lambda value: [[lax.psum_scatter(value, "dp", scatter_dimension=0, tiled=True)]]
    rounds = Rounds()
    now, close = rounds.now, rounds.close

    first, second = pack_attn(w_query, w_key, w_value, w_out)
    small = jnp.concatenate([gain_attn, gain_ffn], 0).astype(F32)[None]
    steps = list(exchange_steps(("dp",)))
    pack, x, g = [], [], []

    def gain_step(value):
        axis, moves, step = steps.pop(0)
        other = lax.ppermute(now(value), axis, moves)
        bit = (ring.me // step) % 2
        both = [jnp.concatenate(pair, 0) for pair in ((value, other), (other, value))]
        return jnp.where(bit == 0, *both)

    masks = frame_mask.astype(BF)[:, None, None]
    chores = [
        lambda: pack.append(pack_ffn(now(w_gate), w_up, w_down, 0)),
        lambda: pack.append(pack_ffn(now(w_gate), w_up, w_down, 1)),
        lambda: x.append(split_sets(now(layer_input), sets)[0]),
        lambda: x.append(split_sets(now(layer_input), sets)[1]),
        lambda: g.append(split_sets(now(cotangent) * masks, sets)[0]),
        lambda: g.append(split_sets(now(cotangent) * masks, sets)[1]),
        lambda: None,
    ]
    chores.pop(0)()
    attn = Gather(rounds, ring, first, second)
    rows = [Gather(rounds, ring, *pack[0])]
    for chore in chores:
        moved = (*attn.step(), *rows[0].step()) if rings else ()
        chore()
        if steps:
            small = gain_step(small)
        held = [v[-1] if not isinstance(v[-1], (list, tuple)) else v[-1][0] for v in (pack, x, g) if v]
        close(small, *held, *moved)
    while steps:
        small = gain_step(small)
    if rings:
        close(*attn.step(), *rows[0].step())
        rows.append(Gather(rounds, ring, *pack[1]))
        move = rows[1].step
    else:
        move = lambda: ()
    gains = small.transpose(1, 0, 2).reshape(2 * sets, width)
    g_attn, g_ffn = [[gains[k * sets + c][None] for c in range(sets)] for k in range(2)]
    w_attn = list(attn.slots()) if rings else [[gather(first)], [gather(second)]]
    w_ffn = [None if rings else [gather(jnp.concatenate(p, 0))] for p in pack]

    def take(c):
        if rings:
            a, b = rows[c].slots()
            w_ffn[c] = [piece for pair in zip(a, b) for piece in pair]

    take(0)
    h1, qkv, mixed, heads = [None] * 2, [None] * 2, [None] * 2, [None] * 2
    moved = move()
    h1[0], qkv[0], mixed[0], part = attend(now(places), x[0], g_attn[0], None, w_attn[0], each)
    heads[0] = HeadSum(rounds, part)
    close(*moved, part[0])
    close(heads[0].near())
    moved = move()
    heads[0].far()
    h1[1], qkv[1], mixed[1], part = attend(now(places), x[1], g_attn[1], qkv[0], w_attn[1], each)
    heads[1] = HeadSum(rounds, part)
    close(*moved, part[0])
    moved = move()
    close(*moved, heads[1].near())
    moved = move()
    heads[1].far()
    close(*moved, heads[0].got)
    close(heads[0].last())

    def grads_of(c, out):
        columns = [(out[0], out[2]), (out[0], out[3]), (g[c], out[1])]
        return weight_grads(now(places), columns, 2 if rings else 0)

    dh, mlp, grads, dm, d_gain_ffn = ([None] * 2 for _ in range(5))
    moved = move()
    out = hidden_units(now(places), x[0], heads[0].sum, g[0], g_ffn[0], w_ffn[0])
    dh[0], mlp[0] = HeadSum(rounds, out[4]), HeadSum(rounds, out[5])
    close(*moved, out[0], heads[1].got)
    moved = move()
    close(dh[0].near(), heads[1].last())
    att = [head.sum for head in heads]
    dh[0].far()
    grads[0] = grads_of(0, out)
    close(*moved, grads[0][0])
    close(*move(), mlp[0].near())
    take(1)
    if rings:
        sums = [Scatter(rounds, ring, grads[0][0::2], grads[0][1::2])]
        move = lambda: sum((s.step() for s in sums if s.k < n), ())
    moved = move()
    out = hidden_units(now(places), x[1], att[1], g[1], g_ffn[1], w_ffn[1])
    dh[1], mlp[1] = HeadSum(rounds, out[4]), HeadSum(rounds, out[5])
    close(*moved, out[0], dh[0].got)
    moved = move()
    close(dh[1].near(), dh[0].last())
    dh[1].far()
    grads[1] = grads_of(1, out)
    close(*moved, grads[1][0], mlp[1].near())
    if rings:
        sums.append(Scatter(rounds, ring, grads[1][0::2], grads[1][1::2]))
    moved = move()
    dm[0], d_gain_ffn[0] = middle_back(now(places), x[0], att[0], g[0], dh[0].sum, g_ffn[0])
    close(*moved, dm[0], dh[1].got)
    mlp[0].far()
    moved = move()
    close(dh[1].last())
    dm[1], d_gain_ffn[1] = middle_back(now(places), x[1], att[1], g[1], dh[1].sum, g_ffn[1])
    close(*moved, dm[1])

    moved = move()
    d_qkv, part, d_gain0 = attend_back(now(places), x, dm, qkv, w_attn, 0, None, each)
    back = [HeadSum(rounds, part)]
    close(*moved, part[0], mlp[0].got)
    close(back[0].near(), mlp[0].last())
    moved = move()
    back[0].far()
    d_qkv, part, d_gain1 = attend_back(now(places), x, dm, qkv, w_attn, 1, d_qkv, each)
    back.append(HeadSum(rounds, part))
    close(*moved, part[0], back[0].got)
    close(back[1].near())
    moved = move()
    back[1].far()
    sides = [
        weight_grads(now(places), [(h1[c], d_qkv[c]), (dm[c], mixed[c])], 1 if rings else 0)
        for c in range(sets)
    ]
    close(*moved, *[side[0] for side in sides], back[0].last())
    if rings:
        sums.append(Scatter(rounds, ring, *sides))
    shared = lax.axis_size("mp")
    d_gains = jnp.concatenate([d_gain0 + d_gain1, *[d / shared for d in d_gain_ffn]], 0)
    steps = list(exchange_steps(("dp", "mp")))

    def sum_step(value):
        axis, moves, _ = steps.pop(0)
        return value + lax.ppermute(now(value), axis, moves)

    gain = gains[:sets]
    moved = move()
    d_gains = sum_step(d_gains)
    mlp[1].far()
    grad_input = input_back(now(places), x, dm, back[0].sum, gain, 0, None, shape)
    close(*moved, grad_input, d_gains, back[1].got)
    moved = move()
    d_gains = sum_step(d_gains)
    close(*moved, back[1].last(), d_gains)
    moved = move()
    d_gains = sum_step(d_gains)
    grad_input = input_back(now(places), x, dm, back[1].sum, gain, 1, grad_input, shape)
    close(*moved, grad_input, d_gains, mlp[1].got)
    moved = move()
    d_gains = sum_step(d_gains)
    close(*moved, mlp[1].last(), d_gains)
    moved = move()
    output = output_of(now(places), x, att, [m.sum for m in mlp], shape)
    d_gains = sum_step(d_gains)
    close(*moved, output, d_gains)
    moved = move()
    if rings:
        ffn_sums = [list(s.sums()) for s in sums[:2]]
    else:
        ffn_sums = [scatter(g_[0]) for g_ in grads]
    d_gate_w, d_up_w, d_down_w = finish([[[now(t) for t in run] for run in side] for side in ffn_sums], 3)
    close(*moved, d_gate_w)
    moved = move()
    while steps:
        d_gains = sum_step(d_gains)
    attn_sums = [[run] for run in sums[2].sums()] if rings else [scatter(side[0]) for side in sides]
    d_query, d_key, d_value, d_out = finish(attn_sums, 4)
    d_gains = lax.dynamic_slice_in_dim(d_gains, ring.me * own, own, 1)
    return (
        output, grad_input, d_gains[:sets], d_query, d_key, d_value, d_out,
        d_gains[sets:], d_gate_w, d_up_w, d_down_w,
    )


def solution(mesh):
    rows = P("dp", None, None)
    gain = P(None, "dp")
    into = P(None, "dp", "mp")
    back = P(None, "mp", "dp")
    weights = (gain, into, into, into, back, gain, into, into, back)
    return jax.shard_map(
        on_device,
        mesh=mesh,
        in_specs=(rows, P("dp"), *weights, rows),
        out_specs=(rows, rows, *weights),
        check_vma=False,
    )
```

time: 651 us -> 529 us (0.81)
  blocking collectives: 39.6 us -> 0 us
  waiting for transfers between devices: 202 us -> 170 us
  Pallas kernels: 225 us -> 206 us
  starting transfers between devices: 126 us -> 109 us
  other arithmetic: 34.3 us -> 18.1 us
    psum x1 -> x0, blocking collectives: 39.6 us -> none  [on_device(): d_gains = lax.psum(d_gains.reshape(2 * sets, width), ('dp', 'mp'))]
    ppermute x111 -> x116, waiting for transfers between devices: 202 us -> 170 us  [the longest x21 48.7 us: step(): lax.ppermute(self.rounds.now(self.a[-1]), 'dp', self.ring.ahead)]
    pallas_call x28 -> x20, Pallas kernels: 225 us -> 206 us  [kernel_call(): pl.pallas_call(body, grid_spec=spec, out_shape=outs, input_output_aliases...]
    ppermute x111 -> x116, starting transfers between devices: 126 us -> 109 us  [the longest x21 26.7 us: step(): lax.ppermute(self.rounds.now(self.a[-1]), 'dp', self.ring.ahead)]
    convert_element_type x53 -> x52, other arithmetic: 31.1 us -> 14.8 us  [the longest x16 8.84 us: add(): return (one.astype(F32) + two.astype(F32)).astype(BF)]
    another operation x0 -> x4, local copies, waits for them, and re-layouts: none -> 7.83 us  [split_sets(): return [parts[:, c].reshape(-1, width) for c in range(sets)]]
  transfers between devices with their start and end apart: 111 -> 116, of which waited for: 43 -> 56; matrix products, arithmetic and copies ran while one was open for 6% -> 5% of each run, Pallas kernels for 34% -> 39%
where the time goes in v3:
time: 529 us; the launch traced here: 519 us
  Pallas kernels  206 us (39%)
  waiting for transfers between devices  170 us (32%)
  starting transfers between devices  109 us (21%)
  other arithmetic  18.1 us (3%)
  local copies, waits for them, and re-layouts  13.2 us (2%)
    pallas_call x20, Pallas kernels, kernel_call(): pl.pallas_call(body, grid_spec=spec, out_shape=outs, input_output_aliases...  206 us
    ppermute x21, waiting for transfers between devices, step(): lax.ppermute(self.rounds.now(self.a[-1]), 'dp', self.ring.ahead)  48.7 us
    ppermute x21, waiting for transfers between devices, step(): self.a = lax.ppermute(self.rounds.now(self.a), 'dp', self.ring.ahead)  40 us
    ppermute x21, waiting for transfers between devices, step(): lax.ppermute(self.rounds.now(self.b[-1]), 'dp', self.ring.behind)  32.4 us
    ppermute x21, starting transfers between devices, step(): lax.ppermute(self.rounds.now(self.a[-1]), 'dp', self.ring.ahead)  26.7 us
    ppermute x21, starting transfers between devices, step(): self.a = lax.ppermute(self.rounds.now(self.a), 'dp', self.ring.ahead)  22 us
    ppermute x21, starting transfers between devices, step(): self.b = lax.ppermute(self.rounds.now(self.b), 'dp', self.ring.behind)  21.2 us
    ppermute x21, starting transfers between devices, step(): lax.ppermute(self.rounds.now(self.b[-1]), 'dp', self.ring.behind)  15.3 us
  transfers between devices with their start and end apart: 116, of which 56 were waited for; matrix products, arithmetic and copies ran while one was open for 5% of the time, Pallas kernels for 39%

profile of v3, /device:TPU:0, one launch (start us, length us, event | category | flops | bytes accessed | tf_op | source)
XLA Modules:
  0.0 519.4 jit_solution(3336008590278397305)
XLA Ops:
  0.7 2.2 shard_map.205
  2.8 3.0 collective-permute-start.3
  5.9 2.0 shard_map.203
  7.8 2.0 collective-permute-start
  9.9 2.0 collective-permute-start.1
  11.9 2.1 shard_map.204
  14.0 6.7 %collective-permute-done.1 = f32[1,4,128]{2,1,0:T(4,128)S(1)} collective-permute-done((f32[1,4,128]{2,1,0:T(4,128)S(1)}, f32[1,4,128]{2,1,0:T(4,128)S(1)}, u32[]{:S(2)}, u32[]{:S(2)}) %collective-permute-start.1) | collective-permute-done | bytes 2080 | tf_op jit(solution)/shard_map/ppermute | solution.py:726
  25.5 2.0 collective-permute-start.8
  27.5 3.2 slice_bitcast_fusion.3.refs_0_.x_ref.x0
  31.6 3.2 collective-permute-done.7.refs_5_.refs_10_
  34.7 2.9 collective-permute-done.8.refs_17_
  37.6 2.6 collective-permute-done.9.refs_10_
  40.7 2.6 collective-permute-start.11
  43.3 2.0 collective-permute-start.13
  47.6 1.9 collective-permute-done.10.refs_7_.refs_5_
  49.5 2.9 collective-permute-done.12.refs_6_.refs_11_
  54.1 3.5 collective-permute-done.14.refs_12_
  57.7 2.0 collective-permute-start.16
  59.7 2.0 collective-permute-start.18
  66.5 2.8 collective-permute-done.17.refs_13_
  69.3 3.0 collective-permute-done.18.refs_14_
  74.8 2.0 collective-permute-start.20
  78.9 8.8 %collective-permute-done.20.refs_8_.refs_13_ = bf16[128,1024]{1,0:T(8,128)(2,1)S(1)} collective-permute-done((bf16[128,1024]{1,0:T(8,128)(2,1)S(1)}, bf16[128,1024]{1,0:T(8,128)(2,1)S(1)}, u32[]{:S(2)}, u32[]{:S(2)}) %collective-permute-start.20) | collective-permute-done | bytes 262176 | tf_op jit(solution)/shard_map/ppermute | solution.py:643
  87.9 1.9 collective-permute-start.26
  91.8 9.9 %collective-permute-done.23.refs_4_.refs_2_ = bf16[128,1024]{1,0:T(8,128)(2,1)S(1)} collective-permute-done((bf16[128,1024]{1,0:T(8,128)(2,1)S(1)}, bf16[128,1024]{1,0:T(8,128)(2,1)S(1)}, u32[]{:S(2)}, u32[]{:S(2)}) %collective-permute-start.23) | collective-permute-done | bytes 262176 | tf_op jit(solution)/shard_map/ppermute | solution.py:642
  106.4 10.7 %collective-permute-done.27.refs_3_.refs_1_ = bf16[128,1024]{1,0:T(8,128)(2,1)S(1)} collective-permute-done((bf16[128,1024]{1,0:T(8,128)(2,1)S(1)}, bf16[128,1024]{1,0:T(8,128)(2,1)S(1)}, u32[]{:S(2)}, u32[]{:S(2)}) %collective-permute-start.27) | collective-permute-done | bytes 262176 | tf_op jit(solution)/shard_map/ppermute | solution.py:642
  118.5 2.1 collective-permute-start.31
  123.0 14.2 %shard_map.206 = (bf16[1024,1024]{1,0:T(8,128)(2,1)}, bf16[1024,768]{1,0:T(8,128)(2,1)}, bf16[1024,256]{1,0:T(8,128)(2,1)}, bf16[512,1024]{1,0:T(8,128)(2,1)}, bf16[512,1024]{1,0:T(8,128)(2,1)}) custom-call(s32[9]{0:T(128)} %pad_add_fusion.places._, bf16[1024,1024]{1,0:T(8,128)(2,1)} %slice_bitcast_fusion.3.refs_0_.x_ref.x0, ...), custom_call_target="tpu_custom_call" | custom-call | flops 1 | bytes 1 | tf_op jit(solution)/shard_map/pallas_call | solution.py:41
  137.3 2.9 collective-permute-done.33
  141.8 2.1 collective-permute-start.35
  143.9 13.2 %shard_map.207 = (bf16[1024,1024]{1,0:T(8,128)(2,1)}, bf16[1024,768]{1,0:T(8,128)(2,1)}, bf16[1024,256]{1,0:T(8,128)(2,1)}, bf16[512,1024]{1,0:T(8,128)(2,1)}, bf16[512,1024]{1,0:T(8,128)(2,1)}) custom-call(s32[9]{0:T(128)} %pad_add_fusion.places._, bf16[1024,1024]{1,0:T(8,128)(2,1)} %slice_bitcast_fusion.2.refs_0_.x_ref.x1, ...), custom_call_target="tpu_custom_call" | custom-call | flops 1 | bytes 1 | tf_op jit(solution)/shard_map/pallas_call | solution.py:41
  158.7 2.0 collective-permute-start.37
  162.4 7.5 %collective-permute-done.37.refs_15_ = bf16[64,3072]{1,0:T(8,128)(2,1)S(1)} collective-permute-done((bf16[64,3072]{1,0:T(8,128)(2,1)S(1)}, bf16[64,3072]{1,0:T(8,128)(2,1)S(1)}, u32[]{:S(2)}, u32[]{:S(2)}) %collective-permute-start.37) | collective-permute-done | bytes 393248 | tf_op jit(solution)/shard_map/ppermute | solution.py:642
  173.7 9.1 %collective-permute-done.34 = bf16[512,1024]{1,0:T(8,128)(2,1)S(1)} collective-permute-done((bf16[512,1024]{1,0:T(8,128)(2,1)S(1)}, bf16[512,1024]{1,0:T(8,128)(2,1)S(1)}, u32[]{:S(2)}, u32[]{:S(2)}) %collective-permute-start.34) | collective-permute-done | bytes 1048608 | tf_op jit(solution)/shard_map/ppermute | solution.py:686
  186.0 2.0 collective-permute-start.43
  188.2 25.7 %shard_map.208 = (bf16[1024,1024]{1,0:T(8,128)(2,1)}, bf16[1024,1024]{1,0:T(8,128)(2,1)}, bf16[1024,1024]{1,0:T(8,128)(2,1)}, bf16[1024,1024]{1,0:T(8,128)(2,1)}...) custom-call(s32[9]{0:T(128)} %pad_add_fusion.places._, ...), custom_call_target="tpu_custom_call" | custom-call | flops 1 | bytes 1 | tf_op jit(solution)/shard_map/pallas_call | solution.py:41
  215.1 2.0 collective-permute-start.48
  218.3 13.9 %shard_map.209 = (bf16[64,3072]{1,0:T(8,128)(2,1)}, bf16[64,3072]{1,0:T(8,128)(2,1)}, bf16[64,3072]{1,0:T(8,128)(2,1)}, bf16[64,3072]{1,0:T(8,128)(2,1)}, bf16[6...) custom-call(s32[9]{0:T(128)} %pad_add_fusion.places._, ...), custom_call_target="tpu_custom_call" | custom-call | flops 1 | bytes 1 | tf_op jit(solution)/shard_map/pallas_call | solution.py:41
  233.9 2.0 collective-permute-start.50
  236.4 8.7 %collective-permute-done.50.refs_7_ = bf16[64,3072]{1,0:T(8,128)(2,1)S(1)} collective-permute-done((bf16[64,3072]{1,0:T(8,128)(2,1)S(1)}, bf16[64,3072]{1,0:T(8,128)(2,1)S(1)}, u32[]{:S(2)}, u32[]{:S(2)}) %collective-permute-start.50) | collective-permute-done | bytes 393248 | tf_op jit(solution)/shard_map/ppermute | solution.py:642
  249.1 25.7 %shard_map.210 = (bf16[1024,1024]{1,0:T(8,128)(2,1)}, bf16[1024,1024]{1,0:T(8,128)(2,1)}, bf16[1024,1024]{1,0:T(8,128)(2,1)}, bf16[1024,1024]{1,0:T(8,128)(2,1)}...) custom-call(s32[9]{0:T(128)} %pad_add_fusion.places._, ...), custom_call_target="tpu_custom_call" | custom-call | flops 1 | bytes 1 | tf_op jit(solution)/shard_map/pallas_call | solution.py:41
  279.7 7.4 %collective-permute-done.56 = bf16[64,3072]{1,0:T(8,128)(2,1)S(1)} collective-permute-done((bf16[64,3072]{1,0:T(8,128)(2,1)S(1)}, bf16[64,3072]{1,0:T(8,128)(2,1)S(1)}, u32[]{:S(2)}, u32[]{:S(2)}) %collective-permute-start.56) | collective-permute-done | bytes 393248 | tf_op jit(solution)/shard_map/ppermute | solution.py:662
  287.9 13.8 %shard_map.211 = (bf16[64,3072]{1,0:T(8,128)(2,1)}, bf16[64,3072]{1,0:T(8,128)(2,1)}, bf16[64,3072]{1,0:T(8,128)(2,1)}, bf16[64,3072]{1,0:T(8,128)(2,1)}, bf16[6...) custom-call(s32[9]{0:T(128)} %pad_add_fusion.places._, ...), custom_call_target="tpu_custom_call" | custom-call | flops 1 | bytes 1 | tf_op jit(solution)/shard_map/pallas_call | solution.py:41
  306.4 7.4 %shard_map.212 = (bf16[1024,1024]{1,0:T(8,128)(2,1)}, f32[1,1024]{1,0:T(1,128)}) custom-call(s32[9]{0:T(128)} %pad_add_fusion.places._, bf16[1024,1024]{1,0:T(8,128)(2,1)} %slice_bitcast_fusion.3.refs_0_.x_ref.x0, bf16[512,1024]{1,0:T(8,128)(2,1)} %copy-done.1, bf16[512,1024]{1,0:T(8,128)(2,1)} %copy-done.3, ...), custom_call_target="tpu_custom_call" | custom-call | flops 1 | bytes 1 | tf_op jit(solution)/shard_map/pallas_call | solution.py:41
  315.1 5.4 %collective-permute-done.63 = bf16[64,3072]{1,0:T(8,128)(2,1)S(1)} collective-permute-done((bf16[64,3072]{1,0:T(8,128)(2,1)}, bf16[64,3072]{1,0:T(8,128)(2,1)S(1)}, u32[]{:S(2)}, u32[]{:S(2)}) %collective-permute-start.63) | collective-permute-done | bytes 393248 | tf_op jit(solution)/shard_map/ppermute | solution.py:662
  326.4 6.8 %collective-permute-done.66 = bf16[64,3072]{1,0:T(8,128)(2,1)S(1)} collective-permute-done((bf16[64,3072]{1,0:T(8,128)(2,1)S(1)}, bf16[64,3072]{1,0:T(8,128)(2,1)S(1)}, u32[]{:S(2)}, u32[]{:S(2)}) %collective-permute-start.66) | collective-permute-done | bytes 393248 | tf_op jit(solution)/shard_map/ppermute | solution.py:662
  335.2 3.2 collective-permute-done.68
  341.1 7.3 %shard_map.213 = (bf16[1024,1024]{1,0:T(8,128)(2,1)}, f32[1,1024]{1,0:T(1,128)}) custom-call(s32[9]{0:T(128)} %pad_add_fusion.places._, bf16[1024,1024]{1,0:T(8,128)(2,1)} %slice_bitcast_fusion.2.refs_0_.x_ref.x1, bf16[512,1024]{1,0:T(8,128)(2,1)} %copy-done.2, bf16[512,1024]{1,0:T(8,128)(2,1)} %copy-done.4, ...), custom_call_target="tpu_custom_call" | custom-call | flops 1 | bytes 1 | tf_op jit(solution)/shard_map/pallas_call | solution.py:41
  352.4 18.1 %shard_map.214 = (bf16[1024,768]{1,0:T(8,128)(2,1)}, bf16[1024,768]{1,0:T(8,128)(2,1)}, bf16[512,1024]{1,0:T(8,128)(2,1)}, bf16[512,1024]{1,0:T(8,128)(2,1)}, f32[2,1024]{1,0:T(2,128)}) custom-call(s32[9]{0:T(128)} %pad_add_fusion.places._, bf16[1024,1024]{1,0:T(8,128)(2,1)} %slice_bitcast_fusion.3.refs_0_.x_ref.x0, ...), custom_call_target="tpu_custom_call" | custom-call | flops 1 | bytes 1 | tf_op jit(solution)/shard_map/pallas_call | solution.py:41
  382.9 18.3 %shard_map.215 = (bf16[1024,768]{1,0:T(8,128)(2,1)}, bf16[1024,768]{1,0:T(8,128)(2,1)}, bf16[512,1024]{1,0:T(8,128)(2,1)}, bf16[512,1024]{1,0:T(8,128)(2,1)}, f32[2,1024]{1,0:T(2,128)}) custom-call(s32[9]{0:T(128)} %pad_add_fusion.places._, bf16[1024,1024]{1,0:T(8,128)(2,1)} %slice_bitcast_fusion.3.refs_0_.x_ref.x0, ...), custom_call_target="tpu_custom_call", output_to_operand_aliasing={{0}: (23, {}), {1}: (24, {})} | custom-call | flops 1 | bytes 1 | tf_op jit(solution)/shard_map/pallas_call | solution.py:41
  409.5 7.5 %shard_map.216 = (bf16[128,1024]{1,0:T(8,128)(2,1)}, bf16[128,1024]{1,0:T(8,128)(2,1)}, bf16[128,1024]{1,0:T(8,128)(2,1)}, bf16[128,1024]{1,0:T(8,128)(2,1)}, bf...) custom-call(s32[9]{0:T(128)} %pad_add_fusion.places._, ...), custom_call_target="tpu_custom_call" | custom-call | flops 1 | bytes 1 | tf_op jit(solution)/shard_map/pallas_call | solution.py:41
  417.0 7.6 %shard_map.217 = (bf16[128,1024]{1,0:T(8,128)(2,1)}, bf16[128,1024]{1,0:T(8,128)(2,1)}, bf16[128,1024]{1,0:T(8,128)(2,1)}, bf16[128,1024]{1,0:T(8,128)(2,1)}, bf...) custom-call(s32[9]{0:T(128)} %pad_add_fusion.places._, ...), custom_call_target="tpu_custom_call" | custom-call | flops 1 | bytes 1 | tf_op jit(solution)/shard_map/pallas_call | solution.py:41
  432.5 6.2 %shard_map.218.refs_0_ = bf16[128,16,1024]{2,1,0:T(8,128)(2,1)} custom-call(s32[9]{0:T(128)} %pad_add_fusion.places._, bf16[1024,1024]{1,0:T(8,128)(2,1)} %slice_bitcast_fusion.3.refs_0_.x_ref.x0, bf16[1024,1024]{1,0:T(8,128)(2,1)} %slice_bitcast_fusion.2.refs_0_.x_ref.x1, bf16[1024,1024]{1,0:T(8,128)(2,1)} %get-tuple-element.358.dm0.refs_2_.refs_3_, ...), custom_call_target="tpu_custom_call" | custom-call | flops 1 | bytes 1 | tf_op jit(solution)/shard_map/pallas_call | solution.py:41
  440.8 5.9 %collective-permute-done.92 = bf16[128,1024]{1,0:T(8,128)(2,1)S(1)} collective-permute-done((bf16[128,1024]{1,0:T(8,128)(2,1)S(1)}, bf16[128,1024]{1,0:T(8,128)(2,1)S(1)}, u32[]{:S(2)}, u32[]{:S(2)}) %collective-permute-start.92) | collective-permute-done | bytes 262176 | tf_op jit(solution)/shard_map/ppermute | solution.py:663
  446.8 4.0 collective-permute-done.94
  454.7 3.9 collective-permute-done.100
  458.9 2.1 collective-permute-start.97
  461.1 7.1 %collective-permute-done.96.refs_4_ = bf16[64,3072]{1,0:T(8,128)(2,1)S(1)} collective-permute-done((bf16[64,3072]{1,0:T(8,128)(2,1)S(1)}, bf16[64,3072]{1,0:T(8,128)(2,1)S(1)}, u32[]{:S(2)}, u32[]{:S(2)}) %collective-permute-start.96) | collective-permute-done | bytes 393248 | tf_op jit(solution)/shard_map/ppermute | solution.py:662
  472.2 6.2 %shard_map.219 = bf16[128,16,1024]{2,1,0:T(8,128)(2,1)} custom-call(s32[9]{0:T(128)} %pad_add_fusion.places._, bf16[1024,1024]{1,0:T(8,128)(2,1)} %slice_bitcast_fusion.3.refs_0_.x_ref.x0, bf16[1024,1024]{1,0:T(8,128)(2,1)} %slice_bitcast_fusion.2.refs_0_.x_ref.x1, ...), custom_call_target="tpu_custom_call", output_to_operand_aliasing={{}: (8, {})} | custom-call | flops 1 | bytes 1 | tf_op jit(solution)/shard_map/pallas_call | solution.py:41
  482.8 5.0 collective-permute-done.105
  491.6 8.5 %shard_map.220 = bf16[128,16,1024]{2,1,0:T(8,128)(2,1)} custom-call(s32[9]{0:T(128)} %pad_add_fusion.places._, bf16[1024,1024]{1,0:T(8,128)(2,1)} %slice_bitcast_fusion.3.refs_0_.x_ref.x0, bf16[1024,1024]{1,0:T(8,128)(2,1)} %slice_bitcast_fusion.2.refs_0_.x_ref.x1, bf16[512,1024]{1,0:T(8,128)(2,1)} %copy-done.1, bf16[512,1024]{1,0:T(8,128)(2,1)} %copy-done.3, ...), custom_call_target="tpu_custom_call" | custom-call | flops 1 | bytes 1 | tf_op jit(solution)/shard_map/pallas_call | solution.py:41
  502.5 3.9 shard_map.221
  511.3 3.6 collective-permute-done.114.refs_0_
  516.8 2.2 shard_map.222
  (501 shorter events, 131.8 us)
Async XLA Ops:
  2.8 19.4 %collective-permute-start.3 = (bf16[64,3072]{1,0:T(8,128)(2,1)}, bf16[64,3072]{1,0:T(8,128)(2,1)S(1)}, u32[]{:S(2)}, u32[]{:S(2)}) collective-permute-start(bf16[64,3072]{1,0:T(8,128)(2,1)} %get-tuple-element.252.refs_5_), channel_id=1, source_target_pairs={{0,8},{8,16},{16,24},{24,28},{28,20},{20,12},{12,4},{4,0},{1,9},{9... | collective-permute-start | bytes 1179656 | tf_op jit(solution)/shard_map/ppermute | solution.py:642
  5.9 16.4 %collective-permute-start.4 = (bf16[64,3072]{1,0:T(8,128)(2,1)}, bf16[64,3072]{1,0:T(8,128)(2,1)S(1)}, u32[]{:S(2)}, u32[]{:S(2)}) collective-permute-start(bf16[64,3072]{1,0:T(8,128)(2,1)} %get-tuple-element.253.refs_6_), channel_id=1, source_target_pairs={{8,0},{16,8},{24,16},{28,24},{20,28},{12,20},{4,12},{0,4},{9,1},{1... | collective-permute-start | bytes 1179656 | tf_op jit(solution)/shard_map/ppermute | solution.py:643
  7.8 13.0 %collective-permute-start = (bf16[128,1024]{1,0:T(8,128)(2,1)}, bf16[128,1024]{1,0:T(8,128)(2,1)S(1)}, u32[]{:S(2)}, u32[]{:S(2)}) collective-permute-start(bf16[128,1024]{1,0:T(8,128)(2,1)} %get-tuple-element.249.refs_2_.refs_0_), channel_id=1, source_target_pairs={{0,8},{8,16},{16,24},{24,28},{28,20},{20,12},{12,4},{4,0},{1,9},{9... | collective-permute-start | bytes 786440 | tf_op jit(solution)/shard_map/ppermute | solution.py:642
  9.9 12.4 %collective-permute-start.2 = (bf16[128,1024]{1,0:T(8,128)(2,1)}, bf16[128,1024]{1,0:T(8,128)(2,1)S(1)}, u32[]{:S(2)}, u32[]{:S(2)}) collective-permute-start(bf16[128,1024]{1,0:T(8,128)(2,1)} %get-tuple-element.251.refs_3_.refs_8_), channel_id=1, source_target_pairs={{8,0},{16,8},{24,16},{28,24},{20,28},{12,20},{4,12},{0,4},{9,1},{1... | collective-permute-start | bytes 786440 | tf_op jit(solution)/shard_map/ppermute | solution.py:643
  25.5 12.1 %collective-permute-start.8 = (bf16[64,3072]{1,0:T(8,128)(2,1)S(1)}, bf16[64,3072]{1,0:T(8,128)(2,1)S(1)}, u32[]{:S(2)}, u32[]{:S(2)}) collective-permute-start(bf16[64,3072]{1,0:T(8,128)(2,1)S(1)} %collective-permute-done.3.refs_19_), channel_id=1, source_target_pairs={{0,8},{8,16},{16,24},{24,28},{28,20},{20,12},{12,4},{4,0},{1,9},{9... | collective-permute-start | bytes 1179656 | tf_op jit(solution)/shard_map/ppermute | solution.py:642
  27.5 12.7 %collective-permute-start.9 = (bf16[64,3072]{1,0:T(8,128)(2,1)S(1)}, bf16[64,3072]{1,0:T(8,128)(2,1)S(1)}, u32[]{:S(2)}, u32[]{:S(2)}) collective-permute-start(bf16[64,3072]{1,0:T(8,128)(2,1)S(1)} %collective-permute-done.4.refs_8_), channel_id=1, source_target_pairs={{8,0},{16,8},{24,16},{28,24},{20,28},{12,20},{4,12},{0,4},{9,1},{1... | collective-permute-start | bytes 1179656 | tf_op jit(solution)/shard_map/ppermute | solution.py:643
  45.3 12.3 %collective-permute-start.14 = (bf16[64,3072]{1,0:T(8,128)(2,1)S(1)}, bf16[64,3072]{1,0:T(8,128)(2,1)S(1)}, u32[]{:S(2)}, u32[]{:S(2)}) collective-permute-start(bf16[64,3072]{1,0:T(8,128)(2,1)S(1)} %collective-permute-done.9.refs_10_), channel_id=1, source_target_pairs={{8,0},{16,8},{24,16},{28,24},{20,28},{12,20},{4,12},{0,4},{9,1},{1... | collective-permute-start | bytes 1179656 | tf_op jit(solution)/shard_map/ppermute | solution.py:643
  59.7 12.6 %collective-permute-start.18 = (bf16[64,3072]{1,0:T(8,128)(2,1)S(1)}, bf16[64,3072]{1,0:T(8,128)(2,1)S(1)}, u32[]{:S(2)}, u32[]{:S(2)}) collective-permute-start(bf16[64,3072]{1,0:T(8,128)(2,1)S(1)} %collective-permute-done.14.refs_12_), channel_id=1, source_target_pairs={{8,0},{16,8},{24,16},{28,24},{20,28},{12,20},{4,12},{0,4},{9,1},{1... | collective-permute-start | bytes 1179656 | tf_op jit(solution)/shard_map/ppermute | solution.py:643
  72.3 15.3 %collective-permute-start.21 = (bf16[64,3072]{1,0:T(8,128)(2,1)S(1)}, bf16[64,3072]{1,0:T(8,128)(2,1)S(1)}, u32[]{:S(2)}, u32[]{:S(2)}) collective-permute-start(bf16[64,3072]{1,0:T(8,128)(2,1)S(1)} %collective-permute-done.17.refs_13_), channel_id=1, source_target_pairs={{0,8},{8,16},{16,24},{24,28},{28,20},{20,12},{12,4},{4,0},{1,9},{9... | collective-permute-start | bytes 1179656 | tf_op jit(solution)/shard_map/ppermute | solution.py:642
  72.9 14.8 %collective-permute-start.22 = (bf16[64,3072]{1,0:T(8,128)(2,1)S(1)}, bf16[64,3072]{1,0:T(8,128)(2,1)S(1)}, u32[]{:S(2)}, u32[]{:S(2)}) collective-permute-start(bf16[64,3072]{1,0:T(8,128)(2,1)S(1)} %collective-permute-done.18.refs_14_), channel_id=1, source_target_pairs={{8,0},{16,8},{24,16},{28,24},{20,28},{12,20},{4,12},{0,4},{9,1},{1... | collective-permute-start | bytes 1179656 | tf_op jit(solution)/shard_map/ppermute | solution.py:643
  74.8 12.9 %collective-permute-start.20 = (bf16[128,1024]{1,0:T(8,128)(2,1)S(1)}, bf16[128,1024]{1,0:T(8,128)(2,1)S(1)}, u32[]{:S(2)}, u32[]{:S(2)}) collective-permute-start(bf16[128,1024]{1,0:T(8,128)(2,1)S(1)} %collective-permute-done.16.refs_7_.refs_12_), channel_id=1, source_target_pairs={{8,0},{16,8},{24,16},{28,24},{20,28},{12,20},{4,12},{0,4},{9,1},{1... | collective-permute-start | bytes 786440 | tf_op jit(solution)/shard_map/ppermute | solution.py:643
  87.7 14.6 %collective-permute-start.25 = (bf16[64,3072]{1,0:T(8,128)(2,1)S(1)}, bf16[64,3072]{1,0:T(8,128)(2,1)S(1)}, u32[]{:S(2)}, u32[]{:S(2)}) collective-permute-start(bf16[64,3072]{1,0:T(8,128)(2,1)S(1)} %collective-permute-done.21.refs_11_), channel_id=1, source_target_pairs={{0,8},{8,16},{16,24},{24,28},{28,20},{20,12},{12,4},{4,0},{1,9},{9... | collective-permute-start | bytes 1179656 | tf_op jit(solution)/shard_map/ppermute | solution.py:642
  87.9 14.5 %collective-permute-start.26 = (bf16[64,3072]{1,0:T(8,128)(2,1)S(1)}, bf16[64,3072]{1,0:T(8,128)(2,1)}, u32[]{:S(2)}, u32[]{:S(2)}) collective-permute-start(bf16[64,3072]{1,0:T(8,128)(2,1)S(1)} %collective-permute-done.22.refs_16_), channel_id=1, source_target_pairs={{8,0},{16,8},{24,16},{28,24},{20,28},{12,20},{4,12},{0,4},{9,1},{1... | collective-permute-start | bytes 1179656 | tf_op jit(solution)/shard_map/ppermute | solution.py:643
  89.9 12.4 %collective-permute-start.24 = (bf16[128,1024]{1,0:T(8,128)(2,1)S(1)}, bf16[128,1024]{1,0:T(8,128)(2,1)S(1)}, u32[]{:S(2)}, u32[]{:S(2)}) collective-permute-start(bf16[128,1024]{1,0:T(8,128)(2,1)S(1)} %collective-permute-done.20.refs_8_.refs_13_), channel_id=1, source_target_pairs={{8,0},{16,8},{24,16},{28,24},{20,28},{12,20},{4,12},{0,4},{9,1},{1... | collective-permute-start | bytes 786440 | tf_op jit(solution)/shard_map/ppermute | solution.py:643
  102.3 16.1 %collective-permute-start.29 = (bf16[64,3072]{1,0:T(8,128)(2,1)S(1)}, bf16[64,3072]{1,0:T(8,128)(2,1)}, u32[]{:S(2)}, u32[]{:S(2)}) collective-permute-start(bf16[64,3072]{1,0:T(8,128)(2,1)S(1)} %collective-permute-done.25.refs_9_), channel_id=1, source_target_pairs={{0,8},{8,16},{16,24},{24,28},{28,20},{20,12},{12,4},{4,0},{1,9},{9... | collective-permute-start | bytes 1179656 | tf_op jit(solution)/shard_map/ppermute | solution.py:642
  103.1 15.3 %collective-permute-start.30 = (bf16[64,3072]{1,0:T(8,128)(2,1)}, bf16[64,3072]{1,0:T(8,128)(2,1)}, u32[]{:S(2)}, u32[]{:S(2)}) collective-permute-start(bf16[64,3072]{1,0:T(8,128)(2,1)} %collective-permute-done.26.refs_18_), channel_id=1, source_target_pairs={{8,0},{16,8},{24,16},{28,24},{20,28},{12,20},{4,12},{0,4},{9,1},{1... | collective-permute-start | bytes 1179656 | tf_op jit(solution)/shard_map/ppermute | solution.py:643
  104.4 12.8 %collective-permute-start.27 = (bf16[128,1024]{1,0:T(8,128)(2,1)S(1)}, bf16[128,1024]{1,0:T(8,128)(2,1)S(1)}, u32[]{:S(2)}, u32[]{:S(2)}) collective-permute-start(bf16[128,1024]{1,0:T(8,128)(2,1)S(1)} %collective-permute-done.23.refs_4_.refs_2_), channel_id=1, source_target_pairs={{0,8},{8,16},{16,24},{24,28},{28,20},{20,12},{12,4},{4,0},{1,9},{9... | collective-permute-start | bytes 786440 | tf_op jit(solution)/shard_map/ppermute | solution.py:642
  105.5 13.0 %collective-permute-start.28 = (bf16[128,1024]{1,0:T(8,128)(2,1)S(1)}, bf16[128,1024]{1,0:T(8,128)(2,1)S(1)}, u32[]{:S(2)}, u32[]{:S(2)}) collective-permute-start(bf16[128,1024]{1,0:T(8,128)(2,1)S(1)} %collective-permute-done.24.refs_9_.refs_14_), channel_id=1, source_target_pairs={{8,0},{16,8},{24,16},{28,24},{20,28},{12,20},{4,12},{0,4},{9,1},{1... | collective-permute-start | bytes 786440 | tf_op jit(solution)/shard_map/ppermute | solution.py:643
  118.5 18.7 %collective-permute-start.31 = (bf16[64,3072]{1,0:T(8,128)(2,1)S(1)}, bf16[64,3072]{1,0:T(8,128)(2,1)S(1)}, u32[]{:S(2)}, u32[]{:S(2)}) collective-permute-start(bf16[64,3072]{1,0:T(8,128)(2,1)S(1)} %copy-done.38), channel_id=1, source_target_pairs={{0,8},{8,16},{16,24},{24,28},{28,20},{20,12},{12,4},{4,0},{1,9},{9... | collective-permute-start | bytes 1179656 | tf_op jit(solution)/shard_map/ppermute | solution.py:642
  120.6 16.6 %collective-permute-start.32 = (bf16[64,3072]{1,0:T(8,128)(2,1)S(1)}, bf16[64,3072]{1,0:T(8,128)(2,1)S(1)}, u32[]{:S(2)}, u32[]{:S(2)}) collective-permute-start(bf16[64,3072]{1,0:T(8,128)(2,1)S(1)} %copy-done.39), channel_id=1, source_target_pairs={{8,0},{16,8},{24,16},{28,24},{20,28},{12,20},{4,12},{0,4},{9,1},{1... | collective-permute-start | bytes 1179656 | tf_op jit(solution)/shard_map/ppermute | solution.py:643
  141.8 15.3 %collective-permute-start.35 = (bf16[64,3072]{1,0:T(8,128)(2,1)S(1)}, bf16[64,3072]{1,0:T(8,128)(2,1)S(1)}, u32[]{:S(2)}, u32[]{:S(2)}) collective-permute-start(bf16[64,3072]{1,0:T(8,128)(2,1)S(1)} %collective-permute-done.31.refs_19_), channel_id=1, source_target_pairs={{0,8},{8,16},{16,24},{24,28},{28,20},{20,12},{12,4},{4,0},{1,9},{9... | collective-permute-start | bytes 1179656 | tf_op jit(solution)/shard_map/ppermute | solution.py:642
  143.9 13.2 %collective-permute-start.36 = (bf16[64,3072]{1,0:T(8,128)(2,1)S(1)}, bf16[64,3072]{1,0:T(8,128)(2,1)S(1)}, u32[]{:S(2)}, u32[]{:S(2)}) collective-permute-start(bf16[64,3072]{1,0:T(8,128)(2,1)S(1)} %collective-permute-done.32.refs_8_), channel_id=1, source_target_pairs={{8,0},{16,8},{24,16},{28,24},{20,28},{12,20},{4,12},{0,4},{9,1},{1... | collective-permute-start | bytes 1179656 | tf_op jit(solution)/shard_map/ppermute | solution.py:643
  157.2 25.6 %collective-permute-start.34 = (bf16[512,1024]{1,0:T(8,128)(2,1)S(1)}, bf16[512,1024]{1,0:T(8,128)(2,1)S(1)}, u32[]{:S(2)}, u32[]{:S(2)}) collective-permute-start(bf16[512,1024]{1,0:T(8,128)(2,1)S(1)} %add_convert_fusion.15), channel_id=1, source_target_pairs={{0,2},{1,3},{2,0},{3,1},{4,6},{5,7},{6,4},{7,5},{8,10},{9,11},{10,... | collective-permute-start | bytes 3145736 | tf_op jit(solution)/shard_map/ppermute | solution.py:686
  183.3 30.7 %collective-permute-start.45 = (bf16[512,1024]{1,0:T(8,128)(2,1)S(1)}, bf16[512,1024]{1,0:T(8,128)(2,1)S(1)}, u32[]{:S(2)}, u32[]{:S(2)}) collective-permute-start(bf16[512,1024]{1,0:T(8,128)(2,1)S(1)} %add_convert_fusion.14), channel_id=1, source_target_pairs={{0,2},{1,3},{2,0},{3,1},{4,6},{5,7},{6,4},{7,5},{8,10},{9,11},{10,... | collective-permute-start | bytes 3145736 | tf_op jit(solution)/shard_map/ppermute | solution.py:686
  186.0 28.0 %collective-permute-start.43 = (bf16[64,3072]{1,0:T(8,128)(2,1)S(1)}, bf16[64,3072]{1,0:T(8,128)(2,1)S(1)}, u32[]{:S(2)}, u32[]{:S(2)}) collective-permute-start(bf16[64,3072]{1,0:T(8,128)(2,1)S(1)} %collective-permute-done.40.refs_13_), channel_id=1, source_target_pairs={{0,8},{8,16},{16,24},{24,28},{28,20},{20,12},{12,4},{4,0},{1,9},{9... | collective-permute-start | bytes 1179656 | tf_op jit(solution)/shard_map/ppermute | solution.py:642
  188.0 26.1 %collective-permute-start.44 = (bf16[64,3072]{1,0:T(8,128)(2,1)S(1)}, bf16[64,3072]{1,0:T(8,128)(2,1)S(1)}, u32[]{:S(2)}, u32[]{:S(2)}) collective-permute-start(bf16[64,3072]{1,0:T(8,128)(2,1)S(1)} %collective-permute-done.41.refs_14_), channel_id=1, source_target_pairs={{8,0},{16,8},{24,16},{28,24},{20,28},{12,20},{4,12},{0,4},{9,1},{1... | collective-permute-start | bytes 1179656 | tf_op jit(solution)/shard_map/ppermute | solution.py:643
  215.1 17.1 %collective-permute-start.48 = (bf16[64,3072]{1,0:T(8,128)(2,1)S(1)}, bf16[64,3072]{1,0:T(8,128)(2,1)S(1)}, u32[]{:S(2)}, u32[]{:S(2)}) collective-permute-start(bf16[64,3072]{1,0:T(8,128)(2,1)S(1)} %collective-permute-done.43.refs_11_), channel_id=1, source_target_pairs={{0,8},{8,16},{16,24},{24,28},{28,20},{20,12},{12,4},{4,0},{1,9},{9... | collective-permute-start | bytes 1179656 | tf_op jit(solution)/shard_map/ppermute | solution.py:642
  217.0 15.2 %collective-permute-start.49 = (bf16[64,3072]{1,0:T(8,128)(2,1)S(1)}, bf16[64,3072]{1,0:T(8,128)(2,1)S(1)}, u32[]{:S(2)}, u32[]{:S(2)}) collective-permute-start(bf16[64,3072]{1,0:T(8,128)(2,1)S(1)} %collective-permute-done.44.refs_16_), channel_id=1, source_target_pairs={{8,0},{16,8},{24,16},{28,24},{20,28},{12,20},{4,12},{0,4},{9,1},{1... | collective-permute-start | bytes 1179656 | tf_op jit(solution)/shard_map/ppermute | solution.py:643
  232.4 42.4 %collective-permute-start.55 = (bf16[512,1024]{1,0:T(8,128)(2,1)S(1)}, bf16[512,1024]{1,0:T(8,128)(2,1)S(1)}, u32[]{:S(2)}, u32[]{:S(2)}) collective-permute-start(bf16[512,1024]{1,0:T(8,128)(2,1)S(1)} %add_convert_fusion.12), channel_id=1, source_target_pairs={{0,2},{1,3},{2,0},{3,1},{4,6},{5,7},{6,4},{7,5},{8,10},{9,11},{10,... | collective-permute-start | bytes 3145736 | tf_op jit(solution)/shard_map/ppermute | solution.py:686
  246.7 28.2 %collective-permute-start.53 = (bf16[64,3072]{1,0:T(8,128)(2,1)}, bf16[64,3072]{1,0:T(8,128)(2,1)S(1)}, u32[]{:S(2)}, u32[]{:S(2)}) collective-permute-start(bf16[64,3072]{1,0:T(8,128)(2,1)} %get-tuple-element.326), channel_id=1, source_target_pairs={{0,8},{8,16},{16,24},{24,28},{28,20},{20,12},{12,4},{4,0},{1,9},{9... | collective-permute-start | bytes 1179656 | tf_op jit(solution)/shard_map/ppermute | solution.py:662
  247.4 27.5 %collective-permute-start.54 = (bf16[64,3072]{1,0:T(8,128)(2,1)}, bf16[64,3072]{1,0:T(8,128)(2,1)S(1)}, u32[]{:S(2)}, u32[]{:S(2)}) collective-permute-start(bf16[64,3072]{1,0:T(8,128)(2,1)} %get-tuple-element.329), channel_id=1, source_target_pairs={{8,0},{16,8},{24,16},{28,24},{20,28},{12,20},{4,12},{0,4},{9,1},{1... | collective-permute-start | bytes 1179656 | tf_op jit(solution)/shard_map/ppermute | solution.py:663
  279.1 22.6 %collective-permute-start.60 = (bf16[512,1024]{1,0:T(8,128)(2,1)}, bf16[512,1024]{1,0:T(8,128)(2,1)S(1)}, u32[]{:S(2)}, u32[]{:S(2)}) collective-permute-start(bf16[512,1024]{1,0:T(8,128)(2,1)} %get-tuple-element.348), channel_id=1, source_target_pairs={{0,1},{1,0},{2,3},{3,2},{4,5},{5,4},{6,7},{7,6},{8,9},{9,8},{10,11... | collective-permute-start | bytes 3145736 | tf_op jit(solution)/shard_map/ppermute | solution.py:681
  279.4 22.8 %collective-permute-start.57 = (bf16[64,3072]{1,0:T(8,128)(2,1)S(1)}, bf16[64,3072]{1,0:T(8,128)(2,1)S(1)}, u32[]{:S(2)}, u32[]{:S(2)}) collective-permute-start(bf16[64,3072]{1,0:T(8,128)(2,1)S(1)} %add_convert_fusion.37), channel_id=1, source_target_pairs={{8,0},{16,8},{24,16},{28,24},{20,28},{12,20},{4,12},{0,4},{9,1},{1... | collective-permute-start | bytes 1179656 | tf_op jit(solution)/shard_map/ppermute | solution.py:663
  287.3 27.1 %collective-permute-start.65 = (bf16[512,1024]{1,0:T(8,128)(2,1)S(1)}, bf16[512,1024]{1,0:T(8,128)(2,1)S(1)}, u32[]{:S(2)}, u32[]{:S(2)}) collective-permute-start(bf16[512,1024]{1,0:T(8,128)(2,1)S(1)} %add_convert_fusion.9), channel_id=1, source_target_pairs={{0,2},{1,3},{2,0},{3,1},{4,6},{5,7},{6,4},{7,5},{8,10},{9,11},{10,... | collective-permute-start | bytes 3145736 | tf_op jit(solution)/shard_map/ppermute | solution.py:686
  302.2 12.1 %collective-permute-start.61 = (bf16[64,3072]{1,0:T(8,128)(2,1)S(1)}, bf16[64,3072]{1,0:T(8,128)(2,1)S(1)}, u32[]{:S(2)}, u32[]{:S(2)}) collective-permute-start(bf16[64,3072]{1,0:T(8,128)(2,1)S(1)} %add_convert_fusion.38), channel_id=1, source_target_pairs={{0,8},{8,16},{16,24},{24,28},{28,20},{20,12},{12,4},{4,0},{1,9},{9... | collective-permute-start | bytes 1179656 | tf_op jit(solution)/shard_map/ppermute | solution.py:662
  303.0 12.1 %collective-permute-start.62 = (bf16[64,3072]{1,0:T(8,128)(2,1)S(1)}, bf16[64,3072]{1,0:T(8,128)(2,1)S(1)}, u32[]{:S(2)}, u32[]{:S(2)}) collective-permute-start(bf16[64,3072]{1,0:T(8,128)(2,1)S(1)} %add_convert_fusion.35), channel_id=1, source_target_pairs={{8,0},{16,8},{24,16},{28,24},{20,28},{12,20},{4,12},{0,4},{9,1},{1... | collective-permute-start | bytes 1179656 | tf_op jit(solution)/shard_map/ppermute | solution.py:663
  304.4 16.2 %collective-permute-start.63 = (bf16[64,3072]{1,0:T(8,128)(2,1)}, bf16[64,3072]{1,0:T(8,128)(2,1)S(1)}, u32[]{:S(2)}, u32[]{:S(2)}) collective-permute-start(bf16[64,3072]{1,0:T(8,128)(2,1)} %get-tuple-element.354), channel_id=1, source_target_pairs={{0,8},{8,16},{16,24},{24,28},{28,20},{20,12},{12,4},{4,0},{1,9},{9... | collective-permute-start | bytes 1179656 | tf_op jit(solution)/shard_map/ppermute | solution.py:662
  305.1 16.1 %collective-permute-start.64 = (bf16[64,3072]{1,0:T(8,128)(2,1)S(1)}, bf16[64,3072]{1,0:T(8,128)(2,1)S(1)}, u32[]{:S(2)}, u32[]{:S(2)}) collective-permute-start(bf16[64,3072]{1,0:T(8,128)(2,1)S(1)} %copy-done.116), channel_id=1, source_target_pairs={{8,0},{16,8},{24,16},{28,24},{20,28},{12,20},{4,12},{0,4},{9,1},{1... | collective-permute-start | bytes 1179656 | tf_op jit(solution)/shard_map/ppermute | solution.py:663
  321.2 12.1 %collective-permute-start.66 = (bf16[64,3072]{1,0:T(8,128)(2,1)S(1)}, bf16[64,3072]{1,0:T(8,128)(2,1)S(1)}, u32[]{:S(2)}, u32[]{:S(2)}) collective-permute-start(bf16[64,3072]{1,0:T(8,128)(2,1)S(1)} %add_convert_fusion.36), channel_id=1, source_target_pairs={{0,8},{8,16},{16,24},{24,28},{28,20},{20,12},{12,4},{4,0},{1,9},{9... | collective-permute-start | bytes 1179656 | tf_op jit(solution)/shard_map/ppermute | solution.py:662
  323.0 12.1 %collective-permute-start.67 = (bf16[64,3072]{1,0:T(8,128)(2,1)S(1)}, bf16[64,3072]{1,0:T(8,128)(2,1)S(1)}, u32[]{:S(2)}, u32[]{:S(2)}) collective-permute-start(bf16[64,3072]{1,0:T(8,128)(2,1)S(1)} %add_convert_fusion.34), channel_id=1, source_target_pairs={{8,0},{16,8},{24,16},{28,24},{20,28},{12,20},{4,12},{0,4},{9,1},{1... | collective-permute-start | bytes 1179656 | tf_op jit(solution)/shard_map/ppermute | solution.py:663
  323.5 14.9 %collective-permute-start.68 = (bf16[64,3072]{1,0:T(8,128)(2,1)S(1)}, bf16[64,3072]{1,0:T(8,128)(2,1)S(1)}, u32[]{:S(2)}, u32[]{:S(2)}) collective-permute-start(bf16[64,3072]{1,0:T(8,128)(2,1)S(1)} %add_convert_fusion.33), channel_id=1, source_target_pairs={{0,8},{8,16},{16,24},{24,28},{28,20},{20,12},{12,4},{4,0},{1,9},{9... | collective-permute-start | bytes 1179656 | tf_op jit(solution)/shard_map/ppermute | solution.py:662
  325.4 14.6 %collective-permute-start.69 = (bf16[64,3072]{1,0:T(8,128)(2,1)S(1)}, bf16[64,3072]{1,0:T(8,128)(2,1)S(1)}, u32[]{:S(2)}, u32[]{:S(2)}) collective-permute-start(bf16[64,3072]{1,0:T(8,128)(2,1)S(1)} %add_convert_fusion.32), channel_id=1, source_target_pairs={{8,0},{16,8},{24,16},{28,24},{20,28},{12,20},{4,12},{0,4},{9,1},{1... | collective-permute-start | bytes 1179656 | tf_op jit(solution)/shard_map/ppermute | solution.py:663
  326.3 13.7 %collective-permute-start.70 = (bf16[512,1024]{1,0:T(8,128)(2,1)S(1)}, bf16[512,1024]{1,0:T(8,128)(2,1)S(1)}, u32[]{:S(2)}, u32[]{:S(2)}) collective-permute-start(bf16[512,1024]{1,0:T(8,128)(2,1)S(1)} %add_convert_fusion.6.dh0), channel_id=1, source_target_pairs={{0,1},{1,0},{2,3},{3,2},{4,5},{5,4},{6,7},{7,6},{8,9},{9,8},{10,11... | collective-permute-start | bytes 3145736 | tf_op jit(solution)/shard_map/ppermute | solution.py:691
  333.3 37.3 %collective-permute-start.75 = (bf16[512,1024]{1,0:T(8,128)(2,1)S(1)}, bf16[512,1024]{1,0:T(8,128)(2,1)S(1)}, u32[]{:S(2)}, u32[]{:S(2)}) collective-permute-start(bf16[512,1024]{1,0:T(8,128)(2,1)S(1)} %add_convert_fusion.10), channel_id=1, source_target_pairs={{0,2},{1,3},{2,0},{3,1},{4,6},{5,7},{6,4},{7,5},{8,10},{9,11},{10,... | collective-permute-start | bytes 3145736 | tf_op jit(solution)/shard_map/ppermute | solution.py:686
  348.4 22.2 %collective-permute-start.71 = (bf16[64,3072]{1,0:T(8,128)(2,1)S(1)}, bf16[64,3072]{1,0:T(8,128)(2,1)S(1)}, u32[]{:S(2)}, u32[]{:S(2)}) collective-permute-start(bf16[64,3072]{1,0:T(8,128)(2,1)S(1)} %add_convert_fusion.31), channel_id=1, source_target_pairs={{0,8},{8,16},{16,24},{24,28},{28,20},{20,12},{12,4},{4,0},{1,9},{9... | collective-permute-start | bytes 1179656 | tf_op jit(solution)/shard_map/ppermute | solution.py:662
  349.4 21.1 %collective-permute-start.72 = (bf16[64,3072]{1,0:T(8,128)(2,1)S(1)}, bf16[64,3072]{1,0:T(8,128)(2,1)S(1)}, u32[]{:S(2)}, u32[]{:S(2)}) collective-permute-start(bf16[64,3072]{1,0:T(8,128)(2,1)S(1)} %add_convert_fusion.30), channel_id=1, source_target_pairs={{8,0},{16,8},{24,16},{28,24},{20,28},{12,20},{4,12},{0,4},{9,1},{1... | collective-permute-start | bytes 1179656 | tf_op jit(solution)/shard_map/ppermute | solution.py:663
  350.4 20.2 %collective-permute-start.73 = (bf16[64,3072]{1,0:T(8,128)(2,1)S(1)}, bf16[64,3072]{1,0:T(8,128)(2,1)S(1)}, u32[]{:S(2)}, u32[]{:S(2)}) collective-permute-start(bf16[64,3072]{1,0:T(8,128)(2,1)S(1)} %add_convert_fusion.29), channel_id=1, source_target_pairs={{0,8},{8,16},{16,24},{24,28},{28,20},{20,12},{12,4},{4,0},{1,9},{9... | collective-permute-start | bytes 1179656 | tf_op jit(solution)/shard_map/ppermute | solution.py:662
  351.5 19.2 %collective-permute-start.74 = (bf16[64,3072]{1,0:T(8,128)(2,1)S(1)}, bf16[64,3072]{1,0:T(8,128)(2,1)S(1)}, u32[]{:S(2)}, u32[]{:S(2)}) collective-permute-start(bf16[64,3072]{1,0:T(8,128)(2,1)S(1)} %add_convert_fusion.28), channel_id=1, source_target_pairs={{8,0},{16,8},{24,16},{28,24},{20,28},{12,20},{4,12},{0,4},{9,1},{1... | collective-permute-start | bytes 1179656 | tf_op jit(solution)/shard_map/ppermute | solution.py:663
  375.6 25.6 %collective-permute-start.82 = (bf16[512,1024]{1,0:T(8,128)(2,1)S(1)}, bf16[512,1024]{1,0:T(8,128)(2,1)S(1)}, u32[]{:S(2)}, u32[]{:S(2)}) collective-permute-start(bf16[512,1024]{1,0:T(8,128)(2,1)S(1)} %add_convert_fusion.5), channel_id=1, source_target_pairs={{0,2},{1,3},{2,0},{3,1},{4,6},{5,7},{6,4},{7,5},{8,10},{9,11},{10,... | collective-permute-start | bytes 3145736 | tf_op jit(solution)/shard_map/ppermute | solution.py:686
  378.0 23.2 %collective-permute-start.78 = (bf16[64,3072]{1,0:T(8,128)(2,1)S(1)}, bf16[64,3072]{1,0:T(8,128)(2,1)S(1)}, u32[]{:S(2)}, u32[]{:S(2)}) collective-permute-start(bf16[64,3072]{1,0:T(8,128)(2,1)S(1)} %add_convert_fusion.27), channel_id=1, source_target_pairs={{0,8},{8,16},{16,24},{24,28},{28,20},{20,12},{12,4},{4,0},{1,9},{9... | collective-permute-start | bytes 1179656 | tf_op jit(solution)/shard_map/ppermute | solution.py:662
  379.1 22.2 %collective-permute-start.79 = (bf16[64,3072]{1,0:T(8,128)(2,1)S(1)}, bf16[64,3072]{1,0:T(8,128)(2,1)S(1)}, u32[]{:S(2)}, u32[]{:S(2)}) collective-permute-start(bf16[64,3072]{1,0:T(8,128)(2,1)S(1)} %add_convert_fusion.26), channel_id=1, source_target_pairs={{8,0},{16,8},{24,16},{28,24},{20,28},{12,20},{4,12},{0,4},{9,1},{1... | collective-permute-start | bytes 1179656 | tf_op jit(solution)/shard_map/ppermute | solution.py:663
  380.1 21.2 %collective-permute-start.80 = (bf16[64,3072]{1,0:T(8,128)(2,1)S(1)}, bf16[64,3072]{1,0:T(8,128)(2,1)S(1)}, u32[]{:S(2)}, u32[]{:S(2)}) collective-permute-start(bf16[64,3072]{1,0:T(8,128)(2,1)S(1)} %add_convert_fusion.25), channel_id=1, source_target_pairs={{0,8},{8,16},{16,24},{24,28},{28,20},{20,12},{12,4},{4,0},{1,9},{9... | collective-permute-start | bytes 1179656 | tf_op jit(solution)/shard_map/ppermute | solution.py:662
  381.1 20.2 %collective-permute-start.81 = (bf16[64,3072]{1,0:T(8,128)(2,1)}, bf16[64,3072]{1,0:T(8,128)(2,1)S(1)}, u32[]{:S(2)}, u32[]{:S(2)}) collective-permute-start(bf16[64,3072]{1,0:T(8,128)(2,1)} %add_convert_fusion.24), channel_id=1, source_target_pairs={{8,0},{16,8},{24,16},{28,24},{20,28},{12,20},{4,12},{0,4},{9,1},{1... | collective-permute-start | bytes 1179656 | tf_op jit(solution)/shard_map/ppermute | solution.py:663
  404.6 20.0 %collective-permute-start.86 = (bf16[64,3072]{1,0:T(8,128)(2,1)S(1)}, bf16[64,3072]{1,0:T(8,128)(2,1)}, u32[]{:S(2)}, u32[]{:S(2)}) collective-permute-start(bf16[64,3072]{1,0:T(8,128)(2,1)S(1)} %get-tuple-element.410), channel_id=1, source_target_pairs={{0,8},{8,16},{16,24},{24,28},{28,20},{20,12},{12,4},{4,0},{1,9},{9... | collective-permute-start | bytes 1179656 | tf_op jit(solution)/shard_map/ppermute | solution.py:662
  406.2 21.1 %collective-permute-start.88 = (bf16[512,1024]{1,0:T(8,128)(2,1)S(1)}, bf16[512,1024]{1,0:T(8,128)(2,1)S(1)}, u32[]{:S(2)}, u32[]{:S(2)}) collective-permute-start(bf16[512,1024]{1,0:T(8,128)(2,1)S(1)} %add_convert_fusion.2.mine), channel_id=1, source_target_pairs={{0,1},{1,0},{2,3},{3,2},{4,5},{5,4},{6,7},{7,6},{8,9},{9,8},{10,11... | collective-permute-start | bytes 3145736 | tf_op jit(solution)/shard_map/ppermute | solution.py:691
  406.5 20.5 %collective-permute-start.84 = (bf16[64,3072]{1,0:T(8,128)(2,1)S(1)}, bf16[64,3072]{1,0:T(8,128)(2,1)S(1)}, u32[]{:S(2)}, u32[]{:S(2)}) collective-permute-start(bf16[64,3072]{1,0:T(8,128)(2,1)S(1)} %get-tuple-element.406), channel_id=1, source_target_pairs={{0,8},{8,16},{16,24},{24,28},{28,20},{20,12},{12,4},{4,0},{1,9},{9... | collective-permute-start | bytes 1179656 | tf_op jit(solution)/shard_map/ppermute | solution.py:662
  407.5 19.4 %collective-permute-start.85 = (bf16[64,3072]{1,0:T(8,128)(2,1)S(1)}, bf16[64,3072]{1,0:T(8,128)(2,1)S(1)}, u32[]{:S(2)}, u32[]{:S(2)}) collective-permute-start(bf16[64,3072]{1,0:T(8,128)(2,1)S(1)} %get-tuple-element.408), channel_id=1, source_target_pairs={{8,0},{16,8},{24,16},{28,24},{20,28},{12,20},{4,12},{0,4},{9,1},{1... | collective-permute-start | bytes 1179656 | tf_op jit(solution)/shard_map/ppermute | solution.py:663
  408.5 18.7 %collective-permute-start.87 = (bf16[64,3072]{1,0:T(8,128)(2,1)S(1)}, bf16[64,3072]{1,0:T(8,128)(2,1)}, u32[]{:S(2)}, u32[]{:S(2)}) collective-permute-start(bf16[64,3072]{1,0:T(8,128)(2,1)S(1)} %get-tuple-element.412), channel_id=1, source_target_pairs={{8,0},{16,8},{24,16},{28,24},{20,28},{12,20},{4,12},{0,4},{9,1},{1... | collective-permute-start | bytes 1179656 | tf_op jit(solution)/shard_map/ppermute | solution.py:663
  424.6 26.1 %collective-permute-start.94 = (bf16[512,1024]{1,0:T(8,128)(2,1)S(1)}, bf16[512,1024]{1,0:T(8,128)(2,1)S(1)}, u32[]{:S(2)}, u32[]{:S(2)}) collective-permute-start(bf16[512,1024]{1,0:T(8,128)(2,1)S(1)} %add_convert_fusion.3), channel_id=1, source_target_pairs={{0,2},{1,3},{2,0},{3,1},{4,6},{5,7},{6,4},{7,5},{8,10},{9,11},{10,... | collective-permute-start | bytes 3145736 | tf_op jit(solution)/shard_map/ppermute | solution.py:686
  427.3 12.3 %collective-permute-start.89 = (bf16[128,1024]{1,0:T(8,128)(2,1)}, bf16[128,1024]{1,0:T(8,128)(2,1)S(1)}, u32[]{:S(2)}, u32[]{:S(2)}) collective-permute-start(bf16[128,1024]{1,0:T(8,128)(2,1)} %get-tuple-element.419), channel_id=1, source_target_pairs={{0,8},{8,16},{16,24},{24,28},{28,20},{20,12},{12,4},{4,0},{1,9},{9... | collective-permute-start | bytes 786440 | tf_op jit(solution)/shard_map/ppermute | solution.py:662
  430.4 20.3 %collective-permute-start.90 = (bf16[64,3072]{1,0:T(8,128)(2,1)S(1)}, bf16[64,3072]{1,0:T(8,128)(2,1)S(1)}, u32[]{:S(2)}, u32[]{:S(2)}) collective-permute-start(bf16[64,3072]{1,0:T(8,128)(2,1)S(1)} %add_convert_fusion.19), channel_id=1, source_target_pairs={{0,8},{8,16},{16,24},{24,28},{28,20},{20,12},{12,4},{4,0},{1,9},{9... | collective-permute-start | bytes 1179656 | tf_op jit(solution)/shard_map/ppermute | solution.py:662
  431.5 19.3 %collective-permute-start.91 = (bf16[64,3072]{1,0:T(8,128)(2,1)S(1)}, bf16[64,3072]{1,0:T(8,128)(2,1)S(1)}, u32[]{:S(2)}, u32[]{:S(2)}) collective-permute-start(bf16[64,3072]{1,0:T(8,128)(2,1)S(1)} %add_convert_fusion.18), channel_id=1, source_target_pairs={{8,0},{16,8},{24,16},{28,24},{20,28},{12,20},{4,12},{0,4},{9,1},{1... | collective-permute-start | bytes 1179656 | tf_op jit(solution)/shard_map/ppermute | solution.py:663
  439.6 38.9 %collective-permute-start.104 = (bf16[512,1024]{1,0:T(8,128)(2,1)S(1)}, bf16[512,1024]{1,0:T(8,128)(2,1)S(1)}, u32[]{:S(2)}, u32[]{:S(2)}) collective-permute-start(bf16[512,1024]{1,0:T(8,128)(2,1)S(1)} %add_convert_fusion.7), channel_id=1, source_target_pairs={{0,2},{1,3},{2,0},{3,1},{4,6},{5,7},{6,4},{7,5},{8,10},{9,11},{10,... | collective-permute-start | bytes 3145736 | tf_op jit(solution)/shard_map/ppermute | solution.py:686
  453.3 15.8 %collective-permute-start.99 = (bf16[512,1024]{1,0:T(8,128)(2,1)S(1)}, bf16[512,1024]{1,0:T(8,128)(2,1)S(1)}, u32[]{:S(2)}, u32[]{:S(2)}) collective-permute-start(bf16[512,1024]{1,0:T(8,128)(2,1)S(1)} %add_convert_fusion.1.mine), channel_id=1, source_target_pairs={{0,1},{1,0},{2,3},{3,2},{4,5},{5,4},{6,7},{7,6},{8,9},{9,8},{10,11... | collective-permute-start | bytes 3145736 | tf_op jit(solution)/shard_map/ppermute | solution.py:691
  (171 other events, 1924.8 us)

commit v4 on v3

--- a/solution.py
+++ b/solution.py
@@ -82,11 +82,11 @@
         return jnp.where(pl.program_id(0) < self.count, pair[1][...], pair[0][...])
 
     def put(self, pair, value):
-        for k in range(2):
-
-            @pl.when((pl.program_id(0) < self.count) == (k == 1))
-            def _():
-                pair[k][...] = value
+        pair[0][...] = value
+
+        @pl.when(pl.program_id(0) < self.count)
+        def _():
+            pair[1][...] = pair[0][...]
 
 
 def split_sets(value, sets):
@@ -95,43 +95,39 @@
     return [parts[:, c].reshape(-1, width) for c in range(sets)]
 
 
-def pack_attn_body(wq, wk, wv, wo, first, second):
-    hw = wq.shape[2]
-    for c, ref in enumerate((first, second)):
+def pack_attn_body(wq, wk, wv, wo, out):
+    own, hw = wq.shape[1:]
+    for c in range(2):
+        rows = slice(c * own, (c + 1) * own)
         for t, w in enumerate((wq, wk, wv)):
-            ref[:, t * hw : (t + 1) * hw] = w[c]
-        ref[:, 3 * hw :] = wo[c].T
+            out[rows, t * hw : (t + 1) * hw] = w[c]
+        out[rows, 3 * hw :] = wo[c].T
 
 
 def pack_attn(wq, wk, wv, wo):
-    own, hw = wq.shape[1:]
-    piece = (own, 4 * hw)
+    sets, own, hw = wq.shape
+    piece = (sets * own, 4 * hw)
     return kernel_call(
         pack_attn_body,
         (1,),
         (wq, wk, wv, wo),
         [whole(w.shape) for w in (wq, wk, wv, wo)],
-        [out_of(piece)] * 2,
-        [whole(piece)] * 2,
+        [out_of(piece)],
+        [whole(piece)],
         0,
-    )
-
-
-def pack_ffn_body(wg, wu, wd, first, second):
+    )[0]
+
+
+def pack_ffn_body(wg, wu, wd, out):
     units = wg.shape[2]
-    half = wg.shape[1] // 2
-    for k, ref in enumerate((first, second)):
-        rows = slice(k * half, (k + 1) * half)
-        ref[:, :units] = wg[0, rows]
-        ref[:, units : 2 * units] = wu[0, rows]
-    turned = wd[0].T
-    first[:, 2 * units :] = turned[:half]
-    second[:, 2 * units :] = turned[half:]
+    out[:, :units] = wg[0]
+    out[:, units : 2 * units] = wu[0]
+    out[:, 2 * units :] = wd[0].T
 
 
 def pack_ffn(wg, wu, wd, c):
     own, units = wg.shape[1:]
-    piece = (own // 2, 3 * units)
+    piece = (own, 3 * units)
     into = pl.BlockSpec((1, own, units), lambda i: (c, 0, 0))
     back = pl.BlockSpec((1, units, own), lambda i: (c, 0, 0))
     return kernel_call(
@@ -139,10 +135,10 @@
         (1,),
         (wg, wu, wd),
         [into, into, back],
-        [out_of(piece)] * 2,
-        [whole(piece)] * 2,
+        [out_of(piece)],
+        [whole(piece)],
         0,
-    )
+    )[0]
 
 
 def norm(value):
@@ -184,25 +180,26 @@
 
 
 class Pieces:
-    def __init__(self, arrays, groups):
-        self.arrays = arrays
-        self.count = len(arrays)
+    def __init__(self, entries, own, groups):
+        self.entries = entries
+        self.own = own
         self.groups = groups
-        self.shape = (sum(a.shape[0] for a in arrays), arrays[0].shape[1])
-        self.scratch = [pltpu.VMEM(self.shape, BF), pltpu.SemaphoreType.DMA((groups, self.count))]
+        self.arrays = []
+        for array, *_ in entries:
+            if not any(array is a for a in self.arrays):
+                self.arrays.append(array)
+        self.count = len(self.arrays)
+        self.shape = (sum(e[4] for e in entries), entries[0][0].shape[1])
+        self.scratch = [pltpu.VMEM(self.shape, BF), pltpu.SemaphoreType.DMA((groups, len(entries)))]
 
     def copies(self, refs, places, memory, sems, group):
         wide = self.shape[1] // self.groups
         cols = pl.ds(group * wide, wide)
-        for k, ref in enumerate(refs):
-            if self.count == 1:
-                start = 0
-            else:
-                parts = self.count // (places.shape[0] - 1)
-                start = (places[k // parts] * parts + k % parts) * ref.shape[0]
-                start = pl.multiple_of(start, ref.shape[0])
-            rows = pl.ds(start, ref.shape[0])
-            yield pltpu.make_async_copy(ref.at[:, cols], memory.at[rows, cols], sems.at[group, k])
+        for k, (array, slot, row, first, rows) in enumerate(self.entries):
+            ref = [r for r, a in zip(refs, self.arrays) if a is array][0]
+            start = row if slot is None else pl.multiple_of(places[slot] * self.own + row, rows)
+            source = ref.at[pl.ds(first, rows), cols]
+            yield pltpu.make_async_copy(source, memory.at[pl.ds(start, rows), cols], sems.at[group, k])
 
     def start(self, refs, places, memory, sems, order):
         @pl.when(pl.program_id(0) == 0)
@@ -248,7 +245,7 @@
 
 def attend(places, x, gain, before, w, steps):
     tokens, width = x.shape
-    pieces, halves = Pieces(w, 1), Halves(tokens)
+    pieces, halves = Pieces(*w, 1), Halves(tokens)
     hw = pieces.shape[1] // 4
     ins = [x, gain]
     specs = [halves.both(width), whole(gain.shape)]
@@ -259,7 +256,7 @@
     *out, mine, other = kernel_call(
         functools.partial(attend_body, pieces, halves, steps, hw, before is not None),
         halves.grid,
-        [*ins, *w],
+        [*ins, *pieces.arrays],
         [*specs, *[HBM] * pieces.count],
         [out_of((tokens, n)) for n in widths] + [out_of((tokens // 2, width))] * 2,
         [halves.both(n) for n in widths] + halves.pair(width),
@@ -301,14 +298,14 @@
 
 def hidden_units(places, x, att, g, gain, w):
     tokens, width = x.shape
-    pieces, halves = Pieces(w, 3), Halves(tokens)
+    pieces, halves = Pieces(*w, 3), Halves(tokens)
     units = pieces.shape[1] // 3
     part = halves.both(width)
     widths = (width, units, units, units)
     *out, dh0, dh1, mlp0, mlp1 = kernel_call(
         functools.partial(units_body, pieces, halves, units),
         halves.grid,
-        (x, *att, g, gain, *w),
+        (x, *att, g, gain, *pieces.arrays),
         [part, *halves.pair(width), part, whole(gain.shape), *[HBM] * pieces.count],
         [out_of((tokens, n)) for n in widths] + [out_of((tokens // 2, width))] * 4,
         [halves.both(n) for n in widths] + halves.pair(width) * 2,
@@ -319,28 +316,35 @@
     return *out, (dh0, dh1), (mlp0, mlp1)
 
 
-def grads_body(columns, parts, steps, places, *refs):
-    inputs = max(right for _, right in columns) + 1
+def grads_body(runs, cut, steps, places, *refs):
+    inputs = max(right for columns in runs for _, right in columns) + 1
     ins, outs = refs[:inputs], refs[inputs:]
     values = []
-    for slots, k in columns:
-        rows = [ins[s][...] for s in slots]
-        rows = jnp.concatenate(rows, axis=1) if len(rows) > 1 else rows[0]
-        values.append(mm(rows, ins[k][...], TN).astype(BF))
-    if parts == 0:
+    for columns in runs:
+        values.append([])
+        for slots, k in columns:
+            rows = [ins[s][...] for s in slots]
+            rows = jnp.concatenate(rows, axis=1) if len(rows) > 1 else rows[0]
+            values[-1].append(mm(rows, ins[k][...], TN).astype(BF))
+    if not cut:
         at = 0
-        for value in values:
+        for value in values[0]:
             outs[0][:, at : at + value.shape[1]] = value
             at += value.shape[1]
         return
     *outs, buffer, sems = outs
     height = outs[0].shape[0]
-    per = buffer.shape[1] // height
+    own = height // len(runs)
+    slots = ROWS // own
 
     def copies(block):
-        for k in range(per):
-            rows = buffer.at[block % 2, pl.ds(k * height, height)]
-            yield pltpu.make_async_copy(rows, outs[block * per + k], sems.at[block % 2, k])
+        at = 0
+        for k in range(slots):
+            t = block * slots + k
+            for ref in outs[t : t + 1] if t < cut else outs[t : t + 2] if t == cut else outs[t + 1 : t + 2]:
+                rows = buffer.at[block % 2, pl.ds(at, ref.shape[0])]
+                yield pltpu.make_async_copy(rows, ref, sems.at[block % 2, at // (height // 2)])
+                at += ref.shape[0]
 
     for block in range(steps):
 
@@ -349,10 +353,14 @@
             if block >= 2:
                 for copy in copies(block - 2):
                     copy.wait()
-            at = 0
-            for value in values:
-                buffer[block % 2, :, at : at + value.shape[1]] = value
-                at += value.shape[1]
+            for k in range(slots):
+                for r, columns in enumerate(values):
+                    at = 0
+                    first = (k * len(runs) + r) * own
+                    for value in columns:
+                        cols = slice(at, at + value.shape[1])
+                        buffer[block % 2, first : first + own, cols] = value[k * own : (k + 1) * own]
+                        at += value.shape[1]
             for copy in copies(block):
                 copy.start()
             if block == steps - 1:
@@ -361,35 +369,43 @@
                         copy.wait()
 
 
-def weight_grads(places, columns, parts):
+def weight_grads(places, runs, cut):
     count = places.shape[0] - 1
-    tokens, width = columns[0][0].shape
+    tokens, width = runs[0][0][0].shape
     own = width // count
     steps = width // ROWS
-    slots = ROWS // own if parts else 1
+    slots = ROWS // own if cut else 1
     ins, specs, marks = [], [], []
-    for left, _ in columns:
-        mark = []
-        for k in range(slots):
-            place = (lambda i, p, k=k: (0, p[i * slots + k])) if parts else (lambda i, p: (0, i))
-            ins.append(left)
-            specs.append(pl.BlockSpec((tokens, ROWS // slots), place))
-            mark.append(len(ins) - 1)
-        marks.append(tuple(mark))
+    for columns in runs:
+        for left, _ in columns:
+            mark = []
+            for k in range(slots):
+                place = (lambda i, p, k=k: (0, p[i * slots + k])) if cut else (lambda i, p: (0, i))
+                ins.append(left)
+                specs.append(pl.BlockSpec((tokens, ROWS // slots), place))
+                mark.append(len(ins) - 1)
+            marks.append(tuple(mark))
     pairs = []
-    for (_, right), mark in zip(columns, marks):
-        ins.append(right)
-        specs.append(whole(right.shape))
-        pairs.append((mark, len(ins) - 1))
-    total = sum(right.shape[1] for _, right in columns)
-    if parts:
-        outs = [out_of((own // parts, total))] * (parts * count)
+    for columns in runs:
+        pairs.append([])
+        for _, right in columns:
+            ins.append(right)
+            specs.append(whole(right.shape))
+            pairs[-1].append((marks.pop(0), len(ins) - 1))
+    total = sum(right.shape[1] for _, right in runs[0])
+    if cut:
+        height = own * len(runs)
+        heights = [height] * cut + [height // 2] * 2 + [height] * (count - cut - 1)
+        outs = [out_of((h, total)) for h in heights]
         out_specs = [HBM] * len(outs)
-        scratch = [pltpu.VMEM((2, ROWS, total), BF), pltpu.SemaphoreType.DMA((2, slots * parts))]
+        scratch = [
+            pltpu.VMEM((2, slots * height, total), BF),
+            pltpu.SemaphoreType.DMA((2, 2 * slots)),
+        ]
     else:
         outs, out_specs, scratch = [out_of((width, total))], [rows_of(ROWS, total)], []
     return kernel_call(
-        functools.partial(grads_body, pairs, parts, steps),
+        functools.partial(grads_body, pairs, cut, steps),
         (steps,),
         ins,
         specs,
@@ -440,9 +456,10 @@
     )
 
 
-def attend_back_body(pieces, steps, hw, places, x0, x1, dm0, dm1, qkv0, qkv1, *refs):
-    n = pieces[0].count
-    sides = (refs[:n], refs[n : 2 * n])
+def attend_back_body(pieces, shared, steps, hw, places, x0, x1, dm0, dm1, qkv0, qkv1, *refs):
+    sides = [
+        [r for a in p.arrays for r, b in zip(refs, shared.arrays) if a is b] for p in pieces
+    ]
     dqkv0, dqkv1, mine, other, dgain, w0, sems0, w1, sems1 = refs[-9:]
     for p, s, w, sems in zip(pieces, sides, (w0, w1), (sems0, sems1)):
         p.start(s, places, w, sems, range(1))
@@ -479,11 +496,11 @@
     for c, (d, w) in enumerate(((dqkv0, w0), (dqkv1, w1))):
         grad = mm(d[...], w[:, : 3 * hw], NT)
         gains.append(jnp.sum(grad * normed[c], axis=0, keepdims=True))
-        for k, ref in enumerate((other, mine)):
-
-            @pl.when(pl.program_id(0) == k)
-            def _():
-                ref[c * ROWS : (c + 1) * ROWS] = grad.astype(BF)
+        mine[c * ROWS : (c + 1) * ROWS] = grad.astype(BF)
+
+    @pl.when(pl.program_id(0) == 0)
+    def _():
+        other[...] = mine[...]
 
     add_up(dgain, jnp.concatenate(gains, axis=0))
 
@@ -491,15 +508,16 @@
 def attend_back(places, x, dm, qkv, w, part, before, steps):
     tokens, width = dm[0].shape
     halves = Halves(tokens)
-    pieces = [Pieces(side, 1) for side in w]
+    pieces = [Pieces(*side, 1) for side in w]
+    shared = Pieces(w[0][0] + w[1][0], w[0][1], 1)
     hw = pieces[0].shape[1] // 4
     spot = lambda i, p: (halves.block(i * halves.count, p) + part, 0)
     flat, thin = pl.BlockSpec((ROWS, width), spot), pl.BlockSpec((ROWS, 3 * hw), spot)
-    ins = [*x, *dm, *qkv, *w[0], *w[1], *(before or ())]
+    ins = [*x, *dm, *qkv, *shared.arrays, *(before or ())]
     specs = [flat] * 4 + [thin] * 2 + [HBM] * (len(ins) - 6)
     alias = {len(ins) - 1: 0, len(ins): 1} if before else {}
     d0, d1, mine, other, d_gain = kernel_call(
-        functools.partial(attend_back_body, pieces, steps, hw),
+        functools.partial(attend_back_body, pieces, shared, steps, hw),
         (2,),
         ins,
         specs,
@@ -571,33 +589,32 @@
     return kernel_call(input_body, (2,), ins, specs, [out_of(shape)], [cube], 0, (), places, alias)[0]
 
 
-def add_terms(refs):
-    total = refs[0][...].astype(F32)
-    for ref in refs[1:]:
-        total = total + ref[...].astype(F32)
-    return total
-
-
 def finish_body(layout, turned, *refs):
-    count = sum(len(terms) for side in layout for terms in side)
-    ins, outs = list(refs[:count]), refs[count:]
-    wide = ins[0].shape[1] // len(outs)
-    for c, side in enumerate(layout):
-        sums = []
-        for terms in side:
-            sums.append(add_terms([ins.pop(0) for _ in terms]))
-        total = jnp.concatenate(sums, axis=0) if len(sums) > 1 else sums[0]
+    count = 1 + max(k for terms, _ in layout for k in terms)
+    ins, outs = refs[:count], refs[count:]
+    own, wide = outs[0].shape[1:]
+    for c, (terms, first) in enumerate(layout):
+        rows = slice(first, first + own)
         for t, ref in enumerate(outs):
-            part = total[:, t * wide : (t + 1) * wide]
-            ref[c] = part.T if t == turned else part
-
-
-def finish(sides, kinds):
-    arrays = [a for side in sides for terms in side for a in terms]
-    own = sum(terms[0].shape[0] for terms in sides[0])
+            cols = slice(t * wide, (t + 1) * wide)
+            total = ins[terms[0]][rows, cols].astype(F32)
+            for k in terms[1:]:
+                total = total + ins[k][rows, cols].astype(F32)
+            ref[c] = total.T if t == turned else total
+
+
+def finish(sides, kinds, own):
+    arrays, layout = [], []
+    for terms, first in sides:
+        spots = []
+        for term in terms:
+            found = [k for k, a in enumerate(arrays) if a is term]
+            if not found:
+                arrays.append(term)
+            spots.append(found[0] if found else len(arrays) - 1)
+        layout.append((spots, first))
     wide = arrays[0].shape[1] // kinds
     shapes = [(len(sides), own, wide)] * (kinds - 1) + [(len(sides), wide, own)]
-    layout = [[[0] * len(terms) for terms in side] for side in sides]
     return kernel_call(
         functools.partial(finish_body, layout, kinds - 1),
         (1,),
@@ -635,36 +652,59 @@
 
 
 class Gather:
-    def __init__(self, rounds, ring, first, second):
-        self.rounds, self.ring, self.a, self.b = rounds, ring, [first], [second]
+    def __init__(self, rounds, ring, shard):
+        self.rounds, self.ring = rounds, ring
+        self.a, self.b = [shard], [shard]
 
     def step(self):
-        self.a.append(lax.ppermute(self.rounds.now(self.a[-1]), "dp", self.ring.ahead))
-        self.b.append(lax.ppermute(self.rounds.now(self.b[-1]), "dp", self.ring.behind))
+        a, b = self.a[-1], self.b[-1]
+        if len(self.a) == self.ring.size // 2:
+            half = a.shape[0] // 2
+            a, b = a[:half], b[half:]
+        self.a.append(lax.ppermute(self.rounds.now(a), "dp", self.ring.ahead))
+        self.b.append(lax.ppermute(self.rounds.now(b), "dp", self.ring.behind))
         return self.a[-1], self.b[-1]
 
-    def slots(self):
-        return [self.a[-t % self.ring.size] for t in range(self.ring.size)], self.b
+    def entries(self, part=0, parts=1):
+        n = self.ring.size
+        own = self.a[0].shape[0] // parts
+        found = []
+        for t in range(n):
+            if t != n // 2:
+                found.append((self.b[t] if t < n // 2 else self.a[n - t], t, 0, part * own, own))
+            elif parts == 1:
+                found.append((self.a[t], t, 0, 0, own // 2))
+                found.append((self.b[t], t, own // 2, 0, own // 2))
+            else:
+                found.append(((self.a[t], self.b[t])[part], t, 0, 0, own))
+        return found, own
 
 
 class Scatter:
-    def __init__(self, rounds, ring, first, second):
-        self.rounds, self.ring, self.first, self.second = rounds, ring, first, second
-        self.a, self.b = first[-1], second[1]
-        self.k = 1
+    def __init__(self, rounds, ring, blocks):
+        self.rounds, self.ring = rounds, ring
+        far = ring.size // 2
+        self.a, self.b = blocks[far], blocks[far + 1]
+        self.blocks = [*blocks[:far], None, *blocks[far + 2 :]]
+        self.k = far
 
     def step(self):
         n = self.ring.size
-        self.k += 1
-        if self.k > 2:
-            self.a = (self.a.astype(F32) + self.first[n - self.k + 1].astype(F32)).astype(BF)
-            self.b = (self.b.astype(F32) + self.second[self.k - 1].astype(F32)).astype(BF)
+        if self.k < n // 2:
+            one, two = self.blocks[self.k].astype(F32), self.blocks[n - self.k].astype(F32)
+            a, b = self.a.astype(F32), self.b.astype(F32)
+            if self.k == n // 2 - 1:
+                half = a.shape[0]
+                a = jnp.pad(a, ((0, half), (0, 0)))
+                b = jnp.pad(b, ((half, 0), (0, 0)))
+            self.a, self.b = (one + a).astype(BF), (two + b).astype(BF)
+        self.k -= 1
         self.a = lax.ppermute(self.rounds.now(self.a), "dp", self.ring.ahead)
         self.b = lax.ppermute(self.rounds.now(self.b), "dp", self.ring.behind)
         return self.a, self.b
 
-    def sums(self):
-        return [self.a, self.first[0]], [self.b, self.second[0]]
+    def terms(self):
+        return [self.blocks[0], self.a, self.b]
 
 
 class HeadSum:
@@ -709,17 +749,18 @@
     each = shape[1] // sets
     ring = Ring(lax.axis_size("dp"))
     rings, n = ring.rings, ring.size
+    far = n // 2 if rings else 0
     own = width // n
     places = jnp.concatenate([ring.order, (lax.axis_index("mp") % 2).astype(jnp.int32)[None]])
     gather = lambda value: lax.all_gather(value, "dp", tiled=True)
-    scatter = lambda value: [[lax.psum_scatter(value, "dp", scatter_dimension=0, tiled=True)]]
+    scatter = lambda value: lax.psum_scatter(value, "dp", scatter_dimension=0, tiled=True)
     rounds = Rounds()
     now, close = rounds.now, rounds.close
 
-    first, second = pack_attn(w_query, w_key, w_value, w_out)
+    attn_own = pack_attn(w_query, w_key, w_value, w_out)
     small = jnp.concatenate([gain_attn, gain_ffn], 0).astype(F32)[None]
     steps = list(exchange_steps(("dp",)))
-    pack, x, g = [], [], []
+    ffn_own, x, g = [], [], []
 
     def gain_step(value):
         axis, moves, step = steps.pop(0)
@@ -730,121 +771,116 @@
 
     masks = frame_mask.astype(BF)[:, None, None]
     chores = [
-        lambda: pack.append(pack_ffn(now(w_gate), w_up, w_down, 0)),
-        lambda: pack.append(pack_ffn(now(w_gate), w_up, w_down, 1)),
+        lambda: ffn_own.append(pack_ffn(now(w_gate), w_up, w_down, 0)),
         lambda: x.append(split_sets(now(layer_input), sets)[0]),
+        lambda: ffn_own.append(pack_ffn(now(w_gate), w_up, w_down, 1)),
         lambda: x.append(split_sets(now(layer_input), sets)[1]),
         lambda: g.append(split_sets(now(cotangent) * masks, sets)[0]),
         lambda: g.append(split_sets(now(cotangent) * masks, sets)[1]),
-        lambda: None,
     ]
-    chores.pop(0)()
-    attn = Gather(rounds, ring, first, second)
-    rows = [Gather(rounds, ring, *pack[0])]
-    for chore in chores:
-        moved = (*attn.step(), *rows[0].step()) if rings else ()
-        chore()
+    attn = Gather(rounds, ring, attn_own)
+    for _ in range(max(far, 3)):
+        moved = attn.step() if rings else ()
+        for chore in chores[:2]:
+            chore()
+        del chores[:2]
         if steps:
             small = gain_step(small)
-        held = [v[-1] if not isinstance(v[-1], (list, tuple)) else v[-1][0] for v in (pack, x, g) if v]
-        close(small, *held, *moved)
+        close(small, *moved, *[v[-1] for v in (ffn_own, x, g) if v])
     while steps:
         small = gain_step(small)
-    if rings:
-        close(*attn.step(), *rows[0].step())
-        rows.append(Gather(rounds, ring, *pack[1]))
-        move = rows[1].step
-    else:
-        move = lambda: ()
     gains = small.transpose(1, 0, 2).reshape(2 * sets, width)
     g_attn, g_ffn = [[gains[k * sets + c][None] for c in range(sets)] for k in range(2)]
-    w_attn = list(attn.slots()) if rings else [[gather(first)], [gather(second)]]
-    w_ffn = [None if rings else [gather(jnp.concatenate(p, 0))] for p in pack]
-
-    def take(c):
+    if rings:
+        rows = [Gather(rounds, ring, shard) for shard in ffn_own]
+        w_attn = [attn.entries(c, sets) for c in range(sets)]
+    else:
+        both = gather(attn_own).reshape(n, sets, own, -1)
+        w_attn = [([(both[:, c].reshape(width, -1), None, 0, 0, width)], width) for c in range(sets)]
+
+    def move(c):
+        return rows[c].step() if rings else ()
+
+    def weights(c):
         if rings:
-            a, b = rows[c].slots()
-            w_ffn[c] = [piece for pair in zip(a, b) for piece in pair]
-
-    take(0)
+            return rows[c].entries()
+        return [(gather(ffn_own[c]), None, 0, 0, width)], width
+
     h1, qkv, mixed, heads = [None] * 2, [None] * 2, [None] * 2, [None] * 2
-    moved = move()
+    moved = move(0)
     h1[0], qkv[0], mixed[0], part = attend(now(places), x[0], g_attn[0], None, w_attn[0], each)
     heads[0] = HeadSum(rounds, part)
     close(*moved, part[0])
     close(heads[0].near())
-    moved = move()
-    heads[0].far()
+    moved = move(0)
+    got = heads[0].far()
     h1[1], qkv[1], mixed[1], part = attend(now(places), x[1], g_attn[1], qkv[0], w_attn[1], each)
     heads[1] = HeadSum(rounds, part)
-    close(*moved, part[0])
-    moved = move()
-    close(*moved, heads[1].near())
-    moved = move()
-    heads[1].far()
-    close(*moved, heads[0].got)
-    close(heads[0].last())
+    close(*moved, part[0], got)
+    close(*move(0), heads[1].near(), heads[0].last())
+    close(*move(0), *move(1), heads[1].far())
 
     def grads_of(c, out):
         columns = [(out[0], out[2]), (out[0], out[3]), (g[c], out[1])]
-        return weight_grads(now(places), columns, 2 if rings else 0)
+        return weight_grads(now(places), [columns], far)
 
     dh, mlp, grads, dm, d_gain_ffn = ([None] * 2 for _ in range(5))
-    moved = move()
-    out = hidden_units(now(places), x[0], heads[0].sum, g[0], g_ffn[0], w_ffn[0])
+    moved = move(1)
+    out = hidden_units(now(places), x[0], heads[0].sum, g[0], g_ffn[0], weights(0))
     dh[0], mlp[0] = HeadSum(rounds, out[4]), HeadSum(rounds, out[5])
-    close(*moved, out[0], heads[1].got)
-    moved = move()
-    close(dh[0].near(), heads[1].last())
+    close(*moved, out[0], heads[1].last())
     att = [head.sum for head in heads]
-    dh[0].far()
+    close(dh[0].near())
+    moved = move(1)
+    got = dh[0].far()
     grads[0] = grads_of(0, out)
-    close(*moved, grads[0][0])
-    close(*move(), mlp[0].near())
-    take(1)
+    close(*moved, grads[0][0], got, mlp[0].near())
+    close(*move(1), dh[0].last())
+
+    sums = [Scatter(rounds, ring, grads[0])] if rings else []
+    add = lambda k: sums[k].step() if rings else ()
+    moved = add(0)
+    got = mlp[0].far()
+    out = hidden_units(now(places), x[1], att[1], g[1], g_ffn[1], weights(1))
+    dh[1], mlp[1] = HeadSum(rounds, out[4]), HeadSum(rounds, out[5])
+    close(*moved, out[0], got)
+    close(dh[1].near(), mlp[0].last())
+    moved = add(0)
+    got = dh[1].far()
+    grads[1] = grads_of(1, out)
+    order = now(places)
+    dm[0], d_gain_ffn[0] = middle_back(order, x[0], att[0], g[0], dh[0].sum, g_ffn[0])
+    close(*moved, grads[1][0], dm[0], got)
+    close(dh[1].last(), mlp[1].near())
     if rings:
-        sums = [Scatter(rounds, ring, grads[0][0::2], grads[0][1::2])]
-        move = lambda: sum((s.step() for s in sums if s.k < n), ())
-    moved = move()
-    out = hidden_units(now(places), x[1], att[1], g[1], g_ffn[1], w_ffn[1])
-    dh[1], mlp[1] = HeadSum(rounds, out[4]), HeadSum(rounds, out[5])
-    close(*moved, out[0], dh[0].got)
-    moved = move()
-    close(dh[1].near(), dh[0].last())
-    dh[1].far()
-    grads[1] = grads_of(1, out)
-    close(*moved, grads[1][0], mlp[1].near())
-    if rings:
-        sums.append(Scatter(rounds, ring, grads[1][0::2], grads[1][1::2]))
-    moved = move()
-    dm[0], d_gain_ffn[0] = middle_back(now(places), x[0], att[0], g[0], dh[0].sum, g_ffn[0])
-    close(*moved, dm[0], dh[1].got)
-    mlp[0].far()
-    moved = move()
-    close(dh[1].last())
+        sums.append(Scatter(rounds, ring, grads[1]))
+
+    moved = (*add(0), *add(1))
+    got = mlp[1].far()
     dm[1], d_gain_ffn[1] = middle_back(now(places), x[1], att[1], g[1], dh[1].sum, g_ffn[1])
-    close(*moved, dm[1])
-
-    moved = move()
     d_qkv, part, d_gain0 = attend_back(now(places), x, dm, qkv, w_attn, 0, None, each)
     back = [HeadSum(rounds, part)]
-    close(*moved, part[0], mlp[0].got)
-    close(back[0].near(), mlp[0].last())
-    moved = move()
-    back[0].far()
+    close(*moved, part[0], got)
+    close(back[0].near(), mlp[1].last())
+    moved = add(0)
+    got = back[0].far()
     d_qkv, part, d_gain1 = attend_back(now(places), x, dm, qkv, w_attn, 1, d_qkv, each)
     back.append(HeadSum(rounds, part))
-    close(*moved, part[0], back[0].got)
-    close(back[1].near())
-    moved = move()
-    back[1].far()
-    sides = [
-        weight_grads(now(places), [(h1[c], d_qkv[c]), (dm[c], mixed[c])], 1 if rings else 0)
-        for c in range(sets)
-    ]
-    close(*moved, *[side[0] for side in sides], back[0].last())
+    close(*moved, part[0], got)
+    close(back[1].near(), back[0].last())
+    gain = gains[:sets]
+    moved = add(1)
+    got = back[1].far()
+    runs = [[(h1[c], d_qkv[c]), (dm[c], mixed[c])] for c in range(sets)]
     if rings:
-        sums.append(Scatter(rounds, ring, *sides))
+        blocks = weight_grads(now(places), runs, far)
+    else:
+        blocks = [weight_grads(now(places), [run], far)[0] for run in runs]
+    grad_input = input_back(now(places), x, dm, back[0].sum, gain, 0, None, shape)
+    close(*moved, blocks[0], grad_input, got)
+    if rings:
+        sums.append(Scatter(rounds, ring, blocks))
+
     shared = lax.axis_size("mp")
     d_gains = jnp.concatenate([d_gain0 + d_gain1, *[d / shared for d in d_gain_ffn]], 0)
     steps = list(exchange_steps(("dp", "mp")))
@@ -853,38 +889,31 @@
         axis, moves, _ = steps.pop(0)
         return value + lax.ppermute(now(value), axis, moves)
 
-    gain = gains[:sets]
-    moved = move()
+    moved = (*add(2), *add(1))
     d_gains = sum_step(d_gains)
-    mlp[1].far()
-    grad_input = input_back(now(places), x, dm, back[0].sum, gain, 0, None, shape)
-    close(*moved, grad_input, d_gains, back[1].got)
-    moved = move()
-    d_gains = sum_step(d_gains)
-    close(*moved, back[1].last(), d_gains)
-    moved = move()
+    output = output_of(now(places), x, att, [m.sum for m in mlp], shape)
+    close(*moved, back[1].last(), d_gains, output)
+    moved = (*add(2), *add(1))
     d_gains = sum_step(d_gains)
     grad_input = input_back(now(places), x, dm, back[1].sum, gain, 1, grad_input, shape)
-    close(*moved, grad_input, d_gains, mlp[1].got)
-    moved = move()
+    close(*moved, grad_input, d_gains)
+    moved = add(2)
     d_gains = sum_step(d_gains)
-    close(*moved, mlp[1].last(), d_gains)
-    moved = move()
-    output = output_of(now(places), x, att, [m.sum for m in mlp], shape)
-    d_gains = sum_step(d_gains)
-    close(*moved, output, d_gains)
-    moved = move()
     if rings:
-        ffn_sums = [list(s.sums()) for s in sums[:2]]
+        ffn_sums = [([now(t) for t in s.terms()], 0) for s in sums[:2]]
     else:
-        ffn_sums = [scatter(g_[0]) for g_ in grads]
-    d_gate_w, d_up_w, d_down_w = finish([[[now(t) for t in run] for run in side] for side in ffn_sums], 3)
-    close(*moved, d_gate_w)
-    moved = move()
+        ffn_sums = [([scatter(b[0])], 0) for b in grads]
+    d_gate_w, d_up_w, d_down_w = finish(ffn_sums, 3, own)
+    close(*moved, d_gate_w, d_gains)
+    moved = add(2)
     while steps:
         d_gains = sum_step(d_gains)
-    attn_sums = [[run] for run in sums[2].sums()] if rings else [scatter(side[0]) for side in sides]
-    d_query, d_key, d_value, d_out = finish(attn_sums, 4)
+    if rings:
+        terms = sums[2].terms()
+        attn_sums = [(terms, c * own) for c in range(sets)]
+    else:
+        attn_sums = [([scatter(b)], 0) for b in blocks]
+    d_query, d_key, d_value, d_out = finish(attn_sums, 4, own)
     d_gains = lax.dynamic_slice_in_dim(d_gains, ring.me * own, own, 1)
     return (
         output, grad_input, d_gains[:sets], d_query, d_key, d_value, d_out,

time: 529 us -> 479 us (0.905)
  starting transfers between devices: 109 us -> 73.6 us
  Pallas kernels: 206 us -> 200 us
    ppermute x5, waiting for transfers between devices: 5.1 us -> 44.4 us  [sum_step(): return value + lax.ppermute(now(value), axis, moves)]
    ppermute x21 -> x12, waiting for transfers between devices: 40 us -> 3.39 us  [step(): self.a = lax.ppermute(self.rounds.now(self.a), 'dp', self.ring.ahead)]
    ppermute x42 -> x24, starting transfers between devices: 42 us -> 26 us  [the longest x12 13.2 us: step(): self.b.append(lax.ppermute(self.rounds.now(b), 'dp', self.ring.behind))]
    ppermute x21 -> x12, waiting for transfers between devices: 13.1 us -> 2.47 us  [step(): self.b = lax.ppermute(self.rounds.now(self.b), 'dp', self.ring.behind)]
    ppermute x21 -> x12, starting transfers between devices: 22 us -> 11.7 us  [step(): self.a = lax.ppermute(self.rounds.now(self.a), 'dp', self.ring.ahead)]
    ppermute x21 -> x12, starting transfers between devices: 21.2 us -> 14.6 us  [step(): self.b = lax.ppermute(self.rounds.now(self.b), 'dp', self.ring.behind)]
    ppermute x42 -> x24, waiting for transfers between devices: 81.1 us -> 75.5 us  [the longest x12 69.3 us: step(): self.a.append(lax.ppermute(self.rounds.now(a), 'dp', self.ring.ahead))]
    pallas_call x20 -> x19, Pallas kernels: 206 us -> 200 us  [kernel_call(): pl.pallas_call(body, grid_spec=spec, out_shape=outs, input_output_aliases...]
  transfers between devices with their start and end apart: 116 -> 80, of which waited for: 56 -> 43; matrix products, arithmetic and copies ran while one was open for 5% -> 5% of each run, Pallas kernels for 39% -> 42%
where the time goes in v4:
time: 479 us; the launch traced here: 472 us
  Pallas kernels  200 us (42%)
  waiting for transfers between devices  168 us (35%)
  starting transfers between devices  73.6 us (15%)
  other arithmetic  14.6 us (3%)
  local copies, waits for them, and re-layouts  12.3 us (3%)
    pallas_call x19, Pallas kernels, kernel_call(): pl.pallas_call(body, grid_spec=spec, out_shape=outs, input_output_aliases...  200 us
    ppermute x12, waiting for transfers between devices, step(): self.a.append(lax.ppermute(self.rounds.now(a), 'dp', self.ring.ahead))  69.3 us
    ppermute x5, waiting for transfers between devices, sum_step(): return value + lax.ppermute(now(value), axis, moves)  44.4 us
    ppermute x8, waiting for transfers between devices, far(): self.got = lax.ppermute(self.rounds.now(self.mine), 'mp', self.far_moves)  17.1 us
    ppermute x12, starting transfers between devices, step(): self.b = lax.ppermute(self.rounds.now(self.b), 'dp', self.ring.behind)  14.6 us
    ppermute x12, starting transfers between devices, step(): self.b.append(lax.ppermute(self.rounds.now(b), 'dp', self.ring.behind))  13.2 us
    ppermute x12, starting transfers between devices, step(): self.a.append(lax.ppermute(self.rounds.now(a), 'dp', self.ring.ahead))  12.9 us
    ppermute x12, starting transfers between devices, step(): self.a = lax.ppermute(self.rounds.now(self.a), 'dp', self.ring.ahead)  11.7 us
  transfers between devices with their start and end apart: 80, of which 43 were waited for; matrix products, arithmetic and copies ran while one was open for 5% of the time, Pallas kernels for 42%

profile of v4, /device:TPU:0, one launch (start us, length us, event | category | flops | bytes accessed | tf_op | source)
XLA Modules:
  0.0 471.6 jit_solution(16223836779045492468)
XLA Ops:
  0.6 2.0 shard_map.203.refs_2_.refs_3_.refs_0_
  2.6 3.0 collective-permute-start.1
  6.3 2.0 collective-permute-start
  8.3 3.1 slice_bitcast_fusion.3.refs_0_.x_ref.x0
  11.4 2.1 shard_map.204.refs_5_
  13.5 4.3 collective-permute-done
  17.8 1.5 collective-permute-done.2.refs_3_.refs_4_.refs_1_
  19.3 1.6 collective-permute-start.4
  21.3 1.6 collective-permute-start.3
  22.9 3.3 slice_bitcast_fusion.2.refs_0_.x_ref.x1
  26.1 2.1 shard_map.205.refs_5_
  28.3 4.8 %collective-permute-done.3 = f32[2,4,128]{2,1,0:T(4,128)S(1)} collective-permute-done((f32[2,4,128]{2,1,0:T(4,128)S(1)}, f32[2,4,128]{2,1,0:T(4,128)S(1)}, u32[]{:S(2)}, u32[]{:S(2)}) %collective-permute-start.3) | collective-permute-done | bytes 4128 | tf_op jit(solution)/shard_map/ppermute | solution.py:767
  33.2 2.8 collective-permute-start.6
  36.3 1.7 collective-permute-start.8
  38.4 2.5 slice_bitcast_fusion
  40.9 6.5 %collective-permute-done.7.refs_7_.refs_8_.refs_5_ = bf16[256,1024]{1,0:T(8,128)(2,1)S(1)} collective-permute-done((bf16[256,1024]{1,0:T(8,128)(2,1)S(1)}, bf16[256,1024]{1,0:T(8,128)(2,1)S(1)}, u32[]{:S(2)}, u32[]{:S(2)}) %collective-permute-start.7) | collective-permute-done | bytes 524320 | tf_op jit(solution)/shard_map/ppermute | solution.py:664
  48.4 1.6 collective-permute-start.10
  50.0 6.0 %collective-permute-done.9.refs_6_.refs_4_ = bf16[128,1024]{1,0:T(8,128)(2,1)S(1)} collective-permute-done((bf16[128,1024]{1,0:T(8,128)(2,1)S(1)}, bf16[128,1024]{1,0:T(8,128)(2,1)S(1)}, u32[]{:S(2)}, u32[]{:S(2)}) %collective-permute-start.9) | collective-permute-done | bytes 262176 | tf_op jit(solution)/shard_map/ppermute | solution.py:664
  60.3 14.0 %shard_map.206 = (bf16[1024,1024]{1,0:T(8,128)(2,1)}, bf16[1024,768]{1,0:T(8,128)(2,1)}, bf16[1024,256]{1,0:T(8,128)(2,1)}, bf16[512,1024]{1,0:T(8,128)(2,1)}, bf16[512,1024]{1,0:T(8,128)(2,1)}) custom-call(s32[9]{0:T(128)} %pad_add_fusion.places._, bf16[1024,1024]{1,0:T(8,128)(2,1)} %slice_bitcast_fusion.3.refs_0_.x_ref.x0, ...), custom_call_target="tpu_custom_call" | custom-call | flops 1 | bytes 1 | tf_op jit(solution)/shard_map/pallas_call | solution.py:41
  74.4 2.9 collective-permute-done.13
  77.3 1.6 add_convert_fusion.15
  78.9 1.6 collective-permute-start.16
  82.5 13.0 %shard_map.207 = (bf16[1024,1024]{1,0:T(8,128)(2,1)}, bf16[1024,768]{1,0:T(8,128)(2,1)}, bf16[1024,256]{1,0:T(8,128)(2,1)}, bf16[512,1024]{1,0:T(8,128)(2,1)}, bf16[512,1024]{1,0:T(8,128)(2,1)}) custom-call(s32[9]{0:T(128)} %pad_add_fusion.places._, bf16[1024,1024]{1,0:T(8,128)(2,1)} %slice_bitcast_fusion.2.refs_0_.x_ref.x1, ...), custom_call_target="tpu_custom_call" | custom-call | flops 1 | bytes 1 | tf_op jit(solution)/shard_map/pallas_call | solution.py:41
  95.5 4.5 collective-permute-done.14.refs_12_
  100.9 3.3 collective-permute-done.16
  107.6 17.1 %collective-permute-done.17.refs_11_ = bf16[128,3072]{1,0:T(8,128)(2,1)S(1)} collective-permute-done((bf16[128,3072]{1,0:T(8,128)(2,1)S(1)}, bf16[128,3072]{1,0:T(8,128)(2,1)S(1)}, u32[]{:S(2)}, u32[]{:S(2)}) %collective-permute-start.17) | collective-permute-done | bytes 786464 | tf_op jit(solution)/shard_map/ppermute | solution.py:664
  125.6 1.5 collective-permute-start.25
  131.3 22.3 %collective-permute-done.22.refs_9_ = bf16[64,3072]{1,0:T(8,128)(2,1)S(1)} collective-permute-done((bf16[64,3072]{1,0:T(8,128)(2,1)S(1)}, bf16[64,3072]{1,0:T(8,128)(2,1)S(1)}, u32[]{:S(2)}, u32[]{:S(2)}) %collective-permute-start.22) | collective-permute-done | bytes 393248 | tf_op jit(solution)/shard_map/ppermute | solution.py:664
  155.5 1.9 collective-permute-start.27
  157.4 25.2 %shard_map.208 = (bf16[1024,1024]{1,0:T(8,128)(2,1)}, bf16[1024,1024]{1,0:T(8,128)(2,1)}, bf16[1024,1024]{1,0:T(8,128)(2,1)}, bf16[1024,1024]{1,0:T(8,128)(2,1)}...) custom-call(s32[9]{0:T(128)} %pad_add_fusion.places._, ...), custom_call_target="tpu_custom_call" | custom-call | flops 1 | bytes 1 | tf_op jit(solution)/shard_map/pallas_call | solution.py:41
  182.7 2.9 collective-permute-done.29
  185.5 1.6 add_convert_fusion.11
  190.0 13.8 %shard_map.209 = (bf16[128,3072]{1,0:T(8,128)(2,1)}, bf16[128,3072]{1,0:T(8,128)(2,1)}, bf16[128,3072]{1,0:T(8,128)(2,1)}, bf16[128,3072]{1,0:T(8,128)(2,1)}, bf...) custom-call(s32[9]{0:T(128)} %pad_add_fusion.places._, ...), custom_call_target="tpu_custom_call" | custom-call | flops 1 | bytes 1 | tf_op jit(solution)/shard_map/pallas_call | solution.py:41
  204.2 3.5 collective-permute-done.30.refs_11_
  208.1 4.7 %collective-permute-done.32 = bf16[512,1024]{1,0:T(8,128)(2,1)S(1)} collective-permute-done((bf16[512,1024]{1,0:T(8,128)(2,1)S(1)}, bf16[512,1024]{1,0:T(8,128)(2,1)S(1)}, u32[]{:S(2)}, u32[]{:S(2)}) %collective-permute-start.32) | collective-permute-done | bytes 1048608 | tf_op jit(solution)/shard_map/ppermute | solution.py:726
  215.5 9.5 %collective-permute-done.34.refs_9_ = bf16[64,3072]{1,0:T(8,128)(2,1)S(1)} collective-permute-done((bf16[64,3072]{1,0:T(8,128)(2,1)S(1)}, bf16[64,3072]{1,0:T(8,128)(2,1)S(1)}, u32[]{:S(2)}, u32[]{:S(2)}) %collective-permute-start.34) | collective-permute-done | bytes 393248 | tf_op jit(solution)/shard_map/ppermute | solution.py:664
  228.2 25.2 %shard_map.210 = (bf16[1024,1024]{1,0:T(8,128)(2,1)}, bf16[1024,1024]{1,0:T(8,128)(2,1)}, bf16[1024,1024]{1,0:T(8,128)(2,1)}, bf16[1024,1024]{1,0:T(8,128)(2,1)}...) custom-call(s32[9]{0:T(128)} %pad_add_fusion.places._, ...), custom_call_target="tpu_custom_call" | custom-call | flops 1 | bytes 1 | tf_op jit(solution)/shard_map/pallas_call | solution.py:41
  254.6 1.7 collective-permute-done.40
  257.7 1.5 collective-permute-start.42
  261.4 13.7 %shard_map.211 = (bf16[128,3072]{1,0:T(8,128)(2,1)}, bf16[128,3072]{1,0:T(8,128)(2,1)}, bf16[128,3072]{1,0:T(8,128)(2,1)}, bf16[128,3072]{1,0:T(8,128)(2,1)}, bf...) custom-call(s32[9]{0:T(128)} %pad_add_fusion.places._, ...), custom_call_target="tpu_custom_call" | custom-call | flops 1 | bytes 1 | tf_op jit(solution)/shard_map/pallas_call | solution.py:41
  275.1 7.5 %shard_map.212 = (bf16[1024,1024]{1,0:T(8,128)(2,1)}, f32[1,1024]{1,0:T(1,128)}) custom-call(s32[9]{0:T(128)} %pad_add_fusion.places._, bf16[1024,1024]{1,0:T(8,128)(2,1)} %slice_bitcast_fusion.3.refs_0_.x_ref.x0, bf16[512,1024]{1,0:T(8,128)(2,1)} %copy-done, bf16[512,1024]{1,0:T(8,128)(2,1)} %copy-done.4, ...), custom_call_target="tpu_custom_call" | custom-call | flops 1 | bytes 1 | tf_op jit(solution)/shard_map/pallas_call | solution.py:41
  287.0 1.5 collective-permute-start.51
  293.0 7.4 %shard_map.213 = (bf16[1024,1024]{1,0:T(8,128)(2,1)}, f32[1,1024]{1,0:T(1,128)}) custom-call(s32[9]{0:T(128)} %pad_add_fusion.places._, bf16[1024,1024]{1,0:T(8,128)(2,1)} %slice_bitcast_fusion.2.refs_0_.x_ref.x1, bf16[512,1024]{1,0:T(8,128)(2,1)} %copy-done.1, bf16[512,1024]{1,0:T(8,128)(2,1)} %copy-done.5, ...), custom_call_target="tpu_custom_call" | custom-call | flops 1 | bytes 1 | tf_op jit(solution)/shard_map/pallas_call | solution.py:41
  300.4 17.6 %shard_map.214 = (bf16[1024,768]{1,0:T(8,128)(2,1)}, bf16[1024,768]{1,0:T(8,128)(2,1)}, bf16[512,1024]{1,0:T(8,128)(2,1)}, bf16[512,1024]{1,0:T(8,128)(2,1)}, f32[2,1024]{1,0:T(2,128)}) custom-call(s32[9]{0:T(128)} %pad_add_fusion.places._, bf16[1024,1024]{1,0:T(8,128)(2,1)} %slice_bitcast_fusion.3.refs_0_.x_ref.x0, ...), custom_call_target="tpu_custom_call" | custom-call | flops 1 | bytes 1 | tf_op jit(solution)/shard_map/pallas_call | solution.py:41
  319.2 1.9 collective-permute-done.52
  325.8 17.6 %shard_map.215 = (bf16[1024,768]{1,0:T(8,128)(2,1)}, bf16[1024,768]{1,0:T(8,128)(2,1)}, bf16[512,1024]{1,0:T(8,128)(2,1)}, bf16[512,1024]{1,0:T(8,128)(2,1)}, f32[2,1024]{1,0:T(2,128)}) custom-call(s32[9]{0:T(128)} %pad_add_fusion.places._, bf16[1024,1024]{1,0:T(8,128)(2,1)} %slice_bitcast_fusion.3.refs_0_.x_ref.x0, ...), custom_call_target="tpu_custom_call", output_to_operand_aliasing={{0}: (16, {}), {1}: (17, {})} | custom-call | flops 1 | bytes 1 | tf_op jit(solution)/shard_map/pallas_call | solution.py:41
  344.0 3.5 collective-permute-done.56
  355.0 11.2 %shard_map.216 = (bf16[256,1024]{1,0:T(8,128)(2,1)}, bf16[256,1024]{1,0:T(8,128)(2,1)}, bf16[256,1024]{1,0:T(8,128)(2,1)}, bf16[256,1024]{1,0:T(8,128)(2,1)}, bf...) custom-call(s32[9]{0:T(128)} %pad_add_fusion.places._, ...), custom_call_target="tpu_custom_call" | custom-call | flops 1 | bytes 1 | tf_op jit(solution)/shard_map/pallas_call | solution.py:41
  366.3 6.3 %shard_map.217.refs_0_ = bf16[128,16,1024]{2,1,0:T(8,128)(2,1)} custom-call(s32[9]{0:T(128)} %pad_add_fusion.places._, bf16[1024,1024]{1,0:T(8,128)(2,1)} %slice_bitcast_fusion.3.refs_0_.x_ref.x0, bf16[1024,1024]{1,0:T(8,128)(2,1)} %slice_bitcast_fusion.2.refs_0_.x_ref.x1, bf16[1024,1024]{1,0:T(8,128)(2,1)} %get-tuple-element.256.dm0.refs_2_.refs_3_, ...), custom_call_target="tpu_custom_call" | custom-call | flops 1 | bytes 1 | tf_op jit(solution)/shard_map/pallas_call | solution.py:41
  373.2 5.3 %collective-permute-done.61 = bf16[512,1024]{1,0:T(8,128)(2,1)S(1)} collective-permute-done((bf16[512,1024]{1,0:T(8,128)(2,1)S(1)}, bf16[512,1024]{1,0:T(8,128)(2,1)S(1)}, u32[]{:S(2)}, u32[]{:S(2)}) %collective-permute-start.61) | collective-permute-done | bytes 1048608 | tf_op jit(solution)/shard_map/ppermute | solution.py:726
  379.9 1.5 collective-permute-start.62
  384.1 8.7 %shard_map.218 = bf16[128,16,1024]{2,1,0:T(8,128)(2,1)} custom-call(s32[9]{0:T(128)} %pad_add_fusion.places._, bf16[1024,1024]{1,0:T(8,128)(2,1)} %slice_bitcast_fusion.3.refs_0_.x_ref.x0, bf16[1024,1024]{1,0:T(8,128)(2,1)} %slice_bitcast_fusion.2.refs_0_.x_ref.x1, bf16[512,1024]{1,0:T(8,128)(2,1)} %copy-done, bf16[512,1024]{1,0:T(8,128)(2,1)} %copy-done.4, ...), custom_call_target="tpu_custom_call" | custom-call | flops 1 | bytes 1 | tf_op jit(solution)/shard_map/pallas_call | solution.py:41
  392.7 10.8 %collective-permute-done.67 = f32[4,1024]{1,0:T(4,128)S(1)} collective-permute-done((f32[4,1024]{1,0:T(4,128)S(1)}, f32[4,1024]{1,0:T(4,128)S(1)}, u32[]{:S(2)}, u32[]{:S(2)}) %collective-permute-start.67) | collective-permute-done | bytes 16416 | tf_op jit(solution)/shard_map/ppermute | solution.py:890
  407.3 2.0 collective-permute-start.72
  409.4 2.1 collective-permute-start.70
  411.7 6.2 %shard_map.219 = bf16[128,16,1024]{2,1,0:T(8,128)(2,1)} custom-call(s32[9]{0:T(128)} %pad_add_fusion.places._, bf16[1024,1024]{1,0:T(8,128)(2,1)} %slice_bitcast_fusion.3.refs_0_.x_ref.x0, bf16[1024,1024]{1,0:T(8,128)(2,1)} %slice_bitcast_fusion.2.refs_0_.x_ref.x1, ...), custom_call_target="tpu_custom_call", output_to_operand_aliasing={{}: (8, {})} | custom-call | flops 1 | bytes 1 | tf_op jit(solution)/shard_map/pallas_call | solution.py:41
  417.8 22.5 %collective-permute-done.68 = f32[4,1024]{1,0:T(4,128)S(1)} collective-permute-done((f32[4,1024]{1,0:T(4,128)S(1)}, f32[4,1024]{1,0:T(4,128)S(1)}, u32[]{:S(2)}, u32[]{:S(2)}) %collective-permute-start.68) | collective-permute-done | bytes 16416 | tf_op jit(solution)/shard_map/ppermute | solution.py:890
  442.9 1.5 collective-permute-start.73
  444.4 4.5 shard_map.220
  449.0 6.7 %collective-permute-done.73 = f32[4,1024]{1,0:T(4,128)S(1)} collective-permute-done((f32[4,1024]{1,0:T(4,128)S(1)}, f32[4,1024]{1,0:T(4,128)S(1)}, u32[]{:S(2)}, u32[]{:S(2)}) %collective-permute-start.73) | collective-permute-done | bytes 16416 | tf_op jit(solution)/shard_map/ppermute | solution.py:890
  456.2 2.0 collective-permute-start.79
  459.9 3.2 collective-permute-done.77
  463.7 3.4 collective-permute-done.78.refs_1_
  468.7 2.4 shard_map.221
  (338 shorter events, 72.8 us)
Async XLA Ops:
  2.6 15.2 %collective-permute-start.1 = (bf16[256,1024]{1,0:T(8,128)(2,1)}, bf16[256,1024]{1,0:T(8,128)(2,1)S(1)}, u32[]{:S(2)}, u32[]{:S(2)}) collective-permute-start(bf16[256,1024]{1,0:T(8,128)(2,1)} %shard_map.203.refs_2_.refs_3_.refs_0_), channel_id=1, source_target_pairs={{0,8},{8,16},{16,24},{24,28},{28,20},{20,12},{12,4},{4,0},{1,9},{9... | collective-permute-start | bytes 1572872 | tf_op jit(solution)/shard_map/ppermute | solution.py:664
  5.7 13.6 %collective-permute-start.2 = (bf16[256,1024]{1,0:T(8,128)(2,1)}, bf16[256,1024]{1,0:T(8,128)(2,1)S(1)}, u32[]{:S(2)}, u32[]{:S(2)}) collective-permute-start(bf16[256,1024]{1,0:T(8,128)(2,1)} %shard_map.203.refs_2_.refs_3_.refs_0_), channel_id=1, source_target_pairs={{8,0},{16,8},{24,16},{28,24},{20,28},{12,20},{4,12},{0,4},{9,1},{1... | collective-permute-start | bytes 1572872 | tf_op jit(solution)/shard_map/ppermute | solution.py:665
  6.3 11.4 %collective-permute-start = (f32[1,4,128]{2,1,0:T(4,128)S(1)}, f32[1,4,128]{2,1,0:T(4,128)S(1)}, u32[]{:S(2)}, u32[]{:S(2)}) collective-permute-start(f32[1,4,128]{2,1,0:T(4,128)S(1)} %maximum_convert_fusion), channel_id=1, source_target_pairs={{0,4},{4,0},{8,12},{12,8},{16,20},{20,16},{24,28},{28,24},{1,5},{5... | collective-permute-start | bytes 6152 | tf_op jit(solution)/shard_map/ppermute | solution.py:767
  19.3 13.9 %collective-permute-start.4 = (bf16[256,1024]{1,0:T(8,128)(2,1)S(1)}, bf16[256,1024]{1,0:T(8,128)(2,1)S(1)}, u32[]{:S(2)}, u32[]{:S(2)}) collective-permute-start(bf16[256,1024]{1,0:T(8,128)(2,1)S(1)} %collective-permute-done.1.refs_9_.refs_10_.refs_7_), channel_id=1, source_target_pairs={{0,8},{8,16},{16,24},{24,28},{28,20},{20,12},{12,4},{4,0},{1,9},{9... | collective-permute-start | bytes 1572872 | tf_op jit(solution)/shard_map/ppermute | solution.py:664
  20.8 12.3 %collective-permute-start.5 = (bf16[256,1024]{1,0:T(8,128)(2,1)S(1)}, bf16[256,1024]{1,0:T(8,128)(2,1)S(1)}, u32[]{:S(2)}, u32[]{:S(2)}) collective-permute-start(bf16[256,1024]{1,0:T(8,128)(2,1)S(1)} %collective-permute-done.2.refs_3_.refs_4_.refs_1_), channel_id=1, source_target_pairs={{8,0},{16,8},{24,16},{28,24},{20,28},{12,20},{4,12},{0,4},{9,1},{1... | collective-permute-start | bytes 1572872 | tf_op jit(solution)/shard_map/ppermute | solution.py:665
  21.3 11.8 %collective-permute-start.3 = (f32[2,4,128]{2,1,0:T(4,128)S(1)}, f32[2,4,128]{2,1,0:T(4,128)S(1)}, u32[]{:S(2)}, u32[]{:S(2)}) collective-permute-start(f32[2,4,128]{2,1,0:T(4,128)S(1)} %maximum_select_fusion.2), channel_id=1, source_target_pairs={{0,8},{4,12},{8,0},{12,4},{16,24},{20,28},{24,16},{28,20},{1,9},{5... | collective-permute-start | bytes 12296 | tf_op jit(solution)/shard_map/ppermute | solution.py:767
  36.0 11.4 %collective-permute-start.7 = (bf16[256,1024]{1,0:T(8,128)(2,1)S(1)}, bf16[256,1024]{1,0:T(8,128)(2,1)S(1)}, u32[]{:S(2)}, u32[]{:S(2)}) collective-permute-start(bf16[256,1024]{1,0:T(8,128)(2,1)S(1)} %collective-permute-done.4.refs_8_.refs_9_.refs_6_), channel_id=1, source_target_pairs={{0,8},{8,16},{16,24},{24,28},{28,20},{20,12},{12,4},{4,0},{1,9},{9... | collective-permute-start | bytes 1572872 | tf_op jit(solution)/shard_map/ppermute | solution.py:664
  36.3 11.6 %collective-permute-start.8 = (bf16[256,1024]{1,0:T(8,128)(2,1)S(1)}, bf16[256,1024]{1,0:T(8,128)(2,1)S(1)}, u32[]{:S(2)}, u32[]{:S(2)}) collective-permute-start(bf16[256,1024]{1,0:T(8,128)(2,1)S(1)} %collective-permute-done.5.refs_4_.refs_5_.refs_2_), channel_id=1, source_target_pairs={{8,0},{16,8},{24,16},{28,24},{20,28},{12,20},{4,12},{0,4},{9,1},{1... | collective-permute-start | bytes 1572872 | tf_op jit(solution)/shard_map/ppermute | solution.py:665
  48.4 8.6 %collective-permute-start.10 = (bf16[128,1024]{1,0:T(8,128)(2,1)S(1)}, bf16[128,1024]{1,0:T(8,128)(2,1)S(1)}, u32[]{:S(2)}, u32[]{:S(2)}) collective-permute-start(bf16[128,1024]{1,0:T(8,128)(2,1)S(1)} %slice.92), channel_id=1, source_target_pairs={{8,0},{16,8},{24,16},{28,24},{20,28},{12,20},{4,12},{0,4},{9,1},{1... | collective-permute-start | bytes 786440 | tf_op jit(solution)/shard_map/ppermute | solution.py:665
  57.0 17.3 %collective-permute-start.11 = (bf16[128,3072]{1,0:T(8,128)(2,1)S(1)}, bf16[128,3072]{1,0:T(8,128)(2,1)}, u32[]{:S(2)}, u32[]{:S(2)}) collective-permute-start(bf16[128,3072]{1,0:T(8,128)(2,1)S(1)} %copy-done.17), channel_id=1, source_target_pairs={{0,8},{8,16},{16,24},{24,28},{28,20},{20,12},{12,4},{4,0},{1,9},{9... | collective-permute-start | bytes 2359304 | tf_op jit(solution)/shard_map/ppermute | solution.py:664
  58.2 16.1 %collective-permute-start.12 = (bf16[128,3072]{1,0:T(8,128)(2,1)S(1)}, bf16[128,3072]{1,0:T(8,128)(2,1)}, u32[]{:S(2)}, u32[]{:S(2)}) collective-permute-start(bf16[128,3072]{1,0:T(8,128)(2,1)S(1)} %copy-done.17), channel_id=1, source_target_pairs={{8,0},{16,8},{24,16},{28,24},{20,28},{12,20},{4,12},{0,4},{9,1},{1... | collective-permute-start | bytes 2359304 | tf_op jit(solution)/shard_map/ppermute | solution.py:665
  78.9 25.3 %collective-permute-start.16 = (bf16[512,1024]{1,0:T(8,128)(2,1)S(1)}, bf16[512,1024]{1,0:T(8,128)(2,1)S(1)}, u32[]{:S(2)}, u32[]{:S(2)}) collective-permute-start(bf16[512,1024]{1,0:T(8,128)(2,1)S(1)} %add_convert_fusion.15), channel_id=1, source_target_pairs={{0,2},{1,3},{2,0},{3,1},{4,6},{5,7},{6,4},{7,5},{8,10},{9,11},{10,... | collective-permute-start | bytes 3145736 | tf_op jit(solution)/shard_map/ppermute | solution.py:726
  80.4 19.5 %collective-permute-start.14 = (bf16[128,3072]{1,0:T(8,128)(2,1)}, bf16[128,3072]{1,0:T(8,128)(2,1)S(1)}, u32[]{:S(2)}, u32[]{:S(2)}) collective-permute-start(bf16[128,3072]{1,0:T(8,128)(2,1)} %collective-permute-done.11.refs_13_), channel_id=1, source_target_pairs={{0,8},{8,16},{16,24},{24,28},{28,20},{20,12},{12,4},{4,0},{1,9},{9... | collective-permute-start | bytes 2359304 | tf_op jit(solution)/shard_map/ppermute | solution.py:664
  81.6 19.2 %collective-permute-start.15 = (bf16[128,3072]{1,0:T(8,128)(2,1)}, bf16[128,3072]{1,0:T(8,128)(2,1)S(1)}, u32[]{:S(2)}, u32[]{:S(2)}) collective-permute-start(bf16[128,3072]{1,0:T(8,128)(2,1)} %collective-permute-done.12.refs_6_), channel_id=1, source_target_pairs={{8,0},{16,8},{24,16},{28,24},{20,28},{12,20},{4,12},{0,4},{9,1},{1... | collective-permute-start | bytes 2359304 | tf_op jit(solution)/shard_map/ppermute | solution.py:665
  104.6 21.0 %collective-permute-start.20 = (bf16[512,1024]{1,0:T(8,128)(2,1)S(1)}, bf16[512,1024]{1,0:T(8,128)(2,1)S(1)}, u32[]{:S(2)}, u32[]{:S(2)}) collective-permute-start(bf16[512,1024]{1,0:T(8,128)(2,1)S(1)} %add_convert_fusion.13.refs_1_.att0.refs_0_), channel_id=1, source_target_pairs={{0,1},{1,0},{2,3},{3,2},{4,5},{5,4},{6,7},{7,6},{8,9},{9,8},{10,11... | collective-permute-start | bytes 3145736 | tf_op jit(solution)/shard_map/ppermute | solution.py:731
  105.1 19.5 %collective-permute-start.17 = (bf16[128,3072]{1,0:T(8,128)(2,1)S(1)}, bf16[128,3072]{1,0:T(8,128)(2,1)S(1)}, u32[]{:S(2)}, u32[]{:S(2)}) collective-permute-start(bf16[128,3072]{1,0:T(8,128)(2,1)S(1)} %collective-permute-done.14.refs_12_), channel_id=1, source_target_pairs={{0,8},{8,16},{16,24},{24,28},{28,20},{20,12},{12,4},{4,0},{1,9},{9... | collective-permute-start | bytes 2359304 | tf_op jit(solution)/shard_map/ppermute | solution.py:664
  106.4 19.2 %collective-permute-start.18 = (bf16[128,3072]{1,0:T(8,128)(2,1)S(1)}, bf16[128,3072]{1,0:T(8,128)(2,1)S(1)}, u32[]{:S(2)}, u32[]{:S(2)}) collective-permute-start(bf16[128,3072]{1,0:T(8,128)(2,1)S(1)} %collective-permute-done.15.refs_7_), channel_id=1, source_target_pairs={{8,0},{16,8},{24,16},{28,24},{20,28},{12,20},{4,12},{0,4},{9,1},{1... | collective-permute-start | bytes 2359304 | tf_op jit(solution)/shard_map/ppermute | solution.py:665
  125.6 28.6 %collective-permute-start.25 = (bf16[512,1024]{1,0:T(8,128)(2,1)S(1)}, bf16[512,1024]{1,0:T(8,128)(2,1)S(1)}, u32[]{:S(2)}, u32[]{:S(2)}) collective-permute-start(bf16[512,1024]{1,0:T(8,128)(2,1)S(1)} %add_convert_fusion.14), channel_id=1, source_target_pairs={{0,2},{1,3},{2,0},{3,1},{4,6},{5,7},{6,4},{7,5},{8,10},{9,11},{10,... | collective-permute-start | bytes 3145736 | tf_op jit(solution)/shard_map/ppermute | solution.py:726
  127.1 27.1 %collective-permute-start.21 = (bf16[128,3072]{1,0:T(8,128)(2,1)S(1)}, bf16[128,3072]{1,0:T(8,128)(2,1)S(1)}, u32[]{:S(2)}, u32[]{:S(2)}) collective-permute-start(bf16[128,3072]{1,0:T(8,128)(2,1)S(1)} %copy-done.18), channel_id=1, source_target_pairs={{0,8},{8,16},{16,24},{24,28},{28,20},{20,12},{12,4},{4,0},{1,9},{9... | collective-permute-start | bytes 2359304 | tf_op jit(solution)/shard_map/ppermute | solution.py:664
  128.0 26.2 %collective-permute-start.24 = (bf16[128,3072]{1,0:T(8,128)(2,1)S(1)}, bf16[128,3072]{1,0:T(8,128)(2,1)S(1)}, u32[]{:S(2)}, u32[]{:S(2)}) collective-permute-start(bf16[128,3072]{1,0:T(8,128)(2,1)S(1)} %copy-done.18), channel_id=1, source_target_pairs={{8,0},{16,8},{24,16},{28,24},{20,28},{12,20},{4,12},{0,4},{9,1},{1... | collective-permute-start | bytes 2359304 | tf_op jit(solution)/shard_map/ppermute | solution.py:665
  129.2 24.4 %collective-permute-start.22 = (bf16[64,3072]{1,0:T(8,128)(2,1)S(1)}, bf16[64,3072]{1,0:T(8,128)(2,1)S(1)}, u32[]{:S(2)}, u32[]{:S(2)}) collective-permute-start(bf16[64,3072]{1,0:T(8,128)(2,1)S(1)} %slice.95), channel_id=1, source_target_pairs={{0,8},{8,16},{16,24},{24,28},{28,20},{20,12},{12,4},{4,0},{1,9},{9... | collective-permute-start | bytes 1179656 | tf_op jit(solution)/shard_map/ppermute | solution.py:664
  130.1 24.1 %collective-permute-start.23 = (bf16[64,3072]{1,0:T(8,128)(2,1)S(1)}, bf16[64,3072]{1,0:T(8,128)(2,1)S(1)}, u32[]{:S(2)}, u32[]{:S(2)}) collective-permute-start(bf16[64,3072]{1,0:T(8,128)(2,1)S(1)} %slice.96), channel_id=1, source_target_pairs={{8,0},{16,8},{24,16},{28,24},{20,28},{12,20},{4,12},{0,4},{9,1},{1... | collective-permute-start | bytes 1179656 | tf_op jit(solution)/shard_map/ppermute | solution.py:665
  154.7 27.9 %collective-permute-start.28 = (bf16[512,1024]{1,0:T(8,128)(2,1)S(1)}, bf16[512,1024]{1,0:T(8,128)(2,1)S(1)}, u32[]{:S(2)}, u32[]{:S(2)}) collective-permute-start(bf16[512,1024]{1,0:T(8,128)(2,1)S(1)} %add_convert_fusion.12.refs_1_.att0.refs_4_), channel_id=1, source_target_pairs={{0,1},{1,0},{2,3},{3,2},{4,5},{5,4},{6,7},{7,6},{8,9},{9,8},{10,11... | collective-permute-start | bytes 3145736 | tf_op jit(solution)/shard_map/ppermute | solution.py:731
  154.8 27.8 %collective-permute-start.26 = (bf16[128,3072]{1,0:T(8,128)(2,1)S(1)}, bf16[128,3072]{1,0:T(8,128)(2,1)}, u32[]{:S(2)}, u32[]{:S(2)}) collective-permute-start(bf16[128,3072]{1,0:T(8,128)(2,1)S(1)} %collective-permute-done.21.refs_13_), channel_id=1, source_target_pairs={{0,8},{8,16},{16,24},{24,28},{28,20},{20,12},{12,4},{4,0},{1,9},{9... | collective-permute-start | bytes 2359304 | tf_op jit(solution)/shard_map/ppermute | solution.py:664
  155.5 27.1 %collective-permute-start.27 = (bf16[128,3072]{1,0:T(8,128)(2,1)S(1)}, bf16[128,3072]{1,0:T(8,128)(2,1)}, u32[]{:S(2)}, u32[]{:S(2)}) collective-permute-start(bf16[128,3072]{1,0:T(8,128)(2,1)S(1)} %collective-permute-done.24.refs_6_), channel_id=1, source_target_pairs={{8,0},{16,8},{24,16},{28,24},{20,28},{12,20},{4,12},{0,4},{9,1},{1... | collective-permute-start | bytes 2359304 | tf_op jit(solution)/shard_map/ppermute | solution.py:665
  187.2 16.6 %collective-permute-start.33 = (bf16[512,1024]{1,0:T(8,128)(2,1)}, bf16[512,1024]{1,0:T(8,128)(2,1)S(1)}, u32[]{:S(2)}, u32[]{:S(2)}) collective-permute-start(bf16[512,1024]{1,0:T(8,128)(2,1)} %get-tuple-element.229), channel_id=1, source_target_pairs={{0,1},{1,0},{2,3},{3,2},{4,5},{5,4},{6,7},{7,6},{8,9},{9,8},{10,11... | collective-permute-start | bytes 3145736 | tf_op jit(solution)/shard_map/ppermute | solution.py:721
  187.4 25.4 %collective-permute-start.32 = (bf16[512,1024]{1,0:T(8,128)(2,1)S(1)}, bf16[512,1024]{1,0:T(8,128)(2,1)S(1)}, u32[]{:S(2)}, u32[]{:S(2)}) collective-permute-start(bf16[512,1024]{1,0:T(8,128)(2,1)S(1)} %add_convert_fusion.11), channel_id=1, source_target_pairs={{0,2},{1,3},{2,0},{3,1},{4,6},{5,7},{6,4},{7,5},{8,10},{9,11},{10,... | collective-permute-start | bytes 3145736 | tf_op jit(solution)/shard_map/ppermute | solution.py:726
  187.9 19.7 %collective-permute-start.30 = (bf16[128,3072]{1,0:T(8,128)(2,1)}, bf16[128,3072]{1,0:T(8,128)(2,1)S(1)}, u32[]{:S(2)}, u32[]{:S(2)}) collective-permute-start(bf16[128,3072]{1,0:T(8,128)(2,1)} %collective-permute-done.26.refs_12_), channel_id=1, source_target_pairs={{0,8},{8,16},{16,24},{24,28},{28,20},{20,12},{12,4},{4,0},{1,9},{9... | collective-permute-start | bytes 2359304 | tf_op jit(solution)/shard_map/ppermute | solution.py:664
  188.6 19.5 %collective-permute-start.31 = (bf16[128,3072]{1,0:T(8,128)(2,1)}, bf16[128,3072]{1,0:T(8,128)(2,1)S(1)}, u32[]{:S(2)}, u32[]{:S(2)}) collective-permute-start(bf16[128,3072]{1,0:T(8,128)(2,1)} %collective-permute-done.27.refs_7_), channel_id=1, source_target_pairs={{8,0},{16,8},{24,16},{28,24},{20,28},{12,20},{4,12},{0,4},{9,1},{1... | collective-permute-start | bytes 2359304 | tf_op jit(solution)/shard_map/ppermute | solution.py:665
  213.2 12.2 %collective-permute-start.36 = (bf16[512,1024]{1,0:T(8,128)(2,1)S(1)}, bf16[512,1024]{1,0:T(8,128)(2,1)S(1)}, u32[]{:S(2)}, u32[]{:S(2)}) collective-permute-start(bf16[512,1024]{1,0:T(8,128)(2,1)S(1)} %add_convert_fusion.9.dh0), channel_id=1, source_target_pairs={{0,1},{1,0},{2,3},{3,2},{4,5},{5,4},{6,7},{7,6},{8,9},{9,8},{10,11... | collective-permute-start | bytes 3145736 | tf_op jit(solution)/shard_map/ppermute | solution.py:731
  213.4 11.6 %collective-permute-start.34 = (bf16[64,3072]{1,0:T(8,128)(2,1)S(1)}, bf16[64,3072]{1,0:T(8,128)(2,1)S(1)}, u32[]{:S(2)}, u32[]{:S(2)}) collective-permute-start(bf16[64,3072]{1,0:T(8,128)(2,1)S(1)} %slice.99), channel_id=1, source_target_pairs={{0,8},{8,16},{16,24},{24,28},{28,20},{20,12},{12,4},{4,0},{1,9},{9... | collective-permute-start | bytes 1179656 | tf_op jit(solution)/shard_map/ppermute | solution.py:664
  214.1 11.2 %collective-permute-start.35 = (bf16[64,3072]{1,0:T(8,128)(2,1)S(1)}, bf16[64,3072]{1,0:T(8,128)(2,1)S(1)}, u32[]{:S(2)}, u32[]{:S(2)}) collective-permute-start(bf16[64,3072]{1,0:T(8,128)(2,1)S(1)} %slice.100), channel_id=1, source_target_pairs={{8,0},{16,8},{24,16},{28,24},{20,28},{12,20},{4,12},{0,4},{9,1},{1... | collective-permute-start | bytes 1179656 | tf_op jit(solution)/shard_map/ppermute | solution.py:665
  225.4 28.0 %collective-permute-start.39 = (bf16[512,1024]{1,0:T(8,128)(2,1)S(1)}, bf16[512,1024]{1,0:T(8,128)(2,1)S(1)}, u32[]{:S(2)}, u32[]{:S(2)}) collective-permute-start(bf16[512,1024]{1,0:T(8,128)(2,1)S(1)} %add_convert_fusion.10), channel_id=1, source_target_pairs={{0,2},{1,3},{2,0},{3,1},{4,6},{5,7},{6,4},{7,5},{8,10},{9,11},{10,... | collective-permute-start | bytes 3145736 | tf_op jit(solution)/shard_map/ppermute | solution.py:726
  226.0 27.4 %collective-permute-start.37 = (bf16[64,3072]{1,0:T(8,128)(2,1)S(1)}, bf16[64,3072]{1,0:T(8,128)(2,1)S(1)}, u32[]{:S(2)}, u32[]{:S(2)}) collective-permute-start(bf16[64,3072]{1,0:T(8,128)(2,1)S(1)} %copy-done.79), channel_id=1, source_target_pairs={{0,8},{8,16},{16,24},{24,28},{28,20},{20,12},{12,4},{4,0},{1,9},{9... | collective-permute-start | bytes 1179656 | tf_op jit(solution)/shard_map/ppermute | solution.py:702
  227.1 26.3 %collective-permute-start.38 = (bf16[64,3072]{1,0:T(8,128)(2,1)S(1)}, bf16[64,3072]{1,0:T(8,128)(2,1)S(1)}, u32[]{:S(2)}, u32[]{:S(2)}) collective-permute-start(bf16[64,3072]{1,0:T(8,128)(2,1)S(1)} %copy-done.77), channel_id=1, source_target_pairs={{8,0},{16,8},{24,16},{28,24},{20,28},{12,20},{4,12},{0,4},{9,1},{1... | collective-permute-start | bytes 1179656 | tf_op jit(solution)/shard_map/ppermute | solution.py:703
  257.7 25.2 %collective-permute-start.42 = (bf16[512,1024]{1,0:T(8,128)(2,1)S(1)}, bf16[512,1024]{1,0:T(8,128)(2,1)S(1)}, u32[]{:S(2)}, u32[]{:S(2)}) collective-permute-start(bf16[512,1024]{1,0:T(8,128)(2,1)S(1)} %add_convert_fusion.8), channel_id=1, source_target_pairs={{0,2},{1,3},{2,0},{3,1},{4,6},{5,7},{6,4},{7,5},{8,10},{9,11},{10,... | collective-permute-start | bytes 3145736 | tf_op jit(solution)/shard_map/ppermute | solution.py:726
  259.3 23.3 %collective-permute-start.43 = (bf16[128,3072]{1,0:T(8,128)(2,1)S(1)}, bf16[128,3072]{1,0:T(8,128)(2,1)S(1)}, u32[]{:S(2)}, u32[]{:S(2)}) collective-permute-start(bf16[128,3072]{1,0:T(8,128)(2,1)S(1)} %add_convert_fusion.27), channel_id=1, source_target_pairs={{0,8},{8,16},{16,24},{24,28},{28,20},{20,12},{12,4},{4,0},{1,9},{9... | collective-permute-start | bytes 2359304 | tf_op jit(solution)/shard_map/ppermute | solution.py:702
  260.5 22.1 %collective-permute-start.44 = (bf16[128,3072]{1,0:T(8,128)(2,1)S(1)}, bf16[128,3072]{1,0:T(8,128)(2,1)S(1)}, u32[]{:S(2)}, u32[]{:S(2)}) collective-permute-start(bf16[128,3072]{1,0:T(8,128)(2,1)S(1)} %add_convert_fusion.26), channel_id=1, source_target_pairs={{8,0},{16,8},{24,16},{28,24},{20,28},{12,20},{4,12},{0,4},{9,1},{1... | collective-permute-start | bytes 2359304 | tf_op jit(solution)/shard_map/ppermute | solution.py:703
  287.0 31.1 %collective-permute-start.51 = (bf16[512,1024]{1,0:T(8,128)(2,1)S(1)}, bf16[512,1024]{1,0:T(8,128)(2,1)S(1)}, u32[]{:S(2)}, u32[]{:S(2)}) collective-permute-start(bf16[512,1024]{1,0:T(8,128)(2,1)S(1)} %add_convert_fusion.5), channel_id=1, source_target_pairs={{0,2},{1,3},{2,0},{3,1},{4,6},{5,7},{6,4},{7,5},{8,10},{9,11},{10,... | collective-permute-start | bytes 3145736 | tf_op jit(solution)/shard_map/ppermute | solution.py:726
  288.7 29.3 %collective-permute-start.48 = (bf16[128,3072]{1,0:T(8,128)(2,1)S(1)}, bf16[128,3072]{1,0:T(8,128)(2,1)S(1)}, u32[]{:S(2)}, u32[]{:S(2)}) collective-permute-start(bf16[128,3072]{1,0:T(8,128)(2,1)S(1)} %add_convert_fusion.24), channel_id=1, source_target_pairs={{0,8},{8,16},{16,24},{24,28},{28,20},{20,12},{12,4},{4,0},{1,9},{9... | collective-permute-start | bytes 2359304 | tf_op jit(solution)/shard_map/ppermute | solution.py:702
  289.9 28.2 %collective-permute-start.49 = (bf16[128,3072]{1,0:T(8,128)(2,1)S(1)}, bf16[128,3072]{1,0:T(8,128)(2,1)S(1)}, u32[]{:S(2)}, u32[]{:S(2)}) collective-permute-start(bf16[128,3072]{1,0:T(8,128)(2,1)S(1)} %add_convert_fusion.23), channel_id=1, source_target_pairs={{8,0},{16,8},{24,16},{28,24},{20,28},{12,20},{4,12},{0,4},{9,1},{1... | collective-permute-start | bytes 2359304 | tf_op jit(solution)/shard_map/ppermute | solution.py:703
  290.8 27.2 %collective-permute-start.50 = (bf16[64,3072]{1,0:T(8,128)(2,1)S(1)}, bf16[64,3072]{1,0:T(8,128)(2,1)S(1)}, u32[]{:S(2)}, u32[]{:S(2)}) collective-permute-start(bf16[64,3072]{1,0:T(8,128)(2,1)S(1)} %copy-done.78), channel_id=1, source_target_pairs={{8,0},{16,8},{24,16},{28,24},{20,28},{12,20},{4,12},{0,4},{9,1},{1... | collective-permute-start | bytes 1179656 | tf_op jit(solution)/shard_map/ppermute | solution.py:703
  292.2 25.9 %collective-permute-start.47 = (bf16[64,3072]{1,0:T(8,128)(2,1)S(1)}, bf16[64,3072]{1,0:T(8,128)(2,1)S(1)}, u32[]{:S(2)}, u32[]{:S(2)}) collective-permute-start(bf16[64,3072]{1,0:T(8,128)(2,1)S(1)} %copy-done.76), channel_id=1, source_target_pairs={{0,8},{8,16},{16,24},{24,28},{28,20},{20,12},{12,4},{4,0},{1,9},{9... | collective-permute-start | bytes 1179656 | tf_op jit(solution)/shard_map/ppermute | solution.py:702
  322.3 25.2 %collective-permute-start.56 = (bf16[512,1024]{1,0:T(8,128)(2,1)S(1)}, bf16[512,1024]{1,0:T(8,128)(2,1)S(1)}, u32[]{:S(2)}, u32[]{:S(2)}) collective-permute-start(bf16[512,1024]{1,0:T(8,128)(2,1)S(1)} %add_convert_fusion.4), channel_id=1, source_target_pairs={{0,2},{1,3},{2,0},{3,1},{4,6},{5,7},{6,4},{7,5},{8,10},{9,11},{10,... | collective-permute-start | bytes 3145736 | tf_op jit(solution)/shard_map/ppermute | solution.py:726
  323.5 19.9 %collective-permute-start.54 = (bf16[128,3072]{1,0:T(8,128)(2,1)S(1)}, bf16[128,3072]{1,0:T(8,128)(2,1)S(1)}, u32[]{:S(2)}, u32[]{:S(2)}) collective-permute-start(bf16[128,3072]{1,0:T(8,128)(2,1)S(1)} %get-tuple-element.282), channel_id=1, source_target_pairs={{0,8},{8,16},{16,24},{24,28},{28,20},{20,12},{12,4},{4,0},{1,9},{9... | collective-permute-start | bytes 2359304 | tf_op jit(solution)/shard_map/ppermute | solution.py:702
  324.7 19.3 %collective-permute-start.55 = (bf16[128,3072]{1,0:T(8,128)(2,1)S(1)}, bf16[128,3072]{1,0:T(8,128)(2,1)S(1)}, u32[]{:S(2)}, u32[]{:S(2)}) collective-permute-start(bf16[128,3072]{1,0:T(8,128)(2,1)S(1)} %get-tuple-element.284), channel_id=1, source_target_pairs={{8,0},{16,8},{24,16},{28,24},{20,28},{12,20},{4,12},{0,4},{9,1},{1... | collective-permute-start | bytes 2359304 | tf_op jit(solution)/shard_map/ppermute | solution.py:703
  351.7 20.9 %collective-permute-start.59 = (bf16[128,3072]{1,0:T(8,128)(2,1)}, bf16[128,3072]{1,0:T(8,128)(2,1)S(1)}, u32[]{:S(2)}, u32[]{:S(2)}) collective-permute-start(bf16[128,3072]{1,0:T(8,128)(2,1)} %get-tuple-element.288), channel_id=1, source_target_pairs={{0,8},{8,16},{16,24},{24,28},{28,20},{20,12},{12,4},{4,0},{1,9},{9... | collective-permute-start | bytes 2359304 | tf_op jit(solution)/shard_map/ppermute | solution.py:702
  353.4 25.0 %collective-permute-start.61 = (bf16[512,1024]{1,0:T(8,128)(2,1)S(1)}, bf16[512,1024]{1,0:T(8,128)(2,1)S(1)}, u32[]{:S(2)}, u32[]{:S(2)}) collective-permute-start(bf16[512,1024]{1,0:T(8,128)(2,1)S(1)} %add_convert_fusion.2), channel_id=1, source_target_pairs={{0,2},{1,3},{2,0},{3,1},{4,6},{5,7},{6,4},{7,5},{8,10},{9,11},{10,... | collective-permute-start | bytes 3145736 | tf_op jit(solution)/shard_map/ppermute | solution.py:726
  354.1 19.1 %collective-permute-start.60 = (bf16[128,3072]{1,0:T(8,128)(2,1)S(1)}, bf16[128,3072]{1,0:T(8,128)(2,1)S(1)}, u32[]{:S(2)}, u32[]{:S(2)}) collective-permute-start(bf16[128,3072]{1,0:T(8,128)(2,1)S(1)} %get-tuple-element.290), channel_id=1, source_target_pairs={{8,0},{16,8},{24,16},{28,24},{20,28},{12,20},{4,12},{0,4},{9,1},{1... | collective-permute-start | bytes 2359304 | tf_op jit(solution)/shard_map/ppermute | solution.py:703
  378.4 25.3 %collective-permute-start.64 = (bf16[128,3072]{1,0:T(8,128)(2,1)S(1)}, bf16[128,3072]{1,0:T(8,128)(2,1)S(1)}, u32[]{:S(2)}, u32[]{:S(2)}) collective-permute-start(bf16[128,3072]{1,0:T(8,128)(2,1)S(1)} %add_convert_fusion.19), channel_id=1, source_target_pairs={{0,8},{8,16},{16,24},{24,28},{28,20},{20,12},{12,4},{4,0},{1,9},{9... | collective-permute-start | bytes 2359304 | tf_op jit(solution)/shard_map/ppermute | solution.py:702
  379.9 23.7 %collective-permute-start.62 = (bf16[128,1024]{1,0:T(8,128)(2,1)}, bf16[128,1024]{1,0:T(8,128)(2,1)S(1)}, u32[]{:S(2)}, u32[]{:S(2)}) collective-permute-start(bf16[128,1024]{1,0:T(8,128)(2,1)} %get-tuple-element.302), channel_id=1, source_target_pairs={{0,8},{8,16},{16,24},{24,28},{28,20},{20,12},{12,4},{4,0},{1,9},{9... | collective-permute-start | bytes 786440 | tf_op jit(solution)/shard_map/ppermute | solution.py:702
  381.4 22.6 %collective-permute-start.63 = (bf16[128,1024]{1,0:T(8,128)(2,1)}, bf16[128,1024]{1,0:T(8,128)(2,1)S(1)}, u32[]{:S(2)}, u32[]{:S(2)}) collective-permute-start(bf16[128,1024]{1,0:T(8,128)(2,1)} %get-tuple-element.304), channel_id=1, source_target_pairs={{8,0},{16,8},{24,16},{28,24},{20,28},{12,20},{4,12},{0,4},{9,1},{1... | collective-permute-start | bytes 786440 | tf_op jit(solution)/shard_map/ppermute | solution.py:703
  382.0 23.1 %collective-permute-start.65 = (bf16[128,3072]{1,0:T(8,128)(2,1)S(1)}, bf16[128,3072]{1,0:T(8,128)(2,1)S(1)}, u32[]{:S(2)}, u32[]{:S(2)}) collective-permute-start(bf16[128,3072]{1,0:T(8,128)(2,1)S(1)} %add_convert_fusion.18), channel_id=1, source_target_pairs={{8,0},{16,8},{24,16},{28,24},{20,28},{12,20},{4,12},{0,4},{9,1},{1... | collective-permute-start | bytes 2359304 | tf_op jit(solution)/shard_map/ppermute | solution.py:703
  382.7 20.8 %collective-permute-start.67 = (f32[4,1024]{1,0:T(4,128)S(1)}, f32[4,1024]{1,0:T(4,128)S(1)}, u32[]{:S(2)}, u32[]{:S(2)}) collective-permute-start(f32[4,1024]{1,0:T(4,128)S(1)} %pad_maximum_fusion), channel_id=1, source_target_pairs={{0,4},{4,0},{8,12},{12,8},{16,20},{20,16},{24,28},{28,24},{1,5},{5... | collective-permute-start | bytes 49160 | tf_op jit(solution)/shard_map/ppermute | solution.py:890
  406.2 34.1 %collective-permute-start.69 = (bf16[256,1024]{1,0:T(8,128)(2,1)S(1)}, bf16[256,1024]{1,0:T(8,128)(2,1)S(1)}, u32[]{:S(2)}, u32[]{:S(2)}) collective-permute-start(bf16[256,1024]{1,0:T(8,128)(2,1)S(1)} %add_convert_fusion.33), channel_id=1, source_target_pairs={{0,8},{8,16},{16,24},{24,28},{28,20},{20,12},{12,4},{4,0},{1,9},{9... | collective-permute-start | bytes 1572872 | tf_op jit(solution)/shard_map/ppermute | solution.py:702
  406.4 34.1 %collective-permute-start.71 = (bf16[128,3072]{1,0:T(8,128)(2,1)S(1)}, bf16[128,3072]{1,0:T(8,128)(2,1)S(1)}, u32[]{:S(2)}, u32[]{:S(2)}) collective-permute-start(bf16[128,3072]{1,0:T(8,128)(2,1)S(1)} %add_convert_fusion.17), channel_id=1, source_target_pairs={{0,8},{8,16},{16,24},{24,28},{28,20},{20,12},{12,4},{4,0},{1,9},{9... | collective-permute-start | bytes 2359304 | tf_op jit(solution)/shard_map/ppermute | solution.py:702
  407.3 33.3 %collective-permute-start.72 = (bf16[128,3072]{1,0:T(8,128)(2,1)S(1)}, bf16[128,3072]{1,0:T(8,128)(2,1)S(1)}, u32[]{:S(2)}, u32[]{:S(2)}) collective-permute-start(bf16[128,3072]{1,0:T(8,128)(2,1)S(1)} %add_convert_fusion.16), channel_id=1, source_target_pairs={{8,0},{16,8},{24,16},{28,24},{20,28},{12,20},{4,12},{0,4},{9,1},{1... | collective-permute-start | bytes 2359304 | tf_op jit(solution)/shard_map/ppermute | solution.py:703
  409.4 31.1 %collective-permute-start.70 = (bf16[256,1024]{1,0:T(8,128)(2,1)S(1)}, bf16[256,1024]{1,0:T(8,128)(2,1)S(1)}, u32[]{:S(2)}, u32[]{:S(2)}) collective-permute-start(bf16[256,1024]{1,0:T(8,128)(2,1)S(1)} %add_convert_fusion.32), channel_id=1, source_target_pairs={{8,0},{16,8},{24,16},{28,24},{20,28},{12,20},{4,12},{0,4},{9,1},{1... | collective-permute-start | bytes 1572872 | tf_op jit(solution)/shard_map/ppermute | solution.py:703
  411.5 28.8 %collective-permute-start.68 = (f32[4,1024]{1,0:T(4,128)S(1)}, f32[4,1024]{1,0:T(4,128)S(1)}, u32[]{:S(2)}, u32[]{:S(2)}) collective-permute-start(f32[4,1024]{1,0:T(4,128)S(1)} %fusion.1), channel_id=1, source_target_pairs={{0,8},{4,12},{8,0},{12,4},{16,24},{20,28},{24,16},{28,20},{1,9},{5... | collective-permute-start | bytes 49160 | tf_op jit(solution)/shard_map/ppermute | solution.py:890
  440.6 15.1 %collective-permute-start.74 = (bf16[256,1024]{1,0:T(8,128)(2,1)S(1)}, bf16[256,1024]{1,0:T(8,128)(2,1)S(1)}, u32[]{:S(2)}, u32[]{:S(2)}) collective-permute-start(bf16[256,1024]{1,0:T(8,128)(2,1)S(1)} %add_convert_fusion.31), channel_id=1, source_target_pairs={{0,8},{8,16},{16,24},{24,28},{28,20},{20,12},{12,4},{4,0},{1,9},{9... | collective-permute-start | bytes 1572872 | tf_op jit(solution)/shard_map/ppermute | solution.py:702
  442.0 13.9 %collective-permute-start.75 = (bf16[256,1024]{1,0:T(8,128)(2,1)S(1)}, bf16[256,1024]{1,0:T(8,128)(2,1)S(1)}, u32[]{:S(2)}, u32[]{:S(2)}) collective-permute-start(bf16[256,1024]{1,0:T(8,128)(2,1)S(1)} %add_convert_fusion.30), channel_id=1, source_target_pairs={{8,0},{16,8},{24,16},{28,24},{20,28},{12,20},{4,12},{0,4},{9,1},{1... | collective-permute-start | bytes 1572872 | tf_op jit(solution)/shard_map/ppermute | solution.py:703
  442.9 12.7 %collective-permute-start.73 = (f32[4,1024]{1,0:T(4,128)S(1)}, f32[4,1024]{1,0:T(4,128)S(1)}, u32[]{:S(2)}, u32[]{:S(2)}) collective-permute-start(f32[4,1024]{1,0:T(4,128)S(1)} %add.196), channel_id=1, source_target_pairs={{0,16},{4,20},{8,24},{12,28},{16,0},{20,4},{24,8},{28,12},{1,17},{... | collective-permute-start | bytes 49160 | tf_op jit(solution)/shard_map/ppermute | solution.py:890
  455.9 11.2 %collective-permute-start.78 = (bf16[256,1024]{1,0:T(8,128)(2,1)S(1)}, bf16[256,1024]{1,0:T(8,128)(2,1)S(1)}, u32[]{:S(2)}, u32[]{:S(2)}) collective-permute-start(bf16[256,1024]{1,0:T(8,128)(2,1)S(1)} %add_convert_fusion.29), channel_id=1, source_target_pairs={{0,8},{8,16},{16,24},{24,28},{28,20},{20,12},{12,4},{4,0},{1,9},{9... | collective-permute-start | bytes 1572872 | tf_op jit(solution)/shard_map/ppermute | solution.py:702
  456.2 11.2 %collective-permute-start.79 = (bf16[256,1024]{1,0:T(8,128)(2,1)S(1)}, bf16[256,1024]{1,0:T(8,128)(2,1)S(1)}, u32[]{:S(2)}, u32[]{:S(2)}) collective-permute-start(bf16[256,1024]{1,0:T(8,128)(2,1)S(1)} %add_convert_fusion.28), channel_id=1, source_target_pairs={{8,0},{16,8},{24,16},{28,24},{20,28},{12,20},{4,12},{0,4},{9,1},{1... | collective-permute-start | bytes 1572872 | tf_op jit(solution)/shard_map/ppermute | solution.py:703
  (97 other events, 923.2 us)

commit v5 on v4

--- a/solution.py
+++ b/solution.py
@@ -710,7 +710,7 @@
 class HeadSum:
     def __init__(self, rounds, pair):
         size = lax.axis_size("mp")
-        self.rounds, self.pair = rounds, pair
+        self.rounds, self.pair, self.got = rounds, pair, []
         self.near_moves = [(i, i ^ 1) for i in range(size)]
         self.far_moves = [(i, i ^ 2) for i in range(size)]
 
@@ -722,12 +722,15 @@
         self.mine = self.add(self.pair[0], got)
         return self.mine
 
-    def far(self):
-        self.got = lax.ppermute(self.rounds.now(self.mine), "mp", self.far_moves)
-        return self.got
+    def far(self, parts=1):
+        rows = self.mine.shape[0] // parts
+        start = len(self.got) * rows
+        self.got.append(lax.ppermute(self.rounds.now(self.mine[start : start + rows]), "mp", self.far_moves))
+        return self.got[-1]
 
     def last(self):
-        self.mine = self.add(self.mine, self.rounds.now(self.got))
+        got = [self.rounds.now(got) for got in self.got]
+        self.mine = self.add(self.mine, jnp.concatenate(got, 0))
         self.sum = (self.mine, lax.ppermute(self.mine, "mp", self.near_moves))
         return self.sum[1]
 
@@ -779,8 +782,11 @@
         lambda: g.append(split_sets(now(cotangent) * masks, sets)[1]),
     ]
     attn = Gather(rounds, ring, attn_own)
-    for _ in range(max(far, 3)):
+    for k in range(max(far, 3)):
         moved = attn.step() if rings else ()
+        if rings and k == far - 1:
+            rows = [Gather(rounds, ring, shard) for shard in ffn_own]
+            moved += rows[0].step()
         for chore in chores[:2]:
             chore()
         del chores[:2]
@@ -792,7 +798,6 @@
     gains = small.transpose(1, 0, 2).reshape(2 * sets, width)
     g_attn, g_ffn = [[gains[k * sets + c][None] for c in range(sets)] for k in range(2)]
     if rings:
-        rows = [Gather(rounds, ring, shard) for shard in ffn_own]
         w_attn = [attn.entries(c, sets) for c in range(sets)]
     else:
         both = gather(attn_own).reshape(n, sets, own, -1)
@@ -818,7 +823,6 @@
     heads[1] = HeadSum(rounds, part)
     close(*moved, part[0], got)
     close(*move(0), heads[1].near(), heads[0].last())
-    close(*move(0), *move(1), heads[1].far())
 
     def grads_of(c, out):
         columns = [(out[0], out[2]), (out[0], out[3]), (g[c], out[1])]
@@ -826,77 +830,69 @@
 
     dh, mlp, grads, dm, d_gain_ffn = ([None] * 2 for _ in range(5))
     moved = move(1)
+    got = heads[1].far()
     out = hidden_units(now(places), x[0], heads[0].sum, g[0], g_ffn[0], weights(0))
     dh[0], mlp[0] = HeadSum(rounds, out[4]), HeadSum(rounds, out[5])
-    close(*moved, out[0], heads[1].last())
+    close(*moved, out[0], got)
+    moved = move(1)
+    grads[0] = grads_of(0, out)
+    close(*moved, grads[0][0], dh[0].near(), mlp[0].near(), heads[1].last())
     att = [head.sum for head in heads]
-    close(dh[0].near())
-    moved = move(1)
-    got = dh[0].far()
-    grads[0] = grads_of(0, out)
-    close(*moved, grads[0][0], got, mlp[0].near())
-    close(*move(1), dh[0].last())
-
     sums = [Scatter(rounds, ring, grads[0])] if rings else []
     add = lambda k: sums[k].step() if rings else ()
+    close(*move(1), mlp[0].far(2))
+    close(*move(1), *add(0), mlp[0].far(2))
+
     moved = add(0)
-    got = mlp[0].far()
+    got = dh[0].far()
     out = hidden_units(now(places), x[1], att[1], g[1], g_ffn[1], weights(1))
     dh[1], mlp[1] = HeadSum(rounds, out[4]), HeadSum(rounds, out[5])
     close(*moved, out[0], got)
-    close(dh[1].near(), mlp[0].last())
+    close(dh[1].near(), dh[0].last(), mlp[0].last())
     moved = add(0)
     got = dh[1].far()
     grads[1] = grads_of(1, out)
-    order = now(places)
-    dm[0], d_gain_ffn[0] = middle_back(order, x[0], att[0], g[0], dh[0].sum, g_ffn[0])
+    dm[0], d_gain_ffn[0] = middle_back(now(places), x[0], att[0], g[0], dh[0].sum, g_ffn[0])
     close(*moved, grads[1][0], dm[0], got)
-    close(dh[1].last(), mlp[1].near())
     if rings:
         sums.append(Scatter(rounds, ring, grads[1]))
 
     moved = (*add(0), *add(1))
-    got = mlp[1].far()
+    dh[1].last()
     dm[1], d_gain_ffn[1] = middle_back(now(places), x[1], att[1], g[1], dh[1].sum, g_ffn[1])
     d_qkv, part, d_gain0 = attend_back(now(places), x, dm, qkv, w_attn, 0, None, each)
     back = [HeadSum(rounds, part)]
-    close(*moved, part[0], got)
-    close(back[0].near(), mlp[1].last())
-    moved = add(0)
+    close(*moved, part[0])
+    close(back[0].near(), mlp[1].near())
+    moved = add(1)
     got = back[0].far()
     d_qkv, part, d_gain1 = attend_back(now(places), x, dm, qkv, w_attn, 1, d_qkv, each)
     back.append(HeadSum(rounds, part))
     close(*moved, part[0], got)
-    close(back[1].near(), back[0].last())
+
+    shared = lax.axis_size("mp")
+    d_gains = jnp.concatenate([d_gain0 + d_gain1, *[d / shared for d in d_gain_ffn]], 0)
+    steps = list(exchange_steps(("mp", "dp")))
+
+    def sum_step(value):
+        axis, moves, _ = steps.pop(0)
+        return value + lax.ppermute(now(value), axis, moves)
+
+    d_gains = sum_step(d_gains)
+    close(back[1].near(), back[0].last(), d_gains)
     gain = gains[:sets]
     moved = add(1)
     got = back[1].far()
+    d_gains = sum_step(d_gains)
     runs = [[(h1[c], d_qkv[c]), (dm[c], mixed[c])] for c in range(sets)]
     if rings:
         blocks = weight_grads(now(places), runs, far)
+        sums.append(Scatter(rounds, ring, blocks))
     else:
         blocks = [weight_grads(now(places), [run], far)[0] for run in runs]
     grad_input = input_back(now(places), x, dm, back[0].sum, gain, 0, None, shape)
-    close(*moved, blocks[0], grad_input, got)
-    if rings:
-        sums.append(Scatter(rounds, ring, blocks))
-
-    shared = lax.axis_size("mp")
-    d_gains = jnp.concatenate([d_gain0 + d_gain1, *[d / shared for d in d_gain_ffn]], 0)
-    steps = list(exchange_steps(("dp", "mp")))
-
-    def sum_step(value):
-        axis, moves, _ = steps.pop(0)
-        return value + lax.ppermute(now(value), axis, moves)
-
-    moved = (*add(2), *add(1))
-    d_gains = sum_step(d_gains)
-    output = output_of(now(places), x, att, [m.sum for m in mlp], shape)
-    close(*moved, back[1].last(), d_gains, output)
-    moved = (*add(2), *add(1))
-    d_gains = sum_step(d_gains)
-    grad_input = input_back(now(places), x, dm, back[1].sum, gain, 1, grad_input, shape)
-    close(*moved, grad_input, d_gains)
+    close(*moved, blocks[0], grad_input, got, d_gains)
+    close(*add(2), *add(1), mlp[1].far())
     moved = add(2)
     d_gains = sum_step(d_gains)
     if rings:
@@ -904,12 +900,18 @@
     else:
         ffn_sums = [([scatter(b[0])], 0) for b in grads]
     d_gate_w, d_up_w, d_down_w = finish(ffn_sums, 3, own)
-    close(*moved, d_gate_w, d_gains)
+    close(*moved, d_gains, d_gate_w, back[1].last(), mlp[1].last())
     moved = add(2)
+    d_gains = sum_step(d_gains)
+    output = output_of(now(places), x, att, [m.sum for m in mlp], shape)
+    close(*moved, output, d_gains)
+    moved = add(2)
+    grad_input = input_back(now(places), x, dm, back[1].sum, gain, 1, grad_input, shape)
     while steps:
         d_gains = sum_step(d_gains)
+    close(*moved, grad_input, d_gains)
     if rings:
-        terms = sums[2].terms()
+        terms = [now(t) for t in sums[2].terms()]
         attn_sums = [(terms, c * own) for c in range(sets)]
     else:
         attn_sums = [([scatter(b)], 0) for b in blocks]

time: 479 us -> 458 us (0.956)
  waiting for transfers between devices: 168 us -> 137 us
    ppermute x5, waiting for transfers between devices: 44.4 us -> 17.4 us  [sum_step(): return value + lax.ppermute(now(value), axis, moves)]
    ppermute x12, waiting for transfers between devices: 69.3 us -> 45.6 us  [step(): self.a.append(lax.ppermute(self.rounds.now(a), 'dp', self.ring.ahead))]
    ppermute x12, waiting for transfers between devices: 3.39 us -> 20.7 us  [step(): self.a = lax.ppermute(self.rounds.now(self.a), 'dp', self.ring.ahead)]
    ppermute x12, waiting for transfers between devices: 2.47 us -> 8.98 us  [step(): self.b = lax.ppermute(self.rounds.now(self.b), 'dp', self.ring.behind)]
    ppermute x8, waiting for transfers between devices: 11.4 us -> 5.96 us  [near(): got = lax.ppermute(self.rounds.now(self.pair[1]), 'mp', self.near_moves)]
    ppermute x8 -> x9, waiting for transfers between devices: 17.1 us -> 20.2 us  [far(): lax.ppermute(self.rounds.now(self.mine[start:start + rows]), 'mp', self.f...]
    ppermute x8 -> x9, starting transfers between devices: 8.38 us -> 10.9 us  [far(): lax.ppermute(self.rounds.now(self.mine[start:start + rows]), 'mp', self.f...]
  transfers between devices with their start and end apart: 80 -> 81, of which waited for: 43 -> 34; matrix products, arithmetic and copies ran while one was open for 5% -> 6% of each run, Pallas kernels for 42% -> 44%
where the time goes in v5:
time: 458 us; the launch traced here: 450 us
  Pallas kernels  200 us (44%)
  waiting for transfers between devices  137 us (30%)
  starting transfers between devices  77.7 us (17%)
  other arithmetic  17.4 us (4%)
  local copies, waits for them, and re-layouts  15 us (3%)
    pallas_call x19, Pallas kernels, kernel_call(): pl.pallas_call(body, grid_spec=spec, out_shape=outs, input_output_aliases...  200 us
    ppermute x12, waiting for transfers between devices, step(): self.a.append(lax.ppermute(self.rounds.now(a), 'dp', self.ring.ahead))  45.6 us
    ppermute x12, waiting for transfers between devices, step(): self.a = lax.ppermute(self.rounds.now(self.a), 'dp', self.ring.ahead)  20.7 us
    ppermute x9, waiting for transfers between devices, far(): lax.ppermute(self.rounds.now(self.mine[start:start + rows]), 'mp', self.f...  20.2 us
    ppermute x5, waiting for transfers between devices, sum_step(): return value + lax.ppermute(now(value), axis, moves)  17.4 us
    ppermute x12, starting transfers between devices, step(): self.b.append(lax.ppermute(self.rounds.now(b), 'dp', self.ring.behind))  15.8 us
    ppermute x12, starting transfers between devices, step(): self.b = lax.ppermute(self.rounds.now(self.b), 'dp', self.ring.behind)  14.7 us
    ppermute x12, starting transfers between devices, step(): self.a = lax.ppermute(self.rounds.now(self.a), 'dp', self.ring.ahead)  11.1 us
  transfers between devices with their start and end apart: 81, of which 34 were waited for; matrix products, arithmetic and copies ran while one was open for 6% of the time, Pallas kernels for 44%

profile of v5, /device:TPU:0, one launch (start us, length us, event | category | flops | bytes accessed | tf_op | source)
XLA Modules:
  0.0 450.3 jit_solution(10984849257338631757)
XLA Ops:
  0.6 2.0 shard_map.203.refs_2_.refs_3_.refs_0_
  2.6 3.0 collective-permute-start.1
  6.3 2.0 collective-permute-start
  8.3 3.1 slice_bitcast_fusion.3.refs_0_.x_ref.x0
  11.4 2.2 shard_map.204.refs_5_
  13.6 4.2 collective-permute-done
  22.9 3.3 slice_bitcast_fusion.2.refs_0_.x_ref.x1
  26.2 2.1 shard_map.205.refs_5_
  28.3 4.9 %collective-permute-done.3 = f32[2,4,128]{2,1,0:T(4,128)S(1)} collective-permute-done((f32[2,4,128]{2,1,0:T(4,128)S(1)}, f32[2,4,128]{2,1,0:T(4,128)S(1)}, u32[]{:S(2)}, u32[]{:S(2)}) %collective-permute-start.3) | collective-permute-done | bytes 4128 | tf_op jit(solution)/shard_map/ppermute | solution.py:770
  33.2 2.8 collective-permute-start.6
  36.3 1.7 collective-permute-start.8
  38.4 2.5 slice_bitcast_fusion
  40.9 6.5 %collective-permute-done.7.refs_7_.refs_8_.refs_5_ = bf16[256,1024]{1,0:T(8,128)(2,1)S(1)} collective-permute-done((bf16[256,1024]{1,0:T(8,128)(2,1)S(1)}, bf16[256,1024]{1,0:T(8,128)(2,1)S(1)}, u32[]{:S(2)}, u32[]{:S(2)}) %collective-permute-start.7) | collective-permute-done | bytes 524320 | tf_op jit(solution)/shard_map/ppermute | solution.py:664
  48.4 1.7 collective-permute-start.12
  50.5 1.7 collective-permute-start.11
  52.3 18.1 %collective-permute-done.10.refs_6_.refs_4_ = bf16[128,1024]{1,0:T(8,128)(2,1)S(1)} collective-permute-done((bf16[128,1024]{1,0:T(8,128)(2,1)S(1)}, bf16[128,1024]{1,0:T(8,128)(2,1)S(1)}, u32[]{:S(2)}, u32[]{:S(2)}) %collective-permute-start.10) | collective-permute-done | bytes 262176 | tf_op jit(solution)/shard_map/ppermute | solution.py:664
  71.4 1.7 collective-permute-start.14
  74.4 14.0 %shard_map.206 = (bf16[1024,1024]{1,0:T(8,128)(2,1)}, bf16[1024,768]{1,0:T(8,128)(2,1)}, bf16[1024,256]{1,0:T(8,128)(2,1)}, bf16[512,1024]{1,0:T(8,128)(2,1)}, bf16[512,1024]{1,0:T(8,128)(2,1)}) custom-call(s32[9]{0:T(128)} %pad_add_fusion.places._, bf16[1024,1024]{1,0:T(8,128)(2,1)} %slice_bitcast_fusion.3.refs_0_.x_ref.x0, ...), custom_call_target="tpu_custom_call" | custom-call | flops 1 | bytes 1 | tf_op jit(solution)/shard_map/pallas_call | solution.py:41
  88.5 2.9 collective-permute-done.15
  91.4 1.6 add_convert_fusion.15
  94.8 1.7 collective-permute-start.17
  96.6 13.0 %shard_map.207 = (bf16[1024,1024]{1,0:T(8,128)(2,1)}, bf16[1024,768]{1,0:T(8,128)(2,1)}, bf16[1024,256]{1,0:T(8,128)(2,1)}, bf16[512,1024]{1,0:T(8,128)(2,1)}, bf16[512,1024]{1,0:T(8,128)(2,1)}) custom-call(s32[9]{0:T(128)} %pad_add_fusion.places._, bf16[1024,1024]{1,0:T(8,128)(2,1)} %slice_bitcast_fusion.2.refs_0_.x_ref.x1, ...), custom_call_target="tpu_custom_call" | custom-call | flops 1 | bytes 1 | tf_op jit(solution)/shard_map/pallas_call | solution.py:41
  109.6 4.3 collective-permute-done.16.refs_11_
  113.9 4.4 collective-permute-done.18
  119.7 1.7 collective-permute-start.20
  121.8 8.6 %collective-permute-done.19.refs_9_ = bf16[64,3072]{1,0:T(8,128)(2,1)S(1)} collective-permute-done((bf16[64,3072]{1,0:T(8,128)(2,1)S(1)}, bf16[64,3072]{1,0:T(8,128)(2,1)S(1)}, u32[]{:S(2)}, u32[]{:S(2)}) %collective-permute-start.19) | collective-permute-done | bytes 393248 | tf_op jit(solution)/shard_map/ppermute | solution.py:664
  134.6 25.2 %shard_map.208 = (bf16[1024,1024]{1,0:T(8,128)(2,1)}, bf16[1024,1024]{1,0:T(8,128)(2,1)}, bf16[1024,1024]{1,0:T(8,128)(2,1)}, bf16[1024,1024]{1,0:T(8,128)(2,1)}...) custom-call(s32[9]{0:T(128)} %pad_add_fusion.places._, ...), custom_call_target="tpu_custom_call" | custom-call | flops 1 | bytes 1 | tf_op jit(solution)/shard_map/pallas_call | solution.py:41
  163.0 13.7 %shard_map.209 = (bf16[128,3072]{1,0:T(8,128)(2,1)}, bf16[128,3072]{1,0:T(8,128)(2,1)}, bf16[128,3072]{1,0:T(8,128)(2,1)}, bf16[128,3072]{1,0:T(8,128)(2,1)}, bf...) custom-call(s32[9]{0:T(128)} %pad_add_fusion.places._, ...), custom_call_target="tpu_custom_call" | custom-call | flops 1 | bytes 1 | tf_op jit(solution)/shard_map/pallas_call | solution.py:41
  178.4 2.5 collective-permute-done.26.refs_12_
  184.7 12.1 %collective-permute-done.33 = bf16[256,1024]{1,0:T(8,128)(2,1)S(1)} collective-permute-done((bf16[256,1024]{1,0:T(8,128)(2,1)S(1)}, bf16[256,1024]{1,0:T(8,128)(2,1)S(1)}, u32[]{:S(2)}, u32[]{:S(2)}) %collective-permute-start.33) | collective-permute-done | bytes 524320 | tf_op jit(solution)/shard_map/ppermute | solution.py:728
  196.8 4.2 collective-permute-done.31.refs_11_
  206.1 7.3 %collective-permute-done.37 = bf16[64,3072]{1,0:T(8,128)(2,1)S(1)} collective-permute-done((bf16[64,3072]{1,0:T(8,128)(2,1)S(1)}, bf16[64,3072]{1,0:T(8,128)(2,1)S(1)}, u32[]{:S(2)}, u32[]{:S(2)}) %collective-permute-start.37) | collective-permute-done | bytes 393248 | tf_op jit(solution)/shard_map/ppermute | solution.py:703
  214.9 4.3 collective-permute-done.36.refs_10_
  223.0 25.2 %shard_map.210 = (bf16[1024,1024]{1,0:T(8,128)(2,1)}, bf16[1024,1024]{1,0:T(8,128)(2,1)}, bf16[1024,1024]{1,0:T(8,128)(2,1)}, bf16[1024,1024]{1,0:T(8,128)(2,1)}...) custom-call(s32[9]{0:T(128)} %pad_add_fusion.places._, ...), custom_call_target="tpu_custom_call" | custom-call | flops 1 | bytes 1 | tf_op jit(solution)/shard_map/pallas_call | solution.py:41
  249.4 1.7 add_convert_fusion.7.refs_2_
  257.5 13.6 %shard_map.211 = (bf16[128,3072]{1,0:T(8,128)(2,1)}, bf16[128,3072]{1,0:T(8,128)(2,1)}, bf16[128,3072]{1,0:T(8,128)(2,1)}, bf16[128,3072]{1,0:T(8,128)(2,1)}, bf...) custom-call(s32[9]{0:T(128)} %pad_add_fusion.places._, ...), custom_call_target="tpu_custom_call" | custom-call | flops 1 | bytes 1 | tf_op jit(solution)/shard_map/pallas_call | solution.py:41
  271.2 7.4 %shard_map.212 = (bf16[1024,1024]{1,0:T(8,128)(2,1)}, f32[1,1024]{1,0:T(1,128)}) custom-call(s32[9]{0:T(128)} %pad_add_fusion.places._, bf16[1024,1024]{1,0:T(8,128)(2,1)} %slice_bitcast_fusion.3.refs_0_.x_ref.x0, bf16[512,1024]{1,0:T(8,128)(2,1)} %copy-done, bf16[512,1024]{1,0:T(8,128)(2,1)} %copy-done.4, ...), custom_call_target="tpu_custom_call" | custom-call | flops 1 | bytes 1 | tf_op jit(solution)/shard_map/pallas_call | solution.py:41
  283.1 1.6 collective-permute-start.52
  285.8 7.4 %shard_map.213 = (bf16[1024,1024]{1,0:T(8,128)(2,1)}, f32[1,1024]{1,0:T(1,128)}) custom-call(s32[9]{0:T(128)} %pad_add_fusion.places._, bf16[1024,1024]{1,0:T(8,128)(2,1)} %slice_bitcast_fusion.2.refs_0_.x_ref.x1, bf16[512,1024]{1,0:T(8,128)(2,1)} %copy-done.1, bf16[512,1024]{1,0:T(8,128)(2,1)} %copy-done.5, ...), custom_call_target="tpu_custom_call" | custom-call | flops 1 | bytes 1 | tf_op jit(solution)/shard_map/pallas_call | solution.py:41
  293.2 17.8 %shard_map.214 = (bf16[1024,768]{1,0:T(8,128)(2,1)}, bf16[1024,768]{1,0:T(8,128)(2,1)}, bf16[512,1024]{1,0:T(8,128)(2,1)}, bf16[512,1024]{1,0:T(8,128)(2,1)}, f32[2,1024]{1,0:T(2,128)}) custom-call(s32[9]{0:T(128)} %pad_add_fusion.places._, bf16[1024,1024]{1,0:T(8,128)(2,1)} %slice_bitcast_fusion.3.refs_0_.x_ref.x0, ...), custom_call_target="tpu_custom_call" | custom-call | flops 1 | bytes 1 | tf_op jit(solution)/shard_map/pallas_call | solution.py:41
  311.7 2.9 collective-permute-done.53
  318.0 1.6 collective-permute-start.56
  319.7 17.6 %shard_map.215 = (bf16[1024,768]{1,0:T(8,128)(2,1)}, bf16[1024,768]{1,0:T(8,128)(2,1)}, bf16[512,1024]{1,0:T(8,128)(2,1)}, bf16[512,1024]{1,0:T(8,128)(2,1)}, f32[2,1024]{1,0:T(2,128)}) custom-call(s32[9]{0:T(128)} %pad_add_fusion.places._, bf16[1024,1024]{1,0:T(8,128)(2,1)} %slice_bitcast_fusion.3.refs_0_.x_ref.x0, ...), custom_call_target="tpu_custom_call", output_to_operand_aliasing={{0}: (16, {}), {1}: (17, {})} | custom-call | flops 1 | bytes 1 | tf_op jit(solution)/shard_map/pallas_call | solution.py:41
  338.1 2.8 collective-permute-done.57
  342.2 2.9 collective-permute-done.60
  351.4 11.3 %shard_map.216 = (bf16[256,1024]{1,0:T(8,128)(2,1)}, bf16[256,1024]{1,0:T(8,128)(2,1)}, bf16[256,1024]{1,0:T(8,128)(2,1)}, bf16[256,1024]{1,0:T(8,128)(2,1)}, bf...) custom-call(s32[9]{0:T(128)} %pad_add_fusion.places._, ...), custom_call_target="tpu_custom_call" | custom-call | flops 1 | bytes 1 | tf_op jit(solution)/shard_map/pallas_call | solution.py:41
  362.7 6.3 %shard_map.217.refs_0_ = bf16[128,16,1024]{2,1,0:T(8,128)(2,1)} custom-call(s32[9]{0:T(128)} %pad_add_fusion.places._, bf16[1024,1024]{1,0:T(8,128)(2,1)} %slice_bitcast_fusion.3.refs_0_.x_ref.x0, bf16[1024,1024]{1,0:T(8,128)(2,1)} %slice_bitcast_fusion.2.refs_0_.x_ref.x1, bf16[1024,1024]{1,0:T(8,128)(2,1)} %get-tuple-element.264.dm0.refs_2_.refs_3_, ...), custom_call_target="tpu_custom_call" | custom-call | flops 1 | bytes 1 | tf_op jit(solution)/shard_map/pallas_call | solution.py:41
  369.0 2.5 collective-permute-done.64
  373.0 1.6 collective-permute-start.69
  374.8 1.7 collective-permute-start.67
  376.8 1.7 collective-permute-start.65
  378.9 19.7 %collective-permute-done.65 = bf16[128,1024]{1,0:T(8,128)(2,1)S(1)} collective-permute-done((bf16[128,1024]{1,0:T(8,128)(2,1)S(1)}, bf16[128,1024]{1,0:T(8,128)(2,1)S(1)}, u32[]{:S(2)}, u32[]{:S(2)}) %collective-permute-start.65) | collective-permute-done | bytes 262176 | tf_op jit(solution)/shard_map/ppermute | solution.py:702
  402.8 1.7 collective-permute-start.71
  404.9 4.5 %shard_map.218 = (f32[2,128,1024]{2,1,0:T(8,128)}, f32[2,128,1024]{2,1,0:T(8,128)}, f32[2,1024,128]{2,1,0:T(8,128)}) custom-call(bf16[128,3072]{1,0:T(8,128)(2,1)} %get-tuple-element.329.refs_0_, bf16[128,3072]{1,0:T(8,128)(2,1)} %copy-done.38, bf16[128,3072]{1,0:T(8,128)(2,1)} %copy-done.39, bf16[128,3072]{1,0:T(8,128)(2,1)} %get-tuple-element.332.refs_3_, ...), custom_call_target="tpu_custom_call" | custom-call | flops 1 | bytes 1 | tf_op jit(solution)/shard_map/pallas_call | solution.py:41
  409.4 6.6 %collective-permute-done.72 = f32[4,1024]{1,0:T(4,128)S(1)} collective-permute-done((f32[4,1024]{1,0:T(4,128)S(1)}, f32[4,1024]{1,0:T(4,128)S(1)}, u32[]{:S(2)}, u32[]{:S(2)}) %collective-permute-start.72) | collective-permute-done | bytes 16416 | tf_op jit(solution)/shard_map/ppermute | solution.py:879
  416.5 1.8 collective-permute-start.75
  418.8 1.7 collective-permute-start.77
  420.5 8.5 %shard_map.219 = bf16[128,16,1024]{2,1,0:T(8,128)(2,1)} custom-call(s32[9]{0:T(128)} %pad_add_fusion.places._, bf16[1024,1024]{1,0:T(8,128)(2,1)} %slice_bitcast_fusion.3.refs_0_.x_ref.x0, bf16[1024,1024]{1,0:T(8,128)(2,1)} %slice_bitcast_fusion.2.refs_0_.x_ref.x1, bf16[512,1024]{1,0:T(8,128)(2,1)} %copy-done, bf16[512,1024]{1,0:T(8,128)(2,1)} %copy-done.4, ...), custom_call_target="tpu_custom_call" | custom-call | flops 1 | bytes 1 | tf_op jit(solution)/shard_map/pallas_call | solution.py:41
  429.1 1.9 collective-permute-done.77
  431.8 1.7 collective-permute-start.80
  433.6 2.0 collective-permute-start.78
  435.5 6.2 %shard_map.220 = bf16[128,16,1024]{2,1,0:T(8,128)(2,1)} custom-call(s32[9]{0:T(128)} %pad_add_fusion.places._, bf16[1024,1024]{1,0:T(8,128)(2,1)} %slice_bitcast_fusion.3.refs_0_.x_ref.x0, bf16[1024,1024]{1,0:T(8,128)(2,1)} %slice_bitcast_fusion.2.refs_0_.x_ref.x1, ...), custom_call_target="tpu_custom_call", output_to_operand_aliasing={{}: (8, {})} | custom-call | flops 1 | bytes 1 | tf_op jit(solution)/shard_map/pallas_call | solution.py:41
  441.7 3.5 collective-permute-done.78
  447.3 2.4 shard_map.221
  (345 shorter events, 72.9 us)
Async XLA Ops:
  2.6 15.2 %collective-permute-start.1 = (bf16[256,1024]{1,0:T(8,128)(2,1)}, bf16[256,1024]{1,0:T(8,128)(2,1)S(1)}, u32[]{:S(2)}, u32[]{:S(2)}) collective-permute-start(bf16[256,1024]{1,0:T(8,128)(2,1)} %shard_map.203.refs_2_.refs_3_.refs_0_), channel_id=1, source_target_pairs={{0,8},{8,16},{16,24},{24,28},{28,20},{20,12},{12,4},{4,0},{1,9},{9... | collective-permute-start | bytes 1572872 | tf_op jit(solution)/shard_map/ppermute | solution.py:664
  5.7 13.6 %collective-permute-start.2 = (bf16[256,1024]{1,0:T(8,128)(2,1)}, bf16[256,1024]{1,0:T(8,128)(2,1)S(1)}, u32[]{:S(2)}, u32[]{:S(2)}) collective-permute-start(bf16[256,1024]{1,0:T(8,128)(2,1)} %shard_map.203.refs_2_.refs_3_.refs_0_), channel_id=1, source_target_pairs={{8,0},{16,8},{24,16},{28,24},{20,28},{12,20},{4,12},{0,4},{9,1},{1... | collective-permute-start | bytes 1572872 | tf_op jit(solution)/shard_map/ppermute | solution.py:665
  19.3 13.9 %collective-permute-start.4 = (bf16[256,1024]{1,0:T(8,128)(2,1)S(1)}, bf16[256,1024]{1,0:T(8,128)(2,1)S(1)}, u32[]{:S(2)}, u32[]{:S(2)}) collective-permute-start(bf16[256,1024]{1,0:T(8,128)(2,1)S(1)} %collective-permute-done.1.refs_9_.refs_10_.refs_7_), channel_id=1, source_target_pairs={{0,8},{8,16},{16,24},{24,28},{28,20},{20,12},{12,4},{4,0},{1,9},{9... | collective-permute-start | bytes 1572872 | tf_op jit(solution)/shard_map/ppermute | solution.py:664
  20.8 12.3 %collective-permute-start.5 = (bf16[256,1024]{1,0:T(8,128)(2,1)S(1)}, bf16[256,1024]{1,0:T(8,128)(2,1)S(1)}, u32[]{:S(2)}, u32[]{:S(2)}) collective-permute-start(bf16[256,1024]{1,0:T(8,128)(2,1)S(1)} %collective-permute-done.2.refs_3_.refs_4_.refs_1_), channel_id=1, source_target_pairs={{8,0},{16,8},{24,16},{28,24},{20,28},{12,20},{4,12},{0,4},{9,1},{1... | collective-permute-start | bytes 1572872 | tf_op jit(solution)/shard_map/ppermute | solution.py:665
  21.3 11.8 %collective-permute-start.3 = (f32[2,4,128]{2,1,0:T(4,128)S(1)}, f32[2,4,128]{2,1,0:T(4,128)S(1)}, u32[]{:S(2)}, u32[]{:S(2)}) collective-permute-start(f32[2,4,128]{2,1,0:T(4,128)S(1)} %maximum_select_fusion.2), channel_id=1, source_target_pairs={{0,8},{4,12},{8,0},{12,4},{16,24},{20,28},{24,16},{28,20},{1,9},{5... | collective-permute-start | bytes 12296 | tf_op jit(solution)/shard_map/ppermute | solution.py:770
  36.3 11.7 %collective-permute-start.8 = (bf16[256,1024]{1,0:T(8,128)(2,1)S(1)}, bf16[256,1024]{1,0:T(8,128)(2,1)S(1)}, u32[]{:S(2)}, u32[]{:S(2)}) collective-permute-start(bf16[256,1024]{1,0:T(8,128)(2,1)S(1)} %collective-permute-done.5.refs_4_.refs_5_.refs_2_), channel_id=1, source_target_pairs={{8,0},{16,8},{24,16},{28,24},{20,28},{12,20},{4,12},{0,4},{9,1},{1... | collective-permute-start | bytes 1572872 | tf_op jit(solution)/shard_map/ppermute | solution.py:665
  48.1 23.0 %collective-permute-start.9 = (bf16[128,3072]{1,0:T(8,128)(2,1)S(1)}, bf16[128,3072]{1,0:T(8,128)(2,1)}, u32[]{:S(2)}, u32[]{:S(2)}) collective-permute-start(bf16[128,3072]{1,0:T(8,128)(2,1)S(1)} %copy-done.18), channel_id=1, source_target_pairs={{0,8},{8,16},{16,24},{24,28},{28,20},{20,12},{12,4},{4,0},{1,9},{9... | collective-permute-start | bytes 2359304 | tf_op jit(solution)/shard_map/ppermute | solution.py:664
  48.4 22.7 %collective-permute-start.12 = (bf16[128,3072]{1,0:T(8,128)(2,1)S(1)}, bf16[128,3072]{1,0:T(8,128)(2,1)}, u32[]{:S(2)}, u32[]{:S(2)}) collective-permute-start(bf16[128,3072]{1,0:T(8,128)(2,1)S(1)} %copy-done.18), channel_id=1, source_target_pairs={{8,0},{16,8},{24,16},{28,24},{20,28},{12,20},{4,12},{0,4},{9,1},{1... | collective-permute-start | bytes 2359304 | tf_op jit(solution)/shard_map/ppermute | solution.py:665
  50.1 20.3 %collective-permute-start.10 = (bf16[128,1024]{1,0:T(8,128)(2,1)S(1)}, bf16[128,1024]{1,0:T(8,128)(2,1)S(1)}, u32[]{:S(2)}, u32[]{:S(2)}) collective-permute-start(bf16[128,1024]{1,0:T(8,128)(2,1)S(1)} %slice.99), channel_id=1, source_target_pairs={{0,8},{8,16},{16,24},{24,28},{28,20},{20,12},{12,4},{4,0},{1,9},{9... | collective-permute-start | bytes 786440 | tf_op jit(solution)/shard_map/ppermute | solution.py:664
  50.5 20.5 %collective-permute-start.11 = (bf16[128,1024]{1,0:T(8,128)(2,1)S(1)}, bf16[128,1024]{1,0:T(8,128)(2,1)S(1)}, u32[]{:S(2)}, u32[]{:S(2)}) collective-permute-start(bf16[128,1024]{1,0:T(8,128)(2,1)S(1)} %slice.100), channel_id=1, source_target_pairs={{8,0},{16,8},{24,16},{28,24},{20,28},{12,20},{4,12},{0,4},{9,1},{1... | collective-permute-start | bytes 786440 | tf_op jit(solution)/shard_map/ppermute | solution.py:665
  71.1 17.3 %collective-permute-start.13 = (bf16[128,3072]{1,0:T(8,128)(2,1)}, bf16[128,3072]{1,0:T(8,128)(2,1)S(1)}, u32[]{:S(2)}, u32[]{:S(2)}) collective-permute-start(bf16[128,3072]{1,0:T(8,128)(2,1)} %collective-permute-done.9.refs_13_), channel_id=1, source_target_pairs={{0,8},{8,16},{16,24},{24,28},{28,20},{20,12},{12,4},{4,0},{1,9},{9... | collective-permute-start | bytes 2359304 | tf_op jit(solution)/shard_map/ppermute | solution.py:664
  71.4 17.0 %collective-permute-start.14 = (bf16[128,3072]{1,0:T(8,128)(2,1)}, bf16[128,3072]{1,0:T(8,128)(2,1)S(1)}, u32[]{:S(2)}, u32[]{:S(2)}) collective-permute-start(bf16[128,3072]{1,0:T(8,128)(2,1)} %collective-permute-done.12.refs_6_), channel_id=1, source_target_pairs={{8,0},{16,8},{24,16},{28,24},{20,28},{12,20},{4,12},{0,4},{9,1},{1... | collective-permute-start | bytes 2359304 | tf_op jit(solution)/shard_map/ppermute | solution.py:665
  93.0 25.3 %collective-permute-start.18 = (bf16[512,1024]{1,0:T(8,128)(2,1)S(1)}, bf16[512,1024]{1,0:T(8,128)(2,1)S(1)}, u32[]{:S(2)}, u32[]{:S(2)}) collective-permute-start(bf16[512,1024]{1,0:T(8,128)(2,1)S(1)} %add_convert_fusion.15), channel_id=1, source_target_pairs={{0,2},{1,3},{2,0},{3,1},{4,6},{5,7},{6,4},{7,5},{8,10},{9,11},{10,... | collective-permute-start | bytes 3145736 | tf_op jit(solution)/shard_map/ppermute | solution.py:728
  94.6 19.3 %collective-permute-start.16 = (bf16[128,3072]{1,0:T(8,128)(2,1)S(1)}, bf16[128,3072]{1,0:T(8,128)(2,1)S(1)}, u32[]{:S(2)}, u32[]{:S(2)}) collective-permute-start(bf16[128,3072]{1,0:T(8,128)(2,1)S(1)} %collective-permute-done.13.refs_12_), channel_id=1, source_target_pairs={{0,8},{8,16},{16,24},{24,28},{28,20},{20,12},{12,4},{4,0},{1,9},{9... | collective-permute-start | bytes 2359304 | tf_op jit(solution)/shard_map/ppermute | solution.py:664
  94.8 19.0 %collective-permute-start.17 = (bf16[128,3072]{1,0:T(8,128)(2,1)S(1)}, bf16[128,3072]{1,0:T(8,128)(2,1)S(1)}, u32[]{:S(2)}, u32[]{:S(2)}) collective-permute-start(bf16[128,3072]{1,0:T(8,128)(2,1)S(1)} %collective-permute-done.14.refs_7_), channel_id=1, source_target_pairs={{8,0},{16,8},{24,16},{28,24},{20,28},{12,20},{4,12},{0,4},{9,1},{1... | collective-permute-start | bytes 2359304 | tf_op jit(solution)/shard_map/ppermute | solution.py:665
  118.7 11.8 %collective-permute-start.22 = (bf16[512,1024]{1,0:T(8,128)(2,1)S(1)}, bf16[512,1024]{1,0:T(8,128)(2,1)S(1)}, u32[]{:S(2)}, u32[]{:S(2)}) collective-permute-start(bf16[512,1024]{1,0:T(8,128)(2,1)S(1)} %add_convert_fusion.13.refs_1_.att0.refs_0_), channel_id=1, source_target_pairs={{0,1},{1,0},{2,3},{3,2},{4,5},{5,4},{6,7},{7,6},{8,9},{9,8},{10,11... | collective-permute-start | bytes 3145736 | tf_op jit(solution)/shard_map/ppermute | solution.py:734
  130.5 29.3 %collective-permute-start.25 = (bf16[512,1024]{1,0:T(8,128)(2,1)S(1)}, bf16[512,1024]{1,0:T(8,128)(2,1)S(1)}, u32[]{:S(2)}, u32[]{:S(2)}) collective-permute-start(bf16[512,1024]{1,0:T(8,128)(2,1)S(1)} %add_convert_fusion.14), channel_id=1, source_target_pairs={{0,2},{1,3},{2,0},{3,1},{4,6},{5,7},{6,4},{7,5},{8,10},{9,11},{10,... | collective-permute-start | bytes 3145736 | tf_op jit(solution)/shard_map/ppermute | solution.py:728
  132.1 27.7 %collective-permute-start.23 = (bf16[128,3072]{1,0:T(8,128)(2,1)S(1)}, bf16[128,3072]{1,0:T(8,128)(2,1)S(1)}, u32[]{:S(2)}, u32[]{:S(2)}) collective-permute-start(bf16[128,3072]{1,0:T(8,128)(2,1)S(1)} %copy-done.17), channel_id=1, source_target_pairs={{0,8},{8,16},{16,24},{24,28},{28,20},{20,12},{12,4},{4,0},{1,9},{9... | collective-permute-start | bytes 2359304 | tf_op jit(solution)/shard_map/ppermute | solution.py:664
  133.3 26.5 %collective-permute-start.24 = (bf16[128,3072]{1,0:T(8,128)(2,1)S(1)}, bf16[128,3072]{1,0:T(8,128)(2,1)S(1)}, u32[]{:S(2)}, u32[]{:S(2)}) collective-permute-start(bf16[128,3072]{1,0:T(8,128)(2,1)S(1)} %copy-done.17), channel_id=1, source_target_pairs={{8,0},{16,8},{24,16},{28,24},{20,28},{12,20},{4,12},{0,4},{9,1},{1... | collective-permute-start | bytes 2359304 | tf_op jit(solution)/shard_map/ppermute | solution.py:665
  159.8 16.9 %collective-permute-start.28 = (bf16[512,1024]{1,0:T(8,128)(2,1)}, bf16[512,1024]{1,0:T(8,128)(2,1)S(1)}, u32[]{:S(2)}, u32[]{:S(2)}) collective-permute-start(bf16[512,1024]{1,0:T(8,128)(2,1)} %get-tuple-element.230), channel_id=1, source_target_pairs={{0,1},{1,0},{2,3},{3,2},{4,5},{5,4},{6,7},{7,6},{8,9},{9,8},{10,11... | collective-permute-start | bytes 3145736 | tf_op jit(solution)/shard_map/ppermute | solution.py:721
  159.9 17.3 %collective-permute-start.29 = (bf16[512,1024]{1,0:T(8,128)(2,1)}, bf16[512,1024]{1,0:T(8,128)(2,1)S(1)}, u32[]{:S(2)}, u32[]{:S(2)}) collective-permute-start(bf16[512,1024]{1,0:T(8,128)(2,1)} %get-tuple-element.233), channel_id=1, source_target_pairs={{0,1},{1,0},{2,3},{3,2},{4,5},{5,4},{6,7},{7,6},{8,9},{9,8},{10,11... | collective-permute-start | bytes 3145736 | tf_op jit(solution)/shard_map/ppermute | solution.py:721
  160.8 21.1 %collective-permute-start.30 = (bf16[512,1024]{1,0:T(8,128)(2,1)S(1)}, bf16[512,1024]{1,0:T(8,128)(2,1)S(1)}, u32[]{:S(2)}, u32[]{:S(2)}) collective-permute-start(bf16[512,1024]{1,0:T(8,128)(2,1)S(1)} %add_convert_fusion.10.refs_1_.att0.refs_4_), channel_id=1, source_target_pairs={{0,1},{1,0},{2,3},{3,2},{4,5},{5,4},{6,7},{7,6},{8,9},{9,8},{10,11... | collective-permute-start | bytes 3145736 | tf_op jit(solution)/shard_map/ppermute | solution.py:734
  161.0 20.0 %collective-permute-start.26 = (bf16[128,3072]{1,0:T(8,128)(2,1)S(1)}, bf16[128,3072]{1,0:T(8,128)(2,1)}, u32[]{:S(2)}, u32[]{:S(2)}) collective-permute-start(bf16[128,3072]{1,0:T(8,128)(2,1)S(1)} %collective-permute-done.23.refs_13_), channel_id=1, source_target_pairs={{0,8},{8,16},{16,24},{24,28},{28,20},{20,12},{12,4},{4,0},{1,9},{9... | collective-permute-start | bytes 2359304 | tf_op jit(solution)/shard_map/ppermute | solution.py:664
  162.2 19.7 %collective-permute-start.27 = (bf16[128,3072]{1,0:T(8,128)(2,1)S(1)}, bf16[128,3072]{1,0:T(8,128)(2,1)}, u32[]{:S(2)}, u32[]{:S(2)}) collective-permute-start(bf16[128,3072]{1,0:T(8,128)(2,1)S(1)} %collective-permute-done.24.refs_6_), channel_id=1, source_target_pairs={{8,0},{16,8},{24,16},{28,24},{20,28},{12,20},{4,12},{0,4},{9,1},{1... | collective-permute-start | bytes 2359304 | tf_op jit(solution)/shard_map/ppermute | solution.py:665
  182.0 19.0 %collective-permute-start.31 = (bf16[128,3072]{1,0:T(8,128)(2,1)}, bf16[128,3072]{1,0:T(8,128)(2,1)S(1)}, u32[]{:S(2)}, u32[]{:S(2)}) collective-permute-start(bf16[128,3072]{1,0:T(8,128)(2,1)} %collective-permute-done.26.refs_12_), channel_id=1, source_target_pairs={{0,8},{8,16},{16,24},{24,28},{28,20},{20,12},{12,4},{4,0},{1,9},{9... | collective-permute-start | bytes 2359304 | tf_op jit(solution)/shard_map/ppermute | solution.py:664
  182.4 18.9 %collective-permute-start.32 = (bf16[128,3072]{1,0:T(8,128)(2,1)}, bf16[128,3072]{1,0:T(8,128)(2,1)S(1)}, u32[]{:S(2)}, u32[]{:S(2)}) collective-permute-start(bf16[128,3072]{1,0:T(8,128)(2,1)} %collective-permute-done.27.refs_7_), channel_id=1, source_target_pairs={{8,0},{16,8},{24,16},{28,24},{20,28},{12,20},{4,12},{0,4},{9,1},{1... | collective-permute-start | bytes 2359304 | tf_op jit(solution)/shard_map/ppermute | solution.py:665
  184.1 12.7 %collective-permute-start.33 = (bf16[256,1024]{1,0:T(8,128)(2,1)S(1)}, bf16[256,1024]{1,0:T(8,128)(2,1)S(1)}, u32[]{:S(2)}, u32[]{:S(2)}) collective-permute-start(bf16[256,1024]{1,0:T(8,128)(2,1)S(1)} %get-tuple-element.237), channel_id=1, source_target_pairs={{0,2},{1,3},{2,0},{3,1},{4,6},{5,7},{6,4},{7,5},{8,10},{9,11},{10,... | collective-permute-start | bytes 1572872 | tf_op jit(solution)/shard_map/ppermute | solution.py:728
  201.4 12.1 %collective-permute-start.37 = (bf16[64,3072]{1,0:T(8,128)(2,1)S(1)}, bf16[64,3072]{1,0:T(8,128)(2,1)S(1)}, u32[]{:S(2)}, u32[]{:S(2)}) collective-permute-start(bf16[64,3072]{1,0:T(8,128)(2,1)S(1)} %copy-done.77), channel_id=1, source_target_pairs={{8,0},{16,8},{24,16},{28,24},{20,28},{12,20},{4,12},{0,4},{9,1},{1... | collective-permute-start | bytes 1179656 | tf_op jit(solution)/shard_map/ppermute | solution.py:703
  202.8 12.1 %collective-permute-start.35 = (bf16[64,3072]{1,0:T(8,128)(2,1)S(1)}, bf16[64,3072]{1,0:T(8,128)(2,1)S(1)}, u32[]{:S(2)}, u32[]{:S(2)}) collective-permute-start(bf16[64,3072]{1,0:T(8,128)(2,1)S(1)} %slice.108), channel_id=1, source_target_pairs={{0,8},{8,16},{16,24},{24,28},{28,20},{20,12},{12,4},{4,0},{1,9},{9... | collective-permute-start | bytes 1179656 | tf_op jit(solution)/shard_map/ppermute | solution.py:664
  203.5 15.6 %collective-permute-start.36 = (bf16[64,3072]{1,0:T(8,128)(2,1)S(1)}, bf16[64,3072]{1,0:T(8,128)(2,1)S(1)}, u32[]{:S(2)}, u32[]{:S(2)}) collective-permute-start(bf16[64,3072]{1,0:T(8,128)(2,1)S(1)} %slice.109), channel_id=1, source_target_pairs={{8,0},{16,8},{24,16},{28,24},{20,28},{12,20},{4,12},{0,4},{9,1},{1... | collective-permute-start | bytes 1179656 | tf_op jit(solution)/shard_map/ppermute | solution.py:665
  205.0 15.2 %collective-permute-start.34 = (bf16[64,3072]{1,0:T(8,128)(2,1)S(1)}, bf16[64,3072]{1,0:T(8,128)(2,1)S(1)}, u32[]{:S(2)}, u32[]{:S(2)}) collective-permute-start(bf16[64,3072]{1,0:T(8,128)(2,1)S(1)} %copy-done.76), channel_id=1, source_target_pairs={{0,8},{8,16},{16,24},{24,28},{28,20},{20,12},{12,4},{4,0},{1,9},{9... | collective-permute-start | bytes 1179656 | tf_op jit(solution)/shard_map/ppermute | solution.py:702
  205.6 14.5 %collective-permute-start.38 = (bf16[256,1024]{1,0:T(8,128)(2,1)S(1)}, bf16[256,1024]{1,0:T(8,128)(2,1)}, u32[]{:S(2)}, u32[]{:S(2)}) collective-permute-start(bf16[256,1024]{1,0:T(8,128)(2,1)S(1)} %get-tuple-element.243), channel_id=1, source_target_pairs={{0,2},{1,3},{2,0},{3,1},{4,6},{5,7},{6,4},{7,5},{8,10},{9,11},{10,... | collective-permute-start | bytes 1572872 | tf_op jit(solution)/shard_map/ppermute | solution.py:728
  220.2 28.1 %collective-permute-start.41 = (bf16[512,1024]{1,0:T(8,128)(2,1)S(1)}, bf16[512,1024]{1,0:T(8,128)(2,1)S(1)}, u32[]{:S(2)}, u32[]{:S(2)}) collective-permute-start(bf16[512,1024]{1,0:T(8,128)(2,1)S(1)} %add_convert_fusion.12), channel_id=1, source_target_pairs={{0,2},{1,3},{2,0},{3,1},{4,6},{5,7},{6,4},{7,5},{8,10},{9,11},{10,... | collective-permute-start | bytes 3145736 | tf_op jit(solution)/shard_map/ppermute | solution.py:728
  220.8 27.4 %collective-permute-start.40 = (bf16[128,3072]{1,0:T(8,128)(2,1)S(1)}, bf16[128,3072]{1,0:T(8,128)(2,1)S(1)}, u32[]{:S(2)}, u32[]{:S(2)}) collective-permute-start(bf16[128,3072]{1,0:T(8,128)(2,1)S(1)} %add_convert_fusion.25), channel_id=1, source_target_pairs={{8,0},{16,8},{24,16},{28,24},{20,28},{12,20},{4,12},{0,4},{9,1},{1... | collective-permute-start | bytes 2359304 | tf_op jit(solution)/shard_map/ppermute | solution.py:703
  222.2 26.0 %collective-permute-start.39 = (bf16[128,3072]{1,0:T(8,128)(2,1)S(1)}, bf16[128,3072]{1,0:T(8,128)(2,1)S(1)}, u32[]{:S(2)}, u32[]{:S(2)}) collective-permute-start(bf16[128,3072]{1,0:T(8,128)(2,1)S(1)} %add_convert_fusion.27), channel_id=1, source_target_pairs={{0,8},{8,16},{16,24},{24,28},{28,20},{20,12},{12,4},{4,0},{1,9},{9... | collective-permute-start | bytes 2359304 | tf_op jit(solution)/shard_map/ppermute | solution.py:702
  254.0 24.6 %collective-permute-start.45 = (bf16[128,3072]{1,0:T(8,128)(2,1)}, bf16[128,3072]{1,0:T(8,128)(2,1)S(1)}, u32[]{:S(2)}, u32[]{:S(2)}) collective-permute-start(bf16[128,3072]{1,0:T(8,128)(2,1)} %get-tuple-element.256), channel_id=1, source_target_pairs={{0,8},{8,16},{16,24},{24,28},{28,20},{20,12},{12,4},{4,0},{1,9},{9... | collective-permute-start | bytes 2359304 | tf_op jit(solution)/shard_map/ppermute | solution.py:702
  254.9 24.9 %collective-permute-start.47 = (bf16[512,1024]{1,0:T(8,128)(2,1)S(1)}, bf16[512,1024]{1,0:T(8,128)(2,1)S(1)}, u32[]{:S(2)}, u32[]{:S(2)}) collective-permute-start(bf16[512,1024]{1,0:T(8,128)(2,1)S(1)} %add_convert_fusion.9), channel_id=1, source_target_pairs={{0,2},{1,3},{2,0},{3,1},{4,6},{5,7},{6,4},{7,5},{8,10},{9,11},{10,... | collective-permute-start | bytes 3145736 | tf_op jit(solution)/shard_map/ppermute | solution.py:728
  256.3 22.5 %collective-permute-start.46 = (bf16[128,3072]{1,0:T(8,128)(2,1)S(1)}, bf16[128,3072]{1,0:T(8,128)(2,1)S(1)}, u32[]{:S(2)}, u32[]{:S(2)}) collective-permute-start(bf16[128,3072]{1,0:T(8,128)(2,1)S(1)} %get-tuple-element.258), channel_id=1, source_target_pairs={{8,0},{16,8},{24,16},{28,24},{20,28},{12,20},{4,12},{0,4},{9,1},{1... | collective-permute-start | bytes 2359304 | tf_op jit(solution)/shard_map/ppermute | solution.py:703
  280.5 30.5 %collective-permute-start.49 = (bf16[128,3072]{1,0:T(8,128)(2,1)S(1)}, bf16[128,3072]{1,0:T(8,128)(2,1)S(1)}, u32[]{:S(2)}, u32[]{:S(2)}) collective-permute-start(bf16[128,3072]{1,0:T(8,128)(2,1)S(1)} %add_convert_fusion.23), channel_id=1, source_target_pairs={{0,8},{8,16},{16,24},{24,28},{28,20},{20,12},{12,4},{4,0},{1,9},{9... | collective-permute-start | bytes 2359304 | tf_op jit(solution)/shard_map/ppermute | solution.py:702
  281.1 29.9 %collective-permute-start.50 = (bf16[128,3072]{1,0:T(8,128)(2,1)S(1)}, bf16[128,3072]{1,0:T(8,128)(2,1)S(1)}, u32[]{:S(2)}, u32[]{:S(2)}) collective-permute-start(bf16[128,3072]{1,0:T(8,128)(2,1)S(1)} %add_convert_fusion.22), channel_id=1, source_target_pairs={{8,0},{16,8},{24,16},{28,24},{20,28},{12,20},{4,12},{0,4},{9,1},{1... | collective-permute-start | bytes 2359304 | tf_op jit(solution)/shard_map/ppermute | solution.py:703
  282.6 28.4 %collective-permute-start.51 = (bf16[64,3072]{1,0:T(8,128)(2,1)}, bf16[64,3072]{1,0:T(8,128)(2,1)S(1)}, u32[]{:S(2)}, u32[]{:S(2)}) collective-permute-start(bf16[64,3072]{1,0:T(8,128)(2,1)} %get-tuple-element.277), channel_id=1, source_target_pairs={{0,8},{8,16},{16,24},{24,28},{28,20},{20,12},{12,4},{4,0},{1,9},{9... | collective-permute-start | bytes 1179656 | tf_op jit(solution)/shard_map/ppermute | solution.py:702
  283.1 27.8 %collective-permute-start.52 = (bf16[64,3072]{1,0:T(8,128)(2,1)S(1)}, bf16[64,3072]{1,0:T(8,128)(2,1)S(1)}, u32[]{:S(2)}, u32[]{:S(2)}) collective-permute-start(bf16[64,3072]{1,0:T(8,128)(2,1)S(1)} %copy-done.78), channel_id=1, source_target_pairs={{8,0},{16,8},{24,16},{28,24},{20,28},{12,20},{4,12},{0,4},{9,1},{1... | collective-permute-start | bytes 1179656 | tf_op jit(solution)/shard_map/ppermute | solution.py:703
  315.7 25.3 %collective-permute-start.57 = (bf16[512,1024]{1,0:T(8,128)(2,1)S(1)}, bf16[512,1024]{1,0:T(8,128)(2,1)S(1)}, u32[]{:S(2)}, u32[]{:S(2)}) collective-permute-start(bf16[512,1024]{1,0:T(8,128)(2,1)S(1)} %add_convert_fusion.5), channel_id=1, source_target_pairs={{0,2},{1,3},{2,0},{3,1},{4,6},{5,7},{6,4},{7,5},{8,10},{9,11},{10,... | collective-permute-start | bytes 3145736 | tf_op jit(solution)/shard_map/ppermute | solution.py:728
  317.3 20.8 %collective-permute-start.55 = (bf16[128,3072]{1,0:T(8,128)(2,1)S(1)}, bf16[128,3072]{1,0:T(8,128)(2,1)S(1)}, u32[]{:S(2)}, u32[]{:S(2)}) collective-permute-start(bf16[128,3072]{1,0:T(8,128)(2,1)S(1)} %add_convert_fusion.21), channel_id=1, source_target_pairs={{0,8},{8,16},{16,24},{24,28},{28,20},{20,12},{12,4},{4,0},{1,9},{9... | collective-permute-start | bytes 2359304 | tf_op jit(solution)/shard_map/ppermute | solution.py:702
  318.0 20.1 %collective-permute-start.56 = (bf16[128,3072]{1,0:T(8,128)(2,1)S(1)}, bf16[128,3072]{1,0:T(8,128)(2,1)S(1)}, u32[]{:S(2)}, u32[]{:S(2)}) collective-permute-start(bf16[128,3072]{1,0:T(8,128)(2,1)S(1)} %add_convert_fusion.20), channel_id=1, source_target_pairs={{8,0},{16,8},{24,16},{28,24},{20,28},{12,20},{4,12},{0,4},{9,1},{1... | collective-permute-start | bytes 2359304 | tf_op jit(solution)/shard_map/ppermute | solution.py:703
  345.6 25.9 %collective-permute-start.61 = (bf16[128,3072]{1,0:T(8,128)(2,1)S(1)}, bf16[128,3072]{1,0:T(8,128)(2,1)}, u32[]{:S(2)}, u32[]{:S(2)}) collective-permute-start(bf16[128,3072]{1,0:T(8,128)(2,1)S(1)} %add_convert_fusion.19), channel_id=1, source_target_pairs={{0,8},{8,16},{16,24},{24,28},{28,20},{20,12},{12,4},{4,0},{1,9},{9... | collective-permute-start | bytes 2359304 | tf_op jit(solution)/shard_map/ppermute | solution.py:702
  346.2 26.7 %collective-permute-start.63 = (bf16[512,1024]{1,0:T(8,128)(2,1)S(1)}, bf16[512,1024]{1,0:T(8,128)(2,1)S(1)}, u32[]{:S(2)}, u32[]{:S(2)}) collective-permute-start(bf16[512,1024]{1,0:T(8,128)(2,1)S(1)} %add_convert_fusion.3), channel_id=1, source_target_pairs={{0,2},{1,3},{2,0},{3,1},{4,6},{5,7},{6,4},{7,5},{8,10},{9,11},{10,... | collective-permute-start | bytes 3145736 | tf_op jit(solution)/shard_map/ppermute | solution.py:728
  348.9 24.1 %collective-permute-start.62 = (bf16[128,3072]{1,0:T(8,128)(2,1)}, bf16[128,3072]{1,0:T(8,128)(2,1)S(1)}, u32[]{:S(2)}, u32[]{:S(2)}) collective-permute-start(bf16[128,3072]{1,0:T(8,128)(2,1)} %add_convert_fusion.18), channel_id=1, source_target_pairs={{8,0},{16,8},{24,16},{28,24},{20,28},{12,20},{4,12},{0,4},{9,1},{1... | collective-permute-start | bytes 2359304 | tf_op jit(solution)/shard_map/ppermute | solution.py:703
  350.2 21.3 %collective-permute-start.64 = (f32[4,1024]{1,0:T(4,128)S(1)}, f32[4,1024]{1,0:T(4,128)S(1)}, u32[]{:S(2)}, u32[]{:S(2)}) collective-permute-start(f32[4,1024]{1,0:T(4,128)S(1)} %fusion.1), channel_id=1, source_target_pairs={{0,2},{1,3},{2,0},{3,1},{4,6},{5,7},{6,4},{7,5},{8,10},{9,11},{10,... | collective-permute-start | bytes 49160 | tf_op jit(solution)/shard_map/ppermute | solution.py:879
  373.0 27.0 %collective-permute-start.69 = (bf16[512,1024]{1,0:T(8,128)(2,1)S(1)}, bf16[512,1024]{1,0:T(8,128)(2,1)S(1)}, u32[]{:S(2)}, u32[]{:S(2)}) collective-permute-start(bf16[512,1024]{1,0:T(8,128)(2,1)S(1)} %add_convert_fusion.4), channel_id=1, source_target_pairs={{0,2},{1,3},{2,0},{3,1},{4,6},{5,7},{6,4},{7,5},{8,10},{9,11},{10,... | collective-permute-start | bytes 3145736 | tf_op jit(solution)/shard_map/ppermute | solution.py:728
  374.8 25.2 %collective-permute-start.67 = (bf16[128,3072]{1,0:T(8,128)(2,1)S(1)}, bf16[128,3072]{1,0:T(8,128)(2,1)S(1)}, u32[]{:S(2)}, u32[]{:S(2)}) collective-permute-start(bf16[128,3072]{1,0:T(8,128)(2,1)S(1)} %add_convert_fusion.17), channel_id=1, source_target_pairs={{0,8},{8,16},{16,24},{24,28},{28,20},{20,12},{12,4},{4,0},{1,9},{9... | collective-permute-start | bytes 2359304 | tf_op jit(solution)/shard_map/ppermute | solution.py:702
  376.5 23.5 %collective-permute-start.68 = (bf16[128,3072]{1,0:T(8,128)(2,1)S(1)}, bf16[128,3072]{1,0:T(8,128)(2,1)S(1)}, u32[]{:S(2)}, u32[]{:S(2)}) collective-permute-start(bf16[128,3072]{1,0:T(8,128)(2,1)S(1)} %add_convert_fusion.16), channel_id=1, source_target_pairs={{8,0},{16,8},{24,16},{28,24},{20,28},{12,20},{4,12},{0,4},{9,1},{1... | collective-permute-start | bytes 2359304 | tf_op jit(solution)/shard_map/ppermute | solution.py:703
  376.8 21.7 %collective-permute-start.65 = (bf16[128,1024]{1,0:T(8,128)(2,1)S(1)}, bf16[128,1024]{1,0:T(8,128)(2,1)S(1)}, u32[]{:S(2)}, u32[]{:S(2)}) collective-permute-start(bf16[128,1024]{1,0:T(8,128)(2,1)S(1)} %copy-done.80), channel_id=1, source_target_pairs={{0,8},{8,16},{16,24},{24,28},{28,20},{20,12},{12,4},{4,0},{1,9},{9... | collective-permute-start | bytes 786440 | tf_op jit(solution)/shard_map/ppermute | solution.py:702
  378.5 21.5 %collective-permute-start.66 = (bf16[128,1024]{1,0:T(8,128)(2,1)S(1)}, bf16[128,1024]{1,0:T(8,128)(2,1)S(1)}, u32[]{:S(2)}, u32[]{:S(2)}) collective-permute-start(bf16[128,1024]{1,0:T(8,128)(2,1)S(1)} %copy-done.79), channel_id=1, source_target_pairs={{8,0},{16,8},{24,16},{28,24},{20,28},{12,20},{4,12},{0,4},{9,1},{1... | collective-permute-start | bytes 786440 | tf_op jit(solution)/shard_map/ppermute | solution.py:703
  400.4 16.0 %collective-permute-start.73 = (bf16[512,1024]{1,0:T(8,128)(2,1)S(1)}, bf16[512,1024]{1,0:T(8,128)(2,1)S(1)}, u32[]{:S(2)}, u32[]{:S(2)}) collective-permute-start(bf16[512,1024]{1,0:T(8,128)(2,1)S(1)} %add_convert_fusion.1.mine), channel_id=1, source_target_pairs={{0,1},{1,0},{2,3},{3,2},{4,5},{5,4},{6,7},{7,6},{8,9},{9,8},{10,11... | collective-permute-start | bytes 3145736 | tf_op jit(solution)/shard_map/ppermute | solution.py:734
  401.1 15.3 %collective-permute-start.74 = (bf16[512,1024]{1,0:T(8,128)(2,1)S(1)}, bf16[512,1024]{1,0:T(8,128)(2,1)S(1)}, u32[]{:S(2)}, u32[]{:S(2)}) collective-permute-start(bf16[512,1024]{1,0:T(8,128)(2,1)S(1)} %add_convert_fusion.refs_6_), channel_id=1, source_target_pairs={{0,1},{1,0},{2,3},{3,2},{4,5},{5,4},{6,7},{7,6},{8,9},{9,8},{10,11... | collective-permute-start | bytes 3145736 | tf_op jit(solution)/shard_map/ppermute | solution.py:734
  401.9 14.0 %collective-permute-start.70 = (bf16[256,1024]{1,0:T(8,128)(2,1)S(1)}, bf16[256,1024]{1,0:T(8,128)(2,1)S(1)}, u32[]{:S(2)}, u32[]{:S(2)}) collective-permute-start(bf16[256,1024]{1,0:T(8,128)(2,1)S(1)} %add_convert_fusion.33), channel_id=1, source_target_pairs={{0,8},{8,16},{16,24},{24,28},{28,20},{20,12},{12,4},{4,0},{1,9},{9... | collective-permute-start | bytes 1572872 | tf_op jit(solution)/shard_map/ppermute | solution.py:702
  402.8 13.7 %collective-permute-start.71 = (bf16[256,1024]{1,0:T(8,128)(2,1)S(1)}, bf16[256,1024]{1,0:T(8,128)(2,1)S(1)}, u32[]{:S(2)}, u32[]{:S(2)}) collective-permute-start(bf16[256,1024]{1,0:T(8,128)(2,1)S(1)} %add_convert_fusion.32), channel_id=1, source_target_pairs={{8,0},{16,8},{24,16},{28,24},{20,28},{12,20},{4,12},{0,4},{9,1},{1... | collective-permute-start | bytes 1572872 | tf_op jit(solution)/shard_map/ppermute | solution.py:703
  416.5 14.5 %collective-permute-start.75 = (bf16[256,1024]{1,0:T(8,128)(2,1)S(1)}, bf16[256,1024]{1,0:T(8,128)(2,1)S(1)}, u32[]{:S(2)}, u32[]{:S(2)}) collective-permute-start(bf16[256,1024]{1,0:T(8,128)(2,1)S(1)} %add_convert_fusion.31), channel_id=1, source_target_pairs={{0,8},{8,16},{16,24},{24,28},{28,20},{20,12},{12,4},{4,0},{1,9},{9... | collective-permute-start | bytes 1572872 | tf_op jit(solution)/shard_map/ppermute | solution.py:702
  418.5 12.8 %collective-permute-start.76 = (bf16[256,1024]{1,0:T(8,128)(2,1)S(1)}, bf16[256,1024]{1,0:T(8,128)(2,1)S(1)}, u32[]{:S(2)}, u32[]{:S(2)}) collective-permute-start(bf16[256,1024]{1,0:T(8,128)(2,1)S(1)} %add_convert_fusion.30), channel_id=1, source_target_pairs={{8,0},{16,8},{24,16},{28,24},{20,28},{12,20},{4,12},{0,4},{9,1},{1... | collective-permute-start | bytes 1572872 | tf_op jit(solution)/shard_map/ppermute | solution.py:703
  418.8 12.2 %collective-permute-start.77 = (f32[4,1024]{1,0:T(4,128)S(1)}, f32[4,1024]{1,0:T(4,128)S(1)}, u32[]{:S(2)}, u32[]{:S(2)}) collective-permute-start(f32[4,1024]{1,0:T(4,128)S(1)} %add.199), channel_id=1, source_target_pairs={{0,8},{4,12},{8,0},{12,4},{16,24},{20,28},{24,16},{28,20},{1,9},{5... | collective-permute-start | bytes 49160 | tf_op jit(solution)/shard_map/ppermute | solution.py:879
  431.2 14.5 %collective-permute-start.79 = (bf16[256,1024]{1,0:T(8,128)(2,1)S(1)}, bf16[256,1024]{1,0:T(8,128)(2,1)S(1)}, u32[]{:S(2)}, u32[]{:S(2)}) collective-permute-start(bf16[256,1024]{1,0:T(8,128)(2,1)S(1)} %add_convert_fusion.29), channel_id=1, source_target_pairs={{0,8},{8,16},{16,24},{24,28},{28,20},{20,12},{12,4},{4,0},{1,9},{9... | collective-permute-start | bytes 1572872 | tf_op jit(solution)/shard_map/ppermute | solution.py:702
  431.8 13.9 %collective-permute-start.80 = (bf16[256,1024]{1,0:T(8,128)(2,1)S(1)}, bf16[256,1024]{1,0:T(8,128)(2,1)S(1)}, u32[]{:S(2)}, u32[]{:S(2)}) collective-permute-start(bf16[256,1024]{1,0:T(8,128)(2,1)S(1)} %add_convert_fusion.28), channel_id=1, source_target_pairs={{8,0},{16,8},{24,16},{28,24},{20,28},{12,20},{4,12},{0,4},{9,1},{1... | collective-permute-start | bytes 1572872 | tf_op jit(solution)/shard_map/ppermute | solution.py:703
  433.6 11.6 %collective-permute-start.78 = (f32[4,1024]{1,0:T(4,128)S(1)}, f32[4,1024]{1,0:T(4,128)S(1)}, u32[]{:S(2)}, u32[]{:S(2)}) collective-permute-start(f32[4,1024]{1,0:T(4,128)S(1)} %add.204), channel_id=1, source_target_pairs={{0,16},{4,20},{8,24},{12,28},{16,0},{20,4},{24,8},{28,12},{1,17},{... | collective-permute-start | bytes 49160 | tf_op jit(solution)/shard_map/ppermute | solution.py:879
  (99 other events, 894.6 us)

commit v6 on v5

--- a/solution.py
+++ b/solution.py
@@ -81,6 +81,10 @@
     def pick(self, pair):
         return jnp.where(pl.program_id(0) < self.count, pair[1][...], pair[0][...])
 
+    def one(self, width, half):
+        shift = 0 if half else self.count
+        return pl.BlockSpec((ROWS, width), lambda i, p: (self.block(i + shift, p), 0))
+
     def put(self, pair, value):
         pair[0][...] = value
 
@@ -162,21 +166,28 @@
     return jnp.where(low, stacked[:half], stacked[half:])
 
 
-def visible(rows, keys, steps):
-    row = lax.broadcasted_iota(jnp.int32, (rows, keys), 0) % SUB
-    key = lax.broadcasted_iota(jnp.int32, (rows, keys), 1)
-    same = row // steps == (key % SUB) // steps
-    if keys == SUB:
-        return same & (row >= key)
-    return same & ((key < SUB) | (row >= key - SUB))
-
-
-def softmax(query, keys, steps):
-    raw = mm(query, keys, NT) * HDIM ** (-0.5)
-    masked = jnp.where(visible(raw.shape[0], raw.shape[1], steps), raw, NEG)
-    top = jnp.max(masked, axis=-1, keepdims=True)
-    power = jnp.exp(masked - top)
-    return power / jnp.sum(power, axis=-1, keepdims=True)
+def hidden_keys(rows, keys, steps, turned=False):
+    shape, axis = ((keys, rows), 1) if turned else ((rows, keys), 0)
+    row = lax.broadcasted_iota(jnp.int32, shape, axis) & (SUB - 1)
+    spot = lax.broadcasted_iota(jnp.int32, shape, 1 - axis)
+    key = spot & (SUB - 1)
+    shift = steps.bit_length() - 1
+    seen = lax.shift_right_logical(row, shift) == lax.shift_right_logical(key, shift)
+    own = spot >= keys - SUB
+    seen = seen & ((row >= key) | jnp.logical_not(own))
+    return jnp.where(seen, 0.0, NEG)
+
+
+def softmax(query, keys, hidden):
+    raw = mm(query, keys, NT) + hidden
+    power = jnp.exp(raw - jnp.max(raw, axis=-1, keepdims=True))
+    return power * (1.0 / jnp.sum(power, axis=-1, keepdims=True))
+
+
+def softmax_turned(query, keys, hidden):
+    raw = mm(keys, query, NT) + hidden
+    power = jnp.exp(raw - jnp.max(raw, axis=0, keepdims=True))
+    return power * (1.0 / jnp.sum(power, axis=0, keepdims=True))
 
 
 class Pieces:
@@ -215,12 +226,12 @@
                 copy.wait()
 
 
-def attend_body(pieces, halves, steps, hw, later, places, *refs):
+def attend_body(pieces, halves, steps, hw, later, filled, places, *refs):
     x_ref, gain_ref, *refs = refs
     if later:
         before_ref, *refs = refs
     w_refs, refs = refs[: pieces.count], refs[pieces.count :]
-    h_ref, qkv_ref, mixed_ref, mine_ref, other_ref, w_ref, sems = refs
+    h_ref, qkv_ref, mixed_ref, *part_refs, w_ref, sems = refs[filled:]
     pieces.start(w_refs, places, w_ref, sems, range(1))
     normed, _ = norm(x_ref[...].astype(F32))
     hidden = (normed * gain_ref[...]).astype(BF)
@@ -228,6 +239,8 @@
     pieces.wait(w_refs, places, w_ref, sems, 0)
     qkv = mm(hidden, w_ref[:, : 3 * hw]).astype(BF)
     qkv_ref[...] = qkv
+    scale = jnp.asarray(HDIM ** (-0.5), BF)
+    hidden_scores = hidden_keys(2 * SUB, 2 * SUB if later else SUB, steps)
     for s in range(x_ref.shape[0] // SUB):
         rows = slice(s * SUB, (s + 1) * SUB)
         for j in range(hw // PAIR):
@@ -238,39 +251,49 @@
                 )
                 k = jnp.concatenate([k_old, k], axis=0)
                 v = jnp.concatenate([v_old, v], axis=0)
-            probs = softmax(stack_heads(q), k, steps).astype(BF)
+            probs = softmax(stack_heads(q) * scale, k, hidden_scores).astype(BF)
             mixed_ref[rows, j * PAIR : (j + 1) * PAIR] = pick_heads(mm(probs, v)).astype(BF)
-    halves.put((mine_ref, other_ref), mm(mixed_ref[...], w_ref[:, 3 * hw :], NT).astype(BF))
-
-
-def attend(places, x, gain, before, w, steps):
+    part = mm(mixed_ref[...], w_ref[:, 3 * hw :], NT).astype(BF)
+    if len(part_refs) == 2:
+        halves.put(part_refs, part)
+    else:
+        part_refs[0][...] = part
+
+
+def attend(places, x, gain, before, w, steps, half=None, filled=()):
     tokens, width = x.shape
     pieces, halves = Pieces(*w, 1), Halves(tokens)
     hw = pieces.shape[1] // 4
+    spec = halves.both if half is None else functools.partial(halves.one, half=half)
     ins = [x, gain]
-    specs = [halves.both(width), whole(gain.shape)]
+    specs = [spec(width), whole(gain.shape)]
     if before is not None:
         ins.append(before)
-        specs.append(halves.both(3 * hw))
+        specs.append(spec(3 * hw))
+    ins += [*pieces.arrays, *filled]
+    specs += [HBM] * (pieces.count + len(filled))
     widths = (width, 3 * hw, hw)
-    *out, mine, other = kernel_call(
-        functools.partial(attend_body, pieces, halves, steps, hw, before is not None),
-        halves.grid,
-        [*ins, *pieces.arrays],
-        [*specs, *[HBM] * pieces.count],
-        [out_of((tokens, n)) for n in widths] + [out_of((tokens // 2, width))] * 2,
-        [halves.both(n) for n in widths] + halves.pair(width),
+    *out, part = kernel_call(
+        functools.partial(attend_body, pieces, halves, steps, hw, before is not None, len(filled)),
+        halves.grid if half is None else (halves.count,),
+        ins,
+        specs,
+        [out_of((tokens, n)) for n in widths] + [out_of((tokens // 2, width))] * (2 if half is None else 1),
+        [spec(n) for n in widths] + (halves.pair(width) if half is None else [rows_of(ROWS, width)]),
         2 * tokens * width * 4 * hw,
         pieces.scratch,
         places,
+        {len(ins) - len(filled) + 1 + k: k for k in range(len(filled))},
     )
-    return *out, (mine, other)
+    if half is None:
+        return *out[:3], (out[3], part)
+    return *out, part
 
 
 def units_body(pieces, halves, units, places, *refs):
     x_ref, att0, att1, g_ref, gain_ref, *refs = refs
     w_refs, refs = refs[: pieces.count], refs[pieces.count :]
-    h_ref, inner_ref, dgate_ref, dup_ref, dh0, dh1, mlp0, mlp1, w_ref, sems = refs
+    h_ref, inner_ref, dboth_ref, dh0, dh1, mlp0, mlp1, w_ref, sems = refs
     pieces.start(w_refs, places, w_ref, sems, (2, 0, 1))
     normed, _ = norm(x_ref[...].astype(F32) + halves.pick((att0, att1)).astype(F32))
     hidden = (normed * gain_ref[...]).astype(BF)
@@ -289,10 +312,9 @@
         sigma = 1.0 / (1.0 + jnp.exp(-gate))
         active = gate * sigma
         inner_ref[:, c[0]] = (active * up).astype(BF)
-        dup_ref[:, c[0]] = (d_inner * active).astype(BF)
-        dgate_ref[:, c[0]] = (d_inner * up * sigma * (1.0 + gate * (1.0 - sigma))).astype(BF)
-    grad = mm(dgate_ref[...], w_ref[:, :units], NT) + mm(dup_ref[...], w_ref[:, units : 2 * units], NT)
-    halves.put((dh0, dh1), grad.astype(BF))
+        dboth_ref[:, c[1]] = (d_inner * active).astype(BF)
+        dboth_ref[:, c[0]] = (d_inner * up * (sigma + active * (1.0 - sigma))).astype(BF)
+    halves.put((dh0, dh1), mm(dboth_ref[...], w_ref[:, : 2 * units], NT).astype(BF))
     halves.put((mlp0, mlp1), mm(inner_ref[...], w_ref[:, 2 * units :], NT).astype(BF))
 
 
@@ -301,7 +323,7 @@
     pieces, halves = Pieces(*w, 3), Halves(tokens)
     units = pieces.shape[1] // 3
     part = halves.both(width)
-    widths = (width, units, units, units)
+    widths = (width, units, 2 * units)
     *out, dh0, dh1, mlp0, mlp1 = kernel_call(
         functools.partial(units_body, pieces, halves, units),
         halves.grid,
@@ -456,17 +478,21 @@
     )
 
 
-def attend_back_body(pieces, shared, steps, hw, places, x0, x1, dm0, dm1, qkv0, qkv1, *refs):
+def attend_back_body(pieces, shared, halves, steps, hw, places, x0, x1, dm0, dm1, qkv0, qkv1, *refs):
     sides = [
         [r for a in p.arrays for r, b in zip(refs, shared.arrays) if a is b] for p in pieces
     ]
-    dqkv0, dqkv1, mine, other, dgain, w0, sems0, w1, sems1 = refs[-9:]
+    parts = refs[-6 - 2 * halves.count : -6]
+    dqkv0, dqkv1 = refs[-8 - 2 * halves.count : -6 - 2 * halves.count]
+    dgain, w0, sems0, w1, sems1, d_hidden = refs[-6:]
     for p, s, w, sems in zip(pieces, sides, (w0, w1), (sems0, sems1)):
         p.start(s, places, w, sems, range(1))
     normed = [norm(x[...].astype(F32))[0] for x in (x0, x1)]
     for p, s, w, sems in zip(pieces, sides, (w0, w1), (sems0, sems1)):
         p.wait(s, places, w, sems, 0)
     scale = HDIM ** (-0.5)
+    low_scale = jnp.asarray(scale, BF)
+    hidden = [hidden_keys(2 * SUB, (1 + c) * SUB, steps, True) for c in range(2)]
     d_mixed = [mm(d[...], w[:, 3 * hw :]).astype(BF) for d, w in ((dm0, w0), (dm1, w1))]
     for s in range(dm0.shape[0] // SUB):
         rows = slice(s * SUB, (s + 1) * SUB)
@@ -478,16 +504,16 @@
             values = (v0, jnp.concatenate([v0, v1], axis=0))
             d_k, d_v = [], []
             for c, (q, out_ref) in enumerate(((q0, dqkv0), (q1, dqkv1))):
-                q_two = stack_heads(q)
+                q_two = stack_heads(q) * low_scale
                 d_two = stack_heads(d_mixed[c][rows, cols[0]])
-                soft = softmax(q_two, keys[c], steps)
-                d_probs = mm(d_two, values[c], NT)
-                inside = jnp.sum(soft * d_probs, axis=-1, keepdims=True)
+                soft = softmax_turned(q_two, keys[c], hidden[c])
+                d_probs = mm(values[c], d_two, NT)
+                inside = jnp.sum(soft * d_probs, axis=0, keepdims=True)
                 d_scores = (soft * (d_probs - inside)).astype(BF)
-                d_q = pick_heads(mm(d_scores, keys[c])) * scale
+                d_q = pick_heads(mm(d_scores, keys[c], TN)) * scale
                 out_ref[rows, cols[0]] = d_q.astype(BF)
-                d_k.append(mm(d_scores, q_two, TN) * scale)
-                d_v.append(mm(soft.astype(BF), d_two, TN))
+                d_k.append(mm(d_scores, q_two))
+                d_v.append(mm(soft.astype(BF), d_two))
             dqkv0[rows, cols[1]] = (d_k[0] + d_k[1][:SUB]).astype(BF)
             dqkv1[rows, cols[1]] = d_k[1][SUB:].astype(BF)
             dqkv0[rows, cols[2]] = (d_v[0] + d_v[1][:SUB]).astype(BF)
@@ -496,39 +522,38 @@
     for c, (d, w) in enumerate(((dqkv0, w0), (dqkv1, w1))):
         grad = mm(d[...], w[:, : 3 * hw], NT)
         gains.append(jnp.sum(grad * normed[c], axis=0, keepdims=True))
-        mine[c * ROWS : (c + 1) * ROWS] = grad.astype(BF)
-
-    @pl.when(pl.program_id(0) == 0)
-    def _():
-        other[...] = mine[...]
+        d_hidden[c] = grad.astype(BF)
+
+    for k, ref in enumerate(parts):
+
+        @pl.when(pl.program_id(0) == k)
+        def _():
+            ref[...] = d_hidden[...]
 
     add_up(dgain, jnp.concatenate(gains, axis=0))
 
 
-def attend_back(places, x, dm, qkv, w, part, before, steps):
+def attend_back(places, x, dm, qkv, w, steps):
     tokens, width = dm[0].shape
     halves = Halves(tokens)
     pieces = [Pieces(*side, 1) for side in w]
     shared = Pieces(w[0][0] + w[1][0], w[0][1], 1)
     hw = pieces[0].shape[1] // 4
-    spot = lambda i, p: (halves.block(i * halves.count, p) + part, 0)
-    flat, thin = pl.BlockSpec((ROWS, width), spot), pl.BlockSpec((ROWS, 3 * hw), spot)
-    ins = [*x, *dm, *qkv, *shared.arrays, *(before or ())]
-    specs = [flat] * 4 + [thin] * 2 + [HBM] * (len(ins) - 6)
-    alias = {len(ins) - 1: 0, len(ins): 1} if before else {}
-    d0, d1, mine, other, d_gain = kernel_call(
-        functools.partial(attend_back_body, pieces, shared, steps, hw),
-        (2,),
-        ins,
-        specs,
-        [out_of((tokens, 3 * hw))] * 2 + [out_of((2 * ROWS, width))] * 2 + [out_of((2, width), F32)],
-        [thin] * 2 + [whole((2 * ROWS, width))] * 2 + [whole((2, width))],
-        8 * ROWS * width * 4 * hw,
-        pieces[0].scratch + pieces[1].scratch,
+    flat, thin = halves.both(width), halves.both(3 * hw)
+    part = (2, ROWS, width)
+    d0, d1, *parts, d_gain = kernel_call(
+        functools.partial(attend_back_body, pieces, shared, halves, steps, hw),
+        halves.grid,
+        [*x, *dm, *qkv, *shared.arrays],
+        [flat] * 4 + [thin] * 2 + [HBM] * shared.count,
+        [out_of((tokens, 3 * hw))] * 2 + [out_of(part)] * (2 * halves.count) + [out_of((2, width), F32)],
+        [thin] * 2 + [whole(part)] * (2 * halves.count) + [whole((2, width))],
+        8 * tokens * width * 4 * hw,
+        pieces[0].scratch + pieces[1].scratch + [pltpu.VMEM(part, BF)],
         places,
-        alias,
     )
-    return (d0, d1), (mine, other), d_gain
+    parts = [part.reshape(-1, width) for part in parts]
+    return (d0, d1), list(zip(parts[halves.count :], parts)), d_gain
 
 
 def store_frames(out_ref, sums):
@@ -563,12 +588,11 @@
 
 
 def input_body(_, x0, x1, dm0, dm1, mine, other, gain_ref, *refs):
-    first = pl.program_id(0) == 0
     sums = []
+    dh = jnp.where(pl.program_id(0) == 0, other[...], mine[...]).astype(F32)
     for c, (x, dm) in enumerate(((x0, dm0), (x1, dm1))):
         rows = slice(c * ROWS, (c + 1) * ROWS)
-        dh = jnp.where(first, other[rows], mine[rows]).astype(F32)
-        back, _ = norm_back(dh, x[...].astype(F32), gain_ref[c : c + 1])
+        back, _ = norm_back(dh[rows], x[...].astype(F32), gain_ref[c : c + 1])
         sums.append(dm[...].astype(F32) + back)
     store_frames(refs[-1], sums)
 
@@ -722,10 +746,11 @@
         self.mine = self.add(self.pair[0], got)
         return self.mine
 
-    def far(self, parts=1):
-        rows = self.mine.shape[0] // parts
-        start = len(self.got) * rows
-        self.got.append(lax.ppermute(self.rounds.now(self.mine[start : start + rows]), "mp", self.far_moves))
+    def far(self, part=1.0):
+        start = sum(got.shape[0] for got in self.got)
+        rows = int(self.mine.shape[0] * part)
+        moved = self.rounds.now(self.mine[start : start + rows])
+        self.got.append(lax.ppermute(moved, "mp", self.far_moves))
         return self.got[-1]
 
     def last(self):
@@ -821,18 +846,21 @@
     got = heads[0].far()
     h1[1], qkv[1], mixed[1], part = attend(now(places), x[1], g_attn[1], qkv[0], w_attn[1], each)
     heads[1] = HeadSum(rounds, part)
+    held, rounds.done = rounds.done, (*rounds.done, part[0])
+    moved += move(0)
+    rounds.done = held
     close(*moved, part[0], got)
-    close(*move(0), heads[1].near(), heads[0].last())
+    close(heads[1].near(), heads[0].last())
 
     def grads_of(c, out):
-        columns = [(out[0], out[2]), (out[0], out[3]), (g[c], out[1])]
+        columns = [(out[0], out[2]), (g[c], out[1])]
         return weight_grads(now(places), [columns], far)
 
     dh, mlp, grads, dm, d_gain_ffn = ([None] * 2 for _ in range(5))
     moved = move(1)
     got = heads[1].far()
     out = hidden_units(now(places), x[0], heads[0].sum, g[0], g_ffn[0], weights(0))
-    dh[0], mlp[0] = HeadSum(rounds, out[4]), HeadSum(rounds, out[5])
+    dh[0], mlp[0] = HeadSum(rounds, out[3]), HeadSum(rounds, out[4])
     close(*moved, out[0], got)
     moved = move(1)
     grads[0] = grads_of(0, out)
@@ -840,75 +868,75 @@
     att = [head.sum for head in heads]
     sums = [Scatter(rounds, ring, grads[0])] if rings else []
     add = lambda k: sums[k].step() if rings else ()
-    close(*move(1), mlp[0].far(2))
-    close(*move(1), *add(0), mlp[0].far(2))
+    close(*move(1), mlp[0].far(0.5))
+    close(*move(1), *add(0), mlp[0].far(0.5))
 
     moved = add(0)
     got = dh[0].far()
     out = hidden_units(now(places), x[1], att[1], g[1], g_ffn[1], weights(1))
-    dh[1], mlp[1] = HeadSum(rounds, out[4]), HeadSum(rounds, out[5])
+    dh[1], mlp[1] = HeadSum(rounds, out[3]), HeadSum(rounds, out[4])
     close(*moved, out[0], got)
-    close(dh[1].near(), dh[0].last(), mlp[0].last())
+    close(dh[1].near(), dh[0].last(), mlp[0].last(), mlp[1].near())
     moved = add(0)
     got = dh[1].far()
     grads[1] = grads_of(1, out)
+    if rings:
+        sums.append(Scatter(rounds, ring, grads[1]))
+        moved += add(1)
     dm[0], d_gain_ffn[0] = middle_back(now(places), x[0], att[0], g[0], dh[0].sum, g_ffn[0])
     close(*moved, grads[1][0], dm[0], got)
-    if rings:
-        sums.append(Scatter(rounds, ring, grads[1]))
+
+    close(dh[1].last())
 
     moved = (*add(0), *add(1))
-    dh[1].last()
+    got = mlp[1].far()
     dm[1], d_gain_ffn[1] = middle_back(now(places), x[1], att[1], g[1], dh[1].sum, g_ffn[1])
-    d_qkv, part, d_gain0 = attend_back(now(places), x, dm, qkv, w_attn, 0, None, each)
-    back = [HeadSum(rounds, part)]
-    close(*moved, part[0])
-    close(back[0].near(), mlp[1].near())
+    d_qkv, part, d_gain_attn = attend_back(now(places), x, dm, qkv, w_attn, each)
+    back = [HeadSum(rounds, p) for p in part]
+    close(*moved, part[0][0], got)
+
+    shared = lax.axis_size("mp")
+    d_gains = jnp.concatenate([d_gain_attn, *[d / shared for d in d_gain_ffn]], 0)
+    steps = list(exchange_steps(("mp", "dp")))
+
+    def sum_step(value, *earlier):
+        axis, moves, _ = steps.pop(0)
+        got = lax.ppermute(now(value), axis, moves)
+        return value + lax.optimization_barrier((got, *earlier))[0]
+
     moved = add(1)
-    got = back[0].far()
-    d_qkv, part, d_gain1 = attend_back(now(places), x, dm, qkv, w_attn, 1, d_qkv, each)
-    back.append(HeadSum(rounds, part))
-    close(*moved, part[0], got)
-
-    shared = lax.axis_size("mp")
-    d_gains = jnp.concatenate([d_gain0 + d_gain1, *[d / shared for d in d_gain_ffn]], 0)
-    steps = list(exchange_steps(("mp", "dp")))
-
-    def sum_step(value):
-        axis, moves, _ = steps.pop(0)
-        return value + lax.ppermute(now(value), axis, moves)
-
-    d_gains = sum_step(d_gains)
-    close(back[1].near(), back[0].last(), d_gains)
-    gain = gains[:sets]
-    moved = add(1)
-    got = back[1].far()
-    d_gains = sum_step(d_gains)
+    mlp[1].last()
+    d_gains = sum_step(sum_step(d_gains))
     runs = [[(h1[c], d_qkv[c]), (dm[c], mixed[c])] for c in range(sets)]
     if rings:
         blocks = weight_grads(now(places), runs, far)
         sums.append(Scatter(rounds, ring, blocks))
     else:
         blocks = [weight_grads(now(places), [run], far)[0] for run in runs]
-    grad_input = input_back(now(places), x, dm, back[0].sum, gain, 0, None, shape)
-    close(*moved, blocks[0], grad_input, got, d_gains)
-    close(*add(2), *add(1), mlp[1].far())
+    close(*moved, blocks[0], *[b.near() for b in back], d_gains)
+    moved = (*add(2), *add(1))
+    got = back[0].far()
+    output = output_of(now(places), x, att, [m.sum for m in mlp], shape)
+    close(*moved, got, output)
     moved = add(2)
     d_gains = sum_step(d_gains)
+    got = back[1].far(0.5)
     if rings:
         ffn_sums = [([now(t) for t in s.terms()], 0) for s in sums[:2]]
     else:
         ffn_sums = [([scatter(b[0])], 0) for b in grads]
     d_gate_w, d_up_w, d_down_w = finish(ffn_sums, 3, own)
-    close(*moved, d_gains, d_gate_w, back[1].last(), mlp[1].last())
+    close(*moved, d_gains, d_gate_w, got, back[0].last())
     moved = add(2)
     d_gains = sum_step(d_gains)
-    output = output_of(now(places), x, att, [m.sum for m in mlp], shape)
-    close(*moved, output, d_gains)
+    got = back[1].far(0.5)
+    grad_input = input_back(now(places), x, dm, back[0].sum, gains[:sets], 0, None, shape)
+    close(*moved, grad_input, d_gains, got)
     moved = add(2)
-    grad_input = input_back(now(places), x, dm, back[1].sum, gain, 1, grad_input, shape)
+    back[1].last()
+    grad_input = input_back(now(places), x, dm, back[1].sum, gains[:sets], 1, grad_input, shape)
     while steps:
-        d_gains = sum_step(d_gains)
+        d_gains = sum_step(d_gains, grad_input)
     close(*moved, grad_input, d_gains)
     if rings:
         terms = [now(t) for t in sums[2].terms()]

time: 458 us -> 446 us (0.974)
  Pallas kernels: 200 us -> 189 us
  other arithmetic: 17.4 us -> 26.6 us
  waiting for transfers between devices: 137 us -> 128 us
    ppermute x12, waiting for transfers between devices: 20.7 us -> 9.06 us  [step(): self.a = lax.ppermute(self.rounds.now(self.a), 'dp', self.ring.ahead)]
    pallas_call x19 -> x18, Pallas kernels: 200 us -> 189 us  [kernel_call(): pl.pallas_call(body, grid_spec=spec, out_shape=outs, input_output_aliases...]
    ppermute x12, waiting for transfers between devices: 8.98 us -> 20 us  [step(): self.b = lax.ppermute(self.rounds.now(self.b), 'dp', self.ring.behind)]
    convert_element_type x17 -> x16, other arithmetic: 6.01 us -> 16.3 us  [step(): self.a, self.b = ((one + a).astype(BF), (two + b).astype(BF))]
    ppermute x14 -> x15, waiting for transfers between devices: 37.6 us -> 34.4 us  [the longest x10 19.6 us: far(): self.got.append(lax.ppermute(moved, 'mp', self.far_moves))]
    ppermute x14 -> x15, starting transfers between devices: 15.6 us -> 13.3 us  [the longest x10 9.31 us: far(): self.got.append(lax.ppermute(moved, 'mp', self.far_moves))]
  transfers between devices with their start and end apart: 81 -> 82, of which waited for: 34 -> 34; matrix products, arithmetic and copies ran while one was open for 6% -> 8% of each run, Pallas kernels for 44% -> 42%
where the time goes in v6:
time: 446 us; the launch traced here: 438 us
  Pallas kernels  189 us (42%)
  waiting for transfers between devices  128 us (29%)
  starting transfers between devices  74 us (17%)
  other arithmetic  26.6 us (6%)
  local copies, waits for them, and re-layouts  17.9 us (4%)
    pallas_call x18, Pallas kernels, kernel_call(): pl.pallas_call(body, grid_spec=spec, out_shape=outs, input_output_aliases...  189 us
    ppermute x12, waiting for transfers between devices, step(): self.a.append(lax.ppermute(self.rounds.now(a), 'dp', self.ring.ahead))  42.4 us
    ppermute x12, waiting for transfers between devices, step(): self.b = lax.ppermute(self.rounds.now(self.b), 'dp', self.ring.behind)  20 us
    ppermute x10, waiting for transfers between devices, far(): self.got.append(lax.ppermute(moved, 'mp', self.far_moves))  19.6 us
    convert_element_type x16, other arithmetic, step(): self.a, self.b = ((one + a).astype(BF), (two + b).astype(BF))  16.3 us
    ppermute x5, waiting for transfers between devices, sum_step(): got = lax.ppermute(now(value), axis, moves)  14.8 us
    ppermute x12, starting transfers between devices, step(): self.a = lax.ppermute(self.rounds.now(self.a), 'dp', self.ring.ahead)  14.6 us
    ppermute x12, starting transfers between devices, step(): self.b.append(lax.ppermute(self.rounds.now(b), 'dp', self.ring.behind))  14.5 us
  transfers between devices with their start and end apart: 82, of which 34 were waited for; matrix products, arithmetic and copies ran while one was open for 8% of the time, Pallas kernels for 42%

profile of v6, /device:TPU:0, one launch (start us, length us, event | category | flops | bytes accessed | tf_op | source)
XLA Modules:
  0.0 438.1 jit_solution(5817183374820506180)
XLA Ops:
  0.6 2.0 shard_map.203.refs_2_.refs_3_.refs_0_
  2.7 3.0 collective-permute-start.1
  6.4 2.0 collective-permute-start
  8.3 3.1 slice_bitcast_fusion.3.refs_0_.x_ref.x0
  11.4 2.1 shard_map.204.refs_5_
  13.6 4.2 collective-permute-done
  19.3 1.6 collective-permute-start.4
  22.9 3.3 slice_bitcast_fusion.2.refs_0_.x_ref.x1
  26.2 2.2 shard_map.205.refs_5_
  28.3 4.8 %collective-permute-done.3 = f32[2,4,128]{2,1,0:T(4,128)S(1)} collective-permute-done((f32[2,4,128]{2,1,0:T(4,128)S(1)}, f32[2,4,128]{2,1,0:T(4,128)S(1)}, u32[]{:S(2)}, u32[]{:S(2)}) %collective-permute-start.3) | collective-permute-done | bytes 4128 | tf_op jit(solution)/shard_map/ppermute | solution.py:795
  33.2 2.8 collective-permute-start.6
  36.3 1.7 collective-permute-start.8
  38.4 2.4 slice_bitcast_fusion
  40.9 6.6 %collective-permute-done.7.refs_7_.refs_8_.refs_5_ = bf16[256,1024]{1,0:T(8,128)(2,1)S(1)} collective-permute-done((bf16[256,1024]{1,0:T(8,128)(2,1)S(1)}, bf16[256,1024]{1,0:T(8,128)(2,1)S(1)}, u32[]{:S(2)}, u32[]{:S(2)}) %collective-permute-start.7) | collective-permute-done | bytes 524320 | tf_op jit(solution)/shard_map/ppermute | solution.py:688
  48.4 1.7 collective-permute-start.12
  50.5 1.7 collective-permute-start.10
  52.3 18.1 %collective-permute-done.9.refs_6_.refs_4_ = bf16[128,1024]{1,0:T(8,128)(2,1)S(1)} collective-permute-done((bf16[128,1024]{1,0:T(8,128)(2,1)S(1)}, bf16[128,1024]{1,0:T(8,128)(2,1)S(1)}, u32[]{:S(2)}, u32[]{:S(2)}) %collective-permute-start.9) | collective-permute-done | bytes 262176 | tf_op jit(solution)/shard_map/ppermute | solution.py:688
  71.4 1.7 collective-permute-start.14
  74.4 14.0 %shard_map.206 = (bf16[1024,1024]{1,0:T(8,128)(2,1)}, bf16[1024,768]{1,0:T(8,128)(2,1)}, bf16[1024,256]{1,0:T(8,128)(2,1)}, bf16[512,1024]{1,0:T(8,128)(2,1)}, bf16[512,1024]{1,0:T(8,128)(2,1)}) custom-call(s32[9]{0:T(128)} %pad_add_fusion.places._, bf16[1024,1024]{1,0:T(8,128)(2,1)} %slice_bitcast_fusion.3.refs_0_.x_ref.x0, ...), custom_call_target="tpu_custom_call" | custom-call | flops 1 | bytes 1 | tf_op jit(solution)/shard_map/pallas_call | solution.py:41
  88.5 2.9 collective-permute-done.15
  91.4 1.6 add_convert_fusion.14
  93.4 1.7 collective-permute-start.17
  96.6 13.0 %shard_map.207 = (bf16[1024,1024]{1,0:T(8,128)(2,1)}, bf16[1024,768]{1,0:T(8,128)(2,1)}, bf16[1024,256]{1,0:T(8,128)(2,1)}, bf16[512,1024]{1,0:T(8,128)(2,1)}, bf16[512,1024]{1,0:T(8,128)(2,1)}) custom-call(s32[9]{0:T(128)} %pad_add_fusion.places._, bf16[1024,1024]{1,0:T(8,128)(2,1)} %slice_bitcast_fusion.2.refs_0_.x_ref.x1, ...), custom_call_target="tpu_custom_call" | custom-call | flops 1 | bytes 1 | tf_op jit(solution)/shard_map/pallas_call | solution.py:41
  109.6 3.1 collective-permute-done.16.refs_11_
  113.1 1.8 collective-permute-start.19
  114.8 4.9 %collective-permute-done.20 = bf16[512,1024]{1,0:T(8,128)(2,1)S(1)} collective-permute-done((bf16[512,1024]{1,0:T(8,128)(2,1)S(1)}, bf16[512,1024]{1,0:T(8,128)(2,1)S(1)}, u32[]{:S(2)}, u32[]{:S(2)}) %collective-permute-start.20) | collective-permute-done | bytes 1048608 | tf_op jit(solution)/shard_map/ppermute | solution.py:753
  119.7 3.3 collective-permute-done.18.refs_9_
  124.2 1.9 collective-permute-done.21
  131.2 24.8 %shard_map.208 = (bf16[1024,1024]{1,0:T(8,128)(2,1)}, bf16[1024,1024]{1,0:T(8,128)(2,1)}, bf16[1024,2048]{1,0:T(8,128)(2,1)}, bf16[512,1024]{1,0:T(8,128)(2,1)},...) custom-call(s32[9]{0:T(128)} %pad_add_fusion.places._, ...), custom_call_target="tpu_custom_call" | custom-call | flops 1 | bytes 1 | tf_op jit(solution)/shard_map/pallas_call | solution.py:41
  160.0 13.5 %shard_map.209 = (bf16[128,3072]{1,0:T(8,128)(2,1)}, bf16[128,3072]{1,0:T(8,128)(2,1)}, bf16[128,3072]{1,0:T(8,128)(2,1)}, bf16[128,3072]{1,0:T(8,128)(2,1)}, bf...) custom-call(s32[9]{0:T(128)} %pad_add_fusion.places._, ...), custom_call_target="tpu_custom_call" | custom-call | flops 1 | bytes 1 | tf_op jit(solution)/shard_map/pallas_call | solution.py:41
  175.2 2.7 collective-permute-done.26.refs_12_
  182.0 12.1 %collective-permute-done.33 = bf16[256,1024]{1,0:T(8,128)(2,1)S(1)} collective-permute-done((bf16[256,1024]{1,0:T(8,128)(2,1)S(1)}, bf16[256,1024]{1,0:T(8,128)(2,1)S(1)}, u32[]{:S(2)}, u32[]{:S(2)}) %collective-permute-start.33) | collective-permute-done | bytes 524320 | tf_op jit(solution)/shard_map/ppermute | solution.py:753
  194.1 4.0 collective-permute-done.31.refs_11_
  199.6 1.8 collective-permute-start.34
  203.4 7.3 %collective-permute-done.36 = bf16[64,3072]{1,0:T(8,128)(2,1)S(1)} collective-permute-done((bf16[64,3072]{1,0:T(8,128)(2,1)S(1)}, bf16[64,3072]{1,0:T(8,128)(2,1)S(1)}, u32[]{:S(2)}, u32[]{:S(2)}) %collective-permute-start.36) | collective-permute-done | bytes 393248 | tf_op jit(solution)/shard_map/ppermute | solution.py:726
  211.6 4.6 %collective-permute-done.34.refs_9_ = bf16[64,3072]{1,0:T(8,128)(2,1)S(1)} collective-permute-done((bf16[64,3072]{1,0:T(8,128)(2,1)S(1)}, bf16[64,3072]{1,0:T(8,128)(2,1)S(1)}, u32[]{:S(2)}, u32[]{:S(2)}) %collective-permute-start.34) | collective-permute-done | bytes 393248 | tf_op jit(solution)/shard_map/ppermute | solution.py:688
  216.2 2.3 collective-permute-done.37
  219.9 1.9 collective-permute-start.40
  221.8 24.8 %shard_map.210 = (bf16[1024,1024]{1,0:T(8,128)(2,1)}, bf16[1024,1024]{1,0:T(8,128)(2,1)}, bf16[1024,2048]{1,0:T(8,128)(2,1)}, bf16[512,1024]{1,0:T(8,128)(2,1)},...) custom-call(s32[9]{0:T(128)} %pad_add_fusion.places._, ...), custom_call_target="tpu_custom_call" | custom-call | flops 1 | bytes 1 | tf_op jit(solution)/shard_map/pallas_call | solution.py:41
  250.4 2.0 collective-permute-done.45
  257.6 13.4 %shard_map.211 = (bf16[128,3072]{1,0:T(8,128)(2,1)}, bf16[128,3072]{1,0:T(8,128)(2,1)}, bf16[128,3072]{1,0:T(8,128)(2,1)}, bf16[128,3072]{1,0:T(8,128)(2,1)}, bf...) custom-call(s32[9]{0:T(128)} %pad_add_fusion.places._, ...), custom_call_target="tpu_custom_call" | custom-call | flops 1 | bytes 1 | tf_op jit(solution)/shard_map/pallas_call | solution.py:41
  271.4 1.7 collective-permute-start.46
  273.1 7.3 %shard_map.212 = (bf16[1024,1024]{1,0:T(8,128)(2,1)}, f32[1,1024]{1,0:T(1,128)}) custom-call(s32[9]{0:T(128)} %pad_add_fusion.places._, bf16[1024,1024]{1,0:T(8,128)(2,1)} %slice_bitcast_fusion.3.refs_0_.x_ref.x0, bf16[512,1024]{1,0:T(8,128)(2,1)} %copy-done, bf16[512,1024]{1,0:T(8,128)(2,1)} %copy-done.2, ...), custom_call_target="tpu_custom_call" | custom-call | flops 1 | bytes 1 | tf_op jit(solution)/shard_map/pallas_call | solution.py:41
  280.4 3.2 collective-permute-done.50
  284.2 2.9 add_convert_fusion.18
  287.1 1.7 collective-permute-start.52
  292.5 7.3 %shard_map.213 = (bf16[1024,1024]{1,0:T(8,128)(2,1)}, f32[1,1024]{1,0:T(1,128)}) custom-call(s32[9]{0:T(128)} %pad_add_fusion.places._, bf16[1024,1024]{1,0:T(8,128)(2,1)} %slice_bitcast_fusion.2.refs_0_.x_ref.x1, bf16[512,1024]{1,0:T(8,128)(2,1)} %copy-done.1, bf16[512,1024]{1,0:T(8,128)(2,1)} %copy-done.3, ...), custom_call_target="tpu_custom_call" | custom-call | flops 1 | bytes 1 | tf_op jit(solution)/shard_map/pallas_call | solution.py:41
  299.9 25.7 %shard_map.214 = (bf16[1024,768]{1,0:T(8,128)(2,1)}, bf16[1024,768]{1,0:T(8,128)(2,1)}, bf16[2,256,1024]{2,1,0:T(8,128)(2,1)}, bf16[2,256,1024]{2,1,0:T(8,128)(2...) custom-call(s32[9]{0:T(128)} %pad_add_fusion.places._, ...), custom_call_target="tpu_custom_call" | custom-call | flops 1 | bytes 1 | tf_op jit(solution)/shard_map/pallas_call | solution.py:41
  326.5 2.2 add_convert_fusion.21
  328.7 1.8 collective-permute-start.57
  334.5 11.3 %shard_map.215 = (bf16[256,1024]{1,0:T(8,128)(2,1)}, bf16[256,1024]{1,0:T(8,128)(2,1)}, bf16[256,1024]{1,0:T(8,128)(2,1)}, bf16[256,1024]{1,0:T(8,128)(2,1)}, bf...) custom-call(s32[9]{0:T(128)} %pad_add_fusion.places._, ...), custom_call_target="tpu_custom_call" | custom-call | flops 1 | bytes 1 | tf_op jit(solution)/shard_map/pallas_call | solution.py:41
  353.4 2.2 add_convert_fusion.15
  358.0 1.7 collective-permute-start.64
  359.7 8.5 %shard_map.216 = bf16[128,16,1024]{2,1,0:T(8,128)(2,1)} custom-call(s32[9]{0:T(128)} %pad_add_fusion.places._, bf16[1024,1024]{1,0:T(8,128)(2,1)} %slice_bitcast_fusion.3.refs_0_.x_ref.x0, bf16[1024,1024]{1,0:T(8,128)(2,1)} %slice_bitcast_fusion.2.refs_0_.x_ref.x1, bf16[512,1024]{1,0:T(8,128)(2,1)} %copy-done, bf16[512,1024]{1,0:T(8,128)(2,1)} %copy-done.2, ...), custom_call_target="tpu_custom_call" | custom-call | flops 1 | bytes 1 | tf_op jit(solution)/shard_map/pallas_call | solution.py:41
  368.2 12.9 %collective-permute-done.65 = bf16[128,1024]{1,0:T(8,128)(2,1)} collective-permute-done((bf16[128,1024]{1,0:T(8,128)(2,1)}, bf16[128,1024]{1,0:T(8,128)(2,1)}, u32[]{:S(2)}, u32[]{:S(2)}) %collective-permute-start.65) | collective-permute-done | bytes 262176 | tf_op jit(solution)/shard_map/ppermute | solution.py:727
  381.2 2.0 add_convert_fusion.30
  389.7 4.5 %shard_map.217 = (f32[2,128,1024]{2,1,0:T(8,128)}, f32[2,128,1024]{2,1,0:T(8,128)}, f32[2,1024,128]{2,1,0:T(8,128)}) custom-call(bf16[128,3072]{1,0:T(8,128)(2,1)} %get-tuple-element.322.refs_0_, bf16[128,3072]{1,0:T(8,128)(2,1)} %copy-done.40, bf16[128,3072]{1,0:T(8,128)(2,1)} %copy-done.41, bf16[128,3072]{1,0:T(8,128)(2,1)} %get-tuple-element.325.refs_3_, ...), custom_call_target="tpu_custom_call" | custom-call | flops 1 | bytes 1 | tf_op jit(solution)/shard_map/pallas_call | solution.py:41
  394.2 6.2 %collective-permute-done.71 = f32[4,1024]{1,0:T(4,128)S(1)} collective-permute-done((f32[4,1024]{1,0:T(4,128)S(1)}, f32[4,1024]{1,0:T(4,128)S(1)}, u32[]{:S(2)}, u32[]{:S(2)}) %collective-permute-start.71) | collective-permute-done | bytes 16416 | tf_op jit(solution)/shard_map/ppermute | solution.py:904
  400.9 1.8 collective-permute-done.72
  406.2 6.2 %shard_map.218.refs_0_ = bf16[128,16,1024]{2,1,0:T(8,128)(2,1)} custom-call(s32[9]{0:T(128)} %pad_add_fusion.places._, bf16[1024,1024]{1,0:T(8,128)(2,1)} %slice_bitcast_fusion.3.refs_0_.x_ref.x0, bf16[1024,1024]{1,0:T(8,128)(2,1)} %slice_bitcast_fusion.2.refs_0_.x_ref.x1, bf16[1024,1024]{1,0:T(8,128)(2,1)} %get-tuple-element.270.dm0.refs_2_.refs_3_, ...), custom_call_target="tpu_custom_call" | custom-call | flops 1 | bytes 1 | tf_op jit(solution)/shard_map/pallas_call | solution.py:41
  412.3 3.1 collective-permute-done.76
  422.4 6.2 %shard_map.219 = bf16[128,16,1024]{2,1,0:T(8,128)(2,1)} custom-call(s32[9]{0:T(128)} %pad_add_fusion.places._, bf16[1024,1024]{1,0:T(8,128)(2,1)} %slice_bitcast_fusion.3.refs_0_.x_ref.x0, bf16[1024,1024]{1,0:T(8,128)(2,1)} %slice_bitcast_fusion.2.refs_0_.x_ref.x1, ...), custom_call_target="tpu_custom_call", output_to_operand_aliasing={{}: (8, {})} | custom-call | flops 1 | bytes 1 | tf_op jit(solution)/shard_map/pallas_call | solution.py:41
  428.6 5.5 %collective-permute-done.79 = f32[4,1024]{1,0:T(4,128)S(1)} collective-permute-done((f32[4,1024]{1,0:T(4,128)S(1)}, f32[4,1024]{1,0:T(4,128)S(1)}, u32[]{:S(2)}, u32[]{:S(2)}) %collective-permute-start.79) | collective-permute-done | bytes 16416 | tf_op jit(solution)/shard_map/ppermute | solution.py:904
  435.5 2.4 shard_map.220
  (346 shorter events, 79.1 us)
Async XLA Ops:
  2.7 15.2 %collective-permute-start.1 = (bf16[256,1024]{1,0:T(8,128)(2,1)}, bf16[256,1024]{1,0:T(8,128)(2,1)S(1)}, u32[]{:S(2)}, u32[]{:S(2)}) collective-permute-start(bf16[256,1024]{1,0:T(8,128)(2,1)} %shard_map.203.refs_2_.refs_3_.refs_0_), channel_id=1, source_target_pairs={{0,8},{8,16},{16,24},{24,28},{28,20},{20,12},{12,4},{4,0},{1,9},{9... | collective-permute-start | bytes 1572872 | tf_op jit(solution)/shard_map/ppermute | solution.py:688
  5.7 13.6 %collective-permute-start.2 = (bf16[256,1024]{1,0:T(8,128)(2,1)}, bf16[256,1024]{1,0:T(8,128)(2,1)S(1)}, u32[]{:S(2)}, u32[]{:S(2)}) collective-permute-start(bf16[256,1024]{1,0:T(8,128)(2,1)} %shard_map.203.refs_2_.refs_3_.refs_0_), channel_id=1, source_target_pairs={{8,0},{16,8},{24,16},{28,24},{20,28},{12,20},{4,12},{0,4},{9,1},{1... | collective-permute-start | bytes 1572872 | tf_op jit(solution)/shard_map/ppermute | solution.py:689
  19.3 13.9 %collective-permute-start.4 = (bf16[256,1024]{1,0:T(8,128)(2,1)S(1)}, bf16[256,1024]{1,0:T(8,128)(2,1)S(1)}, u32[]{:S(2)}, u32[]{:S(2)}) collective-permute-start(bf16[256,1024]{1,0:T(8,128)(2,1)S(1)} %collective-permute-done.1.refs_9_.refs_10_.refs_7_), channel_id=1, source_target_pairs={{0,8},{8,16},{16,24},{24,28},{28,20},{20,12},{12,4},{4,0},{1,9},{9... | collective-permute-start | bytes 1572872 | tf_op jit(solution)/shard_map/ppermute | solution.py:688
  20.9 12.3 %collective-permute-start.5 = (bf16[256,1024]{1,0:T(8,128)(2,1)S(1)}, bf16[256,1024]{1,0:T(8,128)(2,1)S(1)}, u32[]{:S(2)}, u32[]{:S(2)}) collective-permute-start(bf16[256,1024]{1,0:T(8,128)(2,1)S(1)} %collective-permute-done.2.refs_3_.refs_4_.refs_1_), channel_id=1, source_target_pairs={{8,0},{16,8},{24,16},{28,24},{20,28},{12,20},{4,12},{0,4},{9,1},{1... | collective-permute-start | bytes 1572872 | tf_op jit(solution)/shard_map/ppermute | solution.py:689
  48.1 23.0 %collective-permute-start.11 = (bf16[128,3072]{1,0:T(8,128)(2,1)S(1)}, bf16[128,3072]{1,0:T(8,128)(2,1)}, u32[]{:S(2)}, u32[]{:S(2)}) collective-permute-start(bf16[128,3072]{1,0:T(8,128)(2,1)S(1)} %copy-done.18), channel_id=1, source_target_pairs={{0,8},{8,16},{16,24},{24,28},{28,20},{20,12},{12,4},{4,0},{1,9},{9... | collective-permute-start | bytes 2359304 | tf_op jit(solution)/shard_map/ppermute | solution.py:688
  48.4 22.7 %collective-permute-start.12 = (bf16[128,3072]{1,0:T(8,128)(2,1)S(1)}, bf16[128,3072]{1,0:T(8,128)(2,1)}, u32[]{:S(2)}, u32[]{:S(2)}) collective-permute-start(bf16[128,3072]{1,0:T(8,128)(2,1)S(1)} %copy-done.18), channel_id=1, source_target_pairs={{8,0},{16,8},{24,16},{28,24},{20,28},{12,20},{4,12},{0,4},{9,1},{1... | collective-permute-start | bytes 2359304 | tf_op jit(solution)/shard_map/ppermute | solution.py:689
  50.1 20.3 %collective-permute-start.9 = (bf16[128,1024]{1,0:T(8,128)(2,1)S(1)}, bf16[128,1024]{1,0:T(8,128)(2,1)S(1)}, u32[]{:S(2)}, u32[]{:S(2)}) collective-permute-start(bf16[128,1024]{1,0:T(8,128)(2,1)S(1)} %slice.107), channel_id=1, source_target_pairs={{0,8},{8,16},{16,24},{24,28},{28,20},{20,12},{12,4},{4,0},{1,9},{9... | collective-permute-start | bytes 786440 | tf_op jit(solution)/shard_map/ppermute | solution.py:688
  50.5 20.5 %collective-permute-start.10 = (bf16[128,1024]{1,0:T(8,128)(2,1)S(1)}, bf16[128,1024]{1,0:T(8,128)(2,1)S(1)}, u32[]{:S(2)}, u32[]{:S(2)}) collective-permute-start(bf16[128,1024]{1,0:T(8,128)(2,1)S(1)} %slice.109), channel_id=1, source_target_pairs={{8,0},{16,8},{24,16},{28,24},{20,28},{12,20},{4,12},{0,4},{9,1},{1... | collective-permute-start | bytes 786440 | tf_op jit(solution)/shard_map/ppermute | solution.py:689
  71.1 17.3 %collective-permute-start.13 = (bf16[128,3072]{1,0:T(8,128)(2,1)}, bf16[128,3072]{1,0:T(8,128)(2,1)S(1)}, u32[]{:S(2)}, u32[]{:S(2)}) collective-permute-start(bf16[128,3072]{1,0:T(8,128)(2,1)} %collective-permute-done.11.refs_13_), channel_id=1, source_target_pairs={{0,8},{8,16},{16,24},{24,28},{28,20},{20,12},{12,4},{4,0},{1,9},{9... | collective-permute-start | bytes 2359304 | tf_op jit(solution)/shard_map/ppermute | solution.py:688
  71.4 17.0 %collective-permute-start.14 = (bf16[128,3072]{1,0:T(8,128)(2,1)}, bf16[128,3072]{1,0:T(8,128)(2,1)S(1)}, u32[]{:S(2)}, u32[]{:S(2)}) collective-permute-start(bf16[128,3072]{1,0:T(8,128)(2,1)} %collective-permute-done.12.refs_6_), channel_id=1, source_target_pairs={{8,0},{16,8},{24,16},{28,24},{20,28},{12,20},{4,12},{0,4},{9,1},{1... | collective-permute-start | bytes 2359304 | tf_op jit(solution)/shard_map/ppermute | solution.py:689
  93.0 19.6 %collective-permute-start.16 = (bf16[128,3072]{1,0:T(8,128)(2,1)S(1)}, bf16[128,3072]{1,0:T(8,128)(2,1)S(1)}, u32[]{:S(2)}, u32[]{:S(2)}) collective-permute-start(bf16[128,3072]{1,0:T(8,128)(2,1)S(1)} %collective-permute-done.13.refs_12_), channel_id=1, source_target_pairs={{0,8},{8,16},{16,24},{24,28},{28,20},{20,12},{12,4},{4,0},{1,9},{9... | collective-permute-start | bytes 2359304 | tf_op jit(solution)/shard_map/ppermute | solution.py:688
  93.4 19.7 %collective-permute-start.17 = (bf16[128,3072]{1,0:T(8,128)(2,1)S(1)}, bf16[128,3072]{1,0:T(8,128)(2,1)S(1)}, u32[]{:S(2)}, u32[]{:S(2)}) collective-permute-start(bf16[128,3072]{1,0:T(8,128)(2,1)S(1)} %collective-permute-done.14.refs_7_), channel_id=1, source_target_pairs={{8,0},{16,8},{24,16},{28,24},{20,28},{12,20},{4,12},{0,4},{9,1},{1... | collective-permute-start | bytes 2359304 | tf_op jit(solution)/shard_map/ppermute | solution.py:689
  95.1 24.6 %collective-permute-start.20 = (bf16[512,1024]{1,0:T(8,128)(2,1)S(1)}, bf16[512,1024]{1,0:T(8,128)(2,1)S(1)}, u32[]{:S(2)}, u32[]{:S(2)}) collective-permute-start(bf16[512,1024]{1,0:T(8,128)(2,1)S(1)} %add_convert_fusion.14), channel_id=1, source_target_pairs={{0,2},{1,3},{2,0},{3,1},{4,6},{5,7},{6,4},{7,5},{8,10},{9,11},{10,... | collective-permute-start | bytes 3145736 | tf_op jit(solution)/shard_map/ppermute | solution.py:753
  127.3 28.6 %collective-permute-start.25 = (bf16[512,1024]{1,0:T(8,128)(2,1)S(1)}, bf16[512,1024]{1,0:T(8,128)(2,1)S(1)}, u32[]{:S(2)}, u32[]{:S(2)}) collective-permute-start(bf16[512,1024]{1,0:T(8,128)(2,1)S(1)} %add_convert_fusion.13), channel_id=1, source_target_pairs={{0,2},{1,3},{2,0},{3,1},{4,6},{5,7},{6,4},{7,5},{8,10},{9,11},{10,... | collective-permute-start | bytes 3145736 | tf_op jit(solution)/shard_map/ppermute | solution.py:753
  128.8 27.1 %collective-permute-start.23 = (bf16[128,3072]{1,0:T(8,128)(2,1)S(1)}, bf16[128,3072]{1,0:T(8,128)(2,1)S(1)}, u32[]{:S(2)}, u32[]{:S(2)}) collective-permute-start(bf16[128,3072]{1,0:T(8,128)(2,1)S(1)} %copy-done.17), channel_id=1, source_target_pairs={{0,8},{8,16},{16,24},{24,28},{28,20},{20,12},{12,4},{4,0},{1,9},{9... | collective-permute-start | bytes 2359304 | tf_op jit(solution)/shard_map/ppermute | solution.py:688
  130.2 25.8 %collective-permute-start.24 = (bf16[128,3072]{1,0:T(8,128)(2,1)S(1)}, bf16[128,3072]{1,0:T(8,128)(2,1)}, u32[]{:S(2)}, u32[]{:S(2)}) collective-permute-start(bf16[128,3072]{1,0:T(8,128)(2,1)S(1)} %copy-done.17), channel_id=1, source_target_pairs={{8,0},{16,8},{24,16},{28,24},{20,28},{12,20},{4,12},{0,4},{9,1},{1... | collective-permute-start | bytes 2359304 | tf_op jit(solution)/shard_map/ppermute | solution.py:689
  156.0 17.6 %collective-permute-start.28 = (bf16[512,1024]{1,0:T(8,128)(2,1)}, bf16[512,1024]{1,0:T(8,128)(2,1)S(1)}, u32[]{:S(2)}, u32[]{:S(2)}) collective-permute-start(bf16[512,1024]{1,0:T(8,128)(2,1)} %get-tuple-element.224), channel_id=1, source_target_pairs={{0,1},{1,0},{2,3},{3,2},{4,5},{5,4},{6,7},{7,6},{8,9},{9,8},{10,11... | collective-permute-start | bytes 3145736 | tf_op jit(solution)/shard_map/ppermute | solution.py:745
  156.8 17.1 %collective-permute-start.29 = (bf16[512,1024]{1,0:T(8,128)(2,1)}, bf16[512,1024]{1,0:T(8,128)(2,1)S(1)}, u32[]{:S(2)}, u32[]{:S(2)}) collective-permute-start(bf16[512,1024]{1,0:T(8,128)(2,1)} %get-tuple-element.227), channel_id=1, source_target_pairs={{0,1},{1,0},{2,3},{3,2},{4,5},{5,4},{6,7},{7,6},{8,9},{9,8},{10,11... | collective-permute-start | bytes 3145736 | tf_op jit(solution)/shard_map/ppermute | solution.py:745
  157.3 22.0 %collective-permute-start.30 = (bf16[512,1024]{1,0:T(8,128)(2,1)S(1)}, bf16[512,1024]{1,0:T(8,128)(2,1)S(1)}, u32[]{:S(2)}, u32[]{:S(2)}) collective-permute-start(bf16[512,1024]{1,0:T(8,128)(2,1)S(1)} %add_convert_fusion.9.refs_1_.att0.refs_4_), channel_id=1, source_target_pairs={{0,1},{1,0},{2,3},{3,2},{4,5},{5,4},{6,7},{7,6},{8,9},{9,8},{10,11... | collective-permute-start | bytes 3145736 | tf_op jit(solution)/shard_map/ppermute | solution.py:759
  158.0 20.0 %collective-permute-start.26 = (bf16[128,3072]{1,0:T(8,128)(2,1)S(1)}, bf16[128,3072]{1,0:T(8,128)(2,1)S(1)}, u32[]{:S(2)}, u32[]{:S(2)}) collective-permute-start(bf16[128,3072]{1,0:T(8,128)(2,1)S(1)} %copy-done.43), channel_id=1, source_target_pairs={{0,8},{8,16},{16,24},{24,28},{28,20},{20,12},{12,4},{4,0},{1,9},{9... | collective-permute-start | bytes 2359304 | tf_op jit(solution)/shard_map/ppermute | solution.py:688
  159.3 20.0 %collective-permute-start.27 = (bf16[128,3072]{1,0:T(8,128)(2,1)}, bf16[128,3072]{1,0:T(8,128)(2,1)}, u32[]{:S(2)}, u32[]{:S(2)}) collective-permute-start(bf16[128,3072]{1,0:T(8,128)(2,1)} %collective-permute-done.24.refs_6_), channel_id=1, source_target_pairs={{8,0},{16,8},{24,16},{28,24},{20,28},{12,20},{4,12},{0,4},{9,1},{1... | collective-permute-start | bytes 2359304 | tf_op jit(solution)/shard_map/ppermute | solution.py:689
  179.3 18.9 %collective-permute-start.31 = (bf16[128,3072]{1,0:T(8,128)(2,1)S(1)}, bf16[128,3072]{1,0:T(8,128)(2,1)S(1)}, u32[]{:S(2)}, u32[]{:S(2)}) collective-permute-start(bf16[128,3072]{1,0:T(8,128)(2,1)S(1)} %collective-permute-done.26.refs_12_), channel_id=1, source_target_pairs={{0,8},{8,16},{16,24},{24,28},{28,20},{20,12},{12,4},{4,0},{1,9},{9... | collective-permute-start | bytes 2359304 | tf_op jit(solution)/shard_map/ppermute | solution.py:688
  179.7 18.8 %collective-permute-start.32 = (bf16[128,3072]{1,0:T(8,128)(2,1)}, bf16[128,3072]{1,0:T(8,128)(2,1)S(1)}, u32[]{:S(2)}, u32[]{:S(2)}) collective-permute-start(bf16[128,3072]{1,0:T(8,128)(2,1)} %collective-permute-done.27.refs_7_), channel_id=1, source_target_pairs={{8,0},{16,8},{24,16},{28,24},{20,28},{12,20},{4,12},{0,4},{9,1},{1... | collective-permute-start | bytes 2359304 | tf_op jit(solution)/shard_map/ppermute | solution.py:689
  181.4 12.7 %collective-permute-start.33 = (bf16[256,1024]{1,0:T(8,128)(2,1)S(1)}, bf16[256,1024]{1,0:T(8,128)(2,1)S(1)}, u32[]{:S(2)}, u32[]{:S(2)}) collective-permute-start(bf16[256,1024]{1,0:T(8,128)(2,1)S(1)} %get-tuple-element.231), channel_id=1, source_target_pairs={{0,2},{1,3},{2,0},{3,1},{4,6},{5,7},{6,4},{7,5},{8,10},{9,11},{10,... | collective-permute-start | bytes 1572872 | tf_op jit(solution)/shard_map/ppermute | solution.py:753
  198.5 12.1 %collective-permute-start.36 = (bf16[64,3072]{1,0:T(8,128)(2,1)S(1)}, bf16[64,3072]{1,0:T(8,128)(2,1)S(1)}, u32[]{:S(2)}, u32[]{:S(2)}) collective-permute-start(bf16[64,3072]{1,0:T(8,128)(2,1)S(1)} %copy-done.81), channel_id=1, source_target_pairs={{0,8},{8,16},{16,24},{24,28},{28,20},{20,12},{12,4},{4,0},{1,9},{9... | collective-permute-start | bytes 1179656 | tf_op jit(solution)/shard_map/ppermute | solution.py:726
  199.6 16.7 %collective-permute-start.34 = (bf16[64,3072]{1,0:T(8,128)(2,1)S(1)}, bf16[64,3072]{1,0:T(8,128)(2,1)S(1)}, u32[]{:S(2)}, u32[]{:S(2)}) collective-permute-start(bf16[64,3072]{1,0:T(8,128)(2,1)S(1)} %slice.116), channel_id=1, source_target_pairs={{0,8},{8,16},{16,24},{24,28},{28,20},{20,12},{12,4},{4,0},{1,9},{9... | collective-permute-start | bytes 1179656 | tf_op jit(solution)/shard_map/ppermute | solution.py:688
  201.4 14.9 %collective-permute-start.35 = (bf16[64,3072]{1,0:T(8,128)(2,1)S(1)}, bf16[64,3072]{1,0:T(8,128)(2,1)S(1)}, u32[]{:S(2)}, u32[]{:S(2)}) collective-permute-start(bf16[64,3072]{1,0:T(8,128)(2,1)S(1)} %slice.118), channel_id=1, source_target_pairs={{8,0},{16,8},{24,16},{28,24},{20,28},{12,20},{4,12},{0,4},{9,1},{1... | collective-permute-start | bytes 1179656 | tf_op jit(solution)/shard_map/ppermute | solution.py:689
  201.7 16.8 %collective-permute-start.37 = (bf16[64,3072]{1,0:T(8,128)(2,1)S(1)}, bf16[64,3072]{1,0:T(8,128)(2,1)S(1)}, u32[]{:S(2)}, u32[]{:S(2)}) collective-permute-start(bf16[64,3072]{1,0:T(8,128)(2,1)S(1)} %copy-done.80), channel_id=1, source_target_pairs={{8,0},{16,8},{24,16},{28,24},{20,28},{12,20},{4,12},{0,4},{9,1},{1... | collective-permute-start | bytes 1179656 | tf_op jit(solution)/shard_map/ppermute | solution.py:727
  202.8 15.7 %collective-permute-start.38 = (bf16[256,1024]{1,0:T(8,128)(2,1)S(1)}, bf16[256,1024]{1,0:T(8,128)(2,1)S(1)}, u32[]{:S(2)}, u32[]{:S(2)}) collective-permute-start(bf16[256,1024]{1,0:T(8,128)(2,1)S(1)} %get-tuple-element.238), channel_id=1, source_target_pairs={{0,2},{1,3},{2,0},{3,1},{4,6},{5,7},{6,4},{7,5},{8,10},{9,11},{10,... | collective-permute-start | bytes 1572872 | tf_op jit(solution)/shard_map/ppermute | solution.py:753
  218.5 28.1 %collective-permute-start.41 = (bf16[512,1024]{1,0:T(8,128)(2,1)S(1)}, bf16[512,1024]{1,0:T(8,128)(2,1)S(1)}, u32[]{:S(2)}, u32[]{:S(2)}) collective-permute-start(bf16[512,1024]{1,0:T(8,128)(2,1)S(1)} %add_convert_fusion.11), channel_id=1, source_target_pairs={{0,2},{1,3},{2,0},{3,1},{4,6},{5,7},{6,4},{7,5},{8,10},{9,11},{10,... | collective-permute-start | bytes 3145736 | tf_op jit(solution)/shard_map/ppermute | solution.py:753
  219.2 27.4 %collective-permute-start.39 = (bf16[128,3072]{1,0:T(8,128)(2,1)}, bf16[128,3072]{1,0:T(8,128)(2,1)S(1)}, u32[]{:S(2)}, u32[]{:S(2)}) collective-permute-start(bf16[128,3072]{1,0:T(8,128)(2,1)} %add_convert_fusion.26), channel_id=1, source_target_pairs={{0,8},{8,16},{16,24},{24,28},{28,20},{20,12},{12,4},{4,0},{1,9},{9... | collective-permute-start | bytes 2359304 | tf_op jit(solution)/shard_map/ppermute | solution.py:726
  219.9 26.7 %collective-permute-start.40 = (bf16[128,3072]{1,0:T(8,128)(2,1)S(1)}, bf16[128,3072]{1,0:T(8,128)(2,1)S(1)}, u32[]{:S(2)}, u32[]{:S(2)}) collective-permute-start(bf16[128,3072]{1,0:T(8,128)(2,1)S(1)} %add_convert_fusion.25), channel_id=1, source_target_pairs={{8,0},{16,8},{24,16},{28,24},{20,28},{12,20},{4,12},{0,4},{9,1},{1... | collective-permute-start | bytes 2359304 | tf_op jit(solution)/shard_map/ppermute | solution.py:727
  253.9 29.8 %collective-permute-start.47 = (bf16[512,1024]{1,0:T(8,128)(2,1)S(1)}, bf16[512,1024]{1,0:T(8,128)(2,1)S(1)}, u32[]{:S(2)}, u32[]{:S(2)}) collective-permute-start(bf16[512,1024]{1,0:T(8,128)(2,1)S(1)} %add_convert_fusion.8), channel_id=1, source_target_pairs={{0,2},{1,3},{2,0},{3,1},{4,6},{5,7},{6,4},{7,5},{8,10},{9,11},{10,... | collective-permute-start | bytes 3145736 | tf_op jit(solution)/shard_map/ppermute | solution.py:753
  255.6 28.1 %collective-permute-start.48 = (bf16[128,3072]{1,0:T(8,128)(2,1)}, bf16[128,3072]{1,0:T(8,128)(2,1)S(1)}, u32[]{:S(2)}, u32[]{:S(2)}) collective-permute-start(bf16[128,3072]{1,0:T(8,128)(2,1)} %add_convert_fusion.23), channel_id=1, source_target_pairs={{0,8},{8,16},{16,24},{24,28},{28,20},{20,12},{12,4},{4,0},{1,9},{9... | collective-permute-start | bytes 2359304 | tf_op jit(solution)/shard_map/ppermute | solution.py:726
  256.2 27.5 %collective-permute-start.49 = (bf16[128,3072]{1,0:T(8,128)(2,1)S(1)}, bf16[128,3072]{1,0:T(8,128)(2,1)S(1)}, u32[]{:S(2)}, u32[]{:S(2)}) collective-permute-start(bf16[128,3072]{1,0:T(8,128)(2,1)S(1)} %add_convert_fusion.22), channel_id=1, source_target_pairs={{8,0},{16,8},{24,16},{28,24},{20,28},{12,20},{4,12},{0,4},{9,1},{1... | collective-permute-start | bytes 2359304 | tf_op jit(solution)/shard_map/ppermute | solution.py:727
  271.0 12.7 %collective-permute-start.50 = (bf16[64,3072]{1,0:T(8,128)(2,1)}, bf16[64,3072]{1,0:T(8,128)(2,1)S(1)}, u32[]{:S(2)}, u32[]{:S(2)}) collective-permute-start(bf16[64,3072]{1,0:T(8,128)(2,1)} %get-tuple-element.268), channel_id=1, source_target_pairs={{8,0},{16,8},{24,16},{28,24},{20,28},{12,20},{4,12},{0,4},{9,1},{1... | collective-permute-start | bytes 1179656 | tf_op jit(solution)/shard_map/ppermute | solution.py:727
  271.4 12.3 %collective-permute-start.46 = (bf16[64,3072]{1,0:T(8,128)(2,1)}, bf16[64,3072]{1,0:T(8,128)(2,1)}, u32[]{:S(2)}, u32[]{:S(2)}) collective-permute-start(bf16[64,3072]{1,0:T(8,128)(2,1)} %get-tuple-element.261), channel_id=1, source_target_pairs={{0,8},{8,16},{16,24},{24,28},{28,20},{20,12},{12,4},{4,0},{1,9},{9... | collective-permute-start | bytes 1179656 | tf_op jit(solution)/shard_map/ppermute | solution.py:726
  287.1 39.3 %collective-permute-start.52 = (bf16[128,3072]{1,0:T(8,128)(2,1)}, bf16[128,3072]{1,0:T(8,128)(2,1)}, u32[]{:S(2)}, u32[]{:S(2)}) collective-permute-start(bf16[128,3072]{1,0:T(8,128)(2,1)} %get-tuple-element.272), channel_id=1, source_target_pairs={{0,8},{8,16},{16,24},{24,28},{28,20},{20,12},{12,4},{4,0},{1,9},{9... | collective-permute-start | bytes 2359304 | tf_op jit(solution)/shard_map/ppermute | solution.py:726
  289.5 39.2 %collective-permute-start.53 = (bf16[128,3072]{1,0:T(8,128)(2,1)S(1)}, bf16[128,3072]{1,0:T(8,128)(2,1)S(1)}, u32[]{:S(2)}, u32[]{:S(2)}) collective-permute-start(bf16[128,3072]{1,0:T(8,128)(2,1)S(1)} %get-tuple-element.274), channel_id=1, source_target_pairs={{0,8},{8,16},{16,24},{24,28},{28,20},{20,12},{12,4},{4,0},{1,9},{9... | collective-permute-start | bytes 2359304 | tf_op jit(solution)/shard_map/ppermute | solution.py:726
  290.5 38.2 %collective-permute-start.54 = (bf16[128,3072]{1,0:T(8,128)(2,1)S(1)}, bf16[128,3072]{1,0:T(8,128)(2,1)S(1)}, u32[]{:S(2)}, u32[]{:S(2)}) collective-permute-start(bf16[128,3072]{1,0:T(8,128)(2,1)S(1)} %get-tuple-element.276), channel_id=1, source_target_pairs={{8,0},{16,8},{24,16},{28,24},{20,28},{12,20},{4,12},{0,4},{9,1},{1... | collective-permute-start | bytes 2359304 | tf_op jit(solution)/shard_map/ppermute | solution.py:727
  291.5 37.2 %collective-permute-start.55 = (bf16[128,3072]{1,0:T(8,128)(2,1)}, bf16[128,3072]{1,0:T(8,128)(2,1)S(1)}, u32[]{:S(2)}, u32[]{:S(2)}) collective-permute-start(bf16[128,3072]{1,0:T(8,128)(2,1)} %get-tuple-element.278), channel_id=1, source_target_pairs={{8,0},{16,8},{24,16},{28,24},{20,28},{12,20},{4,12},{0,4},{9,1},{1... | collective-permute-start | bytes 2359304 | tf_op jit(solution)/shard_map/ppermute | solution.py:727
  292.0 36.8 %collective-permute-start.56 = (bf16[512,1024]{1,0:T(8,128)(2,1)S(1)}, bf16[512,1024]{1,0:T(8,128)(2,1)S(1)}, u32[]{:S(2)}, u32[]{:S(2)}) collective-permute-start(bf16[512,1024]{1,0:T(8,128)(2,1)S(1)} %add_convert_fusion.5), channel_id=1, source_target_pairs={{0,2},{1,3},{2,0},{3,1},{4,6},{5,7},{6,4},{7,5},{8,10},{9,11},{10,... | collective-permute-start | bytes 3145736 | tf_op jit(solution)/shard_map/ppermute | solution.py:753
  328.7 18.6 %collective-permute-start.57 = (bf16[128,3072]{1,0:T(8,128)(2,1)}, bf16[128,3072]{1,0:T(8,128)(2,1)}, u32[]{:S(2)}, u32[]{:S(2)}) collective-permute-start(bf16[128,3072]{1,0:T(8,128)(2,1)} %add_convert_fusion.21), channel_id=1, source_target_pairs={{0,8},{8,16},{16,24},{24,28},{28,20},{20,12},{12,4},{4,0},{1,9},{9... | collective-permute-start | bytes 2359304 | tf_op jit(solution)/shard_map/ppermute | solution.py:726
  331.7 20.3 %collective-permute-start.58 = (bf16[128,3072]{1,0:T(8,128)(2,1)}, bf16[128,3072]{1,0:T(8,128)(2,1)}, u32[]{:S(2)}, u32[]{:S(2)}) collective-permute-start(bf16[128,3072]{1,0:T(8,128)(2,1)} %add_convert_fusion.17), channel_id=1, source_target_pairs={{8,0},{16,8},{24,16},{28,24},{20,28},{12,20},{4,12},{0,4},{9,1},{1... | collective-permute-start | bytes 2359304 | tf_op jit(solution)/shard_map/ppermute | solution.py:727
  331.9 16.8 %collective-permute-start.59 = (bf16[512,1024]{1,0:T(8,128)(2,1)}, bf16[512,1024]{1,0:T(8,128)(2,1)S(1)}, u32[]{:S(2)}, u32[]{:S(2)}) collective-permute-start(bf16[512,1024]{1,0:T(8,128)(2,1)} %bitcast.16), channel_id=1, source_target_pairs={{0,1},{1,0},{2,3},{3,2},{4,5},{5,4},{6,7},{7,6},{8,9},{9,8},{10,11... | collective-permute-start | bytes 3145736 | tf_op jit(solution)/shard_map/ppermute | solution.py:745
  332.2 17.0 %collective-permute-start.60 = (bf16[512,1024]{1,0:T(8,128)(2,1)}, bf16[512,1024]{1,0:T(8,128)(2,1)S(1)}, u32[]{:S(2)}, u32[]{:S(2)}) collective-permute-start(bf16[512,1024]{1,0:T(8,128)(2,1)} %bitcast.18), channel_id=1, source_target_pairs={{0,1},{1,0},{2,3},{3,2},{4,5},{5,4},{6,7},{7,6},{8,9},{9,8},{10,11... | collective-permute-start | bytes 3145736 | tf_op jit(solution)/shard_map/ppermute | solution.py:745
  332.5 13.3 %collective-permute-start.62 = (f32[4,1024]{1,0:T(4,128)S(1)}, f32[4,1024]{1,0:T(4,128)S(1)}, u32[]{:S(2)}, u32[]{:S(2)}) collective-permute-start(f32[4,1024]{1,0:T(4,128)S(1)} %fusion.2), channel_id=1, source_target_pairs={{0,2},{1,3},{2,0},{3,1},{4,6},{5,7},{6,4},{7,5},{8,10},{9,11},{10,... | collective-permute-start | bytes 49160 | tf_op jit(solution)/shard_map/ppermute | solution.py:904
  345.8 12.1 %collective-permute-start.63 = (bf16[512,1024]{1,0:T(8,128)(2,1)S(1)}, bf16[512,1024]{1,0:T(8,128)(2,1)S(1)}, u32[]{:S(2)}, u32[]{:S(2)}) collective-permute-start(bf16[512,1024]{1,0:T(8,128)(2,1)S(1)} %add_convert_fusion.2.refs_6_), channel_id=1, source_target_pairs={{0,1},{1,0},{2,3},{3,2},{4,5},{5,4},{6,7},{7,6},{8,9},{9,8},{10,11... | collective-permute-start | bytes 3145736 | tf_op jit(solution)/shard_map/ppermute | solution.py:759
  351.9 31.2 %collective-permute-start.68 = (bf16[512,1024]{1,0:T(8,128)(2,1)S(1)}, bf16[512,1024]{1,0:T(8,128)(2,1)S(1)}, u32[]{:S(2)}, u32[]{:S(2)}) collective-permute-start(bf16[512,1024]{1,0:T(8,128)(2,1)S(1)} %add_convert_fusion.3), channel_id=1, source_target_pairs={{0,2},{1,3},{2,0},{3,1},{4,6},{5,7},{6,4},{7,5},{8,10},{9,11},{10,... | collective-permute-start | bytes 3145736 | tf_op jit(solution)/shard_map/ppermute | solution.py:753
  355.7 27.5 %collective-permute-start.66 = (bf16[128,3072]{1,0:T(8,128)(2,1)S(1)}, bf16[128,3072]{1,0:T(8,128)(2,1)S(1)}, u32[]{:S(2)}, u32[]{:S(2)}) collective-permute-start(bf16[128,3072]{1,0:T(8,128)(2,1)S(1)} %add_convert_fusion.16), channel_id=1, source_target_pairs={{0,8},{8,16},{16,24},{24,28},{28,20},{20,12},{12,4},{4,0},{1,9},{9... | collective-permute-start | bytes 2359304 | tf_op jit(solution)/shard_map/ppermute | solution.py:726
  356.6 26.5 %collective-permute-start.67 = (bf16[128,3072]{1,0:T(8,128)(2,1)}, bf16[128,3072]{1,0:T(8,128)(2,1)S(1)}, u32[]{:S(2)}, u32[]{:S(2)}) collective-permute-start(bf16[128,3072]{1,0:T(8,128)(2,1)} %add_convert_fusion.15), channel_id=1, source_target_pairs={{8,0},{16,8},{24,16},{28,24},{20,28},{12,20},{4,12},{0,4},{9,1},{1... | collective-permute-start | bytes 2359304 | tf_op jit(solution)/shard_map/ppermute | solution.py:727
  357.7 23.5 %collective-permute-start.65 = (bf16[128,1024]{1,0:T(8,128)(2,1)}, bf16[128,1024]{1,0:T(8,128)(2,1)}, u32[]{:S(2)}, u32[]{:S(2)}) collective-permute-start(bf16[128,1024]{1,0:T(8,128)(2,1)} %get-tuple-element.312), channel_id=1, source_target_pairs={{8,0},{16,8},{24,16},{28,24},{20,28},{12,20},{4,12},{0,4},{9,1},{1... | collective-permute-start | bytes 786440 | tf_op jit(solution)/shard_map/ppermute | solution.py:727
  358.0 25.2 %collective-permute-start.64 = (bf16[128,1024]{1,0:T(8,128)(2,1)}, bf16[128,1024]{1,0:T(8,128)(2,1)S(1)}, u32[]{:S(2)}, u32[]{:S(2)}) collective-permute-start(bf16[128,1024]{1,0:T(8,128)(2,1)} %get-tuple-element.310), channel_id=1, source_target_pairs={{0,8},{8,16},{16,24},{24,28},{28,20},{20,12},{12,4},{4,0},{1,9},{9... | collective-permute-start | bytes 786440 | tf_op jit(solution)/shard_map/ppermute | solution.py:726
  383.9 16.6 %collective-permute-start.70 = (bf16[256,1024]{1,0:T(8,128)(2,1)}, bf16[256,1024]{1,0:T(8,128)(2,1)S(1)}, u32[]{:S(2)}, u32[]{:S(2)}) collective-permute-start(bf16[256,1024]{1,0:T(8,128)(2,1)} %add_convert_fusion.30), channel_id=1, source_target_pairs={{8,0},{16,8},{24,16},{28,24},{20,28},{12,20},{4,12},{0,4},{9,1},{1... | collective-permute-start | bytes 1572872 | tf_op jit(solution)/shard_map/ppermute | solution.py:727
  385.3 17.3 %collective-permute-start.73 = (bf16[512,1024]{1,0:T(8,128)(2,1)S(1)}, bf16[512,1024]{1,0:T(8,128)(2,1)S(1)}, u32[]{:S(2)}, u32[]{:S(2)}) collective-permute-start(bf16[512,1024]{1,0:T(8,128)(2,1)S(1)} %add_convert_fusion.1.mine), channel_id=1, source_target_pairs={{0,1},{1,0},{2,3},{3,2},{4,5},{5,4},{6,7},{7,6},{8,9},{9,8},{10,11... | collective-permute-start | bytes 3145736 | tf_op jit(solution)/shard_map/ppermute | solution.py:759
  386.0 14.7 %collective-permute-start.69 = (bf16[256,1024]{1,0:T(8,128)(2,1)S(1)}, bf16[256,1024]{1,0:T(8,128)(2,1)S(1)}, u32[]{:S(2)}, u32[]{:S(2)}) collective-permute-start(bf16[256,1024]{1,0:T(8,128)(2,1)S(1)} %add_convert_fusion.32), channel_id=1, source_target_pairs={{0,8},{8,16},{16,24},{24,28},{28,20},{20,12},{12,4},{4,0},{1,9},{9... | collective-permute-start | bytes 1572872 | tf_op jit(solution)/shard_map/ppermute | solution.py:726
  387.2 13.2 %collective-permute-start.71 = (f32[4,1024]{1,0:T(4,128)S(1)}, f32[4,1024]{1,0:T(4,128)S(1)}, u32[]{:S(2)}, u32[]{:S(2)}) collective-permute-start(f32[4,1024]{1,0:T(4,128)S(1)} %add.189), channel_id=1, source_target_pairs={{0,4},{4,0},{8,12},{12,8},{16,20},{20,16},{24,28},{28,24},{1,5},{5... | collective-permute-start | bytes 49160 | tf_op jit(solution)/shard_map/ppermute | solution.py:904
  389.1 13.5 %collective-permute-start.72 = (bf16[256,1024]{1,0:T(8,128)(2,1)}, bf16[256,1024]{1,0:T(8,128)(2,1)S(1)}, u32[]{:S(2)}, u32[]{:S(2)}) collective-permute-start(bf16[256,1024]{1,0:T(8,128)(2,1)} %get-tuple-element.329), channel_id=1, source_target_pairs={{0,2},{1,3},{2,0},{3,1},{4,6},{5,7},{6,4},{7,5},{8,10},{9,11},{10,... | collective-permute-start | bytes 1572872 | tf_op jit(solution)/shard_map/ppermute | solution.py:753
  402.7 12.8 %collective-permute-start.75 = (bf16[256,1024]{1,0:T(8,128)(2,1)S(1)}, bf16[256,1024]{1,0:T(8,128)(2,1)S(1)}, u32[]{:S(2)}, u32[]{:S(2)}) collective-permute-start(bf16[256,1024]{1,0:T(8,128)(2,1)S(1)} %add_convert_fusion.29), channel_id=1, source_target_pairs={{8,0},{16,8},{24,16},{28,24},{20,28},{12,20},{4,12},{0,4},{9,1},{1... | collective-permute-start | bytes 1572872 | tf_op jit(solution)/shard_map/ppermute | solution.py:727
  403.6 12.1 %collective-permute-start.74 = (bf16[256,1024]{1,0:T(8,128)(2,1)S(1)}, bf16[256,1024]{1,0:T(8,128)(2,1)S(1)}, u32[]{:S(2)}, u32[]{:S(2)}) collective-permute-start(bf16[256,1024]{1,0:T(8,128)(2,1)S(1)} %add_convert_fusion.31), channel_id=1, source_target_pairs={{0,8},{8,16},{16,24},{24,28},{28,20},{20,12},{12,4},{4,0},{1,9},{9... | collective-permute-start | bytes 1572872 | tf_op jit(solution)/shard_map/ppermute | solution.py:726
  404.7 11.8 %collective-permute-start.77 = (bf16[256,1024]{1,0:T(8,128)(2,1)S(1)}, bf16[256,1024]{1,0:T(8,128)(2,1)S(1)}, u32[]{:S(2)}, u32[]{:S(2)}) collective-permute-start(bf16[256,1024]{1,0:T(8,128)(2,1)S(1)} %get-tuple-element.336), channel_id=1, source_target_pairs={{0,2},{1,3},{2,0},{3,1},{4,6},{5,7},{6,4},{7,5},{8,10},{9,11},{10,... | collective-permute-start | bytes 1572872 | tf_op jit(solution)/shard_map/ppermute | solution.py:753
  418.2 16.4 %collective-permute-start.80 = (bf16[256,1024]{1,0:T(8,128)(2,1)}, bf16[256,1024]{1,0:T(8,128)(2,1)S(1)}, u32[]{:S(2)}, u32[]{:S(2)}) collective-permute-start(bf16[256,1024]{1,0:T(8,128)(2,1)} %add_convert_fusion.28), channel_id=1, source_target_pairs={{0,8},{8,16},{16,24},{24,28},{28,20},{20,12},{12,4},{4,0},{1,9},{9... | collective-permute-start | bytes 1572872 | tf_op jit(solution)/shard_map/ppermute | solution.py:726
  419.2 15.5 %collective-permute-start.81 = (bf16[256,1024]{1,0:T(8,128)(2,1)S(1)}, bf16[256,1024]{1,0:T(8,128)(2,1)}, u32[]{:S(2)}, u32[]{:S(2)}) collective-permute-start(bf16[256,1024]{1,0:T(8,128)(2,1)S(1)} %add_convert_fusion.27), channel_id=1, source_target_pairs={{8,0},{16,8},{24,16},{28,24},{20,28},{12,20},{4,12},{0,4},{9,1},{1... | collective-permute-start | bytes 1572872 | tf_op jit(solution)/shard_map/ppermute | solution.py:727
  420.3 13.8 %collective-permute-start.79 = (f32[4,1024]{1,0:T(4,128)S(1)}, f32[4,1024]{1,0:T(4,128)S(1)}, u32[]{:S(2)}, u32[]{:S(2)}) collective-permute-start(f32[4,1024]{1,0:T(4,128)S(1)} %add.199), channel_id=1, source_target_pairs={{0,16},{4,20},{8,24},{12,28},{16,0},{20,4},{24,8},{28,12},{1,17},{... | collective-permute-start | bytes 49160 | tf_op jit(solution)/shard_map/ppermute | solution.py:904
  (101 other events, 941.4 us)

commit v7 on v6

--- a/solution.py
+++ b/solution.py
@@ -290,12 +290,18 @@
     return *out, part
 
 
-def units_body(pieces, halves, units, places, *refs):
-    x_ref, att0, att1, g_ref, gain_ref, *refs = refs
-    w_refs, refs = refs[: pieces.count], refs[pieces.count :]
-    h_ref, inner_ref, dboth_ref, dh0, dh1, mlp0, mlp1, w_ref, sems = refs
+def units_body(pieces, halves, units, half, filled, places, x_ref, *refs):
+    if half is None:
+        att0, att1, *refs = refs
+        att = halves.pick((att0, att1))
+    else:
+        att_ref, *refs = refs
+        att = att_ref[...]
+    g_ref, gain_ref, *refs = refs
+    w_refs, refs = refs[: pieces.count], refs[pieces.count + filled :]
+    h_ref, inner_ref, dboth_ref, *sum_refs, w_ref, sems = refs
     pieces.start(w_refs, places, w_ref, sems, (2, 0, 1))
-    normed, _ = norm(x_ref[...].astype(F32) + halves.pick((att0, att1)).astype(F32))
+    normed, _ = norm(x_ref[...].astype(F32) + att.astype(F32))
     hidden = (normed * gain_ref[...]).astype(BF)
     h_ref[...] = hidden
     cut = 256
@@ -314,28 +320,40 @@
         inner_ref[:, c[0]] = (active * up).astype(BF)
         dboth_ref[:, c[1]] = (d_inner * active).astype(BF)
         dboth_ref[:, c[0]] = (d_inner * up * (sigma + active * (1.0 - sigma))).astype(BF)
-    halves.put((dh0, dh1), mm(dboth_ref[...], w_ref[:, : 2 * units], NT).astype(BF))
-    halves.put((mlp0, mlp1), mm(inner_ref[...], w_ref[:, 2 * units :], NT).astype(BF))
-
-
-def hidden_units(places, x, att, g, gain, w):
+    d_hidden = mm(dboth_ref[...], w_ref[:, : 2 * units], NT).astype(BF)
+    if half is None:
+        halves.put(sum_refs[:2], d_hidden)
+        halves.put(sum_refs[2:], mm(inner_ref[...], w_ref[:, 2 * units :], NT).astype(BF))
+    else:
+        sum_refs[0][...] = d_hidden
+        sum_refs[1][...] = mm(inner_ref[...], w_ref[:, 2 * units :], NT).astype(BF)
+
+
+def hidden_units(places, x, att, g, gain, w, half=None, filled=()):
     tokens, width = x.shape
     pieces, halves = Pieces(*w, 3), Halves(tokens)
     units = pieces.shape[1] // 3
-    part = halves.both(width)
+    spec = halves.both if half is None else functools.partial(halves.one, half=half)
+    part = spec(width)
     widths = (width, units, 2 * units)
-    *out, dh0, dh1, mlp0, mlp1 = kernel_call(
-        functools.partial(units_body, pieces, halves, units),
-        halves.grid,
-        (x, *att, g, gain, *pieces.arrays),
-        [part, *halves.pair(width), part, whole(gain.shape), *[HBM] * pieces.count],
-        [out_of((tokens, n)) for n in widths] + [out_of((tokens // 2, width))] * 4,
-        [halves.both(n) for n in widths] + halves.pair(width) * 2,
+    sides = [*att, g, gain] if half is None else [att[half], g, gain]
+    side_specs = halves.pair(width) if half is None else [rows_of(ROWS, width)]
+    ins = [x, *sides, *pieces.arrays, *filled]
+    out = kernel_call(
+        functools.partial(units_body, pieces, halves, units, half, len(filled)),
+        halves.grid if half is None else (halves.count,),
+        ins,
+        [part, *side_specs, part, whole(gain.shape)] + [HBM] * (pieces.count + len(filled)),
+        [out_of((tokens, n)) for n in widths] + [out_of((tokens // 2, width))] * (4 if half is None else 2),
+        [spec(n) for n in widths] + (halves.pair(width) * 2 if half is None else [rows_of(ROWS, width)] * 2),
         12 * tokens * width * units,
         pieces.scratch,
         places,
+        {len(ins) - len(filled) + 1 + k: k for k in range(len(filled))},
     )
-    return *out, (dh0, dh1), (mlp0, mlp1)
+    if half is None:
+        return *out[:3], tuple(out[3:5]), tuple(out[5:])
+    return out[:3], *out[3:]
 
 
 def grads_body(runs, cut, steps, places, *refs):
@@ -478,15 +496,18 @@
     )
 
 
-def attend_back_body(pieces, shared, halves, steps, hw, places, x0, x1, dm0, dm1, qkv0, qkv1, *refs):
+def attend_back_body(pieces, shared, steps, hw, places, x0, x1, g1, dm0, att0, att1, dh0, dh1, gain, qkv0, qkv1, *refs):
     sides = [
         [r for a in p.arrays for r, b in zip(refs, shared.arrays) if a is b] for p in pieces
     ]
-    parts = refs[-6 - 2 * halves.count : -6]
-    dqkv0, dqkv1 = refs[-8 - 2 * halves.count : -6 - 2 * halves.count]
-    dgain, w0, sems0, w1, sems1, d_hidden = refs[-6:]
+    dqkv0, dqkv1, dm1, mine, other, dgain, dgain_ffn, w0, sems0, w1, sems1, d_hidden = refs[-12:]
     for p, s, w, sems in zip(pieces, sides, (w0, w1), (sems0, sems1)):
         p.start(s, places, w, sems, range(1))
+    first = pl.program_id(0) == 0
+    value = x1[...].astype(F32) + jnp.where(first, att1[...], att0[...]).astype(F32)
+    back, d_gain = norm_back(jnp.where(first, dh1[...], dh0[...]).astype(F32), value, gain[...])
+    dm1[...] = (g1[...].astype(F32) + back).astype(BF)
+    add_up(dgain_ffn, d_gain)
     normed = [norm(x[...].astype(F32))[0] for x in (x0, x1)]
     for p, s, w, sems in zip(pieces, sides, (w0, w1), (sems0, sems1)):
         p.wait(s, places, w, sems, 0)
@@ -524,7 +545,7 @@
         gains.append(jnp.sum(grad * normed[c], axis=0, keepdims=True))
         d_hidden[c] = grad.astype(BF)
 
-    for k, ref in enumerate(parts):
+    for k, ref in enumerate((other, mine)):
 
         @pl.when(pl.program_id(0) == k)
         def _():
@@ -533,27 +554,34 @@
     add_up(dgain, jnp.concatenate(gains, axis=0))
 
 
-def attend_back(places, x, dm, qkv, w, steps):
-    tokens, width = dm[0].shape
+def attend_back(places, x, g1, dm0, att1, dh1, gain, qkv, w, part, before, steps):
+    tokens, width = dm0.shape
     halves = Halves(tokens)
     pieces = [Pieces(*side, 1) for side in w]
     shared = Pieces(w[0][0] + w[1][0], w[0][1], 1)
     hw = pieces[0].shape[1] // 4
-    flat, thin = halves.both(width), halves.both(3 * hw)
-    part = (2, ROWS, width)
-    d0, d1, *parts, d_gain = kernel_call(
-        functools.partial(attend_back_body, pieces, shared, halves, steps, hw),
-        halves.grid,
-        [*x, *dm, *qkv, *shared.arrays],
-        [flat] * 4 + [thin] * 2 + [HBM] * shared.count,
-        [out_of((tokens, 3 * hw))] * 2 + [out_of(part)] * (2 * halves.count) + [out_of((2, width), F32)],
-        [thin] * 2 + [whole(part)] * (2 * halves.count) + [whole((2, width))],
-        8 * tokens * width * 4 * hw,
-        pieces[0].scratch + pieces[1].scratch + [pltpu.VMEM(part, BF)],
+    spot = lambda i, p: (halves.block(i * halves.count, p) + part, 0)
+    flat, thin = pl.BlockSpec((ROWS, width), spot), pl.BlockSpec((ROWS, 3 * hw), spot)
+    sums = pl.BlockSpec((ROWS, width), lambda i, p: (part, 0))
+    block = (2, ROWS, width)
+    ins = [*x, g1, dm0, *att1, *dh1, gain, *qkv, *shared.arrays, *before]
+    specs = [flat] * 4 + [sums] * 4 + [whole(gain.shape)] + [thin] * 2
+    d0, d1, dm1, mine, other, d_gain, d_gain_ffn = kernel_call(
+        functools.partial(attend_back_body, pieces, shared, steps, hw),
+        (2,),
+        ins,
+        specs + [HBM] * (len(ins) - len(specs)),
+        [out_of((tokens, 3 * hw))] * 2
+        + [out_of((tokens, width))]
+        + [out_of(block)] * 2
+        + [out_of((2, width), F32), out_of((1, width), F32)],
+        [thin] * 2 + [flat] + [whole(block)] * 2 + [whole((2, width)), whole((1, width))],
+        8 * ROWS * width * 4 * hw,
+        pieces[0].scratch + pieces[1].scratch + [pltpu.VMEM(block, BF)],
         places,
+        {len(ins) - len(before) + 1 + k: k for k in range(len(before))},
     )
-    parts = [part.reshape(-1, width) for part in parts]
-    return (d0, d1), list(zip(parts[halves.count :], parts)), d_gain
+    return (d0, d1, dm1), [part.reshape(-1, width) for part in (mine, other)], (d_gain, d_gain_ffn)
 
 
 def store_frames(out_ref, sums):
@@ -650,6 +678,27 @@
     )
 
 
+def add_body(one, a, two, b, one_out, two_out):
+    one_out[...] = (one[...].astype(F32) + a[...].astype(F32)).astype(BF)
+    two_out[...] = (two[...].astype(F32) + b[...].astype(F32)).astype(BF)
+
+
+def add_ends(one, a, two, b):
+    rows, width = a.shape
+    first = pl.BlockSpec((rows, width), lambda i: (0, 0))
+    last = pl.BlockSpec((rows, width), lambda i: (one.shape[0] // rows - 1, 0))
+    return kernel_call(
+        add_body,
+        (1,),
+        (one, a, two, b),
+        [first, first, last, first],
+        [out_of(one.shape)] * 2,
+        [first, last],
+        0,
+        alias={0: 0, 2: 1},
+    )
+
+
 class Ring:
     def __init__(self, size):
         self.size = size
@@ -715,13 +764,12 @@
     def step(self):
         n = self.ring.size
         if self.k < n // 2:
-            one, two = self.blocks[self.k].astype(F32), self.blocks[n - self.k].astype(F32)
-            a, b = self.a.astype(F32), self.b.astype(F32)
+            one, two = self.blocks[self.k], self.blocks[n - self.k]
             if self.k == n // 2 - 1:
-                half = a.shape[0]
-                a = jnp.pad(a, ((0, half), (0, 0)))
-                b = jnp.pad(b, ((half, 0), (0, 0)))
-            self.a, self.b = (one + a).astype(BF), (two + b).astype(BF)
+                self.a, self.b = add_ends(one, self.a, two, self.b)
+            else:
+                self.a = (one.astype(F32) + self.a.astype(F32)).astype(BF)
+                self.b = (two.astype(F32) + self.b.astype(F32)).astype(BF)
         self.k -= 1
         self.a = lax.ppermute(self.rounds.now(self.a), "dp", self.ring.ahead)
         self.b = lax.ppermute(self.rounds.now(self.b), "dp", self.ring.behind)
@@ -741,10 +789,17 @@
     def add(self, one, two):
         return (one.astype(F32) + two.astype(F32)).astype(BF)
 
+    def near_start(self):
+        self.near_got = lax.ppermute(self.rounds.now(self.pair[1]), "mp", self.near_moves)
+        return self.near_got
+
+    def near_add(self, mine):
+        self.mine = self.add(mine, self.near_got)
+        return self.mine
+
     def near(self):
-        got = lax.ppermute(self.rounds.now(self.pair[1]), "mp", self.near_moves)
-        self.mine = self.add(self.pair[0], got)
-        return self.mine
+        self.near_start()
+        return self.near_add(self.pair[0])
 
     def far(self, part=1.0):
         start = sum(got.shape[0] for got in self.got)
@@ -841,8 +896,8 @@
     h1[0], qkv[0], mixed[0], part = attend(now(places), x[0], g_attn[0], None, w_attn[0], each)
     heads[0] = HeadSum(rounds, part)
     close(*moved, part[0])
-    close(heads[0].near())
     moved = move(0)
+    heads[0].near()
     got = heads[0].far()
     h1[1], qkv[1], mixed[1], part = attend(now(places), x[1], g_attn[1], qkv[0], w_attn[1], each)
     heads[1] = HeadSum(rounds, part)
@@ -858,25 +913,42 @@
 
     dh, mlp, grads, dm, d_gain_ffn = ([None] * 2 for _ in range(5))
     moved = move(1)
-    got = heads[1].far()
-    out = hidden_units(now(places), x[0], heads[0].sum, g[0], g_ffn[0], weights(0))
-    dh[0], mlp[0] = HeadSum(rounds, out[3]), HeadSum(rounds, out[4])
-    close(*moved, out[0], got)
+    got = heads[1].far(0.5)
+    ffn = (x[0], heads[0].sum, g[0], g_ffn[0], weights(0))
+    out, dh_other, mlp_other = hidden_units(now(places), *ffn, half=1)
+    close(*moved, dh_other, got)
     moved = move(1)
+    got = heads[1].far(0.5)
+    dh[0] = HeadSum(rounds, (None, dh_other))
+    mlp[0] = HeadSum(rounds, (None, mlp_other))
+    near = dh[0].near_start(), mlp[0].near_start()
+    out, dh_mine, mlp_mine = hidden_units(now(places), *ffn, half=0, filled=out)
+    close(*moved, dh_mine, got, *near)
+    dh[0].near_add(dh_mine)
+    mlp[0].near_add(mlp_mine)
+    moved = move(1)
+    got = dh[0].far(0.5)
     grads[0] = grads_of(0, out)
-    close(*moved, grads[0][0], dh[0].near(), mlp[0].near(), heads[1].last())
+    close(*moved, grads[0][0], got, heads[1].last())
     att = [head.sum for head in heads]
     sums = [Scatter(rounds, ring, grads[0])] if rings else []
     add = lambda k: sums[k].step() if rings else ()
-    close(*move(1), mlp[0].far(0.5))
-    close(*move(1), *add(0), mlp[0].far(0.5))
-
+    close(*move(1), *add(0), dh[0].far(0.5))
+
+    moved = (*add(0), dh[0].last())
+    got = mlp[0].far(0.5)
+    ffn = (x[1], att[1], g[1], g_ffn[1], weights(1))
+    out, dh_other, mlp_other = hidden_units(now(places), *ffn, half=1)
+    close(*moved, dh_other, got)
     moved = add(0)
-    got = dh[0].far()
-    out = hidden_units(now(places), x[1], att[1], g[1], g_ffn[1], weights(1))
-    dh[1], mlp[1] = HeadSum(rounds, out[3]), HeadSum(rounds, out[4])
-    close(*moved, out[0], got)
-    close(dh[1].near(), dh[0].last(), mlp[0].last(), mlp[1].near())
+    got = mlp[0].far(0.5)
+    dh[1] = HeadSum(rounds, (None, dh_other))
+    mlp[1] = HeadSum(rounds, (None, mlp_other))
+    near = dh[1].near_start(), mlp[1].near_start()
+    out, dh_mine, mlp_mine = hidden_units(now(places), *ffn, half=0, filled=out)
+    close(*moved, dh_mine, got, *near)
+    dh[1].near_add(dh_mine)
+    mlp[1].near_add(mlp_mine)
     moved = add(0)
     got = dh[1].far()
     grads[1] = grads_of(1, out)
@@ -885,17 +957,21 @@
         moved += add(1)
     dm[0], d_gain_ffn[0] = middle_back(now(places), x[0], att[0], g[0], dh[0].sum, g_ffn[0])
     close(*moved, grads[1][0], dm[0], got)
-
-    close(dh[1].last())
-
-    moved = (*add(0), *add(1))
-    got = mlp[1].far()
-    dm[1], d_gain_ffn[1] = middle_back(now(places), x[1], att[1], g[1], dh[1].sum, g_ffn[1])
-    d_qkv, part, d_gain_attn = attend_back(now(places), x, dm, qkv, w_attn, each)
-    back = [HeadSum(rounds, p) for p in part]
-    close(*moved, part[0][0], got)
+    close(dh[1].last(), mlp[0].last())
+
+    moved = add(1)
+    got = mlp[1].far(0.75)
+    backward = (x, g[1], dm[0], att[1], dh[1].sum, g_ffn[1], qkv, w_attn)
+    found, part, d_gain0 = attend_back(now(places), *backward, 0, (), each)
+    back = [HeadSum(rounds, part)]
+    close(*moved, part[0], got)
+    moved = (*add(1), back[0].near(), mlp[1].far(0.25))
+    (*d_qkv, dm[1]), part, d_gain1 = attend_back(now(places), *backward, 1, found, each)
+    back.append(HeadSum(rounds, part))
+    close(*moved, part[0])
 
     shared = lax.axis_size("mp")
+    d_gain_attn, d_gain_ffn[1] = (one + two for one, two in zip(d_gain0, d_gain1))
     d_gains = jnp.concatenate([d_gain_attn, *[d / shared for d in d_gain_ffn]], 0)
     steps = list(exchange_steps(("mp", "dp")))
 
@@ -904,8 +980,8 @@
         got = lax.ppermute(now(value), axis, moves)
         return value + lax.optimization_barrier((got, *earlier))[0]
 
-    moved = add(1)
-    mlp[1].last()
+    moved = (*add(1), back[1].near())
+    got = back[0].far(0.75)
     d_gains = sum_step(sum_step(d_gains))
     runs = [[(h1[c], d_qkv[c]), (dm[c], mixed[c])] for c in range(sets)]
     if rings:
@@ -913,31 +989,31 @@
         sums.append(Scatter(rounds, ring, blocks))
     else:
         blocks = [weight_grads(now(places), [run], far)[0] for run in runs]
-    close(*moved, blocks[0], *[b.near() for b in back], d_gains)
-    moved = (*add(2), *add(1))
-    got = back[0].far()
-    output = output_of(now(places), x, att, [m.sum for m in mlp], shape)
-    close(*moved, got, output)
-    moved = add(2)
+    close(*moved, blocks[0], got, d_gains)
+    moved = (*add(2), mlp[1].last())
+    got = back[0].far(0.25)
     d_gains = sum_step(d_gains)
-    got = back[1].far(0.5)
     if rings:
         ffn_sums = [([now(t) for t in s.terms()], 0) for s in sums[:2]]
     else:
         ffn_sums = [([scatter(b[0])], 0) for b in grads]
     d_gate_w, d_up_w, d_down_w = finish(ffn_sums, 3, own)
-    close(*moved, d_gains, d_gate_w, got, back[0].last())
+    close(*moved, d_gains, d_gate_w, got)
+    moved = (*add(2), back[0].last())
+    d_gains = sum_step(d_gains)
+    got = back[1].far(0.5)
+    output = output_of(now(places), x, att, [m.sum for m in mlp], shape)
+    close(*moved, d_gains, got, output)
     moved = add(2)
-    d_gains = sum_step(d_gains)
+    while steps:
+        d_gains = sum_step(d_gains)
     got = back[1].far(0.5)
     grad_input = input_back(now(places), x, dm, back[0].sum, gains[:sets], 0, None, shape)
     close(*moved, grad_input, d_gains, got)
     moved = add(2)
     back[1].last()
     grad_input = input_back(now(places), x, dm, back[1].sum, gains[:sets], 1, grad_input, shape)
-    while steps:
-        d_gains = sum_step(d_gains, grad_input)
-    close(*moved, grad_input, d_gains)
+    close(*moved, grad_input)
     if rings:
         terms = [now(t) for t in sums[2].terms()]
         attn_sums = [(terms, c * own) for c in range(sets)]

time: 446 us -> 430 us (0.964)
  waiting for transfers between devices: 128 us -> 92.3 us
  Pallas kernels: 189 us -> 203 us
  starting transfers between devices: 74 us -> 82.8 us
  other arithmetic: 26.6 us -> 20.4 us
    ppermute x10 -> x14, waiting for transfers between devices: 19.6 us -> 1.79 us  [far(): self.got.append(lax.ppermute(moved, 'mp', self.far_moves))]
    pallas_call x18 -> x23, Pallas kernels: 189 us -> 203 us  [kernel_call(): pl.pallas_call(body, grid_spec=spec, out_shape=outs, input_output_aliases...]
    ppermute x10 -> x14, starting transfers between devices: 9.31 us -> 19.3 us  [far(): self.got.append(lax.ppermute(moved, 'mp', self.far_moves))]
    ppermute x12, waiting for transfers between devices: 20 us -> 10.8 us  [step(): self.b = lax.ppermute(self.rounds.now(self.b), 'dp', self.ring.behind)]
    convert_element_type x16 -> x12, other arithmetic: 16.3 us -> 7.16 us  [the longest x6 4.01 us: step(): self.a = (one.astype(F32) + self.a.astype(F32)).astype(BF)]
    ppermute x5, waiting for transfers between devices: 14.8 us -> 7.68 us  [sum_step(): got = lax.ppermute(now(value), axis, moves)]
    ppermute x12, waiting for transfers between devices: 42.4 us -> 37.4 us  [step(): self.a.append(lax.ppermute(self.rounds.now(a), 'dp', self.ring.ahead))]
  transfers between devices with their start and end apart: 82 -> 86, of which waited for: 34 -> 33; matrix products, arithmetic and copies ran while one was open for 8% -> 7% of each run, Pallas kernels for 42% -> 47%
where the time goes in v7:
time: 430 us; the launch traced here: 422 us
  Pallas kernels  203 us (47%)
  waiting for transfers between devices  92.3 us (21%)
  starting transfers between devices  82.8 us (19%)
  local copies, waits for them, and re-layouts  20.7 us (5%)
  other arithmetic  20.4 us (5%)
    pallas_call x23, Pallas kernels, kernel_call(): pl.pallas_call(body, grid_spec=spec, out_shape=outs, input_output_aliases...  203 us
    ppermute x12, waiting for transfers between devices, step(): self.a.append(lax.ppermute(self.rounds.now(a), 'dp', self.ring.ahead))  37.4 us
    ppermute x14, starting transfers between devices, far(): self.got.append(lax.ppermute(moved, 'mp', self.far_moves))  19.3 us
    ppermute x12, starting transfers between devices, step(): self.b.append(lax.ppermute(self.rounds.now(b), 'dp', self.ring.behind))  16.5 us
    ppermute x12, starting transfers between devices, step(): self.b = lax.ppermute(self.rounds.now(self.b), 'dp', self.ring.behind)  13.8 us
    ppermute x12, waiting for transfers between devices, step(): self.a = lax.ppermute(self.rounds.now(self.a), 'dp', self.ring.ahead)  12.4 us
    ppermute x12, starting transfers between devices, step(): self.a = lax.ppermute(self.rounds.now(self.a), 'dp', self.ring.ahead)  12.1 us
    convert_element_type x16, other arithmetic, add(): return (one.astype(F32) + two.astype(F32)).astype(BF)  11.5 us
  transfers between devices with their start and end apart: 86, of which 33 were waited for; matrix products, arithmetic and copies ran while one was open for 7% of the time, Pallas kernels for 47%

profile of v7, /device:TPU:0, one launch (start us, length us, event | category | flops | bytes accessed | tf_op | source)
XLA Modules:
  0.0 422.0 jit_solution(13601495658888793796)
XLA Ops:
  0.6 2.0 shard_map.203.refs_2_.refs_3_.refs_0_
  2.6 3.0 collective-permute-start.2
  6.3 2.0 collective-permute-start
  8.3 3.1 slice_bitcast_fusion.3.refs_0_.x_ref.x0
  11.4 2.1 shard_map.204.refs_3_
  13.5 5.7 %collective-permute-done = f32[1,4,128]{2,1,0:T(4,128)S(1)} collective-permute-done((f32[1,4,128]{2,1,0:T(4,128)S(1)}, f32[1,4,128]{2,1,0:T(4,128)S(1)}, u32[]{:S(2)}, u32[]{:S(2)}) %collective-permute-start) | collective-permute-done | bytes 2080 | tf_op jit(solution)/shard_map/ppermute | solution.py:850
  19.6 1.8 collective-permute-start.5
  21.6 3.3 slice_bitcast_fusion.2.refs_0_.x_ref.x1
  24.9 2.1 shard_map.205.refs_3_
  27.0 5.2 %collective-permute-done.3 = f32[2,4,128]{2,1,0:T(4,128)S(1)} collective-permute-done((f32[2,4,128]{2,1,0:T(4,128)S(1)}, f32[2,4,128]{2,1,0:T(4,128)S(1)}, u32[]{:S(2)}, u32[]{:S(2)}) %collective-permute-start.3) | collective-permute-done | bytes 4128 | tf_op jit(solution)/shard_map/ppermute | solution.py:850
  32.2 2.7 collective-permute-start.6
  37.4 2.5 slice_bitcast_fusion
  39.8 6.4 %collective-permute-done.7.refs_7_.refs_8_.refs_5_ = bf16[256,1024]{1,0:T(8,128)(2,1)S(1)} collective-permute-done((bf16[256,1024]{1,0:T(8,128)(2,1)S(1)}, bf16[256,1024]{1,0:T(8,128)(2,1)S(1)}, u32[]{:S(2)}, u32[]{:S(2)}) %collective-permute-start.7) | collective-permute-done | bytes 524320 | tf_op jit(solution)/shard_map/ppermute | solution.py:737
  46.2 2.1 collective-permute-done.8.refs_5_.refs_6_.refs_3_
  50.4 2.0 collective-permute-start.11
  52.5 18.2 %collective-permute-done.10.refs_6_.refs_4_ = bf16[128,1024]{1,0:T(8,128)(2,1)S(1)} collective-permute-done((bf16[128,1024]{1,0:T(8,128)(2,1)S(1)}, bf16[128,1024]{1,0:T(8,128)(2,1)S(1)}, u32[]{:S(2)}, u32[]{:S(2)}) %collective-permute-start.10) | collective-permute-done | bytes 262176 | tf_op jit(solution)/shard_map/ppermute | solution.py:737
  74.4 14.0 %shard_map.206 = (bf16[1024,1024]{1,0:T(8,128)(2,1)}, bf16[1024,768]{1,0:T(8,128)(2,1)}, bf16[1024,256]{1,0:T(8,128)(2,1)}, bf16[512,1024]{1,0:T(8,128)(2,1)}, bf16[512,1024]{1,0:T(8,128)(2,1)}) custom-call(s32[9]{0:T(128)} %pad_add_fusion.places._, bf16[1024,1024]{1,0:T(8,128)(2,1)} %slice_bitcast_fusion.3.refs_0_.x_ref.x0, ...), custom_call_target="tpu_custom_call" | custom-call | flops 1 | bytes 1 | tf_op jit(solution)/shard_map/pallas_call | solution.py:41
  91.5 1.6 add_convert_fusion.15
  93.1 1.6 collective-permute-start.20
  94.6 13.0 %shard_map.207 = (bf16[1024,1024]{1,0:T(8,128)(2,1)}, bf16[1024,768]{1,0:T(8,128)(2,1)}, bf16[1024,256]{1,0:T(8,128)(2,1)}, bf16[512,1024]{1,0:T(8,128)(2,1)}, bf16[512,1024]{1,0:T(8,128)(2,1)}) custom-call(s32[9]{0:T(128)} %pad_add_fusion.places._, bf16[1024,1024]{1,0:T(8,128)(2,1)} %slice_bitcast_fusion.2.refs_0_.x_ref.x1, ...), custom_call_target="tpu_custom_call" | custom-call | flops 1 | bytes 1 | tf_op jit(solution)/shard_map/pallas_call | solution.py:41
  111.2 8.3 %collective-permute-done.17.refs_7_ = bf16[64,3072]{1,0:T(8,128)(2,1)S(1)} collective-permute-done((bf16[64,3072]{1,0:T(8,128)(2,1)S(1)}, bf16[64,3072]{1,0:T(8,128)(2,1)S(1)}, u32[]{:S(2)}, u32[]{:S(2)}) %collective-permute-start.17) | collective-permute-done | bytes 393248 | tf_op jit(solution)/shard_map/ppermute | solution.py:737
  121.0 1.9 collective-permute-done.21
  126.5 1.6 collective-permute-start.25
  128.0 13.9 %shard_map.208 = (bf16[1024,1024]{1,0:T(8,128)(2,1)}, bf16[1024,1024]{1,0:T(8,128)(2,1)}, bf16[1024,2048]{1,0:T(8,128)(2,1)}, bf16[512,1024]{1,0:T(8,128)(2,1)}, bf16[512,1024]{1,0:T(8,128)(2,1)}) custom-call(s32[9]{0:T(128)} %pad_add_fusion.places._, bf16[1024,1024]{1,0:T(8,128)(2,1)} %slice_bitcast_fusion.3.refs_0_.x_ref.x0, bf16[512,1024]{1,0:T(8,128)(2,1)} %copy-done.6, ...), custom_call_target="tpu_custom_call" | custom-call | flops 1 | bytes 1 | tf_op jit(solution)/shard_map/pallas_call | solution.py:41
  141.9 1.8 collective-permute-done.24.refs_4_
  149.0 13.8 %shard_map.209 = (bf16[1024,1024]{1,0:T(8,128)(2,1)}, bf16[1024,1024]{1,0:T(8,128)(2,1)}, bf16[1024,2048]{1,0:T(8,128)(2,1)}, bf16[512,1024]{1,0:T(8,128)(2,1)}, bf16[512,1024]{1,0:T(8,128)(2,1)}) custom-call(s32[9]{0:T(128)} %pad_add_fusion.places._, ...), custom_call_target="tpu_custom_call", output_to_operand_aliasing={{0}: (14, {}), {1}: (15, {}), {2}: (16, {})} | custom-call | flops 1 | bytes 1 | tf_op jit(solution)/shard_map/pallas_call | solution.py:41
  162.9 2.0 collective-permute-done.26.refs_10_
  172.4 13.3 %shard_map.210 = (bf16[128,3072]{1,0:T(8,128)(2,1)}, bf16[128,3072]{1,0:T(8,128)(2,1)}, bf16[128,3072]{1,0:T(8,128)(2,1)}, bf16[128,3072]{1,0:T(8,128)(2,1)}, bf...) custom-call(s32[9]{0:T(128)} %pad_add_fusion.places._, ...), custom_call_target="tpu_custom_call" | custom-call | flops 1 | bytes 1 | tf_op jit(solution)/shard_map/pallas_call | solution.py:41
  187.3 1.8 collective-permute-start.35
  189.4 1.7 collective-permute-start.37
  191.8 7.8 %collective-permute-done.35.a = bf16[64,3072]{1,0:T(8,128)(2,1)S(1)} collective-permute-done((bf16[64,3072]{1,0:T(8,128)(2,1)}, bf16[64,3072]{1,0:T(8,128)(2,1)S(1)}, u32[]{:S(2)}, u32[]{:S(2)}) %collective-permute-start.35) | collective-permute-done | bytes 393248 | tf_op jit(solution)/shard_map/ppermute | solution.py:774
  199.6 1.7 collective-permute-done.36.b
  202.1 2.3 shard_map.211
  206.8 1.7 collective-permute-start.40
  213.3 14.0 %shard_map.212 = (bf16[1024,1024]{1,0:T(8,128)(2,1)}, bf16[1024,1024]{1,0:T(8,128)(2,1)}, bf16[1024,2048]{1,0:T(8,128)(2,1)}, bf16[512,1024]{1,0:T(8,128)(2,1)}, bf16[512,1024]{1,0:T(8,128)(2,1)}) custom-call(s32[9]{0:T(128)} %pad_add_fusion.places._, bf16[1024,1024]{1,0:T(8,128)(2,1)} %slice_bitcast_fusion.2.refs_0_.x_ref.x1, bf16[512,1024]{1,0:T(8,128)(2,1)} %copy-done.2, ...), custom_call_target="tpu_custom_call" | custom-call | flops 1 | bytes 1 | tf_op jit(solution)/shard_map/pallas_call | solution.py:41
  227.6 2.0 collective-permute-done.41
  232.8 1.6 collective-permute-start.46
  235.0 14.0 %shard_map.213 = (bf16[1024,1024]{1,0:T(8,128)(2,1)}, bf16[1024,1024]{1,0:T(8,128)(2,1)}, bf16[1024,2048]{1,0:T(8,128)(2,1)}, bf16[512,1024]{1,0:T(8,128)(2,1)}, bf16[512,1024]{1,0:T(8,128)(2,1)}) custom-call(s32[9]{0:T(128)} %pad_add_fusion.places._, ...), custom_call_target="tpu_custom_call", output_to_operand_aliasing={{0}: (14, {}), {1}: (15, {}), {2}: (16, {})} | custom-call | flops 1 | bytes 1 | tf_op jit(solution)/shard_map/pallas_call | solution.py:41
  250.9 2.6 collective-permute-done.45
  256.5 13.3 %shard_map.214 = (bf16[128,3072]{1,0:T(8,128)(2,1)}, bf16[128,3072]{1,0:T(8,128)(2,1)}, bf16[128,3072]{1,0:T(8,128)(2,1)}, bf16[128,3072]{1,0:T(8,128)(2,1)}, bf...) custom-call(s32[9]{0:T(128)} %pad_add_fusion.places._, ...), custom_call_target="tpu_custom_call" | custom-call | flops 1 | bytes 1 | tf_op jit(solution)/shard_map/pallas_call | solution.py:41
  272.0 7.3 %shard_map.216 = (bf16[1024,1024]{1,0:T(8,128)(2,1)}, f32[1,1024]{1,0:T(1,128)}) custom-call(s32[9]{0:T(128)} %pad_add_fusion.places._, bf16[1024,1024]{1,0:T(8,128)(2,1)} %slice_bitcast_fusion.3.refs_0_.x_ref.x0, bf16[512,1024]{1,0:T(8,128)(2,1)} %copy-done.1, bf16[512,1024]{1,0:T(8,128)(2,1)} %copy-done.6, ...), custom_call_target="tpu_custom_call" | custom-call | flops 1 | bytes 1 | tf_op jit(solution)/shard_map/pallas_call | solution.py:41
  279.3 2.1 collective-permute-done.50.b
  283.0 1.9 add_convert_fusion.6.refs_2_
  285.1 2.6 shard_map.215
  292.4 17.2 %shard_map.217 = (bf16[1024,768]{1,0:T(8,128)(2,1)}, bf16[1024,768]{1,0:T(8,128)(2,1)}, bf16[1024,1024]{1,0:T(8,128)(2,1)}, bf16[2,256,1024]{2,1,0:T(8,128)(2,1)...) custom-call(s32[9]{0:T(128)} %pad_add_fusion.places._, ...), custom_call_target="tpu_custom_call" | custom-call | flops 1 | bytes 1 | tf_op jit(solution)/shard_map/pallas_call | solution.py:41
  311.3 1.6 collective-permute-start.62
  314.3 17.2 %shard_map.218 = (bf16[1024,768]{1,0:T(8,128)(2,1)}, bf16[1024,768]{1,0:T(8,128)(2,1)}, bf16[1024,1024]{1,0:T(8,128)(2,1)}, bf16[2,256,1024]{2,1,0:T(8,128)(2,1)...) custom-call(s32[9]{0:T(128)} %pad_add_fusion.places._, ...), custom_call_target="tpu_custom_call", output_to_operand_aliasing={{0}: (21, {}), {1}: (22, {}), {2}: (23, {})} | custom-call | flops 1 | bytes 1 | tf_op jit(solution)/shard_map/pallas_call | solution.py:41
  338.9 1.6 collective-permute-start.68
  340.5 11.3 %shard_map.219 = (bf16[256,1024]{1,0:T(8,128)(2,1)}, bf16[256,1024]{1,0:T(8,128)(2,1)}, bf16[256,1024]{1,0:T(8,128)(2,1)}, bf16[256,1024]{1,0:T(8,128)(2,1)}, bf...) custom-call(s32[9]{0:T(128)} %pad_add_fusion.places._, ...), custom_call_target="tpu_custom_call" | custom-call | flops 1 | bytes 1 | tf_op jit(solution)/shard_map/pallas_call | solution.py:41
  351.8 3.2 collective-permute-done.68
  361.0 4.5 %shard_map.220 = (f32[2,128,1024]{2,1,0:T(8,128)}, f32[2,128,1024]{2,1,0:T(8,128)}, f32[2,1024,128]{2,1,0:T(8,128)}) custom-call(bf16[128,3072]{1,0:T(8,128)(2,1)} %get-tuple-element.367.refs_0_, bf16[128,3072]{1,0:T(8,128)(2,1)} %copy-done.50, bf16[128,3072]{1,0:T(8,128)(2,1)} %copy-done.51, bf16[128,3072]{1,0:T(8,128)(2,1)} %get-tuple-element.370.refs_3_, ...), custom_call_target="tpu_custom_call" | custom-call | flops 1 | bytes 1 | tf_op jit(solution)/shard_map/pallas_call | solution.py:41
  366.4 2.0 shard_map.222
  369.6 1.5 add_convert_fusion.1.mine
  371.9 2.0 collective-permute-start.75
  374.0 1.6 collective-permute-start.78
  375.6 8.4 %shard_map.221 = bf16[128,16,1024]{2,1,0:T(8,128)(2,1)} custom-call(s32[9]{0:T(128)} %pad_add_fusion.places._, bf16[1024,1024]{1,0:T(8,128)(2,1)} %slice_bitcast_fusion.3.refs_0_.x_ref.x0, bf16[1024,1024]{1,0:T(8,128)(2,1)} %slice_bitcast_fusion.2.refs_0_.x_ref.x1, bf16[512,1024]{1,0:T(8,128)(2,1)} %copy-done.1, bf16[512,1024]{1,0:T(8,128)(2,1)} %copy-done.6, ...), custom_call_target="tpu_custom_call" | custom-call | flops 1 | bytes 1 | tf_op jit(solution)/shard_map/pallas_call | solution.py:41
  384.2 2.0 collective-permute-done.75
  388.1 1.8 collective-permute-start.80
  389.8 1.5 collective-permute-start.82
  392.6 6.2 %shard_map.223.refs_0_ = bf16[128,16,1024]{2,1,0:T(8,128)(2,1)} custom-call(s32[9]{0:T(128)} %pad_add_fusion.places._, bf16[1024,1024]{1,0:T(8,128)(2,1)} %slice_bitcast_fusion.3.refs_0_.x_ref.x0, bf16[1024,1024]{1,0:T(8,128)(2,1)} %slice_bitcast_fusion.2.refs_0_.x_ref.x1, bf16[1024,1024]{1,0:T(8,128)(2,1)} %get-tuple-element.314.dm0.refs_2_.refs_3_, ...), custom_call_target="tpu_custom_call" | custom-call | flops 1 | bytes 1 | tf_op jit(solution)/shard_map/pallas_call | solution.py:41
  398.7 3.3 collective-permute-done.81
  407.7 6.2 %shard_map.224 = bf16[128,16,1024]{2,1,0:T(8,128)(2,1)} custom-call(s32[9]{0:T(128)} %pad_add_fusion.places._, bf16[1024,1024]{1,0:T(8,128)(2,1)} %slice_bitcast_fusion.3.refs_0_.x_ref.x0, bf16[1024,1024]{1,0:T(8,128)(2,1)} %slice_bitcast_fusion.2.refs_0_.x_ref.x1, ...), custom_call_target="tpu_custom_call", output_to_operand_aliasing={{}: (8, {})} | custom-call | flops 1 | bytes 1 | tf_op jit(solution)/shard_map/pallas_call | solution.py:41
  413.8 4.5 %collective-permute-done.84.refs_1_ = bf16[256,1024]{1,0:T(8,128)(2,1)S(1)} collective-permute-done((bf16[256,1024]{1,0:T(8,128)(2,1)}, bf16[256,1024]{1,0:T(8,128)(2,1)S(1)}, u32[]{:S(2)}, u32[]{:S(2)}) %collective-permute-start.84) | collective-permute-done | bytes 524320 | tf_op jit(solution)/shard_map/ppermute | solution.py:774
  419.1 2.4 shard_map.225
  (371 shorter events, 90.2 us)
Async XLA Ops:
  2.6 16.6 %collective-permute-start.2 = (bf16[256,1024]{1,0:T(8,128)(2,1)}, bf16[256,1024]{1,0:T(8,128)(2,1)S(1)}, u32[]{:S(2)}, u32[]{:S(2)}) collective-permute-start(bf16[256,1024]{1,0:T(8,128)(2,1)} %shard_map.203.refs_2_.refs_3_.refs_0_), channel_id=1, source_target_pairs={{8,0},{16,8},{24,16},{28,24},{20,28},{12,20},{4,12},{0,4},{9,1},{1... | collective-permute-start | bytes 1572872 | tf_op jit(solution)/shard_map/ppermute | solution.py:738
  5.6 13.7 %collective-permute-start.1 = (bf16[256,1024]{1,0:T(8,128)(2,1)}, bf16[256,1024]{1,0:T(8,128)(2,1)S(1)}, u32[]{:S(2)}, u32[]{:S(2)}) collective-permute-start(bf16[256,1024]{1,0:T(8,128)(2,1)} %shard_map.203.refs_2_.refs_3_.refs_0_), channel_id=1, source_target_pairs={{0,8},{8,16},{16,24},{24,28},{28,20},{20,12},{12,4},{4,0},{1,9},{9... | collective-permute-start | bytes 1572872 | tf_op jit(solution)/shard_map/ppermute | solution.py:737
  6.3 12.9 %collective-permute-start = (f32[1,4,128]{2,1,0:T(4,128)S(1)}, f32[1,4,128]{2,1,0:T(4,128)S(1)}, u32[]{:S(2)}, u32[]{:S(2)}) collective-permute-start(f32[1,4,128]{2,1,0:T(4,128)S(1)} %maximum_convert_fusion), channel_id=1, source_target_pairs={{0,4},{4,0},{8,12},{12,8},{16,20},{20,16},{24,28},{28,24},{1,5},{5... | collective-permute-start | bytes 6152 | tf_op jit(solution)/shard_map/ppermute | solution.py:850
  19.3 12.9 %collective-permute-start.4 = (bf16[256,1024]{1,0:T(8,128)(2,1)S(1)}, bf16[256,1024]{1,0:T(8,128)(2,1)S(1)}, u32[]{:S(2)}, u32[]{:S(2)}) collective-permute-start(bf16[256,1024]{1,0:T(8,128)(2,1)S(1)} %collective-permute-done.1.refs_9_.refs_10_.refs_7_), channel_id=1, source_target_pairs={{0,8},{8,16},{16,24},{24,28},{28,20},{20,12},{12,4},{4,0},{1,9},{9... | collective-permute-start | bytes 1572872 | tf_op jit(solution)/shard_map/ppermute | solution.py:737
  19.6 12.6 %collective-permute-start.5 = (bf16[256,1024]{1,0:T(8,128)(2,1)S(1)}, bf16[256,1024]{1,0:T(8,128)(2,1)S(1)}, u32[]{:S(2)}, u32[]{:S(2)}) collective-permute-start(bf16[256,1024]{1,0:T(8,128)(2,1)S(1)} %collective-permute-done.2.refs_3_.refs_4_.refs_1_), channel_id=1, source_target_pairs={{8,0},{16,8},{24,16},{28,24},{20,28},{12,20},{4,12},{0,4},{9,1},{1... | collective-permute-start | bytes 1572872 | tf_op jit(solution)/shard_map/ppermute | solution.py:738
  48.3 22.8 %collective-permute-start.12 = (bf16[128,3072]{1,0:T(8,128)(2,1)S(1)}, bf16[128,3072]{1,0:T(8,128)(2,1)S(1)}, u32[]{:S(2)}, u32[]{:S(2)}) collective-permute-start(bf16[128,3072]{1,0:T(8,128)(2,1)S(1)} %copy-done.12), channel_id=1, source_target_pairs={{8,0},{16,8},{24,16},{28,24},{20,28},{12,20},{4,12},{0,4},{9,1},{1... | collective-permute-start | bytes 2359304 | tf_op jit(solution)/shard_map/ppermute | solution.py:738
  49.1 22.0 %collective-permute-start.9 = (bf16[128,3072]{1,0:T(8,128)(2,1)S(1)}, bf16[128,3072]{1,0:T(8,128)(2,1)S(1)}, u32[]{:S(2)}, u32[]{:S(2)}) collective-permute-start(bf16[128,3072]{1,0:T(8,128)(2,1)S(1)} %copy-done.12), channel_id=1, source_target_pairs={{0,8},{8,16},{16,24},{24,28},{28,20},{20,12},{12,4},{4,0},{1,9},{9... | collective-permute-start | bytes 2359304 | tf_op jit(solution)/shard_map/ppermute | solution.py:737
  50.4 20.2 %collective-permute-start.10 = (bf16[128,1024]{1,0:T(8,128)(2,1)S(1)}, bf16[128,1024]{1,0:T(8,128)(2,1)S(1)}, u32[]{:S(2)}, u32[]{:S(2)}) collective-permute-start(bf16[128,1024]{1,0:T(8,128)(2,1)S(1)} %slice.140), channel_id=1, source_target_pairs={{0,8},{8,16},{16,24},{24,28},{28,20},{20,12},{12,4},{4,0},{1,9},{9... | collective-permute-start | bytes 786440 | tf_op jit(solution)/shard_map/ppermute | solution.py:737
  50.4 20.6 %collective-permute-start.11 = (bf16[128,1024]{1,0:T(8,128)(2,1)S(1)}, bf16[128,1024]{1,0:T(8,128)(2,1)S(1)}, u32[]{:S(2)}, u32[]{:S(2)}) collective-permute-start(bf16[128,1024]{1,0:T(8,128)(2,1)S(1)} %slice.141), channel_id=1, source_target_pairs={{8,0},{16,8},{24,16},{28,24},{20,28},{12,20},{4,12},{0,4},{9,1},{1... | collective-permute-start | bytes 786440 | tf_op jit(solution)/shard_map/ppermute | solution.py:738
  71.1 17.4 %collective-permute-start.13 = (bf16[128,3072]{1,0:T(8,128)(2,1)S(1)}, bf16[128,3072]{1,0:T(8,128)(2,1)}, u32[]{:S(2)}, u32[]{:S(2)}) collective-permute-start(bf16[128,3072]{1,0:T(8,128)(2,1)S(1)} %collective-permute-done.9.refs_11_), channel_id=1, source_target_pairs={{0,8},{8,16},{16,24},{24,28},{28,20},{20,12},{12,4},{4,0},{1,9},{9... | collective-permute-start | bytes 2359304 | tf_op jit(solution)/shard_map/ppermute | solution.py:737
  71.7 16.8 %collective-permute-start.14 = (bf16[128,3072]{1,0:T(8,128)(2,1)S(1)}, bf16[128,3072]{1,0:T(8,128)(2,1)}, u32[]{:S(2)}, u32[]{:S(2)}) collective-permute-start(bf16[128,3072]{1,0:T(8,128)(2,1)S(1)} %collective-permute-done.12.refs_4_), channel_id=1, source_target_pairs={{8,0},{16,8},{24,16},{28,24},{20,28},{12,20},{4,12},{0,4},{9,1},{1... | collective-permute-start | bytes 2359304 | tf_op jit(solution)/shard_map/ppermute | solution.py:738
  88.6 20.5 %collective-permute-start.15 = (bf16[128,3072]{1,0:T(8,128)(2,1)}, bf16[128,3072]{1,0:T(8,128)(2,1)S(1)}, u32[]{:S(2)}, u32[]{:S(2)}) collective-permute-start(bf16[128,3072]{1,0:T(8,128)(2,1)} %collective-permute-done.13.refs_10_), channel_id=1, source_target_pairs={{0,8},{8,16},{16,24},{24,28},{28,20},{20,12},{12,4},{4,0},{1,9},{9... | collective-permute-start | bytes 2359304 | tf_op jit(solution)/shard_map/ppermute | solution.py:737
  89.2 19.8 %collective-permute-start.16 = (bf16[128,3072]{1,0:T(8,128)(2,1)}, bf16[128,3072]{1,0:T(8,128)(2,1)S(1)}, u32[]{:S(2)}, u32[]{:S(2)}) collective-permute-start(bf16[128,3072]{1,0:T(8,128)(2,1)} %collective-permute-done.14.refs_5_), channel_id=1, source_target_pairs={{8,0},{16,8},{24,16},{28,24},{20,28},{12,20},{4,12},{0,4},{9,1},{1... | collective-permute-start | bytes 2359304 | tf_op jit(solution)/shard_map/ppermute | solution.py:738
  93.1 26.9 %collective-permute-start.20 = (bf16[512,1024]{1,0:T(8,128)(2,1)S(1)}, bf16[512,1024]{1,0:T(8,128)(2,1)S(1)}, u32[]{:S(2)}, u32[]{:S(2)}) collective-permute-start(bf16[512,1024]{1,0:T(8,128)(2,1)S(1)} %add_convert_fusion.15), channel_id=1, source_target_pairs={{0,2},{1,3},{2,0},{3,1},{4,6},{5,7},{6,4},{7,5},{8,10},{9,11},{10,... | collective-permute-start | bytes 3145736 | tf_op jit(solution)/shard_map/ppermute | solution.py:808
  124.2 19.6 %collective-permute-start.24 = (bf16[128,3072]{1,0:T(8,128)(2,1)S(1)}, bf16[128,3072]{1,0:T(8,128)(2,1)S(1)}, u32[]{:S(2)}, u32[]{:S(2)}) collective-permute-start(bf16[128,3072]{1,0:T(8,128)(2,1)S(1)} %copy-done.11), channel_id=1, source_target_pairs={{8,0},{16,8},{24,16},{28,24},{20,28},{12,20},{4,12},{0,4},{9,1},{1... | collective-permute-start | bytes 2359304 | tf_op jit(solution)/shard_map/ppermute | solution.py:738
  125.4 19.5 %collective-permute-start.23 = (bf16[128,3072]{1,0:T(8,128)(2,1)S(1)}, bf16[128,3072]{1,0:T(8,128)(2,1)S(1)}, u32[]{:S(2)}, u32[]{:S(2)}) collective-permute-start(bf16[128,3072]{1,0:T(8,128)(2,1)S(1)} %copy-done.11), channel_id=1, source_target_pairs={{0,8},{8,16},{16,24},{24,28},{28,20},{20,12},{12,4},{4,0},{1,9},{9... | collective-permute-start | bytes 2359304 | tf_op jit(solution)/shard_map/ppermute | solution.py:737
  126.5 15.4 %collective-permute-start.25 = (bf16[256,1024]{1,0:T(8,128)(2,1)S(1)}, bf16[256,1024]{1,0:T(8,128)(2,1)S(1)}, u32[]{:S(2)}, u32[]{:S(2)}) collective-permute-start(bf16[256,1024]{1,0:T(8,128)(2,1)S(1)} %get-tuple-element.242), channel_id=1, source_target_pairs={{0,2},{1,3},{2,0},{3,1},{4,6},{5,7},{6,4},{7,5},{8,10},{9,11},{10,... | collective-permute-start | bytes 1572872 | tf_op jit(solution)/shard_map/ppermute | solution.py:808
  144.9 20.5 %collective-permute-start.29 = (bf16[512,1024]{1,0:T(8,128)(2,1)}, bf16[512,1024]{1,0:T(8,128)(2,1)S(1)}, u32[]{:S(2)}, u32[]{:S(2)}) collective-permute-start(bf16[512,1024]{1,0:T(8,128)(2,1)} %get-tuple-element.251), channel_id=1, source_target_pairs={{0,1},{1,0},{2,3},{3,2},{4,5},{5,4},{6,7},{7,6},{8,9},{9,8},{10,11... | collective-permute-start | bytes 3145736 | tf_op jit(solution)/shard_map/ppermute | solution.py:793
  144.9 20.5 %collective-permute-start.30 = (bf16[512,1024]{1,0:T(8,128)(2,1)}, bf16[512,1024]{1,0:T(8,128)(2,1)S(1)}, u32[]{:S(2)}, u32[]{:S(2)}) collective-permute-start(bf16[512,1024]{1,0:T(8,128)(2,1)} %get-tuple-element.253), channel_id=1, source_target_pairs={{0,1},{1,0},{2,3},{3,2},{4,5},{5,4},{6,7},{7,6},{8,9},{9,8},{10,11... | collective-permute-start | bytes 3145736 | tf_op jit(solution)/shard_map/ppermute | solution.py:793
  145.4 19.4 %collective-permute-start.26 = (bf16[128,3072]{1,0:T(8,128)(2,1)S(1)}, bf16[128,3072]{1,0:T(8,128)(2,1)S(1)}, u32[]{:S(2)}, u32[]{:S(2)}) collective-permute-start(bf16[128,3072]{1,0:T(8,128)(2,1)S(1)} %collective-permute-done.23.refs_11_), channel_id=1, source_target_pairs={{0,8},{8,16},{16,24},{24,28},{28,20},{20,12},{12,4},{4,0},{1,9},{9... | collective-permute-start | bytes 2359304 | tf_op jit(solution)/shard_map/ppermute | solution.py:737
  146.2 19.2 %collective-permute-start.27 = (bf16[128,3072]{1,0:T(8,128)(2,1)S(1)}, bf16[128,3072]{1,0:T(8,128)(2,1)S(1)}, u32[]{:S(2)}, u32[]{:S(2)}) collective-permute-start(bf16[128,3072]{1,0:T(8,128)(2,1)S(1)} %collective-permute-done.24.refs_4_), channel_id=1, source_target_pairs={{8,0},{16,8},{24,16},{28,24},{20,28},{12,20},{4,12},{0,4},{9,1},{1... | collective-permute-start | bytes 2359304 | tf_op jit(solution)/shard_map/ppermute | solution.py:738
  147.5 15.4 %collective-permute-start.28 = (bf16[256,1024]{1,0:T(8,128)(2,1)S(1)}, bf16[256,1024]{1,0:T(8,128)(2,1)}, u32[]{:S(2)}, u32[]{:S(2)}) collective-permute-start(bf16[256,1024]{1,0:T(8,128)(2,1)S(1)} %get-tuple-element.250), channel_id=1, source_target_pairs={{0,2},{1,3},{2,0},{3,1},{4,6},{5,7},{6,4},{7,5},{8,10},{9,11},{10,... | collective-permute-start | bytes 1572872 | tf_op jit(solution)/shard_map/ppermute | solution.py:808
  166.4 19.3 %collective-permute-start.31 = (bf16[128,3072]{1,0:T(8,128)(2,1)S(1)}, bf16[128,3072]{1,0:T(8,128)(2,1)S(1)}, u32[]{:S(2)}, u32[]{:S(2)}) collective-permute-start(bf16[128,3072]{1,0:T(8,128)(2,1)S(1)} %collective-permute-done.26.refs_10_), channel_id=1, source_target_pairs={{0,8},{8,16},{16,24},{24,28},{28,20},{20,12},{12,4},{4,0},{1,9},{9... | collective-permute-start | bytes 2359304 | tf_op jit(solution)/shard_map/ppermute | solution.py:737
  167.7 18.1 %collective-permute-start.32 = (bf16[128,3072]{1,0:T(8,128)(2,1)S(1)}, bf16[128,3072]{1,0:T(8,128)(2,1)S(1)}, u32[]{:S(2)}, u32[]{:S(2)}) collective-permute-start(bf16[128,3072]{1,0:T(8,128)(2,1)S(1)} %collective-permute-done.27.refs_5_), channel_id=1, source_target_pairs={{8,0},{16,8},{24,16},{28,24},{20,28},{12,20},{4,12},{0,4},{9,1},{1... | collective-permute-start | bytes 2359304 | tf_op jit(solution)/shard_map/ppermute | solution.py:738
  169.9 15.9 %collective-permute-start.34 = (bf16[512,1024]{1,0:T(8,128)(2,1)S(1)}, bf16[512,1024]{1,0:T(8,128)(2,1)S(1)}, u32[]{:S(2)}, u32[]{:S(2)}) collective-permute-start(bf16[512,1024]{1,0:T(8,128)(2,1)S(1)} %add_convert_fusion.11.refs_0_.att0.refs_4_), channel_id=1, source_target_pairs={{0,1},{1,0},{2,3},{3,2},{4,5},{5,4},{6,7},{7,6},{8,9},{9,8},{10,11... | collective-permute-start | bytes 3145736 | tf_op jit(solution)/shard_map/ppermute | solution.py:814
  170.9 14.8 %collective-permute-start.33 = (bf16[256,1024]{1,0:T(8,128)(2,1)S(1)}, bf16[256,1024]{1,0:T(8,128)(2,1)S(1)}, u32[]{:S(2)}, u32[]{:S(2)}) collective-permute-start(bf16[256,1024]{1,0:T(8,128)(2,1)S(1)} %get-tuple-element.264), channel_id=1, source_target_pairs={{0,2},{1,3},{2,0},{3,1},{4,6},{5,7},{6,4},{7,5},{8,10},{9,11},{10,... | collective-permute-start | bytes 1572872 | tf_op jit(solution)/shard_map/ppermute | solution.py:808
  185.8 21.0 %collective-permute-start.39 = (bf16[256,1024]{1,0:T(8,128)(2,1)S(1)}, bf16[256,1024]{1,0:T(8,128)(2,1)S(1)}, u32[]{:S(2)}, u32[]{:S(2)}) collective-permute-start(bf16[256,1024]{1,0:T(8,128)(2,1)S(1)} %get-tuple-element.274), channel_id=1, source_target_pairs={{0,2},{1,3},{2,0},{3,1},{4,6},{5,7},{6,4},{7,5},{8,10},{9,11},{10,... | collective-permute-start | bytes 1572872 | tf_op jit(solution)/shard_map/ppermute | solution.py:808
  187.3 12.3 %collective-permute-start.35 = (bf16[64,3072]{1,0:T(8,128)(2,1)}, bf16[64,3072]{1,0:T(8,128)(2,1)S(1)}, u32[]{:S(2)}, u32[]{:S(2)}) collective-permute-start(bf16[64,3072]{1,0:T(8,128)(2,1)} %get-tuple-element.267), channel_id=1, source_target_pairs={{0,8},{8,16},{16,24},{24,28},{28,20},{20,12},{12,4},{4,0},{1,9},{9... | collective-permute-start | bytes 1179656 | tf_op jit(solution)/shard_map/ppermute | solution.py:774
  189.4 16.4 %collective-permute-start.37 = (bf16[64,3072]{1,0:T(8,128)(2,1)S(1)}, bf16[64,3072]{1,0:T(8,128)(2,1)S(1)}, u32[]{:S(2)}, u32[]{:S(2)}) collective-permute-start(bf16[64,3072]{1,0:T(8,128)(2,1)S(1)} %slice.151), channel_id=1, source_target_pairs={{0,8},{8,16},{16,24},{24,28},{28,20},{20,12},{12,4},{4,0},{1,9},{9... | collective-permute-start | bytes 1179656 | tf_op jit(solution)/shard_map/ppermute | solution.py:737
  191.1 15.7 %collective-permute-start.38 = (bf16[64,3072]{1,0:T(8,128)(2,1)S(1)}, bf16[64,3072]{1,0:T(8,128)(2,1)S(1)}, u32[]{:S(2)}, u32[]{:S(2)}) collective-permute-start(bf16[64,3072]{1,0:T(8,128)(2,1)S(1)} %slice.152), channel_id=1, source_target_pairs={{8,0},{16,8},{24,16},{28,24},{20,28},{12,20},{4,12},{0,4},{9,1},{1... | collective-permute-start | bytes 1179656 | tf_op jit(solution)/shard_map/ppermute | solution.py:738
  206.8 20.6 %collective-permute-start.40 = (bf16[128,3072]{1,0:T(8,128)(2,1)}, bf16[128,3072]{1,0:T(8,128)(2,1)S(1)}, u32[]{:S(2)}, u32[]{:S(2)}) collective-permute-start(bf16[128,3072]{1,0:T(8,128)(2,1)} %get-tuple-element.275), channel_id=1, source_target_pairs={{0,8},{8,16},{16,24},{24,28},{28,20},{20,12},{12,4},{4,0},{1,9},{9... | collective-permute-start | bytes 2359304 | tf_op jit(solution)/shard_map/ppermute | solution.py:774
  208.9 20.6 %collective-permute-start.42 = (bf16[512,1024]{1,0:T(8,128)(2,1)S(1)}, bf16[512,1024]{1,0:T(8,128)(2,1)S(1)}, u32[]{:S(2)}, u32[]{:S(2)}) collective-permute-start(bf16[512,1024]{1,0:T(8,128)(2,1)S(1)} %add_convert_fusion.10.dh0), channel_id=1, source_target_pairs={{0,1},{1,0},{2,3},{3,2},{4,5},{5,4},{6,7},{7,6},{8,9},{9,8},{10,11... | collective-permute-start | bytes 3145736 | tf_op jit(solution)/shard_map/ppermute | solution.py:814
  210.4 19.1 %collective-permute-start.41 = (bf16[128,3072]{1,0:T(8,128)(2,1)S(1)}, bf16[128,3072]{1,0:T(8,128)(2,1)}, u32[]{:S(2)}, u32[]{:S(2)}) collective-permute-start(bf16[128,3072]{1,0:T(8,128)(2,1)S(1)} %copy-done.65), channel_id=1, source_target_pairs={{8,0},{16,8},{24,16},{28,24},{20,28},{12,20},{4,12},{0,4},{9,1},{1... | collective-permute-start | bytes 2359304 | tf_op jit(solution)/shard_map/ppermute | solution.py:775
  211.8 15.7 %collective-permute-start.43 = (bf16[256,1024]{1,0:T(8,128)(2,1)}, bf16[256,1024]{1,0:T(8,128)(2,1)S(1)}, u32[]{:S(2)}, u32[]{:S(2)}) collective-permute-start(bf16[256,1024]{1,0:T(8,128)(2,1)} %get-tuple-element.283), channel_id=1, source_target_pairs={{0,2},{1,3},{2,0},{3,1},{4,6},{5,7},{6,4},{7,5},{8,10},{9,11},{10,... | collective-permute-start | bytes 1572872 | tf_op jit(solution)/shard_map/ppermute | solution.py:808
  229.6 19.5 %collective-permute-start.44 = (bf16[128,3072]{1,0:T(8,128)(2,1)S(1)}, bf16[128,3072]{1,0:T(8,128)(2,1)}, u32[]{:S(2)}, u32[]{:S(2)}) collective-permute-start(bf16[128,3072]{1,0:T(8,128)(2,1)S(1)} %add_convert_fusion.23), channel_id=1, source_target_pairs={{0,8},{8,16},{16,24},{24,28},{28,20},{20,12},{12,4},{4,0},{1,9},{9... | collective-permute-start | bytes 2359304 | tf_op jit(solution)/shard_map/ppermute | solution.py:774
  231.0 19.5 %collective-permute-start.47 = (bf16[512,1024]{1,0:T(8,128)(2,1)}, bf16[512,1024]{1,0:T(8,128)(2,1)S(1)}, u32[]{:S(2)}, u32[]{:S(2)}) collective-permute-start(bf16[512,1024]{1,0:T(8,128)(2,1)} %get-tuple-element.293), channel_id=1, source_target_pairs={{0,1},{1,0},{2,3},{3,2},{4,5},{5,4},{6,7},{7,6},{8,9},{9,8},{10,11... | collective-permute-start | bytes 3145736 | tf_op jit(solution)/shard_map/ppermute | solution.py:793
  231.0 22.6 %collective-permute-start.48 = (bf16[512,1024]{1,0:T(8,128)(2,1)}, bf16[512,1024]{1,0:T(8,128)(2,1)S(1)}, u32[]{:S(2)}, u32[]{:S(2)}) collective-permute-start(bf16[512,1024]{1,0:T(8,128)(2,1)} %get-tuple-element.295), channel_id=1, source_target_pairs={{0,1},{1,0},{2,3},{3,2},{4,5},{5,4},{6,7},{7,6},{8,9},{9,8},{10,11... | collective-permute-start | bytes 3145736 | tf_op jit(solution)/shard_map/ppermute | solution.py:793
  232.8 18.1 %collective-permute-start.46 = (bf16[256,1024]{1,0:T(8,128)(2,1)}, bf16[256,1024]{1,0:T(8,128)(2,1)}, u32[]{:S(2)}, u32[]{:S(2)}) collective-permute-start(bf16[256,1024]{1,0:T(8,128)(2,1)} %get-tuple-element.292), channel_id=1, source_target_pairs={{0,2},{1,3},{2,0},{3,1},{4,6},{5,7},{6,4},{7,5},{8,10},{9,11},{10,... | collective-permute-start | bytes 1572872 | tf_op jit(solution)/shard_map/ppermute | solution.py:808
  234.4 19.2 %collective-permute-start.45 = (bf16[128,3072]{1,0:T(8,128)(2,1)S(1)}, bf16[128,3072]{1,0:T(8,128)(2,1)S(1)}, u32[]{:S(2)}, u32[]{:S(2)}) collective-permute-start(bf16[128,3072]{1,0:T(8,128)(2,1)S(1)} %add_convert_fusion.22), channel_id=1, source_target_pairs={{8,0},{16,8},{24,16},{28,24},{20,28},{12,20},{4,12},{0,4},{9,1},{1... | collective-permute-start | bytes 2359304 | tf_op jit(solution)/shard_map/ppermute | solution.py:775
  253.6 27.8 %collective-permute-start.51 = (bf16[512,1024]{1,0:T(8,128)(2,1)S(1)}, bf16[512,1024]{1,0:T(8,128)(2,1)S(1)}, u32[]{:S(2)}, u32[]{:S(2)}) collective-permute-start(bf16[512,1024]{1,0:T(8,128)(2,1)S(1)} %add_convert_fusion.8), channel_id=1, source_target_pairs={{0,2},{1,3},{2,0},{3,1},{4,6},{5,7},{6,4},{7,5},{8,10},{9,11},{10,... | collective-permute-start | bytes 3145736 | tf_op jit(solution)/shard_map/ppermute | solution.py:808
  254.3 27.1 %collective-permute-start.52 = (bf16[128,3072]{1,0:T(8,128)(2,1)S(1)}, bf16[128,3072]{1,0:T(8,128)(2,1)S(1)}, u32[]{:S(2)}, u32[]{:S(2)}) collective-permute-start(bf16[128,3072]{1,0:T(8,128)(2,1)S(1)} %add_convert_fusion.21), channel_id=1, source_target_pairs={{0,8},{8,16},{16,24},{24,28},{28,20},{20,12},{12,4},{4,0},{1,9},{9... | collective-permute-start | bytes 2359304 | tf_op jit(solution)/shard_map/ppermute | solution.py:774
  255.1 26.3 %collective-permute-start.53 = (bf16[128,3072]{1,0:T(8,128)(2,1)S(1)}, bf16[128,3072]{1,0:T(8,128)(2,1)S(1)}, u32[]{:S(2)}, u32[]{:S(2)}) collective-permute-start(bf16[128,3072]{1,0:T(8,128)(2,1)S(1)} %add_convert_fusion.20), channel_id=1, source_target_pairs={{8,0},{16,8},{24,16},{28,24},{20,28},{12,20},{4,12},{0,4},{9,1},{1... | collective-permute-start | bytes 2359304 | tf_op jit(solution)/shard_map/ppermute | solution.py:775
  287.7 21.9 %collective-permute-start.56 = (bf16[128,3072]{1,0:T(8,128)(2,1)}, bf16[128,3072]{1,0:T(8,128)(2,1)S(1)}, u32[]{:S(2)}, u32[]{:S(2)}) collective-permute-start(bf16[128,3072]{1,0:T(8,128)(2,1)} %get-tuple-element.318), channel_id=1, source_target_pairs={{0,8},{8,16},{16,24},{24,28},{28,20},{20,12},{12,4},{4,0},{1,9},{9... | collective-permute-start | bytes 2359304 | tf_op jit(solution)/shard_map/ppermute | solution.py:774
  289.5 20.3 %collective-permute-start.57 = (bf16[128,3072]{1,0:T(8,128)(2,1)S(1)}, bf16[128,3072]{1,0:T(8,128)(2,1)S(1)}, u32[]{:S(2)}, u32[]{:S(2)}) collective-permute-start(bf16[128,3072]{1,0:T(8,128)(2,1)S(1)} %copy-done.64), channel_id=1, source_target_pairs={{8,0},{16,8},{24,16},{28,24},{20,28},{12,20},{4,12},{0,4},{9,1},{1... | collective-permute-start | bytes 2359304 | tf_op jit(solution)/shard_map/ppermute | solution.py:775
  290.9 19.3 %collective-permute-start.58 = (bf16[384,1024]{1,0:T(8,128)(2,1)S(1)}, bf16[384,1024]{1,0:T(8,128)(2,1)S(1)}, u32[]{:S(2)}, u32[]{:S(2)}) collective-permute-start(bf16[384,1024]{1,0:T(8,128)(2,1)S(1)} %slice.157), channel_id=1, source_target_pairs={{0,2},{1,3},{2,0},{3,1},{4,6},{5,7},{6,4},{7,5},{8,10},{9,11},{10,... | collective-permute-start | bytes 2359304 | tf_op jit(solution)/shard_map/ppermute | solution.py:808
  310.2 21.3 %collective-permute-start.59 = (bf16[128,3072]{1,0:T(8,128)(2,1)S(1)}, bf16[128,3072]{1,0:T(8,128)(2,1)S(1)}, u32[]{:S(2)}, u32[]{:S(2)}) collective-permute-start(bf16[128,3072]{1,0:T(8,128)(2,1)S(1)} %add_convert_fusion.19), channel_id=1, source_target_pairs={{0,8},{8,16},{16,24},{24,28},{28,20},{20,12},{12,4},{4,0},{1,9},{9... | collective-permute-start | bytes 2359304 | tf_op jit(solution)/shard_map/ppermute | solution.py:774
  311.1 21.5 %collective-permute-start.61 = (bf16[512,1024]{1,0:T(8,128)(2,1)}, bf16[512,1024]{1,0:T(8,128)(2,1)S(1)}, u32[]{:S(2)}, u32[]{:S(2)}) collective-permute-start(bf16[512,1024]{1,0:T(8,128)(2,1)} %bitcast.16), channel_id=1, source_target_pairs={{0,1},{1,0},{2,3},{3,2},{4,5},{5,4},{6,7},{7,6},{8,9},{9,8},{10,11... | collective-permute-start | bytes 3145736 | tf_op jit(solution)/shard_map/ppermute | solution.py:793
  311.3 22.2 %collective-permute-start.62 = (bf16[128,1024]{1,0:T(8,128)(2,1)S(1)}, bf16[128,1024]{1,0:T(8,128)(2,1)S(1)}, u32[]{:S(2)}, u32[]{:S(2)}) collective-permute-start(bf16[128,1024]{1,0:T(8,128)(2,1)S(1)} %slice.158), channel_id=1, source_target_pairs={{0,2},{1,3},{2,0},{3,1},{4,6},{5,7},{6,4},{7,5},{8,10},{9,11},{10,... | collective-permute-start | bytes 786440 | tf_op jit(solution)/shard_map/ppermute | solution.py:808
  312.8 20.6 %collective-permute-start.60 = (bf16[128,3072]{1,0:T(8,128)(2,1)S(1)}, bf16[128,3072]{1,0:T(8,128)(2,1)S(1)}, u32[]{:S(2)}, u32[]{:S(2)}) collective-permute-start(bf16[128,3072]{1,0:T(8,128)(2,1)S(1)} %add_convert_fusion.18), channel_id=1, source_target_pairs={{8,0},{16,8},{24,16},{28,24},{20,28},{12,20},{4,12},{0,4},{9,1},{1... | collective-permute-start | bytes 2359304 | tf_op jit(solution)/shard_map/ppermute | solution.py:775
  333.5 21.6 %collective-permute-start.65 = (bf16[512,1024]{1,0:T(8,128)(2,1)}, bf16[512,1024]{1,0:T(8,128)(2,1)S(1)}, u32[]{:S(2)}, u32[]{:S(2)}) collective-permute-start(bf16[512,1024]{1,0:T(8,128)(2,1)} %bitcast.18), channel_id=1, source_target_pairs={{0,1},{1,0},{2,3},{3,2},{4,5},{5,4},{6,7},{7,6},{8,9},{9,8},{10,11... | collective-permute-start | bytes 3145736 | tf_op jit(solution)/shard_map/ppermute | solution.py:793
  335.0 20.6 %collective-permute-start.66 = (bf16[384,1024]{1,0:T(8,128)(2,1)S(1)}, bf16[384,1024]{1,0:T(8,128)(2,1)}, u32[]{:S(2)}, u32[]{:S(2)}) collective-permute-start(bf16[384,1024]{1,0:T(8,128)(2,1)S(1)} %slice.159), channel_id=1, source_target_pairs={{0,2},{1,3},{2,0},{3,1},{4,6},{5,7},{6,4},{7,5},{8,10},{9,11},{10,... | collective-permute-start | bytes 2359304 | tf_op jit(solution)/shard_map/ppermute | solution.py:808
  335.6 20.0 %collective-permute-start.63 = (bf16[128,3072]{1,0:T(8,128)(2,1)}, bf16[128,3072]{1,0:T(8,128)(2,1)S(1)}, u32[]{:S(2)}, u32[]{:S(2)}) collective-permute-start(bf16[128,3072]{1,0:T(8,128)(2,1)} %add_convert_fusion.17), channel_id=1, source_target_pairs={{0,8},{8,16},{16,24},{24,28},{28,20},{20,12},{12,4},{4,0},{1,9},{9... | collective-permute-start | bytes 2359304 | tf_op jit(solution)/shard_map/ppermute | solution.py:774
  336.3 19.3 %collective-permute-start.64 = (bf16[128,3072]{1,0:T(8,128)(2,1)}, bf16[128,3072]{1,0:T(8,128)(2,1)S(1)}, u32[]{:S(2)}, u32[]{:S(2)}) collective-permute-start(bf16[128,3072]{1,0:T(8,128)(2,1)} %add_convert_fusion.16), channel_id=1, source_target_pairs={{8,0},{16,8},{24,16},{28,24},{20,28},{12,20},{4,12},{0,4},{9,1},{1... | collective-permute-start | bytes 2359304 | tf_op jit(solution)/shard_map/ppermute | solution.py:775
  338.9 16.1 %collective-permute-start.68 = (f32[4,1024]{1,0:T(4,128)S(1)}, f32[4,1024]{1,0:T(4,128)S(1)}, u32[]{:S(2)}, u32[]{:S(2)}) collective-permute-start(f32[4,1024]{1,0:T(4,128)S(1)} %fusion.1), channel_id=1, source_target_pairs={{0,2},{1,3},{2,0},{3,1},{4,6},{5,7},{6,4},{7,5},{8,10},{9,11},{10,... | collective-permute-start | bytes 49160 | tf_op jit(solution)/shard_map/ppermute | solution.py:980
  356.1 12.4 %collective-permute-start.71 = (bf16[512,1024]{1,0:T(8,128)(2,1)S(1)}, bf16[512,1024]{1,0:T(8,128)(2,1)S(1)}, u32[]{:S(2)}, u32[]{:S(2)}) collective-permute-start(bf16[512,1024]{1,0:T(8,128)(2,1)S(1)} %add_convert_fusion.2.refs_6_), channel_id=1, source_target_pairs={{0,1},{1,0},{2,3},{3,2},{4,5},{5,4},{6,7},{7,6},{8,9},{9,8},{10,11... | collective-permute-start | bytes 3145736 | tf_op jit(solution)/shard_map/ppermute | solution.py:814
  368.4 15.6 %collective-permute-start.74 = (bf16[256,1024]{1,0:T(8,128)(2,1)}, bf16[256,1024]{1,0:T(8,128)(2,1)S(1)}, u32[]{:S(2)}, u32[]{:S(2)}) collective-permute-start(bf16[256,1024]{1,0:T(8,128)(2,1)} %get-tuple-element.380), channel_id=1, source_target_pairs={{0,8},{8,16},{16,24},{24,28},{28,20},{20,12},{12,4},{4,0},{1,9},{9... | collective-permute-start | bytes 1572872 | tf_op jit(solution)/shard_map/ppermute | solution.py:774
  371.2 16.6 %collective-permute-start.76 = (bf16[512,1024]{1,0:T(8,128)(2,1)S(1)}, bf16[512,1024]{1,0:T(8,128)(2,1)S(1)}, u32[]{:S(2)}, u32[]{:S(2)}) collective-permute-start(bf16[512,1024]{1,0:T(8,128)(2,1)S(1)} %add_convert_fusion.1.mine), channel_id=1, source_target_pairs={{0,1},{1,0},{2,3},{3,2},{4,5},{5,4},{6,7},{7,6},{8,9},{9,8},{10,11... | collective-permute-start | bytes 3145736 | tf_op jit(solution)/shard_map/ppermute | solution.py:814
  371.2 12.8 %collective-permute-start.77 = (f32[4,1024]{1,0:T(4,128)S(1)}, f32[4,1024]{1,0:T(4,128)S(1)}, u32[]{:S(2)}, u32[]{:S(2)}) collective-permute-start(f32[4,1024]{1,0:T(4,128)S(1)} %add.167), channel_id=1, source_target_pairs={{0,8},{4,12},{8,0},{12,4},{16,24},{20,28},{24,16},{28,20},{1,9},{5... | collective-permute-start | bytes 49160 | tf_op jit(solution)/shard_map/ppermute | solution.py:980
  371.9 14.3 %collective-permute-start.75 = (bf16[256,1024]{1,0:T(8,128)(2,1)S(1)}, bf16[256,1024]{1,0:T(8,128)(2,1)S(1)}, u32[]{:S(2)}, u32[]{:S(2)}) collective-permute-start(bf16[256,1024]{1,0:T(8,128)(2,1)S(1)} %copy-done.70), channel_id=1, source_target_pairs={{8,0},{16,8},{24,16},{28,24},{20,28},{12,20},{4,12},{0,4},{9,1},{1... | collective-permute-start | bytes 1572872 | tf_op jit(solution)/shard_map/ppermute | solution.py:775
  374.0 13.8 %collective-permute-start.78 = (bf16[256,1024]{1,0:T(8,128)(2,1)S(1)}, bf16[256,1024]{1,0:T(8,128)(2,1)S(1)}, u32[]{:S(2)}, u32[]{:S(2)}) collective-permute-start(bf16[256,1024]{1,0:T(8,128)(2,1)S(1)} %get-tuple-element.386), channel_id=1, source_target_pairs={{0,2},{1,3},{2,0},{3,1},{4,6},{5,7},{6,4},{7,5},{8,10},{9,11},{10,... | collective-permute-start | bytes 1572872 | tf_op jit(solution)/shard_map/ppermute | solution.py:808
  387.8 14.2 %collective-permute-start.79 = (bf16[256,1024]{1,0:T(8,128)(2,1)S(1)}, bf16[256,1024]{1,0:T(8,128)(2,1)S(1)}, u32[]{:S(2)}, u32[]{:S(2)}) collective-permute-start(bf16[256,1024]{1,0:T(8,128)(2,1)S(1)} %add_convert_fusion.27), channel_id=1, source_target_pairs={{0,8},{8,16},{16,24},{24,28},{28,20},{20,12},{12,4},{4,0},{1,9},{9... | collective-permute-start | bytes 1572872 | tf_op jit(solution)/shard_map/ppermute | solution.py:774
  388.1 14.0 %collective-permute-start.80 = (bf16[256,1024]{1,0:T(8,128)(2,1)S(1)}, bf16[256,1024]{1,0:T(8,128)(2,1)S(1)}, u32[]{:S(2)}, u32[]{:S(2)}) collective-permute-start(bf16[256,1024]{1,0:T(8,128)(2,1)S(1)} %add_convert_fusion.26), channel_id=1, source_target_pairs={{8,0},{16,8},{24,16},{28,24},{20,28},{12,20},{4,12},{0,4},{9,1},{1... | collective-permute-start | bytes 1572872 | tf_op jit(solution)/shard_map/ppermute | solution.py:775
  404.0 14.3 %collective-permute-start.84 = (bf16[256,1024]{1,0:T(8,128)(2,1)}, bf16[256,1024]{1,0:T(8,128)(2,1)S(1)}, u32[]{:S(2)}, u32[]{:S(2)}) collective-permute-start(bf16[256,1024]{1,0:T(8,128)(2,1)} %add_convert_fusion.25), channel_id=1, source_target_pairs={{0,8},{8,16},{16,24},{24,28},{28,20},{20,12},{12,4},{4,0},{1,9},{9... | collective-permute-start | bytes 1572872 | tf_op jit(solution)/shard_map/ppermute | solution.py:774
  404.8 13.9 %collective-permute-start.85 = (bf16[256,1024]{1,0:T(8,128)(2,1)S(1)}, bf16[256,1024]{1,0:T(8,128)(2,1)}, u32[]{:S(2)}, u32[]{:S(2)}) collective-permute-start(bf16[256,1024]{1,0:T(8,128)(2,1)S(1)} %add_convert_fusion.24), channel_id=1, source_target_pairs={{8,0},{16,8},{24,16},{28,24},{20,28},{12,20},{4,12},{0,4},{9,1},{1... | collective-permute-start | bytes 1572872 | tf_op jit(solution)/shard_map/ppermute | solution.py:775
  (109 other events, 801.0 us)

commit v8 on v7

--- a/solution.py
+++ b/solution.py
@@ -905,6 +905,7 @@
     moved += move(0)
     rounds.done = held
     close(*moved, part[0], got)
+    moved = move(1)
     close(heads[1].near(), heads[0].last())
 
     def grads_of(c, out):
@@ -912,7 +913,6 @@
         return weight_grads(now(places), [columns], far)
 
     dh, mlp, grads, dm, d_gain_ffn = ([None] * 2 for _ in range(5))
-    moved = move(1)
     got = heads[1].far(0.5)
     ffn = (x[0], heads[0].sum, g[0], g_ffn[0], weights(0))
     out, dh_other, mlp_other = hidden_units(now(places), *ffn, half=1)

time: 430 us -> 427 us (level)
  transfers between devices with their start and end apart: 86 -> 86, of which waited for: 33 -> 32; matrix products, arithmetic and copies ran while one was open for 7% -> 8% of each run, Pallas kernels for 47% -> 47%
where the time goes in v8:
time: 427 us; the launch traced here: 419 us
  Pallas kernels  203 us (48%)
  waiting for transfers between devices  88.5 us (21%)
  starting transfers between devices  82.9 us (19%)
  local copies, waits for them, and re-layouts  21.5 us (5%)
  other arithmetic  20.4 us (5%)
    pallas_call x23, Pallas kernels, kernel_call(): pl.pallas_call(body, grid_spec=spec, out_shape=outs, input_output_aliases...  203 us
    ppermute x12, waiting for transfers between devices, step(): self.a.append(lax.ppermute(self.rounds.now(a), 'dp', self.ring.ahead))  37.5 us
    ppermute x14, starting transfers between devices, far(): self.got.append(lax.ppermute(moved, 'mp', self.far_moves))  19.4 us
    ppermute x12, starting transfers between devices, step(): self.b.append(lax.ppermute(self.rounds.now(b), 'dp', self.ring.behind))  16.1 us
    ppermute x12, starting transfers between devices, step(): self.b = lax.ppermute(self.rounds.now(self.b), 'dp', self.ring.behind)  14 us
    ppermute x12, waiting for transfers between devices, step(): self.a = lax.ppermute(self.rounds.now(self.a), 'dp', self.ring.ahead)  12.8 us
    ppermute x12, starting transfers between devices, step(): self.a = lax.ppermute(self.rounds.now(self.a), 'dp', self.ring.ahead)  12.4 us
    convert_element_type x16, other arithmetic, add(): return (one.astype(F32) + two.astype(F32)).astype(BF)  11.5 us
  transfers between devices with their start and end apart: 86, of which 32 were waited for; matrix products, arithmetic and copies ran while one was open for 8% of the time, Pallas kernels for 47%

profile of v8, /device:TPU:0, one launch (start us, length us, event | category | flops | bytes accessed | tf_op | source)
XLA Modules:
  0.0 419.3 jit_solution(6158321663836920848)
XLA Ops:
  0.6 2.0 shard_map.203.refs_2_.refs_3_.refs_0_
  2.6 3.0 collective-permute-start.2
  6.3 2.0 collective-permute-start
  8.3 3.1 slice_bitcast_fusion.3.refs_0_.x_ref.x0
  11.4 2.1 shard_map.204.refs_3_
  13.5 5.7 %collective-permute-done = f32[1,4,128]{2,1,0:T(4,128)S(1)} collective-permute-done((f32[1,4,128]{2,1,0:T(4,128)S(1)}, f32[1,4,128]{2,1,0:T(4,128)S(1)}, u32[]{:S(2)}, u32[]{:S(2)}) %collective-permute-start) | collective-permute-done | bytes 2080 | tf_op jit(solution)/shard_map/ppermute | solution.py:850
  19.6 1.8 collective-permute-start.5
  21.6 3.3 slice_bitcast_fusion.2.refs_0_.x_ref.x1
  24.9 2.1 shard_map.205.refs_3_
  27.0 5.2 %collective-permute-done.3 = f32[2,4,128]{2,1,0:T(4,128)S(1)} collective-permute-done((f32[2,4,128]{2,1,0:T(4,128)S(1)}, f32[2,4,128]{2,1,0:T(4,128)S(1)}, u32[]{:S(2)}, u32[]{:S(2)}) %collective-permute-start.3) | collective-permute-done | bytes 4128 | tf_op jit(solution)/shard_map/ppermute | solution.py:850
  32.2 2.7 collective-permute-start.6
  37.4 2.5 slice_bitcast_fusion
  39.8 6.4 %collective-permute-done.7.refs_7_.refs_8_.refs_5_ = bf16[256,1024]{1,0:T(8,128)(2,1)S(1)} collective-permute-done((bf16[256,1024]{1,0:T(8,128)(2,1)S(1)}, bf16[256,1024]{1,0:T(8,128)(2,1)S(1)}, u32[]{:S(2)}, u32[]{:S(2)}) %collective-permute-start.7) | collective-permute-done | bytes 524320 | tf_op jit(solution)/shard_map/ppermute | solution.py:737
  46.2 2.1 collective-permute-done.8.refs_5_.refs_6_.refs_3_
  50.4 2.0 collective-permute-start.11
  52.4 18.2 %collective-permute-done.10.refs_6_.refs_4_ = bf16[128,1024]{1,0:T(8,128)(2,1)S(1)} collective-permute-done((bf16[128,1024]{1,0:T(8,128)(2,1)S(1)}, bf16[128,1024]{1,0:T(8,128)(2,1)S(1)}, u32[]{:S(2)}, u32[]{:S(2)}) %collective-permute-start.10) | collective-permute-done | bytes 262176 | tf_op jit(solution)/shard_map/ppermute | solution.py:737
  74.5 14.0 %shard_map.206 = (bf16[1024,1024]{1,0:T(8,128)(2,1)}, bf16[1024,768]{1,0:T(8,128)(2,1)}, bf16[1024,256]{1,0:T(8,128)(2,1)}, bf16[512,1024]{1,0:T(8,128)(2,1)}, bf16[512,1024]{1,0:T(8,128)(2,1)}) custom-call(s32[9]{0:T(128)} %pad_add_fusion.places._, bf16[1024,1024]{1,0:T(8,128)(2,1)} %slice_bitcast_fusion.3.refs_0_.x_ref.x0, ...), custom_call_target="tpu_custom_call" | custom-call | flops 1 | bytes 1 | tf_op jit(solution)/shard_map/pallas_call | solution.py:41
  91.5 1.6 add_convert_fusion.15
  93.1 1.6 collective-permute-start.20
  94.6 13.0 %shard_map.207 = (bf16[1024,1024]{1,0:T(8,128)(2,1)}, bf16[1024,768]{1,0:T(8,128)(2,1)}, bf16[1024,256]{1,0:T(8,128)(2,1)}, bf16[512,1024]{1,0:T(8,128)(2,1)}, bf16[512,1024]{1,0:T(8,128)(2,1)}) custom-call(s32[9]{0:T(128)} %pad_add_fusion.places._, bf16[1024,1024]{1,0:T(8,128)(2,1)} %slice_bitcast_fusion.2.refs_0_.x_ref.x1, ...), custom_call_target="tpu_custom_call" | custom-call | flops 1 | bytes 1 | tf_op jit(solution)/shard_map/pallas_call | solution.py:41
  111.2 8.3 %collective-permute-done.17.refs_7_ = bf16[64,3072]{1,0:T(8,128)(2,1)S(1)} collective-permute-done((bf16[64,3072]{1,0:T(8,128)(2,1)S(1)}, bf16[64,3072]{1,0:T(8,128)(2,1)S(1)}, u32[]{:S(2)}, u32[]{:S(2)}) %collective-permute-start.17) | collective-permute-done | bytes 393248 | tf_op jit(solution)/shard_map/ppermute | solution.py:737
  124.6 1.6 collective-permute-start.25
  126.1 14.0 %shard_map.208 = (bf16[1024,1024]{1,0:T(8,128)(2,1)}, bf16[1024,1024]{1,0:T(8,128)(2,1)}, bf16[1024,2048]{1,0:T(8,128)(2,1)}, bf16[512,1024]{1,0:T(8,128)(2,1)}, bf16[512,1024]{1,0:T(8,128)(2,1)}) custom-call(s32[9]{0:T(128)} %pad_add_fusion.places._, bf16[1024,1024]{1,0:T(8,128)(2,1)} %slice_bitcast_fusion.3.refs_0_.x_ref.x0, bf16[512,1024]{1,0:T(8,128)(2,1)} %copy-done.6, ...), custom_call_target="tpu_custom_call" | custom-call | flops 1 | bytes 1 | tf_op jit(solution)/shard_map/pallas_call | solution.py:41
  145.8 13.8 %shard_map.209 = (bf16[1024,1024]{1,0:T(8,128)(2,1)}, bf16[1024,1024]{1,0:T(8,128)(2,1)}, bf16[1024,2048]{1,0:T(8,128)(2,1)}, bf16[512,1024]{1,0:T(8,128)(2,1)}, bf16[512,1024]{1,0:T(8,128)(2,1)}) custom-call(s32[9]{0:T(128)} %pad_add_fusion.places._, ...), custom_call_target="tpu_custom_call", output_to_operand_aliasing={{0}: (14, {}), {1}: (15, {}), {2}: (16, {})} | custom-call | flops 1 | bytes 1 | tf_op jit(solution)/shard_map/pallas_call | solution.py:41
  159.6 2.1 collective-permute-done.26.refs_10_
  167.7 1.5 collective-permute-start.33
  169.2 13.3 %shard_map.210 = (bf16[128,3072]{1,0:T(8,128)(2,1)}, bf16[128,3072]{1,0:T(8,128)(2,1)}, bf16[128,3072]{1,0:T(8,128)(2,1)}, bf16[128,3072]{1,0:T(8,128)(2,1)}, bf...) custom-call(s32[9]{0:T(128)} %pad_add_fusion.places._, ...), custom_call_target="tpu_custom_call" | custom-call | flops 1 | bytes 1 | tf_op jit(solution)/shard_map/pallas_call | solution.py:41
  182.6 1.5 collective-permute-start.39
  184.3 2.1 collective-permute-start.35
  186.7 1.7 collective-permute-start.37
  188.8 8.2 %collective-permute-done.35.a = bf16[64,3072]{1,0:T(8,128)(2,1)S(1)} collective-permute-done((bf16[64,3072]{1,0:T(8,128)(2,1)}, bf16[64,3072]{1,0:T(8,128)(2,1)S(1)}, u32[]{:S(2)}, u32[]{:S(2)}) %collective-permute-start.35) | collective-permute-done | bytes 393248 | tf_op jit(solution)/shard_map/ppermute | solution.py:774
  197.0 1.7 collective-permute-done.36.b
  199.4 2.3 shard_map.211
  204.1 1.7 collective-permute-start.40
  210.6 14.1 %shard_map.212 = (bf16[1024,1024]{1,0:T(8,128)(2,1)}, bf16[1024,1024]{1,0:T(8,128)(2,1)}, bf16[1024,2048]{1,0:T(8,128)(2,1)}, bf16[512,1024]{1,0:T(8,128)(2,1)}, bf16[512,1024]{1,0:T(8,128)(2,1)}) custom-call(s32[9]{0:T(128)} %pad_add_fusion.places._, bf16[1024,1024]{1,0:T(8,128)(2,1)} %slice_bitcast_fusion.2.refs_0_.x_ref.x1, bf16[512,1024]{1,0:T(8,128)(2,1)} %copy-done.2, ...), custom_call_target="tpu_custom_call" | custom-call | flops 1 | bytes 1 | tf_op jit(solution)/shard_map/pallas_call | solution.py:41
  225.0 1.8 collective-permute-done.41
  230.1 1.6 collective-permute-start.46
  232.2 14.0 %shard_map.213 = (bf16[1024,1024]{1,0:T(8,128)(2,1)}, bf16[1024,1024]{1,0:T(8,128)(2,1)}, bf16[1024,2048]{1,0:T(8,128)(2,1)}, bf16[512,1024]{1,0:T(8,128)(2,1)}, bf16[512,1024]{1,0:T(8,128)(2,1)}) custom-call(s32[9]{0:T(128)} %pad_add_fusion.places._, ...), custom_call_target="tpu_custom_call", output_to_operand_aliasing={{0}: (14, {}), {1}: (15, {}), {2}: (16, {})} | custom-call | flops 1 | bytes 1 | tf_op jit(solution)/shard_map/pallas_call | solution.py:41
  248.2 2.6 collective-permute-done.45
  253.8 13.3 %shard_map.214 = (bf16[128,3072]{1,0:T(8,128)(2,1)}, bf16[128,3072]{1,0:T(8,128)(2,1)}, bf16[128,3072]{1,0:T(8,128)(2,1)}, bf16[128,3072]{1,0:T(8,128)(2,1)}, bf...) custom-call(s32[9]{0:T(128)} %pad_add_fusion.places._, ...), custom_call_target="tpu_custom_call" | custom-call | flops 1 | bytes 1 | tf_op jit(solution)/shard_map/pallas_call | solution.py:41
  269.2 7.3 %shard_map.216 = (bf16[1024,1024]{1,0:T(8,128)(2,1)}, f32[1,1024]{1,0:T(1,128)}) custom-call(s32[9]{0:T(128)} %pad_add_fusion.places._, bf16[1024,1024]{1,0:T(8,128)(2,1)} %slice_bitcast_fusion.3.refs_0_.x_ref.x0, bf16[512,1024]{1,0:T(8,128)(2,1)} %copy-done.1, bf16[512,1024]{1,0:T(8,128)(2,1)} %copy-done.6, ...), custom_call_target="tpu_custom_call" | custom-call | flops 1 | bytes 1 | tf_op jit(solution)/shard_map/pallas_call | solution.py:41
  276.5 2.1 collective-permute-done.50.b
  280.3 1.9 add_convert_fusion.6.refs_2_
  282.3 2.6 shard_map.215
  288.1 1.5 collective-permute-start.58
  289.6 17.2 %shard_map.217 = (bf16[1024,768]{1,0:T(8,128)(2,1)}, bf16[1024,768]{1,0:T(8,128)(2,1)}, bf16[1024,1024]{1,0:T(8,128)(2,1)}, bf16[2,256,1024]{2,1,0:T(8,128)(2,1)...) custom-call(s32[9]{0:T(128)} %pad_add_fusion.places._, ...), custom_call_target="tpu_custom_call" | custom-call | flops 1 | bytes 1 | tf_op jit(solution)/shard_map/pallas_call | solution.py:41
  308.5 1.6 collective-permute-start.62
  311.5 17.2 %shard_map.218 = (bf16[1024,768]{1,0:T(8,128)(2,1)}, bf16[1024,768]{1,0:T(8,128)(2,1)}, bf16[1024,1024]{1,0:T(8,128)(2,1)}, bf16[2,256,1024]{2,1,0:T(8,128)(2,1)...) custom-call(s32[9]{0:T(128)} %pad_add_fusion.places._, ...), custom_call_target="tpu_custom_call", output_to_operand_aliasing={{0}: (21, {}), {1}: (22, {}), {2}: (23, {})} | custom-call | flops 1 | bytes 1 | tf_op jit(solution)/shard_map/pallas_call | solution.py:41
  336.2 1.6 collective-permute-start.68
  337.7 11.3 %shard_map.219 = (bf16[256,1024]{1,0:T(8,128)(2,1)}, bf16[256,1024]{1,0:T(8,128)(2,1)}, bf16[256,1024]{1,0:T(8,128)(2,1)}, bf16[256,1024]{1,0:T(8,128)(2,1)}, bf...) custom-call(s32[9]{0:T(128)} %pad_add_fusion.places._, ...), custom_call_target="tpu_custom_call" | custom-call | flops 1 | bytes 1 | tf_op jit(solution)/shard_map/pallas_call | solution.py:41
  349.1 3.2 collective-permute-done.68
  358.3 4.5 %shard_map.220 = (f32[2,128,1024]{2,1,0:T(8,128)}, f32[2,128,1024]{2,1,0:T(8,128)}, f32[2,1024,128]{2,1,0:T(8,128)}) custom-call(bf16[128,3072]{1,0:T(8,128)(2,1)} %get-tuple-element.367.refs_0_, bf16[128,3072]{1,0:T(8,128)(2,1)} %copy-done.50, bf16[128,3072]{1,0:T(8,128)(2,1)} %copy-done.51, bf16[128,3072]{1,0:T(8,128)(2,1)} %get-tuple-element.370.refs_3_, ...), custom_call_target="tpu_custom_call" | custom-call | flops 1 | bytes 1 | tf_op jit(solution)/shard_map/pallas_call | solution.py:41
  363.6 2.0 shard_map.222
  366.8 1.5 add_convert_fusion.1.mine
  369.1 2.0 collective-permute-start.75
  371.3 1.6 collective-permute-start.78
  372.8 8.3 %shard_map.221 = bf16[128,16,1024]{2,1,0:T(8,128)(2,1)} custom-call(s32[9]{0:T(128)} %pad_add_fusion.places._, bf16[1024,1024]{1,0:T(8,128)(2,1)} %slice_bitcast_fusion.3.refs_0_.x_ref.x0, bf16[1024,1024]{1,0:T(8,128)(2,1)} %slice_bitcast_fusion.2.refs_0_.x_ref.x1, bf16[512,1024]{1,0:T(8,128)(2,1)} %copy-done.1, bf16[512,1024]{1,0:T(8,128)(2,1)} %copy-done.6, ...), custom_call_target="tpu_custom_call" | custom-call | flops 1 | bytes 1 | tf_op jit(solution)/shard_map/pallas_call | solution.py:41
  381.4 2.1 collective-permute-done.75
  385.3 1.8 collective-permute-start.80
  389.8 6.2 %shard_map.223.refs_0_ = bf16[128,16,1024]{2,1,0:T(8,128)(2,1)} custom-call(s32[9]{0:T(128)} %pad_add_fusion.places._, bf16[1024,1024]{1,0:T(8,128)(2,1)} %slice_bitcast_fusion.3.refs_0_.x_ref.x0, bf16[1024,1024]{1,0:T(8,128)(2,1)} %slice_bitcast_fusion.2.refs_0_.x_ref.x1, bf16[1024,1024]{1,0:T(8,128)(2,1)} %get-tuple-element.314.dm0.refs_2_.refs_3_, ...), custom_call_target="tpu_custom_call" | custom-call | flops 1 | bytes 1 | tf_op jit(solution)/shard_map/pallas_call | solution.py:41
  396.0 3.3 collective-permute-done.81
  404.9 6.2 %shard_map.224 = bf16[128,16,1024]{2,1,0:T(8,128)(2,1)} custom-call(s32[9]{0:T(128)} %pad_add_fusion.places._, bf16[1024,1024]{1,0:T(8,128)(2,1)} %slice_bitcast_fusion.3.refs_0_.x_ref.x0, bf16[1024,1024]{1,0:T(8,128)(2,1)} %slice_bitcast_fusion.2.refs_0_.x_ref.x1, ...), custom_call_target="tpu_custom_call", output_to_operand_aliasing={{}: (8, {})} | custom-call | flops 1 | bytes 1 | tf_op jit(solution)/shard_map/pallas_call | solution.py:41
  411.1 4.5 %collective-permute-done.84.refs_1_ = bf16[256,1024]{1,0:T(8,128)(2,1)S(1)} collective-permute-done((bf16[256,1024]{1,0:T(8,128)(2,1)}, bf16[256,1024]{1,0:T(8,128)(2,1)S(1)}, u32[]{:S(2)}, u32[]{:S(2)}) %collective-permute-start.84) | collective-permute-done | bytes 524320 | tf_op jit(solution)/shard_map/ppermute | solution.py:774
  416.4 2.4 shard_map.225
  (373 shorter events, 87.4 us)
Async XLA Ops:
  2.6 16.6 %collective-permute-start.2 = (bf16[256,1024]{1,0:T(8,128)(2,1)}, bf16[256,1024]{1,0:T(8,128)(2,1)S(1)}, u32[]{:S(2)}, u32[]{:S(2)}) collective-permute-start(bf16[256,1024]{1,0:T(8,128)(2,1)} %shard_map.203.refs_2_.refs_3_.refs_0_), channel_id=1, source_target_pairs={{8,0},{16,8},{24,16},{28,24},{20,28},{12,20},{4,12},{0,4},{9,1},{1... | collective-permute-start | bytes 1572872 | tf_op jit(solution)/shard_map/ppermute | solution.py:738
  5.6 13.7 %collective-permute-start.1 = (bf16[256,1024]{1,0:T(8,128)(2,1)}, bf16[256,1024]{1,0:T(8,128)(2,1)S(1)}, u32[]{:S(2)}, u32[]{:S(2)}) collective-permute-start(bf16[256,1024]{1,0:T(8,128)(2,1)} %shard_map.203.refs_2_.refs_3_.refs_0_), channel_id=1, source_target_pairs={{0,8},{8,16},{16,24},{24,28},{28,20},{20,12},{12,4},{4,0},{1,9},{9... | collective-permute-start | bytes 1572872 | tf_op jit(solution)/shard_map/ppermute | solution.py:737
  6.3 12.9 %collective-permute-start = (f32[1,4,128]{2,1,0:T(4,128)S(1)}, f32[1,4,128]{2,1,0:T(4,128)S(1)}, u32[]{:S(2)}, u32[]{:S(2)}) collective-permute-start(f32[1,4,128]{2,1,0:T(4,128)S(1)} %maximum_convert_fusion), channel_id=1, source_target_pairs={{0,4},{4,0},{8,12},{12,8},{16,20},{20,16},{24,28},{28,24},{1,5},{5... | collective-permute-start | bytes 6152 | tf_op jit(solution)/shard_map/ppermute | solution.py:850
  19.3 12.9 %collective-permute-start.4 = (bf16[256,1024]{1,0:T(8,128)(2,1)S(1)}, bf16[256,1024]{1,0:T(8,128)(2,1)S(1)}, u32[]{:S(2)}, u32[]{:S(2)}) collective-permute-start(bf16[256,1024]{1,0:T(8,128)(2,1)S(1)} %collective-permute-done.1.refs_9_.refs_10_.refs_7_), channel_id=1, source_target_pairs={{0,8},{8,16},{16,24},{24,28},{28,20},{20,12},{12,4},{4,0},{1,9},{9... | collective-permute-start | bytes 1572872 | tf_op jit(solution)/shard_map/ppermute | solution.py:737
  19.6 12.6 %collective-permute-start.5 = (bf16[256,1024]{1,0:T(8,128)(2,1)S(1)}, bf16[256,1024]{1,0:T(8,128)(2,1)S(1)}, u32[]{:S(2)}, u32[]{:S(2)}) collective-permute-start(bf16[256,1024]{1,0:T(8,128)(2,1)S(1)} %collective-permute-done.2.refs_3_.refs_4_.refs_1_), channel_id=1, source_target_pairs={{8,0},{16,8},{24,16},{28,24},{20,28},{12,20},{4,12},{0,4},{9,1},{1... | collective-permute-start | bytes 1572872 | tf_op jit(solution)/shard_map/ppermute | solution.py:738
  48.3 22.8 %collective-permute-start.12 = (bf16[128,3072]{1,0:T(8,128)(2,1)S(1)}, bf16[128,3072]{1,0:T(8,128)(2,1)S(1)}, u32[]{:S(2)}, u32[]{:S(2)}) collective-permute-start(bf16[128,3072]{1,0:T(8,128)(2,1)S(1)} %copy-done.12), channel_id=1, source_target_pairs={{8,0},{16,8},{24,16},{28,24},{20,28},{12,20},{4,12},{0,4},{9,1},{1... | collective-permute-start | bytes 2359304 | tf_op jit(solution)/shard_map/ppermute | solution.py:738
  49.1 22.0 %collective-permute-start.9 = (bf16[128,3072]{1,0:T(8,128)(2,1)S(1)}, bf16[128,3072]{1,0:T(8,128)(2,1)S(1)}, u32[]{:S(2)}, u32[]{:S(2)}) collective-permute-start(bf16[128,3072]{1,0:T(8,128)(2,1)S(1)} %copy-done.12), channel_id=1, source_target_pairs={{0,8},{8,16},{16,24},{24,28},{28,20},{20,12},{12,4},{4,0},{1,9},{9... | collective-permute-start | bytes 2359304 | tf_op jit(solution)/shard_map/ppermute | solution.py:737
  50.4 20.2 %collective-permute-start.10 = (bf16[128,1024]{1,0:T(8,128)(2,1)S(1)}, bf16[128,1024]{1,0:T(8,128)(2,1)S(1)}, u32[]{:S(2)}, u32[]{:S(2)}) collective-permute-start(bf16[128,1024]{1,0:T(8,128)(2,1)S(1)} %slice.140), channel_id=1, source_target_pairs={{0,8},{8,16},{16,24},{24,28},{28,20},{20,12},{12,4},{4,0},{1,9},{9... | collective-permute-start | bytes 786440 | tf_op jit(solution)/shard_map/ppermute | solution.py:737
  50.4 20.6 %collective-permute-start.11 = (bf16[128,1024]{1,0:T(8,128)(2,1)S(1)}, bf16[128,1024]{1,0:T(8,128)(2,1)S(1)}, u32[]{:S(2)}, u32[]{:S(2)}) collective-permute-start(bf16[128,1024]{1,0:T(8,128)(2,1)S(1)} %slice.141), channel_id=1, source_target_pairs={{8,0},{16,8},{24,16},{28,24},{20,28},{12,20},{4,12},{0,4},{9,1},{1... | collective-permute-start | bytes 786440 | tf_op jit(solution)/shard_map/ppermute | solution.py:738
  71.1 17.4 %collective-permute-start.13 = (bf16[128,3072]{1,0:T(8,128)(2,1)S(1)}, bf16[128,3072]{1,0:T(8,128)(2,1)}, u32[]{:S(2)}, u32[]{:S(2)}) collective-permute-start(bf16[128,3072]{1,0:T(8,128)(2,1)S(1)} %collective-permute-done.9.refs_11_), channel_id=1, source_target_pairs={{0,8},{8,16},{16,24},{24,28},{28,20},{20,12},{12,4},{4,0},{1,9},{9... | collective-permute-start | bytes 2359304 | tf_op jit(solution)/shard_map/ppermute | solution.py:737
  71.7 16.8 %collective-permute-start.14 = (bf16[128,3072]{1,0:T(8,128)(2,1)S(1)}, bf16[128,3072]{1,0:T(8,128)(2,1)}, u32[]{:S(2)}, u32[]{:S(2)}) collective-permute-start(bf16[128,3072]{1,0:T(8,128)(2,1)S(1)} %collective-permute-done.12.refs_4_), channel_id=1, source_target_pairs={{8,0},{16,8},{24,16},{28,24},{20,28},{12,20},{4,12},{0,4},{9,1},{1... | collective-permute-start | bytes 2359304 | tf_op jit(solution)/shard_map/ppermute | solution.py:738
  88.6 20.5 %collective-permute-start.15 = (bf16[128,3072]{1,0:T(8,128)(2,1)}, bf16[128,3072]{1,0:T(8,128)(2,1)S(1)}, u32[]{:S(2)}, u32[]{:S(2)}) collective-permute-start(bf16[128,3072]{1,0:T(8,128)(2,1)} %collective-permute-done.13.refs_10_), channel_id=1, source_target_pairs={{0,8},{8,16},{16,24},{24,28},{28,20},{20,12},{12,4},{4,0},{1,9},{9... | collective-permute-start | bytes 2359304 | tf_op jit(solution)/shard_map/ppermute | solution.py:737
  89.2 19.8 %collective-permute-start.16 = (bf16[128,3072]{1,0:T(8,128)(2,1)}, bf16[128,3072]{1,0:T(8,128)(2,1)S(1)}, u32[]{:S(2)}, u32[]{:S(2)}) collective-permute-start(bf16[128,3072]{1,0:T(8,128)(2,1)} %collective-permute-done.14.refs_5_), channel_id=1, source_target_pairs={{8,0},{16,8},{24,16},{28,24},{20,28},{12,20},{4,12},{0,4},{9,1},{1... | collective-permute-start | bytes 2359304 | tf_op jit(solution)/shard_map/ppermute | solution.py:738
  93.1 26.9 %collective-permute-start.20 = (bf16[512,1024]{1,0:T(8,128)(2,1)S(1)}, bf16[512,1024]{1,0:T(8,128)(2,1)S(1)}, u32[]{:S(2)}, u32[]{:S(2)}) collective-permute-start(bf16[512,1024]{1,0:T(8,128)(2,1)S(1)} %add_convert_fusion.15), channel_id=1, source_target_pairs={{0,2},{1,3},{2,0},{3,1},{4,6},{5,7},{6,4},{7,5},{8,10},{9,11},{10,... | collective-permute-start | bytes 3145736 | tf_op jit(solution)/shard_map/ppermute | solution.py:808
  121.0 19.5 %collective-permute-start.22 = (bf16[128,3072]{1,0:T(8,128)(2,1)S(1)}, bf16[128,3072]{1,0:T(8,128)(2,1)S(1)}, u32[]{:S(2)}, u32[]{:S(2)}) collective-permute-start(bf16[128,3072]{1,0:T(8,128)(2,1)S(1)} %copy-done.11), channel_id=1, source_target_pairs={{8,0},{16,8},{24,16},{28,24},{20,28},{12,20},{4,12},{0,4},{9,1},{1... | collective-permute-start | bytes 2359304 | tf_op jit(solution)/shard_map/ppermute | solution.py:738
  122.3 19.4 %collective-permute-start.21 = (bf16[128,3072]{1,0:T(8,128)(2,1)S(1)}, bf16[128,3072]{1,0:T(8,128)(2,1)S(1)}, u32[]{:S(2)}, u32[]{:S(2)}) collective-permute-start(bf16[128,3072]{1,0:T(8,128)(2,1)S(1)} %copy-done.11), channel_id=1, source_target_pairs={{0,8},{8,16},{16,24},{24,28},{28,20},{20,12},{12,4},{4,0},{1,9},{9... | collective-permute-start | bytes 2359304 | tf_op jit(solution)/shard_map/ppermute | solution.py:737
  124.6 17.2 %collective-permute-start.25 = (bf16[256,1024]{1,0:T(8,128)(2,1)S(1)}, bf16[256,1024]{1,0:T(8,128)(2,1)S(1)}, u32[]{:S(2)}, u32[]{:S(2)}) collective-permute-start(bf16[256,1024]{1,0:T(8,128)(2,1)S(1)} %get-tuple-element.242), channel_id=1, source_target_pairs={{0,2},{1,3},{2,0},{3,1},{4,6},{5,7},{6,4},{7,5},{8,10},{9,11},{10,... | collective-permute-start | bytes 1572872 | tf_op jit(solution)/shard_map/ppermute | solution.py:808
  141.7 20.5 %collective-permute-start.29 = (bf16[512,1024]{1,0:T(8,128)(2,1)}, bf16[512,1024]{1,0:T(8,128)(2,1)S(1)}, u32[]{:S(2)}, u32[]{:S(2)}) collective-permute-start(bf16[512,1024]{1,0:T(8,128)(2,1)} %get-tuple-element.251), channel_id=1, source_target_pairs={{0,1},{1,0},{2,3},{3,2},{4,5},{5,4},{6,7},{7,6},{8,9},{9,8},{10,11... | collective-permute-start | bytes 3145736 | tf_op jit(solution)/shard_map/ppermute | solution.py:793
  141.7 20.5 %collective-permute-start.30 = (bf16[512,1024]{1,0:T(8,128)(2,1)}, bf16[512,1024]{1,0:T(8,128)(2,1)S(1)}, u32[]{:S(2)}, u32[]{:S(2)}) collective-permute-start(bf16[512,1024]{1,0:T(8,128)(2,1)} %get-tuple-element.253), channel_id=1, source_target_pairs={{0,1},{1,0},{2,3},{3,2},{4,5},{5,4},{6,7},{7,6},{8,9},{9,8},{10,11... | collective-permute-start | bytes 3145736 | tf_op jit(solution)/shard_map/ppermute | solution.py:793
  142.2 19.5 %collective-permute-start.26 = (bf16[128,3072]{1,0:T(8,128)(2,1)S(1)}, bf16[128,3072]{1,0:T(8,128)(2,1)S(1)}, u32[]{:S(2)}, u32[]{:S(2)}) collective-permute-start(bf16[128,3072]{1,0:T(8,128)(2,1)S(1)} %collective-permute-done.21.refs_11_), channel_id=1, source_target_pairs={{0,8},{8,16},{16,24},{24,28},{28,20},{20,12},{12,4},{4,0},{1,9},{9... | collective-permute-start | bytes 2359304 | tf_op jit(solution)/shard_map/ppermute | solution.py:737
  143.0 19.2 %collective-permute-start.27 = (bf16[128,3072]{1,0:T(8,128)(2,1)S(1)}, bf16[128,3072]{1,0:T(8,128)(2,1)S(1)}, u32[]{:S(2)}, u32[]{:S(2)}) collective-permute-start(bf16[128,3072]{1,0:T(8,128)(2,1)S(1)} %collective-permute-done.22.refs_4_), channel_id=1, source_target_pairs={{8,0},{16,8},{24,16},{28,24},{20,28},{12,20},{4,12},{0,4},{9,1},{1... | collective-permute-start | bytes 2359304 | tf_op jit(solution)/shard_map/ppermute | solution.py:738
  144.3 15.4 %collective-permute-start.28 = (bf16[256,1024]{1,0:T(8,128)(2,1)S(1)}, bf16[256,1024]{1,0:T(8,128)(2,1)}, u32[]{:S(2)}, u32[]{:S(2)}) collective-permute-start(bf16[256,1024]{1,0:T(8,128)(2,1)S(1)} %copy-done.74), channel_id=1, source_target_pairs={{0,2},{1,3},{2,0},{3,1},{4,6},{5,7},{6,4},{7,5},{8,10},{9,11},{10,... | collective-permute-start | bytes 1572872 | tf_op jit(solution)/shard_map/ppermute | solution.py:808
  163.3 19.3 %collective-permute-start.31 = (bf16[128,3072]{1,0:T(8,128)(2,1)S(1)}, bf16[128,3072]{1,0:T(8,128)(2,1)S(1)}, u32[]{:S(2)}, u32[]{:S(2)}) collective-permute-start(bf16[128,3072]{1,0:T(8,128)(2,1)S(1)} %collective-permute-done.26.refs_10_), channel_id=1, source_target_pairs={{0,8},{8,16},{16,24},{24,28},{28,20},{20,12},{12,4},{4,0},{1,9},{9... | collective-permute-start | bytes 2359304 | tf_op jit(solution)/shard_map/ppermute | solution.py:737
  164.6 18.1 %collective-permute-start.32 = (bf16[128,3072]{1,0:T(8,128)(2,1)S(1)}, bf16[128,3072]{1,0:T(8,128)(2,1)S(1)}, u32[]{:S(2)}, u32[]{:S(2)}) collective-permute-start(bf16[128,3072]{1,0:T(8,128)(2,1)S(1)} %collective-permute-done.27.refs_5_), channel_id=1, source_target_pairs={{8,0},{16,8},{24,16},{28,24},{20,28},{12,20},{4,12},{0,4},{9,1},{1... | collective-permute-start | bytes 2359304 | tf_op jit(solution)/shard_map/ppermute | solution.py:738
  166.8 15.9 %collective-permute-start.34 = (bf16[512,1024]{1,0:T(8,128)(2,1)S(1)}, bf16[512,1024]{1,0:T(8,128)(2,1)S(1)}, u32[]{:S(2)}, u32[]{:S(2)}) collective-permute-start(bf16[512,1024]{1,0:T(8,128)(2,1)S(1)} %add_convert_fusion.11.refs_0_.att0.refs_4_), channel_id=1, source_target_pairs={{0,1},{1,0},{2,3},{3,2},{4,5},{5,4},{6,7},{7,6},{8,9},{9,8},{10,11... | collective-permute-start | bytes 3145736 | tf_op jit(solution)/shard_map/ppermute | solution.py:814
  167.7 14.8 %collective-permute-start.33 = (bf16[256,1024]{1,0:T(8,128)(2,1)S(1)}, bf16[256,1024]{1,0:T(8,128)(2,1)S(1)}, u32[]{:S(2)}, u32[]{:S(2)}) collective-permute-start(bf16[256,1024]{1,0:T(8,128)(2,1)S(1)} %get-tuple-element.264), channel_id=1, source_target_pairs={{0,2},{1,3},{2,0},{3,1},{4,6},{5,7},{6,4},{7,5},{8,10},{9,11},{10,... | collective-permute-start | bytes 1572872 | tf_op jit(solution)/shard_map/ppermute | solution.py:808
  182.6 21.4 %collective-permute-start.39 = (bf16[256,1024]{1,0:T(8,128)(2,1)S(1)}, bf16[256,1024]{1,0:T(8,128)(2,1)S(1)}, u32[]{:S(2)}, u32[]{:S(2)}) collective-permute-start(bf16[256,1024]{1,0:T(8,128)(2,1)S(1)} %get-tuple-element.274), channel_id=1, source_target_pairs={{0,2},{1,3},{2,0},{3,1},{4,6},{5,7},{6,4},{7,5},{8,10},{9,11},{10,... | collective-permute-start | bytes 1572872 | tf_op jit(solution)/shard_map/ppermute | solution.py:808
  184.3 12.7 %collective-permute-start.35 = (bf16[64,3072]{1,0:T(8,128)(2,1)}, bf16[64,3072]{1,0:T(8,128)(2,1)S(1)}, u32[]{:S(2)}, u32[]{:S(2)}) collective-permute-start(bf16[64,3072]{1,0:T(8,128)(2,1)} %get-tuple-element.267), channel_id=1, source_target_pairs={{0,8},{8,16},{16,24},{24,28},{28,20},{20,12},{12,4},{4,0},{1,9},{9... | collective-permute-start | bytes 1179656 | tf_op jit(solution)/shard_map/ppermute | solution.py:774
  186.7 16.3 %collective-permute-start.37 = (bf16[64,3072]{1,0:T(8,128)(2,1)S(1)}, bf16[64,3072]{1,0:T(8,128)(2,1)S(1)}, u32[]{:S(2)}, u32[]{:S(2)}) collective-permute-start(bf16[64,3072]{1,0:T(8,128)(2,1)S(1)} %slice.151), channel_id=1, source_target_pairs={{0,8},{8,16},{16,24},{24,28},{28,20},{20,12},{12,4},{4,0},{1,9},{9... | collective-permute-start | bytes 1179656 | tf_op jit(solution)/shard_map/ppermute | solution.py:737
  188.4 15.6 %collective-permute-start.38 = (bf16[64,3072]{1,0:T(8,128)(2,1)S(1)}, bf16[64,3072]{1,0:T(8,128)(2,1)S(1)}, u32[]{:S(2)}, u32[]{:S(2)}) collective-permute-start(bf16[64,3072]{1,0:T(8,128)(2,1)S(1)} %slice.152), channel_id=1, source_target_pairs={{8,0},{16,8},{24,16},{28,24},{20,28},{12,20},{4,12},{0,4},{9,1},{1... | collective-permute-start | bytes 1179656 | tf_op jit(solution)/shard_map/ppermute | solution.py:738
  204.1 20.7 %collective-permute-start.40 = (bf16[128,3072]{1,0:T(8,128)(2,1)}, bf16[128,3072]{1,0:T(8,128)(2,1)S(1)}, u32[]{:S(2)}, u32[]{:S(2)}) collective-permute-start(bf16[128,3072]{1,0:T(8,128)(2,1)} %get-tuple-element.275), channel_id=1, source_target_pairs={{0,8},{8,16},{16,24},{24,28},{28,20},{20,12},{12,4},{4,0},{1,9},{9... | collective-permute-start | bytes 2359304 | tf_op jit(solution)/shard_map/ppermute | solution.py:774
  206.2 20.6 %collective-permute-start.42 = (bf16[512,1024]{1,0:T(8,128)(2,1)S(1)}, bf16[512,1024]{1,0:T(8,128)(2,1)S(1)}, u32[]{:S(2)}, u32[]{:S(2)}) collective-permute-start(bf16[512,1024]{1,0:T(8,128)(2,1)S(1)} %add_convert_fusion.10.dh0), channel_id=1, source_target_pairs={{0,1},{1,0},{2,3},{3,2},{4,5},{5,4},{6,7},{7,6},{8,9},{9,8},{10,11... | collective-permute-start | bytes 3145736 | tf_op jit(solution)/shard_map/ppermute | solution.py:814
  207.7 19.1 %collective-permute-start.41 = (bf16[128,3072]{1,0:T(8,128)(2,1)S(1)}, bf16[128,3072]{1,0:T(8,128)(2,1)}, u32[]{:S(2)}, u32[]{:S(2)}) collective-permute-start(bf16[128,3072]{1,0:T(8,128)(2,1)S(1)} %copy-done.65), channel_id=1, source_target_pairs={{8,0},{16,8},{24,16},{28,24},{20,28},{12,20},{4,12},{0,4},{9,1},{1... | collective-permute-start | bytes 2359304 | tf_op jit(solution)/shard_map/ppermute | solution.py:775
  209.1 15.8 %collective-permute-start.43 = (bf16[256,1024]{1,0:T(8,128)(2,1)}, bf16[256,1024]{1,0:T(8,128)(2,1)S(1)}, u32[]{:S(2)}, u32[]{:S(2)}) collective-permute-start(bf16[256,1024]{1,0:T(8,128)(2,1)} %get-tuple-element.283), channel_id=1, source_target_pairs={{0,2},{1,3},{2,0},{3,1},{4,6},{5,7},{6,4},{7,5},{8,10},{9,11},{10,... | collective-permute-start | bytes 1572872 | tf_op jit(solution)/shard_map/ppermute | solution.py:808
  226.8 19.5 %collective-permute-start.44 = (bf16[128,3072]{1,0:T(8,128)(2,1)S(1)}, bf16[128,3072]{1,0:T(8,128)(2,1)}, u32[]{:S(2)}, u32[]{:S(2)}) collective-permute-start(bf16[128,3072]{1,0:T(8,128)(2,1)S(1)} %add_convert_fusion.23), channel_id=1, source_target_pairs={{0,8},{8,16},{16,24},{24,28},{28,20},{20,12},{12,4},{4,0},{1,9},{9... | collective-permute-start | bytes 2359304 | tf_op jit(solution)/shard_map/ppermute | solution.py:774
  228.2 19.5 %collective-permute-start.47 = (bf16[512,1024]{1,0:T(8,128)(2,1)}, bf16[512,1024]{1,0:T(8,128)(2,1)S(1)}, u32[]{:S(2)}, u32[]{:S(2)}) collective-permute-start(bf16[512,1024]{1,0:T(8,128)(2,1)} %get-tuple-element.293), channel_id=1, source_target_pairs={{0,1},{1,0},{2,3},{3,2},{4,5},{5,4},{6,7},{7,6},{8,9},{9,8},{10,11... | collective-permute-start | bytes 3145736 | tf_op jit(solution)/shard_map/ppermute | solution.py:793
  228.2 22.6 %collective-permute-start.48 = (bf16[512,1024]{1,0:T(8,128)(2,1)}, bf16[512,1024]{1,0:T(8,128)(2,1)S(1)}, u32[]{:S(2)}, u32[]{:S(2)}) collective-permute-start(bf16[512,1024]{1,0:T(8,128)(2,1)} %get-tuple-element.295), channel_id=1, source_target_pairs={{0,1},{1,0},{2,3},{3,2},{4,5},{5,4},{6,7},{7,6},{8,9},{9,8},{10,11... | collective-permute-start | bytes 3145736 | tf_op jit(solution)/shard_map/ppermute | solution.py:793
  230.1 18.1 %collective-permute-start.46 = (bf16[256,1024]{1,0:T(8,128)(2,1)}, bf16[256,1024]{1,0:T(8,128)(2,1)}, u32[]{:S(2)}, u32[]{:S(2)}) collective-permute-start(bf16[256,1024]{1,0:T(8,128)(2,1)} %get-tuple-element.292), channel_id=1, source_target_pairs={{0,2},{1,3},{2,0},{3,1},{4,6},{5,7},{6,4},{7,5},{8,10},{9,11},{10,... | collective-permute-start | bytes 1572872 | tf_op jit(solution)/shard_map/ppermute | solution.py:808
  231.6 19.2 %collective-permute-start.45 = (bf16[128,3072]{1,0:T(8,128)(2,1)S(1)}, bf16[128,3072]{1,0:T(8,128)(2,1)S(1)}, u32[]{:S(2)}, u32[]{:S(2)}) collective-permute-start(bf16[128,3072]{1,0:T(8,128)(2,1)S(1)} %add_convert_fusion.22), channel_id=1, source_target_pairs={{8,0},{16,8},{24,16},{28,24},{20,28},{12,20},{4,12},{0,4},{9,1},{1... | collective-permute-start | bytes 2359304 | tf_op jit(solution)/shard_map/ppermute | solution.py:775
  250.8 27.8 %collective-permute-start.51 = (bf16[512,1024]{1,0:T(8,128)(2,1)S(1)}, bf16[512,1024]{1,0:T(8,128)(2,1)S(1)}, u32[]{:S(2)}, u32[]{:S(2)}) collective-permute-start(bf16[512,1024]{1,0:T(8,128)(2,1)S(1)} %add_convert_fusion.8), channel_id=1, source_target_pairs={{0,2},{1,3},{2,0},{3,1},{4,6},{5,7},{6,4},{7,5},{8,10},{9,11},{10,... | collective-permute-start | bytes 3145736 | tf_op jit(solution)/shard_map/ppermute | solution.py:808
  251.6 27.1 %collective-permute-start.52 = (bf16[128,3072]{1,0:T(8,128)(2,1)S(1)}, bf16[128,3072]{1,0:T(8,128)(2,1)S(1)}, u32[]{:S(2)}, u32[]{:S(2)}) collective-permute-start(bf16[128,3072]{1,0:T(8,128)(2,1)S(1)} %add_convert_fusion.21), channel_id=1, source_target_pairs={{0,8},{8,16},{16,24},{24,28},{28,20},{20,12},{12,4},{4,0},{1,9},{9... | collective-permute-start | bytes 2359304 | tf_op jit(solution)/shard_map/ppermute | solution.py:774
  252.3 26.3 %collective-permute-start.53 = (bf16[128,3072]{1,0:T(8,128)(2,1)S(1)}, bf16[128,3072]{1,0:T(8,128)(2,1)S(1)}, u32[]{:S(2)}, u32[]{:S(2)}) collective-permute-start(bf16[128,3072]{1,0:T(8,128)(2,1)S(1)} %add_convert_fusion.20), channel_id=1, source_target_pairs={{8,0},{16,8},{24,16},{28,24},{20,28},{12,20},{4,12},{0,4},{9,1},{1... | collective-permute-start | bytes 2359304 | tf_op jit(solution)/shard_map/ppermute | solution.py:775
  284.9 21.9 %collective-permute-start.56 = (bf16[128,3072]{1,0:T(8,128)(2,1)}, bf16[128,3072]{1,0:T(8,128)(2,1)S(1)}, u32[]{:S(2)}, u32[]{:S(2)}) collective-permute-start(bf16[128,3072]{1,0:T(8,128)(2,1)} %get-tuple-element.318), channel_id=1, source_target_pairs={{0,8},{8,16},{16,24},{24,28},{28,20},{20,12},{12,4},{4,0},{1,9},{9... | collective-permute-start | bytes 2359304 | tf_op jit(solution)/shard_map/ppermute | solution.py:774
  286.8 20.3 %collective-permute-start.57 = (bf16[128,3072]{1,0:T(8,128)(2,1)S(1)}, bf16[128,3072]{1,0:T(8,128)(2,1)S(1)}, u32[]{:S(2)}, u32[]{:S(2)}) collective-permute-start(bf16[128,3072]{1,0:T(8,128)(2,1)S(1)} %copy-done.64), channel_id=1, source_target_pairs={{8,0},{16,8},{24,16},{28,24},{20,28},{12,20},{4,12},{0,4},{9,1},{1... | collective-permute-start | bytes 2359304 | tf_op jit(solution)/shard_map/ppermute | solution.py:775
  288.1 19.3 %collective-permute-start.58 = (bf16[384,1024]{1,0:T(8,128)(2,1)S(1)}, bf16[384,1024]{1,0:T(8,128)(2,1)S(1)}, u32[]{:S(2)}, u32[]{:S(2)}) collective-permute-start(bf16[384,1024]{1,0:T(8,128)(2,1)S(1)} %slice.157), channel_id=1, source_target_pairs={{0,2},{1,3},{2,0},{3,1},{4,6},{5,7},{6,4},{7,5},{8,10},{9,11},{10,... | collective-permute-start | bytes 2359304 | tf_op jit(solution)/shard_map/ppermute | solution.py:808
  307.4 21.3 %collective-permute-start.59 = (bf16[128,3072]{1,0:T(8,128)(2,1)S(1)}, bf16[128,3072]{1,0:T(8,128)(2,1)S(1)}, u32[]{:S(2)}, u32[]{:S(2)}) collective-permute-start(bf16[128,3072]{1,0:T(8,128)(2,1)S(1)} %add_convert_fusion.19), channel_id=1, source_target_pairs={{0,8},{8,16},{16,24},{24,28},{28,20},{20,12},{12,4},{4,0},{1,9},{9... | collective-permute-start | bytes 2359304 | tf_op jit(solution)/shard_map/ppermute | solution.py:774
  308.3 21.5 %collective-permute-start.61 = (bf16[512,1024]{1,0:T(8,128)(2,1)}, bf16[512,1024]{1,0:T(8,128)(2,1)S(1)}, u32[]{:S(2)}, u32[]{:S(2)}) collective-permute-start(bf16[512,1024]{1,0:T(8,128)(2,1)} %bitcast.16), channel_id=1, source_target_pairs={{0,1},{1,0},{2,3},{3,2},{4,5},{5,4},{6,7},{7,6},{8,9},{9,8},{10,11... | collective-permute-start | bytes 3145736 | tf_op jit(solution)/shard_map/ppermute | solution.py:793
  308.5 22.2 %collective-permute-start.62 = (bf16[128,1024]{1,0:T(8,128)(2,1)S(1)}, bf16[128,1024]{1,0:T(8,128)(2,1)S(1)}, u32[]{:S(2)}, u32[]{:S(2)}) collective-permute-start(bf16[128,1024]{1,0:T(8,128)(2,1)S(1)} %slice.158), channel_id=1, source_target_pairs={{0,2},{1,3},{2,0},{3,1},{4,6},{5,7},{6,4},{7,5},{8,10},{9,11},{10,... | collective-permute-start | bytes 786440 | tf_op jit(solution)/shard_map/ppermute | solution.py:808
  310.1 20.6 %collective-permute-start.60 = (bf16[128,3072]{1,0:T(8,128)(2,1)S(1)}, bf16[128,3072]{1,0:T(8,128)(2,1)S(1)}, u32[]{:S(2)}, u32[]{:S(2)}) collective-permute-start(bf16[128,3072]{1,0:T(8,128)(2,1)S(1)} %add_convert_fusion.18), channel_id=1, source_target_pairs={{8,0},{16,8},{24,16},{28,24},{20,28},{12,20},{4,12},{0,4},{9,1},{1... | collective-permute-start | bytes 2359304 | tf_op jit(solution)/shard_map/ppermute | solution.py:775
  330.7 21.6 %collective-permute-start.65 = (bf16[512,1024]{1,0:T(8,128)(2,1)}, bf16[512,1024]{1,0:T(8,128)(2,1)S(1)}, u32[]{:S(2)}, u32[]{:S(2)}) collective-permute-start(bf16[512,1024]{1,0:T(8,128)(2,1)} %bitcast.18), channel_id=1, source_target_pairs={{0,1},{1,0},{2,3},{3,2},{4,5},{5,4},{6,7},{7,6},{8,9},{9,8},{10,11... | collective-permute-start | bytes 3145736 | tf_op jit(solution)/shard_map/ppermute | solution.py:793
  332.2 20.6 %collective-permute-start.66 = (bf16[384,1024]{1,0:T(8,128)(2,1)S(1)}, bf16[384,1024]{1,0:T(8,128)(2,1)}, u32[]{:S(2)}, u32[]{:S(2)}) collective-permute-start(bf16[384,1024]{1,0:T(8,128)(2,1)S(1)} %slice.159), channel_id=1, source_target_pairs={{0,2},{1,3},{2,0},{3,1},{4,6},{5,7},{6,4},{7,5},{8,10},{9,11},{10,... | collective-permute-start | bytes 2359304 | tf_op jit(solution)/shard_map/ppermute | solution.py:808
  332.8 20.0 %collective-permute-start.63 = (bf16[128,3072]{1,0:T(8,128)(2,1)}, bf16[128,3072]{1,0:T(8,128)(2,1)S(1)}, u32[]{:S(2)}, u32[]{:S(2)}) collective-permute-start(bf16[128,3072]{1,0:T(8,128)(2,1)} %add_convert_fusion.17), channel_id=1, source_target_pairs={{0,8},{8,16},{16,24},{24,28},{28,20},{20,12},{12,4},{4,0},{1,9},{9... | collective-permute-start | bytes 2359304 | tf_op jit(solution)/shard_map/ppermute | solution.py:774
  333.6 19.3 %collective-permute-start.64 = (bf16[128,3072]{1,0:T(8,128)(2,1)}, bf16[128,3072]{1,0:T(8,128)(2,1)S(1)}, u32[]{:S(2)}, u32[]{:S(2)}) collective-permute-start(bf16[128,3072]{1,0:T(8,128)(2,1)} %add_convert_fusion.16), channel_id=1, source_target_pairs={{8,0},{16,8},{24,16},{28,24},{20,28},{12,20},{4,12},{0,4},{9,1},{1... | collective-permute-start | bytes 2359304 | tf_op jit(solution)/shard_map/ppermute | solution.py:775
  336.2 16.1 %collective-permute-start.68 = (f32[4,1024]{1,0:T(4,128)S(1)}, f32[4,1024]{1,0:T(4,128)S(1)}, u32[]{:S(2)}, u32[]{:S(2)}) collective-permute-start(f32[4,1024]{1,0:T(4,128)S(1)} %fusion.1), channel_id=1, source_target_pairs={{0,2},{1,3},{2,0},{3,1},{4,6},{5,7},{6,4},{7,5},{8,10},{9,11},{10,... | collective-permute-start | bytes 49160 | tf_op jit(solution)/shard_map/ppermute | solution.py:980
  353.3 12.4 %collective-permute-start.71 = (bf16[512,1024]{1,0:T(8,128)(2,1)S(1)}, bf16[512,1024]{1,0:T(8,128)(2,1)S(1)}, u32[]{:S(2)}, u32[]{:S(2)}) collective-permute-start(bf16[512,1024]{1,0:T(8,128)(2,1)S(1)} %add_convert_fusion.2.refs_6_), channel_id=1, source_target_pairs={{0,1},{1,0},{2,3},{3,2},{4,5},{5,4},{6,7},{7,6},{8,9},{9,8},{10,11... | collective-permute-start | bytes 3145736 | tf_op jit(solution)/shard_map/ppermute | solution.py:814
  365.7 15.5 %collective-permute-start.74 = (bf16[256,1024]{1,0:T(8,128)(2,1)}, bf16[256,1024]{1,0:T(8,128)(2,1)S(1)}, u32[]{:S(2)}, u32[]{:S(2)}) collective-permute-start(bf16[256,1024]{1,0:T(8,128)(2,1)} %get-tuple-element.380), channel_id=1, source_target_pairs={{0,8},{8,16},{16,24},{24,28},{28,20},{20,12},{12,4},{4,0},{1,9},{9... | collective-permute-start | bytes 1572872 | tf_op jit(solution)/shard_map/ppermute | solution.py:774
  368.4 16.6 %collective-permute-start.76 = (bf16[512,1024]{1,0:T(8,128)(2,1)S(1)}, bf16[512,1024]{1,0:T(8,128)(2,1)S(1)}, u32[]{:S(2)}, u32[]{:S(2)}) collective-permute-start(bf16[512,1024]{1,0:T(8,128)(2,1)S(1)} %add_convert_fusion.1.mine), channel_id=1, source_target_pairs={{0,1},{1,0},{2,3},{3,2},{4,5},{5,4},{6,7},{7,6},{8,9},{9,8},{10,11... | collective-permute-start | bytes 3145736 | tf_op jit(solution)/shard_map/ppermute | solution.py:814
  368.5 12.7 %collective-permute-start.77 = (f32[4,1024]{1,0:T(4,128)S(1)}, f32[4,1024]{1,0:T(4,128)S(1)}, u32[]{:S(2)}, u32[]{:S(2)}) collective-permute-start(f32[4,1024]{1,0:T(4,128)S(1)} %add.167), channel_id=1, source_target_pairs={{0,8},{4,12},{8,0},{12,4},{16,24},{20,28},{24,16},{28,20},{1,9},{5... | collective-permute-start | bytes 49160 | tf_op jit(solution)/shard_map/ppermute | solution.py:980
  369.1 14.4 %collective-permute-start.75 = (bf16[256,1024]{1,0:T(8,128)(2,1)S(1)}, bf16[256,1024]{1,0:T(8,128)(2,1)S(1)}, u32[]{:S(2)}, u32[]{:S(2)}) collective-permute-start(bf16[256,1024]{1,0:T(8,128)(2,1)S(1)} %copy-done.70), channel_id=1, source_target_pairs={{8,0},{16,8},{24,16},{28,24},{20,28},{12,20},{4,12},{0,4},{9,1},{1... | collective-permute-start | bytes 1572872 | tf_op jit(solution)/shard_map/ppermute | solution.py:775
  371.3 13.8 %collective-permute-start.78 = (bf16[256,1024]{1,0:T(8,128)(2,1)S(1)}, bf16[256,1024]{1,0:T(8,128)(2,1)S(1)}, u32[]{:S(2)}, u32[]{:S(2)}) collective-permute-start(bf16[256,1024]{1,0:T(8,128)(2,1)S(1)} %get-tuple-element.386), channel_id=1, source_target_pairs={{0,2},{1,3},{2,0},{3,1},{4,6},{5,7},{6,4},{7,5},{8,10},{9,11},{10,... | collective-permute-start | bytes 1572872 | tf_op jit(solution)/shard_map/ppermute | solution.py:808
  385.0 14.2 %collective-permute-start.79 = (bf16[256,1024]{1,0:T(8,128)(2,1)S(1)}, bf16[256,1024]{1,0:T(8,128)(2,1)S(1)}, u32[]{:S(2)}, u32[]{:S(2)}) collective-permute-start(bf16[256,1024]{1,0:T(8,128)(2,1)S(1)} %add_convert_fusion.27), channel_id=1, source_target_pairs={{0,8},{8,16},{16,24},{24,28},{28,20},{20,12},{12,4},{4,0},{1,9},{9... | collective-permute-start | bytes 1572872 | tf_op jit(solution)/shard_map/ppermute | solution.py:774
  385.3 14.0 %collective-permute-start.80 = (bf16[256,1024]{1,0:T(8,128)(2,1)S(1)}, bf16[256,1024]{1,0:T(8,128)(2,1)S(1)}, u32[]{:S(2)}, u32[]{:S(2)}) collective-permute-start(bf16[256,1024]{1,0:T(8,128)(2,1)S(1)} %add_convert_fusion.26), channel_id=1, source_target_pairs={{8,0},{16,8},{24,16},{28,24},{20,28},{12,20},{4,12},{0,4},{9,1},{1... | collective-permute-start | bytes 1572872 | tf_op jit(solution)/shard_map/ppermute | solution.py:775
  401.3 14.3 %collective-permute-start.84 = (bf16[256,1024]{1,0:T(8,128)(2,1)}, bf16[256,1024]{1,0:T(8,128)(2,1)S(1)}, u32[]{:S(2)}, u32[]{:S(2)}) collective-permute-start(bf16[256,1024]{1,0:T(8,128)(2,1)} %add_convert_fusion.25), channel_id=1, source_target_pairs={{0,8},{8,16},{16,24},{24,28},{28,20},{20,12},{12,4},{4,0},{1,9},{9... | collective-permute-start | bytes 1572872 | tf_op jit(solution)/shard_map/ppermute | solution.py:774
  402.0 13.9 %collective-permute-start.85 = (bf16[256,1024]{1,0:T(8,128)(2,1)S(1)}, bf16[256,1024]{1,0:T(8,128)(2,1)}, u32[]{:S(2)}, u32[]{:S(2)}) collective-permute-start(bf16[256,1024]{1,0:T(8,128)(2,1)S(1)} %add_convert_fusion.24), channel_id=1, source_target_pairs={{8,0},{16,8},{24,16},{28,24},{20,28},{12,20},{4,12},{0,4},{9,1},{1... | collective-permute-start | bytes 1572872 | tf_op jit(solution)/shard_map/ppermute | solution.py:775
  (110 other events, 825.9 us)

commit v9 on v8

--- a/solution.py
+++ b/solution.py
@@ -44,7 +44,7 @@
         out_shape=outs,
         input_output_aliases=alias or {},
         compiler_params=pltpu.CompilerParams(vmem_limit_bytes=56 * MIB),
-        cost_estimate=pl.CostEstimate(flops=1, bytes_accessed=1, transcendentals=0),
+        cost_estimate=pl.CostEstimate(flops=500000000, bytes_accessed=1, transcendentals=0),
     )(*args)
 
 
@@ -870,7 +870,7 @@
         for chore in chores[:2]:
             chore()
         del chores[:2]
-        if steps:
+        if steps and k != 2:
             small = gain_step(small)
         close(small, *moved, *[v[-1] for v in (ffn_own, x, g) if v])
     while steps:

time: 427 us -> 425 us (level)
    ppermute x12, waiting for transfers between devices: 37.5 us -> 19.7 us  [step(): self.a.append(lax.ppermute(self.rounds.now(a), 'dp', self.ring.ahead))]
    ppermute x3, waiting for transfers between devices: 10.9 us -> 27.5 us  [gain_step(): other = lax.ppermute(now(value), axis, moves)]
  transfers between devices with their start and end apart: 86 -> 86, of which waited for: 32 -> 32; matrix products, arithmetic and copies ran while one was open for 8% -> 8% of each run, Pallas kernels for 47% -> 48%
where the time goes in v9:
time: 425 us; the launch traced here: 417 us
  Pallas kernels  203 us (48%)
  waiting for transfers between devices  87 us (20%)
  starting transfers between devices  83.2 us (20%)
  local copies, waits for them, and re-layouts  22.3 us (5%)
  other arithmetic  18.5 us (4%)
    pallas_call x23, Pallas kernels, kernel_call(): pl.pallas_call(body, grid_spec=spec, out_shape=outs, input_output_aliases...  203 us
    ppermute x3, waiting for transfers between devices, gain_step(): other = lax.ppermute(now(value), axis, moves)  27.5 us
    ppermute x12, waiting for transfers between devices, step(): self.a.append(lax.ppermute(self.rounds.now(a), 'dp', self.ring.ahead))  19.7 us
    ppermute x14, starting transfers between devices, far(): self.got.append(lax.ppermute(moved, 'mp', self.far_moves))  19.2 us
    ppermute x12, starting transfers between devices, step(): self.b = lax.ppermute(self.rounds.now(self.b), 'dp', self.ring.behind)  14.6 us
    ppermute x12, starting transfers between devices, step(): self.b.append(lax.ppermute(self.rounds.now(b), 'dp', self.ring.behind))  12.9 us
    ppermute x12, starting transfers between devices, step(): self.a.append(lax.ppermute(self.rounds.now(a), 'dp', self.ring.ahead))  12.9 us
    ppermute x12, waiting for transfers between devices, step(): self.a = lax.ppermute(self.rounds.now(self.a), 'dp', self.ring.ahead)  12.8 us
  transfers between devices with their start and end apart: 86, of which 32 were waited for; matrix products, arithmetic and copies ran while one was open for 8% of the time, Pallas kernels for 48%

profile of v9, /device:TPU:0, one launch (start us, length us, event | category | flops | bytes accessed | tf_op | source)
XLA Modules:
  0.0 417.1 jit_solution(9416204806288242983)
XLA Ops:
  0.6 2.0 shard_map.203.refs_2_.refs_3_.refs_0_
  2.7 3.0 collective-permute-start.2
  6.4 2.0 collective-permute-start
  8.4 3.1 slice_bitcast_fusion.3.refs_0_.x_ref.x0
  11.5 2.1 shard_map.204.refs_3_
  13.6 5.7 %collective-permute-done = f32[1,4,128]{2,1,0:T(4,128)S(1)} collective-permute-done((f32[1,4,128]{2,1,0:T(4,128)S(1)}, f32[1,4,128]{2,1,0:T(4,128)S(1)}, u32[]{:S(2)}, u32[]{:S(2)}) %collective-permute-start) | collective-permute-done | bytes 2080 | tf_op jit(solution)/shard_map/ppermute | solution.py:850
  19.6 1.8 collective-permute-start.5
  21.7 3.3 slice_bitcast_fusion.2.refs_0_.x_ref.x1
  25.0 2.1 shard_map.205.refs_3_
  27.1 5.2 %collective-permute-done.3 = f32[2,4,128]{2,1,0:T(4,128)S(1)} collective-permute-done((f32[2,4,128]{2,1,0:T(4,128)S(1)}, f32[2,4,128]{2,1,0:T(4,128)S(1)}, u32[]{:S(2)}, u32[]{:S(2)}) %collective-permute-start.3) | collective-permute-done | bytes 4128 | tf_op jit(solution)/shard_map/ppermute | solution.py:850
  34.7 2.5 slice_bitcast_fusion
  37.2 6.7 %collective-permute-done.6.refs_7_.refs_8_.refs_5_ = bf16[256,1024]{1,0:T(8,128)(2,1)S(1)} collective-permute-done((bf16[256,1024]{1,0:T(8,128)(2,1)S(1)}, bf16[256,1024]{1,0:T(8,128)(2,1)S(1)}, u32[]{:S(2)}, u32[]{:S(2)}) %collective-permute-start.6) | collective-permute-done | bytes 524320 | tf_op jit(solution)/shard_map/ppermute | solution.py:737
  43.9 1.9 collective-permute-done.7.refs_5_.refs_6_.refs_3_
  49.3 1.8 collective-permute-start.10
  51.3 2.5 collective-permute-start.9
  53.8 16.7 %collective-permute-done.9 = f32[4,4,128]{2,1,0:T(4,128)S(1)} collective-permute-done((f32[4,4,128]{2,1,0:T(4,128)S(1)}, f32[4,4,128]{2,1,0:T(4,128)S(1)}, u32[]{:S(2)}, u32[]{:S(2)}) %collective-permute-start.9) | collective-permute-done | bytes 8224 | tf_op jit(solution)/shard_map/ppermute | solution.py:850
  71.1 1.6 collective-permute-start.14
  73.9 14.0 %shard_map.206 = (bf16[1024,1024]{1,0:T(8,128)(2,1)}, bf16[1024,768]{1,0:T(8,128)(2,1)}, bf16[1024,256]{1,0:T(8,128)(2,1)}, bf16[512,1024]{1,0:T(8,128)(2,1)}, bf16[512,1024]{1,0:T(8,128)(2,1)}) custom-call(s32[9]{0:T(128)} %pad_add_fusion.places._, bf16[1024,1024]{1,0:T(8,128)(2,1)} %slice_bitcast_fusion.3.refs_0_.x_ref.x0, ...), custom_call_target="tpu_custom_call" | custom-call | flops 500000000 | bytes 1 | tf_op jit(solution)/shard_map/pallas_call | solution.py:41
  88.5 1.6 collective-permute-start.16
  90.9 1.6 add_convert_fusion.15
  92.5 1.6 collective-permute-start.20
  94.1 13.0 %shard_map.207 = (bf16[1024,1024]{1,0:T(8,128)(2,1)}, bf16[1024,768]{1,0:T(8,128)(2,1)}, bf16[1024,256]{1,0:T(8,128)(2,1)}, bf16[512,1024]{1,0:T(8,128)(2,1)}, bf16[512,1024]{1,0:T(8,128)(2,1)}) custom-call(s32[9]{0:T(128)} %pad_add_fusion.places._, bf16[1024,1024]{1,0:T(8,128)(2,1)} %slice_bitcast_fusion.2.refs_0_.x_ref.x1, ...), custom_call_target="tpu_custom_call" | custom-call | flops 500000000 | bytes 1 | tf_op jit(solution)/shard_map/pallas_call | solution.py:41
  108.5 1.5 collective-permute-start.17
  110.5 8.3 %collective-permute-done.17.refs_7_ = bf16[64,3072]{1,0:T(8,128)(2,1)S(1)} collective-permute-done((bf16[64,3072]{1,0:T(8,128)(2,1)S(1)}, bf16[64,3072]{1,0:T(8,128)(2,1)S(1)}, u32[]{:S(2)}, u32[]{:S(2)}) %collective-permute-start.17) | collective-permute-done | bytes 393248 | tf_op jit(solution)/shard_map/ppermute | solution.py:737
  121.6 1.6 collective-permute-start.21
  124.6 1.6 collective-permute-start.25
  126.2 14.0 %shard_map.208 = (bf16[1024,1024]{1,0:T(8,128)(2,1)}, bf16[1024,1024]{1,0:T(8,128)(2,1)}, bf16[1024,2048]{1,0:T(8,128)(2,1)}, bf16[512,1024]{1,0:T(8,128)(2,1)}, bf16[512,1024]{1,0:T(8,128)(2,1)}) custom-call(s32[9]{0:T(128)} %pad_add_fusion.places._, bf16[1024,1024]{1,0:T(8,128)(2,1)} %slice_bitcast_fusion.3.refs_0_.x_ref.x0, bf16[512,1024]{1,0:T(8,128)(2,1)} %copy-done.6, ...), custom_call_target="tpu_custom_call" | custom-call | flops 500000000 | bytes 1 | tf_op jit(solution)/shard_map/pallas_call | solution.py:41
  145.1 13.8 %shard_map.209 = (bf16[1024,1024]{1,0:T(8,128)(2,1)}, bf16[1024,1024]{1,0:T(8,128)(2,1)}, bf16[1024,2048]{1,0:T(8,128)(2,1)}, bf16[512,1024]{1,0:T(8,128)(2,1)}, bf16[512,1024]{1,0:T(8,128)(2,1)}) custom-call(s32[9]{0:T(128)} %pad_add_fusion.places._, ...), custom_call_target="tpu_custom_call", output_to_operand_aliasing={{0}: (14, {}), {1}: (15, {}), {2}: (16, {})} | custom-call | flops 500000000 | bytes 1 | tf_op jit(solution)/shard_map/pallas_call | solution.py:41
  159.0 2.1 collective-permute-done.26.refs_10_
  163.3 1.6 collective-permute-start.31
  169.3 13.3 %shard_map.210 = (bf16[128,3072]{1,0:T(8,128)(2,1)}, bf16[128,3072]{1,0:T(8,128)(2,1)}, bf16[128,3072]{1,0:T(8,128)(2,1)}, bf16[128,3072]{1,0:T(8,128)(2,1)}, bf...) custom-call(s32[9]{0:T(128)} %pad_add_fusion.places._, ...), custom_call_target="tpu_custom_call" | custom-call | flops 500000000 | bytes 1 | tf_op jit(solution)/shard_map/pallas_call | solution.py:41
  183.0 1.6 collective-permute-start.39
  189.1 8.1 %collective-permute-done.35.a = bf16[64,3072]{1,0:T(8,128)(2,1)S(1)} collective-permute-done((bf16[64,3072]{1,0:T(8,128)(2,1)}, bf16[64,3072]{1,0:T(8,128)(2,1)S(1)}, u32[]{:S(2)}, u32[]{:S(2)}) %collective-permute-start.35) | collective-permute-done | bytes 393248 | tf_op jit(solution)/shard_map/ppermute | solution.py:774
  198.5 2.3 shard_map.211
  200.9 2.1 collective-permute-done.37.refs_7_
  210.8 14.1 %shard_map.212 = (bf16[1024,1024]{1,0:T(8,128)(2,1)}, bf16[1024,1024]{1,0:T(8,128)(2,1)}, bf16[1024,2048]{1,0:T(8,128)(2,1)}, bf16[512,1024]{1,0:T(8,128)(2,1)}, bf16[512,1024]{1,0:T(8,128)(2,1)}) custom-call(s32[9]{0:T(128)} %pad_add_fusion.places._, bf16[1024,1024]{1,0:T(8,128)(2,1)} %slice_bitcast_fusion.2.refs_0_.x_ref.x1, bf16[512,1024]{1,0:T(8,128)(2,1)} %copy-done.2, ...), custom_call_target="tpu_custom_call" | custom-call | flops 500000000 | bytes 1 | tf_op jit(solution)/shard_map/pallas_call | solution.py:41
  226.7 1.6 collective-permute-start.46
  229.6 14.0 %shard_map.213 = (bf16[1024,1024]{1,0:T(8,128)(2,1)}, bf16[1024,1024]{1,0:T(8,128)(2,1)}, bf16[1024,2048]{1,0:T(8,128)(2,1)}, bf16[512,1024]{1,0:T(8,128)(2,1)}, bf16[512,1024]{1,0:T(8,128)(2,1)}) custom-call(s32[9]{0:T(128)} %pad_add_fusion.places._, ...), custom_call_target="tpu_custom_call", output_to_operand_aliasing={{0}: (14, {}), {1}: (15, {}), {2}: (16, {})} | custom-call | flops 500000000 | bytes 1 | tf_op jit(solution)/shard_map/pallas_call | solution.py:41
  245.8 2.2 collective-permute-done.45
  248.7 1.6 collective-permute-start.52
  250.9 13.4 %shard_map.214 = (bf16[128,3072]{1,0:T(8,128)(2,1)}, bf16[128,3072]{1,0:T(8,128)(2,1)}, bf16[128,3072]{1,0:T(8,128)(2,1)}, bf16[128,3072]{1,0:T(8,128)(2,1)}, bf...) custom-call(s32[9]{0:T(128)} %pad_add_fusion.places._, ...), custom_call_target="tpu_custom_call" | custom-call | flops 500000000 | bytes 1 | tf_op jit(solution)/shard_map/pallas_call | solution.py:41
  266.4 7.3 %shard_map.216 = (bf16[1024,1024]{1,0:T(8,128)(2,1)}, f32[1,1024]{1,0:T(1,128)}) custom-call(s32[9]{0:T(128)} %pad_add_fusion.places._, bf16[1024,1024]{1,0:T(8,128)(2,1)} %slice_bitcast_fusion.3.refs_0_.x_ref.x0, bf16[512,1024]{1,0:T(8,128)(2,1)} %copy-done.1, bf16[512,1024]{1,0:T(8,128)(2,1)} %copy-done.6, ...), custom_call_target="tpu_custom_call" | custom-call | flops 500000000 | bytes 1 | tf_op jit(solution)/shard_map/pallas_call | solution.py:41
  273.7 3.5 collective-permute-done.50.b
  278.8 2.0 add_convert_fusion.6.refs_2_
  281.0 2.6 shard_map.215
  286.9 1.5 collective-permute-start.58
  288.4 17.2 %shard_map.217 = (bf16[1024,768]{1,0:T(8,128)(2,1)}, bf16[1024,768]{1,0:T(8,128)(2,1)}, bf16[1024,1024]{1,0:T(8,128)(2,1)}, bf16[2,256,1024]{2,1,0:T(8,128)(2,1)...) custom-call(s32[9]{0:T(128)} %pad_add_fusion.places._, ...), custom_call_target="tpu_custom_call" | custom-call | flops 500000000 | bytes 1 | tf_op jit(solution)/shard_map/pallas_call | solution.py:41
  307.3 1.5 collective-permute-start.62
  310.0 17.2 %shard_map.218 = (bf16[1024,768]{1,0:T(8,128)(2,1)}, bf16[1024,768]{1,0:T(8,128)(2,1)}, bf16[1024,1024]{1,0:T(8,128)(2,1)}, bf16[2,256,1024]{2,1,0:T(8,128)(2,1)...) custom-call(s32[9]{0:T(128)} %pad_add_fusion.places._, ...), custom_call_target="tpu_custom_call", output_to_operand_aliasing={{0}: (21, {}), {1}: (22, {}), {2}: (23, {})} | custom-call | flops 500000000 | bytes 1 | tf_op jit(solution)/shard_map/pallas_call | solution.py:41
  334.7 1.6 collective-permute-start.68
  336.2 11.3 %shard_map.219 = (bf16[256,1024]{1,0:T(8,128)(2,1)}, bf16[256,1024]{1,0:T(8,128)(2,1)}, bf16[256,1024]{1,0:T(8,128)(2,1)}, bf16[256,1024]{1,0:T(8,128)(2,1)}, bf...) custom-call(s32[9]{0:T(128)} %pad_add_fusion.places._, ...), custom_call_target="tpu_custom_call" | custom-call | flops 500000000 | bytes 1 | tf_op jit(solution)/shard_map/pallas_call | solution.py:41
  347.6 3.2 collective-permute-done.68
  356.8 4.5 %shard_map.220 = (f32[2,128,1024]{2,1,0:T(8,128)}, f32[2,128,1024]{2,1,0:T(8,128)}, f32[2,1024,128]{2,1,0:T(8,128)}) custom-call(bf16[128,3072]{1,0:T(8,128)(2,1)} %get-tuple-element.367.refs_0_, bf16[128,3072]{1,0:T(8,128)(2,1)} %copy-done.49, bf16[128,3072]{1,0:T(8,128)(2,1)} %copy-done.50, bf16[128,3072]{1,0:T(8,128)(2,1)} %get-tuple-element.370.refs_3_, ...), custom_call_target="tpu_custom_call" | custom-call | flops 500000000 | bytes 1 | tf_op jit(solution)/shard_map/pallas_call | solution.py:41
  362.2 2.1 shard_map.222
  365.2 1.5 add_convert_fusion.1.mine
  370.8 8.3 %shard_map.221 = bf16[128,16,1024]{2,1,0:T(8,128)(2,1)} custom-call(s32[9]{0:T(128)} %pad_add_fusion.places._, bf16[1024,1024]{1,0:T(8,128)(2,1)} %slice_bitcast_fusion.3.refs_0_.x_ref.x0, bf16[1024,1024]{1,0:T(8,128)(2,1)} %slice_bitcast_fusion.2.refs_0_.x_ref.x1, bf16[512,1024]{1,0:T(8,128)(2,1)} %copy-done.1, bf16[512,1024]{1,0:T(8,128)(2,1)} %copy-done.6, ...), custom_call_target="tpu_custom_call" | custom-call | flops 500000000 | bytes 1 | tf_op jit(solution)/shard_map/pallas_call | solution.py:41
  379.1 2.7 collective-permute-done.77
  387.1 2.4 collective-permute-start.81
  389.6 6.2 %shard_map.223.refs_0_ = bf16[128,16,1024]{2,1,0:T(8,128)(2,1)} custom-call(s32[9]{0:T(128)} %pad_add_fusion.places._, bf16[1024,1024]{1,0:T(8,128)(2,1)} %slice_bitcast_fusion.3.refs_0_.x_ref.x0, bf16[1024,1024]{1,0:T(8,128)(2,1)} %slice_bitcast_fusion.2.refs_0_.x_ref.x1, bf16[1024,1024]{1,0:T(8,128)(2,1)} %get-tuple-element.314.dm0.refs_2_.refs_3_, ...), custom_call_target="tpu_custom_call" | custom-call | flops 500000000 | bytes 1 | tf_op jit(solution)/shard_map/pallas_call | solution.py:41
  395.7 3.0 collective-permute-done.81
  400.1 1.9 collective-permute-start.85
  403.7 6.2 %shard_map.224 = bf16[128,16,1024]{2,1,0:T(8,128)(2,1)} custom-call(s32[9]{0:T(128)} %pad_add_fusion.places._, bf16[1024,1024]{1,0:T(8,128)(2,1)} %slice_bitcast_fusion.3.refs_0_.x_ref.x0, bf16[1024,1024]{1,0:T(8,128)(2,1)} %slice_bitcast_fusion.2.refs_0_.x_ref.x1, ...), custom_call_target="tpu_custom_call", output_to_operand_aliasing={{}: (8, {})} | custom-call | flops 500000000 | bytes 1 | tf_op jit(solution)/shard_map/pallas_call | solution.py:41
  409.8 4.3 %collective-permute-done.84.refs_1_ = bf16[256,1024]{1,0:T(8,128)(2,1)} collective-permute-done((bf16[256,1024]{1,0:T(8,128)(2,1)S(1)}, bf16[256,1024]{1,0:T(8,128)(2,1)}, u32[]{:S(2)}, u32[]{:S(2)}) %collective-permute-start.84) | collective-permute-done | bytes 524320 | tf_op jit(solution)/shard_map/ppermute | solution.py:774
  414.2 2.4 shard_map.225
  (367 shorter events, 85.6 us)
Async XLA Ops:
  2.7 16.6 %collective-permute-start.2 = (bf16[256,1024]{1,0:T(8,128)(2,1)}, bf16[256,1024]{1,0:T(8,128)(2,1)S(1)}, u32[]{:S(2)}, u32[]{:S(2)}) collective-permute-start(bf16[256,1024]{1,0:T(8,128)(2,1)} %shard_map.203.refs_2_.refs_3_.refs_0_), channel_id=1, source_target_pairs={{8,0},{16,8},{24,16},{28,24},{20,28},{12,20},{4,12},{0,4},{9,1},{1... | collective-permute-start | bytes 1572872 | tf_op jit(solution)/shard_map/ppermute | solution.py:738
  5.7 13.7 %collective-permute-start.1 = (bf16[256,1024]{1,0:T(8,128)(2,1)}, bf16[256,1024]{1,0:T(8,128)(2,1)S(1)}, u32[]{:S(2)}, u32[]{:S(2)}) collective-permute-start(bf16[256,1024]{1,0:T(8,128)(2,1)} %shard_map.203.refs_2_.refs_3_.refs_0_), channel_id=1, source_target_pairs={{0,8},{8,16},{16,24},{24,28},{28,20},{20,12},{12,4},{4,0},{1,9},{9... | collective-permute-start | bytes 1572872 | tf_op jit(solution)/shard_map/ppermute | solution.py:737
  6.4 12.9 %collective-permute-start = (f32[1,4,128]{2,1,0:T(4,128)S(1)}, f32[1,4,128]{2,1,0:T(4,128)S(1)}, u32[]{:S(2)}, u32[]{:S(2)}) collective-permute-start(f32[1,4,128]{2,1,0:T(4,128)S(1)} %maximum_convert_fusion), channel_id=1, source_target_pairs={{0,4},{4,0},{8,12},{12,8},{16,20},{20,16},{24,28},{28,24},{1,5},{5... | collective-permute-start | bytes 6152 | tf_op jit(solution)/shard_map/ppermute | solution.py:850
  19.3 12.9 %collective-permute-start.4 = (bf16[256,1024]{1,0:T(8,128)(2,1)S(1)}, bf16[256,1024]{1,0:T(8,128)(2,1)S(1)}, u32[]{:S(2)}, u32[]{:S(2)}) collective-permute-start(bf16[256,1024]{1,0:T(8,128)(2,1)S(1)} %collective-permute-done.1.refs_9_.refs_10_.refs_7_), channel_id=1, source_target_pairs={{0,8},{8,16},{16,24},{24,28},{28,20},{20,12},{12,4},{4,0},{1,9},{9... | collective-permute-start | bytes 1572872 | tf_op jit(solution)/shard_map/ppermute | solution.py:737
  45.8 24.7 %collective-permute-start.12 = (bf16[128,3072]{1,0:T(8,128)(2,1)S(1)}, bf16[128,3072]{1,0:T(8,128)(2,1)S(1)}, u32[]{:S(2)}, u32[]{:S(2)}) collective-permute-start(bf16[128,3072]{1,0:T(8,128)(2,1)S(1)} %copy-done.12), channel_id=1, source_target_pairs={{8,0},{16,8},{24,16},{28,24},{20,28},{12,20},{4,12},{0,4},{9,1},{1... | collective-permute-start | bytes 2359304 | tf_op jit(solution)/shard_map/ppermute | solution.py:738
  46.4 24.1 %collective-permute-start.8 = (bf16[128,3072]{1,0:T(8,128)(2,1)S(1)}, bf16[128,3072]{1,0:T(8,128)(2,1)S(1)}, u32[]{:S(2)}, u32[]{:S(2)}) collective-permute-start(bf16[128,3072]{1,0:T(8,128)(2,1)S(1)} %copy-done.12), channel_id=1, source_target_pairs={{0,8},{8,16},{16,24},{24,28},{28,20},{20,12},{12,4},{4,0},{1,9},{9... | collective-permute-start | bytes 2359304 | tf_op jit(solution)/shard_map/ppermute | solution.py:737
  49.3 21.3 %collective-permute-start.10 = (bf16[128,1024]{1,0:T(8,128)(2,1)}, bf16[128,1024]{1,0:T(8,128)(2,1)}, u32[]{:S(2)}, u32[]{:S(2)}) collective-permute-start(bf16[128,1024]{1,0:T(8,128)(2,1)} %slice.140), channel_id=1, source_target_pairs={{0,8},{8,16},{16,24},{24,28},{28,20},{20,12},{12,4},{4,0},{1,9},{9... | collective-permute-start | bytes 786440 | tf_op jit(solution)/shard_map/ppermute | solution.py:737
  51.1 19.4 %collective-permute-start.11 = (bf16[128,1024]{1,0:T(8,128)(2,1)}, bf16[128,1024]{1,0:T(8,128)(2,1)}, u32[]{:S(2)}, u32[]{:S(2)}) collective-permute-start(bf16[128,1024]{1,0:T(8,128)(2,1)} %slice.141), channel_id=1, source_target_pairs={{8,0},{16,8},{24,16},{28,24},{20,28},{12,20},{4,12},{0,4},{9,1},{1... | collective-permute-start | bytes 786440 | tf_op jit(solution)/shard_map/ppermute | solution.py:738
  51.3 19.2 %collective-permute-start.9 = (f32[4,4,128]{2,1,0:T(4,128)S(1)}, f32[4,4,128]{2,1,0:T(4,128)S(1)}, u32[]{:S(2)}, u32[]{:S(2)}) collective-permute-start(f32[4,4,128]{2,1,0:T(4,128)S(1)} %maximum_select_fusion.1), channel_id=1, source_target_pairs={{0,16},{4,20},{8,24},{12,28},{16,0},{20,4},{24,8},{28,12},{1,17},{... | collective-permute-start | bytes 24584 | tf_op jit(solution)/shard_map/ppermute | solution.py:850
  70.6 17.3 %collective-permute-start.13 = (bf16[128,3072]{1,0:T(8,128)(2,1)S(1)}, bf16[128,3072]{1,0:T(8,128)(2,1)S(1)}, u32[]{:S(2)}, u32[]{:S(2)}) collective-permute-start(bf16[128,3072]{1,0:T(8,128)(2,1)S(1)} %collective-permute-done.8.refs_11_), channel_id=1, source_target_pairs={{0,8},{8,16},{16,24},{24,28},{28,20},{20,12},{12,4},{4,0},{1,9},{9... | collective-permute-start | bytes 2359304 | tf_op jit(solution)/shard_map/ppermute | solution.py:737
  71.1 16.8 %collective-permute-start.14 = (bf16[128,3072]{1,0:T(8,128)(2,1)S(1)}, bf16[128,3072]{1,0:T(8,128)(2,1)}, u32[]{:S(2)}, u32[]{:S(2)}) collective-permute-start(bf16[128,3072]{1,0:T(8,128)(2,1)S(1)} %collective-permute-done.12.refs_4_), channel_id=1, source_target_pairs={{8,0},{16,8},{24,16},{28,24},{20,28},{12,20},{4,12},{0,4},{9,1},{1... | collective-permute-start | bytes 2359304 | tf_op jit(solution)/shard_map/ppermute | solution.py:738
  88.0 20.4 %collective-permute-start.15 = (bf16[128,3072]{1,0:T(8,128)(2,1)S(1)}, bf16[128,3072]{1,0:T(8,128)(2,1)S(1)}, u32[]{:S(2)}, u32[]{:S(2)}) collective-permute-start(bf16[128,3072]{1,0:T(8,128)(2,1)S(1)} %collective-permute-done.13.refs_10_), channel_id=1, source_target_pairs={{0,8},{8,16},{16,24},{24,28},{28,20},{20,12},{12,4},{4,0},{1,9},{9... | collective-permute-start | bytes 2359304 | tf_op jit(solution)/shard_map/ppermute | solution.py:737
  88.5 19.8 %collective-permute-start.16 = (bf16[128,3072]{1,0:T(8,128)(2,1)}, bf16[128,3072]{1,0:T(8,128)(2,1)S(1)}, u32[]{:S(2)}, u32[]{:S(2)}) collective-permute-start(bf16[128,3072]{1,0:T(8,128)(2,1)} %collective-permute-done.14.refs_5_), channel_id=1, source_target_pairs={{8,0},{16,8},{24,16},{28,24},{20,28},{12,20},{4,12},{0,4},{9,1},{1... | collective-permute-start | bytes 2359304 | tf_op jit(solution)/shard_map/ppermute | solution.py:738
  92.5 27.5 %collective-permute-start.20 = (bf16[512,1024]{1,0:T(8,128)(2,1)S(1)}, bf16[512,1024]{1,0:T(8,128)(2,1)S(1)}, u32[]{:S(2)}, u32[]{:S(2)}) collective-permute-start(bf16[512,1024]{1,0:T(8,128)(2,1)S(1)} %add_convert_fusion.15), channel_id=1, source_target_pairs={{0,2},{1,3},{2,0},{3,1},{4,6},{5,7},{6,4},{7,5},{8,10},{9,11},{10,... | collective-permute-start | bytes 3145736 | tf_op jit(solution)/shard_map/ppermute | solution.py:808
  121.1 19.5 %collective-permute-start.22 = (bf16[128,3072]{1,0:T(8,128)(2,1)S(1)}, bf16[128,3072]{1,0:T(8,128)(2,1)S(1)}, u32[]{:S(2)}, u32[]{:S(2)}) collective-permute-start(bf16[128,3072]{1,0:T(8,128)(2,1)S(1)} %copy-done.11), channel_id=1, source_target_pairs={{8,0},{16,8},{24,16},{28,24},{20,28},{12,20},{4,12},{0,4},{9,1},{1... | collective-permute-start | bytes 2359304 | tf_op jit(solution)/shard_map/ppermute | solution.py:738
  121.6 19.4 %collective-permute-start.21 = (bf16[128,3072]{1,0:T(8,128)(2,1)S(1)}, bf16[128,3072]{1,0:T(8,128)(2,1)S(1)}, u32[]{:S(2)}, u32[]{:S(2)}) collective-permute-start(bf16[128,3072]{1,0:T(8,128)(2,1)S(1)} %copy-done.11), channel_id=1, source_target_pairs={{0,8},{8,16},{16,24},{24,28},{28,20},{20,12},{12,4},{4,0},{1,9},{9... | collective-permute-start | bytes 2359304 | tf_op jit(solution)/shard_map/ppermute | solution.py:737
  124.6 16.5 %collective-permute-start.25 = (bf16[256,1024]{1,0:T(8,128)(2,1)S(1)}, bf16[256,1024]{1,0:T(8,128)(2,1)S(1)}, u32[]{:S(2)}, u32[]{:S(2)}) collective-permute-start(bf16[256,1024]{1,0:T(8,128)(2,1)S(1)} %get-tuple-element.242), channel_id=1, source_target_pairs={{0,2},{1,3},{2,0},{3,1},{4,6},{5,7},{6,4},{7,5},{8,10},{9,11},{10,... | collective-permute-start | bytes 1572872 | tf_op jit(solution)/shard_map/ppermute | solution.py:808
  141.1 21.2 %collective-permute-start.29 = (bf16[512,1024]{1,0:T(8,128)(2,1)}, bf16[512,1024]{1,0:T(8,128)(2,1)S(1)}, u32[]{:S(2)}, u32[]{:S(2)}) collective-permute-start(bf16[512,1024]{1,0:T(8,128)(2,1)} %get-tuple-element.251), channel_id=1, source_target_pairs={{0,1},{1,0},{2,3},{3,2},{4,5},{5,4},{6,7},{7,6},{8,9},{9,8},{10,11... | collective-permute-start | bytes 3145736 | tf_op jit(solution)/shard_map/ppermute | solution.py:793
  141.1 21.2 %collective-permute-start.30 = (bf16[512,1024]{1,0:T(8,128)(2,1)}, bf16[512,1024]{1,0:T(8,128)(2,1)S(1)}, u32[]{:S(2)}, u32[]{:S(2)}) collective-permute-start(bf16[512,1024]{1,0:T(8,128)(2,1)} %get-tuple-element.253), channel_id=1, source_target_pairs={{0,1},{1,0},{2,3},{3,2},{4,5},{5,4},{6,7},{7,6},{8,9},{9,8},{10,11... | collective-permute-start | bytes 3145736 | tf_op jit(solution)/shard_map/ppermute | solution.py:793
  141.6 19.5 %collective-permute-start.26 = (bf16[128,3072]{1,0:T(8,128)(2,1)S(1)}, bf16[128,3072]{1,0:T(8,128)(2,1)S(1)}, u32[]{:S(2)}, u32[]{:S(2)}) collective-permute-start(bf16[128,3072]{1,0:T(8,128)(2,1)S(1)} %collective-permute-done.21.refs_11_), channel_id=1, source_target_pairs={{0,8},{8,16},{16,24},{24,28},{28,20},{20,12},{12,4},{4,0},{1,9},{9... | collective-permute-start | bytes 2359304 | tf_op jit(solution)/shard_map/ppermute | solution.py:737
  143.0 19.2 %collective-permute-start.27 = (bf16[128,3072]{1,0:T(8,128)(2,1)S(1)}, bf16[128,3072]{1,0:T(8,128)(2,1)S(1)}, u32[]{:S(2)}, u32[]{:S(2)}) collective-permute-start(bf16[128,3072]{1,0:T(8,128)(2,1)S(1)} %collective-permute-done.22.refs_4_), channel_id=1, source_target_pairs={{8,0},{16,8},{24,16},{28,24},{20,28},{12,20},{4,12},{0,4},{9,1},{1... | collective-permute-start | bytes 2359304 | tf_op jit(solution)/shard_map/ppermute | solution.py:738
  143.6 15.4 %collective-permute-start.28 = (bf16[256,1024]{1,0:T(8,128)(2,1)S(1)}, bf16[256,1024]{1,0:T(8,128)(2,1)}, u32[]{:S(2)}, u32[]{:S(2)}) collective-permute-start(bf16[256,1024]{1,0:T(8,128)(2,1)S(1)} %copy-done.69), channel_id=1, source_target_pairs={{0,2},{1,3},{2,0},{3,1},{4,6},{5,7},{6,4},{7,5},{8,10},{9,11},{10,... | collective-permute-start | bytes 1572872 | tf_op jit(solution)/shard_map/ppermute | solution.py:808
  163.3 19.4 %collective-permute-start.31 = (bf16[128,3072]{1,0:T(8,128)(2,1)S(1)}, bf16[128,3072]{1,0:T(8,128)(2,1)S(1)}, u32[]{:S(2)}, u32[]{:S(2)}) collective-permute-start(bf16[128,3072]{1,0:T(8,128)(2,1)S(1)} %collective-permute-done.26.refs_10_), channel_id=1, source_target_pairs={{0,8},{8,16},{16,24},{24,28},{28,20},{20,12},{12,4},{4,0},{1,9},{9... | collective-permute-start | bytes 2359304 | tf_op jit(solution)/shard_map/ppermute | solution.py:737
  164.9 18.1 %collective-permute-start.32 = (bf16[128,3072]{1,0:T(8,128)(2,1)S(1)}, bf16[128,3072]{1,0:T(8,128)(2,1)S(1)}, u32[]{:S(2)}, u32[]{:S(2)}) collective-permute-start(bf16[128,3072]{1,0:T(8,128)(2,1)S(1)} %collective-permute-done.27.refs_5_), channel_id=1, source_target_pairs={{8,0},{16,8},{24,16},{28,24},{20,28},{12,20},{4,12},{0,4},{9,1},{1... | collective-permute-start | bytes 2359304 | tf_op jit(solution)/shard_map/ppermute | solution.py:738
  166.8 16.2 %collective-permute-start.34 = (bf16[512,1024]{1,0:T(8,128)(2,1)S(1)}, bf16[512,1024]{1,0:T(8,128)(2,1)S(1)}, u32[]{:S(2)}, u32[]{:S(2)}) collective-permute-start(bf16[512,1024]{1,0:T(8,128)(2,1)S(1)} %add_convert_fusion.11.refs_0_.att0.refs_4_), channel_id=1, source_target_pairs={{0,1},{1,0},{2,3},{3,2},{4,5},{5,4},{6,7},{7,6},{8,9},{9,8},{10,11... | collective-permute-start | bytes 3145736 | tf_op jit(solution)/shard_map/ppermute | solution.py:814
  167.8 14.9 %collective-permute-start.33 = (bf16[256,1024]{1,0:T(8,128)(2,1)S(1)}, bf16[256,1024]{1,0:T(8,128)(2,1)S(1)}, u32[]{:S(2)}, u32[]{:S(2)}) collective-permute-start(bf16[256,1024]{1,0:T(8,128)(2,1)S(1)} %get-tuple-element.264), channel_id=1, source_target_pairs={{0,2},{1,3},{2,0},{3,1},{4,6},{5,7},{6,4},{7,5},{8,10},{9,11},{10,... | collective-permute-start | bytes 1572872 | tf_op jit(solution)/shard_map/ppermute | solution.py:808
  183.0 21.3 %collective-permute-start.39 = (bf16[256,1024]{1,0:T(8,128)(2,1)S(1)}, bf16[256,1024]{1,0:T(8,128)(2,1)S(1)}, u32[]{:S(2)}, u32[]{:S(2)}) collective-permute-start(bf16[256,1024]{1,0:T(8,128)(2,1)S(1)} %get-tuple-element.274), channel_id=1, source_target_pairs={{0,2},{1,3},{2,0},{3,1},{4,6},{5,7},{6,4},{7,5},{8,10},{9,11},{10,... | collective-permute-start | bytes 1572872 | tf_op jit(solution)/shard_map/ppermute | solution.py:808
  187.0 16.0 %collective-permute-start.37 = (bf16[64,3072]{1,0:T(8,128)(2,1)S(1)}, bf16[64,3072]{1,0:T(8,128)(2,1)S(1)}, u32[]{:S(2)}, u32[]{:S(2)}) collective-permute-start(bf16[64,3072]{1,0:T(8,128)(2,1)S(1)} %slice.151), channel_id=1, source_target_pairs={{0,8},{8,16},{16,24},{24,28},{28,20},{20,12},{12,4},{4,0},{1,9},{9... | collective-permute-start | bytes 1179656 | tf_op jit(solution)/shard_map/ppermute | solution.py:737
  187.6 16.6 %collective-permute-start.38 = (bf16[64,3072]{1,0:T(8,128)(2,1)S(1)}, bf16[64,3072]{1,0:T(8,128)(2,1)S(1)}, u32[]{:S(2)}, u32[]{:S(2)}) collective-permute-start(bf16[64,3072]{1,0:T(8,128)(2,1)S(1)} %slice.152), channel_id=1, source_target_pairs={{8,0},{16,8},{24,16},{28,24},{20,28},{12,20},{4,12},{0,4},{9,1},{1... | collective-permute-start | bytes 1179656 | tf_op jit(solution)/shard_map/ppermute | solution.py:738
  204.3 20.7 %collective-permute-start.40 = (bf16[128,3072]{1,0:T(8,128)(2,1)}, bf16[128,3072]{1,0:T(8,128)(2,1)S(1)}, u32[]{:S(2)}, u32[]{:S(2)}) collective-permute-start(bf16[128,3072]{1,0:T(8,128)(2,1)} %get-tuple-element.275), channel_id=1, source_target_pairs={{0,8},{8,16},{16,24},{24,28},{28,20},{20,12},{12,4},{4,0},{1,9},{9... | collective-permute-start | bytes 2359304 | tf_op jit(solution)/shard_map/ppermute | solution.py:774
  205.3 20.5 %collective-permute-start.42 = (bf16[512,1024]{1,0:T(8,128)(2,1)S(1)}, bf16[512,1024]{1,0:T(8,128)(2,1)S(1)}, u32[]{:S(2)}, u32[]{:S(2)}) collective-permute-start(bf16[512,1024]{1,0:T(8,128)(2,1)S(1)} %add_convert_fusion.10.dh0), channel_id=1, source_target_pairs={{0,1},{1,0},{2,3},{3,2},{4,5},{5,4},{6,7},{7,6},{8,9},{9,8},{10,11... | collective-permute-start | bytes 3145736 | tf_op jit(solution)/shard_map/ppermute | solution.py:814
  206.8 19.0 %collective-permute-start.41 = (bf16[128,3072]{1,0:T(8,128)(2,1)S(1)}, bf16[128,3072]{1,0:T(8,128)(2,1)S(1)}, u32[]{:S(2)}, u32[]{:S(2)}) collective-permute-start(bf16[128,3072]{1,0:T(8,128)(2,1)S(1)} %copy-done.64), channel_id=1, source_target_pairs={{8,0},{16,8},{24,16},{28,24},{20,28},{12,20},{4,12},{0,4},{9,1},{1... | collective-permute-start | bytes 2359304 | tf_op jit(solution)/shard_map/ppermute | solution.py:775
  209.3 15.8 %collective-permute-start.43 = (bf16[256,1024]{1,0:T(8,128)(2,1)}, bf16[256,1024]{1,0:T(8,128)(2,1)}, u32[]{:S(2)}, u32[]{:S(2)}) collective-permute-start(bf16[256,1024]{1,0:T(8,128)(2,1)} %get-tuple-element.283), channel_id=1, source_target_pairs={{0,2},{1,3},{2,0},{3,1},{4,6},{5,7},{6,4},{7,5},{8,10},{9,11},{10,... | collective-permute-start | bytes 1572872 | tf_op jit(solution)/shard_map/ppermute | solution.py:808
  225.8 18.2 %collective-permute-start.44 = (bf16[128,3072]{1,0:T(8,128)(2,1)S(1)}, bf16[128,3072]{1,0:T(8,128)(2,1)}, u32[]{:S(2)}, u32[]{:S(2)}) collective-permute-start(bf16[128,3072]{1,0:T(8,128)(2,1)S(1)} %add_convert_fusion.23), channel_id=1, source_target_pairs={{0,8},{8,16},{16,24},{24,28},{28,20},{20,12},{12,4},{4,0},{1,9},{9... | collective-permute-start | bytes 2359304 | tf_op jit(solution)/shard_map/ppermute | solution.py:774
  226.5 18.8 %collective-permute-start.47 = (bf16[512,1024]{1,0:T(8,128)(2,1)}, bf16[512,1024]{1,0:T(8,128)(2,1)S(1)}, u32[]{:S(2)}, u32[]{:S(2)}) collective-permute-start(bf16[512,1024]{1,0:T(8,128)(2,1)} %get-tuple-element.293), channel_id=1, source_target_pairs={{0,1},{1,0},{2,3},{3,2},{4,5},{5,4},{6,7},{7,6},{8,9},{9,8},{10,11... | collective-permute-start | bytes 3145736 | tf_op jit(solution)/shard_map/ppermute | solution.py:793
  226.7 19.1 %collective-permute-start.46 = (bf16[256,1024]{1,0:T(8,128)(2,1)}, bf16[256,1024]{1,0:T(8,128)(2,1)}, u32[]{:S(2)}, u32[]{:S(2)}) collective-permute-start(bf16[256,1024]{1,0:T(8,128)(2,1)} %get-tuple-element.292), channel_id=1, source_target_pairs={{0,2},{1,3},{2,0},{3,1},{4,6},{5,7},{6,4},{7,5},{8,10},{9,11},{10,... | collective-permute-start | bytes 1572872 | tf_op jit(solution)/shard_map/ppermute | solution.py:808
  228.3 19.7 %collective-permute-start.45 = (bf16[128,3072]{1,0:T(8,128)(2,1)S(1)}, bf16[128,3072]{1,0:T(8,128)(2,1)S(1)}, u32[]{:S(2)}, u32[]{:S(2)}) collective-permute-start(bf16[128,3072]{1,0:T(8,128)(2,1)S(1)} %add_convert_fusion.22), channel_id=1, source_target_pairs={{8,0},{16,8},{24,16},{28,24},{20,28},{12,20},{4,12},{0,4},{9,1},{1... | collective-permute-start | bytes 2359304 | tf_op jit(solution)/shard_map/ppermute | solution.py:775
  229.6 18.4 %collective-permute-start.48 = (bf16[512,1024]{1,0:T(8,128)(2,1)}, bf16[512,1024]{1,0:T(8,128)(2,1)S(1)}, u32[]{:S(2)}, u32[]{:S(2)}) collective-permute-start(bf16[512,1024]{1,0:T(8,128)(2,1)} %get-tuple-element.295), channel_id=1, source_target_pairs={{0,1},{1,0},{2,3},{3,2},{4,5},{5,4},{6,7},{7,6},{8,9},{9,8},{10,11... | collective-permute-start | bytes 3145736 | tf_op jit(solution)/shard_map/ppermute | solution.py:793
  248.0 29.3 %collective-permute-start.51 = (bf16[512,1024]{1,0:T(8,128)(2,1)S(1)}, bf16[512,1024]{1,0:T(8,128)(2,1)S(1)}, u32[]{:S(2)}, u32[]{:S(2)}) collective-permute-start(bf16[512,1024]{1,0:T(8,128)(2,1)S(1)} %add_convert_fusion.8), channel_id=1, source_target_pairs={{0,2},{1,3},{2,0},{3,1},{4,6},{5,7},{6,4},{7,5},{8,10},{9,11},{10,... | collective-permute-start | bytes 3145736 | tf_op jit(solution)/shard_map/ppermute | solution.py:808
  248.7 28.5 %collective-permute-start.52 = (bf16[128,3072]{1,0:T(8,128)(2,1)S(1)}, bf16[128,3072]{1,0:T(8,128)(2,1)S(1)}, u32[]{:S(2)}, u32[]{:S(2)}) collective-permute-start(bf16[128,3072]{1,0:T(8,128)(2,1)S(1)} %add_convert_fusion.21), channel_id=1, source_target_pairs={{0,8},{8,16},{16,24},{24,28},{28,20},{20,12},{12,4},{4,0},{1,9},{9... | collective-permute-start | bytes 2359304 | tf_op jit(solution)/shard_map/ppermute | solution.py:774
  250.3 26.9 %collective-permute-start.53 = (bf16[128,3072]{1,0:T(8,128)(2,1)S(1)}, bf16[128,3072]{1,0:T(8,128)(2,1)S(1)}, u32[]{:S(2)}, u32[]{:S(2)}) collective-permute-start(bf16[128,3072]{1,0:T(8,128)(2,1)S(1)} %add_convert_fusion.20), channel_id=1, source_target_pairs={{8,0},{16,8},{24,16},{28,24},{20,28},{12,20},{4,12},{0,4},{9,1},{1... | collective-permute-start | bytes 2359304 | tf_op jit(solution)/shard_map/ppermute | solution.py:775
  264.3 12.9 %collective-permute-start.50 = (bf16[64,3072]{1,0:T(8,128)(2,1)}, bf16[64,3072]{1,0:T(8,128)(2,1)S(1)}, u32[]{:S(2)}, u32[]{:S(2)}) collective-permute-start(bf16[64,3072]{1,0:T(8,128)(2,1)} %get-tuple-element.306), channel_id=1, source_target_pairs={{8,0},{16,8},{24,16},{28,24},{20,28},{12,20},{4,12},{0,4},{9,1},{1... | collective-permute-start | bytes 1179656 | tf_op jit(solution)/shard_map/ppermute | solution.py:775
  283.6 21.9 %collective-permute-start.56 = (bf16[128,3072]{1,0:T(8,128)(2,1)}, bf16[128,3072]{1,0:T(8,128)(2,1)S(1)}, u32[]{:S(2)}, u32[]{:S(2)}) collective-permute-start(bf16[128,3072]{1,0:T(8,128)(2,1)} %get-tuple-element.318), channel_id=1, source_target_pairs={{0,8},{8,16},{16,24},{24,28},{28,20},{20,12},{12,4},{4,0},{1,9},{9... | collective-permute-start | bytes 2359304 | tf_op jit(solution)/shard_map/ppermute | solution.py:774
  285.9 19.9 %collective-permute-start.57 = (bf16[128,3072]{1,0:T(8,128)(2,1)S(1)}, bf16[128,3072]{1,0:T(8,128)(2,1)S(1)}, u32[]{:S(2)}, u32[]{:S(2)}) collective-permute-start(bf16[128,3072]{1,0:T(8,128)(2,1)S(1)} %copy-done.63), channel_id=1, source_target_pairs={{8,0},{16,8},{24,16},{28,24},{20,28},{12,20},{4,12},{0,4},{9,1},{1... | collective-permute-start | bytes 2359304 | tf_op jit(solution)/shard_map/ppermute | solution.py:775
  286.9 19.1 %collective-permute-start.58 = (bf16[384,1024]{1,0:T(8,128)(2,1)S(1)}, bf16[384,1024]{1,0:T(8,128)(2,1)S(1)}, u32[]{:S(2)}, u32[]{:S(2)}) collective-permute-start(bf16[384,1024]{1,0:T(8,128)(2,1)S(1)} %slice.157), channel_id=1, source_target_pairs={{0,2},{1,3},{2,0},{3,1},{4,6},{5,7},{6,4},{7,5},{8,10},{9,11},{10,... | collective-permute-start | bytes 2359304 | tf_op jit(solution)/shard_map/ppermute | solution.py:808
  305.9 21.3 %collective-permute-start.59 = (bf16[128,3072]{1,0:T(8,128)(2,1)S(1)}, bf16[128,3072]{1,0:T(8,128)(2,1)S(1)}, u32[]{:S(2)}, u32[]{:S(2)}) collective-permute-start(bf16[128,3072]{1,0:T(8,128)(2,1)S(1)} %add_convert_fusion.19), channel_id=1, source_target_pairs={{0,8},{8,16},{16,24},{24,28},{28,20},{20,12},{12,4},{4,0},{1,9},{9... | collective-permute-start | bytes 2359304 | tf_op jit(solution)/shard_map/ppermute | solution.py:774
  307.0 21.3 %collective-permute-start.61 = (bf16[512,1024]{1,0:T(8,128)(2,1)}, bf16[512,1024]{1,0:T(8,128)(2,1)S(1)}, u32[]{:S(2)}, u32[]{:S(2)}) collective-permute-start(bf16[512,1024]{1,0:T(8,128)(2,1)} %bitcast.16), channel_id=1, source_target_pairs={{0,1},{1,0},{2,3},{3,2},{4,5},{5,4},{6,7},{7,6},{8,9},{9,8},{10,11... | collective-permute-start | bytes 3145736 | tf_op jit(solution)/shard_map/ppermute | solution.py:793
  307.3 21.9 %collective-permute-start.62 = (bf16[128,1024]{1,0:T(8,128)(2,1)S(1)}, bf16[128,1024]{1,0:T(8,128)(2,1)S(1)}, u32[]{:S(2)}, u32[]{:S(2)}) collective-permute-start(bf16[128,1024]{1,0:T(8,128)(2,1)S(1)} %slice.158), channel_id=1, source_target_pairs={{0,2},{1,3},{2,0},{3,1},{4,6},{5,7},{6,4},{7,5},{8,10},{9,11},{10,... | collective-permute-start | bytes 786440 | tf_op jit(solution)/shard_map/ppermute | solution.py:808
  308.9 20.4 %collective-permute-start.60 = (bf16[128,3072]{1,0:T(8,128)(2,1)S(1)}, bf16[128,3072]{1,0:T(8,128)(2,1)S(1)}, u32[]{:S(2)}, u32[]{:S(2)}) collective-permute-start(bf16[128,3072]{1,0:T(8,128)(2,1)S(1)} %add_convert_fusion.18), channel_id=1, source_target_pairs={{8,0},{16,8},{24,16},{28,24},{20,28},{12,20},{4,12},{0,4},{9,1},{1... | collective-permute-start | bytes 2359304 | tf_op jit(solution)/shard_map/ppermute | solution.py:775
  329.2 21.6 %collective-permute-start.65 = (bf16[512,1024]{1,0:T(8,128)(2,1)}, bf16[512,1024]{1,0:T(8,128)(2,1)S(1)}, u32[]{:S(2)}, u32[]{:S(2)}) collective-permute-start(bf16[512,1024]{1,0:T(8,128)(2,1)} %bitcast.18), channel_id=1, source_target_pairs={{0,1},{1,0},{2,3},{3,2},{4,5},{5,4},{6,7},{7,6},{8,9},{9,8},{10,11... | collective-permute-start | bytes 3145736 | tf_op jit(solution)/shard_map/ppermute | solution.py:793
  330.7 20.6 %collective-permute-start.66 = (bf16[384,1024]{1,0:T(8,128)(2,1)S(1)}, bf16[384,1024]{1,0:T(8,128)(2,1)}, u32[]{:S(2)}, u32[]{:S(2)}) collective-permute-start(bf16[384,1024]{1,0:T(8,128)(2,1)S(1)} %slice.159), channel_id=1, source_target_pairs={{0,2},{1,3},{2,0},{3,1},{4,6},{5,7},{6,4},{7,5},{8,10},{9,11},{10,... | collective-permute-start | bytes 2359304 | tf_op jit(solution)/shard_map/ppermute | solution.py:808
  331.3 20.0 %collective-permute-start.63 = (bf16[128,3072]{1,0:T(8,128)(2,1)}, bf16[128,3072]{1,0:T(8,128)(2,1)S(1)}, u32[]{:S(2)}, u32[]{:S(2)}) collective-permute-start(bf16[128,3072]{1,0:T(8,128)(2,1)} %add_convert_fusion.17), channel_id=1, source_target_pairs={{0,8},{8,16},{16,24},{24,28},{28,20},{20,12},{12,4},{4,0},{1,9},{9... | collective-permute-start | bytes 2359304 | tf_op jit(solution)/shard_map/ppermute | solution.py:774
  332.3 19.3 %collective-permute-start.64 = (bf16[128,3072]{1,0:T(8,128)(2,1)}, bf16[128,3072]{1,0:T(8,128)(2,1)S(1)}, u32[]{:S(2)}, u32[]{:S(2)}) collective-permute-start(bf16[128,3072]{1,0:T(8,128)(2,1)} %add_convert_fusion.16), channel_id=1, source_target_pairs={{8,0},{16,8},{24,16},{28,24},{20,28},{12,20},{4,12},{0,4},{9,1},{1... | collective-permute-start | bytes 2359304 | tf_op jit(solution)/shard_map/ppermute | solution.py:775
  334.7 16.1 %collective-permute-start.68 = (f32[4,1024]{1,0:T(4,128)S(1)}, f32[4,1024]{1,0:T(4,128)S(1)}, u32[]{:S(2)}, u32[]{:S(2)}) collective-permute-start(f32[4,1024]{1,0:T(4,128)S(1)} %fusion.1), channel_id=1, source_target_pairs={{0,2},{1,3},{2,0},{3,1},{4,6},{5,7},{6,4},{7,5},{8,10},{9,11},{10,... | collective-permute-start | bytes 49160 | tf_op jit(solution)/shard_map/ppermute | solution.py:980
  364.3 17.5 %collective-permute-start.74 = (bf16[256,1024]{1,0:T(8,128)(2,1)}, bf16[256,1024]{1,0:T(8,128)(2,1)S(1)}, u32[]{:S(2)}, u32[]{:S(2)}) collective-permute-start(bf16[256,1024]{1,0:T(8,128)(2,1)} %get-tuple-element.380), channel_id=1, source_target_pairs={{0,8},{8,16},{16,24},{24,28},{28,20},{20,12},{12,4},{4,0},{1,9},{9... | collective-permute-start | bytes 1572872 | tf_op jit(solution)/shard_map/ppermute | solution.py:774
  366.8 16.3 %collective-permute-start.76 = (bf16[512,1024]{1,0:T(8,128)(2,1)S(1)}, bf16[512,1024]{1,0:T(8,128)(2,1)S(1)}, u32[]{:S(2)}, u32[]{:S(2)}) collective-permute-start(bf16[512,1024]{1,0:T(8,128)(2,1)S(1)} %add_convert_fusion.1.mine), channel_id=1, source_target_pairs={{0,1},{1,0},{2,3},{3,2},{4,5},{5,4},{6,7},{7,6},{8,9},{9,8},{10,11... | collective-permute-start | bytes 3145736 | tf_op jit(solution)/shard_map/ppermute | solution.py:814
  366.9 15.1 %collective-permute-start.75 = (bf16[256,1024]{1,0:T(8,128)(2,1)S(1)}, bf16[256,1024]{1,0:T(8,128)(2,1)S(1)}, u32[]{:S(2)}, u32[]{:S(2)}) collective-permute-start(bf16[256,1024]{1,0:T(8,128)(2,1)S(1)} %copy-done.79), channel_id=1, source_target_pairs={{8,0},{16,8},{24,16},{28,24},{20,28},{12,20},{4,12},{0,4},{9,1},{1... | collective-permute-start | bytes 1572872 | tf_op jit(solution)/shard_map/ppermute | solution.py:775
  368.5 13.3 %collective-permute-start.77 = (f32[4,1024]{1,0:T(4,128)S(1)}, f32[4,1024]{1,0:T(4,128)S(1)}, u32[]{:S(2)}, u32[]{:S(2)}) collective-permute-start(f32[4,1024]{1,0:T(4,128)S(1)} %add.167), channel_id=1, source_target_pairs={{0,8},{4,12},{8,0},{12,4},{16,24},{20,28},{24,16},{28,20},{1,9},{5... | collective-permute-start | bytes 49160 | tf_op jit(solution)/shard_map/ppermute | solution.py:980
  369.4 13.7 %collective-permute-start.78 = (bf16[256,1024]{1,0:T(8,128)(2,1)S(1)}, bf16[256,1024]{1,0:T(8,128)(2,1)S(1)}, u32[]{:S(2)}, u32[]{:S(2)}) collective-permute-start(bf16[256,1024]{1,0:T(8,128)(2,1)S(1)} %get-tuple-element.386), channel_id=1, source_target_pairs={{0,2},{1,3},{2,0},{3,1},{4,6},{5,7},{6,4},{7,5},{8,10},{9,11},{10,... | collective-permute-start | bytes 1572872 | tf_op jit(solution)/shard_map/ppermute | solution.py:808
  383.1 15.6 %collective-permute-start.79 = (bf16[256,1024]{1,0:T(8,128)(2,1)S(1)}, bf16[256,1024]{1,0:T(8,128)(2,1)S(1)}, u32[]{:S(2)}, u32[]{:S(2)}) collective-permute-start(bf16[256,1024]{1,0:T(8,128)(2,1)S(1)} %add_convert_fusion.27), channel_id=1, source_target_pairs={{0,8},{8,16},{16,24},{24,28},{28,20},{20,12},{12,4},{4,0},{1,9},{9... | collective-permute-start | bytes 1572872 | tf_op jit(solution)/shard_map/ppermute | solution.py:774
  384.3 14.4 %collective-permute-start.80 = (bf16[256,1024]{1,0:T(8,128)(2,1)S(1)}, bf16[256,1024]{1,0:T(8,128)(2,1)S(1)}, u32[]{:S(2)}, u32[]{:S(2)}) collective-permute-start(bf16[256,1024]{1,0:T(8,128)(2,1)S(1)} %add_convert_fusion.26), channel_id=1, source_target_pairs={{8,0},{16,8},{24,16},{28,24},{20,28},{12,20},{4,12},{0,4},{9,1},{1... | collective-permute-start | bytes 1572872 | tf_op jit(solution)/shard_map/ppermute | solution.py:775
  385.1 13.6 %collective-permute-start.82 = (bf16[256,1024]{1,0:T(8,128)(2,1)S(1)}, bf16[256,1024]{1,0:T(8,128)(2,1)S(1)}, u32[]{:S(2)}, u32[]{:S(2)}) collective-permute-start(bf16[256,1024]{1,0:T(8,128)(2,1)S(1)} %get-tuple-element.392), channel_id=1, source_target_pairs={{0,2},{1,3},{2,0},{3,1},{4,6},{5,7},{6,4},{7,5},{8,10},{9,11},{10,... | collective-permute-start | bytes 1572872 | tf_op jit(solution)/shard_map/ppermute | solution.py:808
  399.9 14.2 %collective-permute-start.84 = (bf16[256,1024]{1,0:T(8,128)(2,1)S(1)}, bf16[256,1024]{1,0:T(8,128)(2,1)}, u32[]{:S(2)}, u32[]{:S(2)}) collective-permute-start(bf16[256,1024]{1,0:T(8,128)(2,1)S(1)} %add_convert_fusion.25), channel_id=1, source_target_pairs={{0,8},{8,16},{16,24},{24,28},{28,20},{20,12},{12,4},{4,0},{1,9},{9... | collective-permute-start | bytes 1572872 | tf_op jit(solution)/shard_map/ppermute | solution.py:774
  400.1 14.1 %collective-permute-start.85 = (bf16[256,1024]{1,0:T(8,128)(2,1)S(1)}, bf16[256,1024]{1,0:T(8,128)(2,1)}, u32[]{:S(2)}, u32[]{:S(2)}) collective-permute-start(bf16[256,1024]{1,0:T(8,128)(2,1)S(1)} %add_convert_fusion.24), channel_id=1, source_target_pairs={{8,0},{16,8},{24,16},{28,24},{20,28},{12,20},{4,12},{0,4},{9,1},{1... | collective-permute-start | bytes 1572872 | tf_op jit(solution)/shard_map/ppermute | solution.py:775
  (107 other events, 818.5 us)

commit v10 on v9

--- a/solution.py
+++ b/solution.py
@@ -325,8 +325,8 @@
         halves.put(sum_refs[:2], d_hidden)
         halves.put(sum_refs[2:], mm(inner_ref[...], w_ref[:, 2 * units :], NT).astype(BF))
     else:
-        sum_refs[0][...] = d_hidden
-        sum_refs[1][...] = mm(inner_ref[...], w_ref[:, 2 * units :], NT).astype(BF)
+        sum_refs[0][0] = d_hidden
+        sum_refs[0][1] = mm(inner_ref[...], w_ref[:, 2 * units :], NT).astype(BF)
 
 
 def hidden_units(places, x, att, g, gain, w, half=None, filled=()):
@@ -344,8 +344,9 @@
         halves.grid if half is None else (halves.count,),
         ins,
         [part, *side_specs, part, whole(gain.shape)] + [HBM] * (pieces.count + len(filled)),
-        [out_of((tokens, n)) for n in widths] + [out_of((tokens // 2, width))] * (4 if half is None else 2),
-        [spec(n) for n in widths] + (halves.pair(width) * 2 if half is None else [rows_of(ROWS, width)] * 2),
+        [out_of((tokens, n)) for n in widths]
+        + ([out_of((tokens // 2, width))] * 4 if half is None else [out_of((2, tokens // 2, width))]),
+        [spec(n) for n in widths] + (halves.pair(width) * 2 if half is None else [pl.BlockSpec((2, ROWS, width), lambda i, p: (0, i, 0))]),
         12 * tokens * width * units,
         pieces.scratch,
         places,
@@ -915,17 +916,17 @@
     dh, mlp, grads, dm, d_gain_ffn = ([None] * 2 for _ in range(5))
     got = heads[1].far(0.5)
     ffn = (x[0], heads[0].sum, g[0], g_ffn[0], weights(0))
-    out, dh_other, mlp_other = hidden_units(now(places), *ffn, half=1)
-    close(*moved, dh_other, got)
+    out, other = hidden_units(now(places), *ffn, half=1)
+    close(*moved, other, got)
     moved = move(1)
     got = heads[1].far(0.5)
-    dh[0] = HeadSum(rounds, (None, dh_other))
-    mlp[0] = HeadSum(rounds, (None, mlp_other))
-    near = dh[0].near_start(), mlp[0].near_start()
-    out, dh_mine, mlp_mine = hidden_units(now(places), *ffn, half=0, filled=out)
-    close(*moved, dh_mine, got, *near)
-    dh[0].near_add(dh_mine)
-    mlp[0].near_add(mlp_mine)
+    dh[0], mlp[0] = HeadSum(rounds, (None, other)), HeadSum(rounds, None)
+    near = dh[0].near_start()
+    out, mine = hidden_units(now(places), *ffn, half=0, filled=out)
+    close(*moved, mine, got, near)
+    dh[0].near_got, mlp[0].near_got = near[0], near[1]
+    dh[0].near_add(mine[0])
+    mlp[0].near_add(mine[1])
     moved = move(1)
     got = dh[0].far(0.5)
     grads[0] = grads_of(0, out)
@@ -938,17 +939,17 @@
     moved = (*add(0), dh[0].last())
     got = mlp[0].far(0.5)
     ffn = (x[1], att[1], g[1], g_ffn[1], weights(1))
-    out, dh_other, mlp_other = hidden_units(now(places), *ffn, half=1)
-    close(*moved, dh_other, got)
+    out, other = hidden_units(now(places), *ffn, half=1)
+    close(*moved, other, got)
     moved = add(0)
     got = mlp[0].far(0.5)
-    dh[1] = HeadSum(rounds, (None, dh_other))
-    mlp[1] = HeadSum(rounds, (None, mlp_other))
-    near = dh[1].near_start(), mlp[1].near_start()
-    out, dh_mine, mlp_mine = hidden_units(now(places), *ffn, half=0, filled=out)
-    close(*moved, dh_mine, got, *near)
-    dh[1].near_add(dh_mine)
-    mlp[1].near_add(mlp_mine)
+    dh[1], mlp[1] = HeadSum(rounds, (None, other)), HeadSum(rounds, None)
+    near = dh[1].near_start()
+    out, mine = hidden_units(now(places), *ffn, half=0, filled=out)
+    close(*moved, mine, got, near)
+    dh[1].near_got, mlp[1].near_got = near[0], near[1]
+    dh[1].near_add(mine[0])
+    mlp[1].near_add(mine[1])
     moved = add(0)
     got = dh[1].far()
     grads[1] = grads_of(1, out)

time: 425 us -> 428 us (level)
  waiting for transfers between devices: 87 us -> 93.8 us
    convert_element_type x16 -> x14, other arithmetic: 11.6 us -> 10.9 us  [add(): return (one.astype(F32) + two.astype(F32)).astype(BF)]
  transfers between devices with their start and end apart: 86 -> 84, of which waited for: 32 -> 35; matrix products, arithmetic and copies ran while one was open for 8% -> 8% of each run, Pallas kernels for 48% -> 47%
where the time goes in v10:
time: 428 us; the launch traced here: 421 us
  Pallas kernels  204 us (48%)
  waiting for transfers between devices  93.8 us (22%)
  starting transfers between devices  80.1 us (19%)
  other arithmetic  21.2 us (5%)
  local copies, waits for them, and re-layouts  18.8 us (4%)
    pallas_call x23, Pallas kernels, kernel_call(): pl.pallas_call(body, grid_spec=spec, out_shape=outs, input_output_aliases...  204 us
    ppermute x3, waiting for transfers between devices, gain_step(): other = lax.ppermute(now(value), axis, moves)  27.5 us
    ppermute x12, waiting for transfers between devices, step(): self.a.append(lax.ppermute(self.rounds.now(a), 'dp', self.ring.ahead))  23.3 us
    ppermute x14, starting transfers between devices, far(): self.got.append(lax.ppermute(moved, 'mp', self.far_moves))  18.4 us
    ppermute x12, waiting for transfers between devices, step(): self.a = lax.ppermute(self.rounds.now(self.a), 'dp', self.ring.ahead)  15.1 us
    ppermute x12, starting transfers between devices, step(): self.b = lax.ppermute(self.rounds.now(self.b), 'dp', self.ring.behind)  13.7 us
    ppermute x12, starting transfers between devices, step(): self.a.append(lax.ppermute(self.rounds.now(a), 'dp', self.ring.ahead))  13.2 us
    ppermute x12, starting transfers between devices, step(): self.b.append(lax.ppermute(self.rounds.now(b), 'dp', self.ring.behind))  13 us
  transfers between devices with their start and end apart: 84, of which 35 were waited for; matrix products, arithmetic and copies ran while one was open for 8% of the time, Pallas kernels for 47%

profile of v10, /device:TPU:0, one launch (start us, length us, event | category | flops | bytes accessed | tf_op | source)
XLA Modules:
  0.0 420.8 jit_solution(1604936002396783729)
XLA Ops:
  0.6 2.0 shard_map.203.refs_2_.refs_3_.refs_0_
  2.7 3.0 collective-permute-start.2
  6.4 2.0 collective-permute-start
  8.3 3.1 slice_bitcast_fusion.3.refs_0_.x_ref.x0
  11.5 2.1 shard_map.204.refs_3_
  13.6 5.7 %collective-permute-done = f32[1,4,128]{2,1,0:T(4,128)S(1)} collective-permute-done((f32[1,4,128]{2,1,0:T(4,128)S(1)}, f32[1,4,128]{2,1,0:T(4,128)S(1)}, u32[]{:S(2)}, u32[]{:S(2)}) %collective-permute-start) | collective-permute-done | bytes 2080 | tf_op jit(solution)/shard_map/ppermute | solution.py:851
  19.6 1.8 collective-permute-start.5
  21.7 3.3 slice_bitcast_fusion.2.refs_0_.x_ref.x1
  24.9 2.1 shard_map.205.refs_3_
  27.1 5.1 %collective-permute-done.3 = f32[2,4,128]{2,1,0:T(4,128)S(1)} collective-permute-done((f32[2,4,128]{2,1,0:T(4,128)S(1)}, f32[2,4,128]{2,1,0:T(4,128)S(1)}, u32[]{:S(2)}, u32[]{:S(2)}) %collective-permute-start.3) | collective-permute-done | bytes 4128 | tf_op jit(solution)/shard_map/ppermute | solution.py:851
  34.7 2.4 slice_bitcast_fusion
  37.2 6.8 %collective-permute-done.6.refs_7_.refs_8_.refs_5_ = bf16[256,1024]{1,0:T(8,128)(2,1)S(1)} collective-permute-done((bf16[256,1024]{1,0:T(8,128)(2,1)S(1)}, bf16[256,1024]{1,0:T(8,128)(2,1)S(1)}, u32[]{:S(2)}, u32[]{:S(2)}) %collective-permute-start.6) | collective-permute-done | bytes 524320 | tf_op jit(solution)/shard_map/ppermute | solution.py:738
  43.9 1.9 collective-permute-done.7.refs_5_.refs_6_.refs_3_
  49.3 1.8 collective-permute-start.10
  51.3 2.5 collective-permute-start.9
  53.8 16.7 %collective-permute-done.9 = f32[4,4,128]{2,1,0:T(4,128)S(1)} collective-permute-done((f32[4,4,128]{2,1,0:T(4,128)S(1)}, f32[4,4,128]{2,1,0:T(4,128)S(1)}, u32[]{:S(2)}, u32[]{:S(2)}) %collective-permute-start.9) | collective-permute-done | bytes 8224 | tf_op jit(solution)/shard_map/ppermute | solution.py:851
  71.1 1.6 collective-permute-start.14
  73.9 14.0 %shard_map.206 = (bf16[1024,1024]{1,0:T(8,128)(2,1)}, bf16[1024,768]{1,0:T(8,128)(2,1)}, bf16[1024,256]{1,0:T(8,128)(2,1)}, bf16[512,1024]{1,0:T(8,128)(2,1)}, bf16[512,1024]{1,0:T(8,128)(2,1)}) custom-call(s32[9]{0:T(128)} %pad_add_fusion.places._, bf16[1024,1024]{1,0:T(8,128)(2,1)} %slice_bitcast_fusion.3.refs_0_.x_ref.x0, ...), custom_call_target="tpu_custom_call" | custom-call | flops 500000000 | bytes 1 | tf_op jit(solution)/shard_map/pallas_call | solution.py:41
  88.5 1.6 collective-permute-start.16
  90.9 1.6 add_convert_fusion.12
  92.5 1.6 collective-permute-start.20
  94.1 13.0 %shard_map.207 = (bf16[1024,1024]{1,0:T(8,128)(2,1)}, bf16[1024,768]{1,0:T(8,128)(2,1)}, bf16[1024,256]{1,0:T(8,128)(2,1)}, bf16[512,1024]{1,0:T(8,128)(2,1)}, bf16[512,1024]{1,0:T(8,128)(2,1)}) custom-call(s32[9]{0:T(128)} %pad_add_fusion.places._, bf16[1024,1024]{1,0:T(8,128)(2,1)} %slice_bitcast_fusion.2.refs_0_.x_ref.x1, ...), custom_call_target="tpu_custom_call" | custom-call | flops 500000000 | bytes 1 | tf_op jit(solution)/shard_map/pallas_call | solution.py:41
  108.5 1.5 collective-permute-start.17
  110.5 8.3 %collective-permute-done.17.refs_7_ = bf16[64,3072]{1,0:T(8,128)(2,1)S(1)} collective-permute-done((bf16[64,3072]{1,0:T(8,128)(2,1)S(1)}, bf16[64,3072]{1,0:T(8,128)(2,1)S(1)}, u32[]{:S(2)}, u32[]{:S(2)}) %collective-permute-start.17) | collective-permute-done | bytes 393248 | tf_op jit(solution)/shard_map/ppermute | solution.py:738
  121.6 1.7 collective-permute-start.21
  125.7 14.0 %shard_map.208 = (bf16[1024,1024]{1,0:T(8,128)(2,1)}, bf16[1024,1024]{1,0:T(8,128)(2,1)}, bf16[1024,2048]{1,0:T(8,128)(2,1)}, bf16[2,512,1024]{2,1,0:T(8,128)(2,1)}) custom-call(s32[9]{0:T(128)} %pad_add_fusion.places._, bf16[1024,1024]{1,0:T(8,128)(2,1)} %slice_bitcast_fusion.3.refs_0_.x_ref.x0, bf16[512,1024]{1,0:T(8,128)(2,1)} %copy-done.6, ...), custom_call_target="tpu_custom_call" | custom-call | flops 500000000 | bytes 1 | tf_op jit(solution)/shard_map/pallas_call | solution.py:41
  141.1 1.5 collective-permute-start.26
  143.1 1.5 collective-permute-start.28
  144.6 14.1 %shard_map.209 = (bf16[1024,1024]{1,0:T(8,128)(2,1)}, bf16[1024,1024]{1,0:T(8,128)(2,1)}, bf16[1024,2048]{1,0:T(8,128)(2,1)}, bf16[2,512,1024]{2,1,0:T(8,128)(2,1)}) custom-call(s32[9]{0:T(128)} %pad_add_fusion.places._, bf16[1024,1024]{1,0:T(8,128)(2,1)} %slice_bitcast_fusion.3.refs_0_.x_ref.x0, ...), custom_call_target="tpu_custom_call", output_to_operand_aliasing={{0}: (14, {}), {1}: (15, {}), {2}: (16, {})} | custom-call | flops 500000000 | bytes 1 | tf_op jit(solution)/shard_map/pallas_call | solution.py:41
  158.7 2.4 collective-permute-done.26.refs_10_
  163.6 1.6 collective-permute-start.30
  166.8 2.5 add_convert_fusion.7
  169.4 1.6 collective-permute-start.32
  171.0 13.3 %shard_map.210 = (bf16[128,3072]{1,0:T(8,128)(2,1)}, bf16[128,3072]{1,0:T(8,128)(2,1)}, bf16[128,3072]{1,0:T(8,128)(2,1)}, bf16[128,3072]{1,0:T(8,128)(2,1)}, bf...) custom-call(s32[9]{0:T(128)} %pad_add_fusion.places._, ...), custom_call_target="tpu_custom_call" | custom-call | flops 500000000 | bytes 1 | tf_op jit(solution)/shard_map/pallas_call | solution.py:41
  190.1 8.2 %collective-permute-done.34.a = bf16[64,3072]{1,0:T(8,128)(2,1)S(1)} collective-permute-done((bf16[64,3072]{1,0:T(8,128)(2,1)}, bf16[64,3072]{1,0:T(8,128)(2,1)S(1)}, u32[]{:S(2)}, u32[]{:S(2)}) %collective-permute-start.34) | collective-permute-done | bytes 393248 | tf_op jit(solution)/shard_map/ppermute | solution.py:775
  199.1 5.3 %collective-permute-done.36.refs_7_ = bf16[64,3072]{1,0:T(8,128)(2,1)S(1)} collective-permute-done((bf16[64,3072]{1,0:T(8,128)(2,1)S(1)}, bf16[64,3072]{1,0:T(8,128)(2,1)S(1)}, u32[]{:S(2)}, u32[]{:S(2)}) %collective-permute-start.36) | collective-permute-done | bytes 393248 | tf_op jit(solution)/shard_map/ppermute | solution.py:738
  206.3 2.6 shard_map.211
  209.4 1.5 collective-permute-start.40
  213.3 14.2 %shard_map.212 = (bf16[1024,1024]{1,0:T(8,128)(2,1)}, bf16[1024,1024]{1,0:T(8,128)(2,1)}, bf16[1024,2048]{1,0:T(8,128)(2,1)}, bf16[2,512,1024]{2,1,0:T(8,128)(2,1)}) custom-call(s32[9]{0:T(128)} %pad_add_fusion.places._, bf16[1024,1024]{1,0:T(8,128)(2,1)} %slice_bitcast_fusion.2.refs_0_.x_ref.x1, bf16[512,1024]{1,0:T(8,128)(2,1)} %copy-done.2, ...), custom_call_target="tpu_custom_call" | custom-call | flops 500000000 | bytes 1 | tf_op jit(solution)/shard_map/pallas_call | solution.py:41
  229.1 1.6 add_convert_fusion.20
  235.5 14.2 %shard_map.213 = (bf16[1024,1024]{1,0:T(8,128)(2,1)}, bf16[1024,1024]{1,0:T(8,128)(2,1)}, bf16[1024,2048]{1,0:T(8,128)(2,1)}, bf16[2,512,1024]{2,1,0:T(8,128)(2,1)}) custom-call(s32[9]{0:T(128)} %pad_add_fusion.places._, bf16[1024,1024]{1,0:T(8,128)(2,1)} %slice_bitcast_fusion.2.refs_0_.x_ref.x1, ...), custom_call_target="tpu_custom_call", output_to_operand_aliasing={{0}: (14, {}), {1}: (15, {}), {2}: (16, {})} | custom-call | flops 500000000 | bytes 1 | tf_op jit(solution)/shard_map/pallas_call | solution.py:41
  256.7 13.4 %shard_map.214 = (bf16[128,3072]{1,0:T(8,128)(2,1)}, bf16[128,3072]{1,0:T(8,128)(2,1)}, bf16[128,3072]{1,0:T(8,128)(2,1)}, bf16[128,3072]{1,0:T(8,128)(2,1)}, bf...) custom-call(s32[9]{0:T(128)} %pad_add_fusion.places._, ...), custom_call_target="tpu_custom_call" | custom-call | flops 500000000 | bytes 1 | tf_op jit(solution)/shard_map/pallas_call | solution.py:41
  270.1 1.6 collective-permute-start.48
  272.2 7.3 %shard_map.216 = (bf16[1024,1024]{1,0:T(8,128)(2,1)}, f32[1,1024]{1,0:T(1,128)}) custom-call(s32[9]{0:T(128)} %pad_add_fusion.places._, bf16[1024,1024]{1,0:T(8,128)(2,1)} %slice_bitcast_fusion.3.refs_0_.x_ref.x0, bf16[512,1024]{1,0:T(8,128)(2,1)} %copy-done.1, bf16[512,1024]{1,0:T(8,128)(2,1)} %copy-done.6, ...), custom_call_target="tpu_custom_call" | custom-call | flops 500000000 | bytes 1 | tf_op jit(solution)/shard_map/pallas_call | solution.py:41
  279.5 2.6 collective-permute-done.48.b
  283.7 2.4 shard_map.215
  286.8 1.6 collective-permute-start.54
  291.0 17.2 %shard_map.217 = (bf16[1024,768]{1,0:T(8,128)(2,1)}, bf16[1024,768]{1,0:T(8,128)(2,1)}, bf16[1024,1024]{1,0:T(8,128)(2,1)}, bf16[2,256,1024]{2,1,0:T(8,128)(2,1)...) custom-call(s32[9]{0:T(128)} %pad_add_fusion.places._, ...), custom_call_target="tpu_custom_call" | custom-call | flops 500000000 | bytes 1 | tf_op jit(solution)/shard_map/pallas_call | solution.py:41
  313.0 17.2 %shard_map.218 = (bf16[1024,768]{1,0:T(8,128)(2,1)}, bf16[1024,768]{1,0:T(8,128)(2,1)}, bf16[1024,1024]{1,0:T(8,128)(2,1)}, bf16[2,256,1024]{2,1,0:T(8,128)(2,1)...) custom-call(s32[9]{0:T(128)} %pad_add_fusion.places._, ...), custom_call_target="tpu_custom_call", output_to_operand_aliasing={{0}: (21, {}), {1}: (22, {}), {2}: (23, {})} | custom-call | flops 500000000 | bytes 1 | tf_op jit(solution)/shard_map/pallas_call | solution.py:41
  339.2 11.3 %shard_map.219 = (bf16[256,1024]{1,0:T(8,128)(2,1)}, bf16[256,1024]{1,0:T(8,128)(2,1)}, bf16[256,1024]{1,0:T(8,128)(2,1)}, bf16[256,1024]{1,0:T(8,128)(2,1)}, bf...) custom-call(s32[9]{0:T(128)} %pad_add_fusion.places._, ...), custom_call_target="tpu_custom_call" | custom-call | flops 500000000 | bytes 1 | tf_op jit(solution)/shard_map/pallas_call | solution.py:41
  350.6 3.2 collective-permute-done.66
  359.8 4.5 %shard_map.220 = (f32[2,128,1024]{2,1,0:T(8,128)}, f32[2,128,1024]{2,1,0:T(8,128)}, f32[2,1024,128]{2,1,0:T(8,128)}) custom-call(bf16[128,3072]{1,0:T(8,128)(2,1)} %get-tuple-element.355.refs_0_, bf16[128,3072]{1,0:T(8,128)(2,1)} %copy-done.44, bf16[128,3072]{1,0:T(8,128)(2,1)} %copy-done.45, bf16[128,3072]{1,0:T(8,128)(2,1)} %get-tuple-element.358.refs_3_, ...), custom_call_target="tpu_custom_call" | custom-call | flops 500000000 | bytes 1 | tf_op jit(solution)/shard_map/pallas_call | solution.py:41
  366.2 2.0 shard_map.222
  369.1 1.5 add_convert_fusion.1.mine
  370.8 1.6 collective-permute-start.73
  374.3 8.5 %shard_map.221 = bf16[128,16,1024]{2,1,0:T(8,128)(2,1)} custom-call(s32[9]{0:T(128)} %pad_add_fusion.places._, bf16[1024,1024]{1,0:T(8,128)(2,1)} %slice_bitcast_fusion.3.refs_0_.x_ref.x0, bf16[1024,1024]{1,0:T(8,128)(2,1)} %slice_bitcast_fusion.2.refs_0_.x_ref.x1, bf16[512,1024]{1,0:T(8,128)(2,1)} %copy-done.1, bf16[512,1024]{1,0:T(8,128)(2,1)} %copy-done.6, ...), custom_call_target="tpu_custom_call" | custom-call | flops 500000000 | bytes 1 | tf_op jit(solution)/shard_map/pallas_call | solution.py:41
  382.8 3.1 collective-permute-done.75
  390.6 1.8 collective-permute-start.79
  392.5 6.2 %shard_map.223.refs_0_ = bf16[128,16,1024]{2,1,0:T(8,128)(2,1)} custom-call(s32[9]{0:T(128)} %pad_add_fusion.places._, bf16[1024,1024]{1,0:T(8,128)(2,1)} %slice_bitcast_fusion.3.refs_0_.x_ref.x0, bf16[1024,1024]{1,0:T(8,128)(2,1)} %slice_bitcast_fusion.2.refs_0_.x_ref.x1, bf16[1024,1024]{1,0:T(8,128)(2,1)} %get-tuple-element.303.dm0.refs_2_.refs_3_, ...), custom_call_target="tpu_custom_call" | custom-call | flops 500000000 | bytes 1 | tf_op jit(solution)/shard_map/pallas_call | solution.py:41
  398.6 3.8 collective-permute-done.79
  403.9 1.9 collective-permute-start.83
  407.3 6.2 %shard_map.224 = bf16[128,16,1024]{2,1,0:T(8,128)(2,1)} custom-call(s32[9]{0:T(128)} %pad_add_fusion.places._, bf16[1024,1024]{1,0:T(8,128)(2,1)} %slice_bitcast_fusion.3.refs_0_.x_ref.x0, bf16[1024,1024]{1,0:T(8,128)(2,1)} %slice_bitcast_fusion.2.refs_0_.x_ref.x1, ...), custom_call_target="tpu_custom_call", output_to_operand_aliasing={{}: (8, {})} | custom-call | flops 500000000 | bytes 1 | tf_op jit(solution)/shard_map/pallas_call | solution.py:41
  413.5 4.4 %collective-permute-done.82.refs_1_ = bf16[256,1024]{1,0:T(8,128)(2,1)} collective-permute-done((bf16[256,1024]{1,0:T(8,128)(2,1)S(1)}, bf16[256,1024]{1,0:T(8,128)(2,1)}, u32[]{:S(2)}, u32[]{:S(2)}) %collective-permute-start.82) | collective-permute-done | bytes 524320 | tf_op jit(solution)/shard_map/ppermute | solution.py:775
  418.0 2.4 shard_map.225
  (351 shorter events, 85.3 us)
Async XLA Ops:
  2.7 16.6 %collective-permute-start.2 = (bf16[256,1024]{1,0:T(8,128)(2,1)}, bf16[256,1024]{1,0:T(8,128)(2,1)S(1)}, u32[]{:S(2)}, u32[]{:S(2)}) collective-permute-start(bf16[256,1024]{1,0:T(8,128)(2,1)} %shard_map.203.refs_2_.refs_3_.refs_0_), channel_id=1, source_target_pairs={{8,0},{16,8},{24,16},{28,24},{20,28},{12,20},{4,12},{0,4},{9,1},{1... | collective-permute-start | bytes 1572872 | tf_op jit(solution)/shard_map/ppermute | solution.py:739
  5.6 13.7 %collective-permute-start.1 = (bf16[256,1024]{1,0:T(8,128)(2,1)}, bf16[256,1024]{1,0:T(8,128)(2,1)S(1)}, u32[]{:S(2)}, u32[]{:S(2)}) collective-permute-start(bf16[256,1024]{1,0:T(8,128)(2,1)} %shard_map.203.refs_2_.refs_3_.refs_0_), channel_id=1, source_target_pairs={{0,8},{8,16},{16,24},{24,28},{28,20},{20,12},{12,4},{4,0},{1,9},{9... | collective-permute-start | bytes 1572872 | tf_op jit(solution)/shard_map/ppermute | solution.py:738
  6.4 12.9 %collective-permute-start = (f32[1,4,128]{2,1,0:T(4,128)S(1)}, f32[1,4,128]{2,1,0:T(4,128)S(1)}, u32[]{:S(2)}, u32[]{:S(2)}) collective-permute-start(f32[1,4,128]{2,1,0:T(4,128)S(1)} %maximum_convert_fusion), channel_id=1, source_target_pairs={{0,4},{4,0},{8,12},{12,8},{16,20},{20,16},{24,28},{28,24},{1,5},{5... | collective-permute-start | bytes 6152 | tf_op jit(solution)/shard_map/ppermute | solution.py:851
  19.3 12.9 %collective-permute-start.4 = (bf16[256,1024]{1,0:T(8,128)(2,1)S(1)}, bf16[256,1024]{1,0:T(8,128)(2,1)S(1)}, u32[]{:S(2)}, u32[]{:S(2)}) collective-permute-start(bf16[256,1024]{1,0:T(8,128)(2,1)S(1)} %collective-permute-done.1.refs_9_.refs_10_.refs_7_), channel_id=1, source_target_pairs={{0,8},{8,16},{16,24},{24,28},{28,20},{20,12},{12,4},{4,0},{1,9},{9... | collective-permute-start | bytes 1572872 | tf_op jit(solution)/shard_map/ppermute | solution.py:738
  19.6 12.6 %collective-permute-start.5 = (bf16[256,1024]{1,0:T(8,128)(2,1)S(1)}, bf16[256,1024]{1,0:T(8,128)(2,1)S(1)}, u32[]{:S(2)}, u32[]{:S(2)}) collective-permute-start(bf16[256,1024]{1,0:T(8,128)(2,1)S(1)} %collective-permute-done.2.refs_3_.refs_4_.refs_1_), channel_id=1, source_target_pairs={{8,0},{16,8},{24,16},{28,24},{20,28},{12,20},{4,12},{0,4},{9,1},{1... | collective-permute-start | bytes 1572872 | tf_op jit(solution)/shard_map/ppermute | solution.py:739
  45.8 24.7 %collective-permute-start.12 = (bf16[128,3072]{1,0:T(8,128)(2,1)S(1)}, bf16[128,3072]{1,0:T(8,128)(2,1)S(1)}, u32[]{:S(2)}, u32[]{:S(2)}) collective-permute-start(bf16[128,3072]{1,0:T(8,128)(2,1)S(1)} %copy-done.12), channel_id=1, source_target_pairs={{8,0},{16,8},{24,16},{28,24},{20,28},{12,20},{4,12},{0,4},{9,1},{1... | collective-permute-start | bytes 2359304 | tf_op jit(solution)/shard_map/ppermute | solution.py:739
  46.4 24.1 %collective-permute-start.8 = (bf16[128,3072]{1,0:T(8,128)(2,1)S(1)}, bf16[128,3072]{1,0:T(8,128)(2,1)S(1)}, u32[]{:S(2)}, u32[]{:S(2)}) collective-permute-start(bf16[128,3072]{1,0:T(8,128)(2,1)S(1)} %copy-done.12), channel_id=1, source_target_pairs={{0,8},{8,16},{16,24},{24,28},{28,20},{20,12},{12,4},{4,0},{1,9},{9... | collective-permute-start | bytes 2359304 | tf_op jit(solution)/shard_map/ppermute | solution.py:738
  49.3 21.3 %collective-permute-start.10 = (bf16[128,1024]{1,0:T(8,128)(2,1)}, bf16[128,1024]{1,0:T(8,128)(2,1)}, u32[]{:S(2)}, u32[]{:S(2)}) collective-permute-start(bf16[128,1024]{1,0:T(8,128)(2,1)} %slice.196), channel_id=1, source_target_pairs={{0,8},{8,16},{16,24},{24,28},{28,20},{20,12},{12,4},{4,0},{1,9},{9... | collective-permute-start | bytes 786440 | tf_op jit(solution)/shard_map/ppermute | solution.py:738
  51.1 19.4 %collective-permute-start.11 = (bf16[128,1024]{1,0:T(8,128)(2,1)}, bf16[128,1024]{1,0:T(8,128)(2,1)}, u32[]{:S(2)}, u32[]{:S(2)}) collective-permute-start(bf16[128,1024]{1,0:T(8,128)(2,1)} %slice.197), channel_id=1, source_target_pairs={{8,0},{16,8},{24,16},{28,24},{20,28},{12,20},{4,12},{0,4},{9,1},{1... | collective-permute-start | bytes 786440 | tf_op jit(solution)/shard_map/ppermute | solution.py:739
  51.3 19.2 %collective-permute-start.9 = (f32[4,4,128]{2,1,0:T(4,128)S(1)}, f32[4,4,128]{2,1,0:T(4,128)S(1)}, u32[]{:S(2)}, u32[]{:S(2)}) collective-permute-start(f32[4,4,128]{2,1,0:T(4,128)S(1)} %maximum_select_fusion.1), channel_id=1, source_target_pairs={{0,16},{4,20},{8,24},{12,28},{16,0},{20,4},{24,8},{28,12},{1,17},{... | collective-permute-start | bytes 24584 | tf_op jit(solution)/shard_map/ppermute | solution.py:851
  70.6 17.3 %collective-permute-start.13 = (bf16[128,3072]{1,0:T(8,128)(2,1)S(1)}, bf16[128,3072]{1,0:T(8,128)(2,1)S(1)}, u32[]{:S(2)}, u32[]{:S(2)}) collective-permute-start(bf16[128,3072]{1,0:T(8,128)(2,1)S(1)} %collective-permute-done.8.refs_11_), channel_id=1, source_target_pairs={{0,8},{8,16},{16,24},{24,28},{28,20},{20,12},{12,4},{4,0},{1,9},{9... | collective-permute-start | bytes 2359304 | tf_op jit(solution)/shard_map/ppermute | solution.py:738
  71.1 16.9 %collective-permute-start.14 = (bf16[128,3072]{1,0:T(8,128)(2,1)S(1)}, bf16[128,3072]{1,0:T(8,128)(2,1)}, u32[]{:S(2)}, u32[]{:S(2)}) collective-permute-start(bf16[128,3072]{1,0:T(8,128)(2,1)S(1)} %collective-permute-done.12.refs_4_), channel_id=1, source_target_pairs={{8,0},{16,8},{24,16},{28,24},{20,28},{12,20},{4,12},{0,4},{9,1},{1... | collective-permute-start | bytes 2359304 | tf_op jit(solution)/shard_map/ppermute | solution.py:739
  88.0 20.4 %collective-permute-start.15 = (bf16[128,3072]{1,0:T(8,128)(2,1)S(1)}, bf16[128,3072]{1,0:T(8,128)(2,1)S(1)}, u32[]{:S(2)}, u32[]{:S(2)}) collective-permute-start(bf16[128,3072]{1,0:T(8,128)(2,1)S(1)} %collective-permute-done.13.refs_10_), channel_id=1, source_target_pairs={{0,8},{8,16},{16,24},{24,28},{28,20},{20,12},{12,4},{4,0},{1,9},{9... | collective-permute-start | bytes 2359304 | tf_op jit(solution)/shard_map/ppermute | solution.py:738
  88.5 19.8 %collective-permute-start.16 = (bf16[128,3072]{1,0:T(8,128)(2,1)}, bf16[128,3072]{1,0:T(8,128)(2,1)S(1)}, u32[]{:S(2)}, u32[]{:S(2)}) collective-permute-start(bf16[128,3072]{1,0:T(8,128)(2,1)} %collective-permute-done.14.refs_5_), channel_id=1, source_target_pairs={{8,0},{16,8},{24,16},{28,24},{20,28},{12,20},{4,12},{0,4},{9,1},{1... | collective-permute-start | bytes 2359304 | tf_op jit(solution)/shard_map/ppermute | solution.py:739
  92.5 27.5 %collective-permute-start.20 = (bf16[512,1024]{1,0:T(8,128)(2,1)S(1)}, bf16[512,1024]{1,0:T(8,128)(2,1)S(1)}, u32[]{:S(2)}, u32[]{:S(2)}) collective-permute-start(bf16[512,1024]{1,0:T(8,128)(2,1)S(1)} %add_convert_fusion.12), channel_id=1, source_target_pairs={{0,2},{1,3},{2,0},{3,1},{4,6},{5,7},{6,4},{7,5},{8,10},{9,11},{10,... | collective-permute-start | bytes 3145736 | tf_op jit(solution)/shard_map/ppermute | solution.py:809
  121.1 19.5 %collective-permute-start.22 = (bf16[128,3072]{1,0:T(8,128)(2,1)S(1)}, bf16[128,3072]{1,0:T(8,128)(2,1)S(1)}, u32[]{:S(2)}, u32[]{:S(2)}) collective-permute-start(bf16[128,3072]{1,0:T(8,128)(2,1)S(1)} %copy-done.11), channel_id=1, source_target_pairs={{8,0},{16,8},{24,16},{28,24},{20,28},{12,20},{4,12},{0,4},{9,1},{1... | collective-permute-start | bytes 2359304 | tf_op jit(solution)/shard_map/ppermute | solution.py:739
  121.6 19.4 %collective-permute-start.21 = (bf16[128,3072]{1,0:T(8,128)(2,1)S(1)}, bf16[128,3072]{1,0:T(8,128)(2,1)S(1)}, u32[]{:S(2)}, u32[]{:S(2)}) collective-permute-start(bf16[128,3072]{1,0:T(8,128)(2,1)S(1)} %copy-done.11), channel_id=1, source_target_pairs={{0,8},{8,16},{16,24},{24,28},{28,20},{20,12},{12,4},{4,0},{1,9},{9... | collective-permute-start | bytes 2359304 | tf_op jit(solution)/shard_map/ppermute | solution.py:738
  124.2 16.8 %collective-permute-start.25 = (bf16[256,1024]{1,0:T(8,128)(2,1)S(1)}, bf16[256,1024]{1,0:T(8,128)(2,1)S(1)}, u32[]{:S(2)}, u32[]{:S(2)}) collective-permute-start(bf16[256,1024]{1,0:T(8,128)(2,1)S(1)} %get-tuple-element.236), channel_id=1, source_target_pairs={{0,2},{1,3},{2,0},{3,1},{4,6},{5,7},{6,4},{7,5},{8,10},{9,11},{10,... | collective-permute-start | bytes 1572872 | tf_op jit(solution)/shard_map/ppermute | solution.py:809
  141.1 21.3 %collective-permute-start.29 = (bf16[2,512,1024]{2,1,0:T(8,128)(2,1)}, bf16[2,512,1024]{2,1,0:T(8,128)(2,1)S(1)}, u32[]{:S(2)}, u32[]{:S(2)}) collective-permute-start(bf16[2,512,1024]{2,1,0:T(8,128)(2,1)} %get-tuple-element.245), channel_id=1, source_target_pairs={{0,1},{1,0},{2,3},{3,2},{4,5},{5,4},{6,7},{7,6},{8,9},{9,8},{10,11... | collective-permute-start | bytes 6291464 | tf_op jit(solution)/shard_map/ppermute | solution.py:794
  141.1 20.1 %collective-permute-start.26 = (bf16[128,3072]{1,0:T(8,128)(2,1)S(1)}, bf16[128,3072]{1,0:T(8,128)(2,1)}, u32[]{:S(2)}, u32[]{:S(2)}) collective-permute-start(bf16[128,3072]{1,0:T(8,128)(2,1)S(1)} %collective-permute-done.21.refs_11_), channel_id=1, source_target_pairs={{0,8},{8,16},{16,24},{24,28},{28,20},{20,12},{12,4},{4,0},{1,9},{9... | collective-permute-start | bytes 2359304 | tf_op jit(solution)/shard_map/ppermute | solution.py:738
  142.6 19.7 %collective-permute-start.27 = (bf16[128,3072]{1,0:T(8,128)(2,1)S(1)}, bf16[128,3072]{1,0:T(8,128)(2,1)}, u32[]{:S(2)}, u32[]{:S(2)}) collective-permute-start(bf16[128,3072]{1,0:T(8,128)(2,1)S(1)} %collective-permute-done.22.refs_4_), channel_id=1, source_target_pairs={{8,0},{16,8},{24,16},{28,24},{20,28},{12,20},{4,12},{0,4},{9,1},{1... | collective-permute-start | bytes 2359304 | tf_op jit(solution)/shard_map/ppermute | solution.py:739
  143.1 15.6 %collective-permute-start.28 = (bf16[256,1024]{1,0:T(8,128)(2,1)S(1)}, bf16[256,1024]{1,0:T(8,128)(2,1)S(1)}, u32[]{:S(2)}, u32[]{:S(2)}) collective-permute-start(bf16[256,1024]{1,0:T(8,128)(2,1)S(1)} %get-tuple-element.244), channel_id=1, source_target_pairs={{0,2},{1,3},{2,0},{3,1},{4,6},{5,7},{6,4},{7,5},{8,10},{9,11},{10,... | collective-permute-start | bytes 1572872 | tf_op jit(solution)/shard_map/ppermute | solution.py:809
  163.6 20.7 %collective-permute-start.30 = (bf16[128,3072]{1,0:T(8,128)(2,1)}, bf16[128,3072]{1,0:T(8,128)(2,1)S(1)}, u32[]{:S(2)}, u32[]{:S(2)}) collective-permute-start(bf16[128,3072]{1,0:T(8,128)(2,1)} %collective-permute-done.26.refs_10_), channel_id=1, source_target_pairs={{0,8},{8,16},{16,24},{24,28},{28,20},{20,12},{12,4},{4,0},{1,9},{9... | collective-permute-start | bytes 2359304 | tf_op jit(solution)/shard_map/ppermute | solution.py:738
  165.2 19.1 %collective-permute-start.31 = (bf16[128,3072]{1,0:T(8,128)(2,1)}, bf16[128,3072]{1,0:T(8,128)(2,1)S(1)}, u32[]{:S(2)}, u32[]{:S(2)}) collective-permute-start(bf16[128,3072]{1,0:T(8,128)(2,1)} %collective-permute-done.27.refs_5_), channel_id=1, source_target_pairs={{8,0},{16,8},{24,16},{28,24},{20,28},{12,20},{4,12},{0,4},{9,1},{1... | collective-permute-start | bytes 2359304 | tf_op jit(solution)/shard_map/ppermute | solution.py:739
  166.5 17.9 %collective-permute-start.33 = (bf16[512,1024]{1,0:T(8,128)(2,1)S(1)}, bf16[512,1024]{1,0:T(8,128)(2,1)S(1)}, u32[]{:S(2)}, u32[]{:S(2)}) collective-permute-start(bf16[512,1024]{1,0:T(8,128)(2,1)S(1)} %add_convert_fusion.8.refs_0_.att0.refs_4_), channel_id=1, source_target_pairs={{0,1},{1,0},{2,3},{3,2},{4,5},{5,4},{6,7},{7,6},{8,9},{9,8},{10,11... | collective-permute-start | bytes 3145736 | tf_op jit(solution)/shard_map/ppermute | solution.py:815
  169.4 14.9 %collective-permute-start.32 = (bf16[256,1024]{1,0:T(8,128)(2,1)S(1)}, bf16[256,1024]{1,0:T(8,128)(2,1)S(1)}, u32[]{:S(2)}, u32[]{:S(2)}) collective-permute-start(bf16[256,1024]{1,0:T(8,128)(2,1)S(1)} %get-tuple-element.256), channel_id=1, source_target_pairs={{0,2},{1,3},{2,0},{3,1},{4,6},{5,7},{6,4},{7,5},{8,10},{9,11},{10,... | collective-permute-start | bytes 1572872 | tf_op jit(solution)/shard_map/ppermute | solution.py:809
  184.4 21.3 %collective-permute-start.38 = (bf16[256,1024]{1,0:T(8,128)(2,1)S(1)}, bf16[256,1024]{1,0:T(8,128)(2,1)S(1)}, u32[]{:S(2)}, u32[]{:S(2)}) collective-permute-start(bf16[256,1024]{1,0:T(8,128)(2,1)S(1)} %get-tuple-element.266), channel_id=1, source_target_pairs={{0,2},{1,3},{2,0},{3,1},{4,6},{5,7},{6,4},{7,5},{8,10},{9,11},{10,... | collective-permute-start | bytes 1572872 | tf_op jit(solution)/shard_map/ppermute | solution.py:809
  185.9 12.3 %collective-permute-start.34 = (bf16[64,3072]{1,0:T(8,128)(2,1)}, bf16[64,3072]{1,0:T(8,128)(2,1)S(1)}, u32[]{:S(2)}, u32[]{:S(2)}) collective-permute-start(bf16[64,3072]{1,0:T(8,128)(2,1)} %get-tuple-element.259), channel_id=1, source_target_pairs={{0,8},{8,16},{16,24},{24,28},{28,20},{20,12},{12,4},{4,0},{1,9},{9... | collective-permute-start | bytes 1179656 | tf_op jit(solution)/shard_map/ppermute | solution.py:775
  188.0 16.4 %collective-permute-start.36 = (bf16[64,3072]{1,0:T(8,128)(2,1)S(1)}, bf16[64,3072]{1,0:T(8,128)(2,1)S(1)}, u32[]{:S(2)}, u32[]{:S(2)}) collective-permute-start(bf16[64,3072]{1,0:T(8,128)(2,1)S(1)} %slice.208), channel_id=1, source_target_pairs={{0,8},{8,16},{16,24},{24,28},{28,20},{20,12},{12,4},{4,0},{1,9},{9... | collective-permute-start | bytes 1179656 | tf_op jit(solution)/shard_map/ppermute | solution.py:738
  188.9 16.8 %collective-permute-start.37 = (bf16[64,3072]{1,0:T(8,128)(2,1)S(1)}, bf16[64,3072]{1,0:T(8,128)(2,1)S(1)}, u32[]{:S(2)}, u32[]{:S(2)}) collective-permute-start(bf16[64,3072]{1,0:T(8,128)(2,1)S(1)} %slice.209), channel_id=1, source_target_pairs={{8,0},{16,8},{24,16},{28,24},{20,28},{12,20},{4,12},{0,4},{9,1},{1... | collective-permute-start | bytes 1179656 | tf_op jit(solution)/shard_map/ppermute | solution.py:739
  206.2 22.8 %collective-permute-start.41 = (bf16[512,1024]{1,0:T(8,128)(2,1)S(1)}, bf16[512,1024]{1,0:T(8,128)(2,1)S(1)}, u32[]{:S(2)}, u32[]{:S(2)}) collective-permute-start(bf16[512,1024]{1,0:T(8,128)(2,1)S(1)} %fusion.2.dh0), channel_id=1, source_target_pairs={{0,1},{1,0},{2,3},{3,2},{4,5},{5,4},{6,7},{7,6},{8,9},{9,8},{10,11... | collective-permute-start | bytes 3145736 | tf_op jit(solution)/shard_map/ppermute | solution.py:815
  208.9 20.0 %collective-permute-start.39 = (bf16[128,3072]{1,0:T(8,128)(2,1)}, bf16[128,3072]{1,0:T(8,128)(2,1)}, u32[]{:S(2)}, u32[]{:S(2)}) collective-permute-start(bf16[128,3072]{1,0:T(8,128)(2,1)} %get-tuple-element.267), channel_id=1, source_target_pairs={{0,8},{8,16},{16,24},{24,28},{28,20},{20,12},{12,4},{4,0},{1,9},{9... | collective-permute-start | bytes 2359304 | tf_op jit(solution)/shard_map/ppermute | solution.py:775
  209.4 19.6 %collective-permute-start.40 = (bf16[128,3072]{1,0:T(8,128)(2,1)}, bf16[128,3072]{1,0:T(8,128)(2,1)S(1)}, u32[]{:S(2)}, u32[]{:S(2)}) collective-permute-start(bf16[128,3072]{1,0:T(8,128)(2,1)} %get-tuple-element.269), channel_id=1, source_target_pairs={{8,0},{16,8},{24,16},{28,24},{20,28},{12,20},{4,12},{0,4},{9,1},{1... | collective-permute-start | bytes 2359304 | tf_op jit(solution)/shard_map/ppermute | solution.py:776
  211.8 15.7 %collective-permute-start.42 = (bf16[256,1024]{1,0:T(8,128)(2,1)S(1)}, bf16[256,1024]{1,0:T(8,128)(2,1)S(1)}, u32[]{:S(2)}, u32[]{:S(2)}) collective-permute-start(bf16[256,1024]{1,0:T(8,128)(2,1)S(1)} %get-tuple-element.274), channel_id=1, source_target_pairs={{0,2},{1,3},{2,0},{3,1},{4,6},{5,7},{6,4},{7,5},{8,10},{9,11},{10,... | collective-permute-start | bytes 1572872 | tf_op jit(solution)/shard_map/ppermute | solution.py:809
  229.0 22.8 %collective-permute-start.46 = (bf16[2,512,1024]{2,1,0:T(8,128)(2,1)}, bf16[2,512,1024]{2,1,0:T(8,128)(2,1)S(1)}, u32[]{:S(2)}, u32[]{:S(2)}) collective-permute-start(bf16[2,512,1024]{2,1,0:T(8,128)(2,1)} %get-tuple-element.284), channel_id=1, source_target_pairs={{0,1},{1,0},{2,3},{3,2},{4,5},{5,4},{6,7},{7,6},{8,9},{9,8},{10,11... | collective-permute-start | bytes 6291464 | tf_op jit(solution)/shard_map/ppermute | solution.py:794
  230.7 19.8 %collective-permute-start.43 = (bf16[128,3072]{1,0:T(8,128)(2,1)S(1)}, bf16[128,3072]{1,0:T(8,128)(2,1)}, u32[]{:S(2)}, u32[]{:S(2)}) collective-permute-start(bf16[128,3072]{1,0:T(8,128)(2,1)S(1)} %add_convert_fusion.20), channel_id=1, source_target_pairs={{0,8},{8,16},{16,24},{24,28},{28,20},{20,12},{12,4},{4,0},{1,9},{9... | collective-permute-start | bytes 2359304 | tf_op jit(solution)/shard_map/ppermute | solution.py:775
  232.6 20.2 %collective-permute-start.45 = (bf16[256,1024]{1,0:T(8,128)(2,1)}, bf16[256,1024]{1,0:T(8,128)(2,1)S(1)}, u32[]{:S(2)}, u32[]{:S(2)}) collective-permute-start(bf16[256,1024]{1,0:T(8,128)(2,1)} %get-tuple-element.283), channel_id=1, source_target_pairs={{0,2},{1,3},{2,0},{3,1},{4,6},{5,7},{6,4},{7,5},{8,10},{9,11},{10,... | collective-permute-start | bytes 1572872 | tf_op jit(solution)/shard_map/ppermute | solution.py:809
  234.1 19.4 %collective-permute-start.44 = (bf16[128,3072]{1,0:T(8,128)(2,1)}, bf16[128,3072]{1,0:T(8,128)(2,1)S(1)}, u32[]{:S(2)}, u32[]{:S(2)}) collective-permute-start(bf16[128,3072]{1,0:T(8,128)(2,1)} %add_convert_fusion.19), channel_id=1, source_target_pairs={{8,0},{16,8},{24,16},{28,24},{20,28},{12,20},{4,12},{0,4},{9,1},{1... | collective-permute-start | bytes 2359304 | tf_op jit(solution)/shard_map/ppermute | solution.py:776
  253.5 28.6 %collective-permute-start.49 = (bf16[512,1024]{1,0:T(8,128)(2,1)S(1)}, bf16[512,1024]{1,0:T(8,128)(2,1)S(1)}, u32[]{:S(2)}, u32[]{:S(2)}) collective-permute-start(bf16[512,1024]{1,0:T(8,128)(2,1)S(1)} %get-tuple-element.297), channel_id=1, source_target_pairs={{0,2},{1,3},{2,0},{3,1},{4,6},{5,7},{6,4},{7,5},{8,10},{9,11},{10,... | collective-permute-start | bytes 3145736 | tf_op jit(solution)/shard_map/ppermute | solution.py:809
  254.6 27.5 %collective-permute-start.50 = (bf16[128,3072]{1,0:T(8,128)(2,1)S(1)}, bf16[128,3072]{1,0:T(8,128)(2,1)S(1)}, u32[]{:S(2)}, u32[]{:S(2)}) collective-permute-start(bf16[128,3072]{1,0:T(8,128)(2,1)S(1)} %add_convert_fusion.18), channel_id=1, source_target_pairs={{0,8},{8,16},{16,24},{24,28},{28,20},{20,12},{12,4},{4,0},{1,9},{9... | collective-permute-start | bytes 2359304 | tf_op jit(solution)/shard_map/ppermute | solution.py:775
  255.9 26.3 %collective-permute-start.51 = (bf16[128,3072]{1,0:T(8,128)(2,1)S(1)}, bf16[128,3072]{1,0:T(8,128)(2,1)S(1)}, u32[]{:S(2)}, u32[]{:S(2)}) collective-permute-start(bf16[128,3072]{1,0:T(8,128)(2,1)S(1)} %add_convert_fusion.17), channel_id=1, source_target_pairs={{8,0},{16,8},{24,16},{28,24},{20,28},{12,20},{4,12},{0,4},{9,1},{1... | collective-permute-start | bytes 2359304 | tf_op jit(solution)/shard_map/ppermute | solution.py:776
  286.8 21.4 %collective-permute-start.54 = (bf16[128,3072]{1,0:T(8,128)(2,1)}, bf16[128,3072]{1,0:T(8,128)(2,1)S(1)}, u32[]{:S(2)}, u32[]{:S(2)}) collective-permute-start(bf16[128,3072]{1,0:T(8,128)(2,1)} %get-tuple-element.307), channel_id=1, source_target_pairs={{0,8},{8,16},{16,24},{24,28},{28,20},{20,12},{12,4},{4,0},{1,9},{9... | collective-permute-start | bytes 2359304 | tf_op jit(solution)/shard_map/ppermute | solution.py:775
  288.4 20.0 %collective-permute-start.55 = (bf16[128,3072]{1,0:T(8,128)(2,1)}, bf16[128,3072]{1,0:T(8,128)(2,1)}, u32[]{:S(2)}, u32[]{:S(2)}) collective-permute-start(bf16[128,3072]{1,0:T(8,128)(2,1)} %get-tuple-element.309), channel_id=1, source_target_pairs={{8,0},{16,8},{24,16},{28,24},{20,28},{12,20},{4,12},{0,4},{9,1},{1... | collective-permute-start | bytes 2359304 | tf_op jit(solution)/shard_map/ppermute | solution.py:776
  289.0 19.5 %collective-permute-start.56 = (bf16[384,1024]{1,0:T(8,128)(2,1)S(1)}, bf16[384,1024]{1,0:T(8,128)(2,1)S(1)}, u32[]{:S(2)}, u32[]{:S(2)}) collective-permute-start(bf16[384,1024]{1,0:T(8,128)(2,1)S(1)} %slice_bitcast_fusion.4), channel_id=1, source_target_pairs={{0,2},{1,3},{2,0},{3,1},{4,6},{5,7},{6,4},{7,5},{8,10},{9,11},{10,... | collective-permute-start | bytes 2359304 | tf_op jit(solution)/shard_map/ppermute | solution.py:809
  308.5 21.8 %collective-permute-start.57 = (bf16[128,3072]{1,0:T(8,128)(2,1)S(1)}, bf16[128,3072]{1,0:T(8,128)(2,1)S(1)}, u32[]{:S(2)}, u32[]{:S(2)}) collective-permute-start(bf16[128,3072]{1,0:T(8,128)(2,1)S(1)} %add_convert_fusion.16), channel_id=1, source_target_pairs={{0,8},{8,16},{16,24},{24,28},{28,20},{20,12},{12,4},{4,0},{1,9},{9... | collective-permute-start | bytes 2359304 | tf_op jit(solution)/shard_map/ppermute | solution.py:775
  309.8 21.5 %collective-permute-start.59 = (bf16[512,1024]{1,0:T(8,128)(2,1)}, bf16[512,1024]{1,0:T(8,128)(2,1)S(1)}, u32[]{:S(2)}, u32[]{:S(2)}) collective-permute-start(bf16[512,1024]{1,0:T(8,128)(2,1)} %bitcast.24), channel_id=1, source_target_pairs={{0,1},{1,0},{2,3},{3,2},{4,5},{5,4},{6,7},{7,6},{8,9},{9,8},{10,11... | collective-permute-start | bytes 3145736 | tf_op jit(solution)/shard_map/ppermute | solution.py:794
  311.2 21.0 %collective-permute-start.60 = (bf16[128,1024]{1,0:T(8,128)(2,1)}, bf16[128,1024]{1,0:T(8,128)(2,1)S(1)}, u32[]{:S(2)}, u32[]{:S(2)}) collective-permute-start(bf16[128,1024]{1,0:T(8,128)(2,1)} %slice_bitcast_fusion.9), channel_id=1, source_target_pairs={{0,2},{1,3},{2,0},{3,1},{4,6},{5,7},{6,4},{7,5},{8,10},{9,11},{10,... | collective-permute-start | bytes 786440 | tf_op jit(solution)/shard_map/ppermute | solution.py:809
  312.3 19.9 %collective-permute-start.58 = (bf16[128,3072]{1,0:T(8,128)(2,1)S(1)}, bf16[128,3072]{1,0:T(8,128)(2,1)S(1)}, u32[]{:S(2)}, u32[]{:S(2)}) collective-permute-start(bf16[128,3072]{1,0:T(8,128)(2,1)S(1)} %add_convert_fusion.15), channel_id=1, source_target_pairs={{8,0},{16,8},{24,16},{28,24},{20,28},{12,20},{4,12},{0,4},{9,1},{1... | collective-permute-start | bytes 2359304 | tf_op jit(solution)/shard_map/ppermute | solution.py:776
  332.2 21.6 %collective-permute-start.63 = (bf16[512,1024]{1,0:T(8,128)(2,1)}, bf16[512,1024]{1,0:T(8,128)(2,1)S(1)}, u32[]{:S(2)}, u32[]{:S(2)}) collective-permute-start(bf16[512,1024]{1,0:T(8,128)(2,1)} %bitcast.27), channel_id=1, source_target_pairs={{0,1},{1,0},{2,3},{3,2},{4,5},{5,4},{6,7},{7,6},{8,9},{9,8},{10,11... | collective-permute-start | bytes 3145736 | tf_op jit(solution)/shard_map/ppermute | solution.py:794
  333.7 20.6 %collective-permute-start.64 = (bf16[384,1024]{1,0:T(8,128)(2,1)S(1)}, bf16[384,1024]{1,0:T(8,128)(2,1)}, u32[]{:S(2)}, u32[]{:S(2)}) collective-permute-start(bf16[384,1024]{1,0:T(8,128)(2,1)S(1)} %slice.219), channel_id=1, source_target_pairs={{0,2},{1,3},{2,0},{3,1},{4,6},{5,7},{6,4},{7,5},{8,10},{9,11},{10,... | collective-permute-start | bytes 2359304 | tf_op jit(solution)/shard_map/ppermute | solution.py:809
  335.0 19.6 %collective-permute-start.61 = (bf16[128,3072]{1,0:T(8,128)(2,1)}, bf16[128,3072]{1,0:T(8,128)(2,1)S(1)}, u32[]{:S(2)}, u32[]{:S(2)}) collective-permute-start(bf16[128,3072]{1,0:T(8,128)(2,1)} %add_convert_fusion.14), channel_id=1, source_target_pairs={{0,8},{8,16},{16,24},{24,28},{28,20},{20,12},{12,4},{4,0},{1,9},{9... | collective-permute-start | bytes 2359304 | tf_op jit(solution)/shard_map/ppermute | solution.py:775
  336.2 19.3 %collective-permute-start.62 = (bf16[128,3072]{1,0:T(8,128)(2,1)}, bf16[128,3072]{1,0:T(8,128)(2,1)S(1)}, u32[]{:S(2)}, u32[]{:S(2)}) collective-permute-start(bf16[128,3072]{1,0:T(8,128)(2,1)} %add_convert_fusion.13), channel_id=1, source_target_pairs={{8,0},{16,8},{24,16},{28,24},{20,28},{12,20},{4,12},{0,4},{9,1},{1... | collective-permute-start | bytes 2359304 | tf_op jit(solution)/shard_map/ppermute | solution.py:776
  338.4 15.4 %collective-permute-start.66 = (f32[4,1024]{1,0:T(4,128)S(1)}, f32[4,1024]{1,0:T(4,128)S(1)}, u32[]{:S(2)}, u32[]{:S(2)}) collective-permute-start(f32[4,1024]{1,0:T(4,128)S(1)} %fusion.5), channel_id=1, source_target_pairs={{0,2},{1,3},{2,0},{3,1},{4,6},{5,7},{6,4},{7,5},{8,10},{9,11},{10,... | collective-permute-start | bytes 49160 | tf_op jit(solution)/shard_map/ppermute | solution.py:981
  356.0 12.3 %collective-permute-start.69 = (bf16[512,1024]{1,0:T(8,128)(2,1)S(1)}, bf16[512,1024]{1,0:T(8,128)(2,1)S(1)}, u32[]{:S(2)}, u32[]{:S(2)}) collective-permute-start(bf16[512,1024]{1,0:T(8,128)(2,1)S(1)} %fusion.refs_6_), channel_id=1, source_target_pairs={{0,1},{1,0},{2,3},{3,2},{4,5},{5,4},{6,7},{7,6},{8,9},{9,8},{10,11... | collective-permute-start | bytes 3145736 | tf_op jit(solution)/shard_map/ppermute | solution.py:815
  368.3 17.6 %collective-permute-start.72 = (bf16[256,1024]{1,0:T(8,128)(2,1)}, bf16[256,1024]{1,0:T(8,128)(2,1)S(1)}, u32[]{:S(2)}, u32[]{:S(2)}) collective-permute-start(bf16[256,1024]{1,0:T(8,128)(2,1)} %get-tuple-element.368), channel_id=1, source_target_pairs={{0,8},{8,16},{16,24},{24,28},{28,20},{20,12},{12,4},{4,0},{1,9},{9... | collective-permute-start | bytes 1572872 | tf_op jit(solution)/shard_map/ppermute | solution.py:775
  370.7 16.3 %collective-permute-start.74 = (bf16[512,1024]{1,0:T(8,128)(2,1)S(1)}, bf16[512,1024]{1,0:T(8,128)(2,1)S(1)}, u32[]{:S(2)}, u32[]{:S(2)}) collective-permute-start(bf16[512,1024]{1,0:T(8,128)(2,1)S(1)} %add_convert_fusion.1.mine), channel_id=1, source_target_pairs={{0,1},{1,0},{2,3},{3,2},{4,5},{5,4},{6,7},{7,6},{8,9},{9,8},{10,11... | collective-permute-start | bytes 3145736 | tf_op jit(solution)/shard_map/ppermute | solution.py:815
  370.8 15.4 %collective-permute-start.73 = (bf16[256,1024]{1,0:T(8,128)(2,1)}, bf16[256,1024]{1,0:T(8,128)(2,1)S(1)}, u32[]{:S(2)}, u32[]{:S(2)}) collective-permute-start(bf16[256,1024]{1,0:T(8,128)(2,1)} %get-tuple-element.370), channel_id=1, source_target_pairs={{8,0},{16,8},{24,16},{28,24},{20,28},{12,20},{4,12},{0,4},{9,1},{1... | collective-permute-start | bytes 1572872 | tf_op jit(solution)/shard_map/ppermute | solution.py:776
  372.4 13.5 %collective-permute-start.75 = (f32[4,1024]{1,0:T(4,128)S(1)}, f32[4,1024]{1,0:T(4,128)S(1)}, u32[]{:S(2)}, u32[]{:S(2)}) collective-permute-start(f32[4,1024]{1,0:T(4,128)S(1)} %add.171), channel_id=1, source_target_pairs={{0,8},{4,12},{8,0},{12,4},{16,24},{20,28},{24,16},{28,20},{1,9},{5... | collective-permute-start | bytes 49160 | tf_op jit(solution)/shard_map/ppermute | solution.py:981
  373.3 13.7 %collective-permute-start.76 = (bf16[256,1024]{1,0:T(8,128)(2,1)S(1)}, bf16[256,1024]{1,0:T(8,128)(2,1)S(1)}, u32[]{:S(2)}, u32[]{:S(2)}) collective-permute-start(bf16[256,1024]{1,0:T(8,128)(2,1)S(1)} %get-tuple-element.374), channel_id=1, source_target_pairs={{0,2},{1,3},{2,0},{3,1},{4,6},{5,7},{6,4},{7,5},{8,10},{9,11},{10,... | collective-permute-start | bytes 1572872 | tf_op jit(solution)/shard_map/ppermute | solution.py:809
  387.0 15.5 %collective-permute-start.77 = (bf16[256,1024]{1,0:T(8,128)(2,1)S(1)}, bf16[256,1024]{1,0:T(8,128)(2,1)S(1)}, u32[]{:S(2)}, u32[]{:S(2)}) collective-permute-start(bf16[256,1024]{1,0:T(8,128)(2,1)S(1)} %add_convert_fusion.24), channel_id=1, source_target_pairs={{0,8},{8,16},{16,24},{24,28},{28,20},{20,12},{12,4},{4,0},{1,9},{9... | collective-permute-start | bytes 1572872 | tf_op jit(solution)/shard_map/ppermute | solution.py:775
  388.2 14.2 %collective-permute-start.78 = (bf16[256,1024]{1,0:T(8,128)(2,1)S(1)}, bf16[256,1024]{1,0:T(8,128)(2,1)S(1)}, u32[]{:S(2)}, u32[]{:S(2)}) collective-permute-start(bf16[256,1024]{1,0:T(8,128)(2,1)S(1)} %add_convert_fusion.23), channel_id=1, source_target_pairs={{8,0},{16,8},{24,16},{28,24},{20,28},{12,20},{4,12},{0,4},{9,1},{1... | collective-permute-start | bytes 1572872 | tf_op jit(solution)/shard_map/ppermute | solution.py:776
  389.0 13.5 %collective-permute-start.80 = (bf16[256,1024]{1,0:T(8,128)(2,1)S(1)}, bf16[256,1024]{1,0:T(8,128)(2,1)S(1)}, u32[]{:S(2)}, u32[]{:S(2)}) collective-permute-start(bf16[256,1024]{1,0:T(8,128)(2,1)S(1)} %get-tuple-element.380), channel_id=1, source_target_pairs={{0,2},{1,3},{2,0},{3,1},{4,6},{5,7},{6,4},{7,5},{8,10},{9,11},{10,... | collective-permute-start | bytes 1572872 | tf_op jit(solution)/shard_map/ppermute | solution.py:809
  403.7 14.2 %collective-permute-start.82 = (bf16[256,1024]{1,0:T(8,128)(2,1)S(1)}, bf16[256,1024]{1,0:T(8,128)(2,1)}, u32[]{:S(2)}, u32[]{:S(2)}) collective-permute-start(bf16[256,1024]{1,0:T(8,128)(2,1)S(1)} %add_convert_fusion.22), channel_id=1, source_target_pairs={{0,8},{8,16},{16,24},{24,28},{28,20},{20,12},{12,4},{4,0},{1,9},{9... | collective-permute-start | bytes 1572872 | tf_op jit(solution)/shard_map/ppermute | solution.py:775
  403.9 14.1 %collective-permute-start.83 = (bf16[256,1024]{1,0:T(8,128)(2,1)S(1)}, bf16[256,1024]{1,0:T(8,128)(2,1)}, u32[]{:S(2)}, u32[]{:S(2)}) collective-permute-start(bf16[256,1024]{1,0:T(8,128)(2,1)S(1)} %add_convert_fusion.21), channel_id=1, source_target_pairs={{8,0},{16,8},{24,16},{28,24},{20,28},{12,20},{4,12},{0,4},{9,1},{1... | collective-permute-start | bytes 1572872 | tf_op jit(solution)/shard_map/ppermute | solution.py:776
  (100 other events, 809.3 us)
